TPU v7x, 32 devices: a whole 2x2x4 slice. The times are simulated.
32 devices in a mesh: wide: 8 (over y, x, core), narrow: 4 (over z).
Axes of the slice: x: 2, y: 2, z: 4, core: 2. Of those that a mesh axis runs over, the one named last changes fastest.
Arguments:
- token_ids: int32 [32, 512], P('wide'), may hold values from 0 to 30521
- doc_ids: int32 [32, 512], P(('wide', 'narrow')), may hold values from 0 to 5, never falling along the last dimension, each value on 1 to 256 neighbouring positions
- mlm_pos: int32 [32, 80], P(('wide', 'narrow')), may hold values from 0 to 511
- mlm_labels: int32 [32, 80], P('wide'), may hold values from 0 to 30521
- mlm_valid: int32 [32, 80], P('wide'), may hold values from 0 to 1, as said below
- table: float32 [30528, 1024], P('narrow', 'wide')
- table_m: float32 [30528, 1024], P('narrow', 'wide'), may hold values from -0.0012207031 to 0.0012207031
- table_v: float32 [30528, 1024], P('narrow', 'wide'), may hold values from 3.90625e-08 to 1.5625e-07
- small: float32 [528, 1024], replicated
- small_m: float32 [528, 1024], replicated, may hold values from -0.0012207031 to 0.0012207031
- small_v: float32 [528, 1024], replicated, may hold values from 3.90625e-08 to 1.5625e-07
- layer: float32 [1024, 12288], P('narrow', 'wide'), may hold values from -0.1875 to 0.1875
- layer_m: float32 [1024, 12288], P('narrow'), may hold values from -0.0012207031 to 0.0012207031
- layer_v: float32 [1024, 12288], P('narrow', 'wide'), may hold values from 3.90625e-08 to 1.5625e-07
- worker_err: float32 [8, 1024, 12288], P('wide', 'narrow'), may hold values from -0.00036621094 to 0.00036621094
- server_err: float32 [1024, 12288], P('narrow', 'wide'), may hold values from -0.00036621094 to 0.00036621094
Outputs:
- loss: float32 [2], replicated
- new_table: float32 [30528, 1024], P('narrow', 'wide')
- new_table_m: float32 [30528, 1024], P('narrow', 'wide')
- new_small: float32 [528, 1024], replicated
- new_small_m: float32 [528, 1024], replicated
- new_layer: float32 [1024, 12288], P('narrow', 'wide')
- new_layer_m: float32 [1024, 12288], P('narrow')
- new_worker_err: float32 [8, 1024, 12288], P('wide', 'narrow')
- new_server_err: float32 [1024, 12288], P('narrow', 'wide')
- norms: float32 [2, 6], replicated
Inputs may be any that keep to these rules, and one draw needn't show every extreme that they name: `doc_ids`: document numbers never fall along a packed row. `mlm_valid`: the first masked slot of every packed row is valid.
All inputs are finite; a program needn't handle non-finite values. Where the computation divides by a largest or mean magnitude, that divisor is 1e-20 or more.
Results may differ from a plain program's by a relative error of at most 0.012.
Values may be sent and summed in bfloat16 or wider, within the bound.
No kernel may reach another device: no remote copies, remote signals or barrier semaphores. Data moves between devices by JAX's collectives and lax.ppermute only.
A program may use at most 384 MiB of HBM per device.

v0:
```python
import jax
import jax.numpy as jnp
from jax import lax
from jax.sharding import PartitionSpec as P

D = 1024
HEADS = 16
HEAD = 64
FF = 4096
VREAL = 30522
L = 512
MPS = 80


LN_EPS = 1e-12
BETA = 0.9
DECAY = 0.01
RATE = 0.25
OPT_EPS = 1e-06
MAG_EPS = 1e-08


def joined(value, axis, join):
    pieces = jax.tree.map(lambda part: lax.all_gather(part, axis), value)
    head = jax.tree.map(lambda part: part[0], pieces)
    tail = jax.tree.map(lambda part: part[1:], pieces)
    subtotal, _ = lax.scan(lambda subtotal, slab: (join(subtotal, slab), None), head, tail)
    return subtotal


def norm_rows(x, gain, shift):
    mean = jnp.mean(x, axis=-1, keepdims=True)
    cent = x - mean
    var = jnp.mean(cent * cent, axis=-1, keepdims=True)
    return cent * lax.rsqrt(var + LN_EPS) * gain + shift


def gelu_exact(upper):
    return jax.nn.gelu(upper, approximate=False)


def matmul(left, right):
    return jnp.dot(left, right, preferred_element_type=jnp.float32)


def matmul_tn(left, right):
    return lax.dot_general(
        left, right, (((0,), (0,)), ((), ())), preferred_element_type=jnp.float32
    )


def matmul_nt(left, right):
    return lax.dot_general(
        left, right, (((1,), (1,)), ((), ())), preferred_element_type=jnp.float32
    )


def score_block(heads, docs):
    raw = (
        jnp.einsum(
            "sqhd,skhd->shqk", heads[:, :, 0], heads[:, :, 1], preferred_element_type=jnp.float32
        )
        * 0.125
    )
    same = (docs[:, :, None] == docs[:, None, :])[:, None]
    return jnp.where(same, raw, -1000000000.0)


def merge_rows(first, second):
    peak = jnp.maximum(first[0], second[0])
    total = first[1] * jnp.exp(first[0] - peak) + second[1] * jnp.exp(second[0] - peak)
    return (peak, total, first[2] + second[2])


def layer_forward(embedded, docs, small, weights):
    seqs = docs.shape[0]
    base = L + 2
    x0 = norm_rows(embedded, small[base], small[base + 1])
    act = x0.astype(jnp.bfloat16)
    bias = jnp.concatenate([small[base + 6], jnp.zeros((D,), jnp.float32), small[base + 7]])
    qkv = (matmul(act, weights[:, 0 : 3 * D]) + bias).astype(jnp.bfloat16)
    heads = qkv.reshape(seqs, L, 3, HEADS, HEAD)
    scores = score_block(heads, docs)
    top = jnp.max(scores, axis=-1, keepdims=True)
    lse = top + jnp.log(jnp.sum(jnp.exp(scores - top), axis=-1, keepdims=True))
    prob = jnp.exp(scores - lse).astype(jnp.bfloat16)
    out = jnp.einsum("shqk,skhd->sqhd", prob, heads[:, :, 2], preferred_element_type=jnp.float32)
    out = out.reshape(seqs * L, D).astype(jnp.bfloat16)
    rone = x0 + (matmul(out, weights[:, 3 * D : 4 * D]) + small[base + 8])
    hone = norm_rows(rone, small[base + 2], small[base + 3])
    fin = hone.astype(jnp.bfloat16)
    upper = matmul(fin, weights[:, 4 * D : 4 * D + FF]) + small[base + 10 :].reshape(FF)
    gated = gelu_exact(upper).astype(jnp.bfloat16)
    rtwo = hone + (matmul_nt(gated, weights[:, 4 * D + FF :]) + small[base + 9])
    htwo = norm_rows(rtwo, small[base + 4], small[base + 5])
    return (htwo, (embedded, act, qkv, lse, out, rone, fin, upper, gated, rtwo))


def layer_backward(dhtwo, kept, docs, small, weights):
    embedded, act, qkv, lse, out, rone, fin, upper, gated, rtwo = kept
    seqs = docs.shape[0]
    base = L + 2
    _, pull = jax.vjp(norm_rows, rtwo, small[base + 4], small[base + 5])
    drtwo, dgain_two, dshift_two = pull(dhtwo)
    dffn = drtwo.astype(jnp.bfloat16)
    dgated = matmul(dffn, weights[:, 4 * D + FF :])
    _, pull = jax.vjp(gelu_exact, upper)
    dupper = pull(dgated)[0].astype(jnp.bfloat16)
    dhone = drtwo + matmul_nt(dupper, weights[:, 4 * D : 4 * D + FF])
    _, pull = jax.vjp(norm_rows, rone, small[base + 2], small[base + 3])
    drone, dgain_one, dshift_one = pull(dhone)
    dattn = drone.astype(jnp.bfloat16)
    dout = (
        matmul_nt(dattn, weights[:, 3 * D : 4 * D])
        .astype(jnp.bfloat16)
        .reshape(seqs, L, HEADS, HEAD)
    )
    heads = qkv.reshape(seqs, L, 3, HEADS, HEAD)
    prob = jnp.exp(score_block(heads, docs) - lse)
    dvalue = jnp.einsum(
        "shqk,sqhd->skhd", prob.astype(jnp.bfloat16), dout, preferred_element_type=jnp.float32
    )
    dprob = jnp.einsum("sqhd,skhd->shqk", dout, heads[:, :, 2], preferred_element_type=jnp.float32)
    dscore = (prob * (dprob - jnp.sum(prob * dprob, axis=-1, keepdims=True))).astype(jnp.bfloat16)
    dquery = (
        jnp.einsum("shqk,skhd->sqhd", dscore, heads[:, :, 1], preferred_element_type=jnp.float32)
        * 0.125
    )
    dkey = (
        jnp.einsum("shqk,sqhd->skhd", dscore, heads[:, :, 0], preferred_element_type=jnp.float32)
        * 0.125
    )
    dqkv = jnp.stack([dquery, dkey, dvalue], axis=2).reshape(seqs * L, 3 * D).astype(jnp.bfloat16)
    dxzero = drone + matmul_nt(dqkv, weights[:, 0 : 3 * D])
    _, pull = jax.vjp(norm_rows, embedded, small[base], small[base + 1])
    dembed, dgain_emb, dshift_emb = pull(dxzero)
    bias_qkv = jnp.sum(dqkv, axis=0, dtype=jnp.float32)
    vectors = jnp.stack(
        [
            dgain_emb,
            dshift_emb,
            dgain_one,
            dshift_one,
            dgain_two,
            dshift_two,
            bias_qkv[0:D],
            bias_qkv[2 * D : 3 * D],
            jnp.sum(dattn, axis=0, dtype=jnp.float32),
            jnp.sum(dffn, axis=0, dtype=jnp.float32),
        ]
    )
    bias_up = jnp.sum(dupper, axis=0, dtype=jnp.float32).reshape(FF // D, D)
    return (
        dembed,
        jnp.concatenate([vectors, bias_up], axis=0),
        (act, dqkv, out, dattn, fin, dupper, dffn, gated),
    )


def weight_block(lefts, rights):
    blocks = []
    for left, right in zip(lefts, rights):
        blocks.append(matmul_tn(left, right))
    return jnp.concatenate(blocks, axis=1)


def shards(
    token_ids,
    doc_ids,
    mlm_pos,
    mlm_labels,
    mlm_valid,
    table,
    table_m,
    table_v,
    small,
    small_m,
    small_v,
    layer,
    layer_m,
    layer_v,
    worker_err,
    server_err,
):
    n_wide = lax.axis_size("wide")
    narrow_me = lax.axis_index("narrow")
    wide_me = lax.axis_index("wide")
    seqs = doc_ids.shape[0]
    layer_cols, table_cols = (
        lax.all_gather(layer.astype(jnp.bfloat16), "wide", axis=1, tiled=True),
        lax.all_gather(table.astype(jnp.bfloat16), "wide", axis=1, tiled=True),
    )
    weights = lax.all_gather(layer_cols, "narrow", axis=0, tiled=True)
    vshard = table_cols.shape[0]
    local_ids = token_ids - narrow_me * vshard
    inside = (local_ids >= 0) & (local_ids < vshard)
    picked = jnp.take(table_cols, jnp.clip(local_ids, 0, vshard - 1), axis=0)
    picked = jnp.where(inside[..., None], picked.astype(jnp.float32), 0.0)
    looked = lax.psum_scatter(
        picked.astype(jnp.bfloat16), "narrow", scatter_dimension=0, tiled=True
    ).astype(jnp.float32)
    even_doc = (doc_ids % 2 == 0)[..., None]
    embedded = looked + small[0:L][None] + jnp.where(even_doc, small[L], small[L + 1])
    htwo, kept = layer_forward(embedded.reshape(seqs * L, D), doc_ids, small, weights)
    hmask = jnp.take_along_axis(htwo.reshape(seqs, L, D), mlm_pos[..., None], axis=1)
    hmask = hmask.reshape(seqs * MPS, D).astype(jnp.bfloat16)
    group_h = lax.all_gather(hmask, "narrow", axis=0, tiled=True)
    vocab = narrow_me * vshard + jnp.arange(vshard)
    logits = jnp.where((vocab < VREAL)[None], matmul_nt(group_h, table_cols), -1000000000.0)
    labels = mlm_labels.reshape(-1)
    hit = vocab[None] == labels[:, None]
    top = jnp.max(logits, axis=1)
    total = jnp.sum(jnp.exp(logits - top[:, None]), axis=1)
    target = jnp.sum(jnp.where(hit, logits, 0.0), axis=1)
    top, total, target = joined((top, total, target), "narrow", merge_rows)
    lse = top + jnp.log(total)
    flags = mlm_valid.reshape(-1).astype(jnp.float32)
    own = seqs * MPS
    own_loss = lax.dynamic_slice_in_dim(flags * (lse - target), narrow_me * own, own)
    own_flags = lax.dynamic_slice_in_dim(flags, narrow_me * own, own)
    loss_sum, count = lax.psum((jnp.sum(own_loss), jnp.sum(own_flags)), ("wide", "narrow"))
    dlogit = (
        (jnp.exp(logits - lse[:, None]) - hit.astype(jnp.float32)) * (flags / count)[:, None]
    ).astype(jnp.bfloat16)
    dhmask = lax.psum_scatter(matmul(dlogit, table_cols), "narrow", scatter_dimension=0, tiled=True)
    table_head = matmul_tn(dlogit, group_h)
    dhtwo = (
        jnp.zeros((seqs, L, D), jnp.float32)
        .at[jnp.arange(seqs)[:, None], mlm_pos]
        .add(dhmask.reshape(seqs, MPS, D))
    )
    dembed, vectors, saved = layer_backward(
        dhtwo.reshape(seqs * L, D), kept, doc_ids, small, weights
    )
    act, dqkv, out, dattn, fin, dupper, dffn, gated = saved
    worker_grad = lax.psum_scatter(
        weight_block((act, out, fin, dffn), (dqkv, dattn, dupper, gated)).astype(jnp.bfloat16),
        "narrow",
        scatter_dimension=0,
        tiled=True,
    ).astype(jnp.float32)
    dembed_rows = dembed.reshape(seqs, L, D)
    seg_even = jnp.sum(jnp.where(even_doc, dembed_rows, 0.0), axis=(0, 1))
    seg_odd = jnp.sum(jnp.where(even_doc, 0.0, dembed_rows), axis=(0, 1))
    small_grad = jnp.concatenate(
        [jnp.sum(dembed_rows, axis=0), seg_even[None], seg_odd[None], vectors], axis=0
    )
    group_rows = lax.all_gather(dembed_rows.astype(jnp.bfloat16), "narrow", axis=0, tiled=True)
    slots = jnp.where(inside, local_ids, vshard).reshape(-1)
    table_grad = table_head.at[slots].add(
        group_rows.reshape(-1, D).astype(jnp.float32), mode="drop"
    )
    table_grad = lax.psum_scatter(
        table_grad.astype(jnp.bfloat16), "wide", scatter_dimension=1, tiled=True
    ).astype(jnp.float32)
    span = BETA * layer_m + (1.0 - BETA) * worker_grad + worker_err[0]
    scale = jnp.mean(jnp.abs(span)) + MAG_EPS
    sent = scale * jnp.tanh(span / scale)
    new_worker = (span - sent)[None]
    part_cols = layer.shape[1]
    summed = lax.psum(sent.astype(jnp.bfloat16), "wide").astype(jnp.float32)
    mixed = lax.dynamic_slice_in_dim(summed, wide_me * part_cols, part_cols, 1) / n_wide
    server_in = mixed + server_err
    sscale = jnp.mean(jnp.abs(server_in)) + MAG_EPS
    server_out = sscale * jnp.tanh(server_in / sscale)
    new_server = server_in - server_out
    new_m = lax.all_gather(server_out.astype(jnp.bfloat16), "wide", axis=1, tiled=True).astype(
        server_out.dtype
    )
    layer_upd = server_out / (jnp.sqrt(layer_v) + OPT_EPS) + DECAY * layer
    column = wide_me * part_cols + jnp.arange(part_cols)
    which = (
        (column >= 3 * D).astype(jnp.int32)
        + (column >= 4 * D).astype(jnp.int32)
        + (column >= 4 * D + FF).astype(jnp.int32)
    )
    onehot = (which[:, None] == jnp.arange(4)[None]).astype(jnp.float32)
    wsq = jnp.sum(jnp.sum(layer * layer, axis=0)[:, None] * onehot, axis=0)
    usq = jnp.sum(jnp.sum(layer_upd * layer_upd, axis=0)[:, None] * onehot, axis=0)
    table_mom = BETA * table_m + (1.0 - BETA) * table_grad
    table_upd = table_mom / (jnp.sqrt(table_v) + OPT_EPS) + DECAY * table
    parts = jnp.concatenate(
        [wsq, usq, jnp.sum(table * table)[None], jnp.sum(table_upd * table_upd)[None]]
    )
    small_grad, sums = lax.psum((small_grad, parts), ("wide", "narrow"))
    small_mom = BETA * small_m + (1.0 - BETA) * small_grad
    small_upd = small_mom / (jnp.sqrt(small_v) + OPT_EPS) + DECAY * small
    wnorm = jnp.sqrt(jnp.concatenate([sums[0:4], sums[8:9], jnp.sum(small * small)[None]]))
    unorm = jnp.sqrt(jnp.concatenate([sums[4:8], sums[9:10], jnp.sum(small_upd * small_upd)[None]]))
    ratio = wnorm / unorm
    new_layer = layer - RATE * jnp.sum(onehot * ratio[None, 0:4], axis=1)[None] * layer_upd
    new_table = table - RATE * ratio[4] * table_upd
    new_small = small - RATE * ratio[5] * small_upd
    return (
        jnp.stack([loss_sum, count]),
        new_table,
        table_mom,
        new_small,
        small_mom,
        new_layer,
        new_m,
        new_worker,
        new_server,
        jnp.stack([wnorm, unorm]),
    )


def solution(mesh):
    placed = (
        P("wide", None),
        P(("wide", "narrow"), None),
        P(("wide", "narrow"), None),
        P("wide", None),
        P("wide", None),
        P("narrow", "wide"),
        P("narrow", "wide"),
        P("narrow", "wide"),
        P(),
        P(),
        P(),
        P("narrow", "wide"),
        P("narrow", None),
        P("narrow", "wide"),
        P("wide", "narrow", None),
        P("narrow", "wide"),
    )
    return jax.shard_map(
        shards,
        mesh=mesh,
        in_specs=placed,
        out_specs=(
            P(),
            P("narrow", "wide"),
            P("narrow", "wide"),
            P(),
            P(),
            P("narrow", "wide"),
            P("narrow", None),
            P("wide", "narrow", None),
            P("narrow", "wide"),
            P(),
        ),
        check_vma=False,
    )
```

profile of v0, /device:TPU:0, one launch (start us, length us, event | category | flops | bytes accessed | tf_op | source)
XLA Modules:
  0.0 1904.0 jit_solution(10974478764891968816)
XLA Ops:
  7.2 3.7 convert_element_type.184
  12.7 89.1 %all-gather.10.cloned.1.call-done = bf16[7632,1024]{1,0:T(8,128)(2,1)} async-done(((bf16[7632,128]{1,0:T(8,128)(2,1)}), bf16[7632,1024]{1,0:T(8,128)(2,1)}) %all-gather.10.cloned.1.call-update) | async-done | bytes 15630352 | tf_op jit(solution)/shard_map/all_gather | solution.py:191
  101.8 18.4 gather_fusion
  120.2 4.2 select_convert_fusion
  124.5 25.3 %all-gather.12.cloned.1.call-done = bf16[256,12288]{1,0:T(8,128)(2,1)} async-done(((bf16[256,1536]{1,0:T(8,128)(2,1)}), bf16[256,12288]{1,0:T(8,128)(2,1)}) %all-gather.12.cloned.1.call-update) | async-done | bytes 6291472 | tf_op jit(solution)/shard_map/all_gather | solution.py:190
  150.7 44.1 %psum.36 = f32[]{:T(128)} all-reduce(f32[]{:T(128)} %dynamic-slice_reduce_fusion.3), channel_id=1, replica_groups=mesh['wide'=8,'narrow'=4] {'wide','narrow'}, use_global_device_ids=true, to_apply=%region_17.18 | all-reduce | flops 1 | bytes 8 | tf_op jit(solution)/shard_map/psum | solution.py:221
  199.5 31.1 %reduce-scatter.7.cloned.1.call-done = bf16[1,512,1024]{2,1,0:T(8,128)(2,1)} async-done(((bf16[4,512,1024]{2,1,0:T(8,128)(2,1)}), bf16[1,512,1024]{2,1,0:T(8,128)(2,1)}) %reduce-scatter.7.cloned.1.call-update) | async-done | bytes 1048592 | tf_op jit(solution)/shard_map/reduce_scatter | solution.py:199
  234.0 423.8 %all-gather.14.cloned.1.call-done = bf16[1024,12288]{1,0:T(8,128)(2,1)} async-done(((bf16[256,12288]{1,0:T(8,128)(2,1)}), bf16[1024,12288]{1,0:T(8,128)(2,1)}) %all-gather.14.cloned.1.call-update) | async-done | bytes 25165840 | tf_op jit(solution)/shard_map/all_gather | solution.py:193
  657.7 8.6 add_convert_fusion.1
  666.4 3.2 copy.50
  669.6 7.5 fusion
  677.0 9.2 exponential_reduce_fusion
  686.3 8.4 convolution_convert_fusion.4
  694.8 3.5 fusion.100
  698.8 26.4 %multiply_convert_fusion.1 = (bf16[512,4096]{1,0:T(8,128)(2,1)S(1)}, f32[512,4096]{1,0:T(8,128)}, f32[512,4096]{1,0:T(8,128)}) fusion(f32[4096]{0:T(1024)S(1)} %bitcast.184, bf16[1024,12288]{1,0:T(8,128)(2,1)} %all-gather.14.cloned.1.call-done, f32[512,1024]{1,0:T(8,128)S(1)} %get-tuple-element.154, f32[1024]{0:T(1024)S(1)} %bitcast.206, ...), kind=kOutput, calls=%fused_computation.35 | convolution fusion | flops 4436000768 | bytes 31485952 | tf_op jit(solution)/shard_map/dot_general | solution.py:43
  725.2 9.7 fusion.101
  738.3 16.9 all_gather.39
  755.1 11.4 fusion.102
  766.8 6.3 fusion.2
  773.6 17.1 all-reduce.5
  792.7 14.0 fusion.88
  806.8 29.4 %reduce-scatter.9.cloned.1.call-done = f32[80,1024]{1,0:T(8,128)} async-done(((f32[320,1024]{1,0:T(8,128)}), f32[80,1024]{1,0:T(8,128)}) %reduce-scatter.9.cloned.1.call-update) | async-done | bytes 327696 | tf_op jit(solution)/shard_map/reduce_scatter | solution.py:225
  836.2 3.1 scatter_custom_fusion
  839.3 3.1 multiply_reduce_fusion.5
  843.4 14.3 convert_reduce_fusion
  857.8 9.8 multiply_reduce_fusion.6
  870.6 4.0 fusion.44
  874.6 2.3 copy.52
  876.9 12.3 multiply_reduce_fusion
  889.2 12.4 multiply_convert_fusion
  903.1 2.6 multiply_bitcast_fusion
  905.8 8.0 convolution_bitcast_fusion
  917.1 6.3 multiply_reduce_fusion.7
  927.2 3.8 convolution_convert_fusion.3
  931.0 4.5 copy.56
  935.6 8.1 convolution_convert_fusion.2
  943.7 6.9 convolution_convert_fusion
  950.6 7.3 convolution_convert_fusion.1
  957.8 16.9 pad_maximum_fusion
  976.4 4.4 concatenate.66
  980.8 20.0 %fusion.86 = f32[7632,1024]{1,0:T(8,128)} fusion(bf16[320,1024]{1,0:T(8,128)(2,1)S(1)} %copy-done.22, f32[320,7632]{1,0:T(8,128)} %get-tuple-element.159, f32[320]{0:T(512)S(1)} %get-tuple-element.142, f32[320]{0:T(512)S(1)} %get-tuple-element.112, s32[7632]{0:T(1024)S(1)} %iota_add_fusion, s32[320]{0:T(512)S(1)} %eq.71), kind=kOutput, calls=%fused_computation.219 | convolution fusion | flops 5016360960 | bytes 41719360 | tf_op jit(solution)/shard_map/dot_general | solution.py:47
  1000.8 6.1 all-gather.18.cloned.1.call-done
  1006.9 39.5 %scatter_custom_fusion.1 = f32[7632,1024]{1,0:T(8,128)} fusion(f32[7632,1024]{1,0:T(8,128)} %fusion.86, s32[2048]{0:T(1024)S(1)} %bitcast.205, bf16[2048,1024]{1,0:T(8,128)(2,1)} %all-gather.18.cloned.1.call-done), kind=kCustom, calls=%fused_computation.31 | custom fusion | flops 4194304 | bytes 35454976 | tf_op jit(solution)/shard_map/scatter-add | solution.py:250
  1046.4 16.4 convert_element_type.220
  1062.8 20.4 %copy.61 = bf16[7632,1024]{0,1:T(8,128)(2,1)} copy(bf16[7632,1024]{1,0:T(8,128)(2,1)} %convert_element_type.220) | data formatting | bytes 31260672
  1083.2 339.1 %reduce-scatter.11.cloned.1.call-done = bf16[256,12288]{1,0:T(8,128)(2,1)} async-done(((bf16[1024,12288]{1,0:T(8,128)(2,1)}), bf16[256,12288]{1,0:T(8,128)(2,1)}) %reduce-scatter.11.cloned.1.call-update) | async-done | bytes 6291472 | tf_op jit(solution)/shard_map/reduce_scatter | solution.py:236
  1422.3 17.1 abs_reduce_fusion
  1440.1 11.7 subtract_bitcast_fusion
  1453.6 111.3 %all-reduce.11.cloned.1.call-done = f32[528,1024]{1,0:T(8,128)} async-done(((f32[528,1024]{1,0:T(8,128)}), f32[528,1024]{1,0:T(8,128)}) %all-reduce.11.cloned.1.call-update) | async-done | bytes 2162704 | tf_op jit(solution)/shard_map/psum | solution.py:285
  1564.8 6.2 multiply_reduce_fusion.3
  1571.0 106.1 %reduce-scatter.13.cloned.1.call-done = bf16[128,7632]{1,0:T(8,128)(2,1)} async-done(((bf16[1024,7632]{1,0:T(8,128)(2,1)}), bf16[128,7632]{1,0:T(8,128)(2,1)}) %reduce-scatter.13.cloned.1.call-update) | async-done | bytes 1953808
  1677.2 4.0 copy.62
  1681.1 8.2 multiply_reduce_fusion.2
  1689.3 95.5 %all-reduce.9.cloned.1.call-done = bf16[256,12288]{1,0:T(8,128)(2,1)} async-done(((bf16[256,12288]{1,0:T(8,128)(2,1)}), bf16[256,12288]{1,0:T(8,128)(2,1)}) %all-reduce.9.cloned.1.call-update) | async-done | bytes 6291472 | tf_op jit(solution)/shard_map/psum | solution.py:261
  1784.8 2.6 abs_reduce_fusion.1
  1788.1 3.7 multiply_reduce_fusion.15
  1793.3 39.7 %all-reduce.4 = (f32[1]{0:T(128)}, f32[10]{0:T(128)S(1)}) all-reduce(f32[1]{0:T(128)} %bitcast.27, f32[10]{0:T(128)S(1)} %pad_maximum_fusion.4), channel_id=1, replica_groups=mesh['wide'=8,'narrow'=4] {'wide','narrow'}, use_global_device_ids=true, to_apply=%region_15.16 | all-reduce | flops 11 | bytes 88 | tf_op jit(solution)/shard_map/psum | solution.py:221
  1833.7 2.6 fusion.78
  1836.4 5.4 fusion.64
  1845.5 2.6 maximum_sqrt_fusion.1
  1848.7 5.1 multiply_subtract_fusion.1
  1854.7 5.8 multiply_subtract_fusion
  1860.6 27.7 %all-gather.16.cloned.1.call-done = bf16[256,12288]{1,0:T(8,128)(2,1)} async-done(((bf16[256,1536]{1,0:T(8,128)(2,1)}), bf16[256,12288]{1,0:T(8,128)(2,1)}) %all-gather.16.cloned.1.call-update) | async-done | bytes 6291472 | tf_op jit(solution)/shard_map/all_gather | solution.py:267
  1888.2 9.1 convert_element_type.227
  (272 shorter events, 39.0 us)
Async XLA Ops:
  7.2 3.8 copy-start.12
  7.2 94.6 %all-gather.10.cloned.1.call-start = ((), (), s32[]{:S(2)}) async-start(), calls=%async_computation.4 | async-start | bytes 17584128 | tf_op jit(solution)/shard_map/all_gather | solution.py:191
  10.9 138.9 %all-gather.12.cloned.1.call-start = ((), (), s32[]{:S(2)}) async-start(), calls=%async_computation.6 | async-start | bytes 7077888 | tf_op jit(solution)/shard_map/all_gather | solution.py:190
  12.0 218.6 %reduce-scatter.7.cloned.1.call-start = ((), (), s32[]{:S(2)}) async-start(), calls=%async_computation.5 | async-start | bytes 5242880 | tf_op jit(solution)/shard_map/reduce_scatter | solution.py:199
  124.4 25.5 %copy-start.64 = (s32[4,80]{1,0:T(4,128)S(1)}, s32[4,80]{1,0:T(4,128)}, u32[]{:S(2)}) copy-start(s32[4,80]{1,0:T(4,128)} %param.22) | copy-start | bytes 3844
  124.4 70.4 %copy-start.3 = (f32[528,1024]{1,0:T(8,128)S(1)}, f32[528,1024]{1,0:T(8,128)}, u32[]{:S(2)}) copy-start(f32[528,1024]{1,0:T(8,128)} %param.26) | copy-start | bytes 6488068
  124.4 71.0 %copy-start.65 = (s32[4,80]{1,0:T(4,128)S(1)}, s32[4,80]{1,0:T(4,128)}, u32[]{:S(2)}) copy-start(s32[4,80]{1,0:T(4,128)} %param.21) | copy-start | bytes 3844
  124.5 71.1 %copy-start.70 = (u32[32]{0:T(128)S(1)}, u32[32]{0:T(128)}, u32[]{:S(2)}) copy-start(u32[32]{0:T(128)} %constant.227) | copy-start | bytes 388
  124.5 72.3 %copy-start.67 = (s32[1,80]{1,0:T(1,128)S(1)}, s32[1,80]{1,0:T(1,128)}, u32[]{:S(2)}) copy-start(s32[1,80]{1,0:T(1,128)} %param.20) | copy-start | bytes 964
  124.5 74.2 %copy-start.29 = (s32[1,512]{1,0:T(1,128)S(1)}, s32[1,512]{1,0:T(1,128)}, u32[]{:S(2)}) copy-start(s32[1,512]{1,0:T(1,128)} %param.19) | copy-start | bytes 6148
  124.5 533.2 %all-gather.14.cloned.1.call-start = ((), (), s32[]{:S(2)}) async-start(), calls=%async_computation.7 | async-start | bytes 31457280 | tf_op jit(solution)/shard_map/all_gather | solution.py:193
  149.9 686.4 %reduce-scatter.9.cloned.1.call-start = ((), (), s32[]{:S(2)}) async-start(), calls=%async_computation.8 | async-start | bytes 1638400 | tf_op jit(solution)/shard_map/reduce_scatter | solution.py:225
  150.0 83.9 %copy-start.51 = (f32[320]{0:T(512)}, f32[320]{0:T(512)S(1)}, u32[]{:S(2)}) copy-start(f32[320]{0:T(512)S(1)} %convert_element_type.183) | copy-start | bytes 3844
  198.6 467.7 %copy-start.39 = (f32[1,1024]{1,0:T(1,128)}, f32[1,1024]{1,0:T(1,128)S(1)}, u32[]{:S(2)}) copy-start(f32[1,1024]{1,0:T(1,128)S(1)} %get-tuple-element.133) | copy-start | bytes 12292
  198.6 467.7 %copy-start.57 = (f32[1,1024]{1,0:T(1,128)}, f32[1,1024]{1,0:T(1,128)S(1)}, u32[]{:S(2)}) copy-start(f32[1,1024]{1,0:T(1,128)S(1)} %get-tuple-element.132) | copy-start | bytes 12292
  198.7 459.1 %copy-start.53 = (pred[512]{0:T(512)(128)(4,1)}, pred[512]{0:T(512)(128)(4,1)S(1)}, u32[]{:S(2)}) copy-start(pred[512]{0:T(512)(128)(4,1)S(1)} %compare_reduce_fusion) | copy-start | bytes 1540
  232.3 462.5 %copy-start.30 = (f32[512]{0:T(512)}, f32[512]{0:T(512)S(1)}, u32[]{:S(2)}) copy-start(f32[512]{0:T(512)S(1)} %broadcast_multiply_fusion.3) | copy-start | bytes 6148
  233.9 432.4 %copy-start.32 = (f32[512]{0:T(512)}, f32[512]{0:T(512)S(1)}, u32[]{:S(2)}) copy-start(f32[512]{0:T(512)S(1)} %multiply_reduce_fusion.13) | copy-start | bytes 6148
  234.0 432.4 %copy-start.44 = (f32[512]{0:T(512)}, f32[512]{0:T(512)S(1)}, u32[]{:S(2)}) copy-start(f32[512]{0:T(512)S(1)} %fusion.72) | copy-start | bytes 6148
  669.6 16.7 copy-start.1
  686.2 8.5 copy-start.6
  686.3 8.5 copy-start.40
  686.3 8.5 copy-start.45
  686.3 8.5 copy-start.58
  686.3 8.5 copy-start.61
  694.7 3.6 copy-start.69
  694.8 3.9 copy-start.34
  694.8 3.9 copy-start.37
  694.8 3.9 copy-start.55
  698.4 26.8 %copy-start.14 = (f32[512,1024]{1,0:T(8,128)}, f32[512,1024]{1,0:T(8,128)S(1)}, u32[]{:S(2)}) copy-start(f32[512,1024]{1,0:T(8,128)S(1)} %get-tuple-element.154) | copy-start | bytes 6291460
  698.7 26.4 %copy-start.47 = (f32[512]{0:T(512)}, f32[512]{0:T(512)S(1)}, u32[]{:S(2)}) copy-start(f32[512]{0:T(512)S(1)} %fusion.73) | copy-start | bytes 6148
  698.8 26.4 %copy-start.60 = (f32[1,1024]{1,0:T(1,128)S(1)}, f32[1,1024]{1,0:T(1,128)}, u32[]{:S(2)}) copy-start(f32[1,1024]{1,0:T(1,128)} %get-tuple-element.126) | copy-start | bytes 12292
  725.2 9.7 copy-start.71
  734.9 20.2 %copy-start.50 = (pred[7632]{0:T(1024)(128)(4,1)S(1)}, pred[7632]{0:T(1024)(128)(4,1)}, u32[]{:S(2)}) copy-start(pred[7632]{0:T(1024)(128)(4,1)} %broadcast_compare_fusion.1) | copy-start | bytes 22900
  755.1 11.4 copy-start.21
  766.8 24.7 %copy-start.52 = (f32[320]{0:T(512)S(1)}, f32[320]{0:T(512)}, u32[]{:S(2)}) copy-start(f32[320]{0:T(512)} %copy-done.51) | copy-start | bytes 3844
  792.7 14.0 copy-start.68
  806.7 200.1 %all-gather.18.cloned.1.call-start = ((), (), s32[]{:S(2)}) async-start(), calls=%async_computation.13 | async-start | bytes 5242880 | tf_op jit(solution)/shard_map/all_gather | solution.py:248
  843.4 14.4 copy-start.23
  843.4 14.4 copy-start.15
  843.4 14.4 copy-start.38
  843.4 14.4 copy-start.48
  857.8 9.8 copy-start.73
  870.6 6.3 copy-start.2
  913.8 3.4 copy-start.18
  914.4 9.0 copy-start.20
  917.1 6.4 copy-start.33
  927.1 495.2 %reduce-scatter.11.cloned.1.call-start = ((), (), s32[]{:S(2)}) async-start(), calls=%async_computation.9 | async-start | bytes 31457280 | tf_op jit(solution)/shard_map/reduce_scatter | solution.py:236
  931.0 4.5 copy-start.59
  935.5 8.1 copy-start.24
  935.6 8.1 copy-start.72
  943.6 6.9 copy-start.16
  943.6 6.9 copy-start.49
  943.7 6.9 copy-start.56
  943.7 6.9 copy-start.74
  950.5 7.3 copy-start.13
  974.8 6.0 copy-start.22
  974.8 590.0 %all-reduce.11.cloned.1.call-start = ((), (), s32[]{:S(2)}) async-start(), calls=%async_computation.11 | async-start | bytes 4325376 | tf_op jit(solution)/shard_map/psum | solution.py:285
  980.8 696.4 %reduce-scatter.13.cloned.1.call-start = ((), (), s32[]{:S(2)}) async-start(), calls=%async_computation.14 | async-start | bytes 17694720
  1083.2 701.7 %all-reduce.9.cloned.1.call-start = ((), (), s32[]{:S(2)}) async-start(), calls=%async_computation.10 | async-start | bytes 12582912 | tf_op jit(solution)/shard_map/psum | solution.py:261
  1451.8 113.0 %copy-start.4 = (f32[528,1024]{1,0:T(8,128)S(1)}, f32[528,1024]{1,0:T(8,128)}, u32[]{:S(2)}) copy-start(f32[528,1024]{1,0:T(8,128)} %param.26) | copy-start | bytes 6488068
  1451.8 436.4 %all-gather.16.cloned.1.call-start = ((), (), s32[]{:S(2)}) async-start(), calls=%async_computation.12 | async-start | bytes 7077888 | tf_op jit(solution)/shard_map/all_gather | solution.py:267
  1848.7 5.1 copy-start
  1848.7 6.0 copy-start.11
  (22 other events, 40.1 us)
Sparse Core Ops, SparseCore 0:
  11.1 90.7 all-gather.9
  104.3 45.5 all-gather.11
  152.7 77.7 reduce-scatter.6
  232.1 425.6 all-gather.13
  806.8 29.3 reduce-scatter.8
  927.3 79.5 all-gather.17
  1009.3 412.9 reduce-scatter.10
  1428.4 136.3 all-reduce.10
  1568.7 108.3 reduce-scatter.12
  1680.6 104.1 all-reduce.8
  1841.9 46.2 all-gather.15
where the time goes:
time: 1910 us; the launch traced here: 1900 us
  waiting for transfers between devices  1280 us (67%)
  other arithmetic  215 us (11%)
  matrix products  194 us (10%)
  blocking collectives  118 us (6%)
  local copies, waits for them, and re-layouts  73.3 us (4%)
    all_gather x1, waiting for transfers between devices, shards(): weights = lax.all_gather(layer_cols, 'narrow', axis=0, tiled=True)  424 us
    reduce_scatter x1, waiting for transfers between devices, shards(): lax.psum_scatter(weight_block((act, out, fin, dffn), (dqkv, dattn, dupper...  339 us
    psum x1, waiting for transfers between devices, shards(): small_grad, sums = lax.psum((small_grad, parts), ('wide', 'narrow'))  111 us
    unnamed x12, waiting for transfers between devices  106 us
    psum x1, waiting for transfers between devices, shards(): summed = lax.psum(sent.astype(jnp.bfloat16), 'wide').astype(jnp.float32)  95.5 us
    all_gather x1, waiting for transfers between devices, shards(): lax.all_gather(table.astype(jnp.bfloat16), 'wide', axis=1, tiled=True)  89.1 us
    psum x2, blocking collectives, shards(): lax.psum((jnp.sum(own_loss), jnp.sum(own_flags)), ('wide', 'narrow'))  83.8 us
    dot_general x5, matrix products, matmul(): return jnp.dot(left, right, preferred_element_type=jnp.float32)  66.8 us
  transfers between devices with their start and end apart: 11, of which 11 were waited for; matrix products, arithmetic and copies ran while one was open for 13% of the time, Pallas kernels for 0%

commit v1 on v0

--- a/solution.py
+++ b/solution.py
@@ -157,11 +157,102 @@
     )
 
 
-def weight_block(lefts, rights):
-    blocks = []
-    for left, right in zip(lefts, rights):
-        blocks.append(matmul_tn(left, right))
-    return jnp.concatenate(blocks, axis=1)
+def swap_pairs(size, bit):
+    return [(place, place ^ bit) for place in range(size)]
+
+
+def summed_over(value, axis):
+    size = lax.axis_size(axis)
+    if size & (size - 1):
+        return lax.psum(value, axis)
+    bit = 1
+    while bit < size:
+        value = value + lax.ppermute(value, axis, swap_pairs(size, bit))
+        bit *= 2
+    return value
+
+
+def worker_piece(left, right):
+    grad = matmul_tn(left, right).astype(jnp.bfloat16)
+    return lax.psum_scatter(grad, "narrow", scatter_dimension=0, tiled=True).astype(jnp.float32)
+
+
+def paired_piece(left, right):
+    n_wide, n_narrow = lax.axis_size("wide"), lax.axis_size("narrow")
+    core = lax.axis_index("wide") % 2
+    narrow_me = lax.axis_index("narrow")
+    pair, side = narrow_me // 2, narrow_me % 2
+    rows = D // n_narrow
+
+    def block(core_of, side_of):
+        part = lax.dynamic_slice_in_dim(left, (2 * core_of + side_of) * rows, rows, 1)
+        return matmul_tn(part, right)
+
+    cores = swap_pairs(n_wide, 1)
+    sides = swap_pairs(n_narrow, 1)
+    moves = []
+    for wide in range(n_wide):
+        for narrow in range(n_narrow):
+            if narrow // 2 != wide % 2:
+                target_wide = wide - wide % 2 + narrow // 2
+                target_narrow = 2 * (wide % 2) + narrow % 2
+                moves.append((wide * n_narrow + narrow, target_wide * n_narrow + target_narrow))
+    away = lax.ppermute(block(1 - core, 1 - side).astype(jnp.bfloat16), "wide", cores)
+    near = lax.ppermute(block(1 - core, side).astype(jnp.bfloat16), "wide", cores)
+    away = (block(core, 1 - side) + away.astype(jnp.float32)).astype(jnp.bfloat16)
+    away = lax.ppermute(away, "narrow", sides)
+    total = block(core, side) + near.astype(jnp.float32) + away.astype(jnp.float32)
+    total = total.astype(jnp.bfloat16)
+    moved = lax.ppermute(total, ("wide", "narrow"), moves)
+    return jnp.where(pair == core, total, moved).astype(jnp.float32)
+
+
+def hosted_rows(token_ids, mlm_labels, mlm_valid, doc_ids, mlm_pos):
+    n_wide, n_narrow = lax.axis_size("wide"), lax.axis_size("narrow")
+    core = lax.axis_index("wide") % 2
+    packed = jnp.concatenate([token_ids, mlm_labels, mlm_valid], axis=1)
+    other = lax.ppermute(packed, "wide", swap_pairs(n_wide, 1))
+    both = jnp.where(core == 0, jnp.stack([packed, other]), jnp.stack([other, packed]))
+    both = both.reshape(2, 2, 2, packed.shape[1])
+    column = lax.dynamic_index_in_dim(both, core, 2, keepdims=False).reshape(4, packed.shape[1])
+    moves = []
+    for wide in range(n_wide):
+        for row in range(n_narrow):
+            target_wide = wide - wide % 2 + row % 2
+            target_narrow = 2 * (wide % 2) + row // 2
+            moves.append((wide * n_narrow + row, target_wide * n_narrow + target_narrow))
+    own = lax.ppermute(jnp.concatenate([doc_ids, mlm_pos], axis=1), ("wide", "narrow"), moves)
+    return (
+        column[:, 0:L],
+        column[:, L : L + MPS],
+        column[:, L + MPS :],
+        own[:, 0:L],
+        own[:, L:],
+    )
+
+
+def scattered_sum(sent):
+    n_wide = lax.axis_size("wide")
+    wide_me = lax.axis_index("wide")
+    rows, cols = sent.shape
+    part = cols // n_wide
+    if n_wide != 8:
+        whole = lax.psum(sent.astype(jnp.bfloat16), "wide").astype(jnp.float32)
+        return lax.dynamic_slice_in_dim(whole, wide_me * part, part, 1)
+    core, x, y = wide_me % 2, wide_me // 2 % 2, wide_me // 4
+    blocks = sent.reshape(rows, 2, 2, 2, part)
+
+    def step(value, dim, place, bit):
+        give = lax.dynamic_index_in_dim(value, 1 - place, dim, keepdims=False).astype(jnp.bfloat16)
+        keep = lax.dynamic_index_in_dim(value, place, dim, keepdims=False)
+        take = lax.ppermute(give, "wide", swap_pairs(n_wide, bit))
+        return keep.astype(jnp.float32) + take.astype(jnp.float32)
+
+    blocks = step(blocks, 3, core, 1)
+    upper, lower = blocks[0 : rows // 2], blocks[rows // 2 :]
+    upper, lower = step(upper, 2, x, 2), step(lower, 1, y, 4)
+    upper, lower = step(upper, 1, y, 4), step(lower, 1, x, 2)
+    return jnp.concatenate([upper, lower], axis=0)
 
 
 def shards(
@@ -185,12 +276,17 @@
     n_wide = lax.axis_size("wide")
     narrow_me = lax.axis_index("narrow")
     wide_me = lax.axis_index("wide")
+    n_narrow = lax.axis_size("narrow")
     seqs = doc_ids.shape[0]
-    layer_cols, table_cols = (
-        lax.all_gather(layer.astype(jnp.bfloat16), "wide", axis=1, tiled=True),
-        lax.all_gather(table.astype(jnp.bfloat16), "wide", axis=1, tiled=True),
-    )
-    weights = lax.all_gather(layer_cols, "narrow", axis=0, tiled=True)
+    paired = n_wide % 2 == 0 and n_narrow == 4 and seqs == 1
+    count = summed_over(jnp.sum(mlm_valid.astype(jnp.float32)), "wide")
+    if paired:
+        token_ids, mlm_labels, mlm_valid, doc_ids, mlm_pos = hosted_rows(
+            token_ids, mlm_labels, mlm_valid, doc_ids, mlm_pos
+        )
+    table_cols = lax.all_gather(table.astype(jnp.bfloat16), "wide", axis=1, tiled=True)
+    layer_rows = lax.all_gather(layer.astype(jnp.bfloat16), "narrow", axis=0, tiled=True)
+    weights = lax.all_gather(layer_rows, "wide", axis=1, tiled=True)
     vshard = table_cols.shape[0]
     local_ids = token_ids - narrow_me * vshard
     inside = (local_ids >= 0) & (local_ids < vshard)
@@ -217,8 +313,6 @@
     flags = mlm_valid.reshape(-1).astype(jnp.float32)
     own = seqs * MPS
     own_loss = lax.dynamic_slice_in_dim(flags * (lse - target), narrow_me * own, own)
-    own_flags = lax.dynamic_slice_in_dim(flags, narrow_me * own, own)
-    loss_sum, count = lax.psum((jnp.sum(own_loss), jnp.sum(own_flags)), ("wide", "narrow"))
     dlogit = (
         (jnp.exp(logits - lse[:, None]) - hit.astype(jnp.float32)) * (flags / count)[:, None]
     ).astype(jnp.bfloat16)
@@ -233,12 +327,10 @@
         dhtwo.reshape(seqs * L, D), kept, doc_ids, small, weights
     )
     act, dqkv, out, dattn, fin, dupper, dffn, gated = saved
-    worker_grad = lax.psum_scatter(
-        weight_block((act, out, fin, dffn), (dqkv, dattn, dupper, gated)).astype(jnp.bfloat16),
-        "narrow",
-        scatter_dimension=0,
-        tiled=True,
-    ).astype(jnp.float32)
+    piece = paired_piece if paired else worker_piece
+    worker_grad = jnp.concatenate(
+        [piece(act, dqkv), piece(out, dattn), piece(fin, dupper), piece(dffn, gated)], axis=1
+    )
     dembed_rows = dembed.reshape(seqs, L, D)
     seg_even = jnp.sum(jnp.where(even_doc, dembed_rows, 0.0), axis=(0, 1))
     seg_odd = jnp.sum(jnp.where(even_doc, 0.0, dembed_rows), axis=(0, 1))
@@ -258,8 +350,7 @@
     sent = scale * jnp.tanh(span / scale)
     new_worker = (span - sent)[None]
     part_cols = layer.shape[1]
-    summed = lax.psum(sent.astype(jnp.bfloat16), "wide").astype(jnp.float32)
-    mixed = lax.dynamic_slice_in_dim(summed, wide_me * part_cols, part_cols, 1) / n_wide
+    mixed = scattered_sum(sent) / n_wide
     server_in = mixed + server_err
     sscale = jnp.mean(jnp.abs(server_in)) + MAG_EPS
     server_out = sscale * jnp.tanh(server_in / sscale)
@@ -280,9 +371,17 @@
     table_mom = BETA * table_m + (1.0 - BETA) * table_grad
     table_upd = table_mom / (jnp.sqrt(table_v) + OPT_EPS) + DECAY * table
     parts = jnp.concatenate(
-        [wsq, usq, jnp.sum(table * table)[None], jnp.sum(table_upd * table_upd)[None]]
-    )
-    small_grad, sums = lax.psum((small_grad, parts), ("wide", "narrow"))
+        [
+            wsq,
+            usq,
+            jnp.sum(table * table)[None],
+            jnp.sum(table_upd * table_upd)[None],
+            jnp.sum(own_loss)[None],
+        ]
+    )
+    small_grad = lax.psum(small_grad, ("wide", "narrow"))
+    sums = summed_over(summed_over(parts, "wide"), "narrow")
+    loss_sum = sums[10]
     small_mom = BETA * small_m + (1.0 - BETA) * small_grad
     small_upd = small_mom / (jnp.sqrt(small_v) + OPT_EPS) + DECAY * small
     wnorm = jnp.sqrt(jnp.concatenate([sums[0:4], sums[8:9], jnp.sum(small * small)[None]]))

time: 1910 us -> 1420 us (0.74)
  waiting for transfers between devices: 1280 us -> 745 us
  blocking collectives: 118 us -> 36 us
  starting transfers between devices: 0.66 us -> 75.8 us
  local copies, waits for them, and re-layouts: 73.3 us -> 111 us
    reduce_scatter x1 -> x0, waiting for transfers between devices: 339 us -> none  [shards(): lax.psum_scatter(weight_block((act, out, fin, dffn), (dqkv, dattn, dupper...]
    all_gather x2, waiting for transfers between devices: 449 us -> 167 us  [the longest x1 124 us: shards(): weights = lax.all_gather(layer_rows, 'wide', axis=1, tiled=True)]
    ppermute x0 -> x31, waiting for transfers between devices: none -> 252 us  [the longest x4 218 us: paired_piece(): away = lax.ppermute(away, 'narrow', sides)]
    psum x2 -> x1, waiting for transfers between devices: 207 us -> 1.63 us  [shards(): small_grad = lax.psum(small_grad, ('wide', 'narrow'))]
    psum x2 -> x0, blocking collectives: 83.8 us -> none  [shards(): lax.psum((jnp.sum(own_loss), jnp.sum(own_flags)), ('wide', 'narrow'))]
    ppermute x0 -> x31, starting transfers between devices: none -> 75.2 us  [the longest x5 51.3 us: step(): take = lax.ppermute(give, 'wide', swap_pairs(n_wide, bit))]
    reduce_scatter x1, waiting for transfers between devices: 31.1 us -> 63.2 us  [shards(): lax.psum_scatter(picked.astype(jnp.bfloat16), 'narrow', scatter_dimension...]
    dot_general x5 -> x17, matrix products: 46 us -> 58.6 us  [matmul_tn(): lax.dot_general(left, right, (((0,), (0,)), ((), ())), preferred_element_...]
  transfers between devices with their start and end apart: 11 -> 40, of which waited for: 11 -> 22; matrix products, arithmetic and copies ran while one was open for 13% -> 20% of each run, Pallas kernels for 0% -> 0%
where the time goes in v1:
time: 1420 us; the launch traced here: 1410 us
  waiting for transfers between devices  745 us (52%)
  other arithmetic  211 us (15%)
  matrix products  209 us (15%)
  local copies, waits for them, and re-layouts  111 us (8%)
  starting transfers between devices  75.8 us (5%)
  blocking collectives  36 us (3%)
  between operations  21.5 us (2%)
    ppermute x4, waiting for transfers between devices, paired_piece(): away = lax.ppermute(away, 'narrow', sides)  218 us
    all_gather x1, waiting for transfers between devices, shards(): weights = lax.all_gather(layer_rows, 'wide', axis=1, tiled=True)  124 us
    unnamed x10, waiting for transfers between devices  104 us
    all_gather x1, waiting for transfers between devices, shards(): lax.all_gather(table.astype(jnp.bfloat16), 'wide', axis=1, tiled=True)  87.7 us
    dot_general x5, matrix products, matmul(): return jnp.dot(left, right, preferred_element_type=jnp.float32)  65.2 us
    reduce_scatter x1, waiting for transfers between devices, shards(): lax.psum_scatter(picked.astype(jnp.bfloat16), 'narrow', scatter_dimension...  63.2 us
    dot_general x17, matrix products, matmul_tn(): lax.dot_general(left, right, (((0,), (0,)), ((), ())), preferred_element_...  58.6 us
    ppermute x5, starting transfers between devices, step(): take = lax.ppermute(give, 'wide', swap_pairs(n_wide, bit))  51.3 us
  transfers between devices with their start and end apart: 40, of which 22 were waited for; matrix products, arithmetic and copies ran while one was open for 20% of the time, Pallas kernels for 0%

profile of v1, /device:TPU:0, one launch (start us, length us, event | category | flops | bytes accessed | tf_op | source)
XLA Modules:
  0.0 1409.5 jit_solution(2074626856499721207)
XLA Ops:
  7.2 3.7 convert_element_type.296
  14.2 87.7 %all-gather.10.cloned.1.call-done = bf16[7632,1024]{1,0:T(8,128)(2,1)} async-done(((bf16[7632,128]{1,0:T(8,128)(2,1)}), bf16[7632,1024]{1,0:T(8,128)(2,1)}) %all-gather.10.cloned.1.call-update) | async-done | bytes 15630352 | tf_op jit(solution)/shard_map/all_gather | solution.py:287
  101.8 18.4 %gather_fusion = bf16[2048,1024]{1,0:T(8,128)(2,1)} fusion(bf16[7632,1024]{1,0:T(8,128)(2,1)} %all-gather.10.cloned.1.call-done, s32[2048]{0:T(1024)S(1)} %broadcast_clamp_fusion), kind=kCustom, calls=%fused_computation | custom fusion | bytes 8396800 | tf_op jit(solution)/shard_map/jit(_take)/gather | solution.py:293
  120.2 4.2 select_convert_fusion
  124.5 43.0 %all-gather.12.cloned.1.call-done = bf16[1024,1536]{1,0:T(8,128)(2,1)} async-done(((bf16[256,1536]{1,0:T(8,128)(2,1)}), bf16[1024,1536]{1,0:T(8,128)(2,1)}) %all-gather.12.cloned.1.call-update) | async-done | bytes 3145744 | tf_op jit(solution)/shard_map/all_gather | solution.py:288
  177.7 2.8 collective-permute-start.4
  182.7 63.2 %reduce-scatter.6.cloned.1.call-done = bf16[1,512,1024]{2,1,0:T(8,128)(2,1)} async-done(((bf16[4,512,1024]{2,1,0:T(8,128)(2,1)}), bf16[1,512,1024]{2,1,0:T(8,128)(2,1)}) %reduce-scatter.6.cloned.1.call-update) | async-done | bytes 1048592 | tf_op jit(solution)/shard_map/reduce_scatter | solution.py:295
  249.8 123.8 %all-gather.14.cloned.1.call-done = bf16[1024,12288]{1,0:T(8,128)(2,1)} async-done(((bf16[1024,1536]{1,0:T(8,128)(2,1)}), bf16[1024,12288]{1,0:T(8,128)(2,1)}) %all-gather.14.cloned.1.call-update) | async-done | bytes 25165840 | tf_op jit(solution)/shard_map/all_gather | solution.py:289
  373.6 7.5 add_convert_fusion.1
  381.1 4.8 copy.53
  386.0 9.9 fusion
  395.9 9.2 exponential_reduce_fusion
  405.1 10.2 convolution_convert_fusion.6
  415.4 3.5 fusion.146
  420.1 26.0 %multiply_convert_fusion.1 = (bf16[512,4096]{1,0:T(8,128)(2,1)S(1)}, f32[512,4096]{1,0:T(8,128)}, f32[512,4096]{1,0:T(8,128)}) fusion(f32[4096]{0:T(1024)S(1)} %bitcast.237, bf16[512,1024]{1,0:T(8,128)(2,1)S(1)} %fusion.37, bf16[1024,12288]{1,0:T(8,128)(2,1)} %all-gather.14.cloned.1.call-done), kind=kOutput, calls=%fused_computation.33 | convolution fusion | flops 4433379328 | bytes 30425088 | tf_op jit(solution)/shard_map/dot_general | solution.py:43
  446.2 9.2 fusion.147
  457.1 18.1 %all_gather.39 = bf16[320,1024]{1,0:T(8,128)(2,1)S(1)} all-gather(bf16[80,1024]{1,0:T(8,128)(2,1)S(1)} %select_convert_fusion.1), channel_id=1, replica_groups=mesh['wide'=8,'narrow'=4] {'narrow'}, dimensions={0}, use_global_device_ids=true | all-gather | bytes 819200 | tf_op jit(solution)/shard_map/all_gather | solution.py:303
  475.1 11.4 fusion.148
  486.8 6.3 fusion.1
  493.7 18.0 %all-reduce.4 = (f32[1280]{0:T(1024)S(1)}, f32[1280]{0:T(1024)S(1)}, f32[1280]{0:T(1024)S(1)}) all-reduce(f32[1280]{0:T(1024)S(1)} %dynamic-update-slice, f32[1280]{0:T(1024)S(1)} %dynamic-update-slice.1, f32[1280]{0:T(1024)S(1)} %dynamic-update-slice.2), channel_id=2, replica_groups=mesh['wide'=8,'narrow'=4] {'narrow'}, use_global_device_ids=true, to_apply=%add.1 | all-reduce | flops 3840 | bytes 30720
  513.0 14.0 fusion.131
  527.1 28.5 %reduce-scatter.8.cloned.1.call-done = f32[80,1024]{1,0:T(8,128)} async-done(((f32[320,1024]{1,0:T(8,128)}), f32[80,1024]{1,0:T(8,128)}) %reduce-scatter.8.cloned.1.call-update) | async-done | bytes 327696 | tf_op jit(solution)/shard_map/reduce_scatter | solution.py:319
  555.6 3.1 scatter_custom_fusion
  558.7 3.1 multiply_reduce_fusion.5
  569.2 14.1 %convert_reduce_fusion = (f32[4096]{0:T(1024)}, bf16[512,4096]{1,0:T(8,128)(2,1)S(1)}) fusion(f32[512,4096]{1,0:T(8,128)} %get-tuple-element.116, bf16[512,1024]{1,0:T(8,128)(2,1)S(1)} %get-tuple-element.92, bf16[1024,12288]{1,0:T(8,128)(2,1)} %all-gather.14.cloned.1.call-done, f32[512,4096]{1,0:T(8,128)} %get-tuple-element.159, f32[4096]{0:T(1024)S(1)} %bitcast.238), kind=kOutput, calls=%fused_computation.31 | convolution fusion | flops 4330614784 | bytes 30441472 | tf_op jit(solution)/shard_map/dot_general | solution.py:43
  588.8 7.7 multiply_reduce_fusion.6
  600.2 3.9 fusion.45
  606.6 10.3 convolution_bitcast_fusion
  616.9 12.1 multiply_reduce_fusion
  629.0 12.2 multiply_convert_fusion
  650.9 6.7 multiply_reduce_fusion.7
  662.0 3.3 fusion.64
  665.3 4.2 fusion.72
  681.1 4.4 add_convert_fusion.5
  685.5 146.9 %collective-permute-done.11 = bf16[256,1024]{1,0:T(8,128)(2,1)} collective-permute-done((bf16[256,1024]{1,0:T(8,128)(2,1)}, bf16[256,1024]{1,0:T(8,128)(2,1)}, u32[]{:S(2)}, u32[]{:S(2)}) %collective-permute-start.11) | collective-permute-done | bytes 524320 | tf_op jit(solution)/shard_map/ppermute | solution.py:203
  836.5 3.7 add_convert_fusion.6
  842.2 3.5 add_convert_fusion.2
  848.0 70.6 %collective-permute-done.15 = bf16[256,4096]{1,0:T(8,128)(2,1)} collective-permute-done((bf16[256,4096]{1,0:T(8,128)(2,1)S(1)}, bf16[256,4096]{1,0:T(8,128)(2,1)}, u32[]{:S(2)}, u32[]{:S(2)}) %collective-permute-start.15) | collective-permute-done | bytes 2097184 | tf_op jit(solution)/shard_map/ppermute | solution.py:203
  918.6 4.1 add_convert_fusion.4
  924.7 2.9 broadcast_select_fusion.2
  929.1 3.6 broadcast_select_fusion.1
  932.8 8.8 abs_reduce_fusion
  942.2 12.6 subtract_bitcast_fusion
  954.9 16.6 %reshape.677 = f32[256,2,2,2,1536]{4,3,2,1,0:T(2,128)} reshape(f32[256,12288]{1,0:T(8,128)} %get-tuple-element.122) | data formatting | bytes 25165824 | tf_op jit(solution)/shard_map/reshape | solution.py:243
  971.4 8.5 constant_dynamic-slice_fusion
  979.9 3.4 copy.77
  983.3 46.7 %collective-permute-start.21 = (bf16[256,2,2,1536]{3,0,2,1:T(8,128)(2,1)}, bf16[256,2,2,1536]{3,0,2,1:T(8,128)(2,1)}, u32[]{:S(2)}, u32[]{:S(2)}) collective-permute-start(bf16[256,2,2,1536]{3,0,2,1:T(8,128)(2,1)} %bitcast.189), channel_id=1, source_target_pairs={{0,4},{4,0},{8,12},{12,8},{16,20},{20,16},{24,28},{28,24},{1,5},{5... | collective-permute-start | bytes 9437192 | tf_op jit(solution)/shard_map/ppermute | solution.py:248
  1030.0 8.6 constant_dynamic-slice_fusion.1
  1038.6 3.9 bitcast_add_fusion.1
  1053.0 4.4 concatenate.80
  1057.7 12.5 collective-permute-done.24
  1076.7 6.9 collective-permute-done.25
  1087.2 3.9 multiply_reduce_fusion.14
  1091.3 19.9 %fusion.129 = f32[7632,1024]{1,0:T(8,128)} fusion(bf16[320,1024]{1,0:T(8,128)(2,1)} %copy-done.34, f32[320,7632]{1,0:T(8,128)} %get-tuple-element.163, f32[320]{0:T(512)S(1)} %copy-done.63, f32[320]{0:T(512)S(1)} %copy-done.61, s32[7632]{0:T(1024)S(1)} %copy-done.48, s32[320]{0:T(512)S(1)} %copy-done.57), kind=kOutput, calls=%fused_computation.292 | convolution fusion | flops 5016360960 | bytes 41719360 | tf_op jit(solution)/shard_map/dot_general | solution.py:47
  1111.2 38.8 %scatter_custom_fusion.1 = f32[7632,1024]{1,0:T(8,128)} fusion(f32[7632,1024]{1,0:T(8,128)} %fusion.129, s32[2048]{0:T(1024)S(1)} %bitcast.248, bf16[2048,1024]{1,0:T(8,128)(2,1)} %all-gather.18.cloned.1.call-done), kind=kCustom, calls=%fused_computation.29 | custom fusion | flops 4194304 | bytes 35454976 | tf_op jit(solution)/shard_map/scatter-add | solution.py:342
  1150.0 16.4 %convert_element_type.370 = bf16[7632,1024]{1,0:T(8,128)(2,1)} convert(f32[7632,1024]{1,0:T(8,128)} %scatter_custom_fusion.1) | non-fusion elementwise | flops 7815168 | bytes 46891008 | tf_op jit(solution)/shard_map/convert_element_type | solution.py:346
  1166.4 20.8 %copy.65 = bf16[7632,1024]{0,1:T(8,128)(2,1)} copy(bf16[7632,1024]{1,0:T(8,128)(2,1)} %convert_element_type.370) | data formatting | bytes 31260672
  1190.4 6.2 multiply_reduce_fusion.3
  1196.8 40.9 %all-gather.16.cloned.1.call-done = bf16[256,12288]{1,0:T(8,128)(2,1)} async-done(((bf16[256,1536]{1,0:T(8,128)(2,1)}), bf16[256,12288]{1,0:T(8,128)(2,1)}) %all-gather.16.cloned.1.call-update) | async-done | bytes 6291472 | tf_op jit(solution)/shard_map/all_gather | solution.py:358
  1237.7 9.1 convert_element_type.377
  1246.7 103.7 %reduce-scatter.10.cloned.1.call-done = bf16[128,7632]{1,0:T(8,128)(2,1)} async-done(((bf16[1024,7632]{1,0:T(8,128)(2,1)}), bf16[128,7632]{1,0:T(8,128)(2,1)}) %reduce-scatter.10.cloned.1.call-update) | async-done | bytes 1953808
  1350.4 4.0 copy.66
  1354.4 8.1 multiply_reduce_fusion.1
  1387.3 8.2 multiply_subtract_fusion
  (392 shorter events, 131.7 us)
Async XLA Ops:
  7.2 94.6 %all-gather.10.cloned.1.call-start = ((), (), s32[]{:S(2)}) async-start(), calls=%async_computation.3 | async-start | bytes 17584128 | tf_op jit(solution)/shard_map/all_gather | solution.py:287
  10.9 156.6 %all-gather.12.cloned.1.call-start = ((), (), s32[]{:S(2)}) async-start(), calls=%async_computation.5 | async-start | bytes 3932160 | tf_op jit(solution)/shard_map/all_gather | solution.py:288
  12.0 233.8 %reduce-scatter.6.cloned.1.call-start = ((), (), s32[]{:S(2)}) async-start(), calls=%async_computation.4 | async-start | bytes 5242880 | tf_op jit(solution)/shard_map/reduce_scatter | solution.py:295
  12.1 1.3 collective-permute-start
  124.4 43.8 %copy-start.75 = (s32[1,512]{1,0:T(1,128)S(1)}, s32[1,512]{1,0:T(1,128)}, u32[]{:S(2)}) copy-start(s32[1,512]{1,0:T(1,128)} %param.19) | copy-start | bytes 6148
  124.4 43.8 %copy-start.76 = (s32[1,80]{1,0:T(1,128)S(1)}, s32[1,80]{1,0:T(1,128)}, u32[]{:S(2)}) copy-start(s32[1,80]{1,0:T(1,128)} %param.20) | copy-start | bytes 964
  124.4 46.5 %copy-start.77 = (u32[32]{0:T(128)S(1)}, u32[32]{0:T(128)}, u32[]{:S(2)}) copy-start(u32[32]{0:T(128)} %constant.329) | copy-start | bytes 388
  124.4 249.2 %all-gather.14.cloned.1.call-start = ((), (), s32[]{:S(2)}) async-start(), calls=%async_computation.6 | async-start | bytes 28311552 | tf_op jit(solution)/shard_map/all_gather | solution.py:289
  167.5 388.1 %reduce-scatter.8.cloned.1.call-start = ((), (), s32[]{:S(2)}) async-start(), calls=%async_computation.7 | async-start | bytes 1638400 | tf_op jit(solution)/shard_map/reduce_scatter | solution.py:319
  168.2 3.9 collective-permute-start.2
  168.2 13.9 collective-permute-start.1
  170.0 245.4 %copy-start.51 = (f32[1,1024]{1,0:T(1,128)}, f32[1,1024]{1,0:T(1,128)S(1)}, u32[]{:S(2)}) copy-start(f32[1,1024]{1,0:T(1,128)S(1)} %get-tuple-element.134) | copy-start | bytes 12292
  170.0 342.9 %copy-start.47 = (s32[7632]{0:T(1024)}, s32[7632]{0:T(1024)S(1)}, u32[]{:S(2)}) copy-start(s32[7632]{0:T(1024)S(1)} %iota_add_fusion) | copy-start | bytes 91588
  173.4 3.7 collective-permute-start.3
  177.7 3.7 collective-permute-start.4
  182.2 66.4 %copy-start.72 = (pred[512]{0:T(512)(128)(4,1)}, pred[512]{0:T(512)(128)(4,1)S(1)}, u32[]{:S(2)}) copy-start(pred[512]{0:T(512)(128)(4,1)S(1)} %compare_reduce_fusion) | copy-start | bytes 1540
  182.4 222.7 %copy-start.23 = (pred[512,512]{0,1:T(8,128)(4,1)}, pred[512,512]{0,1:T(8,128)(4,1)S(1)}, u32[]{:S(2)}) copy-start(pred[512,512]{0,1:T(8,128)(4,1)S(1)} %broadcast_compare_fusion) | copy-start | bytes 786436
  182.7 330.3 %copy-start.56 = (s32[320]{0:T(512)}, s32[320]{0:T(512)S(1)}, u32[]{:S(2)}) copy-start(s32[320]{0:T(512)S(1)} %eq.97) | copy-start | bytes 3844
  248.2 167.2 %copy-start.5 = (f32[1,512,1024]{2,1,0:T(8,128)}, f32[1,512,1024]{2,1,0:T(8,128)S(1)}, u32[]{:S(2)}) copy-start(f32[1,512,1024]{2,1,0:T(8,128)S(1)} %get-tuple-element.118) | copy-start | bytes 6291460
  248.2 167.2 %copy-start.54 = (f32[512]{0:T(512)}, f32[512]{0:T(512)S(1)}, u32[]{:S(2)}) copy-start(f32[512]{0:T(512)S(1)} %broadcast_multiply_fusion.3) | copy-start | bytes 6148
  248.6 166.8 %copy-start.58 = (f32[512]{0:T(512)}, f32[512]{0:T(512)S(1)}, u32[]{:S(2)}) copy-start(f32[512]{0:T(512)S(1)} %fusion.118) | copy-start | bytes 6148
  249.8 131.3 %copy-start.30 = (bf16[512,1024]{1,0:T(8,128)(2,1)}, bf16[512,1024]{1,0:T(8,128)(2,1)S(1)}, u32[]{:S(2)}) copy-start(bf16[512,1024]{1,0:T(8,128)(2,1)S(1)} %fusion.36) | copy-start | bytes 3145732
  418.9 27.3 %copy-start.9 = (f32[512,1024]{1,0:T(8,128)}, f32[512,1024]{1,0:T(8,128)S(1)}, u32[]{:S(2)}) copy-start(f32[512,1024]{1,0:T(8,128)S(1)} %get-tuple-element.158) | copy-start | bytes 6291460
  420.1 26.1 %copy-start.28 = (bf16[512,1024]{1,0:T(8,128)(2,1)}, bf16[512,1024]{1,0:T(8,128)(2,1)S(1)}, u32[]{:S(2)}) copy-start(bf16[512,1024]{1,0:T(8,128)(2,1)S(1)} %fusion.37) | copy-start | bytes 3145732
  527.0 584.2 %all-gather.18.cloned.1.call-start = ((), (), s32[]{:S(2)}) async-start(), calls=%async_computation.10 | async-start | bytes 5242880 | tf_op jit(solution)/shard_map/all_gather | solution.py:340
  569.2 14.1 %copy-start.29 = (bf16[512,1024]{1,0:T(8,128)(2,1)S(1)}, bf16[512,1024]{1,0:T(8,128)(2,1)}, u32[]{:S(2)}) copy-start(bf16[512,1024]{1,0:T(8,128)(2,1)} %copy-done.28) | copy-start | bytes 3145732
  649.8 22.3 %collective-permute-start.18 = (bf16[256,4096]{1,0:T(8,128)(2,1)S(1)}, bf16[256,4096]{1,0:T(8,128)(2,1)S(1)}, u32[]{:S(2)}, u32[]{:S(2)}) collective-permute-start(bf16[256,4096]{1,0:T(8,128)(2,1)S(1)} %copy-done.38), channel_id=1, source_target_pairs={{0,4},{4,0},{8,12},{12,8},{16,20},{20,16},{24,28},{28,24},{1,5},{5... | collective-permute-start | bytes 6291464 | tf_op jit(solution)/shard_map/ppermute | solution.py:200
  649.8 28.3 %collective-permute-start.14 = (bf16[256,4096]{1,0:T(8,128)(2,1)S(1)}, bf16[256,4096]{1,0:T(8,128)(2,1)S(1)}, u32[]{:S(2)}, u32[]{:S(2)}) collective-permute-start(bf16[256,4096]{1,0:T(8,128)(2,1)S(1)} %copy-done.37), channel_id=1, source_target_pairs={{0,4},{4,0},{8,12},{12,8},{16,20},{20,16},{24,28},{28,24},{1,5},{5... | collective-permute-start | bytes 6291464 | tf_op jit(solution)/shard_map/ppermute | solution.py:200
  650.3 24.5 %collective-permute-start.10 = (bf16[256,1024]{1,0:T(8,128)(2,1)S(1)}, bf16[256,1024]{1,0:T(8,128)(2,1)S(1)}, u32[]{:S(2)}, u32[]{:S(2)}) collective-permute-start(bf16[256,1024]{1,0:T(8,128)(2,1)S(1)} %copy-done.46), channel_id=1, source_target_pairs={{0,4},{4,0},{8,12},{12,8},{16,20},{20,16},{24,28},{28,24},{1,5},{5... | collective-permute-start | bytes 1572872 | tf_op jit(solution)/shard_map/ppermute | solution.py:200
  650.4 24.5 %collective-permute-start.9 = (bf16[256,1024]{1,0:T(8,128)(2,1)S(1)}, bf16[256,1024]{1,0:T(8,128)(2,1)S(1)}, u32[]{:S(2)}, u32[]{:S(2)}) collective-permute-start(bf16[256,1024]{1,0:T(8,128)(2,1)S(1)} %copy-done.45), channel_id=1, source_target_pairs={{0,4},{4,0},{8,12},{12,8},{16,20},{20,16},{24,28},{28,24},{1,5},{5... | collective-permute-start | bytes 1572872 | tf_op jit(solution)/shard_map/ppermute | solution.py:201
  650.8 18.7 %collective-permute-start.6 = (bf16[256,3072]{1,0:T(8,128)(2,1)S(1)}, bf16[256,3072]{1,0:T(8,128)(2,1)S(1)}, u32[]{:S(2)}, u32[]{:S(2)}) collective-permute-start(bf16[256,3072]{1,0:T(8,128)(2,1)S(1)} %convolution_convert_fusion.4), channel_id=1, source_target_pairs={{0,4},{4,0},{8,12},{12,8},{16,20},{20,16},{24,28},{28,24},{1,5},{5... | collective-permute-start | bytes 4718600 | tf_op jit(solution)/shard_map/ppermute | solution.py:200
  669.5 162.9 %collective-permute-start.5 = (bf16[256,3072]{1,0:T(8,128)(2,1)}, bf16[256,3072]{1,0:T(8,128)(2,1)}, u32[]{:S(2)}, u32[]{:S(2)}) collective-permute-start(bf16[256,3072]{1,0:T(8,128)(2,1)} %convolution_convert_fusion.5), channel_id=1, source_target_pairs={{0,4},{4,0},{8,12},{12,8},{16,20},{20,16},{24,28},{28,24},{1,5},{5... | collective-permute-start | bytes 4718600 | tf_op jit(solution)/shard_map/ppermute | solution.py:201
  672.1 162.7 %collective-permute-start.7 = (bf16[256,3072]{1,0:T(8,128)(2,1)}, bf16[256,3072]{1,0:T(8,128)(2,1)}, u32[]{:S(2)}, u32[]{:S(2)}) collective-permute-start(bf16[256,3072]{1,0:T(8,128)(2,1)} %add_convert_fusion.7), channel_id=1, source_target_pairs={{0,1},{1,0},{2,3},{3,2},{4,5},{5,4},{6,7},{7,6},{8,9},{9,8},{10,11... | collective-permute-start | bytes 4718600 | tf_op jit(solution)/shard_map/ppermute | solution.py:203
  674.8 165.4 %collective-permute-start.17 = (bf16[256,4096]{1,0:T(8,128)(2,1)}, bf16[256,4096]{1,0:T(8,128)(2,1)}, u32[]{:S(2)}, u32[]{:S(2)}) collective-permute-start(bf16[256,4096]{1,0:T(8,128)(2,1)} %convolution_convert_fusion.1), channel_id=1, source_target_pairs={{0,4},{4,0},{8,12},{12,8},{16,20},{20,16},{24,28},{28,24},{1,5},{5... | collective-permute-start | bytes 6291464 | tf_op jit(solution)/shard_map/ppermute | solution.py:201
  674.9 167.3 %collective-permute-start.19 = (bf16[256,4096]{1,0:T(8,128)(2,1)}, bf16[256,4096]{1,0:T(8,128)(2,1)}, u32[]{:S(2)}, u32[]{:S(2)}) collective-permute-start(bf16[256,4096]{1,0:T(8,128)(2,1)} %add_convert_fusion.3), channel_id=1, source_target_pairs={{0,1},{1,0},{2,3},{3,2},{4,5},{5,4},{6,7},{7,6},{8,9},{9,8},{10,11... | collective-permute-start | bytes 6291464 | tf_op jit(solution)/shard_map/ppermute | solution.py:203
  678.2 154.3 %collective-permute-start.11 = (bf16[256,1024]{1,0:T(8,128)(2,1)}, bf16[256,1024]{1,0:T(8,128)(2,1)}, u32[]{:S(2)}, u32[]{:S(2)}) collective-permute-start(bf16[256,1024]{1,0:T(8,128)(2,1)} %add_convert_fusion.11), channel_id=1, source_target_pairs={{0,1},{1,0},{2,3},{3,2},{4,5},{5,4},{6,7},{7,6},{8,9},{9,8},{10,11... | collective-permute-start | bytes 1572872 | tf_op jit(solution)/shard_map/ppermute | solution.py:203
  681.0 151.8 %copy-start.27 = (f32[256,1024]{1,0:T(8,128)S(1)}, f32[256,1024]{1,0:T(8,128)}, u32[]{:S(2)}) copy-start(f32[256,1024]{1,0:T(8,128)} %fusion.80) | copy-start | bytes 3145732
  681.0 509.4 %all-reduce.7.cloned.1.call-start = ((), (), s32[]{:S(2)}) async-start(), calls=%async_computation.8 | async-start | bytes 4325376 | tf_op jit(solution)/shard_map/psum | solution.py:382
  681.1 151.4 %copy-start.36 = (bf16[256,4096]{1,0:T(8,128)(2,1)S(1)}, bf16[256,4096]{1,0:T(8,128)(2,1)}, u32[]{:S(2)}) copy-start(bf16[256,4096]{1,0:T(8,128)(2,1)} %convolution_convert_fusion.3) | copy-start | bytes 6291460
  681.1 151.7 %copy-start.44 = (bf16[256,1024]{1,0:T(8,128)(2,1)S(1)}, bf16[256,1024]{1,0:T(8,128)(2,1)}, u32[]{:S(2)}) copy-start(bf16[256,1024]{1,0:T(8,128)(2,1)} %copy-done.43) | copy-start | bytes 1572868
  681.1 155.4 %copy-start.17 = (f32[256,3072]{1,0:T(8,128)S(1)}, f32[256,3072]{1,0:T(8,128)}, u32[]{:S(2)}) copy-start(f32[256,3072]{1,0:T(8,128)} %fusion.88) | copy-start | bytes 9437188
  832.4 15.6 %collective-permute-start.13 = (bf16[256,4096]{1,0:T(8,128)(2,1)S(1)}, bf16[256,4096]{1,0:T(8,128)(2,1)S(1)}, u32[]{:S(2)}, u32[]{:S(2)}) collective-permute-start(bf16[256,4096]{1,0:T(8,128)(2,1)S(1)} %copy-done.36), channel_id=1, source_target_pairs={{0,4},{4,0},{8,12},{12,8},{16,20},{20,16},{24,28},{28,24},{1,5},{5... | collective-permute-start | bytes 6291464 | tf_op jit(solution)/shard_map/ppermute | solution.py:201
  832.4 86.2 %collective-permute-start.15 = (bf16[256,4096]{1,0:T(8,128)(2,1)S(1)}, bf16[256,4096]{1,0:T(8,128)(2,1)}, u32[]{:S(2)}, u32[]{:S(2)}) collective-permute-start(bf16[256,4096]{1,0:T(8,128)(2,1)S(1)} %add_convert_fusion.5), channel_id=1, source_target_pairs={{0,1},{1,0},{2,3},{3,2},{4,5},{5,4},{6,7},{7,6},{8,9},{9,8},{10,11... | collective-permute-start | bytes 6291464 | tf_op jit(solution)/shard_map/ppermute | solution.py:203
  834.9 88.6 %collective-permute-start.12 = (bf16[256,1024]{1,0:T(8,128)(2,1)}, bf16[256,1024]{1,0:T(8,128)(2,1)}, u32[]{:S(2)}, u32[]{:S(2)}) collective-permute-start(bf16[256,1024]{1,0:T(8,128)(2,1)} %add_convert_fusion.10), channel_id=1, source_target_pairs={{2,4},{3,5},{4,2},{5,3},{10,12},{11,13},{12,10},{13,11},{18,20},{1... | collective-permute-start | bytes 1572872 | tf_op jit(solution)/shard_map/ppermute | solution.py:206
  840.2 78.4 %copy-start.12 = (f32[256,4096]{1,0:T(8,128)S(1)}, f32[256,4096]{1,0:T(8,128)}, u32[]{:S(2)}) copy-start(f32[256,4096]{1,0:T(8,128)} %fusion.72) | copy-start | bytes 12582916
  840.2 84.5 %collective-permute-start.8 = (bf16[256,3072]{1,0:T(8,128)(2,1)}, bf16[256,3072]{1,0:T(8,128)(2,1)}, u32[]{:S(2)}, u32[]{:S(2)}) collective-permute-start(bf16[256,3072]{1,0:T(8,128)(2,1)} %add_convert_fusion.6), channel_id=1, source_target_pairs={{2,4},{3,5},{4,2},{5,3},{10,12},{11,13},{12,10},{13,11},{18,20},{1... | collective-permute-start | bytes 4718600 | tf_op jit(solution)/shard_map/ppermute | solution.py:206
  842.2 90.5 %slice-start.3 = ((s8[12582912]{0:T(1024)(128)(4,1)}), s8[4194304]{0:T(1024)(128)(4,1)S(1)}, s32[]{:S(2)}) async-start(s8[12582912]{0:T(1024)(128)(4,1)} %bitcast.206), calls=%async_computation.15 | async-start | bytes 8388608
  845.7 87.0 %slice-start.4 = ((s8[12582912]{0:T(1024)(128)(4,1)}), s8[4194304]{0:T(1024)(128)(4,1)S(1)}, s32[]{:S(2)}) async-start(s8[12582912]{0:T(1024)(128)(4,1)} %bitcast.206), calls=%async_computation.16 | async-start | bytes 8388608
  845.7 81.9 %collective-permute-start.20 = (bf16[256,4096]{1,0:T(8,128)(2,1)S(1)}, bf16[256,4096]{1,0:T(8,128)(2,1)}, u32[]{:S(2)}, u32[]{:S(2)}) collective-permute-start(bf16[256,4096]{1,0:T(8,128)(2,1)S(1)} %add_convert_fusion.2), channel_id=1, source_target_pairs={{2,4},{3,5},{4,2},{5,3},{10,12},{11,13},{12,10},{13,11},{18,20},{1... | collective-permute-start | bytes 6291464 | tf_op jit(solution)/shard_map/ppermute | solution.py:206
  918.6 14.1 %slice-start.1 = ((s8[12582912]{0:T(1024)(128)(4,1)}), s8[4194304]{0:T(1024)(128)(4,1)S(1)}, s32[]{:S(2)}) async-start(s8[12582912]{0:T(1024)(128)(4,1)} %bitcast.204), calls=%async_computation.13 | async-start | bytes 8388608
  922.7 6.4 collective-permute-start.16
  983.3 55.3 %collective-permute-start.21 = (bf16[256,2,2,1536]{3,0,2,1:T(8,128)(2,1)}, bf16[256,2,2,1536]{3,0,2,1:T(8,128)(2,1)}, u32[]{:S(2)}, u32[]{:S(2)}) collective-permute-start(bf16[256,2,2,1536]{3,0,2,1:T(8,128)(2,1)} %bitcast.189), channel_id=1, source_target_pairs={{0,4},{4,0},{8,12},{12,8},{16,20},{20,16},{24,28},{28,24},{1,5},{5... | collective-permute-start | bytes 9437192 | tf_op jit(solution)/shard_map/ppermute | solution.py:248
  1047.5 22.7 %collective-permute-start.24 = (bf16[128,2,1536]{2,0,1:T(8,128)(2,1)}, bf16[128,2,1536]{2,0,1:T(8,128)(2,1)}, u32[]{:S(2)}, u32[]{:S(2)}) collective-permute-start(bf16[128,2,1536]{2,0,1:T(8,128)(2,1)} %fusion.55), channel_id=1, source_target_pairs={{0,16},{4,20},{8,24},{12,28},{16,0},{20,4},{24,8},{28,12},{1,17},{... | collective-permute-start | bytes 2359304 | tf_op jit(solution)/shard_map/ppermute | solution.py:248
  1051.3 23.9 %collective-permute-start.22 = (bf16[128,2,1536]{2,0,1:T(8,128)(2,1)}, bf16[128,2,1536]{2,0,1:T(8,128)(2,1)}, u32[]{:S(2)}, u32[]{:S(2)}) collective-permute-start(bf16[128,2,1536]{2,0,1:T(8,128)(2,1)} %fusion.54), channel_id=1, source_target_pairs={{0,8},{4,12},{8,0},{12,4},{16,24},{20,28},{24,16},{28,20},{1,9},{5... | collective-permute-start | bytes 2359304 | tf_op jit(solution)/shard_map/ppermute | solution.py:248
  1057.4 17.9 %copy-start.18 = (f32[128,2,2,1536]{3,0,2,1:T(8,128)S(1)}, f32[128,2,2,1536]{3,0,2,1:T(8,128)}, u32[]{:S(2)}) copy-start(f32[128,2,2,1536]{3,0,2,1:T(8,128)} %get-tuple-element.123) | copy-start | bytes 9437188
  1057.4 180.2 %all-gather.16.cloned.1.call-start = ((), (), s32[]{:S(2)}) async-start(), calls=%async_computation.9 | async-start | bytes 7077888 | tf_op jit(solution)/shard_map/all_gather | solution.py:358
  1072.1 11.5 collective-permute-start.25
  1076.6 8.6 collective-permute-start.23
  1091.1 259.3 %reduce-scatter.10.cloned.1.call-start = ((), (), s32[]{:S(2)}) async-start(), calls=%async_computation.11 | async-start | bytes 17694720
  1364.5 1.1 collective-permute-start.26
  1365.6 3.5 collective-permute-start.27
  1369.2 3.5 collective-permute-start.28
  1372.7 3.5 collective-permute-start.29
  1376.3 4.4 collective-permute-start.30
  (60 other events, 339.9 us)
Sparse Core Ops, SparseCore 0:
  11.1 90.7 all-gather.9
  104.0 63.4 all-gather.11
  170.4 75.4 reduce-scatter.5
  247.7 125.8 all-gather.13
  527.1 28.4 reduce-scatter.7
  681.1 143.8 all-gather.17
  1057.5 132.8 all-reduce.6
  1192.9 44.7 all-gather.15
  1241.2 109.1 reduce-scatter.9

commit v2 on v1

--- a/solution.py
+++ b/solution.py
@@ -103,18 +103,23 @@
     _, pull = jax.vjp(norm_rows, rtwo, small[base + 4], small[base + 5])
     drtwo, dgain_two, dshift_two = pull(dhtwo)
     dffn = drtwo.astype(jnp.bfloat16)
+    down = WorkerPiece(dffn, gated)
     dgated = matmul(dffn, weights[:, 4 * D + FF :])
     _, pull = jax.vjp(gelu_exact, upper)
     dupper = pull(dgated)[0].astype(jnp.bfloat16)
+    dupper, _ = after(dupper, *down.waits())
+    down.across()
+    up = WorkerPiece(fin, dupper)
     dhone = drtwo + matmul_nt(dupper, weights[:, 4 * D : 4 * D + FF])
     _, pull = jax.vjp(norm_rows, rone, small[base + 2], small[base + 3])
     drone, dgain_one, dshift_one = pull(dhone)
     dattn = drone.astype(jnp.bfloat16)
-    dout = (
-        matmul_nt(dattn, weights[:, 3 * D : 4 * D])
-        .astype(jnp.bfloat16)
-        .reshape(seqs, L, HEADS, HEAD)
-    )
+    attn = WorkerPiece(out, dattn)
+    dout = matmul_nt(dattn, weights[:, 3 * D : 4 * D]).astype(jnp.bfloat16)
+    dout, _ = after(dout, *up.waits(), *attn.waits())
+    up.across()
+    attn.across()
+    dout = dout.reshape(seqs, L, HEADS, HEAD)
     heads = qkv.reshape(seqs, L, 3, HEADS, HEAD)
     prob = jnp.exp(score_block(heads, docs) - lse)
     dvalue = jnp.einsum(
@@ -122,6 +127,8 @@
     )
     dprob = jnp.einsum("sqhd,skhd->shqk", dout, heads[:, :, 2], preferred_element_type=jnp.float32)
     dscore = (prob * (dprob - jnp.sum(prob * dprob, axis=-1, keepdims=True))).astype(jnp.bfloat16)
+    dscore, _ = after(dscore, *down.waits_across())
+    grad_down = down.finish()
     dquery = (
         jnp.einsum("shqk,skhd->sqhd", dscore, heads[:, :, 1], preferred_element_type=jnp.float32)
         * 0.125
@@ -131,9 +138,15 @@
         * 0.125
     )
     dqkv = jnp.stack([dquery, dkey, dvalue], axis=2).reshape(seqs * L, 3 * D).astype(jnp.bfloat16)
+    qkv_piece = WorkerPiece(act, dqkv)
     dxzero = drone + matmul_nt(dqkv, weights[:, 0 : 3 * D])
     _, pull = jax.vjp(norm_rows, embedded, small[base], small[base + 1])
     dembed, dgain_emb, dshift_emb = pull(dxzero)
+    dembed, _ = after(dembed, *qkv_piece.waits(), *attn.waits_across())
+    qkv_piece.across()
+    grads = jnp.concatenate(
+        [qkv_piece.finish(), attn.finish(), up.finish(), grad_down], axis=1
+    )
     bias_qkv = jnp.sum(dqkv, axis=0, dtype=jnp.float32)
     vectors = jnp.stack(
         [
@@ -150,15 +163,23 @@
         ]
     )
     bias_up = jnp.sum(dupper, axis=0, dtype=jnp.float32).reshape(FF // D, D)
-    return (
-        dembed,
-        jnp.concatenate([vectors, bias_up], axis=0),
-        (act, dqkv, out, dattn, fin, dupper, dffn, gated),
-    )
+    return (dembed, jnp.concatenate([vectors, bias_up], axis=0), grads)
+
+
+def paired_mesh():
+    return lax.axis_size("wide") == 8 and lax.axis_size("narrow") == 4
+
+
+def after(values, *awaited):
+    return lax.optimization_barrier((values, awaited))
 
 
 def swap_pairs(size, bit):
     return [(place, place ^ bit) for place in range(size)]
+
+
+def cycle(size, by):
+    return [(place, (place + by) % size) for place in range(size)]
 
 
 def summed_over(value, axis):
@@ -172,39 +193,111 @@
     return value
 
 
-def worker_piece(left, right):
-    grad = matmul_tn(left, right).astype(jnp.bfloat16)
-    return lax.psum_scatter(grad, "narrow", scatter_dimension=0, tiled=True).astype(jnp.float32)
-
-
-def paired_piece(left, right):
-    n_wide, n_narrow = lax.axis_size("wide"), lax.axis_size("narrow")
-    core = lax.axis_index("wide") % 2
-    narrow_me = lax.axis_index("narrow")
-    pair, side = narrow_me // 2, narrow_me % 2
-    rows = D // n_narrow
-
-    def block(core_of, side_of):
-        part = lax.dynamic_slice_in_dim(left, (2 * core_of + side_of) * rows, rows, 1)
-        return matmul_tn(part, right)
-
-    cores = swap_pairs(n_wide, 1)
-    sides = swap_pairs(n_narrow, 1)
-    moves = []
-    for wide in range(n_wide):
-        for narrow in range(n_narrow):
-            if narrow // 2 != wide % 2:
-                target_wide = wide - wide % 2 + narrow // 2
-                target_narrow = 2 * (wide % 2) + narrow % 2
-                moves.append((wide * n_narrow + narrow, target_wide * n_narrow + target_narrow))
-    away = lax.ppermute(block(1 - core, 1 - side).astype(jnp.bfloat16), "wide", cores)
-    near = lax.ppermute(block(1 - core, side).astype(jnp.bfloat16), "wide", cores)
-    away = (block(core, 1 - side) + away.astype(jnp.float32)).astype(jnp.bfloat16)
-    away = lax.ppermute(away, "narrow", sides)
-    total = block(core, side) + near.astype(jnp.float32) + away.astype(jnp.float32)
-    total = total.astype(jnp.bfloat16)
-    moved = lax.ppermute(total, ("wide", "narrow"), moves)
-    return jnp.where(pair == core, total, moved).astype(jnp.float32)
+def gathered_near(value):
+    size = lax.axis_size("narrow")
+    rows = value.shape[0]
+    around = [value]
+    for by in range(1, size):
+        around.append(lax.ppermute(value, "narrow", cycle(size, size - by)))
+    twice = jnp.concatenate(around + around[:-1], axis=0)
+    start = lax.rem(size - lax.axis_index("narrow"), size) * rows
+    return lax.dynamic_slice_in_dim(twice, start, size * rows, 0)
+
+
+def scattered_near(value):
+    size = lax.axis_size("narrow")
+    rows = value.shape[0] // size
+    place = lax.axis_index("narrow")
+    total = lax.dynamic_slice_in_dim(value, place * rows, rows, 0)
+    for by in range(1, size):
+        target = lax.rem(place + by, size)
+        give = lax.dynamic_slice_in_dim(value, target * rows, rows, 0).astype(jnp.bfloat16)
+        take = lax.ppermute(give, "narrow", cycle(size, by))
+        total = total + take.astype(jnp.float32)
+    return total
+
+
+def chain_gather(value):
+    size = lax.axis_size("narrow")
+    rows = value.shape[0]
+    rising, falling = value, value
+    low, high = [], []
+    for step in range(1, size):
+        rising = lax.ppermute(rising, "narrow", [(i, i + 1) for i in range(step - 1, size - 1)])
+        falling = lax.ppermute(falling, "narrow", [(i, i - 1) for i in range(1, size - step + 1)])
+        low.append(rising)
+        high.append(falling)
+    line = jnp.concatenate(low[::-1] + [value] + high, axis=0)
+    start = (size - 1 - lax.axis_index("narrow")) * rows
+    return lax.dynamic_slice_in_dim(line, start, size * rows, 0)
+
+
+def chain_scatter(value):
+    size = lax.axis_size("narrow")
+    place = lax.axis_index("narrow")
+
+    def block(index):
+        return lax.dynamic_index_in_dim(value, jnp.clip(index, 0, size - 1), 0, keepdims=False)
+
+    rising, falling = None, None
+    for step in range(1, size):
+        up, down = block(size - step + place), block(step + place - size)
+        if rising is not None:
+            up, down = up + rising, down + falling
+        rising = lax.ppermute(up, "narrow", [(i, i + 1) for i in range(step)])
+        falling = lax.ppermute(down, "narrow", [(size - 1 - i, size - 2 - i) for i in range(step)])
+    return block(place) + rising + falling
+
+
+class WorkerPiece:
+    def __init__(self, left, right):
+        self.left, self.right = left, right
+        self.paired = paired_mesh()
+        if not self.paired:
+            return
+        self.core = lax.axis_index("wide") % 2
+        self.pair, self.side = lax.axis_index("narrow") // 2, lax.axis_index("narrow") % 2
+        cores = swap_pairs(lax.axis_size("wide"), 1)
+        self.far = lax.ppermute(self.low(1 - self.core, 1 - self.side), "wide", cores)
+        self.near = lax.ppermute(self.low(1 - self.core, self.side), "wide", cores)
+
+    def block(self, core, side):
+        rows = D // lax.axis_size("narrow")
+        part = lax.dynamic_slice_in_dim(self.left, (2 * core + side) * rows, rows, 1)
+        return matmul_tn(part, self.right)
+
+    def low(self, core, side):
+        return self.block(core, side).astype(jnp.bfloat16)
+
+    def waits(self):
+        return (self.far, self.near) if self.paired else ()
+
+    def across(self):
+        if self.paired:
+            away = self.block(self.core, 1 - self.side) + self.far.astype(jnp.float32)
+            sides = swap_pairs(lax.axis_size("narrow"), 1)
+            self.away = lax.ppermute(away.astype(jnp.bfloat16), "narrow", sides)
+
+    def waits_across(self):
+        return (self.away,) if self.paired else ()
+
+    def finish(self):
+        if not self.paired:
+            grad = matmul_tn(self.left, self.right).astype(jnp.bfloat16)
+            return lax.psum_scatter(grad, "narrow", scatter_dimension=0, tiled=True)
+        n_wide, n_narrow = lax.axis_size("wide"), lax.axis_size("narrow")
+        total = self.block(self.core, self.side)
+        total = total + self.near.astype(jnp.float32) + self.away.astype(jnp.float32)
+        total = total.astype(jnp.bfloat16)
+        moves = []
+        for wide in range(n_wide):
+            for narrow in range(n_narrow):
+                if narrow // 2 != wide % 2:
+                    target_wide = wide - wide % 2 + narrow // 2
+                    target = target_wide * n_narrow + 2 * (wide % 2) + narrow % 2
+                    moves.append((wide * n_narrow + narrow, target))
+        moved = lax.ppermute(total, ("wide", "narrow"), moves)
+        return jnp.where(self.pair == self.core, total, moved)
 
 
 def hosted_rows(token_ids, mlm_labels, mlm_valid, doc_ids, mlm_pos):
@@ -231,28 +324,68 @@
     )
 
 
+def wide_places():
+    wide_me = lax.axis_index("wide")
+    return wide_me % 2, wide_me // 2 % 2, wide_me // 4
+
+
 def scattered_sum(sent):
     n_wide = lax.axis_size("wide")
-    wide_me = lax.axis_index("wide")
     rows, cols = sent.shape
     part = cols // n_wide
-    if n_wide != 8:
+    if not paired_mesh():
         whole = lax.psum(sent.astype(jnp.bfloat16), "wide").astype(jnp.float32)
-        return lax.dynamic_slice_in_dim(whole, wide_me * part, part, 1)
-    core, x, y = wide_me % 2, wide_me // 2 % 2, wide_me // 4
-    blocks = sent.reshape(rows, 2, 2, 2, part)
-
-    def step(value, dim, place, bit):
-        give = lax.dynamic_index_in_dim(value, 1 - place, dim, keepdims=False).astype(jnp.bfloat16)
-        keep = lax.dynamic_index_in_dim(value, place, dim, keepdims=False)
-        take = lax.ppermute(give, "wide", swap_pairs(n_wide, bit))
-        return keep.astype(jnp.float32) + take.astype(jnp.float32)
-
-    blocks = step(blocks, 3, core, 1)
-    upper, lower = blocks[0 : rows // 2], blocks[rows // 2 :]
-    upper, lower = step(upper, 2, x, 2), step(lower, 1, y, 4)
-    upper, lower = step(upper, 1, y, 4), step(lower, 1, x, 2)
-    return jnp.concatenate([upper, lower], axis=0)
+        return lax.dynamic_slice_in_dim(whole, lax.axis_index("wide") * part, part, 1)
+    core, x, y = wide_places()
+
+    def block(value, place):
+        return lax.dynamic_slice_in_dim(value, place * part, part, 1)
+
+    give = [block(sent, 2 * chip + 1 - core).astype(jnp.bfloat16) for chip in range(4)]
+    take = [lax.ppermute(part_of, "wide", swap_pairs(n_wide, 1)) for part_of in give]
+    chips = jnp.stack([block(sent, 2 * chip + core) + take[chip] for chip in range(4)])
+    half = rows // 2
+
+    def send(value, bit):
+        return lax.ppermute(value.astype(jnp.bfloat16), "wide", swap_pairs(n_wide, bit))
+
+    def pick(value, index):
+        return lax.dynamic_index_in_dim(value, index, 0, keepdims=False)
+
+    upper, lower = chips[:, 0:half], chips[:, half:]
+    upper_far = send(pick(upper, 2 * (1 - y) + 1 - x), 2)
+    upper_near = send(pick(upper, 2 * y + 1 - x), 2)
+    lower_far = send(pick(lower, 2 * (1 - y) + 1 - x), 4)
+    lower_near = send(pick(lower, 2 * (1 - y) + x), 4)
+    upper_far = send(pick(upper, 2 * (1 - y) + x) + upper_far, 4)
+    lower_far = send(pick(lower, 2 * y + 1 - x) + lower_far, 2)
+    own_upper = pick(upper, 2 * y + x) + upper_near + upper_far
+    own_lower = pick(lower, 2 * y + x) + lower_near + lower_far
+    return jnp.concatenate([own_upper, own_lower], axis=0)
+
+
+def small_total(value):
+    if not paired_mesh():
+        return lax.psum(value, ("wide", "narrow"))
+    n_wide, n_narrow = lax.axis_size("wide"), lax.axis_size("narrow")
+    places = list(zip((1, 2, 4), wide_places()))
+    for bit, place in places:
+        half = value.shape[1] // 2
+        give = lax.dynamic_slice_in_dim(value, (1 - place) * half, half, 1).astype(jnp.bfloat16)
+        keep = lax.dynamic_slice_in_dim(value, place * half, half, 1)
+        value = keep + lax.ppermute(give, "wide", swap_pairs(n_wide, bit)).astype(jnp.float32)
+    bit = 1
+    while bit < n_narrow:
+        low = value.astype(jnp.bfloat16)
+        other = lax.ppermute(low, "narrow", swap_pairs(n_narrow, bit))
+        value = low.astype(jnp.float32) + other.astype(jnp.float32)
+        bit *= 2
+    value = value.astype(jnp.bfloat16)
+    for bit, place in reversed(places):
+        other = lax.ppermute(value, "wide", swap_pairs(n_wide, bit))
+        first, second = jnp.where(place == 0, value, other), jnp.where(place == 0, other, value)
+        value = jnp.concatenate([first, second], axis=1)
+    return value.astype(jnp.float32)
 
 
 def shards(
@@ -276,31 +409,40 @@
     n_wide = lax.axis_size("wide")
     narrow_me = lax.axis_index("narrow")
     wide_me = lax.axis_index("wide")
-    n_narrow = lax.axis_size("narrow")
     seqs = doc_ids.shape[0]
-    paired = n_wide % 2 == 0 and n_narrow == 4 and seqs == 1
+    paired = paired_mesh()
     count = summed_over(jnp.sum(mlm_valid.astype(jnp.float32)), "wide")
     if paired:
         token_ids, mlm_labels, mlm_valid, doc_ids, mlm_pos = hosted_rows(
             token_ids, mlm_labels, mlm_valid, doc_ids, mlm_pos
         )
     table_cols = lax.all_gather(table.astype(jnp.bfloat16), "wide", axis=1, tiled=True)
-    layer_rows = lax.all_gather(layer.astype(jnp.bfloat16), "narrow", axis=0, tiled=True)
+    if paired:
+        layer_rows = chain_gather(layer.astype(jnp.bfloat16))
+    else:
+        layer_rows = lax.all_gather(layer.astype(jnp.bfloat16), "narrow", axis=0, tiled=True)
+    layer_rows, (table_cols,) = after(layer_rows, table_cols)
     weights = lax.all_gather(layer_rows, "wide", axis=1, tiled=True)
     vshard = table_cols.shape[0]
     local_ids = token_ids - narrow_me * vshard
     inside = (local_ids >= 0) & (local_ids < vshard)
     picked = jnp.take(table_cols, jnp.clip(local_ids, 0, vshard - 1), axis=0)
     picked = jnp.where(inside[..., None], picked.astype(jnp.float32), 0.0)
-    looked = lax.psum_scatter(
-        picked.astype(jnp.bfloat16), "narrow", scatter_dimension=0, tiled=True
-    ).astype(jnp.float32)
+    picked = picked.astype(jnp.bfloat16)
+    if paired:
+        looked = chain_scatter(picked)[None]
+    else:
+        looked = lax.psum_scatter(picked, "narrow", scatter_dimension=0, tiled=True)
+    looked = looked.astype(jnp.float32)
     even_doc = (doc_ids % 2 == 0)[..., None]
     embedded = looked + small[0:L][None] + jnp.where(even_doc, small[L], small[L + 1])
     htwo, kept = layer_forward(embedded.reshape(seqs * L, D), doc_ids, small, weights)
     hmask = jnp.take_along_axis(htwo.reshape(seqs, L, D), mlm_pos[..., None], axis=1)
     hmask = hmask.reshape(seqs * MPS, D).astype(jnp.bfloat16)
-    group_h = lax.all_gather(hmask, "narrow", axis=0, tiled=True)
+    if paired:
+        group_h = gathered_near(hmask)
+    else:
+        group_h = lax.all_gather(hmask, "narrow", axis=0, tiled=True)
     vocab = narrow_me * vshard + jnp.arange(vshard)
     logits = jnp.where((vocab < VREAL)[None], matmul_nt(group_h, table_cols), -1000000000.0)
     labels = mlm_labels.reshape(-1)
@@ -308,7 +450,13 @@
     top = jnp.max(logits, axis=1)
     total = jnp.sum(jnp.exp(logits - top[:, None]), axis=1)
     target = jnp.sum(jnp.where(hit, logits, 0.0), axis=1)
-    top, total, target = joined((top, total, target), "narrow", merge_rows)
+    if paired:
+        stats = gathered_near(jnp.stack([top, total, target])[None])
+        top, total, target = stats[0]
+        for place in range(1, stats.shape[0]):
+            top, total, target = merge_rows((top, total, target), tuple(stats[place]))
+    else:
+        top, total, target = joined((top, total, target), "narrow", merge_rows)
     lse = top + jnp.log(total)
     flags = mlm_valid.reshape(-1).astype(jnp.float32)
     own = seqs * MPS
@@ -316,20 +464,19 @@
     dlogit = (
         (jnp.exp(logits - lse[:, None]) - hit.astype(jnp.float32)) * (flags / count)[:, None]
     ).astype(jnp.bfloat16)
-    dhmask = lax.psum_scatter(matmul(dlogit, table_cols), "narrow", scatter_dimension=0, tiled=True)
+    dhmask = matmul(dlogit, table_cols)
+    if paired:
+        dhmask = scattered_near(dhmask)
+    else:
+        dhmask = lax.psum_scatter(dhmask, "narrow", scatter_dimension=0, tiled=True)
     table_head = matmul_tn(dlogit, group_h)
     dhtwo = (
         jnp.zeros((seqs, L, D), jnp.float32)
         .at[jnp.arange(seqs)[:, None], mlm_pos]
         .add(dhmask.reshape(seqs, MPS, D))
     )
-    dembed, vectors, saved = layer_backward(
+    dembed, vectors, worker_grad = layer_backward(
         dhtwo.reshape(seqs * L, D), kept, doc_ids, small, weights
-    )
-    act, dqkv, out, dattn, fin, dupper, dffn, gated = saved
-    piece = paired_piece if paired else worker_piece
-    worker_grad = jnp.concatenate(
-        [piece(act, dqkv), piece(out, dattn), piece(fin, dupper), piece(dffn, gated)], axis=1
     )
     dembed_rows = dembed.reshape(seqs, L, D)
     seg_even = jnp.sum(jnp.where(even_doc, dembed_rows, 0.0), axis=(0, 1))
@@ -342,10 +489,9 @@
     table_grad = table_head.at[slots].add(
         group_rows.reshape(-1, D).astype(jnp.float32), mode="drop"
     )
-    table_grad = lax.psum_scatter(
-        table_grad.astype(jnp.bfloat16), "wide", scatter_dimension=1, tiled=True
-    ).astype(jnp.float32)
-    span = BETA * layer_m + (1.0 - BETA) * worker_grad + worker_err[0]
+    cut = table_grad.astype(jnp.bfloat16).reshape(vshard, n_wide, D // n_wide).transpose(1, 0, 2)
+    table_grad = lax.psum_scatter(cut, "wide", scatter_dimension=0).astype(jnp.float32)
+    span = BETA * layer_m + (1.0 - BETA) * worker_grad.astype(jnp.float32) + worker_err[0]
     scale = jnp.mean(jnp.abs(span)) + MAG_EPS
     sent = scale * jnp.tanh(span / scale)
     new_worker = (span - sent)[None]
@@ -379,7 +525,7 @@
             jnp.sum(own_loss)[None],
         ]
     )
-    small_grad = lax.psum(small_grad, ("wide", "narrow"))
+    small_grad = small_total(small_grad)
     sums = summed_over(summed_over(parts, "wide"), "narrow")
     loss_sum = sums[10]
     small_mom = BETA * small_m + (1.0 - BETA) * small_grad

time: 1420 us -> 1110 us (0.78)
  waiting for transfers between devices: 745 us -> 420 us
  starting transfers between devices: 75.8 us -> 178 us
  local copies, waits for them, and re-layouts: 111 us -> 69.1 us
  blocking collectives: 36 us -> 0 us
    all_gather x1, waiting for transfers between devices: 124 us -> 0.02 us  [shards(): weights = lax.all_gather(layer_rows, 'wide', axis=1, tiled=True)]
    ppermute x21 -> x55, waiting for transfers between devices: 240 us -> 352 us  [the longest x4 131 us: across(): self.away = lax.ppermute(away.astype(jnp.bfloat16), 'narrow', sides)]
    ppermute x21 -> x55, starting transfers between devices: 62 us -> 166 us  [the longest x4 107 us: scattered_sum(): lax.ppermute(part_of, 'wide', swap_pairs(n_wide, 1))]
    unnamed x10 -> x5, waiting for transfers between devices: 104 us -> 0.08 us
    all_gather x1, waiting for transfers between devices: 87.7 us -> 22.1 us  [shards(): lax.all_gather(table.astype(jnp.bfloat16), 'wide', axis=1, tiled=True)]
    reduce_scatter x2 -> x1, waiting for transfers between devices: 91.7 us -> 32.2 us  [shards(): lax.psum_scatter(cut, 'wide', scatter_dimension=0).astype(jnp.float32)]
    all_gather x1 -> x0, waiting for transfers between devices: 43 us -> none  [shards(): lax.all_gather(layer.astype(jnp.bfloat16), 'narrow', axis=0, tiled=True)]
    convert_element_type x10 -> x8, other arithmetic: 48.4 us -> 7.14 us  [the longest x1 2.84 us: shards(): picked = picked.astype(jnp.bfloat16)]
  transfers between devices with their start and end apart: 40 -> 70, of which waited for: 22 -> 45; matrix products, arithmetic and copies ran while one was open for 20% -> 26% of each run, Pallas kernels for 0% -> 0%
where the time goes in v2:
time: 1110 us; the launch traced here: 1100 us
  waiting for transfers between devices  420 us (38%)
  matrix products  211 us (19%)
  other arithmetic  197 us (18%)
  starting transfers between devices  178 us (16%)
  local copies, waits for them, and re-layouts  69.1 us (6%)
  between operations  21.3 us (2%)
    ppermute x4, waiting for transfers between devices, across(): self.away = lax.ppermute(away.astype(jnp.bfloat16), 'narrow', sides)  131 us
    ppermute x4, starting transfers between devices, scattered_sum(): lax.ppermute(part_of, 'wide', swap_pairs(n_wide, 1))  107 us
    ppermute x3, waiting for transfers between devices, chain_scatter(): rising = lax.ppermute(up, 'narrow', [(i, i + 1) for i in range(step)])  61.9 us
    dot_general x5, matrix products, matmul(): return jnp.dot(left, right, preferred_element_type=jnp.float32)  59.2 us
    dot_general x17, matrix products, matmul_tn(): lax.dot_general(left, right, (((0,), (0,)), ((), ())), preferred_element_...  58.4 us
    scatter-add x1, other arithmetic, shards(): table_head.at[slots]  39.6 us
    dot_general x5, matrix products, matmul_nt(): lax.dot_general(left, right, (((1,), (1,)), ((), ())), preferred_element_...  36.7 us
    ppermute x3, waiting for transfers between devices, chain_gather(): lax.ppermute(falling, 'narrow', [(i, i - 1) for i in range(1, size - step...  35.5 us
  transfers between devices with their start and end apart: 70, of which 45 were waited for; matrix products, arithmetic and copies ran while one was open for 26% of the time, Pallas kernels for 0%

profile of v2, /device:TPU:0, one launch (start us, length us, event | category | flops | bytes accessed | tf_op | source)
XLA Modules:
  0.0 1096.4 jit_solution(18221700846951252869)
XLA Ops:
  7.2 3.7 convert_element_type.387
  11.1 5.0 collective-permute-start.1
  17.4 15.4 %collective-permute-done.1 = bf16[256,1536]{1,0:T(8,128)(2,1)S(1)} collective-permute-done((bf16[256,1536]{1,0:T(8,128)(2,1)S(1)}, bf16[256,1536]{1,0:T(8,128)(2,1)S(1)}, u32[]{:S(2)}, u32[]{:S(2)}) %collective-permute-start.1) | collective-permute-done | bytes 786464 | tf_op jit(solution)/shard_map/ppermute | solution.py:226
  39.8 18.3 %collective-permute-done.5 = bf16[256,1536]{1,0:T(8,128)(2,1)} collective-permute-done((bf16[256,1536]{1,0:T(8,128)(2,1)S(1)}, bf16[256,1536]{1,0:T(8,128)(2,1)}, u32[]{:S(2)}, u32[]{:S(2)}) %collective-permute-start.5) | collective-permute-done | bytes 786464 | tf_op jit(solution)/shard_map/ppermute | solution.py:227
  63.3 14.5 %collective-permute-done.6 = bf16[256,1536]{1,0:T(8,128)(2,1)S(1)} collective-permute-done((bf16[256,1536]{1,0:T(8,128)(2,1)}, bf16[256,1536]{1,0:T(8,128)(2,1)S(1)}, u32[]{:S(2)}, u32[]{:S(2)}) %collective-permute-start.6) | collective-permute-done | bytes 786464 | tf_op jit(solution)/shard_map/ppermute | solution.py:227
  79.8 22.1 %all-gather.6.cloned.1.call-done = bf16[7632,1024]{1,0:T(8,128)(2,1)} async-done(((bf16[7632,128]{1,0:T(8,128)(2,1)}), bf16[7632,1024]{1,0:T(8,128)(2,1)}) %all-gather.6.cloned.1.call-update) | async-done | bytes 15630352 | tf_op jit(solution)/shard_map/all_gather | solution.py:419
  103.9 18.4 %gather_fusion = bf16[2048,1024]{1,0:T(8,128)(2,1)} fusion(bf16[7632,1024]{1,0:T(8,128)(2,1)} %all-gather.6.cloned.1.call-done, s32[2048]{0:T(1024)S(1)} %broadcast_clamp_fusion), kind=kCustom, calls=%fused_computation | custom fusion | bytes 8396800 | tf_op jit(solution)/shard_map/jit(_take)/gather | solution.py:429
  132.5 21.1 %collective-permute-done.7 = bf16[512,1024]{1,0:T(8,128)(2,1)S(1)} collective-permute-done((bf16[512,1024]{1,0:T(8,128)(2,1)S(1)}, bf16[512,1024]{1,0:T(8,128)(2,1)S(1)}, u32[]{:S(2)}, u32[]{:S(2)}) %collective-permute-start.7) | collective-permute-done | bytes 1048608 | tf_op jit(solution)/shard_map/ppermute | solution.py:247
  154.9 4.5 collective-permute-start.8
  159.4 21.9 %collective-permute-done.8 = bf16[512,1024]{1,0:T(8,128)(2,1)S(1)} collective-permute-done((bf16[512,1024]{1,0:T(8,128)(2,1)S(1)}, bf16[512,1024]{1,0:T(8,128)(2,1)S(1)}, u32[]{:S(2)}, u32[]{:S(2)}) %collective-permute-start.8) | collective-permute-done | bytes 1048608 | tf_op jit(solution)/shard_map/ppermute | solution.py:247
  199.5 6.3 collective-permute-start.9
  210.4 19.0 %collective-permute-done.9 = bf16[512,1024]{1,0:T(8,128)(2,1)S(1)} collective-permute-done((bf16[512,1024]{1,0:T(8,128)(2,1)}, bf16[512,1024]{1,0:T(8,128)(2,1)S(1)}, u32[]{:S(2)}, u32[]{:S(2)}) %collective-permute-start.9) | collective-permute-done | bytes 1048608 | tf_op jit(solution)/shard_map/ppermute | solution.py:247
  229.4 7.4 collective-permute-done.12
  240.2 7.9 add_convert_fusion.1
  248.1 4.8 copy.43
  252.9 9.9 fusion.4
  262.9 9.2 exponential_reduce_fusion
  272.1 10.3 convolution_convert_fusion.6
  282.4 3.5 fusion.203
  286.9 26.0 %multiply_convert_fusion.1 = (bf16[512,4096]{1,0:T(8,128)(2,1)S(1)}, f32[512,4096]{1,0:T(8,128)}, f32[512,4096]{1,0:T(8,128)}) fusion(f32[4096]{0:T(1024)S(1)} %bitcast.267, bf16[512,1024]{1,0:T(8,128)(2,1)S(1)} %fusion.55, bf16[1024,12288]{1,0:T(8,128)(2,1)} %all-gather.8.cloned.1.call-done), kind=kOutput, calls=%fused_computation.37 | convolution fusion | flops 4433379328 | bytes 30425088 | tf_op jit(solution)/shard_map/dot_general | solution.py:43
  313.0 9.2 fusion.204
  333.9 7.1 collective-permute-done.15
  344.3 9.6 fusion.205
  363.8 8.9 fusion.189
  376.2 5.4 collective-permute-done.25
  381.6 5.3 collective-permute-done.24
  399.9 13.0 %add_convert_fusion = bf16[512,4096]{1,0:T(8,128)(2,1)S(1)} fusion(f32[512,4096]{1,0:T(8,128)} %get-tuple-element.77, f32[512,4096]{1,0:T(8,128)} %get-tuple-element.144, f32[4096]{0:T(1024)S(1)} %bitcast.268, bf16[512,1024]{1,0:T(8,128)(2,1)S(1)} %get-tuple-element.52, bf16[1024,12288]{1,0:T(8,128)(2,1)} %all-gather.8.cloned.1.call-done), kind=kOutput, calls=%fused_computation.36 | convolution fusion | flops 4326424576 | bytes 30425088 | tf_op jit(solution)/shard_map/dot_general | solution.py:43
  416.0 8.7 multiply_reduce_fusion.6
  435.8 11.5 %collective-permute-done.37 = bf16[256,1024]{1,0:T(8,128)(2,1)} collective-permute-done((bf16[256,1024]{1,0:T(8,128)(2,1)S(1)}, bf16[256,1024]{1,0:T(8,128)(2,1)}, u32[]{:S(2)}, u32[]{:S(2)}) %collective-permute-start.37) | collective-permute-done | bytes 524320 | tf_op jit(solution)/shard_map/ppermute | solution.py:279
  449.8 4.9 add_convert_fusion.3
  460.1 11.3 %convolution_bitcast_fusion = bf16[1,512,1,16,64]{1,4,3,2,0:T(8,128)(2,1)} fusion(bf16[512,16,64]{0,2,1:T(8,128)(2,1)} %bitcast.244, f32[16,512,512]{1,2,0:T(8,128)} %get-tuple-element.141, f32[16,512]{1,0:T(8,128)S(1)} %copy-done.49, pred[512,512]{0,1:T(8,128)(4,1)S(1)} %copy-done.34), kind=kOutput, calls=%fused_computation.135 | convolution fusion | flops 553648128 | bytes 19169280 | tf_op jit(solution)/shard_map/shqk,sqhd->skhd/dot_general | solution.py:125
  471.3 17.9 %fusion.38 = bf16[1,16,512,512]{2,3,1,0:T(8,128)(2,1)} fusion(f32[16,512,512]{1,2,0:T(8,128)} %get-tuple-element.141, f32[16,512]{1,0:T(8,128)S(1)} %copy-done.49, pred[512,512]{0,1:T(8,128)(4,1)S(1)} %copy-done.34, bf16[512,16,64]{0,2,1:T(8,128)(2,1)} %bitcast.245, bf16[1,512,3,16,64]{1,4,3,2,0:T(8,128)(2,1)S(1)} %bitcast.233), kind=kOutput, calls=%fused_computation.74 | convolution fusion | flops 1115693568 | bytes 46727168 | tf_op jit(solution)/shard_map/sub | solution.py:129
  489.3 18.3 %collective-permute-done.32 = bf16[256,4096]{1,0:T(8,128)(2,1)} collective-permute-done((bf16[256,4096]{1,0:T(8,128)(2,1)}, bf16[256,4096]{1,0:T(8,128)(2,1)}, u32[]{:S(2)}, u32[]{:S(2)}) %collective-permute-start.32) | collective-permute-done | bytes 2097184 | tf_op jit(solution)/shard_map/ppermute | solution.py:279
  507.6 6.0 multiply_bitcast_fusion
  520.7 5.4 add_convert_fusion.2
  533.6 6.3 multiply_reduce_fusion.7
  539.9 3.6 add_convert_fusion.5
  546.0 55.4 %collective-permute-done.39 = bf16[256,4096]{1,0:T(8,128)(2,1)S(1)} collective-permute-done((bf16[256,4096]{1,0:T(8,128)(2,1)S(1)}, bf16[256,4096]{1,0:T(8,128)(2,1)S(1)}, u32[]{:S(2)}, u32[]{:S(2)}) %collective-permute-start.39) | collective-permute-done | bytes 2097184 | tf_op jit(solution)/shard_map/ppermute | solution.py:279
  601.4 4.5 fusion.42
  609.8 45.8 %collective-permute-done.35 = bf16[256,3072]{1,0:T(8,128)(2,1)} collective-permute-done((bf16[256,3072]{1,0:T(8,128)(2,1)}, bf16[256,3072]{1,0:T(8,128)(2,1)}, u32[]{:S(2)}, u32[]{:S(2)}) %collective-permute-start.35) | collective-permute-done | bytes 1572896 | tf_op jit(solution)/shard_map/ppermute | solution.py:279
  664.6 11.5 %abs_reduce_fusion = (f32[]{:T(128)}, f32[256,12288]{1,0:T(8,128)}) fusion(f32[1,256,12288]{2,1,0:T(8,128)S(1)} %bitcast.238, bf16[256,4096]{1,0:T(8,128)(2,1)S(1)} %broadcast_select_fusion, bf16[256,4096]{1,0:T(8,128)(2,1)S(1)} %broadcast_select_fusion.1, bf16[256,1024]{1,0:T(8,128)(2,1)S(1)} %copy-done.35, ...), kind=kLoop, calls=%fused_computation.17 | loop fusion | flops 44040192 | bytes 44040196 | tf_op jit(solution)/shard_map/reduce_sum | solution.py:495
  676.7 10.6 subtract_bitcast_fusion
  687.3 4.8 copy-done.7
  693.9 106.4 %collective-permute-start.42 = (bf16[256,1536]{1,0:T(8,128)(2,1)}, bf16[256,1536]{1,0:T(8,128)(2,1)S(1)}, u32[]{:S(2)}, u32[]{:S(2)}) collective-permute-start(bf16[256,1536]{1,0:T(8,128)(2,1)} %get-tuple-element.86), channel_id=1, source_target_pairs={{0,4},{4,0},{8,12},{12,8},{16,20},{20,16},{24,28},{28,24},{1,5},{5... | collective-permute-start | bytes 2359304 | tf_op jit(solution)/shard_map/ppermute | solution.py:345
  805.8 4.1 add_bitcast_fusion.3
  817.9 8.0 collective-permute-done.50
  829.5 4.7 collective-permute-done.49
  834.3 9.3 collective-permute-done.51
  848.0 3.9 multiply_reduce_fusion.14
  852.3 19.8 %fusion.81 = f32[7632,1024]{1,0:T(8,128)} fusion(bf16[560,1024]{1,0:T(8,128)(2,1)} %constant_dynamic-update-slice_fusion.7, s32[]{:T(128)S(6)} %select_n.352, f32[320,7632]{1,0:T(8,128)} %copy-done.6, f32[320]{0:T(512)S(1)} %copy-done.60, f32[320]{0:T(512)S(1)} %copy-done.58, s32[7632]{0:T(1024)S(1)} %copy-done.44, s32[320]{0:T(512)S(1)} %copy-done.54), kind=kOutput, calls=%fused_computation.189 | convolution fusion | flops 5016360960 | bytes 41780804 | tf_op jit(solution)/shard_map/dot_general | solution.py:47
  872.1 39.6 %scatter_custom_fusion.1 = f32[7632,1024]{1,0:T(8,128)} fusion(f32[7632,1024]{1,0:T(8,128)} %fusion.81, s32[2048]{0:T(1024)S(1)} %bitcast.278, bf16[2048,1024]{1,0:T(8,128)(2,1)} %all-gather.12.cloned.1.call-done), kind=kCustom, calls=%fused_computation.33 | custom fusion | flops 4194304 | bytes 35454976 | tf_op jit(solution)/shard_map/scatter-add | solution.py:489
  911.7 16.3 %bitcast_bitcast_fusion = bf16[8,7632,128]{2,1,0:T(8,128)(2,1)} fusion(f32[7632,1024]{1,0:T(8,128)} %scatter_custom_fusion.1), kind=kLoop, calls=%fused_computation.11 | loop fusion | flops 7815168 | bytes 46891008 | tf_op jit(solution)/shard_map/transpose | solution.py:492
  931.5 7.1 concatenate.97
  945.5 7.8 collective-permute-done.58
  954.2 4.3 collective-permute-done.59
  958.7 5.0 collective-permute-done.60
  963.8 6.8 collective-permute-done.61
  971.3 7.2 collective-permute-done.62
  979.4 12.6 %collective-permute-done.63 = bf16[528,256]{1,0:T(8,128)(2,1)S(1)} collective-permute-done((bf16[528,256]{1,0:T(8,128)(2,1)S(1)}, bf16[528,256]{1,0:T(8,128)(2,1)S(1)}, u32[]{:S(2)}, u32[]{:S(2)}) %collective-permute-start.63) | collective-permute-done | bytes 270368 | tf_op jit(solution)/shard_map/ppermute | solution.py:385
  994.3 5.7 multiply_reduce_fusion.3
  1000.2 9.1 convert_element_type.498
  1009.3 32.2 %reduce-scatter.2.cloned.1.call-done = bf16[1,7632,128]{2,1,0:T(8,128)(2,1)} async-done(((bf16[8,7632,128]{2,1,0:T(8,128)(2,1)}), bf16[1,7632,128]{2,1,0:T(8,128)(2,1)}) %reduce-scatter.2.cloned.1.call-update) | async-done | bytes 1953808 | tf_op jit(solution)/shard_map/reduce_scatter | solution.py:493
  1041.5 8.1 multiply_reduce_fusion.1
  1074.3 8.2 multiply_subtract_fusion
  (447 shorter events, 214.9 us)
Async XLA Ops:
  7.2 94.6 %all-gather.6.cloned.1.call-start = ((), (), s32[]{:S(2)}) async-start(), calls=%async_computation.1 | async-start | bytes 17584128 | tf_op jit(solution)/shard_map/all_gather | solution.py:419
  10.9 229.3 %all-gather.8.cloned.1.call-start = ((), (), s32[]{:S(2)}) async-start(), calls=%async_computation.2 | async-start | bytes 28311552 | tf_op jit(solution)/shard_map/all_gather | solution.py:425
  11.1 21.7 %collective-permute-start.1 = (bf16[256,1536]{1,0:T(8,128)(2,1)S(1)}, bf16[256,1536]{1,0:T(8,128)(2,1)S(1)}, u32[]{:S(2)}, u32[]{:S(2)}) collective-permute-start(bf16[256,1536]{1,0:T(8,128)(2,1)S(1)} %convert_element_type.386), channel_id=1, source_target_pairs={{0,1},{1,2},{2,3},{4,5},{5,6},{6,7},{8,9},{9,10},{10,11},{12,13},{... | collective-permute-start | bytes 2359304 | tf_op jit(solution)/shard_map/ppermute | solution.py:226
  16.1 20.9 %collective-permute-start.4 = (bf16[256,1536]{1,0:T(8,128)(2,1)S(1)}, bf16[256,1536]{1,0:T(8,128)(2,1)S(1)}, u32[]{:S(2)}, u32[]{:S(2)}) collective-permute-start(bf16[256,1536]{1,0:T(8,128)(2,1)S(1)} %convert_element_type.386), channel_id=1, source_target_pairs={{1,0},{2,1},{3,2},{5,4},{6,5},{7,6},{9,8},{10,9},{11,10},{13,12},{... | collective-permute-start | bytes 2359304 | tf_op jit(solution)/shard_map/ppermute | solution.py:227
  32.8 5.5 collective-permute-start.2
  37.0 21.2 %collective-permute-start.5 = (bf16[256,1536]{1,0:T(8,128)(2,1)S(1)}, bf16[256,1536]{1,0:T(8,128)(2,1)}, u32[]{:S(2)}, u32[]{:S(2)}) collective-permute-start(bf16[256,1536]{1,0:T(8,128)(2,1)S(1)} %collective-permute-done.4), channel_id=1, source_target_pairs={{1,0},{2,1},{5,4},{6,5},{9,8},{10,9},{13,12},{14,13},{17,16},{18,1... | collective-permute-start | bytes 2359304 | tf_op jit(solution)/shard_map/ppermute | solution.py:227
  38.3 21.2 %collective-permute-start.3 = (bf16[256,1536]{1,0:T(8,128)(2,1)}, bf16[256,1536]{1,0:T(8,128)(2,1)}, u32[]{:S(2)}, u32[]{:S(2)}) collective-permute-start(bf16[256,1536]{1,0:T(8,128)(2,1)} %collective-permute-done.2), channel_id=1, source_target_pairs={{2,3},{6,7},{10,11},{14,15},{18,19},{22,23},{26,27},{30,31}} | collective-permute-start | bytes 2359304 | tf_op jit(solution)/shard_map/ppermute | solution.py:226
  58.1 19.7 %collective-permute-start.6 = (bf16[256,1536]{1,0:T(8,128)(2,1)}, bf16[256,1536]{1,0:T(8,128)(2,1)S(1)}, u32[]{:S(2)}, u32[]{:S(2)}) collective-permute-start(bf16[256,1536]{1,0:T(8,128)(2,1)} %collective-permute-done.5), channel_id=1, source_target_pairs={{1,0},{5,4},{9,8},{13,12},{17,16},{21,20},{25,24},{29,28}} | collective-permute-start | bytes 2359304 | tf_op jit(solution)/shard_map/ppermute | solution.py:227
  101.8 770.3 %all-gather.12.cloned.1.call-start = ((), (), s32[]{:S(2)}) async-start(), calls=%async_computation.5 | async-start | bytes 5242880 | tf_op jit(solution)/shard_map/all_gather | solution.py:487
  127.3 26.2 %collective-permute-start.7 = (bf16[512,1024]{1,0:T(8,128)(2,1)S(1)}, bf16[512,1024]{1,0:T(8,128)(2,1)S(1)}, u32[]{:S(2)}, u32[]{:S(2)}) collective-permute-start(bf16[512,1024]{1,0:T(8,128)(2,1)S(1)} %get-tuple-element.94), channel_id=1, source_target_pairs={{0,1},{4,5},{8,9},{12,13},{16,17},{20,21},{24,25},{28,29}} | collective-permute-start | bytes 3145736 | tf_op jit(solution)/shard_map/ppermute | solution.py:247
  130.8 28.6 %collective-permute-start.10 = (bf16[512,1024]{1,0:T(8,128)(2,1)S(1)}, bf16[512,1024]{1,0:T(8,128)(2,1)}, u32[]{:S(2)}, u32[]{:S(2)}) collective-permute-start(bf16[512,1024]{1,0:T(8,128)(2,1)S(1)} %get-tuple-element.95), channel_id=1, source_target_pairs={{3,2},{7,6},{11,10},{15,14},{19,18},{23,22},{27,26},{31,30}} | collective-permute-start | bytes 3145736 | tf_op jit(solution)/shard_map/ppermute | solution.py:248
  154.9 26.4 %collective-permute-start.8 = (bf16[512,1024]{1,0:T(8,128)(2,1)S(1)}, bf16[512,1024]{1,0:T(8,128)(2,1)S(1)}, u32[]{:S(2)}, u32[]{:S(2)}) collective-permute-start(bf16[512,1024]{1,0:T(8,128)(2,1)S(1)} %bitcast_add_fusion.4), channel_id=1, source_target_pairs={{0,1},{1,2},{4,5},{5,6},{8,9},{9,10},{12,13},{13,14},{16,17},{17,1... | collective-permute-start | bytes 3145736 | tf_op jit(solution)/shard_map/ppermute | solution.py:247
  184.3 21.5 %collective-permute-start.11 = (bf16[512,1024]{1,0:T(8,128)(2,1)S(1)}, bf16[512,1024]{1,0:T(8,128)(2,1)S(1)}, u32[]{:S(2)}, u32[]{:S(2)}) collective-permute-start(bf16[512,1024]{1,0:T(8,128)(2,1)S(1)} %get-tuple-element.93), channel_id=1, source_target_pairs={{3,2},{2,1},{7,6},{6,5},{11,10},{10,9},{15,14},{14,13},{19,18},{18... | collective-permute-start | bytes 3145736 | tf_op jit(solution)/shard_map/ppermute | solution.py:248
  185.7 3.9 collective-permute-start.20
  185.7 22.8 %collective-permute-start.13 = (s32[1,592]{1,0:T(1,128)S(1)}, s32[1,592]{1,0:T(1,128)S(1)}, u32[]{:S(2)}, u32[]{:S(2)}) collective-permute-start(s32[1,592]{1,0:T(1,128)S(1)} %pad_add_fusion.1), channel_id=1, source_target_pairs={{0,0},{1,4},{2,1},{3,5},{4,2},{5,6},{6,3},{7,7},{8,8},{9,12},{10,9... | collective-permute-start | bytes 7112 | tf_op jit(solution)/shard_map/ppermute | solution.py:317
  190.8 3.7 collective-permute-start.21
  195.2 3.7 collective-permute-start.22
  199.5 29.9 %collective-permute-start.9 = (bf16[512,1024]{1,0:T(8,128)(2,1)}, bf16[512,1024]{1,0:T(8,128)(2,1)S(1)}, u32[]{:S(2)}, u32[]{:S(2)}) collective-permute-start(bf16[512,1024]{1,0:T(8,128)(2,1)} %get-tuple-element.92), channel_id=1, source_target_pairs={{0,1},{1,2},{2,3},{4,5},{5,6},{6,7},{8,9},{9,10},{10,11},{12,13},{... | collective-permute-start | bytes 3145736 | tf_op jit(solution)/shard_map/ppermute | solution.py:247
  207.1 29.6 %collective-permute-start.12 = (bf16[512,1024]{1,0:T(8,128)(2,1)S(1)}, bf16[512,1024]{1,0:T(8,128)(2,1)S(1)}, u32[]{:S(2)}, u32[]{:S(2)}) collective-permute-start(bf16[512,1024]{1,0:T(8,128)(2,1)S(1)} %bitcast_add_fusion.3), channel_id=1, source_target_pairs={{3,2},{2,1},{1,0},{7,6},{6,5},{5,4},{11,10},{10,9},{9,8},{15,14},{... | collective-permute-start | bytes 3145736 | tf_op jit(solution)/shard_map/ppermute | solution.py:248
  326.2 7.0 collective-permute-start.14
  327.3 13.6 %collective-permute-start.15 = (bf16[80,1024]{1,0:T(8,128)(2,1)S(1)}, bf16[80,1024]{1,0:T(8,128)(2,1)S(1)}, u32[]{:S(2)}, u32[]{:S(2)}) collective-permute-start(bf16[80,1024]{1,0:T(8,128)(2,1)S(1)} %get-tuple-element.75), channel_id=1, source_target_pairs={{0,2},{1,3},{2,0},{3,1},{4,6},{5,7},{6,4},{7,5},{8,10},{9,11},{10,... | collective-permute-start | bytes 491528 | tf_op jit(solution)/shard_map/ppermute | solution.py:201
  329.7 11.9 %collective-permute-start.16 = (bf16[80,1024]{1,0:T(8,128)(2,1)S(1)}, bf16[80,1024]{1,0:T(8,128)(2,1)S(1)}, u32[]{:S(2)}, u32[]{:S(2)}) collective-permute-start(bf16[80,1024]{1,0:T(8,128)(2,1)S(1)} %get-tuple-element.75), channel_id=1, source_target_pairs={{0,1},{1,2},{2,3},{3,0},{4,5},{5,6},{6,7},{7,4},{8,9},{9,10},{10,1... | collective-permute-start | bytes 491528 | tf_op jit(solution)/shard_map/ppermute | solution.py:201
  356.6 3.7 collective-permute-start.17
  356.7 4.6 collective-permute-start.18
  357.7 5.4 collective-permute-start.19
  373.8 7.8 collective-permute-start.25
  375.5 11.4 %collective-permute-start.24 = (bf16[80,1024]{1,0:T(8,128)(2,1)S(1)}, bf16[80,1024]{1,0:T(8,128)(2,1)S(1)}, u32[]{:S(2)}, u32[]{:S(2)}) collective-permute-start(bf16[80,1024]{1,0:T(8,128)(2,1)S(1)} %get-tuple-element.118), channel_id=1, source_target_pairs={{0,2},{1,3},{2,0},{3,1},{4,6},{5,7},{6,4},{7,5},{8,10},{9,11},{10,... | collective-permute-start | bytes 491528 | tf_op jit(solution)/shard_map/ppermute | solution.py:215
  375.5 11.4 %collective-permute-start.23 = (bf16[80,1024]{1,0:T(8,128)(2,1)S(1)}, bf16[80,1024]{1,0:T(8,128)(2,1)S(1)}, u32[]{:S(2)}, u32[]{:S(2)}) collective-permute-start(bf16[80,1024]{1,0:T(8,128)(2,1)S(1)} %get-tuple-element.116), channel_id=1, source_target_pairs={{0,1},{1,2},{2,3},{3,0},{4,5},{5,6},{6,7},{7,4},{8,9},{9,10},{10,1... | collective-permute-start | bytes 491528 | tf_op jit(solution)/shard_map/ppermute | solution.py:215
  396.7 16.2 %collective-permute-start.26 = (bf16[256,4096]{1,0:T(8,128)(2,1)S(1)}, bf16[256,4096]{1,0:T(8,128)(2,1)S(1)}, u32[]{:S(2)}, u32[]{:S(2)}) collective-permute-start(bf16[256,4096]{1,0:T(8,128)(2,1)S(1)} %convolution_convert_fusion.3), channel_id=1, source_target_pairs={{0,4},{4,0},{8,12},{12,8},{16,20},{20,16},{24,28},{28,24},{1,5},{5... | collective-permute-start | bytes 6291464 | tf_op jit(solution)/shard_map/ppermute | solution.py:261
  399.4 13.5 %collective-permute-start.27 = (bf16[256,4096]{1,0:T(8,128)(2,1)}, bf16[256,4096]{1,0:T(8,128)(2,1)}, u32[]{:S(2)}, u32[]{:S(2)}) collective-permute-start(bf16[256,4096]{1,0:T(8,128)(2,1)} %convolution_convert_fusion.2), channel_id=1, source_target_pairs={{0,4},{4,0},{8,12},{12,8},{16,20},{20,16},{24,28},{28,24},{1,5},{5... | collective-permute-start | bytes 6291464 | tf_op jit(solution)/shard_map/ppermute | solution.py:262
  415.6 43.2 %collective-permute-start.28 = (bf16[256,4096]{1,0:T(8,128)(2,1)}, bf16[256,4096]{1,0:T(8,128)(2,1)}, u32[]{:S(2)}, u32[]{:S(2)}) collective-permute-start(bf16[256,4096]{1,0:T(8,128)(2,1)} %convolution_convert_fusion.1), channel_id=1, source_target_pairs={{0,4},{4,0},{8,12},{12,8},{16,20},{20,16},{24,28},{28,24},{1,5},{5... | collective-permute-start | bytes 6291464 | tf_op jit(solution)/shard_map/ppermute | solution.py:261
  427.8 4.5 collective-permute-start.30
  430.6 28.2 %collective-permute-start.29 = (bf16[256,4096]{1,0:T(8,128)(2,1)}, bf16[256,4096]{1,0:T(8,128)(2,1)}, u32[]{:S(2)}, u32[]{:S(2)}) collective-permute-start(bf16[256,4096]{1,0:T(8,128)(2,1)} %convolution_convert_fusion), channel_id=1, source_target_pairs={{0,4},{4,0},{8,12},{12,8},{16,20},{20,16},{24,28},{28,24},{1,5},{5... | collective-permute-start | bytes 6291464 | tf_op jit(solution)/shard_map/ppermute | solution.py:262
  432.8 14.5 %collective-permute-start.37 = (bf16[256,1024]{1,0:T(8,128)(2,1)S(1)}, bf16[256,1024]{1,0:T(8,128)(2,1)}, u32[]{:S(2)}, u32[]{:S(2)}) collective-permute-start(bf16[256,1024]{1,0:T(8,128)(2,1)S(1)} %add_convert_fusion.9), channel_id=1, source_target_pairs={{0,1},{1,0},{2,3},{3,2},{4,5},{5,4},{6,7},{7,6},{8,9},{9,8},{10,11... | collective-permute-start | bytes 1572872 | tf_op jit(solution)/shard_map/ppermute | solution.py:279
  448.8 9.0 collective-permute-start.38
  454.7 52.9 %collective-permute-start.32 = (bf16[256,4096]{1,0:T(8,128)(2,1)}, bf16[256,4096]{1,0:T(8,128)(2,1)}, u32[]{:S(2)}, u32[]{:S(2)}) collective-permute-start(bf16[256,4096]{1,0:T(8,128)(2,1)} %add_convert_fusion.3), channel_id=1, source_target_pairs={{0,1},{1,0},{2,3},{3,2},{4,5},{5,4},{6,7},{7,6},{8,9},{9,8},{10,11... | collective-permute-start | bytes 6291464 | tf_op jit(solution)/shard_map/ppermute | solution.py:279
  526.1 133.1 %collective-permute-start.41 = (bf16[256,4096]{1,0:T(8,128)(2,1)}, bf16[256,4096]{1,0:T(8,128)(2,1)}, u32[]{:S(2)}, u32[]{:S(2)}) collective-permute-start(bf16[256,4096]{1,0:T(8,128)(2,1)} %add_convert_fusion.2), channel_id=1, source_target_pairs={{2,4},{3,5},{4,2},{5,3},{10,12},{11,13},{12,10},{13,11},{18,20},{1... | collective-permute-start | bytes 6291464 | tf_op jit(solution)/shard_map/ppermute | solution.py:299
  531.1 70.3 %collective-permute-start.39 = (bf16[256,4096]{1,0:T(8,128)(2,1)S(1)}, bf16[256,4096]{1,0:T(8,128)(2,1)S(1)}, u32[]{:S(2)}, u32[]{:S(2)}) collective-permute-start(bf16[256,4096]{1,0:T(8,128)(2,1)S(1)} %fusion.43), channel_id=1, source_target_pairs={{0,1},{1,0},{2,3},{3,2},{4,5},{5,4},{6,7},{7,6},{8,9},{9,8},{10,11... | collective-permute-start | bytes 6291464 | tf_op jit(solution)/shard_map/ppermute | solution.py:279
  531.2 8.8 collective-permute-start.34
  532.4 13.6 %collective-permute-start.33 = (bf16[256,3072]{1,0:T(8,128)(2,1)S(1)}, bf16[256,3072]{1,0:T(8,128)(2,1)}, u32[]{:S(2)}, u32[]{:S(2)}) collective-permute-start(bf16[256,3072]{1,0:T(8,128)(2,1)S(1)} %convolution_convert_fusion.5), channel_id=1, source_target_pairs={{0,4},{4,0},{8,12},{12,8},{16,20},{20,16},{24,28},{28,24},{1,5},{5... | collective-permute-start | bytes 4718600 | tf_op jit(solution)/shard_map/ppermute | solution.py:262
  543.5 112.0 %collective-permute-start.35 = (bf16[256,3072]{1,0:T(8,128)(2,1)}, bf16[256,3072]{1,0:T(8,128)(2,1)}, u32[]{:S(2)}, u32[]{:S(2)}) collective-permute-start(bf16[256,3072]{1,0:T(8,128)(2,1)} %add_convert_fusion.5), channel_id=1, source_target_pairs={{0,1},{1,0},{2,3},{3,2},{4,5},{5,4},{6,7},{7,6},{8,9},{9,8},{10,11... | collective-permute-start | bytes 4718600 | tf_op jit(solution)/shard_map/ppermute | solution.py:279
  605.9 55.4 %collective-permute-start.40 = (bf16[256,4096]{1,0:T(8,128)(2,1)}, bf16[256,4096]{1,0:T(8,128)(2,1)}, u32[]{:S(2)}, u32[]{:S(2)}) collective-permute-start(bf16[256,4096]{1,0:T(8,128)(2,1)} %fusion.42), channel_id=1, source_target_pairs={{2,4},{3,5},{4,2},{5,3},{10,12},{11,13},{12,10},{13,11},{18,20},{1... | collective-permute-start | bytes 6291464 | tf_op jit(solution)/shard_map/ppermute | solution.py:299
  609.7 390.5 %all-gather.10.cloned.1.call-start = ((), (), s32[]{:S(2)}) async-start(), calls=%async_computation.4 | async-start | bytes 7077888 | tf_op jit(solution)/shard_map/all_gather | solution.py:504
  658.3 5.0 collective-permute-start.36
  693.9 108.6 %collective-permute-start.42 = (bf16[256,1536]{1,0:T(8,128)(2,1)}, bf16[256,1536]{1,0:T(8,128)(2,1)S(1)}, u32[]{:S(2)}, u32[]{:S(2)}) collective-permute-start(bf16[256,1536]{1,0:T(8,128)(2,1)} %get-tuple-element.86), channel_id=1, source_target_pairs={{0,4},{4,0},{8,12},{12,8},{16,20},{20,16},{24,28},{28,24},{1,5},{5... | collective-permute-start | bytes 2359304 | tf_op jit(solution)/shard_map/ppermute | solution.py:345
  800.4 4.4 collective-permute-start.44
  800.9 5.0 collective-permute-start.43
  813.7 12.3 %collective-permute-start.50 = (bf16[128,1536]{1,0:T(8,128)(2,1)}, bf16[128,1536]{1,0:T(8,128)(2,1)}, u32[]{:S(2)}, u32[]{:S(2)}) collective-permute-start(bf16[128,1536]{1,0:T(8,128)(2,1)} %get-tuple-element.99), channel_id=1, source_target_pairs={{0,16},{4,20},{8,24},{12,28},{16,0},{20,4},{24,8},{28,12},{1,17},{... | collective-permute-start | bytes 1179656 | tf_op jit(solution)/shard_map/ppermute | solution.py:350
  814.2 20.0 %collective-permute-start.49 = (bf16[128,1536]{1,0:T(8,128)(2,1)S(1)}, bf16[128,1536]{1,0:T(8,128)(2,1)S(1)}, u32[]{:S(2)}, u32[]{:S(2)}) collective-permute-start(bf16[128,1536]{1,0:T(8,128)(2,1)S(1)} %get-tuple-element.98), channel_id=1, source_target_pairs={{0,16},{4,20},{8,24},{12,28},{16,0},{20,4},{24,8},{28,12},{1,17},{... | collective-permute-start | bytes 1179656 | tf_op jit(solution)/shard_map/ppermute | solution.py:350
  815.8 13.0 %collective-permute-start.47 = (bf16[128,1536]{1,0:T(8,128)(2,1)S(1)}, bf16[128,1536]{1,0:T(8,128)(2,1)S(1)}, u32[]{:S(2)}, u32[]{:S(2)}) collective-permute-start(bf16[128,1536]{1,0:T(8,128)(2,1)S(1)} %get-tuple-element.97), channel_id=1, source_target_pairs={{0,8},{4,12},{8,0},{12,4},{16,24},{20,28},{24,16},{28,20},{1,9},{5... | collective-permute-start | bytes 1179656 | tf_op jit(solution)/shard_map/ppermute | solution.py:350
  817.4 27.5 %collective-permute-start.46 = (bf16[128,1536]{1,0:T(8,128)(2,1)S(1)}, bf16[128,1536]{1,0:T(8,128)(2,1)S(1)}, u32[]{:S(2)}, u32[]{:S(2)}) collective-permute-start(bf16[128,1536]{1,0:T(8,128)(2,1)S(1)} %get-tuple-element.96), channel_id=1, source_target_pairs={{0,8},{4,12},{8,0},{12,4},{16,24},{20,28},{24,16},{28,20},{1,9},{5... | collective-permute-start | bytes 1179656 | tf_op jit(solution)/shard_map/ppermute | solution.py:350
  827.3 16.3 %collective-permute-start.51 = (bf16[128,1536]{1,0:T(8,128)(2,1)S(1)}, bf16[128,1536]{1,0:T(8,128)(2,1)S(1)}, u32[]{:S(2)}, u32[]{:S(2)}) collective-permute-start(bf16[128,1536]{1,0:T(8,128)(2,1)S(1)} %fusion.77), channel_id=1, source_target_pairs={{0,8},{4,12},{8,0},{12,4},{16,24},{20,28},{24,16},{28,20},{1,9},{5... | collective-permute-start | bytes 1179656 | tf_op jit(solution)/shard_map/ppermute | solution.py:350
  828.9 15.9 %collective-permute-start.48 = (bf16[128,1536]{1,0:T(8,128)(2,1)S(1)}, bf16[128,1536]{1,0:T(8,128)(2,1)S(1)}, u32[]{:S(2)}, u32[]{:S(2)}) collective-permute-start(bf16[128,1536]{1,0:T(8,128)(2,1)S(1)} %fusion.79), channel_id=1, source_target_pairs={{0,16},{4,20},{8,24},{12,28},{16,0},{20,4},{24,8},{28,12},{1,17},{... | collective-permute-start | bytes 1179656 | tf_op jit(solution)/shard_map/ppermute | solution.py:350
  851.9 189.6 %reduce-scatter.2.cloned.1.call-start = ((), (), s32[]{:S(2)}) async-start(), calls=%async_computation.3 | async-start | bytes 17584128 | tf_op jit(solution)/shard_map/reduce_scatter | solution.py:493
  944.8 8.5 collective-permute-start.58
  953.5 5.1 collective-permute-start.59
  958.6 5.1 collective-permute-start.60
  963.7 6.9 collective-permute-start.61
  970.6 7.9 collective-permute-start.62
  978.7 13.3 %collective-permute-start.63 = (bf16[528,256]{1,0:T(8,128)(2,1)S(1)}, bf16[528,256]{1,0:T(8,128)(2,1)S(1)}, u32[]{:S(2)}, u32[]{:S(2)}) collective-permute-start(bf16[528,256]{1,0:T(8,128)(2,1)S(1)} %pad_maximum_fusion.2), channel_id=1, source_target_pairs={{0,8},{4,12},{8,0},{12,4},{16,24},{20,28},{24,16},{28,20},{1,9},{5... | collective-permute-start | bytes 811016 | tf_op jit(solution)/shard_map/ppermute | solution.py:385
  1052.7 3.5 collective-permute-start.53
  1056.3 3.5 collective-permute-start.54
  1059.8 3.5 collective-permute-start.55
  1063.4 4.4 collective-permute-start.56
  (88 other events, 1265.2 us)
Sparse Core Ops, SparseCore 0:
  11.1 90.7 all-gather.5
  104.3 125.3 all-gather.7
  609.8 146.1 all-gather.11
  852.1 43.8 all-gather.9
  928.2 113.3 reduce-scatter.1

commit v3 on v2

--- a/solution.py
+++ b/solution.py
@@ -1,6 +1,8 @@
 import jax
 import jax.numpy as jnp
 from jax import lax
+from jax.experimental import pallas as pl
+from jax.experimental.pallas import tpu as pltpu
 from jax.sharding import PartitionSpec as P
 
 D = 1024
@@ -103,32 +105,31 @@
     _, pull = jax.vjp(norm_rows, rtwo, small[base + 4], small[base + 5])
     drtwo, dgain_two, dshift_two = pull(dhtwo)
     dffn = drtwo.astype(jnp.bfloat16)
-    down = WorkerPiece(dffn, gated)
+    down = WorkerPiece((dffn, gated))
     dgated = matmul(dffn, weights[:, 4 * D + FF :])
     _, pull = jax.vjp(gelu_exact, upper)
     dupper = pull(dgated)[0].astype(jnp.bfloat16)
-    dupper, _ = after(dupper, *down.waits())
+    dupper = down.received(dupper)
     down.across()
-    up = WorkerPiece(fin, dupper)
+    up = WorkerPiece((fin, dupper))
     dhone = drtwo + matmul_nt(dupper, weights[:, 4 * D : 4 * D + FF])
     _, pull = jax.vjp(norm_rows, rone, small[base + 2], small[base + 3])
     drone, dgain_one, dshift_one = pull(dhone)
     dattn = drone.astype(jnp.bfloat16)
-    attn = WorkerPiece(out, dattn)
     dout = matmul_nt(dattn, weights[:, 3 * D : 4 * D]).astype(jnp.bfloat16)
-    dout, _ = after(dout, *up.waits(), *attn.waits())
+    dout = up.received(dout)
     up.across()
-    attn.across()
     dout = dout.reshape(seqs, L, HEADS, HEAD)
     heads = qkv.reshape(seqs, L, 3, HEADS, HEAD)
     prob = jnp.exp(score_block(heads, docs) - lse)
     dvalue = jnp.einsum(
         "shqk,sqhd->skhd", prob.astype(jnp.bfloat16), dout, preferred_element_type=jnp.float32
     )
+    dout, dvalue = down.crossed(dout, dvalue)
+    if down.paired:
+        down.finish()
     dprob = jnp.einsum("sqhd,skhd->shqk", dout, heads[:, :, 2], preferred_element_type=jnp.float32)
     dscore = (prob * (dprob - jnp.sum(prob * dprob, axis=-1, keepdims=True))).astype(jnp.bfloat16)
-    dscore, _ = after(dscore, *down.waits_across())
-    grad_down = down.finish()
     dquery = (
         jnp.einsum("shqk,skhd->sqhd", dscore, heads[:, :, 1], preferred_element_type=jnp.float32)
         * 0.125
@@ -138,15 +139,16 @@
         * 0.125
     )
     dqkv = jnp.stack([dquery, dkey, dvalue], axis=2).reshape(seqs * L, 3 * D).astype(jnp.bfloat16)
-    qkv_piece = WorkerPiece(act, dqkv)
+    (dqkv,) = up.crossed(dqkv)
+    if up.paired:
+        up.finish()
+    mixed = WorkerPiece((act, dqkv), (out, dattn))
     dxzero = drone + matmul_nt(dqkv, weights[:, 0 : 3 * D])
     _, pull = jax.vjp(norm_rows, embedded, small[base], small[base + 1])
     dembed, dgain_emb, dshift_emb = pull(dxzero)
-    dembed, _ = after(dembed, *qkv_piece.waits(), *attn.waits_across())
-    qkv_piece.across()
-    grads = jnp.concatenate(
-        [qkv_piece.finish(), attn.finish(), up.finish(), grad_down], axis=1
-    )
+    dembed = mixed.received(dembed)
+    if down.paired:
+        dembed, down.result = together(dembed, down.result)
     bias_qkv = jnp.sum(dqkv, axis=0, dtype=jnp.float32)
     vectors = jnp.stack(
         [
@@ -163,15 +165,15 @@
         ]
     )
     bias_up = jnp.sum(dupper, axis=0, dtype=jnp.float32).reshape(FF // D, D)
-    return (dembed, jnp.concatenate([vectors, bias_up], axis=0), grads)
+    return (dembed, jnp.concatenate([vectors, bias_up], axis=0), (mixed, up, down))
 
 
 def paired_mesh():
     return lax.axis_size("wide") == 8 and lax.axis_size("narrow") == 4
 
 
-def after(values, *awaited):
-    return lax.optimization_barrier((values, awaited))
+def together(*values):
+    return lax.optimization_barrier(values)
 
 
 def swap_pairs(size, bit):
@@ -250,45 +252,53 @@
 
 
 class WorkerPiece:
-    def __init__(self, left, right):
-        self.left, self.right = left, right
+    def __init__(self, *pairs):
+        self.pairs = pairs
         self.paired = paired_mesh()
         if not self.paired:
             return
         self.core = lax.axis_index("wide") % 2
         self.pair, self.side = lax.axis_index("narrow") // 2, lax.axis_index("narrow") % 2
         cores = swap_pairs(lax.axis_size("wide"), 1)
-        self.far = lax.ppermute(self.low(1 - self.core, 1 - self.side), "wide", cores)
-        self.near = lax.ppermute(self.low(1 - self.core, self.side), "wide", cores)
-
-    def block(self, core, side):
+        self.far = lax.ppermute(self.block(1 - self.core, 1 - self.side), "wide", cores)
+        self.near = lax.ppermute(self.block(1 - self.core, self.side), "wide", cores)
+
+    def block(self, core, side, *terms):
         rows = D // lax.axis_size("narrow")
-        part = lax.dynamic_slice_in_dim(self.left, (2 * core + side) * rows, rows, 1)
-        return matmul_tn(part, self.right)
-
-    def low(self, core, side):
-        return self.block(core, side).astype(jnp.bfloat16)
-
-    def waits(self):
-        return (self.far, self.near) if self.paired else ()
+        blocks, start = [], 0
+        for left, right in self.pairs:
+            part = lax.dynamic_slice_in_dim(left, (2 * core + side) * rows, rows, 1)
+            total = matmul_tn(part, right)
+            for term in terms:
+                total = total + term[:, start : start + right.shape[1]].astype(jnp.float32)
+            blocks.append(total.astype(jnp.bfloat16))
+            start += right.shape[1]
+        return blocks[0] if len(blocks) == 1 else jnp.concatenate(blocks, axis=1)
+
+    def received(self, value):
+        if self.paired:
+            value, self.far, self.near = together(value, self.far, self.near)
+        return value
 
     def across(self):
         if self.paired:
-            away = self.block(self.core, 1 - self.side) + self.far.astype(jnp.float32)
             sides = swap_pairs(lax.axis_size("narrow"), 1)
-            self.away = lax.ppermute(away.astype(jnp.bfloat16), "narrow", sides)
-
-    def waits_across(self):
-        return (self.away,) if self.paired else ()
+            away = self.block(self.core, 1 - self.side, self.far)
+            self.away = lax.ppermute(away, "narrow", sides)
+
+    def crossed(self, *values):
+        if self.paired:
+            *values, self.away = together(*values, self.away)
+        return values
 
     def finish(self):
         if not self.paired:
-            grad = matmul_tn(self.left, self.right).astype(jnp.bfloat16)
-            return lax.psum_scatter(grad, "narrow", scatter_dimension=0, tiled=True)
+            blocks = [matmul_tn(left, right).astype(jnp.bfloat16) for left, right in self.pairs]
+            grad = jnp.concatenate(blocks, axis=1)
+            self.result = lax.psum_scatter(grad, "narrow", scatter_dimension=0, tiled=True)
+            return
         n_wide, n_narrow = lax.axis_size("wide"), lax.axis_size("narrow")
-        total = self.block(self.core, self.side)
-        total = total + self.near.astype(jnp.float32) + self.away.astype(jnp.float32)
-        total = total.astype(jnp.bfloat16)
+        total = self.block(self.core, self.side, self.near, self.away)
         moves = []
         for wide in range(n_wide):
             for narrow in range(n_narrow):
@@ -297,17 +307,20 @@
                     target = target_wide * n_narrow + 2 * (wide % 2) + narrow % 2
                     moves.append((wide * n_narrow + narrow, target))
         moved = lax.ppermute(total, ("wide", "narrow"), moves)
-        return jnp.where(self.pair == self.core, total, moved)
+        self.result = jnp.where(self.pair == self.core, total, moved)
 
 
 def hosted_rows(token_ids, mlm_labels, mlm_valid, doc_ids, mlm_pos):
     n_wide, n_narrow = lax.axis_size("wide"), lax.axis_size("narrow")
-    core = lax.axis_index("wide") % 2
-    packed = jnp.concatenate([token_ids, mlm_labels, mlm_valid], axis=1)
-    other = lax.ppermute(packed, "wide", swap_pairs(n_wide, 1))
-    both = jnp.where(core == 0, jnp.stack([packed, other]), jnp.stack([other, packed]))
-    both = both.reshape(2, 2, 2, packed.shape[1])
-    column = lax.dynamic_index_in_dim(both, core, 2, keepdims=False).reshape(4, packed.shape[1])
+    packed = jnp.concatenate([token_ids, mlm_labels, mlm_valid], axis=1)[None]
+    for bit, place in zip((1, 2, 4), wide_places()):
+        other = lax.ppermute(packed, "wide", swap_pairs(n_wide, bit))
+        first, second = jnp.where(place == 0, packed, other), jnp.where(place == 0, other, packed)
+        packed = jnp.concatenate([first, second], axis=0)
+    width = packed.shape[2]
+    hosted = packed.reshape(n_wide // 2, 2, 2, 2, width).transpose(1, 2, 0, 3, 4)
+    hosted = hosted.reshape(n_narrow, n_wide, width)
+    column = lax.dynamic_index_in_dim(hosted, lax.axis_index("wide"), 1, keepdims=False)
     moves = []
     for wide in range(n_wide):
         for row in range(n_narrow):
@@ -316,12 +329,101 @@
             moves.append((wide * n_narrow + row, target_wide * n_narrow + target_narrow))
     own = lax.ppermute(jnp.concatenate([doc_ids, mlm_pos], axis=1), ("wide", "narrow"), moves)
     return (
-        column[:, 0:L],
+        hosted[:, :, 0:L],
         column[:, L : L + MPS],
         column[:, L + MPS :],
         own[:, 0:L],
         own[:, L:],
     )
+
+
+FREE = pl.CostEstimate(flops=0, bytes_accessed=0, transcendentals=0)
+STREAMS = 4
+
+
+def take_kernel(ids_ref, table_ref, out_ref, held, rows):
+    step, count, size = pl.program_id(0), out_ref.shape[0], table_ref.shape[0]
+
+    @pl.when(step == 0)
+    def _():
+        held[0:size, :] = table_ref[...]
+        held[size:, :] = jnp.zeros((8, table_ref.shape[1]), jnp.float32)
+
+    @pl.loop(0, count, step=16)
+    def _(first):
+        for by in range(16):
+            place = ids_ref[step * count + first + by]
+            rows[pl.ds(first + by, 1), :] = held[pl.ds(place, 1), :]
+
+    out_ref[...] = rows[...].astype(out_ref.dtype)
+
+
+def taken_rows(ids, table):
+    size, cols = table.shape
+    chunk = 2048
+    return pl.pallas_call(
+        take_kernel,
+        grid_spec=pltpu.PrefetchScalarGridSpec(
+            num_scalar_prefetch=1,
+            grid=(ids.shape[0] // chunk,),
+            in_specs=[pl.BlockSpec((size, cols), lambda step, ids: (0, 0))],
+            out_specs=pl.BlockSpec((chunk, cols), lambda step, ids: (step, 0)),
+            scratch_shapes=[
+                pltpu.VMEM((size + 8, cols), jnp.float32),
+                pltpu.VMEM((chunk, cols), jnp.float32),
+            ],
+        ),
+        out_shape=jax.ShapeDtypeStruct((ids.shape[0], cols), jnp.bfloat16),
+        compiler_params=pltpu.CompilerParams(vmem_limit_bytes=32 * 2**20),
+        cost_estimate=FREE,
+        name="take_rows",
+    )(ids, table)
+
+
+def add_kernel(ids_ref, rows_ref, out_ref, rows, *sums):
+    step, count, size = pl.program_id(0), rows_ref.shape[1], out_ref.shape[0]
+    stream = pl.num_programs(0) * count
+
+    @pl.when(step == 0)
+    def _():
+        for part in sums:
+            part[...] = jnp.zeros_like(part)
+
+    rows[...] = rows_ref[...].astype(jnp.float32)
+
+    @pl.loop(0, count, step=8)
+    def _(first):
+        for by in range(8):
+            for index, part in enumerate(sums):
+                place = ids_ref[index * stream + step * count + first + by]
+                part[pl.ds(place, 1), :] += rows[index, pl.ds(first + by, 1), :]
+
+    @pl.when(step == pl.num_programs(0) - 1)
+    def _():
+        total = sums[0][0:size, :]
+        for part in sums[1:]:
+            total = total + part[0:size, :]
+        out_ref[...] = total
+
+
+def added_rows(ids, values, size):
+    count, cols = values.shape
+    chunk = 512
+    return pl.pallas_call(
+        add_kernel,
+        grid_spec=pltpu.PrefetchScalarGridSpec(
+            num_scalar_prefetch=1,
+            grid=(count // STREAMS // chunk,),
+            in_specs=[pl.BlockSpec((STREAMS, chunk, cols), lambda step, ids: (0, step, 0))],
+            out_specs=pl.BlockSpec((size, cols), lambda step, ids: (0, 0)),
+            scratch_shapes=[pltpu.VMEM((STREAMS, chunk, cols), jnp.float32)]
+            + [pltpu.VMEM((size + 8, cols), jnp.float32)] * STREAMS,
+        ),
+        out_shape=jax.ShapeDtypeStruct((size, cols), jnp.float32),
+        compiler_params=pltpu.CompilerParams(vmem_limit_bytes=40 * 2**20),
+        cost_estimate=FREE,
+        name="add_rows",
+    )(ids, values.reshape(STREAMS, count // STREAMS, cols))
 
 
 def wide_places():
@@ -406,32 +508,37 @@
     worker_err,
     server_err,
 ):
-    n_wide = lax.axis_size("wide")
+    n_wide, n_narrow = lax.axis_size("wide"), lax.axis_size("narrow")
     narrow_me = lax.axis_index("narrow")
     wide_me = lax.axis_index("wide")
     seqs = doc_ids.shape[0]
     paired = paired_mesh()
+    vshard = table.shape[0]
     count = summed_over(jnp.sum(mlm_valid.astype(jnp.float32)), "wide")
+    table_low, layer_low = table.astype(jnp.bfloat16), layer.astype(jnp.bfloat16)
     if paired:
         token_ids, mlm_labels, mlm_valid, doc_ids, mlm_pos = hosted_rows(
             token_ids, mlm_labels, mlm_valid, doc_ids, mlm_pos
         )
-    table_cols = lax.all_gather(table.astype(jnp.bfloat16), "wide", axis=1, tiled=True)
-    if paired:
-        layer_rows = chain_gather(layer.astype(jnp.bfloat16))
+        layer_rows = chain_gather(layer_low)
     else:
-        layer_rows = lax.all_gather(layer.astype(jnp.bfloat16), "narrow", axis=0, tiled=True)
-    layer_rows, (table_cols,) = after(layer_rows, table_cols)
+        layer_rows = lax.all_gather(layer_low, "narrow", axis=0, tiled=True)
     weights = lax.all_gather(layer_rows, "wide", axis=1, tiled=True)
-    vshard = table_cols.shape[0]
     local_ids = token_ids - narrow_me * vshard
     inside = (local_ids >= 0) & (local_ids < vshard)
-    picked = jnp.take(table_cols, jnp.clip(local_ids, 0, vshard - 1), axis=0)
-    picked = jnp.where(inside[..., None], picked.astype(jnp.float32), 0.0)
-    picked = picked.astype(jnp.bfloat16)
     if paired:
-        looked = chain_scatter(picked)[None]
+        slots = jnp.where(inside, local_ids, vshard).reshape(-1)
+        picked = taken_rows(slots, table).reshape(n_narrow, n_wide * L, -1)
+        looked = chain_scatter(picked).reshape(n_wide, L, -1)
+        looked = lax.all_to_all(looked, "wide", 0, 0)
+        looked = looked.transpose(1, 0, 2).reshape(1, L, D)
+        table_low, weights = together(table_low, weights)
+        table_cols = lax.all_gather(table_low, "wide", axis=1, tiled=True)
     else:
+        slots = jnp.where(inside, local_ids, vshard).reshape(-1)
+        table_cols = lax.all_gather(table_low, "wide", axis=1, tiled=True)
+        picked = jnp.take(table_cols, jnp.clip(local_ids, 0, vshard - 1), axis=0)
+        picked = jnp.where(inside[..., None], picked, 0.0)
         looked = lax.psum_scatter(picked, "narrow", scatter_dimension=0, tiled=True)
     looked = looked.astype(jnp.float32)
     even_doc = (doc_ids % 2 == 0)[..., None]
@@ -469,13 +576,12 @@
         dhmask = scattered_near(dhmask)
     else:
         dhmask = lax.psum_scatter(dhmask, "narrow", scatter_dimension=0, tiled=True)
-    table_head = matmul_tn(dlogit, group_h)
     dhtwo = (
         jnp.zeros((seqs, L, D), jnp.float32)
         .at[jnp.arange(seqs)[:, None], mlm_pos]
         .add(dhmask.reshape(seqs, MPS, D))
     )
-    dembed, vectors, worker_grad = layer_backward(
+    dembed, vectors, pieces = layer_backward(
         dhtwo.reshape(seqs * L, D), kept, doc_ids, small, weights
     )
     dembed_rows = dembed.reshape(seqs, L, D)
@@ -484,13 +590,42 @@
     small_grad = jnp.concatenate(
         [jnp.sum(dembed_rows, axis=0), seg_even[None], seg_odd[None], vectors], axis=0
     )
-    group_rows = lax.all_gather(dembed_rows.astype(jnp.bfloat16), "narrow", axis=0, tiled=True)
-    slots = jnp.where(inside, local_ids, vshard).reshape(-1)
-    table_grad = table_head.at[slots].add(
-        group_rows.reshape(-1, D).astype(jnp.float32), mode="drop"
-    )
-    cut = table_grad.astype(jnp.bfloat16).reshape(vshard, n_wide, D // n_wide).transpose(1, 0, 2)
-    table_grad = lax.psum_scatter(cut, "wide", scatter_dimension=0).astype(jnp.float32)
+    mixed = pieces[0]
+    if paired:
+        cut = dembed.astype(jnp.bfloat16).reshape(L, n_wide, D // n_wide).transpose(1, 0, 2)
+        cut = lax.all_to_all(cut, "wide", 0, 0).reshape(n_wide * L, D // n_wide)
+        cut, small_grad, dlogit = together(mixed.received(cut), small_grad, dlogit)
+        mixed.across()
+        group_rows = lax.all_gather(cut, "narrow", axis=0, tiled=True)
+        (group_rows,) = mixed.crossed(group_rows)
+        mixed.finish()
+        blocks = group_h.reshape(-1, n_wide, D // n_wide)
+        table_head = jnp.einsum("sv,swc->wvc", dlogit, blocks, preferred_element_type=jnp.float32)
+        table_head = table_head.astype(jnp.bfloat16)
+        table_head = lax.psum_scatter(table_head, "wide", scatter_dimension=0)
+        table_grad = added_rows(slots, group_rows, vshard)
+        table_grad = table_grad + table_head.astype(jnp.float32)
+    else:
+        mixed.finish()
+        pieces[1].finish()
+        pieces[2].finish()
+        group_rows = lax.all_gather(dembed_rows.astype(jnp.bfloat16), "narrow", axis=0, tiled=True)
+        table_grad = matmul_tn(dlogit, group_h).at[slots].add(
+            group_rows.reshape(-1, D).astype(jnp.float32), mode="drop"
+        )
+        cut = table_grad.astype(jnp.bfloat16).reshape(vshard, n_wide, D // n_wide)
+        table_grad = lax.psum_scatter(cut.transpose(1, 0, 2), "wide", scatter_dimension=0)
+        table_grad = table_grad.astype(jnp.float32)
+    small_grad = small_total(small_grad)
+    small_mom = BETA * small_m + (1.0 - BETA) * small_grad
+    small_upd = small_mom / (jnp.sqrt(small_v) + OPT_EPS) + DECAY * small
+    small_norms = (jnp.sum(small * small)[None], jnp.sum(small_upd * small_upd)[None])
+    table_mom = BETA * table_m + (1.0 - BETA) * table_grad
+    table_upd = table_mom / (jnp.sqrt(table_v) + OPT_EPS) + DECAY * table
+    table_norms = (jnp.sum(table * table)[None], jnp.sum(table_upd * table_upd)[None])
+    worker_grad = jnp.concatenate([piece.result for piece in pieces], axis=1)
+    if paired:
+        worker_grad, table_norms, small_norms = together(worker_grad, table_norms, small_norms)
     span = BETA * layer_m + (1.0 - BETA) * worker_grad.astype(jnp.float32) + worker_err[0]
     scale = jnp.mean(jnp.abs(span)) + MAG_EPS
     sent = scale * jnp.tanh(span / scale)
@@ -514,24 +649,11 @@
     onehot = (which[:, None] == jnp.arange(4)[None]).astype(jnp.float32)
     wsq = jnp.sum(jnp.sum(layer * layer, axis=0)[:, None] * onehot, axis=0)
     usq = jnp.sum(jnp.sum(layer_upd * layer_upd, axis=0)[:, None] * onehot, axis=0)
-    table_mom = BETA * table_m + (1.0 - BETA) * table_grad
-    table_upd = table_mom / (jnp.sqrt(table_v) + OPT_EPS) + DECAY * table
-    parts = jnp.concatenate(
-        [
-            wsq,
-            usq,
-            jnp.sum(table * table)[None],
-            jnp.sum(table_upd * table_upd)[None],
-            jnp.sum(own_loss)[None],
-        ]
-    )
-    small_grad = small_total(small_grad)
+    parts = jnp.concatenate([wsq, usq, *table_norms, jnp.sum(own_loss)[None]])
     sums = summed_over(summed_over(parts, "wide"), "narrow")
     loss_sum = sums[10]
-    small_mom = BETA * small_m + (1.0 - BETA) * small_grad
-    small_upd = small_mom / (jnp.sqrt(small_v) + OPT_EPS) + DECAY * small
-    wnorm = jnp.sqrt(jnp.concatenate([sums[0:4], sums[8:9], jnp.sum(small * small)[None]]))
-    unorm = jnp.sqrt(jnp.concatenate([sums[4:8], sums[9:10], jnp.sum(small_upd * small_upd)[None]]))
+    wnorm = jnp.sqrt(jnp.concatenate([sums[0:4], sums[8:9], small_norms[0]]))
+    unorm = jnp.sqrt(jnp.concatenate([sums[4:8], sums[9:10], small_norms[1]]))
     ratio = wnorm / unorm
     new_layer = layer - RATE * jnp.sum(onehot * ratio[None, 0:4], axis=1)[None] * layer_upd
     new_table = table - RATE * ratio[4] * table_upd

time: 1110 us -> 1120 us (level)
  starting transfers between devices: 178 us -> 110 us
  waiting for transfers between devices: 420 us -> 478 us
  Pallas kernels: 0 us -> 52.4 us
  other arithmetic: 197 us -> 177 us
    all_gather x1, waiting for transfers between devices: 0.02 us -> 84.1 us  [shards(): weights = lax.all_gather(layer_rows, 'wide', axis=1, tiled=True)]
    ppermute x2, waiting for transfers between devices: 11.8 us -> 94.2 us  [small_total(): other = lax.ppermute(low, 'narrow', swap_pairs(n_narrow, bit))]
    ppermute x4, starting transfers between devices: 107 us -> 29.3 us  [scattered_sum(): lax.ppermute(part_of, 'wide', swap_pairs(n_wide, 1))]
    ppermute x13 -> x12, waiting for transfers between devices: 135 us -> 74.8 us  [the longest x3 68.8 us: across(): self.away = lax.ppermute(away, 'narrow', sides)]
    pallas_call x0 -> x2, Pallas kernels: none -> 52.4 us  [the longest x1 32.2 us: added_rows(): pl.pallas_call(add_kernel, grid_spec=pltpu.PrefetchScalarGridSpec(num_sca...]
    scatter-add x1 -> x0, other arithmetic: 39.6 us -> none  [shards(): table_head.at[slots]]
    ppermute x3, waiting for transfers between devices: 61.9 us -> 27.1 us  [chain_scatter(): rising = lax.ppermute(up, 'narrow', [(i, i + 1) for i in range(step)])]
    dot_general x0 -> x2, matrix products: none -> 28.6 us  [the longest x1 14.5 us: layer_backward(): jnp.einsum('sqhd,skhd->shqk', dout, heads[:, :, 2], preferred_element_typ...]
  transfers between devices with their start and end apart: 70 -> 70, of which waited for: 45 -> 43; matrix products, arithmetic and copies ran while one was open for 26% -> 26% of each run, Pallas kernels for 0% -> 5%
where the time goes in v3:
time: 1120 us; the launch traced here: 1110 us
  waiting for transfers between devices  478 us (43%)
  matrix products  211 us (19%)
  other arithmetic  177 us (16%)
  starting transfers between devices  110 us (10%)
  local copies, waits for them, and re-layouts  63.8 us (6%)
  Pallas kernels  52.4 us (5%)
  between operations  21.4 us (2%)
    ppermute x2, waiting for transfers between devices, small_total(): other = lax.ppermute(low, 'narrow', swap_pairs(n_narrow, bit))  94.2 us
    all_gather x1, waiting for transfers between devices, shards(): weights = lax.all_gather(layer_rows, 'wide', axis=1, tiled=True)  84.1 us
    ppermute x3, waiting for transfers between devices, across(): self.away = lax.ppermute(away, 'narrow', sides)  68.8 us
    dot_general x5, matrix products, matmul(): return jnp.dot(left, right, preferred_element_type=jnp.float32)  60.3 us
    dot_general x16, matrix products, matmul_tn(): lax.dot_general(left, right, (((0,), (0,)), ((), ())), preferred_element_...  42.7 us
    dot_general x5, matrix products, matmul_nt(): lax.dot_general(left, right, (((1,), (1,)), ((), ())), preferred_element_...  40.4 us
    ppermute x3, waiting for transfers between devices, chain_gather(): lax.ppermute(falling, 'narrow', [(i, i - 1) for i in range(1, size - step...  35.3 us
    pallas_call x1, Pallas kernels, added_rows(): pl.pallas_call(add_kernel, grid_spec=pltpu.PrefetchScalarGridSpec(num_sca...  32.2 us
  transfers between devices with their start and end apart: 70, of which 43 were waited for; matrix products, arithmetic and copies ran while one was open for 26% of the time, Pallas kernels for 5%

profile of v3, /device:TPU:0, one launch (start us, length us, event | category | flops | bytes accessed | tf_op | source)
XLA Modules:
  0.0 1113.8 jit_solution(3921567817322611614)
XLA Ops:
  8.8 5.0 collective-permute-start.10
  15.1 15.4 %collective-permute-done.10 = bf16[256,1536]{1,0:T(8,128)(2,1)S(1)} collective-permute-done((bf16[256,1536]{1,0:T(8,128)(2,1)S(1)}, bf16[256,1536]{1,0:T(8,128)(2,1)S(1)}, u32[]{:S(2)}, u32[]{:S(2)}) %collective-permute-start.10) | collective-permute-done | bytes 786464 | tf_op jit(solution)/shard_map/ppermute | solution.py:228
  37.6 18.2 %collective-permute-done.14 = bf16[256,1536]{1,0:T(8,128)(2,1)} collective-permute-done((bf16[256,1536]{1,0:T(8,128)(2,1)S(1)}, bf16[256,1536]{1,0:T(8,128)(2,1)}, u32[]{:S(2)}, u32[]{:S(2)}) %collective-permute-start.14) | collective-permute-done | bytes 786464 | tf_op jit(solution)/shard_map/ppermute | solution.py:229
  60.9 14.5 %collective-permute-done.15 = bf16[256,1536]{1,0:T(8,128)(2,1)S(1)} collective-permute-done((bf16[256,1536]{1,0:T(8,128)(2,1)}, bf16[256,1536]{1,0:T(8,128)(2,1)S(1)}, u32[]{:S(2)}, u32[]{:S(2)}) %collective-permute-start.15) | collective-permute-done | bytes 786464 | tf_op jit(solution)/shard_map/ppermute | solution.py:229
  90.4 20.2 %take_rows.1 = bf16[16384,128]{1,0:T(8,128)(2,1)S(1)} custom-call(s32[16384]{0:T(1024)S(1)} %bitcast.257, f32[7632,128]{1,0:T(8,128)S(1)} %copy-done), custom_call_target="tpu_custom_call" | custom-call | tf_op jit(solution)/shard_map/take_rows/pallas_call | solution.py:364
  114.7 3.6 convert_element_type.368
  119.9 84.1 %all-gather.5.cloned.1.call-done = bf16[1024,12288]{1,0:T(8,128)(2,1)} async-done(((bf16[1024,1536]{1,0:T(8,128)(2,1)}), bf16[1024,12288]{1,0:T(8,128)(2,1)}) %all-gather.5.cloned.1.call-update) | async-done | bytes 25165840 | tf_op jit(solution)/shard_map/all_gather | solution.py:526
  205.4 4.4 collective-permute-start.4
  209.8 21.8 %collective-permute-done.4 = bf16[4096,128]{1,0:T(8,128)(2,1)} collective-permute-done((bf16[4096,128]{1,0:T(8,128)(2,1)S(1)}, bf16[4096,128]{1,0:T(8,128)(2,1)}, u32[]{:S(2)}, u32[]{:S(2)}) %collective-permute-start.4) | collective-permute-done | bytes 1048608 | tf_op jit(solution)/shard_map/ppermute | solution.py:249
  236.5 5.1 collective-permute-start.5
  259.7 5.2 collective-permute-done.5
  264.9 24.4 %collective-permute-done.8 = bf16[4096,128]{1,0:T(8,128)(2,1)S(1)} collective-permute-done((bf16[4096,128]{1,0:T(8,128)(2,1)S(1)}, bf16[4096,128]{1,0:T(8,128)(2,1)S(1)}, u32[]{:S(2)}, u32[]{:S(2)}) %collective-permute-start.8) | collective-permute-done | bytes 1048608 | tf_op jit(solution)/shard_map/ppermute | solution.py:250
  291.9 3.6 all-to-all-start
  300.7 10.2 all-to-all-done
  314.8 7.6 add_convert_fusion.1
  322.4 5.1 copy.60
  327.5 9.9 fusion
  337.4 9.2 exponential_reduce_fusion
  346.7 10.2 convolution_convert_fusion.6
  361.5 26.0 %multiply_convert_fusion.1 = (bf16[512,4096]{1,0:T(8,128)(2,1)S(1)}, f32[512,4096]{1,0:T(8,128)}, f32[512,4096]{1,0:T(8,128)}) fusion(f32[4096]{0:T(1024)S(1)} %bitcast.303, bf16[512,1024]{1,0:T(8,128)(2,1)S(1)} %fusion.43, bf16[1024,12288]{1,0:T(8,128)(2,1)} %all-gather.5.cloned.1.call-done), kind=kOutput, calls=%fused_computation.26 | convolution fusion | flops 4433379328 | bytes 30425088 | tf_op jit(solution)/shard_map/dot_general | solution.py:45
  387.6 9.2 fusion.172
  408.7 7.5 collective-permute-done.17
  419.6 9.3 fusion.173
  438.9 5.2 fusion.4
  444.1 10.0 fusion.174
  457.6 5.5 collective-permute-done.27
  463.1 5.2 collective-permute-done.26
  486.3 13.1 %add_convert_fusion = bf16[512,4096]{1,0:T(8,128)(2,1)S(1)} fusion(f32[512,4096]{1,0:T(8,128)} %get-tuple-element.123, f32[512,4096]{1,0:T(8,128)} %get-tuple-element.195, f32[4096]{0:T(1024)} %bitcast.302, bf16[512,1024]{1,0:T(8,128)(2,1)S(1)} %get-tuple-element.111, bf16[1024,12288]{1,0:T(8,128)(2,1)} %all-gather.5.cloned.1.call-done), kind=kOutput, calls=%fused_computation.25 | convolution fusion | flops 4326424576 | bytes 30425088 | tf_op jit(solution)/shard_map/dot_general | solution.py:45
  499.4 12.7 %multiply_reduce_fusion.6 = (f32[1024]{0:T(1024)}, f32[512]{0:T(512)S(1)}, f32[1024]{0:T(1024)}, f32[512,1024]{1,0:T(8,128)}) fusion(f32[512,1024]{1,0:T(8,128)S(1)} %copy-done.20, f32[512]{0:T(512)S(1)} %copy-done.65, f32[512]{0:T(512)S(1)} %broadcast_multiply_fusion.2, f32[1024]{0:T(1024)S(1)} %bitcast.291, bf16[512,4096]{1,0:T(8,128)(2,1)S(1)} %add_convert_fusion, ...), kind=kOutput, calls=%fused_computation.101 | convolution fusion | flops 4300207616 | bytes 18894848 | tf_op jit(solution)/shard_map/dot_general | solution.py:55
  529.3 11.3 %convolution_bitcast_fusion = bf16[1,512,16,64]{1,3,2,0:T(8,128)(2,1)} fusion(bf16[512,16,64]{0,2,1:T(8,128)(2,1)} %bitcast.272, f32[16,512,512]{1,2,0:T(8,128)} %get-tuple-element.192, f32[16,512]{1,0:T(8,128)S(1)} %copy-done.56, pred[512,512]{0,1:T(8,128)(4,1)S(1)} %copy-done.36), kind=kOutput, calls=%fused_computation.131 | convolution fusion | flops 553648128 | bytes 19169280 | tf_op jit(solution)/shard_map/shqk,sqhd->skhd/dot_general | solution.py:125
  540.5 25.5 %collective-permute-done.32 = bf16[256,4096]{1,0:T(8,128)(2,1)} collective-permute-done((bf16[256,4096]{1,0:T(8,128)(2,1)}, bf16[256,4096]{1,0:T(8,128)(2,1)}, u32[]{:S(2)}, u32[]{:S(2)}) %collective-permute-start.32) | collective-permute-done | bytes 2097184 | tf_op jit(solution)/shard_map/ppermute | solution.py:287
  566.0 14.5 %multiply_reduce_fusion = (f32[16,512]{1,0:T(8,128)S(1)}, f32[16,512,512]{1,2,0:T(8,128)}) fusion(f32[16,512,512]{1,2,0:T(8,128)} %get-tuple-element.192, f32[16,512]{1,0:T(8,128)S(1)} %copy-done.56, pred[512,512]{0,1:T(8,128)(4,1)S(1)} %copy-done.36, bf16[1,512,3,16,64]{1,4,3,2,0:T(8,128)(2,1)S(1)} %bitcast.269, bf16[1,512,16,64]{1,3,2,0:T(8,128)(2,1)} %bitcast.273), kind=kOutput, calls=%fused_computation.3 | convolution fusion | flops 557834240 | bytes 35979264 | tf_op jit(solution)/shard_map/sqhd,skhd->shqk/dot_general | solution.py:131
  580.5 5.7 fusion.26
  586.5 4.6 add_convert_fusion.2
  593.1 11.3 %multiply_convert_fusion = bf16[16,512,512]{1,2,0:T(8,128)(2,1)} fusion(f32[16,512,512]{1,2,0:T(8,128)} %get-tuple-element.202, f32[16,512,512]{1,2,0:T(8,128)S(1)} %bitcast.260, f32[16,512]{1,0:T(8,128)S(1)} %get-tuple-element.201, f32[16,512]{1,0:T(8,128)S(1)} %copy-done.56, pred[512,512]{0,1:T(8,128)(4,1)S(1)} %copy-done.36), kind=kLoop, calls=%fused_computation.2 | loop fusion | flops 25165824 | bytes 42270720 | tf_op jit(solution)/shard_map/convert_element_type | solution.py:132
  604.5 6.2 fusion.57
  612.5 43.3 %collective-permute-done.33 = bf16[256,4096]{1,0:T(8,128)(2,1)} collective-permute-done((bf16[256,4096]{1,0:T(8,128)(2,1)}, bf16[256,4096]{1,0:T(8,128)(2,1)}, u32[]{:S(2)}, u32[]{:S(2)}) %collective-permute-start.33) | collective-permute-done | bytes 2097184 | tf_op jit(solution)/shard_map/ppermute | solution.py:287
  660.4 6.3 multiply_reduce_fusion.7
  667.6 3.9 broadcast_select_fusion.2
  673.8 6.5 all-to-all-start.1
  684.2 7.1 concatenate.111
  691.3 4.6 all-to-all-done.1
  696.0 14.1 %convert_bitcast_fusion = bf16[8,7632,128]{2,1,0:T(8,128)(2,1)} fusion(bf16[320,7632]{1,0:T(8,128)(2,1)} %fusion.4, bf16[560,1024]{1,0:T(8,128)(2,1)} %constant_dynamic-update-slice_fusion.7, s32[]{:T(128)S(6)} %select_n.350), kind=kOutput, calls=%fused_computation.7 | convolution fusion | flops 5009522688 | bytes 21200900 | tf_op jit(solution)/shard_map/sv,swc->wvc/dot_general | solution.py:603
  718.6 6.7 collective-permute-done.41
  731.9 87.8 %collective-permute-done.43 = bf16[528,128]{1,0:T(8,128)(2,1)S(1)} collective-permute-done((bf16[528,128]{1,0:T(8,128)(2,1)S(1)}, bf16[528,128]{1,0:T(8,128)(2,1)S(1)}, u32[]{:S(2)}, u32[]{:S(2)}) %collective-permute-start.43) | collective-permute-done | bytes 135200 | tf_op jit(solution)/shard_map/ppermute | solution.py:482
  822.4 6.4 collective-permute-done.44
  830.5 8.8 fusion.25
  861.0 32.2 %add_rows.1 = f32[7632,128]{1,0:T(8,128)S(1)} custom-call(s32[16384]{0:T(1024)S(1)} %bitcast.258, bf16[4,4096,128]{2,1,0:T(8,128)(2,1)S(1)} %bitcast.256), custom_call_target="tpu_custom_call" | custom-call | tf_op jit(solution)/shard_map/add_rows/pallas_call | solution.py:412
  896.2 6.2 pad_maximum_fusion
  902.4 27.9 %reduce-scatter.2.cloned.1.call-done = bf16[1,7632,128]{2,1,0:T(8,128)(2,1)} async-done(((bf16[8,7632,128]{2,1,0:T(8,128)(2,1)}), bf16[1,7632,128]{2,1,0:T(8,128)(2,1)}) %reduce-scatter.2.cloned.1.call-update) | async-done | bytes 1953808 | tf_op jit(solution)/shard_map/reduce_scatter | solution.py:605
  930.3 10.0 multiply_reduce_fusion.1
  940.3 15.5 %abs_reduce_fusion = (f32[]{:T(128)}, f32[256,12288]{1,0:T(8,128)}) fusion(f32[1,256,12288]{2,1,0:T(8,128)} %param.30, bf16[256,12288]{1,0:T(8,128)(2,1)S(1)} %copy-done.17, f32[256,12288]{1,0:T(8,128)} %param.28), kind=kLoop, calls=%fused_computation.12 | loop fusion | flops 22020096 | bytes 44040196 | tf_op jit(solution)/shard_map/reduce_sum | solution.py:630
  956.4 10.6 subtract_bitcast_fusion
  967.0 4.8 copy-done.11
  973.6 28.8 %collective-permute-start.48 = (bf16[256,1536]{1,0:T(8,128)(2,1)}, bf16[256,1536]{1,0:T(8,128)(2,1)S(1)}, u32[]{:S(2)}, u32[]{:S(2)}) collective-permute-start(bf16[256,1536]{1,0:T(8,128)(2,1)} %get-tuple-element.132), channel_id=1, source_target_pairs={{0,4},{4,0},{8,12},{12,8},{16,20},{20,16},{24,28},{28,24},{1,5},{5... | collective-permute-start | bytes 2359304 | tf_op jit(solution)/shard_map/ppermute | solution.py:447
  1007.9 4.1 add_bitcast_fusion.3
  1020.2 8.0 collective-permute-done.56
  1031.8 4.7 collective-permute-done.55
  1036.5 9.3 collective-permute-done.57
  1050.2 3.9 multiply_reduce_fusion.14
  1069.5 4.4 collective-permute-done.62
  1083.8 5.5 multiply_subtract_fusion.1
  1092.0 3.8 multiply_subtract_fusion
  1097.8 9.1 convert_element_type.473
  (485 shorter events, 247.4 us)
Async XLA Ops:
  7.2 196.9 %all-gather.5.cloned.1.call-start = ((), (), s32[]{:S(2)}) async-start(), calls=%async_computation.3 | async-start | bytes 28311552 | tf_op jit(solution)/shard_map/all_gather | solution.py:526
  8.8 21.7 %collective-permute-start.10 = (bf16[256,1536]{1,0:T(8,128)(2,1)S(1)}, bf16[256,1536]{1,0:T(8,128)(2,1)S(1)}, u32[]{:S(2)}, u32[]{:S(2)}) collective-permute-start(bf16[256,1536]{1,0:T(8,128)(2,1)S(1)} %convert_element_type.369), channel_id=1, source_target_pairs={{0,1},{1,2},{2,3},{4,5},{5,6},{6,7},{8,9},{9,10},{10,11},{12,13},{... | collective-permute-start | bytes 2359304 | tf_op jit(solution)/shard_map/ppermute | solution.py:228
  13.8 20.9 %collective-permute-start.13 = (bf16[256,1536]{1,0:T(8,128)(2,1)S(1)}, bf16[256,1536]{1,0:T(8,128)(2,1)S(1)}, u32[]{:S(2)}, u32[]{:S(2)}) collective-permute-start(bf16[256,1536]{1,0:T(8,128)(2,1)S(1)} %convert_element_type.369), channel_id=1, source_target_pairs={{1,0},{2,1},{3,2},{5,4},{6,5},{7,6},{9,8},{10,9},{11,10},{13,12},{... | collective-permute-start | bytes 2359304 | tf_op jit(solution)/shard_map/ppermute | solution.py:229
  30.6 5.5 collective-permute-start.11
  34.7 21.1 %collective-permute-start.14 = (bf16[256,1536]{1,0:T(8,128)(2,1)S(1)}, bf16[256,1536]{1,0:T(8,128)(2,1)}, u32[]{:S(2)}, u32[]{:S(2)}) collective-permute-start(bf16[256,1536]{1,0:T(8,128)(2,1)S(1)} %collective-permute-done.13), channel_id=1, source_target_pairs={{1,0},{2,1},{5,4},{6,5},{9,8},{10,9},{13,12},{14,13},{17,16},{18,1... | collective-permute-start | bytes 2359304 | tf_op jit(solution)/shard_map/ppermute | solution.py:229
  36.0 21.1 %collective-permute-start.12 = (bf16[256,1536]{1,0:T(8,128)(2,1)}, bf16[256,1536]{1,0:T(8,128)(2,1)}, u32[]{:S(2)}, u32[]{:S(2)}) collective-permute-start(bf16[256,1536]{1,0:T(8,128)(2,1)} %collective-permute-done.11), channel_id=1, source_target_pairs={{2,3},{6,7},{10,11},{14,15},{18,19},{22,23},{26,27},{30,31}} | collective-permute-start | bytes 2359304 | tf_op jit(solution)/shard_map/ppermute | solution.py:228
  55.8 19.6 %collective-permute-start.15 = (bf16[256,1536]{1,0:T(8,128)(2,1)}, bf16[256,1536]{1,0:T(8,128)(2,1)S(1)}, u32[]{:S(2)}, u32[]{:S(2)}) collective-permute-start(bf16[256,1536]{1,0:T(8,128)(2,1)} %collective-permute-done.14), channel_id=1, source_target_pairs={{1,0},{5,4},{9,8},{13,12},{17,16},{21,20},{25,24},{29,28}} | collective-permute-start | bytes 2359304 | tf_op jit(solution)/shard_map/ppermute | solution.py:229
  77.4 342.2 %all-gather.7.cloned.1.call-start = ((), (), s32[]{:S(2)}) async-start(), calls=%async_computation.4 | async-start | bytes 17584128 | tf_op jit(solution)/shard_map/all_gather | solution.py:536
  79.4 3.9 collective-permute-start.1
  83.3 4.2 collective-permute-start.2
  112.8 91.3 %collective-permute-start.3 = (bf16[4096,128]{1,0:T(8,128)(2,1)S(1)}, bf16[4096,128]{1,0:T(8,128)(2,1)S(1)}, u32[]{:S(2)}, u32[]{:S(2)}) collective-permute-start(bf16[4096,128]{1,0:T(8,128)(2,1)S(1)} %get-tuple-element.140), channel_id=1, source_target_pairs={{0,1},{4,5},{8,9},{12,13},{16,17},{20,21},{24,25},{28,29}} | collective-permute-start | bytes 3145736 | tf_op jit(solution)/shard_map/ppermute | solution.py:249
  118.3 91.5 %collective-permute-start.6 = (bf16[4096,128]{1,0:T(8,128)(2,1)S(1)}, bf16[4096,128]{1,0:T(8,128)(2,1)}, u32[]{:S(2)}, u32[]{:S(2)}) collective-permute-start(bf16[4096,128]{1,0:T(8,128)(2,1)S(1)} %get-tuple-element.141), channel_id=1, source_target_pairs={{3,2},{7,6},{11,10},{15,14},{19,18},{23,22},{27,26},{31,30}} | collective-permute-start | bytes 3145736 | tf_op jit(solution)/shard_map/ppermute | solution.py:250
  205.4 26.2 %collective-permute-start.4 = (bf16[4096,128]{1,0:T(8,128)(2,1)S(1)}, bf16[4096,128]{1,0:T(8,128)(2,1)}, u32[]{:S(2)}, u32[]{:S(2)}) collective-permute-start(bf16[4096,128]{1,0:T(8,128)(2,1)S(1)} %bitcast_add_fusion.4), channel_id=1, source_target_pairs={{0,1},{1,2},{4,5},{5,6},{8,9},{9,10},{12,13},{13,14},{16,17},{17,1... | collective-permute-start | bytes 3145736 | tf_op jit(solution)/shard_map/ppermute | solution.py:249
  235.0 6.6 collective-permute-start.7
  236.5 12.9 %collective-permute-start.22 = (f32[]{:T(128)}, f32[]{:T(128)}, u32[]{:S(2)}, u32[]{:S(2)}) collective-permute-start(f32[]{:T(128)} %convert_reduce_fusion.4), channel_id=1, source_target_pairs={{0,4},{4,0},{8,12},{12,8},{16,20},{20,16},{24,28},{28,24},{1,5},{5... | collective-permute-start | bytes 20 | tf_op jit(solution)/shard_map/ppermute | solution.py:193
  236.5 28.4 %collective-permute-start.5 = (bf16[4096,128]{1,0:T(8,128)(2,1)}, bf16[4096,128]{1,0:T(8,128)(2,1)S(1)}, u32[]{:S(2)}, u32[]{:S(2)}) collective-permute-start(bf16[4096,128]{1,0:T(8,128)(2,1)} %get-tuple-element.138), channel_id=1, source_target_pairs={{0,1},{1,2},{2,3},{4,5},{5,6},{6,7},{8,9},{9,10},{10,11},{12,13},{... | collective-permute-start | bytes 3145736 | tf_op jit(solution)/shard_map/ppermute | solution.py:249
  242.9 46.4 %collective-permute-start.8 = (bf16[4096,128]{1,0:T(8,128)(2,1)S(1)}, bf16[4096,128]{1,0:T(8,128)(2,1)S(1)}, u32[]{:S(2)}, u32[]{:S(2)}) collective-permute-start(bf16[4096,128]{1,0:T(8,128)(2,1)S(1)} %bitcast_add_fusion.3), channel_id=1, source_target_pairs={{3,2},{2,1},{1,0},{7,6},{6,5},{5,4},{11,10},{10,9},{9,8},{15,14},{... | collective-permute-start | bytes 3145736 | tf_op jit(solution)/shard_map/ppermute | solution.py:250
  244.3 14.9 %collective-permute-start.9 = (s32[1,592]{1,0:T(1,128)S(1)}, s32[1,592]{1,0:T(1,128)S(1)}, u32[]{:S(2)}, u32[]{:S(2)}) collective-permute-start(s32[1,592]{1,0:T(1,128)S(1)} %pad_add_fusion.3), channel_id=1, source_target_pairs={{0,0},{1,4},{2,1},{3,5},{4,2},{5,6},{6,3},{7,7},{8,8},{9,12},{10,9... | collective-permute-start | bytes 7112 | tf_op jit(solution)/shard_map/ppermute | solution.py:330
  250.6 3.6 collective-permute-start.23
  254.8 3.7 collective-permute-start.24
  291.9 18.9 %all-to-all-start = ((bf16[8,512,128]{2,1,0:T(8,128)(2,1)}), bf16[8,512,128]{2,1,0:T(8,128)(2,1)S(1)}, u32[]{:S(2)}, u32[]{:S(2)}) async-start(bf16[8,512,128]{2,1,0:T(8,128)(2,1)} %bitcast.10), calls=%async_computation | async-start | bytes 2097152 | tf_op jit(solution)/shard_map/all_to_all | solution.py:533
  400.8 7.2 collective-permute-start.16
  402.7 13.5 %collective-permute-start.17 = (bf16[80,1024]{1,0:T(8,128)(2,1)S(1)}, bf16[80,1024]{1,0:T(8,128)(2,1)S(1)}, u32[]{:S(2)}, u32[]{:S(2)}) collective-permute-start(bf16[80,1024]{1,0:T(8,128)(2,1)S(1)} %get-tuple-element.121), channel_id=1, source_target_pairs={{0,2},{1,3},{2,0},{3,1},{4,6},{5,7},{6,4},{7,5},{8,10},{9,11},{10,... | collective-permute-start | bytes 491528 | tf_op jit(solution)/shard_map/ppermute | solution.py:203
  404.9 12.0 %collective-permute-start.18 = (bf16[80,1024]{1,0:T(8,128)(2,1)S(1)}, bf16[80,1024]{1,0:T(8,128)(2,1)S(1)}, u32[]{:S(2)}, u32[]{:S(2)}) collective-permute-start(bf16[80,1024]{1,0:T(8,128)(2,1)S(1)} %get-tuple-element.121), channel_id=1, source_target_pairs={{0,1},{1,2},{2,3},{3,0},{4,5},{5,6},{6,7},{7,4},{8,9},{9,10},{10,1... | collective-permute-start | bytes 491528 | tf_op jit(solution)/shard_map/ppermute | solution.py:203
  431.6 3.7 collective-permute-start.19
  431.7 4.6 collective-permute-start.20
  432.7 5.4 collective-permute-start.21
  455.3 7.8 collective-permute-start.27
  457.0 11.4 %collective-permute-start.26 = (bf16[80,1024]{1,0:T(8,128)(2,1)S(1)}, bf16[80,1024]{1,0:T(8,128)(2,1)S(1)}, u32[]{:S(2)}, u32[]{:S(2)}) collective-permute-start(bf16[80,1024]{1,0:T(8,128)(2,1)S(1)} %get-tuple-element.164), channel_id=1, source_target_pairs={{0,2},{1,3},{2,0},{3,1},{4,6},{5,7},{6,4},{7,5},{8,10},{9,11},{10,... | collective-permute-start | bytes 491528 | tf_op jit(solution)/shard_map/ppermute | solution.py:217
  457.0 11.3 %collective-permute-start.25 = (bf16[80,1024]{1,0:T(8,128)(2,1)S(1)}, bf16[80,1024]{1,0:T(8,128)(2,1)S(1)}, u32[]{:S(2)}, u32[]{:S(2)}) collective-permute-start(bf16[80,1024]{1,0:T(8,128)(2,1)S(1)} %get-tuple-element.162), channel_id=1, source_target_pairs={{0,1},{1,2},{2,3},{3,0},{4,5},{5,6},{6,7},{7,4},{8,9},{9,10},{10,1... | collective-permute-start | bytes 491528 | tf_op jit(solution)/shard_map/ppermute | solution.py:217
  479.8 19.6 %collective-permute-start.28 = (bf16[256,4096]{1,0:T(8,128)(2,1)}, bf16[256,4096]{1,0:T(8,128)(2,1)S(1)}, u32[]{:S(2)}, u32[]{:S(2)}) collective-permute-start(bf16[256,4096]{1,0:T(8,128)(2,1)} %convolution_convert_fusion.3), channel_id=1, source_target_pairs={{0,4},{4,0},{8,12},{12,8},{16,20},{20,16},{24,28},{28,24},{1,5},{5... | collective-permute-start | bytes 6291464 | tf_op jit(solution)/shard_map/ppermute | solution.py:263
  482.4 17.0 %collective-permute-start.29 = (bf16[256,4096]{1,0:T(8,128)(2,1)}, bf16[256,4096]{1,0:T(8,128)(2,1)S(1)}, u32[]{:S(2)}, u32[]{:S(2)}) collective-permute-start(bf16[256,4096]{1,0:T(8,128)(2,1)} %convolution_convert_fusion.2), channel_id=1, source_target_pairs={{0,4},{4,0},{8,12},{12,8},{16,20},{20,16},{24,28},{28,24},{1,5},{5... | collective-permute-start | bytes 6291464 | tf_op jit(solution)/shard_map/ppermute | solution.py:264
  514.8 11.6 %collective-permute-start.30 = (bf16[256,4096]{1,0:T(8,128)(2,1)S(1)}, bf16[256,4096]{1,0:T(8,128)(2,1)S(1)}, u32[]{:S(2)}, u32[]{:S(2)}) collective-permute-start(bf16[256,4096]{1,0:T(8,128)(2,1)S(1)} %convolution_convert_fusion.1), channel_id=1, source_target_pairs={{0,4},{4,0},{8,12},{12,8},{16,20},{20,16},{24,28},{28,24},{1,5},{5... | collective-permute-start | bytes 6291464 | tf_op jit(solution)/shard_map/ppermute | solution.py:263
  514.9 12.8 %collective-permute-start.31 = (bf16[256,4096]{1,0:T(8,128)(2,1)S(1)}, bf16[256,4096]{1,0:T(8,128)(2,1)}, u32[]{:S(2)}, u32[]{:S(2)}) collective-permute-start(bf16[256,4096]{1,0:T(8,128)(2,1)S(1)} %convolution_convert_fusion), channel_id=1, source_target_pairs={{0,4},{4,0},{8,12},{12,8},{16,20},{20,16},{24,28},{28,24},{1,5},{5... | collective-permute-start | bytes 6291464 | tf_op jit(solution)/shard_map/ppermute | solution.py:264
  518.1 47.9 %collective-permute-start.32 = (bf16[256,4096]{1,0:T(8,128)(2,1)}, bf16[256,4096]{1,0:T(8,128)(2,1)}, u32[]{:S(2)}, u32[]{:S(2)}) collective-permute-start(bf16[256,4096]{1,0:T(8,128)(2,1)} %add_convert_fusion.3), channel_id=1, source_target_pairs={{0,1},{1,0},{2,3},{3,2},{4,5},{5,4},{6,7},{7,6},{8,9},{9,8},{10,11... | collective-permute-start | bytes 6291464 | tf_op jit(solution)/shard_map/ppermute | solution.py:287
  586.2 69.5 %collective-permute-start.33 = (bf16[256,4096]{1,0:T(8,128)(2,1)}, bf16[256,4096]{1,0:T(8,128)(2,1)}, u32[]{:S(2)}, u32[]{:S(2)}) collective-permute-start(bf16[256,4096]{1,0:T(8,128)(2,1)} %fusion.26), channel_id=1, source_target_pairs={{0,1},{1,0},{2,3},{3,2},{4,5},{5,4},{6,7},{7,6},{8,9},{9,8},{10,11... | collective-permute-start | bytes 6291464 | tf_op jit(solution)/shard_map/ppermute | solution.py:287
  591.1 76.5 %collective-permute-start.36 = (bf16[256,4096]{1,0:T(8,128)(2,1)}, bf16[256,4096]{1,0:T(8,128)(2,1)}, u32[]{:S(2)}, u32[]{:S(2)}) collective-permute-start(bf16[256,4096]{1,0:T(8,128)(2,1)} %add_convert_fusion.2), channel_id=1, source_target_pairs={{2,4},{3,5},{4,2},{5,3},{10,12},{11,13},{12,10},{13,11},{18,20},{1... | collective-permute-start | bytes 6291464 | tf_op jit(solution)/shard_map/ppermute | solution.py:309
  658.1 13.4 %collective-permute-start.34 = (bf16[256,4096]{1,0:T(8,128)(2,1)S(1)}, bf16[256,4096]{1,0:T(8,128)(2,1)S(1)}, u32[]{:S(2)}, u32[]{:S(2)}) collective-permute-start(bf16[256,4096]{1,0:T(8,128)(2,1)S(1)} %pad_maximum_fusion.3), channel_id=1, source_target_pairs={{0,4},{4,0},{8,12},{12,8},{16,20},{20,16},{24,28},{28,24},{1,5},{5... | collective-permute-start | bytes 6291464 | tf_op jit(solution)/shard_map/ppermute | solution.py:263
  659.1 12.4 %collective-permute-start.35 = (bf16[256,4096]{1,0:T(8,128)(2,1)S(1)}, bf16[256,4096]{1,0:T(8,128)(2,1)S(1)}, u32[]{:S(2)}, u32[]{:S(2)}) collective-permute-start(bf16[256,4096]{1,0:T(8,128)(2,1)S(1)} %pad_maximum_fusion.4), channel_id=1, source_target_pairs={{0,4},{4,0},{8,12},{12,8},{16,20},{20,16},{24,28},{28,24},{1,5},{5... | collective-permute-start | bytes 6291464 | tf_op jit(solution)/shard_map/ppermute | solution.py:264
  673.8 22.0 %all-to-all-start.1 = ((bf16[8,512,128]{2,1,0:T(8,128)(2,1)}), bf16[8,512,128]{2,1,0:T(8,128)(2,1)}, u32[]{:S(2)}, u32[]{:S(2)}) async-start(bf16[8,512,128]{2,1,0:T(8,128)(2,1)} %bitcast.274), calls=%async_computation.1 | async-start | bytes 2097152 | tf_op jit(solution)/shard_map/all_to_all | solution.py:596
  680.4 164.0 %all-gather.9.cloned.1.call-start = ((), (), s32[]{:S(2)}) async-start(), calls=%async_computation.5 | async-start | bytes 5242880 | tf_op jit(solution)/shard_map/all_gather | solution.py:599
  695.9 234.4 %reduce-scatter.2.cloned.1.call-start = ((), (), s32[]{:S(2)}) async-start(), calls=%async_computation.6 | async-start | bytes 17584128 | tf_op jit(solution)/shard_map/reduce_scatter | solution.py:605
  710.1 387.7 %all-gather.11.cloned.1.call-start = ((), (), s32[]{:S(2)}) async-start(), calls=%async_computation.7 | async-start | bytes 7077888 | tf_op jit(solution)/shard_map/all_gather | solution.py:639
  716.4 8.9 collective-permute-start.41
  725.5 5.4 collective-permute-start.42
  727.6 116.8 %collective-permute-start.37 = (bf16[256,4096]{1,0:T(8,128)(2,1)}, bf16[256,4096]{1,0:T(8,128)(2,1)}, u32[]{:S(2)}, u32[]{:S(2)}) collective-permute-start(bf16[256,4096]{1,0:T(8,128)(2,1)} %pad_maximum_fusion.5), channel_id=1, source_target_pairs={{0,1},{1,0},{2,3},{3,2},{4,5},{5,4},{6,7},{7,6},{8,9},{9,8},{10,11... | collective-permute-start | bytes 6291464 | tf_op jit(solution)/shard_map/ppermute | solution.py:287
  731.8 87.9 %collective-permute-start.43 = (bf16[528,128]{1,0:T(8,128)(2,1)S(1)}, bf16[528,128]{1,0:T(8,128)(2,1)S(1)}, u32[]{:S(2)}, u32[]{:S(2)}) collective-permute-start(bf16[528,128]{1,0:T(8,128)(2,1)S(1)} %add_convert_fusion.9), channel_id=1, source_target_pairs={{0,1},{1,0},{2,3},{3,2},{4,5},{5,4},{6,7},{7,6},{8,9},{9,8},{10,11... | collective-permute-start | bytes 405512 | tf_op jit(solution)/shard_map/ppermute | solution.py:482
  819.7 9.1 collective-permute-start.44
  828.8 12.5 %collective-permute-start.45 = (bf16[528,128]{1,0:T(8,128)(2,1)S(1)}, bf16[528,128]{1,0:T(8,128)(2,1)}, u32[]{:S(2)}, u32[]{:S(2)}) collective-permute-start(bf16[528,128]{1,0:T(8,128)(2,1)S(1)} %add_convert_fusion.7), channel_id=1, source_target_pairs={{0,16},{4,20},{8,24},{12,28},{16,0},{20,4},{24,8},{28,12},{1,17},{... | collective-permute-start | bytes 405512 | tf_op jit(solution)/shard_map/ppermute | solution.py:487
  839.3 16.2 %collective-permute-start.39 = (bf16[256,4096]{1,0:T(8,128)(2,1)}, bf16[256,4096]{1,0:T(8,128)(2,1)}, u32[]{:S(2)}, u32[]{:S(2)}) collective-permute-start(bf16[256,4096]{1,0:T(8,128)(2,1)} %fusion.25), channel_id=1, source_target_pairs={{2,4},{3,5},{4,2},{5,3},{10,12},{11,13},{12,10},{13,11},{18,20},{1... | collective-permute-start | bytes 6291464 | tf_op jit(solution)/shard_map/ppermute | solution.py:309
  843.0 8.0 collective-permute-start.46
  849.9 43.3 %collective-permute-start.38 = (bf16[256,4096]{1,0:T(8,128)(2,1)S(1)}, bf16[256,4096]{1,0:T(8,128)(2,1)S(1)}, u32[]{:S(2)}, u32[]{:S(2)}) collective-permute-start(bf16[256,4096]{1,0:T(8,128)(2,1)S(1)} %pad_maximum_fusion.6), channel_id=1, source_target_pairs={{2,4},{3,5},{4,2},{5,3},{10,12},{11,13},{12,10},{13,11},{18,20},{1... | collective-permute-start | bytes 6291464 | tf_op jit(solution)/shard_map/ppermute | solution.py:309
  852.2 5.1 collective-permute-start.47
  973.6 30.9 %collective-permute-start.48 = (bf16[256,1536]{1,0:T(8,128)(2,1)}, bf16[256,1536]{1,0:T(8,128)(2,1)S(1)}, u32[]{:S(2)}, u32[]{:S(2)}) collective-permute-start(bf16[256,1536]{1,0:T(8,128)(2,1)} %get-tuple-element.132), channel_id=1, source_target_pairs={{0,4},{4,0},{8,12},{12,8},{16,20},{20,16},{24,28},{28,24},{1,5},{5... | collective-permute-start | bytes 2359304 | tf_op jit(solution)/shard_map/ppermute | solution.py:447
  1002.4 4.4 collective-permute-start.50
  1002.9 5.0 collective-permute-start.49
  1016.0 12.3 %collective-permute-start.56 = (bf16[128,1536]{1,0:T(8,128)(2,1)}, bf16[128,1536]{1,0:T(8,128)(2,1)}, u32[]{:S(2)}, u32[]{:S(2)}) collective-permute-start(bf16[128,1536]{1,0:T(8,128)(2,1)} %get-tuple-element.145), channel_id=1, source_target_pairs={{0,16},{4,20},{8,24},{12,28},{16,0},{20,4},{24,8},{28,12},{1,17},{... | collective-permute-start | bytes 1179656 | tf_op jit(solution)/shard_map/ppermute | solution.py:452
  1016.6 19.9 %collective-permute-start.55 = (bf16[128,1536]{1,0:T(8,128)(2,1)S(1)}, bf16[128,1536]{1,0:T(8,128)(2,1)S(1)}, u32[]{:S(2)}, u32[]{:S(2)}) collective-permute-start(bf16[128,1536]{1,0:T(8,128)(2,1)S(1)} %get-tuple-element.144), channel_id=1, source_target_pairs={{0,16},{4,20},{8,24},{12,28},{16,0},{20,4},{24,8},{28,12},{1,17},{... | collective-permute-start | bytes 1179656 | tf_op jit(solution)/shard_map/ppermute | solution.py:452
  1018.1 13.1 %collective-permute-start.53 = (bf16[128,1536]{1,0:T(8,128)(2,1)S(1)}, bf16[128,1536]{1,0:T(8,128)(2,1)S(1)}, u32[]{:S(2)}, u32[]{:S(2)}) collective-permute-start(bf16[128,1536]{1,0:T(8,128)(2,1)S(1)} %get-tuple-element.143), channel_id=1, source_target_pairs={{0,8},{4,12},{8,0},{12,4},{16,24},{20,28},{24,16},{28,20},{1,9},{5... | collective-permute-start | bytes 1179656 | tf_op jit(solution)/shard_map/ppermute | solution.py:452
  1019.7 27.4 %collective-permute-start.52 = (bf16[128,1536]{1,0:T(8,128)(2,1)S(1)}, bf16[128,1536]{1,0:T(8,128)(2,1)S(1)}, u32[]{:S(2)}, u32[]{:S(2)}) collective-permute-start(bf16[128,1536]{1,0:T(8,128)(2,1)S(1)} %get-tuple-element.142), channel_id=1, source_target_pairs={{0,8},{4,12},{8,0},{12,4},{16,24},{20,28},{24,16},{28,20},{1,9},{5... | collective-permute-start | bytes 1179656 | tf_op jit(solution)/shard_map/ppermute | solution.py:452
  1029.6 16.3 %collective-permute-start.57 = (bf16[128,1536]{1,0:T(8,128)(2,1)S(1)}, bf16[128,1536]{1,0:T(8,128)(2,1)S(1)}, u32[]{:S(2)}, u32[]{:S(2)}) collective-permute-start(bf16[128,1536]{1,0:T(8,128)(2,1)S(1)} %fusion.65), channel_id=1, source_target_pairs={{0,8},{4,12},{8,0},{12,4},{16,24},{20,28},{24,16},{28,20},{1,9},{5... | collective-permute-start | bytes 1179656 | tf_op jit(solution)/shard_map/ppermute | solution.py:452
  1031.3 15.8 %collective-permute-start.54 = (bf16[128,1536]{1,0:T(8,128)(2,1)S(1)}, bf16[128,1536]{1,0:T(8,128)(2,1)S(1)}, u32[]{:S(2)}, u32[]{:S(2)}) collective-permute-start(bf16[128,1536]{1,0:T(8,128)(2,1)S(1)} %fusion.67), channel_id=1, source_target_pairs={{0,16},{4,20},{8,24},{12,28},{16,0},{20,4},{24,8},{28,12},{1,17},{... | collective-permute-start | bytes 1179656 | tf_op jit(solution)/shard_map/ppermute | solution.py:452
  1062.4 3.5 collective-permute-start.60
  1069.5 4.4 collective-permute-start.62
  (103 other events, 1145.0 us)
Sparse Core Ops, SparseCore 0:
  77.5 126.5 all-gather.4
  206.5 88.0 all-gather.6
  696.0 115.7 all-gather.8
  815.4 114.8 reduce-scatter.1
  1054.3 43.4 all-gather.10

commit v4 on v3

--- a/solution.py
+++ b/solution.py
@@ -21,6 +21,8 @@
 OPT_EPS = 1e-06
 MAG_EPS = 1e-08
 
+FREE = pl.CostEstimate(flops=0, bytes_accessed=0, transcendentals=0)
+
 
 def joined(value, axis, join):
     pieces = jax.tree.map(lambda part: lax.all_gather(part, axis), value)
@@ -57,15 +59,90 @@
     )
 
 
-def score_block(heads, docs):
-    raw = (
-        jnp.einsum(
-            "sqhd,skhd->shqk", heads[:, :, 0], heads[:, :, 1], preferred_element_type=jnp.float32
-        )
-        * 0.125
-    )
-    same = (docs[:, :, None] == docs[:, None, :])[:, None]
-    return jnp.where(same, raw, -1000000000.0)
+def attend_kernel(q_ref, k_ref, v_ref, key_doc_ref, query_doc_ref, out_ref, lse_ref):
+    same = key_doc_ref[...] == query_doc_ref[...]
+    lane = lax.broadcasted_iota(jnp.int32, (1, 2 * HEAD), 1)
+    outs = []
+    for head in range(2):
+        mine = lane // HEAD == head
+        query = jnp.where(mine, q_ref[...] * 0.125, 0).astype(jnp.bfloat16)
+        scores = jnp.where(same, matmul_nt(k_ref[...], query), -1000000000.0)
+        top = jnp.max(scores, axis=0, keepdims=True)
+        power = jnp.exp(scores - top)
+        total = jnp.sum(power, axis=0, keepdims=True)
+        lse_ref[0, head : head + 1, :] = top + jnp.log(total)
+        prob = (power * (1.0 / total)).astype(jnp.bfloat16)
+        outs.append(matmul_tn(prob, v_ref[...]))
+    out_ref[...] = jnp.where(lane < HEAD, outs[0], outs[1]).astype(jnp.bfloat16)
+
+
+def head_pairs(offset):
+    return pl.BlockSpec((L, 2 * HEAD), lambda pair: (0, offset * HEADS // 2 + pair))
+
+
+def attend(qkv, docs):
+    return pl.pallas_call(
+        attend_kernel,
+        grid=(HEADS // 2,),
+        in_specs=[
+            head_pairs(0),
+            head_pairs(1),
+            head_pairs(2),
+            pl.BlockSpec((L, 1), lambda pair: (0, 0)),
+            pl.BlockSpec((1, L), lambda pair: (0, 0)),
+        ],
+        out_specs=[head_pairs(0), pl.BlockSpec((1, 2, L), lambda pair: (pair, 0, 0))],
+        out_shape=[
+            jax.ShapeDtypeStruct((L, D), jnp.bfloat16),
+            jax.ShapeDtypeStruct((HEADS // 2, 2, L), jnp.float32),
+        ],
+        compiler_params=pltpu.CompilerParams(vmem_limit_bytes=40 * 2**20),
+        cost_estimate=FREE,
+        name="attend",
+    )(qkv, qkv, qkv, docs.reshape(L, 1), docs.reshape(1, L))
+
+
+def attend_back_kernel(q_ref, k_ref, v_ref, do_ref, lse_ref, key_doc_ref, query_doc_ref, out_ref):
+    pair = pl.program_id(0)
+    same = key_doc_ref[...] == query_doc_ref[...]
+    lane = lax.broadcasted_iota(jnp.int32, (1, 2 * HEAD), 1)
+    both = []
+    for head in range(2):
+        mine = lane // HEAD == head
+        query = jnp.where(mine, q_ref[...] * 0.125, 0).astype(jnp.bfloat16)
+        dout = jnp.where(mine, do_ref[...], 0).astype(jnp.bfloat16)
+        scores = jnp.where(same, matmul_nt(k_ref[...], query), -1000000000.0)
+        prob = jnp.exp(scores - lse_ref[0, head : head + 1, :])
+        dvalue = matmul(prob.astype(jnp.bfloat16), dout)
+        dprob = matmul_nt(v_ref[...], dout)
+        delta = jnp.sum(prob * dprob, axis=0, keepdims=True)
+        dscore = (prob * (dprob - delta)).astype(jnp.bfloat16)
+        both.append((matmul_tn(dscore, k_ref[...]) * 0.125, matmul(dscore, query), dvalue))
+    for part in range(3):
+        value = jnp.where(lane < HEAD, both[0][part], both[1][part]).astype(jnp.bfloat16)
+        start = pl.multiple_of(part * D + pair * 2 * HEAD, 2 * HEAD)
+        out_ref[:, pl.ds(start, 2 * HEAD)] = value
+
+
+def attend_back(qkv, dout, lse, docs):
+    return pl.pallas_call(
+        attend_back_kernel,
+        grid=(HEADS // 2,),
+        in_specs=[
+            head_pairs(0),
+            head_pairs(1),
+            head_pairs(2),
+            head_pairs(0),
+            pl.BlockSpec((1, 2, L), lambda pair: (pair, 0, 0)),
+            pl.BlockSpec((L, 1), lambda pair: (0, 0)),
+            pl.BlockSpec((1, L), lambda pair: (0, 0)),
+        ],
+        out_specs=pl.BlockSpec((L, 3 * D), lambda pair: (0, 0)),
+        out_shape=jax.ShapeDtypeStruct((L, 3 * D), jnp.bfloat16),
+        compiler_params=pltpu.CompilerParams(vmem_limit_bytes=40 * 2**20),
+        cost_estimate=FREE,
+        name="attend_back",
+    )(qkv, qkv, qkv, dout, lse, docs.reshape(L, 1), docs.reshape(1, L))
 
 
 def merge_rows(first, second):
@@ -75,19 +152,12 @@
 
 
 def layer_forward(embedded, docs, small, weights):
-    seqs = docs.shape[0]
     base = L + 2
     x0 = norm_rows(embedded, small[base], small[base + 1])
     act = x0.astype(jnp.bfloat16)
     bias = jnp.concatenate([small[base + 6], jnp.zeros((D,), jnp.float32), small[base + 7]])
     qkv = (matmul(act, weights[:, 0 : 3 * D]) + bias).astype(jnp.bfloat16)
-    heads = qkv.reshape(seqs, L, 3, HEADS, HEAD)
-    scores = score_block(heads, docs)
-    top = jnp.max(scores, axis=-1, keepdims=True)
-    lse = top + jnp.log(jnp.sum(jnp.exp(scores - top), axis=-1, keepdims=True))
-    prob = jnp.exp(scores - lse).astype(jnp.bfloat16)
-    out = jnp.einsum("shqk,skhd->sqhd", prob, heads[:, :, 2], preferred_element_type=jnp.float32)
-    out = out.reshape(seqs * L, D).astype(jnp.bfloat16)
+    out, lse = attend(qkv, docs)
     rone = x0 + (matmul(out, weights[:, 3 * D : 4 * D]) + small[base + 8])
     hone = norm_rows(rone, small[base + 2], small[base + 3])
     fin = hone.astype(jnp.bfloat16)
@@ -100,7 +170,6 @@
 
 def layer_backward(dhtwo, kept, docs, small, weights):
     embedded, act, qkv, lse, out, rone, fin, upper, gated, rtwo = kept
-    seqs = docs.shape[0]
     base = L + 2
     _, pull = jax.vjp(norm_rows, rtwo, small[base + 4], small[base + 5])
     drtwo, dgain_two, dshift_two = pull(dhtwo)
@@ -119,36 +188,17 @@
     dout = matmul_nt(dattn, weights[:, 3 * D : 4 * D]).astype(jnp.bfloat16)
     dout = up.received(dout)
     up.across()
-    dout = dout.reshape(seqs, L, HEADS, HEAD)
-    heads = qkv.reshape(seqs, L, 3, HEADS, HEAD)
-    prob = jnp.exp(score_block(heads, docs) - lse)
-    dvalue = jnp.einsum(
-        "shqk,sqhd->skhd", prob.astype(jnp.bfloat16), dout, preferred_element_type=jnp.float32
-    )
-    dout, dvalue = down.crossed(dout, dvalue)
-    if down.paired:
-        down.finish()
-    dprob = jnp.einsum("sqhd,skhd->shqk", dout, heads[:, :, 2], preferred_element_type=jnp.float32)
-    dscore = (prob * (dprob - jnp.sum(prob * dprob, axis=-1, keepdims=True))).astype(jnp.bfloat16)
-    dquery = (
-        jnp.einsum("shqk,skhd->sqhd", dscore, heads[:, :, 1], preferred_element_type=jnp.float32)
-        * 0.125
-    )
-    dkey = (
-        jnp.einsum("shqk,sqhd->skhd", dscore, heads[:, :, 0], preferred_element_type=jnp.float32)
-        * 0.125
-    )
-    dqkv = jnp.stack([dquery, dkey, dvalue], axis=2).reshape(seqs * L, 3 * D).astype(jnp.bfloat16)
-    (dqkv,) = up.crossed(dqkv)
-    if up.paired:
-        up.finish()
+    dqkv = attend_back(qkv, dout, lse, docs)
+    (dqkv,) = down.crossed(dqkv)
+    down.finish()
     mixed = WorkerPiece((act, dqkv), (out, dattn))
     dxzero = drone + matmul_nt(dqkv, weights[:, 0 : 3 * D])
     _, pull = jax.vjp(norm_rows, embedded, small[base], small[base + 1])
     dembed, dgain_emb, dshift_emb = pull(dxzero)
     dembed = mixed.received(dembed)
-    if down.paired:
-        dembed, down.result = together(dembed, down.result)
+    dembed, mixed.far = up.crossed(dembed, mixed.far) if up.paired else (dembed, None)
+    up.finish()
+    mixed.across()
     bias_qkv = jnp.sum(dqkv, axis=0, dtype=jnp.float32)
     vectors = jnp.stack(
         [
@@ -337,7 +387,6 @@
     )
 
 
-FREE = pl.CostEstimate(flops=0, bytes_accessed=0, transcendentals=0)
 STREAMS = 4
 
 
@@ -421,7 +470,7 @@
         ),
         out_shape=jax.ShapeDtypeStruct((size, cols), jnp.float32),
         compiler_params=pltpu.CompilerParams(vmem_limit_bytes=40 * 2**20),
-        cost_estimate=FREE,
+        cost_estimate=pl.CostEstimate(flops=0, bytes_accessed=10**8, transcendentals=0),
         name="add_rows",
     )(ids, values.reshape(STREAMS, count // STREAMS, cols))
 
@@ -466,16 +515,20 @@
     return jnp.concatenate([own_upper, own_lower], axis=0)
 
 
+def small_halved(value):
+    n_wide = lax.axis_size("wide")
+    for bit, place in zip((1, 2, 4), wide_places()):
+        half = value.shape[1] // 2
+        give = lax.dynamic_slice_in_dim(value, (1 - place) * half, half, 1).astype(jnp.bfloat16)
+        keep = lax.dynamic_slice_in_dim(value, place * half, half, 1)
+        value = keep + lax.ppermute(give, "wide", swap_pairs(n_wide, bit)).astype(jnp.float32)
+    return value
+
+
 def small_total(value):
     if not paired_mesh():
         return lax.psum(value, ("wide", "narrow"))
     n_wide, n_narrow = lax.axis_size("wide"), lax.axis_size("narrow")
-    places = list(zip((1, 2, 4), wide_places()))
-    for bit, place in places:
-        half = value.shape[1] // 2
-        give = lax.dynamic_slice_in_dim(value, (1 - place) * half, half, 1).astype(jnp.bfloat16)
-        keep = lax.dynamic_slice_in_dim(value, place * half, half, 1)
-        value = keep + lax.ppermute(give, "wide", swap_pairs(n_wide, bit)).astype(jnp.float32)
     bit = 1
     while bit < n_narrow:
         low = value.astype(jnp.bfloat16)
@@ -483,7 +536,7 @@
         value = low.astype(jnp.float32) + other.astype(jnp.float32)
         bit *= 2
     value = value.astype(jnp.bfloat16)
-    for bit, place in reversed(places):
+    for bit, place in reversed(list(zip((1, 2, 4), wide_places()))):
         other = lax.ppermute(value, "wide", swap_pairs(n_wide, bit))
         first, second = jnp.where(place == 0, value, other), jnp.where(place == 0, other, value)
         value = jnp.concatenate([first, second], axis=1)
@@ -532,7 +585,7 @@
         looked = chain_scatter(picked).reshape(n_wide, L, -1)
         looked = lax.all_to_all(looked, "wide", 0, 0)
         looked = looked.transpose(1, 0, 2).reshape(1, L, D)
-        table_low, weights = together(table_low, weights)
+        table_low, weights, looked = together(table_low, weights, looked)
         table_cols = lax.all_gather(table_low, "wide", axis=1, tiled=True)
     else:
         slots = jnp.where(inside, local_ids, vshard).reshape(-1)
@@ -574,6 +627,10 @@
     dhmask = matmul(dlogit, table_cols)
     if paired:
         dhmask = scattered_near(dhmask)
+        blocks = group_h.reshape(-1, n_wide, D // n_wide)
+        table_head = jnp.einsum("sv,swc->wvc", dlogit, blocks, preferred_element_type=jnp.float32)
+        table_head, dhmask = together(table_head.astype(jnp.bfloat16), dhmask)
+        table_head = lax.psum_scatter(table_head, "wide", scatter_dimension=0)
     else:
         dhmask = lax.psum_scatter(dhmask, "narrow", scatter_dimension=0, tiled=True)
     dhtwo = (
@@ -594,21 +651,16 @@
     if paired:
         cut = dembed.astype(jnp.bfloat16).reshape(L, n_wide, D // n_wide).transpose(1, 0, 2)
         cut = lax.all_to_all(cut, "wide", 0, 0).reshape(n_wide * L, D // n_wide)
-        cut, small_grad, dlogit = together(mixed.received(cut), small_grad, dlogit)
-        mixed.across()
+        small_grad = small_halved(small_grad)
+        down, up = pieces[2], pieces[1]
+        cut, mixed.away, small_grad, down.result, up.result, table_head = together(
+            cut, mixed.away, small_grad, down.result, up.result, table_head
+        )
+        mixed.finish()
+        cut, mixed.result = together(cut, mixed.result)
         group_rows = lax.all_gather(cut, "narrow", axis=0, tiled=True)
-        (group_rows,) = mixed.crossed(group_rows)
-        mixed.finish()
-        blocks = group_h.reshape(-1, n_wide, D // n_wide)
-        table_head = jnp.einsum("sv,swc->wvc", dlogit, blocks, preferred_element_type=jnp.float32)
-        table_head = table_head.astype(jnp.bfloat16)
-        table_head = lax.psum_scatter(table_head, "wide", scatter_dimension=0)
-        table_grad = added_rows(slots, group_rows, vshard)
-        table_grad = table_grad + table_head.astype(jnp.float32)
     else:
         mixed.finish()
-        pieces[1].finish()
-        pieces[2].finish()
         group_rows = lax.all_gather(dembed_rows.astype(jnp.bfloat16), "narrow", axis=0, tiled=True)
         table_grad = matmul_tn(dlogit, group_h).at[slots].add(
             group_rows.reshape(-1, D).astype(jnp.float32), mode="drop"
@@ -616,6 +668,17 @@
         cut = table_grad.astype(jnp.bfloat16).reshape(vshard, n_wide, D // n_wide)
         table_grad = lax.psum_scatter(cut.transpose(1, 0, 2), "wide", scatter_dimension=0)
         table_grad = table_grad.astype(jnp.float32)
+    worker_grad = jnp.concatenate([piece.result for piece in pieces], axis=1)
+    span = BETA * layer_m + (1.0 - BETA) * worker_grad.astype(jnp.float32) + worker_err[0]
+    scale = jnp.mean(jnp.abs(span)) + MAG_EPS
+    sent = scale * jnp.tanh(span / scale)
+    new_worker = (span - sent)[None]
+    part_cols = layer.shape[1]
+    server_in = scattered_sum(sent) / n_wide + server_err
+    if paired:
+        server_in, group_rows, small_grad = together(server_in, group_rows, small_grad)
+        table_grad = added_rows(slots, group_rows, vshard)
+        table_grad = table_grad + table_head.astype(jnp.float32)
     small_grad = small_total(small_grad)
     small_mom = BETA * small_m + (1.0 - BETA) * small_grad
     small_upd = small_mom / (jnp.sqrt(small_v) + OPT_EPS) + DECAY * small
@@ -623,16 +686,6 @@
     table_mom = BETA * table_m + (1.0 - BETA) * table_grad
     table_upd = table_mom / (jnp.sqrt(table_v) + OPT_EPS) + DECAY * table
     table_norms = (jnp.sum(table * table)[None], jnp.sum(table_upd * table_upd)[None])
-    worker_grad = jnp.concatenate([piece.result for piece in pieces], axis=1)
-    if paired:
-        worker_grad, table_norms, small_norms = together(worker_grad, table_norms, small_norms)
-    span = BETA * layer_m + (1.0 - BETA) * worker_grad.astype(jnp.float32) + worker_err[0]
-    scale = jnp.mean(jnp.abs(span)) + MAG_EPS
-    sent = scale * jnp.tanh(span / scale)
-    new_worker = (span - sent)[None]
-    part_cols = layer.shape[1]
-    mixed = scattered_sum(sent) / n_wide
-    server_in = mixed + server_err
     sscale = jnp.mean(jnp.abs(server_in)) + MAG_EPS
     server_out = sscale * jnp.tanh(server_in / sscale)
     new_server = server_in - server_out

time: 1120 us -> 942 us (0.84)
  waiting for transfers between devices: 478 us -> 337 us
  matrix products: 211 us -> 157 us
  other arithmetic: 177 us -> 145 us
  Pallas kernels: 52.4 us -> 80.4 us
  starting transfers between devices: 110 us -> 135 us
    all_gather x1, waiting for transfers between devices: 84.1 us -> 0.02 us  [shards(): weights = lax.all_gather(layer_rows, 'wide', axis=1, tiled=True)]
    ppermute x2, waiting for transfers between devices: 94.2 us -> 11.7 us  [small_total(): other = lax.ppermute(low, 'narrow', swap_pairs(n_narrow, bit))]
    dot_general x6 -> x0, matrix products: 53.5 us -> none  [the longest x1 14.5 us: layer_backward(): jnp.einsum('sqhd,skhd->shqk', dout, heads[:, :, 2], preferred_element_typ...]
    ppermute x3, waiting for transfers between devices: 68.8 us -> 108 us  [across(): self.away = lax.ppermute(away, 'narrow', sides)]
    pallas_call x0 -> x2, Pallas kernels: none -> 28.2 us  [the longest x1 16.5 us: attend_back(): pl.pallas_call(attend_back_kernel, grid=(HEADS // 2,), in_specs=[head_pai...]
    ppermute x3, waiting for transfers between devices: 27.1 us -> 55.2 us  [chain_scatter(): rising = lax.ppermute(up, 'narrow', [(i, i + 1) for i in range(step)])]
    reduce_scatter x1, waiting for transfers between devices: 27.9 us -> 0.01 us  [shards(): table_head = lax.psum_scatter(table_head, 'wide', scatter_dimension=0)]
    ppermute x4, starting transfers between devices: 29.3 us -> 49.8 us  [scattered_sum(): lax.ppermute(part_of, 'wide', swap_pairs(n_wide, 1))]
  transfers between devices with their start and end apart: 70 -> 70, of which waited for: 43 -> 37; matrix products, arithmetic and copies ran while one was open for 26% -> 30% of each run, Pallas kernels for 5% -> 9%
where the time goes in v4:
time: 942 us; the launch traced here: 934 us
  waiting for transfers between devices  337 us (36%)
  matrix products  157 us (17%)
  other arithmetic  145 us (15%)
  starting transfers between devices  135 us (14%)
  Pallas kernels  80.4 us (9%)
  local copies, waits for them, and re-layouts  58.6 us (6%)
  between operations  20.8 us (2%)
    ppermute x3, waiting for transfers between devices, across(): self.away = lax.ppermute(away, 'narrow', sides)  108 us
    dot_general x5, matrix products, matmul(): return jnp.dot(left, right, preferred_element_type=jnp.float32)  62.3 us
    ppermute x3, waiting for transfers between devices, chain_scatter(): rising = lax.ppermute(up, 'narrow', [(i, i + 1) for i in range(step)])  55.2 us
    ppermute x4, starting transfers between devices, scattered_sum(): lax.ppermute(part_of, 'wide', swap_pairs(n_wide, 1))  49.8 us
    dot_general x5, matrix products, matmul_nt(): lax.dot_general(left, right, (((1,), (1,)), ((), ())), preferred_element_...  40 us
    dot_general x16, matrix products, matmul_tn(): lax.dot_general(left, right, (((0,), (0,)), ((), ())), preferred_element_...  36.7 us
    ppermute x3, waiting for transfers between devices, chain_gather(): lax.ppermute(falling, 'narrow', [(i, i - 1) for i in range(1, size - step...  35.3 us
    pallas_call x1, Pallas kernels, added_rows(): pl.pallas_call(add_kernel, grid_spec=pltpu.PrefetchScalarGridSpec(num_sca...  32 us
  transfers between devices with their start and end apart: 70, of which 37 were waited for; matrix products, arithmetic and copies ran while one was open for 30% of the time, Pallas kernels for 9%

profile of v4, /device:TPU:0, one launch (start us, length us, event | category | flops | bytes accessed | tf_op | source)
XLA Modules:
  0.0 934.1 jit_solution(8355565542741207807)
XLA Ops:
  8.7 5.1 collective-permute-start.1
  15.1 15.4 %collective-permute-done.1 = bf16[256,1536]{1,0:T(8,128)(2,1)S(1)} collective-permute-done((bf16[256,1536]{1,0:T(8,128)(2,1)S(1)}, bf16[256,1536]{1,0:T(8,128)(2,1)S(1)}, u32[]{:S(2)}, u32[]{:S(2)}) %collective-permute-start.1) | collective-permute-done | bytes 786464 | tf_op jit(solution)/shard_map/ppermute | solution.py:278
  37.6 18.2 %collective-permute-done.5 = bf16[256,1536]{1,0:T(8,128)(2,1)} collective-permute-done((bf16[256,1536]{1,0:T(8,128)(2,1)S(1)}, bf16[256,1536]{1,0:T(8,128)(2,1)}, u32[]{:S(2)}, u32[]{:S(2)}) %collective-permute-start.5) | collective-permute-done | bytes 786464 | tf_op jit(solution)/shard_map/ppermute | solution.py:279
  60.9 14.5 %collective-permute-done.6 = bf16[256,1536]{1,0:T(8,128)(2,1)S(1)} collective-permute-done((bf16[256,1536]{1,0:T(8,128)(2,1)}, bf16[256,1536]{1,0:T(8,128)(2,1)S(1)}, u32[]{:S(2)}, u32[]{:S(2)}) %collective-permute-start.6) | collective-permute-done | bytes 786464 | tf_op jit(solution)/shard_map/ppermute | solution.py:279
  90.5 20.2 %take_rows.1 = bf16[16384,128]{1,0:T(8,128)(2,1)S(1)} custom-call(s32[16384]{0:T(1024)S(1)} %bitcast.212, f32[7632,128]{1,0:T(8,128)S(1)} %copy-done.2), custom_call_target="tpu_custom_call" | custom-call | tf_op jit(solution)/shard_map/take_rows/pallas_call | solution.py:413
  116.4 18.8 %collective-permute-done.10 = bf16[4096,128]{1,0:T(8,128)(2,1)S(1)} collective-permute-done((bf16[4096,128]{1,0:T(8,128)(2,1)S(1)}, bf16[4096,128]{1,0:T(8,128)(2,1)S(1)}, u32[]{:S(2)}, u32[]{:S(2)}) %collective-permute-start.10) | collective-permute-done | bytes 1048608 | tf_op jit(solution)/shard_map/ppermute | solution.py:299
  136.5 4.5 collective-permute-start.11
  141.0 19.8 %collective-permute-done.11 = bf16[4096,128]{1,0:T(8,128)(2,1)S(1)} collective-permute-done((bf16[4096,128]{1,0:T(8,128)(2,1)S(1)}, bf16[4096,128]{1,0:T(8,128)(2,1)S(1)}, u32[]{:S(2)}, u32[]{:S(2)}) %collective-permute-start.11) | collective-permute-done | bytes 1048608 | tf_op jit(solution)/shard_map/ppermute | solution.py:299
  160.8 3.4 bitcast_add_fusion.5
  164.9 5.0 collective-permute-start.12
  172.6 16.7 %collective-permute-done.12 = bf16[4096,128]{1,0:T(8,128)(2,1)S(1)} collective-permute-done((bf16[4096,128]{1,0:T(8,128)(2,1)}, bf16[4096,128]{1,0:T(8,128)(2,1)S(1)}, u32[]{:S(2)}, u32[]{:S(2)}) %collective-permute-start.12) | collective-permute-done | bytes 1048608 | tf_op jit(solution)/shard_map/ppermute | solution.py:299
  189.2 23.6 %collective-permute-done.15 = bf16[4096,128]{1,0:T(8,128)(2,1)S(1)} collective-permute-done((bf16[4096,128]{1,0:T(8,128)(2,1)S(1)}, bf16[4096,128]{1,0:T(8,128)(2,1)S(1)}, u32[]{:S(2)}, u32[]{:S(2)}) %collective-permute-start.15) | collective-permute-done | bytes 1048608 | tf_op jit(solution)/shard_map/ppermute | solution.py:300
  215.2 3.8 all-to-all-start
  219.0 3.6 convert_element_type.329
  222.6 11.8 %all-to-all-done = bf16[8,512,128]{2,1,0:T(8,128)(2,1)S(1)} async-done(((bf16[8,512,128]{2,1,0:T(8,128)(2,1)}), bf16[8,512,128]{2,1,0:T(8,128)(2,1)S(1)}, u32[]{:S(2)}, u32[]{:S(2)}) %all-to-all-start) | async-done | bytes 1048608 | tf_op jit(solution)/shard_map/all_to_all | solution.py:586
  239.1 3.6 collective-permute-start.22
  261.6 6.8 add_convert_fusion.1.q_ref.k_ref.v_ref
  268.5 11.7 %attend.1 = (bf16[512,1024]{1,0:T(8,128)(2,1)S(1)}, f32[8,2,512]{2,1,0:T(2,128)S(1)}) custom-call(bf16[512,3072]{1,0:T(8,128)(2,1)S(1)} %add_convert_fusion.1.q_ref.k_ref.v_ref, bf16[512,3072]{1,0:T(8,128)(2,1)S(1)} %add_convert_fusion.1.q_ref.k_ref.v_ref, bf16[512,3072]{1,0:T(8,128)(2,1)S(1)} %add_convert_fusion.1.q_ref.k_ref.v_ref, ...), custom_call_target="tpu_custom_call" | custom-call | tf_op jit(solution)/shard_map/attend/pallas_call | solution.py:84
  280.3 3.5 fusion.151
  284.6 26.1 %multiply_convert_fusion = (bf16[512,4096]{1,0:T(8,128)(2,1)S(1)}, f32[512,4096]{1,0:T(8,128)}, f32[512,4096]{1,0:T(8,128)}) fusion(f32[4096]{0:T(1024)S(1)} %bitcast.237, bf16[512,1024]{1,0:T(8,128)(2,1)S(1)} %fusion.39, bf16[1024,12288]{1,0:T(8,128)(2,1)} %all-gather.5.cloned.1.call-done), kind=kOutput, calls=%fused_computation.19 | convolution fusion | flops 4433379328 | bytes 30425088 | tf_op jit(solution)/shard_map/dot_general | solution.py:47
  310.7 9.2 fusion.152
  328.9 8.2 collective-permute-done.17
  340.5 11.3 %fusion.153 = (f32[320]{0:T(512)S(1)}, f32[320,7632]{1,0:T(8,128)}) fusion(bf16[7632,1024]{1,0:T(8,128)(2,1)} %all-gather.7.cloned.1.call-done, bf16[560,1024]{1,0:T(8,128)(2,1)} %constant_dynamic-update-slice_fusion.7, s32[]{:T(128)S(6)} %select_n.352, pred[7632]{0:T(1024)(128)(4,1)S(1)} %copy-done.73), kind=kOutput, calls=%fused_computation.380 | convolution fusion | flops 5006591488 | bytes 26063572 | tf_op jit(solution)/shard_map/dot_general | solution.py:57
  351.8 6.6 exponential_reduce_fusion
  365.8 11.6 %fusion.135 = f32[320,1024]{1,0:T(8,128)S(1)} fusion(bf16[7632,1024]{1,0:T(8,128)(2,1)} %all-gather.7.cloned.1.call-done, f32[320,7632]{1,0:T(8,128)S(1)} %copy-done.35, f32[320]{0:T(512)S(1)} %get-tuple-element.185, f32[320]{0:T(512)S(1)} %get-tuple-element.104, s32[7632]{0:T(1024)S(1)} %iota_add_fusion, s32[320]{0:T(512)} %copy-done.74), kind=kOutput, calls=%fused_computation.366 | convolution fusion | flops 5016360960 | bytes 26744384 | tf_op jit(solution)/shard_map/dot_general | solution.py:47
  382.1 17.8 %convert_bitcast_fusion = bf16[8,7632,128]{2,1,0:T(8,128)(2,1)} fusion(f32[320,7632]{1,0:T(8,128)} %get-tuple-element.201, f32[320]{0:T(512)} %copy-done.83, f32[320]{0:T(512)} %copy-done.82, s32[7632]{0:T(1024)S(1)} %iota_add_fusion, s32[320]{0:T(512)S(1)} %copy-done.75, bf16[560,1024]{1,0:T(8,128)(2,1)} %constant_dynamic-update-slice_fusion.7, ...), kind=kOutput, calls=%fused_computation.2 | convolution fusion | flops 5024176128 | bytes 26152004 | tf_op jit(solution)/shard_map/sv,swc->wvc/dot_general | solution.py:631
  402.5 3.3 scatter_custom_fusion
  419.5 3.4 fusion.72
  422.9 14.4 %add_convert_fusion = bf16[512,4096]{1,0:T(8,128)(2,1)S(1)} fusion(f32[512,4096]{1,0:T(8,128)} %get-tuple-element.123, f32[512,4096]{1,0:T(8,128)} %get-tuple-element.197, f32[4096]{0:T(1024)S(1)} %bitcast.238, bf16[512,1024]{1,0:T(8,128)(2,1)S(1)} %get-tuple-element.111, bf16[1024,12288]{1,0:T(8,128)(2,1)} %all-gather.5.cloned.1.call-done), kind=kOutput, calls=%fused_computation.18 | convolution fusion | flops 4326424576 | bytes 30425088 | tf_op jit(solution)/shard_map/dot_general | solution.py:47
  437.4 3.2 convolution_convert_fusion
  443.7 3.7 add_convert_fusion.3
  447.4 10.3 %multiply_reduce_fusion.5 = (f32[1024]{0:T(1024)S(1)}, f32[512]{0:T(512)S(1)}, f32[1024]{0:T(1024)S(1)}, f32[512,1024]{1,0:T(8,128)}) fusion(f32[512,1024]{1,0:T(8,128)S(1)} %copy-done.27, f32[512]{0:T(512)S(1)} %fusion.117, f32[512]{0:T(512)S(1)} %broadcast_multiply_fusion.2, f32[1024]{0:T(1024)S(1)} %bitcast.227, ...), kind=kOutput, calls=%fused_computation.90 | convolution fusion | flops 4300207616 | bytes 18894848 | tf_op jit(solution)/shard_map/dot_general | solution.py:57
  472.2 16.5 %attend_back.1 = bf16[512,3072]{1,0:T(8,128)(2,1)S(1)} custom-call(bf16[512,3072]{1,0:T(8,128)(2,1)S(1)} %copy-done.1, bf16[512,3072]{1,0:T(8,128)(2,1)S(1)} %copy-done.1, bf16[512,3072]{1,0:T(8,128)(2,1)S(1)} %copy-done.1, bf16[512,1024]{1,0:T(8,128)(2,1)S(1)} %fusion.47.do_ref, f32[8,2,512]{2,1,0:T(2,128)S(1)} %get-tuple-element.49.lse_ref, ...), custom_call_target="tpu_custom_call" | custom-call | tf_op jit(solution)/shard_map/attend_back/pallas_call | solution.py:128
  488.7 18.9 %collective-permute-done.32 = bf16[256,4096]{1,0:T(8,128)(2,1)} collective-permute-done((bf16[256,4096]{1,0:T(8,128)(2,1)}, bf16[256,4096]{1,0:T(8,128)(2,1)}, u32[]{:S(2)}, u32[]{:S(2)}) %collective-permute-start.32) | collective-permute-done | bytes 2097184 | tf_op jit(solution)/shard_map/ppermute | solution.py:337
  512.2 4.1 add_convert_fusion.2
  516.3 6.3 multiply_reduce_fusion.6
  526.2 47.5 %collective-permute-done.35 = bf16[256,4096]{1,0:T(8,128)(2,1)S(1)} collective-permute-done((bf16[256,4096]{1,0:T(8,128)(2,1)S(1)}, bf16[256,4096]{1,0:T(8,128)(2,1)S(1)}, u32[]{:S(2)}, u32[]{:S(2)}) %collective-permute-start.35) | collective-permute-done | bytes 2097184 | tf_op jit(solution)/shard_map/ppermute | solution.py:337
  573.7 4.7 fusion.23
  582.0 6.9 concatenate.112
  603.4 4.3 all-to-all-start.1
  610.8 3.1 broadcast_select_fusion.2
  613.9 11.0 %collective-permute-done.39 = bf16[528,128]{1,0:T(8,128)(2,1)S(1)} collective-permute-done((bf16[528,128]{1,0:T(8,128)(2,1)S(1)}, bf16[528,128]{1,0:T(8,128)(2,1)S(1)}, u32[]{:S(2)}, u32[]{:S(2)}) %collective-permute-start.39) | collective-permute-done | bytes 135200 | tf_op jit(solution)/shard_map/ppermute | solution.py:524
  625.0 3.1 broadcast_select_fusion.1
  628.1 41.8 %collective-permute-done.36 = bf16[256,4096]{1,0:T(8,128)(2,1)} collective-permute-done((bf16[256,4096]{1,0:T(8,128)(2,1)}, bf16[256,4096]{1,0:T(8,128)(2,1)}, u32[]{:S(2)}, u32[]{:S(2)}) %collective-permute-start.36) | collective-permute-done | bytes 2097184 | tf_op jit(solution)/shard_map/ppermute | solution.py:337
  669.9 3.3 fusion.30
  679.1 3.7 broadcast_select_fusion
  682.8 15.7 %abs_reduce_fusion = (f32[]{:T(128)}, f32[256,12288]{1,0:T(8,128)}) fusion(f32[1,256,12288]{2,1,0:T(8,128)} %param.30, bf16[256,4096]{1,0:T(8,128)(2,1)S(1)} %copy-done.41, bf16[256,4096]{1,0:T(8,128)(2,1)} %broadcast_select_fusion.1, bf16[256,4096]{1,0:T(8,128)(2,1)} %broadcast_select_fusion, f32[256,12288]{1,0:T(8,128)} %param.28), kind=kLoop, calls=%fused_computation.6 | loop fusion | flops 37748736 | bytes 44040196 | tf_op jit(solution)/shard_map/reduce_sum | solution.py:673
  699.2 10.6 %subtract_bitcast_fusion = (f32[1,256,12288]{2,1,0:T(8,128)}, f32[256,12288]{1,0:T(8,128)S(1)}) fusion(f32[256,12288]{1,0:T(8,128)} %get-tuple-element.109, f32[]{:T(128)S(6)} %add.740), kind=kLoop, calls=%fused_computation.4 | loop fusion | flops 9437184 | bytes 37748740 | tf_op jit(solution)/shard_map/broadcast_in_dim | solution.py:675
  709.8 4.8 copy-done.19
  716.4 49.3 %collective-permute-start.43 = (bf16[256,1536]{1,0:T(8,128)(2,1)}, bf16[256,1536]{1,0:T(8,128)(2,1)S(1)}, u32[]{:S(2)}, u32[]{:S(2)}) collective-permute-start(bf16[256,1536]{1,0:T(8,128)(2,1)} %get-tuple-element.132), channel_id=1, source_target_pairs={{0,4},{4,0},{8,12},{12,8},{16,20},{20,16},{24,28},{28,24},{1,5},{5... | collective-permute-start | bytes 2359304 | tf_op jit(solution)/shard_map/ppermute | solution.py:496
  771.2 4.2 add_bitcast_fusion.3
  783.1 8.0 collective-permute-done.48
  794.5 5.0 collective-permute-done.47
  799.5 9.3 collective-permute-done.49
  812.1 4.2 fusion.87
  816.5 5.0 collective-permute-done.58
  822.5 6.7 collective-permute-done.59
  834.9 32.0 %add_rows.1 = f32[7632,128]{1,0:T(8,128)S(1)} custom-call(s32[16384]{0:T(1024)S(1)} %bitcast.213, bf16[4,4096,128]{2,1,0:T(8,128)(2,1)S(1)} %bitcast.211), custom_call_target="tpu_custom_call" | custom-call | bytes 100000000 | tf_op jit(solution)/shard_map/add_rows/pallas_call | solution.py:461
  868.5 6.6 multiply_reduce_fusion
  886.0 3.5 collective-permute-done.56
  889.6 4.4 collective-permute-done.57
  896.1 4.5 multiply_reduce_fusion.2
  914.3 3.8 multiply_subtract_fusion
  918.1 9.1 convert_element_type.428
  (455 shorter events, 212.8 us)
Async XLA Ops:
  7.2 230.6 %all-gather.5.cloned.1.call-start = ((), (), s32[]{:S(2)}) async-start(), calls=%async_computation.3 | async-start | bytes 28311552 | tf_op jit(solution)/shard_map/all_gather | solution.py:579
  8.7 21.8 %collective-permute-start.1 = (bf16[256,1536]{1,0:T(8,128)(2,1)S(1)}, bf16[256,1536]{1,0:T(8,128)(2,1)S(1)}, u32[]{:S(2)}, u32[]{:S(2)}) collective-permute-start(bf16[256,1536]{1,0:T(8,128)(2,1)S(1)} %convert_element_type.330), channel_id=1, source_target_pairs={{0,1},{1,2},{2,3},{4,5},{5,6},{6,7},{8,9},{9,10},{10,11},{12,13},{... | collective-permute-start | bytes 2359304 | tf_op jit(solution)/shard_map/ppermute | solution.py:278
  13.8 20.9 %collective-permute-start.4 = (bf16[256,1536]{1,0:T(8,128)(2,1)S(1)}, bf16[256,1536]{1,0:T(8,128)(2,1)S(1)}, u32[]{:S(2)}, u32[]{:S(2)}) collective-permute-start(bf16[256,1536]{1,0:T(8,128)(2,1)S(1)} %convert_element_type.330), channel_id=1, source_target_pairs={{1,0},{2,1},{3,2},{5,4},{6,5},{7,6},{9,8},{10,9},{11,10},{13,12},{... | collective-permute-start | bytes 2359304 | tf_op jit(solution)/shard_map/ppermute | solution.py:279
  30.6 5.5 collective-permute-start.2
  34.7 21.1 %collective-permute-start.5 = (bf16[256,1536]{1,0:T(8,128)(2,1)S(1)}, bf16[256,1536]{1,0:T(8,128)(2,1)}, u32[]{:S(2)}, u32[]{:S(2)}) collective-permute-start(bf16[256,1536]{1,0:T(8,128)(2,1)S(1)} %collective-permute-done.4), channel_id=1, source_target_pairs={{1,0},{2,1},{5,4},{6,5},{9,8},{10,9},{13,12},{14,13},{17,16},{18,1... | collective-permute-start | bytes 2359304 | tf_op jit(solution)/shard_map/ppermute | solution.py:279
  36.0 21.1 %collective-permute-start.3 = (bf16[256,1536]{1,0:T(8,128)(2,1)}, bf16[256,1536]{1,0:T(8,128)(2,1)}, u32[]{:S(2)}, u32[]{:S(2)}) collective-permute-start(bf16[256,1536]{1,0:T(8,128)(2,1)} %collective-permute-done.2), channel_id=1, source_target_pairs={{2,3},{6,7},{10,11},{14,15},{18,19},{22,23},{26,27},{30,31}} | collective-permute-start | bytes 2359304 | tf_op jit(solution)/shard_map/ppermute | solution.py:278
  55.8 19.6 %collective-permute-start.6 = (bf16[256,1536]{1,0:T(8,128)(2,1)}, bf16[256,1536]{1,0:T(8,128)(2,1)S(1)}, u32[]{:S(2)}, u32[]{:S(2)}) collective-permute-start(bf16[256,1536]{1,0:T(8,128)(2,1)} %collective-permute-done.5), channel_id=1, source_target_pairs={{1,0},{5,4},{9,8},{13,12},{17,16},{21,20},{25,24},{29,28}} | collective-permute-start | bytes 2359304 | tf_op jit(solution)/shard_map/ppermute | solution.py:279
  79.4 3.9 collective-permute-start.8
  83.3 4.2 collective-permute-start.9
  112.8 22.3 %collective-permute-start.10 = (bf16[4096,128]{1,0:T(8,128)(2,1)S(1)}, bf16[4096,128]{1,0:T(8,128)(2,1)S(1)}, u32[]{:S(2)}, u32[]{:S(2)}) collective-permute-start(bf16[4096,128]{1,0:T(8,128)(2,1)S(1)} %get-tuple-element.140), channel_id=1, source_target_pairs={{0,1},{4,5},{8,9},{12,13},{16,17},{20,21},{24,25},{28,29}} | collective-permute-start | bytes 3145736 | tf_op jit(solution)/shard_map/ppermute | solution.py:299
  114.8 26.2 %collective-permute-start.13 = (bf16[4096,128]{1,0:T(8,128)(2,1)S(1)}, bf16[4096,128]{1,0:T(8,128)(2,1)}, u32[]{:S(2)}, u32[]{:S(2)}) collective-permute-start(bf16[4096,128]{1,0:T(8,128)(2,1)S(1)} %get-tuple-element.141), channel_id=1, source_target_pairs={{3,2},{7,6},{11,10},{15,14},{19,18},{23,22},{27,26},{31,30}} | collective-permute-start | bytes 3145736 | tf_op jit(solution)/shard_map/ppermute | solution.py:300
  136.5 24.3 %collective-permute-start.11 = (bf16[4096,128]{1,0:T(8,128)(2,1)S(1)}, bf16[4096,128]{1,0:T(8,128)(2,1)S(1)}, u32[]{:S(2)}, u32[]{:S(2)}) collective-permute-start(bf16[4096,128]{1,0:T(8,128)(2,1)S(1)} %bitcast_add_fusion.4), channel_id=1, source_target_pairs={{0,1},{1,2},{4,5},{5,6},{8,9},{9,10},{12,13},{13,14},{16,17},{17,1... | collective-permute-start | bytes 3145736 | tf_op jit(solution)/shard_map/ppermute | solution.py:299
  164.2 5.8 collective-permute-start.14
  164.9 24.4 %collective-permute-start.12 = (bf16[4096,128]{1,0:T(8,128)(2,1)}, bf16[4096,128]{1,0:T(8,128)(2,1)S(1)}, u32[]{:S(2)}, u32[]{:S(2)}) collective-permute-start(bf16[4096,128]{1,0:T(8,128)(2,1)} %get-tuple-element.138), channel_id=1, source_target_pairs={{0,1},{1,2},{2,3},{4,5},{5,6},{6,7},{8,9},{9,10},{10,11},{12,13},{... | collective-permute-start | bytes 3145736 | tf_op jit(solution)/shard_map/ppermute | solution.py:299
  171.3 41.6 %collective-permute-start.15 = (bf16[4096,128]{1,0:T(8,128)(2,1)S(1)}, bf16[4096,128]{1,0:T(8,128)(2,1)S(1)}, u32[]{:S(2)}, u32[]{:S(2)}) collective-permute-start(bf16[4096,128]{1,0:T(8,128)(2,1)S(1)} %bitcast_add_fusion.3), channel_id=1, source_target_pairs={{3,2},{2,1},{1,0},{7,6},{6,5},{5,4},{11,10},{10,9},{9,8},{15,14},{... | collective-permute-start | bytes 3145736 | tf_op jit(solution)/shard_map/ppermute | solution.py:300
  215.2 19.2 %all-to-all-start = ((bf16[8,512,128]{2,1,0:T(8,128)(2,1)}), bf16[8,512,128]{2,1,0:T(8,128)(2,1)S(1)}, u32[]{:S(2)}, u32[]{:S(2)}) async-start(bf16[8,512,128]{2,1,0:T(8,128)(2,1)} %bitcast.14), calls=%async_computation | async-start | bytes 2097152 | tf_op jit(solution)/shard_map/all_to_all | solution.py:586
  219.0 121.5 %all-gather.7.cloned.1.call-start = ((), (), s32[]{:S(2)}) async-start(), calls=%async_computation.4 | async-start | bytes 17584128 | tf_op jit(solution)/shard_map/all_gather | solution.py:589
  237.8 432.1 %reduce-scatter.2.cloned.1.call-start = ((), (), s32[]{:S(2)}) async-start(), calls=%async_computation.5 | async-start | bytes 17584128 | tf_op jit(solution)/shard_map/reduce_scatter | solution.py:633
  237.9 17.1 %collective-permute-start = (s32[1,592]{1,0:T(1,128)S(1)}, s32[1,592]{1,0:T(1,128)S(1)}, u32[]{:S(2)}, u32[]{:S(2)}) collective-permute-start(s32[1,592]{1,0:T(1,128)S(1)} %pad_add_fusion.3), channel_id=1, source_target_pairs={{0,0},{1,4},{2,1},{3,5},{4,2},{5,6},{6,3},{7,7},{8,8},{9,12},{10,9... | collective-permute-start | bytes 7112 | tf_op jit(solution)/shard_map/ppermute | solution.py:380
  239.1 6.1 collective-permute-start.22
  246.4 3.7 collective-permute-start.23
  250.7 3.7 collective-permute-start.24
  322.5 5.7 collective-permute-start.16
  322.5 14.6 %collective-permute-start.17 = (bf16[80,1024]{1,0:T(8,128)(2,1)S(1)}, bf16[80,1024]{1,0:T(8,128)(2,1)S(1)}, u32[]{:S(2)}, u32[]{:S(2)}) collective-permute-start(bf16[80,1024]{1,0:T(8,128)(2,1)S(1)} %get-tuple-element.121), channel_id=1, source_target_pairs={{0,2},{1,3},{2,0},{3,1},{4,6},{5,7},{6,4},{7,5},{8,10},{9,11},{10,... | collective-permute-start | bytes 491528 | tf_op jit(solution)/shard_map/ppermute | solution.py:253
  324.5 13.4 %collective-permute-start.18 = (bf16[80,1024]{1,0:T(8,128)(2,1)S(1)}, bf16[80,1024]{1,0:T(8,128)(2,1)S(1)}, u32[]{:S(2)}, u32[]{:S(2)}) collective-permute-start(bf16[80,1024]{1,0:T(8,128)(2,1)S(1)} %get-tuple-element.121), channel_id=1, source_target_pairs={{0,1},{1,2},{2,3},{3,0},{4,5},{5,6},{6,7},{7,4},{8,9},{9,10},{10,1... | collective-permute-start | bytes 491528 | tf_op jit(solution)/shard_map/ppermute | solution.py:253
  358.4 3.7 collective-permute-start.19
  358.5 4.6 collective-permute-start.20
  359.6 5.4 collective-permute-start.21
  378.1 21.8 %collective-permute-start.25 = (bf16[80,1024]{1,0:T(8,128)(2,1)}, bf16[80,1024]{1,0:T(8,128)(2,1)}, u32[]{:S(2)}, u32[]{:S(2)}) collective-permute-start(bf16[80,1024]{1,0:T(8,128)(2,1)} %get-tuple-element.164), channel_id=1, source_target_pairs={{0,1},{1,2},{2,3},{3,0},{4,5},{5,6},{6,7},{7,4},{8,9},{9,10},{10,1... | collective-permute-start | bytes 491528 | tf_op jit(solution)/shard_map/ppermute | solution.py:267
  378.5 21.4 %collective-permute-start.26 = (bf16[80,1024]{1,0:T(8,128)(2,1)}, bf16[80,1024]{1,0:T(8,128)(2,1)}, u32[]{:S(2)}, u32[]{:S(2)}) collective-permute-start(bf16[80,1024]{1,0:T(8,128)(2,1)} %get-tuple-element.166), channel_id=1, source_target_pairs={{0,2},{1,3},{2,0},{3,1},{4,6},{5,7},{6,4},{7,5},{8,10},{9,11},{10,... | collective-permute-start | bytes 491528 | tf_op jit(solution)/shard_map/ppermute | solution.py:267
  380.4 19.5 %collective-permute-start.27 = (bf16[80,1024]{1,0:T(8,128)(2,1)}, bf16[80,1024]{1,0:T(8,128)(2,1)}, u32[]{:S(2)}, u32[]{:S(2)}) collective-permute-start(bf16[80,1024]{1,0:T(8,128)(2,1)} %get-tuple-element.165), channel_id=1, source_target_pairs={{0,3},{1,0},{2,1},{3,2},{4,7},{5,4},{6,5},{7,6},{8,11},{9,8},{10,9... | collective-permute-start | bytes 491528 | tf_op jit(solution)/shard_map/ppermute | solution.py:267
  415.1 22.2 %collective-permute-start.29 = (bf16[256,4096]{1,0:T(8,128)(2,1)}, bf16[256,4096]{1,0:T(8,128)(2,1)S(1)}, u32[]{:S(2)}, u32[]{:S(2)}) collective-permute-start(bf16[256,4096]{1,0:T(8,128)(2,1)} %convolution_convert_fusion.2), channel_id=1, source_target_pairs={{0,4},{4,0},{8,12},{12,8},{16,20},{20,16},{24,28},{28,24},{1,5},{5... | collective-permute-start | bytes 6291464 | tf_op jit(solution)/shard_map/ppermute | solution.py:314
  417.7 19.6 %collective-permute-start.28 = (bf16[256,4096]{1,0:T(8,128)(2,1)}, bf16[256,4096]{1,0:T(8,128)(2,1)}, u32[]{:S(2)}, u32[]{:S(2)}) collective-permute-start(bf16[256,4096]{1,0:T(8,128)(2,1)} %convolution_convert_fusion.3), channel_id=1, source_target_pairs={{0,4},{4,0},{8,12},{12,8},{16,20},{20,16},{24,28},{28,24},{1,5},{5... | collective-permute-start | bytes 6291464 | tf_op jit(solution)/shard_map/ppermute | solution.py:313
  440.5 26.4 %collective-permute-start.31 = (bf16[256,4096]{1,0:T(8,128)(2,1)}, bf16[256,4096]{1,0:T(8,128)(2,1)}, u32[]{:S(2)}, u32[]{:S(2)}) collective-permute-start(bf16[256,4096]{1,0:T(8,128)(2,1)} %convolution_convert_fusion), channel_id=1, source_target_pairs={{0,4},{4,0},{8,12},{12,8},{16,20},{20,16},{24,28},{28,24},{1,5},{5... | collective-permute-start | bytes 6291464 | tf_op jit(solution)/shard_map/ppermute | solution.py:314
  443.2 23.7 %collective-permute-start.30 = (bf16[256,4096]{1,0:T(8,128)(2,1)}, bf16[256,4096]{1,0:T(8,128)(2,1)}, u32[]{:S(2)}, u32[]{:S(2)}) collective-permute-start(bf16[256,4096]{1,0:T(8,128)(2,1)} %convolution_convert_fusion.1), channel_id=1, source_target_pairs={{0,4},{4,0},{8,12},{12,8},{16,20},{20,16},{24,28},{28,24},{1,5},{5... | collective-permute-start | bytes 6291464 | tf_op jit(solution)/shard_map/ppermute | solution.py:313
  458.7 48.9 %collective-permute-start.32 = (bf16[256,4096]{1,0:T(8,128)(2,1)}, bf16[256,4096]{1,0:T(8,128)(2,1)}, u32[]{:S(2)}, u32[]{:S(2)}) collective-permute-start(bf16[256,4096]{1,0:T(8,128)(2,1)} %add_convert_fusion.3), channel_id=1, source_target_pairs={{0,1},{1,0},{2,3},{3,2},{4,5},{5,4},{6,7},{7,6},{8,9},{9,8},{10,11... | collective-permute-start | bytes 6291464 | tf_op jit(solution)/shard_map/ppermute | solution.py:337
  470.0 103.7 %collective-permute-start.35 = (bf16[256,4096]{1,0:T(8,128)(2,1)S(1)}, bf16[256,4096]{1,0:T(8,128)(2,1)S(1)}, u32[]{:S(2)}, u32[]{:S(2)}) collective-permute-start(bf16[256,4096]{1,0:T(8,128)(2,1)S(1)} %fusion.24), channel_id=1, source_target_pairs={{0,1},{1,0},{2,3},{3,2},{4,5},{5,4},{6,7},{7,6},{8,9},{9,8},{10,11... | collective-permute-start | bytes 6291464 | tf_op jit(solution)/shard_map/ppermute | solution.py:337
  508.8 17.4 %collective-permute-start.34 = (bf16[256,4096]{1,0:T(8,128)(2,1)S(1)}, bf16[256,4096]{1,0:T(8,128)(2,1)}, u32[]{:S(2)}, u32[]{:S(2)}) collective-permute-start(bf16[256,4096]{1,0:T(8,128)(2,1)S(1)} %pad_maximum_fusion.2), channel_id=1, source_target_pairs={{0,4},{4,0},{8,12},{12,8},{16,20},{20,16},{24,28},{28,24},{1,5},{5... | collective-permute-start | bytes 6291464 | tf_op jit(solution)/shard_map/ppermute | solution.py:314
  510.1 16.1 %collective-permute-start.33 = (bf16[256,4096]{1,0:T(8,128)(2,1)S(1)}, bf16[256,4096]{1,0:T(8,128)(2,1)}, u32[]{:S(2)}, u32[]{:S(2)}) collective-permute-start(bf16[256,4096]{1,0:T(8,128)(2,1)S(1)} %pad_maximum_fusion.1), channel_id=1, source_target_pairs={{0,4},{4,0},{8,12},{12,8},{16,20},{20,16},{24,28},{28,24},{1,5},{5... | collective-permute-start | bytes 6291464 | tf_op jit(solution)/shard_map/ppermute | solution.py:313
  522.6 88.2 %collective-permute-start.40 = (bf16[256,4096]{1,0:T(8,128)(2,1)}, bf16[256,4096]{1,0:T(8,128)(2,1)}, u32[]{:S(2)}, u32[]{:S(2)}) collective-permute-start(bf16[256,4096]{1,0:T(8,128)(2,1)} %add_convert_fusion.2), channel_id=1, source_target_pairs={{2,4},{3,5},{4,2},{5,3},{10,12},{11,13},{12,10},{13,11},{18,20},{1... | collective-permute-start | bytes 6291464 | tf_op jit(solution)/shard_map/ppermute | solution.py:359
  578.4 46.6 %collective-permute-start.41 = (bf16[256,4096]{1,0:T(8,128)(2,1)}, bf16[256,4096]{1,0:T(8,128)(2,1)}, u32[]{:S(2)}, u32[]{:S(2)}) collective-permute-start(bf16[256,4096]{1,0:T(8,128)(2,1)} %fusion.23), channel_id=1, source_target_pairs={{2,4},{3,5},{4,2},{5,3},{10,12},{11,13},{12,10},{13,11},{18,20},{1... | collective-permute-start | bytes 6291464 | tf_op jit(solution)/shard_map/ppermute | solution.py:359
  590.2 4.7 collective-permute-start.37
  596.9 10.9 %collective-permute-start.38 = (bf16[528,256]{1,0:T(8,128)(2,1)}, bf16[528,256]{1,0:T(8,128)(2,1)S(1)}, u32[]{:S(2)}, u32[]{:S(2)}) collective-permute-start(bf16[528,256]{1,0:T(8,128)(2,1)} %dynamic-slice_convert_fusion.9), channel_id=1, source_target_pairs={{0,8},{4,12},{8,0},{12,4},{16,24},{20,28},{24,16},{28,20},{1,9},{5... | collective-permute-start | bytes 811016 | tf_op jit(solution)/shard_map/ppermute | solution.py:524
  599.8 70.1 %collective-permute-start.36 = (bf16[256,4096]{1,0:T(8,128)(2,1)}, bf16[256,4096]{1,0:T(8,128)(2,1)}, u32[]{:S(2)}, u32[]{:S(2)}) collective-permute-start(bf16[256,4096]{1,0:T(8,128)(2,1)} %pad_maximum_fusion.3), channel_id=1, source_target_pairs={{0,1},{1,0},{2,3},{3,2},{4,5},{5,4},{6,7},{7,6},{8,9},{9,8},{10,11... | collective-permute-start | bytes 6291464 | tf_op jit(solution)/shard_map/ppermute | solution.py:337
  603.4 24.7 %all-to-all-start.1 = ((bf16[8,512,128]{2,1,0:T(8,128)(2,1)}), bf16[8,512,128]{2,1,0:T(8,128)(2,1)}, u32[]{:S(2)}, u32[]{:S(2)}) async-start(bf16[8,512,128]{2,1,0:T(8,128)(2,1)} %bitcast.214), calls=%async_computation.1 | async-start | bytes 2097152 | tf_op jit(solution)/shard_map/all_to_all | solution.py:653
  607.7 202.8 %all-gather.9.cloned.1.call-start = ((), (), s32[]{:S(2)}) async-start(), calls=%async_computation.6 | async-start | bytes 5242880 | tf_op jit(solution)/shard_map/all_gather | solution.py:661
  608.9 16.0 %collective-permute-start.39 = (bf16[528,128]{1,0:T(8,128)(2,1)S(1)}, bf16[528,128]{1,0:T(8,128)(2,1)S(1)}, u32[]{:S(2)}, u32[]{:S(2)}) collective-permute-start(bf16[528,128]{1,0:T(8,128)(2,1)S(1)} %dynamic-slice_convert_fusion.13), channel_id=1, source_target_pairs={{0,16},{4,20},{8,24},{12,28},{16,0},{20,4},{24,8},{28,12},{1,17},{... | collective-permute-start | bytes 405512 | tf_op jit(solution)/shard_map/ppermute | solution.py:524
  682.8 235.3 %all-gather.11.cloned.1.call-start = ((), (), s32[]{:S(2)}) async-start(), calls=%async_computation.7 | async-start | bytes 7077888 | tf_op jit(solution)/shard_map/all_gather | solution.py:692
  716.4 51.4 %collective-permute-start.43 = (bf16[256,1536]{1,0:T(8,128)(2,1)}, bf16[256,1536]{1,0:T(8,128)(2,1)S(1)}, u32[]{:S(2)}, u32[]{:S(2)}) collective-permute-start(bf16[256,1536]{1,0:T(8,128)(2,1)} %get-tuple-element.132), channel_id=1, source_target_pairs={{0,4},{4,0},{8,12},{12,8},{16,20},{20,16},{24,28},{28,24},{1,5},{5... | collective-permute-start | bytes 2359304 | tf_op jit(solution)/shard_map/ppermute | solution.py:496
  765.7 4.4 collective-permute-start.45
  766.2 5.0 collective-permute-start.46
  778.9 12.3 %collective-permute-start.48 = (bf16[128,1536]{1,0:T(8,128)(2,1)}, bf16[128,1536]{1,0:T(8,128)(2,1)}, u32[]{:S(2)}, u32[]{:S(2)}) collective-permute-start(bf16[128,1536]{1,0:T(8,128)(2,1)} %get-tuple-element.143), channel_id=1, source_target_pairs={{0,8},{4,12},{8,0},{12,4},{16,24},{20,28},{24,16},{28,20},{1,9},{5... | collective-permute-start | bytes 1179656 | tf_op jit(solution)/shard_map/ppermute | solution.py:501
  779.8 19.7 %collective-permute-start.47 = (bf16[128,1536]{1,0:T(8,128)(2,1)}, bf16[128,1536]{1,0:T(8,128)(2,1)S(1)}, u32[]{:S(2)}, u32[]{:S(2)}) collective-permute-start(bf16[128,1536]{1,0:T(8,128)(2,1)} %get-tuple-element.142), channel_id=1, source_target_pairs={{0,8},{4,12},{8,0},{12,4},{16,24},{20,28},{24,16},{28,20},{1,9},{5... | collective-permute-start | bytes 1179656 | tf_op jit(solution)/shard_map/ppermute | solution.py:501
  781.0 12.2 %collective-permute-start.51 = (bf16[128,1536]{1,0:T(8,128)(2,1)S(1)}, bf16[128,1536]{1,0:T(8,128)(2,1)S(1)}, u32[]{:S(2)}, u32[]{:S(2)}) collective-permute-start(bf16[128,1536]{1,0:T(8,128)(2,1)S(1)} %get-tuple-element.145), channel_id=1, source_target_pairs={{0,16},{4,20},{8,24},{12,28},{16,0},{20,4},{24,8},{28,12},{1,17},{... | collective-permute-start | bytes 1179656 | tf_op jit(solution)/shard_map/ppermute | solution.py:501
  781.8 28.2 %collective-permute-start.50 = (bf16[128,1536]{1,0:T(8,128)(2,1)S(1)}, bf16[128,1536]{1,0:T(8,128)(2,1)S(1)}, u32[]{:S(2)}, u32[]{:S(2)}) collective-permute-start(bf16[128,1536]{1,0:T(8,128)(2,1)S(1)} %get-tuple-element.144), channel_id=1, source_target_pairs={{0,16},{4,20},{8,24},{12,28},{16,0},{20,4},{24,8},{28,12},{1,17},{... | collective-permute-start | bytes 1179656 | tf_op jit(solution)/shard_map/ppermute | solution.py:501
  792.5 16.3 %collective-permute-start.49 = (bf16[128,1536]{1,0:T(8,128)(2,1)S(1)}, bf16[128,1536]{1,0:T(8,128)(2,1)S(1)}, u32[]{:S(2)}, u32[]{:S(2)}) collective-permute-start(bf16[128,1536]{1,0:T(8,128)(2,1)S(1)} %fusion.60), channel_id=1, source_target_pairs={{0,16},{4,20},{8,24},{12,28},{16,0},{20,4},{24,8},{28,12},{1,17},{... | collective-permute-start | bytes 1179656 | tf_op jit(solution)/shard_map/ppermute | solution.py:501
  793.3 16.7 %collective-permute-start.52 = (bf16[128,1536]{1,0:T(8,128)(2,1)S(1)}, bf16[128,1536]{1,0:T(8,128)(2,1)S(1)}, u32[]{:S(2)}, u32[]{:S(2)}) collective-permute-start(bf16[128,1536]{1,0:T(8,128)(2,1)S(1)} %fusion.58), channel_id=1, source_target_pairs={{0,8},{4,12},{8,0},{12,4},{16,24},{20,28},{24,16},{28,20},{1,9},{5... | collective-permute-start | bytes 1179656 | tf_op jit(solution)/shard_map/ppermute | solution.py:501
  816.4 5.1 collective-permute-start.58
  821.5 7.7 collective-permute-start.59
  829.2 37.7 %collective-permute-start.60 = (bf16[528,128]{1,0:T(8,128)(2,1)S(1)}, bf16[528,128]{1,0:T(8,128)(2,1)S(1)}, u32[]{:S(2)}, u32[]{:S(2)}) collective-permute-start(bf16[528,128]{1,0:T(8,128)(2,1)S(1)} %add_convert_fusion.6), channel_id=1, source_target_pairs={{0,16},{4,20},{8,24},{12,28},{16,0},{20,4},{24,8},{28,12},{1,17},{... | collective-permute-start | bytes 405512 | tf_op jit(solution)/shard_map/ppermute | solution.py:540
  867.0 8.2 collective-permute-start.61
  875.3 20.6 %collective-permute-start.62 = (bf16[528,512]{1,0:T(8,128)(2,1)S(1)}, bf16[528,512]{1,0:T(8,128)(2,1)S(1)}, u32[]{:S(2)}, u32[]{:S(2)}) collective-permute-start(bf16[528,512]{1,0:T(8,128)(2,1)S(1)} %pad_maximum_fusion.5), channel_id=1, source_target_pairs={{0,4},{4,0},{8,12},{12,8},{16,20},{20,16},{24,28},{28,24},{1,5},{5... | collective-permute-start | bytes 1622024 | tf_op jit(solution)/shard_map/ppermute | solution.py:540
  878.9 3.5 collective-permute-start.54
  889.6 4.4 collective-permute-start.57
  (92 other events, 1012.9 us)
Sparse Core Ops, SparseCore 0:
  77.5 126.5 all-gather.4
  237.9 86.0 all-gather.6
  402.0 111.9 reduce-scatter.1
  682.9 127.1 all-gather.8
  816.5 46.9 all-gather.10

commit v5 on v4

--- a/solution.py
+++ b/solution.py
@@ -1,3 +1,5 @@
+import functools
+
 import jax
 import jax.numpy as jnp
 from jax import lax
@@ -245,15 +247,18 @@
     return value
 
 
-def gathered_near(value):
+def gathered_near(value, beside=None):
     size = lax.axis_size("narrow")
     rows = value.shape[0]
     around = [value]
     for by in range(1, size):
         around.append(lax.ppermute(value, "narrow", cycle(size, size - by)))
+    if beside is not None:
+        *around, beside = together(*around, beside)
     twice = jnp.concatenate(around + around[:-1], axis=0)
     start = lax.rem(size - lax.axis_index("narrow"), size) * rows
-    return lax.dynamic_slice_in_dim(twice, start, size * rows, 0)
+    whole = lax.dynamic_slice_in_dim(twice, start, size * rows, 0)
+    return whole if beside is None else (whole, beside)
 
 
 def scattered_near(value):
@@ -269,36 +274,15 @@
     return total
 
 
-def chain_gather(value):
-    size = lax.axis_size("narrow")
-    rows = value.shape[0]
-    rising, falling = value, value
-    low, high = [], []
-    for step in range(1, size):
-        rising = lax.ppermute(rising, "narrow", [(i, i + 1) for i in range(step - 1, size - 1)])
-        falling = lax.ppermute(falling, "narrow", [(i, i - 1) for i in range(1, size - step + 1)])
-        low.append(rising)
-        high.append(falling)
-    line = jnp.concatenate(low[::-1] + [value] + high, axis=0)
-    start = (size - 1 - lax.axis_index("narrow")) * rows
-    return lax.dynamic_slice_in_dim(line, start, size * rows, 0)
-
-
-def chain_scatter(value):
+def sent_around(blocks):
     size = lax.axis_size("narrow")
     place = lax.axis_index("narrow")
 
-    def block(index):
-        return lax.dynamic_index_in_dim(value, jnp.clip(index, 0, size - 1), 0, keepdims=False)
-
-    rising, falling = None, None
-    for step in range(1, size):
-        up, down = block(size - step + place), block(step + place - size)
-        if rising is not None:
-            up, down = up + rising, down + falling
-        rising = lax.ppermute(up, "narrow", [(i, i + 1) for i in range(step)])
-        falling = lax.ppermute(down, "narrow", [(size - 1 - i, size - 2 - i) for i in range(step)])
-    return block(place) + rising + falling
+    def block(by):
+        return lax.dynamic_index_in_dim(blocks, lax.rem(place + by, size), 0, keepdims=False)
+
+    moved = [lax.ppermute(block(by), "narrow", cycle(size, by)) for by in range(1, size)]
+    return jnp.stack([block(0)] + moved)
 
 
 class WorkerPiece:
@@ -387,92 +371,285 @@
     )
 
 
-STREAMS = 4
-
-
-def take_kernel(ids_ref, table_ref, out_ref, held, rows):
-    step, count, size = pl.program_id(0), out_ref.shape[0], table_ref.shape[0]
+STREAMS = 2
+
+
+class Owners:
+    def __init__(self, tokens, vshard):
+        size = lax.axis_size("narrow")
+        place = lax.axis_index("narrow")
+        count = tokens.shape[1]
+        self.room = count * 7 // 16
+        owner = tokens // vshard
+        held = (owner[None] == jnp.arange(size)[:, None, None]).astype(jnp.bfloat16)
+        tiles = held.reshape(-1, count // 128, 128)
+        order = jnp.arange(128)
+        within = jnp.einsum(
+            "btl,lm->btm",
+            tiles,
+            (order[:, None] < order[None]).astype(jnp.bfloat16),
+            preferred_element_type=jnp.float32,
+        )
+        sums = jnp.sum(tiles.astype(jnp.float32), axis=2)
+        tile = jnp.arange(count // 128)
+        before = jnp.sum(jnp.where(tile[:, None] < tile[None], sums[:, :, None], 0.0), axis=1)
+        rank = (within + before[..., None]).reshape(size, size, count) * held.astype(jnp.float32)
+        rank = jnp.sum(rank, axis=0).astype(jnp.int32)
+        self.full = jnp.max(jnp.sum(sums, axis=1)) > self.room
+        self.count, self.vshard = count, vshard
+        own = lax.dynamic_index_in_dim(owner, place, 0, keepdims=False)
+        self.rank = lax.dynamic_index_in_dim(rank, place, 0, keepdims=False)
+        self.behind = lax.rem(place - own + size, size)
+        self.slots = jnp.where(owner == place, tokens - place * vshard, vshard)
+
+    def behind_slots(self, room):
+        return self.behind * room + jnp.minimum(self.rank, room - 1)
+
+    def packed(self, slots):
+        base = self.vshard + 1
+        order = jnp.arange(self.count) * base + slots
+        order = jnp.where(slots < self.vshard, order, order + self.count * base)
+        order = lax.sort(order)
+        return order % base, order // base % self.count
+
+
+def pack_kernel(ids_ref, table_ref, out_ref, held, *rows):
+    step, count, size = pl.program_id(0), out_ref.shape[1], table_ref.shape[0]
 
     @pl.when(step == 0)
     def _():
         held[0:size, :] = table_ref[...]
         held[size:, :] = jnp.zeros((8, table_ref.shape[1]), jnp.float32)
-
-    @pl.loop(0, count, step=16)
+        for part in rows:
+            part[...] = jnp.zeros_like(part)
+
+    base = [(step * len(rows) + index) * count for index in range(len(rows))]
+
+    def some(turn, used):
+        used = list(used)
+        for by in range(8):
+            for index, part in enumerate(rows):
+                place = ids_ref[base[index] + turn * 8 + by]
+                part[pl.ds(used[index], 1), :] = held[pl.ds(place, 1), :]
+                used[index] = used[index] + jnp.where(place < size, 1, 0)
+        return tuple(used)
+
+    lax.fori_loop(0, count // 8, some, (0,) * len(rows))
+    for index, part in enumerate(rows):
+        out_ref[index] = part[0:count, :].astype(out_ref.dtype)
+
+
+def packed_rows(ids, table):
+    size, cols = table.shape
+    places, count = ids.shape
+    return pl.pallas_call(
+        pack_kernel,
+        grid_spec=pltpu.PrefetchScalarGridSpec(
+            num_scalar_prefetch=1,
+            grid=(places // STREAMS,),
+            in_specs=[pl.BlockSpec((size, cols), lambda step, ids: (0, 0))],
+            out_specs=pl.BlockSpec((STREAMS, count, cols), lambda step, ids: (step, 0, 0)),
+            scratch_shapes=[pltpu.VMEM((size + 8, cols), jnp.float32)]
+            + [pltpu.VMEM((count + 8, cols), jnp.float32)] * STREAMS,
+        ),
+        out_shape=jax.ShapeDtypeStruct((places, count, cols), jnp.bfloat16),
+        compiler_params=pltpu.CompilerParams(vmem_limit_bytes=40 * 2**20),
+        cost_estimate=pl.CostEstimate(flops=0, bytes_accessed=15 * 10**7, transcendentals=0),
+        name="pack_rows",
+    )(ids.reshape(-1), table)
+
+
+def take_kernel(ids_ref, table_ref, out_ref, held, rows):
+    held[...] = table_ref[...].astype(jnp.float32)
+
+    @pl.loop(0, out_ref.shape[0], step=16)
     def _(first):
         for by in range(16):
-            place = ids_ref[step * count + first + by]
-            rows[pl.ds(first + by, 1), :] = held[pl.ds(place, 1), :]
+            rows[pl.ds(first + by, 1), :] = held[pl.ds(ids_ref[first + by], 1), :]
 
     out_ref[...] = rows[...].astype(out_ref.dtype)
 
 
 def taken_rows(ids, table):
-    size, cols = table.shape
-    chunk = 2048
+    count, cols = ids.shape[0], table.shape[1]
     return pl.pallas_call(
         take_kernel,
         grid_spec=pltpu.PrefetchScalarGridSpec(
             num_scalar_prefetch=1,
-            grid=(ids.shape[0] // chunk,),
-            in_specs=[pl.BlockSpec((size, cols), lambda step, ids: (0, 0))],
-            out_specs=pl.BlockSpec((chunk, cols), lambda step, ids: (step, 0)),
+            grid=(1,),
+            in_specs=[pl.BlockSpec(table.shape, lambda step, ids: (0, 0))],
+            out_specs=pl.BlockSpec((count, cols), lambda step, ids: (0, 0)),
             scratch_shapes=[
-                pltpu.VMEM((size + 8, cols), jnp.float32),
-                pltpu.VMEM((chunk, cols), jnp.float32),
+                pltpu.VMEM(table.shape, jnp.float32),
+                pltpu.VMEM((count, cols), jnp.float32),
             ],
         ),
-        out_shape=jax.ShapeDtypeStruct((ids.shape[0], cols), jnp.bfloat16),
-        compiler_params=pltpu.CompilerParams(vmem_limit_bytes=32 * 2**20),
+        out_shape=jax.ShapeDtypeStruct((count, cols), table.dtype),
+        compiler_params=pltpu.CompilerParams(vmem_limit_bytes=40 * 2**20),
         cost_estimate=FREE,
         name="take_rows",
     )(ids, table)
 
 
-def add_kernel(ids_ref, rows_ref, out_ref, rows, *sums):
-    step, count, size = pl.program_id(0), rows_ref.shape[1], out_ref.shape[0]
-    stream = pl.num_programs(0) * count
-
-    @pl.when(step == 0)
-    def _():
-        for part in sums:
-            part[...] = jnp.zeros_like(part)
-
+def add_kernel(length, ids_ref, from_ref, rows_ref, out_ref, rows, *sums):
+    size, each = out_ref.shape[0], rows_ref.shape[1]
+    for part in sums:
+        part[...] = jnp.zeros_like(part)
     rows[...] = rows_ref[...].astype(jnp.float32)
 
-    @pl.loop(0, count, step=8)
+    @pl.loop(0, length, step=8)
     def _(first):
         for by in range(8):
             for index, part in enumerate(sums):
-                place = ids_ref[index * stream + step * count + first + by]
-                part[pl.ds(place, 1), :] += rows[index, pl.ds(first + by, 1), :]
-
-    @pl.when(step == pl.num_programs(0) - 1)
-    def _():
-        total = sums[0][0:size, :]
-        for part in sums[1:]:
-            total = total + part[0:size, :]
-        out_ref[...] = total
-
-
-def added_rows(ids, values, size):
-    count, cols = values.shape
-    chunk = 512
+                place = ids_ref[index * each + first + by]
+                row = from_ref[index * each + first + by]
+                part[pl.ds(place, 1), :] += rows[index, pl.ds(row, 1), :]
+
+    total = sums[0][0:size, :]
+    for part in sums[1:]:
+        total = total + part[0:size, :]
+    out_ref[...] = total
+
+
+def added_rows(ids, rows, values, size, length):
+    places, count, cols = values.shape
     return pl.pallas_call(
-        add_kernel,
+        functools.partial(add_kernel, length),
         grid_spec=pltpu.PrefetchScalarGridSpec(
-            num_scalar_prefetch=1,
-            grid=(count // STREAMS // chunk,),
-            in_specs=[pl.BlockSpec((STREAMS, chunk, cols), lambda step, ids: (0, step, 0))],
-            out_specs=pl.BlockSpec((size, cols), lambda step, ids: (0, 0)),
-            scratch_shapes=[pltpu.VMEM((STREAMS, chunk, cols), jnp.float32)]
-            + [pltpu.VMEM((size + 8, cols), jnp.float32)] * STREAMS,
+            num_scalar_prefetch=2,
+            grid=(1,),
+            in_specs=[pl.BlockSpec(values.shape, lambda step, ids, rows: (0, 0, 0))],
+            out_specs=pl.BlockSpec((size, cols), lambda step, ids, rows: (0, 0)),
+            scratch_shapes=[pltpu.VMEM(values.shape, jnp.float32)]
+            + [pltpu.VMEM((size + 8, cols), jnp.float32)] * places,
         ),
         out_shape=jax.ShapeDtypeStruct((size, cols), jnp.float32),
-        compiler_params=pltpu.CompilerParams(vmem_limit_bytes=40 * 2**20),
-        cost_estimate=pl.CostEstimate(flops=0, bytes_accessed=10**8, transcendentals=0),
+        compiler_params=pltpu.CompilerParams(vmem_limit_bytes=56 * 2**20),
+        cost_estimate=pl.CostEstimate(flops=0, bytes_accessed=5 * 10**7, transcendentals=0),
         name="add_rows",
-    )(ids, values.reshape(STREAMS, count // STREAMS, cols))
+    )(ids.reshape(-1), rows.reshape(-1), values)
+
+
+def span_kernel(momentum_ref, grad_ref, error_ref, span_ref, sum_ref):
+    grad = grad_ref[...].astype(jnp.float32)
+    span = BETA * momentum_ref[...] + (1.0 - BETA) * grad + error_ref[0]
+    span_ref[...] = span
+
+    @pl.when(pl.program_id(0) == 0)
+    def _():
+        sum_ref[...] = jnp.zeros_like(sum_ref)
+
+    sum_ref[...] += jnp.sum(jnp.abs(span), axis=0, keepdims=True)
+
+
+def span_of(momentum, grad, error, start):
+    rows, cols = grad.shape
+    block = 1024
+    first = start // block
+    span, sums = pl.pallas_call(
+        span_kernel,
+        grid=(cols // block,),
+        in_specs=[
+            pl.BlockSpec((rows, block), lambda step: (0, first + step)),
+            pl.BlockSpec((rows, block), lambda step: (0, step)),
+            pl.BlockSpec((1, rows, block), lambda step: (0, 0, first + step)),
+        ],
+        out_specs=[
+            pl.BlockSpec((rows, block), lambda step: (0, step)),
+            pl.BlockSpec((1, block), lambda step: (0, 0)),
+        ],
+        out_shape=[
+            jax.ShapeDtypeStruct((rows, cols), jnp.float32),
+            jax.ShapeDtypeStruct((1, block), jnp.float32),
+        ],
+        compiler_params=pltpu.CompilerParams(vmem_limit_bytes=24 * 2**20),
+        cost_estimate=FREE,
+        name="span",
+    )(momentum, grad, error)
+    return span, jnp.sum(sums)
+
+
+def press_kernel(steps, scale_ref, *refs):
+    *span_refs, error_ref, sent_ref = refs
+    step = pl.program_id(0)
+    scale = scale_ref[0]
+    inverse = scale_ref[1]
+    for index, span_ref in enumerate(span_refs):
+
+        @pl.when((step >= steps[index]) & (step < steps[index + 1]))
+        def _():
+            span = span_ref[...]
+            sent = scale * jnp.tanh(span * inverse)
+            error_ref[0] = span - sent
+            sent_ref[0] = sent.astype(jnp.bfloat16)
+
+
+def pressed(spans, scale, parts):
+    rows = spans[0].shape[0]
+    cols = sum(span.shape[1] for span in spans)
+    block = 512
+    each = cols // parts // block
+    steps = [0]
+    for span in spans:
+        steps.append(steps[-1] + span.shape[1] // block)
+
+    def of(index):
+        low, count = steps[index], steps[index + 1] - steps[index]
+        return pl.BlockSpec((rows, block), lambda step: (0, jnp.clip(step - low, 0, count - 1)))
+
+    return pl.pallas_call(
+        functools.partial(press_kernel, steps),
+        grid=(steps[-1],),
+        in_specs=[pl.BlockSpec(memory_space=pltpu.SMEM)] + [of(i) for i in range(len(spans))],
+        out_specs=[
+            pl.BlockSpec((1, rows, block), lambda step: (0, 0, step)),
+            pl.BlockSpec((1, rows, block), lambda step: (step // each, 0, step % each)),
+        ],
+        out_shape=[
+            jax.ShapeDtypeStruct((1, rows, cols), jnp.float32),
+            jax.ShapeDtypeStruct((parts, rows, cols // parts), jnp.bfloat16),
+        ],
+        compiler_params=pltpu.CompilerParams(vmem_limit_bytes=24 * 2**20),
+        cost_estimate=FREE,
+        name="press",
+    )(jnp.stack([scale, 1.0 / scale]), *spans)
+
+
+def update_kernel(grad_ref, head_ref, table_ref, first_ref, second_ref, *out_refs):
+    first_out, update_ref, weight_sum, update_sum = out_refs
+    grad = grad_ref[...] + head_ref[...].astype(jnp.float32)
+    first = BETA * first_ref[...] + (1.0 - BETA) * grad
+    table = table_ref[...]
+    update = first / (jnp.sqrt(second_ref[...]) + OPT_EPS) + DECAY * table
+    first_out[...] = first
+    update_ref[...] = update
+
+    @pl.when(pl.program_id(0) == 0)
+    def _():
+        weight_sum[...] = jnp.zeros_like(weight_sum)
+        update_sum[...] = jnp.zeros_like(update_sum)
+
+    weight_sum[...] += jnp.sum(table * table, axis=0, keepdims=True)
+    update_sum[...] += jnp.sum(update * update, axis=0, keepdims=True)
+
+
+def table_update(grad, head, table, first, second):
+    size, cols = table.shape
+    block = size // 9 if size % 9 == 0 and size // 9 % 16 == 0 else size
+    whole = pl.BlockSpec((block, cols), lambda step: (step, 0))
+    line = pl.BlockSpec((1, cols), lambda step: (0, 0))
+    moment, update, *sums = pl.pallas_call(
+        update_kernel,
+        grid=(size // block,),
+        in_specs=[whole] * 5,
+        out_specs=[whole, whole, line, line],
+        out_shape=[jax.ShapeDtypeStruct((size, cols), jnp.float32)] * 2
+        + [jax.ShapeDtypeStruct((1, cols), jnp.float32)] * 2,
+        compiler_params=pltpu.CompilerParams(vmem_limit_bytes=56 * 2**20),
+        cost_estimate=FREE,
+        name="update",
+    )(grad, head, table, first, second)
+    return moment, update, tuple(jnp.sum(part)[None] for part in sums)
 
 
 def wide_places():
@@ -482,20 +659,7 @@
 
 def scattered_sum(sent):
     n_wide = lax.axis_size("wide")
-    rows, cols = sent.shape
-    part = cols // n_wide
-    if not paired_mesh():
-        whole = lax.psum(sent.astype(jnp.bfloat16), "wide").astype(jnp.float32)
-        return lax.dynamic_slice_in_dim(whole, lax.axis_index("wide") * part, part, 1)
     core, x, y = wide_places()
-
-    def block(value, place):
-        return lax.dynamic_slice_in_dim(value, place * part, part, 1)
-
-    give = [block(sent, 2 * chip + 1 - core).astype(jnp.bfloat16) for chip in range(4)]
-    take = [lax.ppermute(part_of, "wide", swap_pairs(n_wide, 1)) for part_of in give]
-    chips = jnp.stack([block(sent, 2 * chip + core) + take[chip] for chip in range(4)])
-    half = rows // 2
 
     def send(value, bit):
         return lax.ppermute(value.astype(jnp.bfloat16), "wide", swap_pairs(n_wide, bit))
@@ -503,15 +667,27 @@
     def pick(value, index):
         return lax.dynamic_index_in_dim(value, index, 0, keepdims=False)
 
-    upper, lower = chips[:, 0:half], chips[:, half:]
-    upper_far = send(pick(upper, 2 * (1 - y) + 1 - x), 2)
-    upper_near = send(pick(upper, 2 * y + 1 - x), 2)
-    lower_far = send(pick(lower, 2 * (1 - y) + 1 - x), 4)
-    lower_near = send(pick(lower, 2 * (1 - y) + x), 4)
-    upper_far = send(pick(upper, 2 * (1 - y) + x) + upper_far, 4)
-    lower_far = send(pick(lower, 2 * y + 1 - x) + lower_far, 2)
-    own_upper = pick(upper, 2 * y + x) + upper_near + upper_far
-    own_lower = pick(lower, 2 * y + x) + lower_near + lower_far
+    rows, cols = sent.shape[1:]
+    by_core = sent.reshape(n_wide // 2, 2, rows, cols)
+    give = lax.dynamic_index_in_dim(by_core, 1 - core, 1, keepdims=False)
+    keep = lax.dynamic_index_in_dim(by_core, core, 1, keepdims=False)
+    take = send(give, 1)
+    half = rows // 2
+
+    def chip(y_of, x_of, part):
+        low, high = part * half, (part + 1) * half
+        index = 2 * y_of + x_of
+        own, other = pick(keep[:, low:high], index), pick(take[:, low:high], index)
+        return own.astype(jnp.float32) + other.astype(jnp.float32)
+
+    upper_far = send(chip(1 - y, 1 - x, 0), 2)
+    lower_far = send(chip(1 - y, 1 - x, 1), 4)
+    upper_near = send(chip(y, 1 - x, 0), 2)
+    lower_near = send(chip(1 - y, x, 1), 4)
+    upper_far = send(chip(1 - y, x, 0) + upper_far.astype(jnp.float32), 4)
+    lower_far = send(chip(y, 1 - x, 1) + lower_far.astype(jnp.float32), 2)
+    own_upper = chip(y, x, 0) + upper_near.astype(jnp.float32) + upper_far.astype(jnp.float32)
+    own_lower = chip(y, x, 1) + lower_near.astype(jnp.float32) + lower_far.astype(jnp.float32)
     return jnp.concatenate([own_upper, own_lower], axis=0)
 
 
@@ -526,8 +702,6 @@
 
 
 def small_total(value):
-    if not paired_mesh():
-        return lax.psum(value, ("wide", "narrow"))
     n_wide, n_narrow = lax.axis_size("wide"), lax.axis_size("narrow")
     bit = 1
     while bit < n_narrow:
@@ -573,21 +747,32 @@
         token_ids, mlm_labels, mlm_valid, doc_ids, mlm_pos = hosted_rows(
             token_ids, mlm_labels, mlm_valid, doc_ids, mlm_pos
         )
-        layer_rows = chain_gather(layer_low)
+        owners = Owners(token_ids.reshape(n_narrow, n_wide * L), vshard)
+        picked = packed_rows(owners.slots, table)
+        layer_rows, picked = gathered_near(layer_low, picked)
     else:
         layer_rows = lax.all_gather(layer_low, "narrow", axis=0, tiled=True)
     weights = lax.all_gather(layer_rows, "wide", axis=1, tiled=True)
-    local_ids = token_ids - narrow_me * vshard
-    inside = (local_ids >= 0) & (local_ids < vshard)
     if paired:
-        slots = jnp.where(inside, local_ids, vshard).reshape(-1)
-        picked = taken_rows(slots, table).reshape(n_narrow, n_wide * L, -1)
-        looked = chain_scatter(picked).reshape(n_wide, L, -1)
-        looked = lax.all_to_all(looked, "wide", 0, 0)
+
+        def looked_up(room):
+            rows = sent_around(picked[:, 0:room])
+            return taken_rows(owners.behind_slots(room), rows.reshape(n_narrow * room, -1))
+
+        layer_rows, picked = together(layer_rows, picked)
+        looked = looked_up(owners.room)
+        looked = lax.cond(owners.full, lambda: looked_up(owners.count), lambda: looked)
+        looked = lax.all_to_all(looked.reshape(n_wide, L, -1), "wide", 0, 0)
         looked = looked.transpose(1, 0, 2).reshape(1, L, D)
-        table_low, weights, looked = together(table_low, weights, looked)
+        looked, slots = together(looked, owners.slots)
+        packed_ids, packed_rows_at = owners.packed(slots)
+        table_low, weights, looked, packed_ids, packed_rows_at = together(
+            table_low, weights, looked, packed_ids, packed_rows_at
+        )
         table_cols = lax.all_gather(table_low, "wide", axis=1, tiled=True)
     else:
+        local_ids = token_ids - narrow_me * vshard
+        inside = (local_ids >= 0) & (local_ids < vshard)
         slots = jnp.where(inside, local_ids, vshard).reshape(-1)
         table_cols = lax.all_gather(table_low, "wide", axis=1, tiled=True)
         picked = jnp.take(table_cols, jnp.clip(local_ids, 0, vshard - 1), axis=0)
@@ -651,14 +836,14 @@
     if paired:
         cut = dembed.astype(jnp.bfloat16).reshape(L, n_wide, D // n_wide).transpose(1, 0, 2)
         cut = lax.all_to_all(cut, "wide", 0, 0).reshape(n_wide * L, D // n_wide)
-        small_grad = small_halved(small_grad)
+        small_grad = small_total(small_halved(small_grad))
         down, up = pieces[2], pieces[1]
         cut, mixed.away, small_grad, down.result, up.result, table_head = together(
             cut, mixed.away, small_grad, down.result, up.result, table_head
         )
         mixed.finish()
         cut, mixed.result = together(cut, mixed.result)
-        group_rows = lax.all_gather(cut, "narrow", axis=0, tiled=True)
+        group_rows = lax.all_gather(cut, "narrow", axis=0)
     else:
         mixed.finish()
         group_rows = lax.all_gather(dembed_rows.astype(jnp.bfloat16), "narrow", axis=0, tiled=True)
@@ -668,30 +853,50 @@
         cut = table_grad.astype(jnp.bfloat16).reshape(vshard, n_wide, D // n_wide)
         table_grad = lax.psum_scatter(cut.transpose(1, 0, 2), "wide", scatter_dimension=0)
         table_grad = table_grad.astype(jnp.float32)
-    worker_grad = jnp.concatenate([piece.result for piece in pieces], axis=1)
-    span = BETA * layer_m + (1.0 - BETA) * worker_grad.astype(jnp.float32) + worker_err[0]
-    scale = jnp.mean(jnp.abs(span)) + MAG_EPS
-    sent = scale * jnp.tanh(span / scale)
-    new_worker = (span - sent)[None]
     part_cols = layer.shape[1]
-    server_in = scattered_sum(sent) / n_wide + server_err
     if paired:
-        server_in, group_rows, small_grad = together(server_in, group_rows, small_grad)
-        table_grad = added_rows(slots, group_rows, vshard)
-        table_grad = table_grad + table_head.astype(jnp.float32)
-    small_grad = small_total(small_grad)
+        spans, total, start = [], 0.0, [0, 4 * D, 8 * D]
+        for piece, first in zip(pieces[::-1], start[::-1]):
+            span, amount = span_of(layer_m, piece.result, worker_err, first)
+            spans.insert(0, span)
+            total = total + amount
+        scale = total / (layer_m.shape[0] * layer_m.shape[1]) + MAG_EPS
+        new_worker, sent = pressed(spans, scale, n_wide)
+        server_in = scattered_sum(sent) / n_wide + server_err
+    else:
+        worker_grad = jnp.concatenate([piece.result for piece in pieces], axis=1)
+        span = BETA * layer_m + (1.0 - BETA) * worker_grad.astype(jnp.float32) + worker_err[0]
+        scale = jnp.mean(jnp.abs(span)) + MAG_EPS
+        sent = scale * jnp.tanh(span / scale)
+        new_worker = (span - sent)[None]
+        summed = lax.psum(sent.astype(jnp.bfloat16), "wide").astype(jnp.float32)
+        mixed = lax.dynamic_slice_in_dim(summed, wide_me * part_cols, part_cols, 1) / n_wide
+        server_in = mixed + server_err
+    sscale = jnp.mean(jnp.abs(server_in)) + MAG_EPS
+    server_out = sscale * jnp.tanh(server_in / sscale)
+    new_server = server_in - server_out
+    server_low = server_out.astype(jnp.bfloat16)
+    if paired:
+        server_low, group_rows = together(server_low, group_rows)
+
+        def added(length):
+            return added_rows(packed_ids, packed_rows_at, group_rows, vshard, length)
+
+        table_grad = lax.cond(
+            owners.full, lambda: added(owners.count), lambda: added(owners.room)
+        )
+        table_mom, table_upd, table_norms = table_update(
+            table_grad, table_head, table, table_m, table_v
+        )
+    else:
+        small_grad = lax.psum(small_grad, ("wide", "narrow"))
+        table_mom = BETA * table_m + (1.0 - BETA) * table_grad
+        table_upd = table_mom / (jnp.sqrt(table_v) + OPT_EPS) + DECAY * table
+        table_norms = (jnp.sum(table * table)[None], jnp.sum(table_upd * table_upd)[None])
     small_mom = BETA * small_m + (1.0 - BETA) * small_grad
     small_upd = small_mom / (jnp.sqrt(small_v) + OPT_EPS) + DECAY * small
     small_norms = (jnp.sum(small * small)[None], jnp.sum(small_upd * small_upd)[None])
-    table_mom = BETA * table_m + (1.0 - BETA) * table_grad
-    table_upd = table_mom / (jnp.sqrt(table_v) + OPT_EPS) + DECAY * table
-    table_norms = (jnp.sum(table * table)[None], jnp.sum(table_upd * table_upd)[None])
-    sscale = jnp.mean(jnp.abs(server_in)) + MAG_EPS
-    server_out = sscale * jnp.tanh(server_in / sscale)
-    new_server = server_in - server_out
-    new_m = lax.all_gather(server_out.astype(jnp.bfloat16), "wide", axis=1, tiled=True).astype(
-        server_out.dtype
-    )
+    new_m = lax.all_gather(server_low, "wide", axis=1, tiled=True).astype(jnp.float32)
     layer_upd = server_out / (jnp.sqrt(layer_v) + OPT_EPS) + DECAY * layer
     column = wide_me * part_cols + jnp.arange(part_cols)
     which = (

time: 942 us -> 1050 us (1.11)
  waiting for transfers between devices: 337 us -> 411 us
  Pallas kernels: 80.4 us -> 142 us
  other arithmetic: 145 us -> 116 us
  starting transfers between devices: 135 us -> 106 us
  local copies, waits for them, and re-layouts: 58.6 us -> 81.1 us
    all_gather x1, waiting for transfers between devices: 0.02 us -> 122 us  [shards(): weights = lax.all_gather(layer_rows, 'wide', axis=1, tiled=True)]
    ppermute x16 -> x3, waiting for transfers between devices: 135 us -> 27.2 us  [sent_around(): lax.ppermute(block(by), 'narrow', cycle(size, by))]
    pallas_call x1 -> x7, Pallas kernels: 32 us -> 108 us  [the longest x1 52.4 us: packed_rows(): pl.pallas_call(pack_kernel, grid_spec=pltpu.PrefetchScalarGridSpec(num_sc...]
    ppermute x16 -> x3, starting transfers between devices: 77 us -> 5.88 us  [sent_around(): lax.ppermute(block(by), 'narrow', cycle(size, by))]
    ppermute x2, waiting for transfers between devices: 11.7 us -> 48.2 us  [small_total(): other = lax.ppermute(low, 'narrow', swap_pairs(n_narrow, bit))]
    all_gather x2, waiting for transfers between devices: 0.02 us -> 30.1 us  [the longest x1 30.1 us: shards(): group_rows = lax.all_gather(cut, 'narrow', axis=0)]
    ppermute x6 -> x7, starting transfers between devices: 6.03 us -> 29.4 us  [send(): lax.ppermute(value.astype(jnp.bfloat16), 'wide', swap_pairs(n_wide, bit))]
    ppermute x3, waiting for transfers between devices: 108 us -> 86.4 us  [across(): self.away = lax.ppermute(away, 'narrow', sides)]
  transfers between devices with their start and end apart: 70 -> 61, of which waited for: 37 -> 33; matrix products, arithmetic and copies ran while one was open for 30% -> 23% of each run, Pallas kernels for 9% -> 11%
where the time goes in v5:
time: 1050 us; the launch traced here: 1040 us
  waiting for transfers between devices  411 us (39%)
  matrix products  158 us (15%)
  Pallas kernels  142 us (14%)
  other arithmetic  116 us (11%)
  starting transfers between devices  106 us (10%)
  local copies, waits for them, and re-layouts  81.1 us (8%)
  between operations  25.5 us (2%)
    all_gather x1, waiting for transfers between devices, shards(): weights = lax.all_gather(layer_rows, 'wide', axis=1, tiled=True)  122 us
    ppermute x3, waiting for transfers between devices, across(): self.away = lax.ppermute(away, 'narrow', sides)  86.4 us
    dot_general x5, matrix products, matmul(): return jnp.dot(left, right, preferred_element_type=jnp.float32)  63.5 us
    pallas_call x1, Pallas kernels, packed_rows(): pl.pallas_call(pack_kernel, grid_spec=pltpu.PrefetchScalarGridSpec(num_sc...  52.4 us
    ppermute x2, waiting for transfers between devices, small_total(): other = lax.ppermute(low, 'narrow', swap_pairs(n_narrow, bit))  48.2 us
    unnamed x223, local copies, waits for them, and re-layouts  43 us
    dot_general x5, matrix products, matmul_nt(): lax.dot_general(left, right, (((1,), (1,)), ((), ())), preferred_element_...  40.1 us
    dot_general x16, matrix products, matmul_tn(): lax.dot_general(left, right, (((0,), (0,)), ((), ())), preferred_element_...  36.4 us
  transfers between devices with their start and end apart: 61, of which 33 were waited for; matrix products, arithmetic and copies ran while one was open for 23% of the time, Pallas kernels for 11%

profile of v5, /device:TPU:0, one launch (start us, length us, event | category | flops | bytes accessed | tf_op | source)
XLA Modules:
  0.0 1040.4 jit_solution(17554508980184681922)
XLA Ops:
  15.3 3.7 collective-permute-start.4
  29.9 52.4 %pack_rows.1 = bf16[4,4096,128]{2,1,0:T(8,128)(2,1)} custom-call(s32[16384]{0:T(1024)S(1)} %fusion.96.ids_ref, f32[7632,128]{1,0:T(8,128)S(1)} %copy-done.5), custom_call_target="tpu_custom_call" | custom-call | bytes 150000000 | tf_op jit(solution)/shard_map/pack_rows/pallas_call | solution.py:445
  82.4 3.9 collective-permute-done.5
  97.2 9.5 collective-permute-done.10
  106.7 17.7 %collective-permute-done.11 = bf16[1792,128]{1,0:T(8,128)(2,1)S(1)} collective-permute-done((bf16[1792,128]{1,0:T(8,128)(2,1)S(1)}, bf16[1792,128]{1,0:T(8,128)(2,1)S(1)}, u32[]{:S(2)}, u32[]{:S(2)}) %collective-permute-start.11) | collective-permute-done | bytes 458784 | tf_op jit(solution)/shard_map/ppermute | solution.py:284
  124.6 6.6 take_rows.3
  131.2 3.6 all-to-all-start
  134.8 15.3 %all-to-all-done = bf16[8,512,128]{2,1,0:T(8,128)(2,1)S(1)} async-done(((bf16[8,512,128]{2,1,0:T(8,128)(2,1)}), bf16[8,512,128]{2,1,0:T(8,128)(2,1)S(1)}, u32[]{:S(2)}, u32[]{:S(2)}) %all-to-all-start) | async-done | bytes 1048608 | tf_op jit(solution)/shard_map/all_to_all | solution.py:765
  152.7 3.6 convert_element_type.385
  156.2 7.7 sort.9.cloned.1.call-done
  165.6 122.2 %all-gather.6.cloned.1.call-done = bf16[1024,12288]{1,0:T(8,128)(2,1)} async-done(((bf16[1024,1536]{1,0:T(8,128)(2,1)}), bf16[1024,12288]{1,0:T(8,128)(2,1)}) %all-gather.6.cloned.1.call-update) | async-done | bytes 25165840 | tf_op jit(solution)/shard_map/all_gather | solution.py:755
  289.2 3.8 collective-permute-start.19
  313.4 6.8 add_convert_fusion.1.q_ref.k_ref.v_ref
  320.3 11.7 %attend.1 = (bf16[512,1024]{1,0:T(8,128)(2,1)S(1)}, f32[8,2,512]{2,1,0:T(2,128)S(1)}) custom-call(bf16[512,3072]{1,0:T(8,128)(2,1)S(1)} %add_convert_fusion.1.q_ref.k_ref.v_ref, bf16[512,3072]{1,0:T(8,128)(2,1)S(1)} %add_convert_fusion.1.q_ref.k_ref.v_ref, bf16[512,3072]{1,0:T(8,128)(2,1)S(1)} %add_convert_fusion.1.q_ref.k_ref.v_ref, ...), custom_call_target="tpu_custom_call" | custom-call | tf_op jit(solution)/shard_map/attend/pallas_call | solution.py:86
  332.0 3.5 fusion.167
  336.4 26.1 %multiply_convert_fusion = (bf16[512,4096]{1,0:T(8,128)(2,1)S(1)}, f32[512,4096]{1,0:T(8,128)}, f32[512,4096]{1,0:T(8,128)}) fusion(f32[4096]{0:T(1024)S(1)} %bitcast.281, bf16[512,1024]{1,0:T(8,128)(2,1)S(1)} %fusion.39, bf16[1024,12288]{1,0:T(8,128)(2,1)} %all-gather.6.cloned.1.call-done), kind=kOutput, calls=%fused_computation.21 | convolution fusion | flops 4433379328 | bytes 30425088 | tf_op jit(solution)/shard_map/dot_general | solution.py:49
  362.6 9.2 fusion.168
  380.9 9.2 collective-permute-done.14
  393.4 11.3 %fusion.169 = (f32[320]{0:T(512)S(1)}, f32[320,7632]{1,0:T(8,128)}) fusion(bf16[7632,1024]{1,0:T(8,128)(2,1)} %all-gather.8.cloned.1.call-done, bf16[560,1024]{1,0:T(8,128)(2,1)} %constant_dynamic-update-slice_fusion.7, s32[]{:T(128)S(6)} %select_n.414, pred[7632]{0:T(1024)(128)(4,1)S(1)} %copy-done.86), kind=kOutput, calls=%fused_computation.413 | convolution fusion | flops 5006591488 | bytes 26063572 | tf_op jit(solution)/shard_map/dot_general | solution.py:59
  404.7 6.6 exponential_reduce_fusion
  419.0 11.5 %fusion.149 = f32[320,1024]{1,0:T(8,128)S(1)} fusion(bf16[7632,1024]{1,0:T(8,128)(2,1)} %all-gather.8.cloned.1.call-done, f32[320,7632]{1,0:T(8,128)S(1)} %copy-done.38, f32[320]{0:T(512)S(1)} %get-tuple-element.268, f32[320]{0:T(512)S(1)} %get-tuple-element.180, s32[7632]{0:T(1024)S(1)} %iota_add_fusion, s32[320]{0:T(512)} %copy-done.87), kind=kOutput, calls=%fused_computation.398 | convolution fusion | flops 5016360960 | bytes 26744384 | tf_op jit(solution)/shard_map/dot_general | solution.py:49
  435.4 17.8 %convert_bitcast_fusion = bf16[8,7632,128]{2,1,0:T(8,128)(2,1)} fusion(f32[320,7632]{1,0:T(8,128)} %get-tuple-element.284, f32[320]{0:T(512)} %copy-done.96, f32[320]{0:T(512)} %copy-done.95, s32[7632]{0:T(1024)S(1)} %iota_add_fusion, s32[320]{0:T(512)S(1)} %copy-done.88, bf16[560,1024]{1,0:T(8,128)(2,1)} %constant_dynamic-update-slice_fusion.7, ...), kind=kOutput, calls=%fused_computation.8 | convolution fusion | flops 5024176128 | bytes 26152004 | tf_op jit(solution)/shard_map/sv,swc->wvc/dot_general | solution.py:816
  464.4 4.2 convolution_convert_fusion.2
  472.3 15.6 %add_convert_fusion = bf16[512,4096]{1,0:T(8,128)(2,1)S(1)} fusion(f32[512,4096]{1,0:T(8,128)} %get-tuple-element.198, f32[512,4096]{1,0:T(8,128)} %get-tuple-element.280, f32[4096]{0:T(1024)S(1)} %bitcast.282, bf16[512,1024]{1,0:T(8,128)(2,1)S(1)} %get-tuple-element.186, bf16[1024,12288]{1,0:T(8,128)(2,1)} %all-gather.6.cloned.1.call-done), kind=kOutput, calls=%fused_computation.20 | convolution fusion | flops 4326424576 | bytes 30425088 | tf_op jit(solution)/shard_map/dot_general | solution.py:49
  494.5 3.8 add_convert_fusion.3
  498.3 9.8 multiply_reduce_fusion.3
  514.6 3.5 fusion.47.do_ref
  522.6 16.5 %attend_back.1 = bf16[512,3072]{1,0:T(8,128)(2,1)S(1)} custom-call(bf16[512,3072]{1,0:T(8,128)(2,1)S(1)} %copy-done.4, bf16[512,3072]{1,0:T(8,128)(2,1)S(1)} %copy-done.4, bf16[512,3072]{1,0:T(8,128)(2,1)S(1)} %copy-done.4, bf16[512,1024]{1,0:T(8,128)(2,1)S(1)} %fusion.47.do_ref, f32[8,2,512]{2,1,0:T(2,128)S(1)} %get-tuple-element.112.lse_ref, ...), custom_call_target="tpu_custom_call" | custom-call | tf_op jit(solution)/shard_map/attend_back/pallas_call | solution.py:130
  539.2 18.8 %collective-permute-done.29 = bf16[256,4096]{1,0:T(8,128)(2,1)} collective-permute-done((bf16[256,4096]{1,0:T(8,128)(2,1)}, bf16[256,4096]{1,0:T(8,128)(2,1)}, u32[]{:S(2)}, u32[]{:S(2)}) %collective-permute-start.29) | collective-permute-done | bytes 2097184 | tf_op jit(solution)/shard_map/ppermute | solution.py:321
  561.8 6.3 multiply_reduce_fusion.4
  569.8 32.6 %collective-permute-done.32 = bf16[256,4096]{1,0:T(8,128)(2,1)S(1)} collective-permute-done((bf16[256,4096]{1,0:T(8,128)(2,1)S(1)}, bf16[256,4096]{1,0:T(8,128)(2,1)S(1)}, u32[]{:S(2)}, u32[]{:S(2)}) %collective-permute-start.32) | collective-permute-done | bytes 2097184 | tf_op jit(solution)/shard_map/ppermute | solution.py:321
  604.0 6.9 concatenate.109
  613.0 3.7 fusion.72
  619.7 4.1 add_convert_fusion.2
  627.4 4.8 fusion.23
  636.2 4.5 collective-permute-done.37
  640.7 15.4 %collective-permute-start.38 = (bf16[528,128]{1,0:T(8,128)(2,1)S(1)}, bf16[528,128]{1,0:T(8,128)(2,1)S(1)}, u32[]{:S(2)}, u32[]{:S(2)}) collective-permute-start(bf16[528,128]{1,0:T(8,128)(2,1)S(1)} %add_convert_fusion.11), channel_id=1, source_target_pairs={{0,2},{1,3},{2,0},{3,1},{4,6},{5,7},{6,4},{7,5},{8,10},{9,11},{10,... | collective-permute-start | bytes 405512 | tf_op jit(solution)/shard_map/ppermute | solution.py:709
  659.5 43.7 %collective-permute-done.38 = bf16[528,128]{1,0:T(8,128)(2,1)S(1)} collective-permute-done((bf16[528,128]{1,0:T(8,128)(2,1)S(1)}, bf16[528,128]{1,0:T(8,128)(2,1)S(1)}, u32[]{:S(2)}, u32[]{:S(2)}) %collective-permute-start.38) | collective-permute-done | bytes 135200 | tf_op jit(solution)/shard_map/ppermute | solution.py:709
  706.0 4.3 all-to-all-start.1
  715.5 15.0 %collective-permute-done.40 = bf16[528,256]{1,0:T(8,128)(2,1)S(1)} collective-permute-done((bf16[528,256]{1,0:T(8,128)(2,1)S(1)}, bf16[528,256]{1,0:T(8,128)(2,1)S(1)}, u32[]{:S(2)}, u32[]{:S(2)}) %collective-permute-start.40) | collective-permute-done | bytes 270368 | tf_op jit(solution)/shard_map/ppermute | solution.py:714
  735.7 35.0 %collective-permute-done.33 = bf16[256,4096]{1,0:T(8,128)(2,1)} collective-permute-done((bf16[256,4096]{1,0:T(8,128)(2,1)}, bf16[256,4096]{1,0:T(8,128)(2,1)}, u32[]{:S(2)}, u32[]{:S(2)}) %collective-permute-start.33) | collective-permute-done | bytes 2097184 | tf_op jit(solution)/shard_map/ppermute | solution.py:321
  770.7 3.3 fusion.30
  779.9 4.6 copy-done
  784.5 3.9 span.3
  791.0 4.6 copy-done.1
  797.2 4.0 span.4
  805.9 4.6 copy-done.2
  810.5 3.9 span.5
  824.4 12.4 %press.1 = (f32[1,256,12288]{2,1,0:T(8,128)}, bf16[8,256,1536]{2,1,0:T(8,128)(2,1)S(1)}) custom-call(f32[2]{0:T(128)S(1)} %pad_maximum_fusion.10.scale_ref, f32[256,4096]{1,0:T(8,128)S(1)} %copy-done.14, f32[256,4096]{1,0:T(8,128)S(1)} %copy-done.12, f32[256,4096]{1,0:T(8,128)S(1)} %copy-done.10), custom_call_target="tpu_custom_call" | custom-call | tf_op jit(solution)/shard_map/press/pallas_call | solution.py:600
  839.1 24.4 %collective-permute-start.45 = (bf16[4,256,1536]{2,1,0:T(8,128)(2,1)}, bf16[4,256,1536]{2,1,0:T(8,128)(2,1)}, u32[]{:S(2)}, u32[]{:S(2)}) collective-permute-start(bf16[4,256,1536]{2,1,0:T(8,128)(2,1)} %get-tuple-element.210), channel_id=1, source_target_pairs={{0,4},{4,0},{8,12},{12,8},{16,20},{20,16},{24,28},{28,24},{1,5},{5... | collective-permute-start | bytes 9437192 | tf_op jit(solution)/shard_map/ppermute | solution.py:665
  865.1 3.9 collective-permute-done.45
  877.1 7.8 collective-permute-done.47
  888.0 5.3 collective-permute-done.46
  893.3 9.4 collective-permute-done.48
  906.9 5.0 multiply_reduce_fusion.11
  912.0 30.1 %all-gather.12.cloned.1.call-done = bf16[16384,128]{1,0:T(8,128)(2,1)} async-done(((bf16[4096,128]{1,0:T(8,128)(2,1)}), bf16[16384,128]{1,0:T(8,128)(2,1)}) %all-gather.12.cloned.1.call-update) | async-done | bytes 4194320 | tf_op jit(solution)/shard_map/all_gather | solution.py:846
  943.6 6.4 multiply_reduce_fusion
  950.1 20.0 %conditional.3 = (f32[7632,128]{1,0:T(8,128)}) conditional(s32[]{:T(128)} %convert_element_type.389, (s32[4,4096]{1,0:T(4,128)S(1)}, s32[4,4096]{1,0:T(4,128)S(1)}, bf16[4,4096,128]{2,1,0:T(8,128)(2,1)S(1)}) %tuple.158, (s32[4,4096]{1,0:T(4,128)S(1)}, s32[4,4096]{1,0:T(4,128)S(1)}, bf16[4,4096,128]{2,1,0:T(8,128)(2,1)S(1)}) %tuple.159), branch_computations={%region_46.47_spmd, %region_47.48_spmd} | conditional | bytes 50262152 | solution.py:885
  951.4 18.4 %add_rows.2 = f32[7632,128]{1,0:T(8,128)} custom-call(s32[16384]{0:T(1024)} %bitcast.249, s32[16384]{0:T(1024)} %bitcast.250, bf16[4,4096,128]{2,1,0:T(8,128)(2,1)S(1)} %get-tuple-element.30.rows_ref), custom_call_target="tpu_custom_call" | custom-call | bytes 50000000 | tf_op jit(solution)/shard_map/cond/branch_0_fun/add_rows/pallas_call | solution.py:516
  970.1 12.5 %update.1 = (f32[7632,128]{1,0:T(8,128)}, f32[7632,128]{1,0:T(8,128)}, f32[1,128]{1,0:T(1,128)}, f32[1,128]{1,0:T(1,128)}) custom-call(f32[7632,128]{1,0:T(8,128)} %get-tuple-element.290.grad_ref, bf16[7632,128]{1,0:T(8,128)(2,1)} %bitcast.237, f32[7632,128]{1,0:T(8,128)} %table_ref.3, f32[7632,128]{1,0:T(8,128)} %first_ref.1, f32[7632,128]{1,0:T(8,128)} %second_ref.1), custom_call_target="tpu_custom_call" | custom-call | tf_op jit(solution)/shard_map/update/pallas_call | solution.py:641
  995.4 3.5 collective-permute-done.55
  999.8 3.6 collective-permute-done.56
  1013.3 4.7 multiply_subtract_fusion.1
  1023.3 9.1 convert_element_type.496
  (503 shorter events, 217.4 us)
Async XLA Ops:
  8.8 1.3 collective-permute-start.7
  10.9 9.1 collective-permute-start.8
  15.3 67.0 %collective-permute-start.4 = (bf16[256,1536]{1,0:T(8,128)(2,1)S(1)}, bf16[256,1536]{1,0:T(8,128)(2,1)S(1)}, u32[]{:S(2)}, u32[]{:S(2)}) collective-permute-start(bf16[256,1536]{1,0:T(8,128)(2,1)S(1)} %convert_element_type.386), channel_id=1, source_target_pairs={{0,3},{1,0},{2,1},{3,2},{4,7},{5,4},{6,5},{7,6},{8,11},{9,8},{10,9... | collective-permute-start | bytes 2359304 | tf_op jit(solution)/shard_map/ppermute | solution.py:255
  19.0 67.3 %collective-permute-start.5 = (bf16[256,1536]{1,0:T(8,128)(2,1)S(1)}, bf16[256,1536]{1,0:T(8,128)(2,1)S(1)}, u32[]{:S(2)}, u32[]{:S(2)}) collective-permute-start(bf16[256,1536]{1,0:T(8,128)(2,1)S(1)} %convert_element_type.386), channel_id=1, source_target_pairs={{0,2},{1,3},{2,0},{3,1},{4,6},{5,7},{6,4},{7,5},{8,10},{9,11},{10,... | collective-permute-start | bytes 2359304 | tf_op jit(solution)/shard_map/ppermute | solution.py:255
  19.0 67.3 %collective-permute-start.6 = (bf16[256,1536]{1,0:T(8,128)(2,1)S(1)}, bf16[256,1536]{1,0:T(8,128)(2,1)}, u32[]{:S(2)}, u32[]{:S(2)}) collective-permute-start(bf16[256,1536]{1,0:T(8,128)(2,1)S(1)} %convert_element_type.386), channel_id=1, source_target_pairs={{0,1},{1,2},{2,3},{3,0},{4,5},{5,6},{6,7},{7,4},{8,9},{9,10},{10,1... | collective-permute-start | bytes 2359304 | tf_op jit(solution)/shard_map/ppermute | solution.py:255
  20.0 4.2 collective-permute-start.9
  91.3 15.4 %collective-permute-start.10 = (bf16[1792,128]{1,0:T(8,128)(2,1)S(1)}, bf16[1792,128]{1,0:T(8,128)(2,1)S(1)}, u32[]{:S(2)}, u32[]{:S(2)}) collective-permute-start(bf16[1792,128]{1,0:T(8,128)(2,1)S(1)} %get-tuple-element.235), channel_id=1, source_target_pairs={{0,1},{1,2},{2,3},{3,0},{4,5},{5,6},{6,7},{7,4},{8,9},{9,10},{10,1... | collective-permute-start | bytes 1376264 | tf_op jit(solution)/shard_map/ppermute | solution.py:284
  92.2 32.2 %collective-permute-start.11 = (bf16[1792,128]{1,0:T(8,128)(2,1)S(1)}, bf16[1792,128]{1,0:T(8,128)(2,1)S(1)}, u32[]{:S(2)}, u32[]{:S(2)}) collective-permute-start(bf16[1792,128]{1,0:T(8,128)(2,1)S(1)} %get-tuple-element.234), channel_id=1, source_target_pairs={{0,2},{1,3},{2,0},{3,1},{4,6},{5,7},{6,4},{7,5},{8,10},{9,11},{10,... | collective-permute-start | bytes 1376264 | tf_op jit(solution)/shard_map/ppermute | solution.py:284
  94.3 30.1 %collective-permute-start.12 = (bf16[1792,128]{1,0:T(8,128)(2,1)S(1)}, bf16[1792,128]{1,0:T(8,128)(2,1)S(1)}, u32[]{:S(2)}, u32[]{:S(2)}) collective-permute-start(bf16[1792,128]{1,0:T(8,128)(2,1)S(1)} %get-tuple-element.233), channel_id=1, source_target_pairs={{0,3},{1,0},{2,1},{3,2},{4,7},{5,4},{6,5},{7,6},{8,11},{9,8},{10,9... | collective-permute-start | bytes 1376264 | tf_op jit(solution)/shard_map/ppermute | solution.py:284
  131.2 18.9 %all-to-all-start = ((bf16[8,512,128]{2,1,0:T(8,128)(2,1)}), bf16[8,512,128]{2,1,0:T(8,128)(2,1)S(1)}, u32[]{:S(2)}, u32[]{:S(2)}) async-start(bf16[8,512,128]{2,1,0:T(8,128)(2,1)} %bitcast.23), calls=%async_computation | async-start | bytes 2097152 | tf_op jit(solution)/shard_map/all_to_all | solution.py:765
  152.0 135.8 %all-gather.6.cloned.1.call-start = ((), (), s32[]{:S(2)}) async-start(), calls=%async_computation.3 | async-start | bytes 28311552 | tf_op jit(solution)/shard_map/all_gather | solution.py:755
  152.6 135.3 %copy-start.94 = (s32[1,512]{1,0:T(1,128)S(1)}, s32[1,512]{1,0:T(1,128)}, u32[]{:S(2)}) copy-start(s32[1,512]{1,0:T(1,128)} %param.21) | copy-start | bytes 6148
  152.6 240.8 %all-gather.8.cloned.1.call-start = ((), (), s32[]{:S(2)}) async-start(), calls=%async_computation.4 | async-start | bytes 17584128 | tf_op jit(solution)/shard_map/all_gather | solution.py:772
  152.6 136.0 %copy-start.75 = (s32[4,80]{1,0:T(4,128)S(1)}, s32[4,80]{1,0:T(4,128)}, u32[]{:S(2)}) copy-start(s32[4,80]{1,0:T(4,128)} %param.24) | copy-start | bytes 3844
  156.2 137.4 %copy-start.28 = (f32[528,1024]{1,0:T(8,128)S(1)}, f32[528,1024]{1,0:T(8,128)}, u32[]{:S(2)}) copy-start(f32[528,1024]{1,0:T(8,128)} %param.28) | copy-start | bytes 6488068
  287.9 482.9 %reduce-scatter.2.cloned.1.call-start = ((), (), s32[]{:S(2)}) async-start(), calls=%async_computation.5 | async-start | bytes 17584128 | tf_op jit(solution)/shard_map/reduce_scatter | solution.py:818
  287.9 17.4 %collective-permute-start.3 = (s32[1,592]{1,0:T(1,128)S(1)}, s32[1,592]{1,0:T(1,128)S(1)}, u32[]{:S(2)}, u32[]{:S(2)}) collective-permute-start(s32[1,592]{1,0:T(1,128)S(1)} %pad_add_fusion.3), channel_id=1, source_target_pairs={{0,0},{1,4},{2,1},{3,5},{4,2},{5,6},{6,3},{7,7},{8,8},{9,12},{10,9... | collective-permute-start | bytes 7112 | tf_op jit(solution)/shard_map/ppermute | solution.py:364
  289.2 6.3 collective-permute-start.19
  296.8 3.6 collective-permute-start.20
  301.1 3.6 collective-permute-start.21
  374.3 5.9 collective-permute-start.13
  375.5 14.5 %collective-permute-start.14 = (bf16[80,1024]{1,0:T(8,128)(2,1)S(1)}, bf16[80,1024]{1,0:T(8,128)(2,1)S(1)}, u32[]{:S(2)}, u32[]{:S(2)}) collective-permute-start(bf16[80,1024]{1,0:T(8,128)(2,1)S(1)} %get-tuple-element.196), channel_id=1, source_target_pairs={{0,2},{1,3},{2,0},{3,1},{4,6},{5,7},{6,4},{7,5},{8,10},{9,11},{10,... | collective-permute-start | bytes 491528 | tf_op jit(solution)/shard_map/ppermute | solution.py:255
  377.2 13.5 %collective-permute-start.15 = (bf16[80,1024]{1,0:T(8,128)(2,1)S(1)}, bf16[80,1024]{1,0:T(8,128)(2,1)S(1)}, u32[]{:S(2)}, u32[]{:S(2)}) collective-permute-start(bf16[80,1024]{1,0:T(8,128)(2,1)S(1)} %get-tuple-element.196), channel_id=1, source_target_pairs={{0,1},{1,2},{2,3},{3,0},{4,5},{5,6},{6,7},{7,4},{8,9},{9,10},{10,1... | collective-permute-start | bytes 491528 | tf_op jit(solution)/shard_map/ppermute | solution.py:255
  411.3 3.7 collective-permute-start.16
  411.4 4.6 collective-permute-start.17
  412.8 5.4 collective-permute-start.18
  431.4 21.8 %collective-permute-start.22 = (bf16[80,1024]{1,0:T(8,128)(2,1)}, bf16[80,1024]{1,0:T(8,128)(2,1)}, u32[]{:S(2)}, u32[]{:S(2)}) collective-permute-start(bf16[80,1024]{1,0:T(8,128)(2,1)} %get-tuple-element.239), channel_id=1, source_target_pairs={{0,1},{1,2},{2,3},{3,0},{4,5},{5,6},{6,7},{7,4},{8,9},{9,10},{10,1... | collective-permute-start | bytes 491528 | tf_op jit(solution)/shard_map/ppermute | solution.py:272
  431.7 21.4 %collective-permute-start.23 = (bf16[80,1024]{1,0:T(8,128)(2,1)}, bf16[80,1024]{1,0:T(8,128)(2,1)}, u32[]{:S(2)}, u32[]{:S(2)}) collective-permute-start(bf16[80,1024]{1,0:T(8,128)(2,1)} %get-tuple-element.241), channel_id=1, source_target_pairs={{0,2},{1,3},{2,0},{3,1},{4,6},{5,7},{6,4},{7,5},{8,10},{9,11},{10,... | collective-permute-start | bytes 491528 | tf_op jit(solution)/shard_map/ppermute | solution.py:272
  433.3 19.9 %collective-permute-start.24 = (bf16[80,1024]{1,0:T(8,128)(2,1)}, bf16[80,1024]{1,0:T(8,128)(2,1)}, u32[]{:S(2)}, u32[]{:S(2)}) collective-permute-start(bf16[80,1024]{1,0:T(8,128)(2,1)} %get-tuple-element.240), channel_id=1, source_target_pairs={{0,3},{1,0},{2,1},{3,2},{4,7},{5,4},{6,5},{7,6},{8,11},{9,8},{10,9... | collective-permute-start | bytes 491528 | tf_op jit(solution)/shard_map/ppermute | solution.py:272
  468.7 19.2 %collective-permute-start.26 = (bf16[256,4096]{1,0:T(8,128)(2,1)S(1)}, bf16[256,4096]{1,0:T(8,128)(2,1)S(1)}, u32[]{:S(2)}, u32[]{:S(2)}) collective-permute-start(bf16[256,4096]{1,0:T(8,128)(2,1)S(1)} %convolution_convert_fusion.2), channel_id=1, source_target_pairs={{0,4},{4,0},{8,12},{12,8},{16,20},{20,16},{24,28},{28,24},{1,5},{5... | collective-permute-start | bytes 6291464 | tf_op jit(solution)/shard_map/ppermute | solution.py:298
  470.9 17.0 %collective-permute-start.25 = (bf16[256,4096]{1,0:T(8,128)(2,1)S(1)}, bf16[256,4096]{1,0:T(8,128)(2,1)}, u32[]{:S(2)}, u32[]{:S(2)}) collective-permute-start(bf16[256,4096]{1,0:T(8,128)(2,1)S(1)} %convolution_convert_fusion.3), channel_id=1, source_target_pairs={{0,4},{4,0},{8,12},{12,8},{16,20},{20,16},{24,28},{28,24},{1,5},{5... | collective-permute-start | bytes 6291464 | tf_op jit(solution)/shard_map/ppermute | solution.py:297
  491.2 27.0 %collective-permute-start.28 = (bf16[256,4096]{1,0:T(8,128)(2,1)}, bf16[256,4096]{1,0:T(8,128)(2,1)}, u32[]{:S(2)}, u32[]{:S(2)}) collective-permute-start(bf16[256,4096]{1,0:T(8,128)(2,1)} %convolution_convert_fusion), channel_id=1, source_target_pairs={{0,4},{4,0},{8,12},{12,8},{16,20},{20,16},{24,28},{28,24},{1,5},{5... | collective-permute-start | bytes 6291464 | tf_op jit(solution)/shard_map/ppermute | solution.py:298
  494.5 23.7 %collective-permute-start.27 = (bf16[256,4096]{1,0:T(8,128)(2,1)}, bf16[256,4096]{1,0:T(8,128)(2,1)}, u32[]{:S(2)}, u32[]{:S(2)}) collective-permute-start(bf16[256,4096]{1,0:T(8,128)(2,1)} %convolution_convert_fusion.1), channel_id=1, source_target_pairs={{0,4},{4,0},{8,12},{12,8},{16,20},{20,16},{24,28},{28,24},{1,5},{5... | collective-permute-start | bytes 6291464 | tf_op jit(solution)/shard_map/ppermute | solution.py:297
  509.1 48.8 %collective-permute-start.29 = (bf16[256,4096]{1,0:T(8,128)(2,1)}, bf16[256,4096]{1,0:T(8,128)(2,1)}, u32[]{:S(2)}, u32[]{:S(2)}) collective-permute-start(bf16[256,4096]{1,0:T(8,128)(2,1)} %add_convert_fusion.3), channel_id=1, source_target_pairs={{0,1},{1,0},{2,3},{3,2},{4,5},{5,4},{6,7},{7,6},{8,9},{9,8},{10,11... | collective-permute-start | bytes 6291464 | tf_op jit(solution)/shard_map/ppermute | solution.py:321
  521.3 81.0 %collective-permute-start.32 = (bf16[256,4096]{1,0:T(8,128)(2,1)S(1)}, bf16[256,4096]{1,0:T(8,128)(2,1)S(1)}, u32[]{:S(2)}, u32[]{:S(2)}) collective-permute-start(bf16[256,4096]{1,0:T(8,128)(2,1)S(1)} %fusion.24), channel_id=1, source_target_pairs={{0,1},{1,0},{2,3},{3,2},{4,5},{5,4},{6,7},{7,6},{8,9},{9,8},{10,11... | collective-permute-start | bytes 6291464 | tf_op jit(solution)/shard_map/ppermute | solution.py:321
  559.1 10.6 %collective-permute-start.31 = (bf16[256,4096]{1,0:T(8,128)(2,1)S(1)}, bf16[256,4096]{1,0:T(8,128)(2,1)S(1)}, u32[]{:S(2)}, u32[]{:S(2)}) collective-permute-start(bf16[256,4096]{1,0:T(8,128)(2,1)S(1)} %pad_maximum_fusion.2), channel_id=1, source_target_pairs={{0,4},{4,0},{8,12},{12,8},{16,20},{20,16},{24,28},{28,24},{1,5},{5... | collective-permute-start | bytes 6291464 | tf_op jit(solution)/shard_map/ppermute | solution.py:298
  560.5 9.3 collective-permute-start.30
  613.0 3.7 collective-permute-start.34
  618.2 9.0 collective-permute-start.35
  623.8 88.5 %collective-permute-start.42 = (bf16[256,4096]{1,0:T(8,128)(2,1)}, bf16[256,4096]{1,0:T(8,128)(2,1)}, u32[]{:S(2)}, u32[]{:S(2)}) collective-permute-start(bf16[256,4096]{1,0:T(8,128)(2,1)} %add_convert_fusion.2), channel_id=1, source_target_pairs={{2,4},{3,5},{4,2},{5,3},{10,12},{11,13},{12,10},{13,11},{18,20},{1... | collective-permute-start | bytes 6291464 | tf_op jit(solution)/shard_map/ppermute | solution.py:343
  627.3 6.4 collective-permute-start.36
  633.8 6.9 collective-permute-start.37
  640.7 62.5 %collective-permute-start.38 = (bf16[528,128]{1,0:T(8,128)(2,1)S(1)}, bf16[528,128]{1,0:T(8,128)(2,1)S(1)}, u32[]{:S(2)}, u32[]{:S(2)}) collective-permute-start(bf16[528,128]{1,0:T(8,128)(2,1)S(1)} %add_convert_fusion.11), channel_id=1, source_target_pairs={{0,2},{1,3},{2,0},{3,1},{4,6},{5,7},{6,4},{7,5},{8,10},{9,11},{10,... | collective-permute-start | bytes 405512 | tf_op jit(solution)/shard_map/ppermute | solution.py:709
  657.5 73.2 %collective-permute-start.43 = (bf16[256,4096]{1,0:T(8,128)(2,1)}, bf16[256,4096]{1,0:T(8,128)(2,1)}, u32[]{:S(2)}, u32[]{:S(2)}) collective-permute-start(bf16[256,4096]{1,0:T(8,128)(2,1)} %fusion.23), channel_id=1, source_target_pairs={{2,4},{3,5},{4,2},{5,3},{10,12},{11,13},{12,10},{13,11},{18,20},{1... | collective-permute-start | bytes 6291464 | tf_op jit(solution)/shard_map/ppermute | solution.py:343
  703.3 7.1 collective-permute-start.39
  704.8 65.9 %collective-permute-start.33 = (bf16[256,4096]{1,0:T(8,128)(2,1)}, bf16[256,4096]{1,0:T(8,128)(2,1)}, u32[]{:S(2)}, u32[]{:S(2)}) collective-permute-start(bf16[256,4096]{1,0:T(8,128)(2,1)} %pad_maximum_fusion.3), channel_id=1, source_target_pairs={{0,1},{1,0},{2,3},{3,2},{4,5},{5,4},{6,7},{7,6},{8,9},{9,8},{10,11... | collective-permute-start | bytes 6291464 | tf_op jit(solution)/shard_map/ppermute | solution.py:321
  706.0 29.7 %all-to-all-start.1 = ((bf16[8,512,128]{2,1,0:T(8,128)(2,1)}), bf16[8,512,128]{2,1,0:T(8,128)(2,1)}, u32[]{:S(2)}, u32[]{:S(2)}) async-start(bf16[8,512,128]{2,1,0:T(8,128)(2,1)} %bitcast.235), calls=%async_computation.1 | async-start | bytes 2097152 | tf_op jit(solution)/shard_map/all_to_all | solution.py:838
  710.3 231.8 %all-gather.12.cloned.1.call-start = ((), (), s32[]{:S(2)}) async-start(), calls=%async_computation.7 | async-start | bytes 5242880 | tf_op jit(solution)/shard_map/all_gather | solution.py:846
  710.4 20.0 %collective-permute-start.40 = (bf16[528,256]{1,0:T(8,128)(2,1)S(1)}, bf16[528,256]{1,0:T(8,128)(2,1)S(1)}, u32[]{:S(2)}, u32[]{:S(2)}) collective-permute-start(bf16[528,256]{1,0:T(8,128)(2,1)S(1)} %pad_maximum_fusion.7), channel_id=1, source_target_pairs={{0,8},{4,12},{8,0},{12,4},{16,24},{20,28},{24,16},{28,20},{1,9},{5... | collective-permute-start | bytes 811016 | tf_op jit(solution)/shard_map/ppermute | solution.py:714
  730.6 3.2 collective-permute-start.41
  777.9 27.2 %collective-permute-start.44 = (bf16[256,4096]{1,0:T(8,128)(2,1)}, bf16[256,4096]{1,0:T(8,128)(2,1)}, u32[]{:S(2)}, u32[]{:S(2)}) collective-permute-start(bf16[256,4096]{1,0:T(8,128)(2,1)} %pad_maximum_fusion.4), channel_id=1, source_target_pairs={{2,4},{3,5},{4,2},{5,3},{10,12},{11,13},{12,10},{13,11},{18,20},{1... | collective-permute-start | bytes 6291464 | tf_op jit(solution)/shard_map/ppermute | solution.py:343
  839.1 30.0 %collective-permute-start.45 = (bf16[4,256,1536]{2,1,0:T(8,128)(2,1)}, bf16[4,256,1536]{2,1,0:T(8,128)(2,1)}, u32[]{:S(2)}, u32[]{:S(2)}) collective-permute-start(bf16[4,256,1536]{2,1,0:T(8,128)(2,1)} %get-tuple-element.210), channel_id=1, source_target_pairs={{0,4},{4,0},{8,12},{12,8},{16,20},{20,16},{24,28},{28,24},{1,5},{5... | collective-permute-start | bytes 9437192 | tf_op jit(solution)/shard_map/ppermute | solution.py:665
  863.5 159.8 %all-gather.10.cloned.1.call-start = ((), (), s32[]{:S(2)}) async-start(), calls=%async_computation.6 | async-start | bytes 7077888 | tf_op jit(solution)/shard_map/all_gather | solution.py:899
  872.7 12.2 %collective-permute-start.47 = (bf16[128,1536]{1,0:T(8,128)(2,1)}, bf16[128,1536]{1,0:T(8,128)(2,1)S(1)}, u32[]{:S(2)}, u32[]{:S(2)}) collective-permute-start(bf16[128,1536]{1,0:T(8,128)(2,1)} %get-tuple-element.212), channel_id=1, source_target_pairs={{0,8},{4,12},{8,0},{12,4},{16,24},{20,28},{24,16},{28,20},{1,9},{5... | collective-permute-start | bytes 1179656 | tf_op jit(solution)/shard_map/ppermute | solution.py:665
  873.5 19.8 %collective-permute-start.46 = (bf16[128,1536]{1,0:T(8,128)(2,1)}, bf16[128,1536]{1,0:T(8,128)(2,1)S(1)}, u32[]{:S(2)}, u32[]{:S(2)}) collective-permute-start(bf16[128,1536]{1,0:T(8,128)(2,1)} %get-tuple-element.211), channel_id=1, source_target_pairs={{0,8},{4,12},{8,0},{12,4},{16,24},{20,28},{24,16},{28,20},{1,9},{5... | collective-permute-start | bytes 1179656 | tf_op jit(solution)/shard_map/ppermute | solution.py:665
  875.0 12.1 %collective-permute-start.50 = (bf16[128,1536]{1,0:T(8,128)(2,1)S(1)}, bf16[128,1536]{1,0:T(8,128)(2,1)S(1)}, u32[]{:S(2)}, u32[]{:S(2)}) collective-permute-start(bf16[128,1536]{1,0:T(8,128)(2,1)S(1)} %get-tuple-element.218), channel_id=1, source_target_pairs={{0,16},{4,20},{8,24},{12,28},{16,0},{20,4},{24,8},{28,12},{1,17},{... | collective-permute-start | bytes 1179656 | tf_op jit(solution)/shard_map/ppermute | solution.py:665
  875.1 28.8 %collective-permute-start.49 = (bf16[128,1536]{1,0:T(8,128)(2,1)S(1)}, bf16[128,1536]{1,0:T(8,128)(2,1)S(1)}, u32[]{:S(2)}, u32[]{:S(2)}) collective-permute-start(bf16[128,1536]{1,0:T(8,128)(2,1)S(1)} %get-tuple-element.217), channel_id=1, source_target_pairs={{0,16},{4,20},{8,24},{12,28},{16,0},{20,4},{24,8},{28,12},{1,17},{... | collective-permute-start | bytes 1179656 | tf_op jit(solution)/shard_map/ppermute | solution.py:665
  886.0 16.7 %collective-permute-start.48 = (bf16[128,1536]{1,0:T(8,128)(2,1)S(1)}, bf16[128,1536]{1,0:T(8,128)(2,1)S(1)}, u32[]{:S(2)}, u32[]{:S(2)}) collective-permute-start(bf16[128,1536]{1,0:T(8,128)(2,1)S(1)} %fusion.59), channel_id=1, source_target_pairs={{0,16},{4,20},{8,24},{12,28},{16,0},{20,4},{24,8},{28,12},{1,17},{... | collective-permute-start | bytes 1179656 | tf_op jit(solution)/shard_map/ppermute | solution.py:665
  887.2 16.7 %collective-permute-start.51 = (bf16[128,1536]{1,0:T(8,128)(2,1)S(1)}, bf16[128,1536]{1,0:T(8,128)(2,1)S(1)}, u32[]{:S(2)}, u32[]{:S(2)}) collective-permute-start(bf16[128,1536]{1,0:T(8,128)(2,1)S(1)} %fusion.57), channel_id=1, source_target_pairs={{0,8},{4,12},{8,0},{12,4},{16,24},{20,28},{24,16},{28,20},{1,9},{5... | collective-permute-start | bytes 1179656 | tf_op jit(solution)/shard_map/ppermute | solution.py:665
  987.1 1.1 collective-permute-start.52
  988.3 3.5 collective-permute-start.53
  991.8 3.5 collective-permute-start.54
  995.4 3.5 collective-permute-start.55
  998.9 4.4 collective-permute-start.56
  (98 other events, 1107.8 us)
Sparse Core Ops, SparseCore 0:
  152.1 11.6 sort.11.cloned.1.call-done
  863.6 78.4 all-gather.11
  (1 shorter events, 0.0 us)
Sparse Core Ops, SparseCore 1:
  154.9 132.8 all-gather.5
  290.1 87.8 all-gather.7
  462.7 111.3 reduce-scatter.1
  942.2 43.9 all-gather.9

commit v6 on v5

--- a/solution.py
+++ b/solution.py
@@ -198,9 +198,9 @@
     _, pull = jax.vjp(norm_rows, embedded, small[base], small[base + 1])
     dembed, dgain_emb, dshift_emb = pull(dxzero)
     dembed = mixed.received(dembed)
-    dembed, mixed.far = up.crossed(dembed, mixed.far) if up.paired else (dembed, None)
+    mixed.across()
+    (dembed,) = up.crossed(dembed)
     up.finish()
-    mixed.across()
     bias_qkv = jnp.sum(dqkv, axis=0, dtype=jnp.float32)
     vectors = jnp.stack(
         [
@@ -281,8 +281,9 @@
     def block(by):
         return lax.dynamic_index_in_dim(blocks, lax.rem(place + by, size), 0, keepdims=False)
 
-    moved = [lax.ppermute(block(by), "narrow", cycle(size, by)) for by in range(1, size)]
-    return jnp.stack([block(0)] + moved)
+    return [block(0)] + [
+        lax.ppermute(block(by), "narrow", cycle(size, by)) for by in range(1, size)
+    ]
 
 
 class WorkerPiece:
@@ -399,18 +400,25 @@
         self.count, self.vshard = count, vshard
         own = lax.dynamic_index_in_dim(owner, place, 0, keepdims=False)
         self.rank = lax.dynamic_index_in_dim(rank, place, 0, keepdims=False)
+        self.owner = own
         self.behind = lax.rem(place - own + size, size)
         self.slots = jnp.where(owner == place, tokens - place * vshard, vshard)
 
     def behind_slots(self, room):
         return self.behind * room + jnp.minimum(self.rank, room - 1)
 
+    def owner_slots(self):
+        return self.owner * self.count + self.rank
+
     def packed(self, slots):
+        size = lax.axis_size("narrow")
         base = self.vshard + 1
         order = jnp.arange(self.count) * base + slots
         order = jnp.where(slots < self.vshard, order, order + self.count * base)
-        order = lax.sort(order)
-        return order % base, order // base % self.count
+        backward = (lax.sort(order) % base)[::-1]
+        backward = jnp.concatenate([backward, backward], axis=0)
+        start = size - 1 - lax.axis_index("narrow")
+        return lax.dynamic_slice_in_dim(backward, start, size, 0)
 
 
 def pack_kernel(ids_ref, table_ref, out_ref, held, *rows):
@@ -491,19 +499,54 @@
     )(ids, table)
 
 
-def add_kernel(length, ids_ref, from_ref, rows_ref, out_ref, rows, *sums):
-    size, each = out_ref.shape[0], rows_ref.shape[1]
-    for part in sums:
+def put_kernel(ids_ref, rows_ref, out_ref, rows, held):
+    rows[...] = rows_ref[...].astype(jnp.float32)
+    held[...] = jnp.zeros_like(held)
+
+    @pl.loop(0, rows_ref.shape[0], step=16)
+    def _(first):
+        for by in range(16):
+            held[pl.ds(ids_ref[first + by], 1), :] = rows[pl.ds(first + by, 1), :]
+
+    out_ref[...] = held[...].astype(out_ref.dtype)
+
+
+def put_rows(ids, values, size):
+    cols = values.shape[1]
+    return pl.pallas_call(
+        put_kernel,
+        grid_spec=pltpu.PrefetchScalarGridSpec(
+            num_scalar_prefetch=1,
+            grid=(1,),
+            in_specs=[pl.BlockSpec(values.shape, lambda step, ids: (0, 0))],
+            out_specs=pl.BlockSpec((size, cols), lambda step, ids: (0, 0)),
+            scratch_shapes=[
+                pltpu.VMEM(values.shape, jnp.float32),
+                pltpu.VMEM((size, cols), jnp.float32),
+            ],
+        ),
+        out_shape=jax.ShapeDtypeStruct((size, cols), values.dtype),
+        compiler_params=pltpu.CompilerParams(vmem_limit_bytes=40 * 2**20),
+        cost_estimate=FREE,
+        name="put_rows",
+    )(ids, values)
+
+
+def add_kernel(ids_ref, *refs):
+    count = (len(refs) - 1) // 3
+    rows_refs, out_ref, rows, sums = refs[:count], refs[count], refs[count + 1 : 2 * count + 1], refs[2 * count + 1 :]
+    size, length = out_ref.shape[0], rows_refs[0].shape[0]
+    each = ids_ref.shape[0] // count
+    for part, held, rows_ref in zip(sums, rows, rows_refs):
         part[...] = jnp.zeros_like(part)
-    rows[...] = rows_ref[...].astype(jnp.float32)
+        held[...] = rows_ref[...].astype(jnp.float32)
 
     @pl.loop(0, length, step=8)
     def _(first):
         for by in range(8):
             for index, part in enumerate(sums):
                 place = ids_ref[index * each + first + by]
-                row = from_ref[index * each + first + by]
-                part[pl.ds(place, 1), :] += rows[index, pl.ds(row, 1), :]
+                part[pl.ds(place, 1), :] += rows[index][pl.ds(first + by, 1), :]
 
     total = sums[0][0:size, :]
     for part in sums[1:]:
@@ -511,23 +554,24 @@
     out_ref[...] = total
 
 
-def added_rows(ids, rows, values, size, length):
-    places, count, cols = values.shape
+def added_rows(ids, values, size):
+    length, cols = values[0].shape
+    block = pl.BlockSpec((length, cols), lambda step, ids: (0, 0))
     return pl.pallas_call(
-        functools.partial(add_kernel, length),
+        add_kernel,
         grid_spec=pltpu.PrefetchScalarGridSpec(
-            num_scalar_prefetch=2,
+            num_scalar_prefetch=1,
             grid=(1,),
-            in_specs=[pl.BlockSpec(values.shape, lambda step, ids, rows: (0, 0, 0))],
-            out_specs=pl.BlockSpec((size, cols), lambda step, ids, rows: (0, 0)),
-            scratch_shapes=[pltpu.VMEM(values.shape, jnp.float32)]
-            + [pltpu.VMEM((size + 8, cols), jnp.float32)] * places,
+            in_specs=[block] * len(values),
+            out_specs=pl.BlockSpec((size, cols), lambda step, ids: (0, 0)),
+            scratch_shapes=[pltpu.VMEM((length, cols), jnp.float32)] * len(values)
+            + [pltpu.VMEM((size + 8, cols), jnp.float32)] * len(values),
         ),
         out_shape=jax.ShapeDtypeStruct((size, cols), jnp.float32),
         compiler_params=pltpu.CompilerParams(vmem_limit_bytes=56 * 2**20),
-        cost_estimate=pl.CostEstimate(flops=0, bytes_accessed=5 * 10**7, transcendentals=0),
+        cost_estimate=FREE,
         name="add_rows",
-    )(ids.reshape(-1), rows.reshape(-1), values)
+    )(ids.reshape(-1), *values)
 
 
 def span_kernel(momentum_ref, grad_ref, error_ref, span_ref, sum_ref):
@@ -701,14 +745,14 @@
     return value
 
 
-def small_total(value):
+def small_total(parts):
     n_wide, n_narrow = lax.axis_size("wide"), lax.axis_size("narrow")
-    bit = 1
-    while bit < n_narrow:
-        low = value.astype(jnp.bfloat16)
-        other = lax.ppermute(low, "narrow", swap_pairs(n_narrow, bit))
-        value = low.astype(jnp.float32) + other.astype(jnp.float32)
-        bit *= 2
+    parts = jnp.stack(parts + parts[:-1])
+    start = lax.rem(lax.axis_index("narrow") + 1, n_narrow)
+    parts = lax.dynamic_slice_in_dim(parts, start, n_narrow, 0).astype(jnp.float32)
+    value = parts[0]
+    for place in range(1, n_narrow):
+        value = value + parts[place]
     value = value.astype(jnp.bfloat16)
     for bit, place in reversed(list(zip((1, 2, 4), wide_places()))):
         other = lax.ppermute(value, "wide", swap_pairs(n_wide, bit))
@@ -757,18 +801,14 @@
 
         def looked_up(room):
             rows = sent_around(picked[:, 0:room])
-            return taken_rows(owners.behind_slots(room), rows.reshape(n_narrow * room, -1))
+            return taken_rows(owners.behind_slots(room), jnp.concatenate(rows, axis=0))
 
         layer_rows, picked = together(layer_rows, picked)
         looked = looked_up(owners.room)
         looked = lax.cond(owners.full, lambda: looked_up(owners.count), lambda: looked)
         looked = lax.all_to_all(looked.reshape(n_wide, L, -1), "wide", 0, 0)
         looked = looked.transpose(1, 0, 2).reshape(1, L, D)
-        looked, slots = together(looked, owners.slots)
-        packed_ids, packed_rows_at = owners.packed(slots)
-        table_low, weights, looked, packed_ids, packed_rows_at = together(
-            table_low, weights, looked, packed_ids, packed_rows_at
-        )
+        table_low, weights, looked = together(table_low, weights, looked)
         table_cols = lax.all_gather(table_low, "wide", axis=1, tiled=True)
     else:
         local_ids = token_ids - narrow_me * vshard
@@ -785,6 +825,8 @@
     hmask = jnp.take_along_axis(htwo.reshape(seqs, L, D), mlm_pos[..., None], axis=1)
     hmask = hmask.reshape(seqs * MPS, D).astype(jnp.bfloat16)
     if paired:
+        slots, hmask = together(owners.slots, hmask)
+        packed_ids = owners.packed(slots)
         group_h = gathered_near(hmask)
     else:
         group_h = lax.all_gather(hmask, "narrow", axis=0, tiled=True)
@@ -836,14 +878,28 @@
     if paired:
         cut = dembed.astype(jnp.bfloat16).reshape(L, n_wide, D // n_wide).transpose(1, 0, 2)
         cut = lax.all_to_all(cut, "wide", 0, 0).reshape(n_wide * L, D // n_wide)
-        small_grad = small_total(small_halved(small_grad))
+        halved = small_halved(small_grad).astype(jnp.bfloat16)
+        placed = put_rows(owners.owner_slots(), cut, n_narrow * owners.count)
+        placed = placed.reshape(n_narrow, owners.count, -1)
+        near = placed[:, 0 : owners.room]
+        wider = jnp.broadcast_to(halved[None], (n_narrow,) + halved.shape)
+        near = sent_around(jnp.concatenate([near, wider], axis=1))
         down, up = pieces[2], pieces[1]
-        cut, mixed.away, small_grad, down.result, up.result, table_head = together(
-            cut, mixed.away, small_grad, down.result, up.result, table_head
+        *near, mixed.away, down.result, up.result, table_head = together(
+            *near, mixed.away, down.result, up.result, table_head
         )
         mixed.finish()
-        cut, mixed.result = together(cut, mixed.result)
-        group_rows = lax.all_gather(cut, "narrow", axis=0)
+        table_grad = added_rows(packed_ids, [part[0 : owners.room] for part in near], vshard)
+        table_grad = lax.cond(
+            owners.full,
+            lambda: added_rows(packed_ids, sent_around(placed), vshard),
+            lambda: table_grad,
+        )
+        table_mom, table_upd, table_norms = table_update(
+            table_grad, table_head, table, table_m, table_v
+        )
+        small_grad = small_total([part[owners.room :] for part in near])
+        mixed.result, table_norms, small_grad = together(mixed.result, table_norms, small_grad)
     else:
         mixed.finish()
         group_rows = lax.all_gather(dembed_rows.astype(jnp.bfloat16), "narrow", axis=0, tiled=True)
@@ -876,19 +932,7 @@
     server_out = sscale * jnp.tanh(server_in / sscale)
     new_server = server_in - server_out
     server_low = server_out.astype(jnp.bfloat16)
-    if paired:
-        server_low, group_rows = together(server_low, group_rows)
-
-        def added(length):
-            return added_rows(packed_ids, packed_rows_at, group_rows, vshard, length)
-
-        table_grad = lax.cond(
-            owners.full, lambda: added(owners.count), lambda: added(owners.room)
-        )
-        table_mom, table_upd, table_norms = table_update(
-            table_grad, table_head, table, table_m, table_v
-        )
-    else:
+    if not paired:
         small_grad = lax.psum(small_grad, ("wide", "narrow"))
         table_mom = BETA * table_m + (1.0 - BETA) * table_grad
         table_upd = table_mom / (jnp.sqrt(table_v) + OPT_EPS) + DECAY * table

time: 1050 us -> 950 us (0.905)
  waiting for transfers between devices: 411 us -> 321 us
  starting transfers between devices: 106 us -> 78 us
    all_gather x1, waiting for transfers between devices: 122 us -> 50.6 us  [shards(): weights = lax.all_gather(layer_rows, 'wide', axis=1, tiled=True)]
    ppermute x3 -> x6, waiting for transfers between devices: 27.2 us -> 92.2 us  [sent_around(): lax.ppermute(block(by), 'narrow', cycle(size, by))]
    ppermute x2 -> x0, waiting for transfers between devices: 48.2 us -> none  [small_total(): other = lax.ppermute(low, 'narrow', swap_pairs(n_narrow, bit))]
    all_gather x1 -> x0, waiting for transfers between devices: 30.1 us -> none  [shards(): group_rows = lax.all_gather(cut, 'narrow', axis=0)]
    ppermute x7, starting transfers between devices: 29.4 us -> 8.71 us  [send(): lax.ppermute(value.astype(jnp.bfloat16), 'wide', swap_pairs(n_wide, bit))]
    ppermute x2 -> x0, starting transfers between devices: 15.7 us -> none  [small_total(): other = lax.ppermute(low, 'narrow', swap_pairs(n_narrow, bit))]
    ppermute x3, waiting for transfers between devices: 86.4 us -> 70.9 us  [across(): self.away = lax.ppermute(away, 'narrow', sides)]
    unnamed x223 -> x221, local copies, waits for them, and re-layouts: 43 us -> 52.8 us
  transfers between devices with their start and end apart: 61 -> 61, of which waited for: 33 -> 31; matrix products, arithmetic and copies ran while one was open for 23% -> 26% of each run, Pallas kernels for 11% -> 14%
where the time goes in v6:
time: 950 us; the launch traced here: 942 us
  waiting for transfers between devices  321 us (34%)
  matrix products  156 us (16%)
  Pallas kernels  149 us (16%)
  other arithmetic  114 us (12%)
  local copies, waits for them, and re-layouts  90.6 us (10%)
  starting transfers between devices  78 us (8%)
  between operations  23 us (2%)
  loops' own time  9.7 us (1%)
    ppermute x6, waiting for transfers between devices, sent_around(): lax.ppermute(block(by), 'narrow', cycle(size, by))  92.2 us
    ppermute x3, waiting for transfers between devices, across(): self.away = lax.ppermute(away, 'narrow', sides)  70.9 us
    dot_general x5, matrix products, matmul(): return jnp.dot(left, right, preferred_element_type=jnp.float32)  62.5 us
    unnamed x221, local copies, waits for them, and re-layouts  52.8 us
    pallas_call x1, Pallas kernels, packed_rows(): pl.pallas_call(pack_kernel, grid_spec=pltpu.PrefetchScalarGridSpec(num_sc...  52.4 us
    all_gather x1, waiting for transfers between devices, shards(): weights = lax.all_gather(layer_rows, 'wide', axis=1, tiled=True)  50.6 us
    dot_general x5, matrix products, matmul_nt(): lax.dot_general(left, right, (((1,), (1,)), ((), ())), preferred_element_...  39.6 us
    dot_general x16, matrix products, matmul_tn(): lax.dot_general(left, right, (((0,), (0,)), ((), ())), preferred_element_...  35.9 us
  transfers between devices with their start and end apart: 61, of which 31 were waited for; matrix products, arithmetic and copies ran while one was open for 26% of the time, Pallas kernels for 14%

profile of v6, /device:TPU:0, one launch (start us, length us, event | category | flops | bytes accessed | tf_op | source)
XLA Modules:
  0.0 941.8 jit_solution(14356231353134699949)
XLA Ops:
  18.5 3.7 collective-permute-start.10
  25.7 52.4 %pack_rows.1 = bf16[4,4096,128]{2,1,0:T(8,128)(2,1)} custom-call(s32[16384]{0:T(1024)S(1)} %fusion.105.ids_ref, f32[7632,128]{1,0:T(8,128)S(1)} %copy-done.5), custom_call_target="tpu_custom_call" | custom-call | bytes 150000000 | tf_op jit(solution)/shard_map/pack_rows/pallas_call | solution.py:453
  78.1 10.2 %collective-permute-done.11 = bf16[256,1536]{1,0:T(8,128)(2,1)S(1)} collective-permute-done((bf16[256,1536]{1,0:T(8,128)(2,1)S(1)}, bf16[256,1536]{1,0:T(8,128)(2,1)S(1)}, u32[]{:S(2)}, u32[]{:S(2)}) %collective-permute-start.11) | collective-permute-done | bytes 786464 | tf_op jit(solution)/shard_map/ppermute | solution.py:255
  99.9 9.6 %collective-permute-done.13 = bf16[1792,128]{1,0:T(8,128)(2,1)S(1)} collective-permute-done((bf16[1792,128]{1,0:T(8,128)(2,1)S(1)}, bf16[1792,128]{1,0:T(8,128)(2,1)S(1)}, u32[]{:S(2)}, u32[]{:S(2)}) %collective-permute-start.13) | collective-permute-done | bytes 458784 | tf_op jit(solution)/shard_map/ppermute | solution.py:285
  109.5 16.5 %collective-permute-done.14 = bf16[1792,128]{1,0:T(8,128)(2,1)S(1)} collective-permute-done((bf16[1792,128]{1,0:T(8,128)(2,1)S(1)}, bf16[1792,128]{1,0:T(8,128)(2,1)S(1)}, u32[]{:S(2)}, u32[]{:S(2)}) %collective-permute-start.14) | collective-permute-done | bytes 458784 | tf_op jit(solution)/shard_map/ppermute | solution.py:285
  126.1 6.6 take_rows.3
  132.7 9.7 %conditional.2 = (bf16[4096,128]{1,0:T(8,128)(2,1)}) conditional(s32[]{:T(128)} %convert_element_type.383, bf16[4096,128]{1,0:T(8,128)(2,1)} %take_rows.3, (s32[4096]{0:T(1024)S(1)}, s32[4096]{0:T(1024)S(1)}, bf16[4,4096,128]{2,1,0:T(8,128)(2,1)}) %tuple.157), branch_computations={%region_7.8_spmd, %region_8.9_spmd} | conditional | flops 16789544 | bytes 29409868 | solution.py:808
  142.4 3.6 all-to-all-start
  146.1 3.8 convert_element_type.381
  149.9 23.0 %all-to-all-done = bf16[8,512,128]{2,1,0:T(8,128)(2,1)S(1)} async-done(((bf16[8,512,128]{2,1,0:T(8,128)(2,1)}), bf16[8,512,128]{2,1,0:T(8,128)(2,1)S(1)}, u32[]{:S(2)}, u32[]{:S(2)}) %all-to-all-start) | async-done | bytes 1048608 | tf_op jit(solution)/shard_map/all_to_all | solution.py:809
  176.2 50.6 %all-gather.4.cloned.1.call-done = bf16[1024,12288]{1,0:T(8,128)(2,1)} async-done(((bf16[1024,1536]{1,0:T(8,128)(2,1)}), bf16[1024,12288]{1,0:T(8,128)(2,1)}) %all-gather.4.cloned.1.call-update) | async-done | bytes 25165840 | tf_op jit(solution)/shard_map/all_gather | solution.py:799
  228.2 3.8 collective-permute-start.22
  248.5 6.8 add_convert_fusion.1.q_ref.k_ref.v_ref
  255.3 11.7 %attend.1 = (bf16[512,1024]{1,0:T(8,128)(2,1)S(1)}, f32[8,2,512]{2,1,0:T(2,128)S(1)}) custom-call(bf16[512,3072]{1,0:T(8,128)(2,1)S(1)} %add_convert_fusion.1.q_ref.k_ref.v_ref, bf16[512,3072]{1,0:T(8,128)(2,1)S(1)} %add_convert_fusion.1.q_ref.k_ref.v_ref, bf16[512,3072]{1,0:T(8,128)(2,1)S(1)} %add_convert_fusion.1.q_ref.k_ref.v_ref, ...), custom_call_target="tpu_custom_call" | custom-call | tf_op jit(solution)/shard_map/attend/pallas_call | solution.py:86
  267.1 4.0 fusion.176
  271.9 26.1 %multiply_convert_fusion = (bf16[512,4096]{1,0:T(8,128)(2,1)S(1)}, f32[512,4096]{1,0:T(8,128)}, f32[512,4096]{1,0:T(8,128)}) fusion(f32[4096]{0:T(1024)S(1)} %bitcast.296, bf16[512,1024]{1,0:T(8,128)(2,1)S(1)} %fusion.39, bf16[1024,12288]{1,0:T(8,128)(2,1)} %all-gather.4.cloned.1.call-done), kind=kOutput, calls=%fused_computation.25 | convolution fusion | flops 4433379328 | bytes 30425088 | tf_op jit(solution)/shard_map/dot_general | solution.py:49
  298.1 9.2 fusion.177
  313.2 3.7 collective-permute-done.16
  317.6 6.4 collective-permute-done.17
  327.4 11.3 %fusion.178 = (f32[320]{0:T(512)S(1)}, f32[320,7632]{1,0:T(8,128)}) fusion(bf16[7632,1024]{1,0:T(8,128)(2,1)} %all-gather.6.cloned.1.call-done, bf16[560,1024]{1,0:T(8,128)(2,1)} %constant_dynamic-update-slice_fusion.7, s32[]{:T(128)S(6)} %select_n.426, pred[7632]{0:T(1024)(128)(4,1)S(1)} %copy-done.85), kind=kOutput, calls=%fused_computation.441 | convolution fusion | flops 5006591488 | bytes 26063572 | tf_op jit(solution)/shard_map/dot_general | solution.py:59
  338.7 6.4 exponential_reduce_fusion
  352.6 11.7 %fusion.157 = f32[320,1024]{1,0:T(8,128)S(1)} fusion(bf16[7632,1024]{1,0:T(8,128)(2,1)} %all-gather.6.cloned.1.call-done, f32[320,7632]{1,0:T(8,128)S(1)} %copy-done.38, f32[320]{0:T(512)S(1)} %get-tuple-element.262, f32[320]{0:T(512)S(1)} %get-tuple-element.167, s32[7632]{0:T(1024)S(1)} %copy-done.66, s32[320]{0:T(512)} %copy-done.86), kind=kOutput, calls=%fused_computation.425 | convolution fusion | flops 5016360960 | bytes 26744384 | tf_op jit(solution)/shard_map/dot_general | solution.py:49
  369.2 17.7 %convert_bitcast_fusion = bf16[8,7632,128]{2,1,0:T(8,128)(2,1)} fusion(f32[320,7632]{1,0:T(8,128)} %get-tuple-element.278, f32[320]{0:T(512)} %copy-done.94, f32[320]{0:T(512)S(1)} %get-tuple-element.167, s32[7632]{0:T(1024)S(1)} %copy-done.66, s32[320]{0:T(512)S(1)} %copy-done.87, bf16[560,1024]{1,0:T(8,128)(2,1)} %constant_dynamic-update-slice_fusion.7, ...), kind=kOutput, calls=%fused_computation.12 | convolution fusion | flops 5024176128 | bytes 26151236 | tf_op jit(solution)/shard_map/sv,swc->wvc/dot_general | solution.py:858
  390.4 3.5 scatter_custom_fusion
  406.9 3.4 fusion.81
  410.3 13.8 %add_convert_fusion = bf16[512,4096]{1,0:T(8,128)(2,1)S(1)} fusion(f32[512,4096]{1,0:T(8,128)} %get-tuple-element.183, f32[512,4096]{1,0:T(8,128)} %get-tuple-element.274, f32[4096]{0:T(1024)S(1)} %bitcast.297, bf16[512,1024]{1,0:T(8,128)(2,1)S(1)} %get-tuple-element.173, bf16[1024,12288]{1,0:T(8,128)(2,1)} %all-gather.4.cloned.1.call-done), kind=kOutput, calls=%fused_computation.24 | convolution fusion | flops 4326424576 | bytes 30425088 | tf_op jit(solution)/shard_map/dot_general | solution.py:49
  430.8 9.8 %multiply_reduce_fusion.3 = (f32[1024]{0:T(1024)S(1)}, f32[512]{0:T(512)S(1)}, f32[1024]{0:T(1024)S(1)}, f32[512,1024]{1,0:T(8,128)}) fusion(f32[512,1024]{1,0:T(8,128)S(1)} %copy-done.31, f32[512]{0:T(512)S(1)} %fusion.139, f32[512]{0:T(512)S(1)} %broadcast_multiply_fusion.2, f32[1024]{0:T(1024)S(1)} %bitcast.286, ...), kind=kOutput, calls=%fused_computation.101 | convolution fusion | flops 4300207616 | bytes 18894848 | tf_op jit(solution)/shard_map/dot_general | solution.py:59
  441.1 3.9 add_convert_fusion.3
  455.8 16.8 %attend_back.1 = bf16[512,3072]{1,0:T(8,128)(2,1)S(1)} custom-call(bf16[512,3072]{1,0:T(8,128)(2,1)S(1)} %copy-done.4, bf16[512,3072]{1,0:T(8,128)(2,1)S(1)} %copy-done.4, bf16[512,3072]{1,0:T(8,128)(2,1)S(1)} %copy-done.4, bf16[512,1024]{1,0:T(8,128)(2,1)S(1)} %fusion.47.do_ref, f32[8,2,512]{2,1,0:T(2,128)S(1)} %get-tuple-element.99.lse_ref, ...), custom_call_target="tpu_custom_call" | custom-call | tf_op jit(solution)/shard_map/attend_back/pallas_call | solution.py:130
  472.6 20.1 %collective-permute-done.32 = bf16[256,4096]{1,0:T(8,128)(2,1)} collective-permute-done((bf16[256,4096]{1,0:T(8,128)(2,1)}, bf16[256,4096]{1,0:T(8,128)(2,1)}, u32[]{:S(2)}, u32[]{:S(2)}) %collective-permute-start.32) | collective-permute-done | bytes 2097184 | tf_op jit(solution)/shard_map/ppermute | solution.py:322
  503.4 3.9 add_convert_fusion.2
  507.3 6.2 multiply_reduce_fusion.4
  517.2 50.8 %collective-permute-done.35 = bf16[256,4096]{1,0:T(8,128)(2,1)S(1)} collective-permute-done((bf16[256,4096]{1,0:T(8,128)(2,1)S(1)}, bf16[256,4096]{1,0:T(8,128)(2,1)S(1)}, u32[]{:S(2)}, u32[]{:S(2)}) %collective-permute-start.35) | collective-permute-done | bytes 2097184 | tf_op jit(solution)/shard_map/ppermute | solution.py:322
  568.0 4.5 fusion.23
  576.0 7.1 concatenate.121
  599.3 4.3 all-to-all-start.1
  607.5 3.1 broadcast_select_fusion.2.grad_ref
  610.6 8.5 all-to-all-done.1
  619.1 7.4 put_rows.1
  629.8 3.6 collective-permute-start.41
  636.5 26.5 %collective-permute-done.39 = bf16[2320,128]{1,0:T(8,128)(2,1)} collective-permute-done((bf16[2320,128]{1,0:T(8,128)(2,1)S(1)}, bf16[2320,128]{1,0:T(8,128)(2,1)}, u32[]{:S(2)}, u32[]{:S(2)}) %collective-permute-start.39) | collective-permute-done | bytes 593952 | tf_op jit(solution)/shard_map/ppermute | solution.py:285
  663.0 6.9 collective-permute-done.40
  669.9 32.7 %collective-permute-done.41 = bf16[2320,128]{1,0:T(8,128)(2,1)} collective-permute-done((bf16[2320,128]{1,0:T(8,128)(2,1)S(1)}, bf16[2320,128]{1,0:T(8,128)(2,1)}, u32[]{:S(2)}, u32[]{:S(2)}) %collective-permute-start.41) | collective-permute-done | bytes 593952 | tf_op jit(solution)/shard_map/ppermute | solution.py:285
  702.6 3.3 fusion.30
  721.4 5.5 collective-permute-done.47
  734.9 17.8 %add_rows.3 = f32[7632,128]{1,0:T(8,128)} custom-call(s32[16384]{0:T(1024)} %bitcast.265, bf16[1792,128]{1,0:T(8,128)(2,1)} %slice.251.refs_0_, bf16[1792,128]{1,0:T(8,128)(2,1)} %slice.252.refs_1_, bf16[1792,128]{1,0:T(8,128)(2,1)} %slice.253.refs_2_, bf16[1792,128]{1,0:T(8,128)(2,1)} %slice.254.refs_3_), custom_call_target="tpu_custom_call" | custom-call | tf_op jit(solution)/shard_map/add_rows/pallas_call | solution.py:560
  752.7 12.5 %update.1 = (f32[7632,128]{1,0:T(8,128)}, f32[7632,128]{1,0:T(8,128)}, f32[1,128]{1,0:T(1,128)}, f32[1,128]{1,0:T(1,128)}) custom-call(f32[7632,128]{1,0:T(8,128)} %get-tuple-element.284.grad_ref, bf16[7632,128]{1,0:T(8,128)(2,1)} %bitcast.262, f32[7632,128]{1,0:T(8,128)} %table_ref.3, f32[7632,128]{1,0:T(8,128)} %first_ref.1, f32[7632,128]{1,0:T(8,128)} %second_ref.1), custom_call_target="tpu_custom_call" | custom-call | tf_op jit(solution)/shard_map/update/pallas_call | solution.py:685
  767.7 4.6 copy-done
  772.2 3.9 span.3
  778.8 4.6 copy-done.1
  784.9 3.9 span.4
  796.7 4.6 copy-done.2
  801.2 3.9 span.5
  815.1 12.6 %press.1 = (f32[1,256,12288]{2,1,0:T(8,128)}, bf16[8,256,1536]{2,1,0:T(8,128)(2,1)S(1)}) custom-call(f32[2]{0:T(128)S(1)} %pad_maximum_fusion.10.scale_ref, f32[256,4096]{1,0:T(8,128)S(1)} %copy-done.14, f32[256,4096]{1,0:T(8,128)S(1)} %copy-done.12, f32[256,4096]{1,0:T(8,128)S(1)} %copy-done.10), custom_call_target="tpu_custom_call" | custom-call | tf_op jit(solution)/shard_map/press/pallas_call | solution.py:644
  833.4 4.3 collective-permute-done.49
  845.5 7.8 collective-permute-done.51
  857.2 4.6 collective-permute-done.50
  861.8 9.4 collective-permute-done.52
  875.4 5.0 multiply_reduce_fusion.11
  881.9 6.2 multiply_reduce_fusion
  898.3 3.5 collective-permute-done.59
  902.2 4.1 collective-permute-done.60
  916.0 4.8 multiply_subtract_fusion.1
  926.0 9.1 convert_element_type.484
  (510 shorter events, 237.6 us)
Async XLA Ops:
  7.2 219.6 %all-gather.4.cloned.1.call-start = ((), (), s32[]{:S(2)}) async-start(), calls=%async_computation.3 | async-start | bytes 28311552 | tf_op jit(solution)/shard_map/all_gather | solution.py:799
  8.0 1.3 collective-permute-start.6
  10.1 4.7 collective-permute-start.7
  14.9 8.3 collective-permute-start.8
  18.5 59.7 %collective-permute-start.10 = (bf16[256,1536]{1,0:T(8,128)(2,1)S(1)}, bf16[256,1536]{1,0:T(8,128)(2,1)S(1)}, u32[]{:S(2)}, u32[]{:S(2)}) collective-permute-start(bf16[256,1536]{1,0:T(8,128)(2,1)S(1)} %convert_element_type.382), channel_id=1, source_target_pairs={{0,3},{1,0},{2,1},{3,2},{4,7},{5,4},{6,5},{7,6},{8,11},{9,8},{10,9... | collective-permute-start | bytes 2359304 | tf_op jit(solution)/shard_map/ppermute | solution.py:255
  22.1 66.2 %collective-permute-start.11 = (bf16[256,1536]{1,0:T(8,128)(2,1)S(1)}, bf16[256,1536]{1,0:T(8,128)(2,1)S(1)}, u32[]{:S(2)}, u32[]{:S(2)}) collective-permute-start(bf16[256,1536]{1,0:T(8,128)(2,1)S(1)} %convert_element_type.382), channel_id=1, source_target_pairs={{0,2},{1,3},{2,0},{3,1},{4,6},{5,7},{6,4},{7,5},{8,10},{9,11},{10,... | collective-permute-start | bytes 2359304 | tf_op jit(solution)/shard_map/ppermute | solution.py:255
  22.1 66.2 %collective-permute-start.12 = (bf16[256,1536]{1,0:T(8,128)(2,1)S(1)}, bf16[256,1536]{1,0:T(8,128)(2,1)S(1)}, u32[]{:S(2)}, u32[]{:S(2)}) collective-permute-start(bf16[256,1536]{1,0:T(8,128)(2,1)S(1)} %convert_element_type.382), channel_id=1, source_target_pairs={{0,1},{1,2},{2,3},{3,0},{4,5},{5,6},{6,7},{7,4},{8,9},{9,10},{10,1... | collective-permute-start | bytes 2359304 | tf_op jit(solution)/shard_map/ppermute | solution.py:255
  23.4 67.5 %copy-start.64 = (s32[4,8,672]{2,1,0:T(8,128)}, s32[4,8,672]{2,1,0:T(8,128)S(1)}, u32[]{:S(2)}) copy-start(s32[4,8,672]{2,1,0:T(8,128)S(1)} %reshape.661) | copy-start | bytes 258052
  94.1 15.4 %collective-permute-start.13 = (bf16[1792,128]{1,0:T(8,128)(2,1)S(1)}, bf16[1792,128]{1,0:T(8,128)(2,1)S(1)}, u32[]{:S(2)}, u32[]{:S(2)}) collective-permute-start(bf16[1792,128]{1,0:T(8,128)(2,1)S(1)} %get-tuple-element.228), channel_id=1, source_target_pairs={{0,1},{1,2},{2,3},{3,0},{4,5},{5,6},{6,7},{7,4},{8,9},{9,10},{10,1... | collective-permute-start | bytes 1376264 | tf_op jit(solution)/shard_map/ppermute | solution.py:285
  95.1 31.0 %collective-permute-start.14 = (bf16[1792,128]{1,0:T(8,128)(2,1)S(1)}, bf16[1792,128]{1,0:T(8,128)(2,1)S(1)}, u32[]{:S(2)}, u32[]{:S(2)}) collective-permute-start(bf16[1792,128]{1,0:T(8,128)(2,1)S(1)} %get-tuple-element.227), channel_id=1, source_target_pairs={{0,2},{1,3},{2,0},{3,1},{4,6},{5,7},{6,4},{7,5},{8,10},{9,11},{10,... | collective-permute-start | bytes 1376264 | tf_op jit(solution)/shard_map/ppermute | solution.py:285
  97.0 29.0 %collective-permute-start.15 = (bf16[1792,128]{1,0:T(8,128)(2,1)S(1)}, bf16[1792,128]{1,0:T(8,128)(2,1)S(1)}, u32[]{:S(2)}, u32[]{:S(2)}) collective-permute-start(bf16[1792,128]{1,0:T(8,128)(2,1)S(1)} %get-tuple-element.226), channel_id=1, source_target_pairs={{0,3},{1,0},{2,1},{3,2},{4,7},{5,4},{6,5},{7,6},{8,11},{9,8},{10,9... | collective-permute-start | bytes 1376264 | tf_op jit(solution)/shard_map/ppermute | solution.py:285
  142.4 30.5 %all-to-all-start = ((bf16[8,512,128]{2,1,0:T(8,128)(2,1)}), bf16[8,512,128]{2,1,0:T(8,128)(2,1)S(1)}, u32[]{:S(2)}, u32[]{:S(2)}) async-start(bf16[8,512,128]{2,1,0:T(8,128)(2,1)} %bitcast.22), calls=%async_computation | async-start | bytes 2097152 | tf_op jit(solution)/shard_map/all_to_all | solution.py:809
  146.0 181.4 %all-gather.6.cloned.1.call-start = ((), (), s32[]{:S(2)}) async-start(), calls=%async_computation.4 | async-start | bytes 17584128 | tf_op jit(solution)/shard_map/all_gather | solution.py:812
  174.5 57.4 %copy-start.28 = (f32[528,1024]{1,0:T(8,128)S(1)}, f32[528,1024]{1,0:T(8,128)}, u32[]{:S(2)}) copy-start(f32[528,1024]{1,0:T(8,128)} %param.28) | copy-start | bytes 6488068
  226.8 475.8 %reduce-scatter.2.cloned.1.call-start = ((), (), s32[]{:S(2)}) async-start(), calls=%async_computation.5 | async-start | bytes 17584128 | tf_op jit(solution)/shard_map/reduce_scatter | solution.py:860
  226.9 17.9 %collective-permute-start.9 = (s32[1,592]{1,0:T(1,128)S(1)}, s32[1,592]{1,0:T(1,128)S(1)}, u32[]{:S(2)}, u32[]{:S(2)}) collective-permute-start(s32[1,592]{1,0:T(1,128)S(1)} %pad_add_fusion.3), channel_id=1, source_target_pairs={{0,0},{1,4},{2,1},{3,5},{4,2},{5,6},{6,3},{7,7},{8,8},{9,12},{10,9... | collective-permute-start | bytes 7112 | tf_op jit(solution)/shard_map/ppermute | solution.py:365
  228.2 6.9 collective-permute-start.22
  236.3 3.7 collective-permute-start.23
  240.5 3.7 collective-permute-start.24
  309.3 7.6 collective-permute-start.16
  310.5 13.5 %collective-permute-start.17 = (bf16[80,1024]{1,0:T(8,128)(2,1)S(1)}, bf16[80,1024]{1,0:T(8,128)(2,1)S(1)}, u32[]{:S(2)}, u32[]{:S(2)}) collective-permute-start(bf16[80,1024]{1,0:T(8,128)(2,1)S(1)} %select_convert_fusion), channel_id=1, source_target_pairs={{0,2},{1,3},{2,0},{3,1},{4,6},{5,7},{6,4},{7,5},{8,10},{9,11},{10,... | collective-permute-start | bytes 491528 | tf_op jit(solution)/shard_map/ppermute | solution.py:255
  311.6 13.1 %collective-permute-start.18 = (bf16[80,1024]{1,0:T(8,128)(2,1)S(1)}, bf16[80,1024]{1,0:T(8,128)(2,1)S(1)}, u32[]{:S(2)}, u32[]{:S(2)}) collective-permute-start(bf16[80,1024]{1,0:T(8,128)(2,1)S(1)} %select_convert_fusion), channel_id=1, source_target_pairs={{0,1},{1,2},{2,3},{3,0},{4,5},{5,6},{6,7},{7,4},{8,9},{9,10},{10,1... | collective-permute-start | bytes 491528 | tf_op jit(solution)/shard_map/ppermute | solution.py:255
  345.2 3.7 collective-permute-start.19
  345.3 4.6 collective-permute-start.20
  346.5 5.4 collective-permute-start.21
  365.2 21.8 %collective-permute-start.25 = (bf16[80,1024]{1,0:T(8,128)(2,1)}, bf16[80,1024]{1,0:T(8,128)(2,1)}, u32[]{:S(2)}, u32[]{:S(2)}) collective-permute-start(bf16[80,1024]{1,0:T(8,128)(2,1)} %get-tuple-element.232), channel_id=1, source_target_pairs={{0,1},{1,2},{2,3},{3,0},{4,5},{5,6},{6,7},{7,4},{8,9},{9,10},{10,1... | collective-permute-start | bytes 491528 | tf_op jit(solution)/shard_map/ppermute | solution.py:272
  365.6 21.4 %collective-permute-start.26 = (bf16[80,1024]{1,0:T(8,128)(2,1)}, bf16[80,1024]{1,0:T(8,128)(2,1)}, u32[]{:S(2)}, u32[]{:S(2)}) collective-permute-start(bf16[80,1024]{1,0:T(8,128)(2,1)} %get-tuple-element.234), channel_id=1, source_target_pairs={{0,2},{1,3},{2,0},{3,1},{4,6},{5,7},{6,4},{7,5},{8,10},{9,11},{10,... | collective-permute-start | bytes 491528 | tf_op jit(solution)/shard_map/ppermute | solution.py:272
  367.4 19.6 %collective-permute-start.27 = (bf16[80,1024]{1,0:T(8,128)(2,1)}, bf16[80,1024]{1,0:T(8,128)(2,1)}, u32[]{:S(2)}, u32[]{:S(2)}) collective-permute-start(bf16[80,1024]{1,0:T(8,128)(2,1)} %get-tuple-element.233), channel_id=1, source_target_pairs={{0,3},{1,0},{2,1},{3,2},{4,7},{5,4},{6,5},{7,6},{8,11},{9,8},{10,9... | collective-permute-start | bytes 491528 | tf_op jit(solution)/shard_map/ppermute | solution.py:272
  388.9 330.8 %sort.9.cloned.1.call-start = ((), (), s32[]{:S(2)}) async-start(), calls=%async_computation.7 | async-start | bytes 196640 | tf_op jit(solution)/shard_map/sort | solution.py:418
  402.4 21.7 %collective-permute-start.29 = (bf16[256,4096]{1,0:T(8,128)(2,1)}, bf16[256,4096]{1,0:T(8,128)(2,1)S(1)}, u32[]{:S(2)}, u32[]{:S(2)}) collective-permute-start(bf16[256,4096]{1,0:T(8,128)(2,1)} %convolution_convert_fusion.2), channel_id=1, source_target_pairs={{0,4},{4,0},{8,12},{12,8},{16,20},{20,16},{24,28},{28,24},{1,5},{5... | collective-permute-start | bytes 6291464 | tf_op jit(solution)/shard_map/ppermute | solution.py:299
  405.1 19.1 %collective-permute-start.28 = (bf16[256,4096]{1,0:T(8,128)(2,1)}, bf16[256,4096]{1,0:T(8,128)(2,1)}, u32[]{:S(2)}, u32[]{:S(2)}) collective-permute-start(bf16[256,4096]{1,0:T(8,128)(2,1)} %convolution_convert_fusion.3), channel_id=1, source_target_pairs={{0,4},{4,0},{8,12},{12,8},{16,20},{20,16},{24,28},{28,24},{1,5},{5... | collective-permute-start | bytes 6291464 | tf_op jit(solution)/shard_map/ppermute | solution.py:298
  440.6 15.2 %collective-permute-start.31 = (bf16[256,4096]{1,0:T(8,128)(2,1)}, bf16[256,4096]{1,0:T(8,128)(2,1)}, u32[]{:S(2)}, u32[]{:S(2)}) collective-permute-start(bf16[256,4096]{1,0:T(8,128)(2,1)} %convolution_convert_fusion), channel_id=1, source_target_pairs={{0,4},{4,0},{8,12},{12,8},{16,20},{20,16},{24,28},{28,24},{1,5},{5... | collective-permute-start | bytes 6291464 | tf_op jit(solution)/shard_map/ppermute | solution.py:299
  440.6 15.2 %collective-permute-start.30 = (bf16[256,4096]{1,0:T(8,128)(2,1)}, bf16[256,4096]{1,0:T(8,128)(2,1)}, u32[]{:S(2)}, u32[]{:S(2)}) collective-permute-start(bf16[256,4096]{1,0:T(8,128)(2,1)} %convolution_convert_fusion.1), channel_id=1, source_target_pairs={{0,4},{4,0},{8,12},{12,8},{16,20},{20,16},{24,28},{28,24},{1,5},{5... | collective-permute-start | bytes 6291464 | tf_op jit(solution)/shard_map/ppermute | solution.py:298
  445.0 47.7 %collective-permute-start.32 = (bf16[256,4096]{1,0:T(8,128)(2,1)}, bf16[256,4096]{1,0:T(8,128)(2,1)}, u32[]{:S(2)}, u32[]{:S(2)}) collective-permute-start(bf16[256,4096]{1,0:T(8,128)(2,1)} %add_convert_fusion.3), channel_id=1, source_target_pairs={{0,1},{1,0},{2,3},{3,2},{4,5},{5,4},{6,7},{7,6},{8,9},{9,8},{10,11... | collective-permute-start | bytes 6291464 | tf_op jit(solution)/shard_map/ppermute | solution.py:322
  498.9 69.1 %collective-permute-start.35 = (bf16[256,4096]{1,0:T(8,128)(2,1)S(1)}, bf16[256,4096]{1,0:T(8,128)(2,1)S(1)}, u32[]{:S(2)}, u32[]{:S(2)}) collective-permute-start(bf16[256,4096]{1,0:T(8,128)(2,1)S(1)} %fusion.24), channel_id=1, source_target_pairs={{0,1},{1,0},{2,3},{3,2},{4,5},{5,4},{6,7},{7,6},{8,9},{9,8},{10,11... | collective-permute-start | bytes 6291464 | tf_op jit(solution)/shard_map/ppermute | solution.py:322
  500.7 16.5 %collective-permute-start.34 = (bf16[256,4096]{1,0:T(8,128)(2,1)S(1)}, bf16[256,4096]{1,0:T(8,128)(2,1)}, u32[]{:S(2)}, u32[]{:S(2)}) collective-permute-start(bf16[256,4096]{1,0:T(8,128)(2,1)S(1)} %pad_maximum_fusion.2), channel_id=1, source_target_pairs={{0,4},{4,0},{8,12},{12,8},{16,20},{20,16},{24,28},{28,24},{1,5},{5... | collective-permute-start | bytes 6291464 | tf_op jit(solution)/shard_map/ppermute | solution.py:299
  501.0 16.2 %collective-permute-start.33 = (bf16[256,4096]{1,0:T(8,128)(2,1)S(1)}, bf16[256,4096]{1,0:T(8,128)(2,1)}, u32[]{:S(2)}, u32[]{:S(2)}) collective-permute-start(bf16[256,4096]{1,0:T(8,128)(2,1)S(1)} %pad_maximum_fusion.1), channel_id=1, source_target_pairs={{0,4},{4,0},{8,12},{12,8},{16,20},{20,16},{24,28},{28,24},{1,5},{5... | collective-permute-start | bytes 6291464 | tf_op jit(solution)/shard_map/ppermute | solution.py:298
  513.5 94.0 %collective-permute-start.43 = (bf16[256,4096]{1,0:T(8,128)(2,1)}, bf16[256,4096]{1,0:T(8,128)(2,1)}, u32[]{:S(2)}, u32[]{:S(2)}) collective-permute-start(bf16[256,4096]{1,0:T(8,128)(2,1)} %add_convert_fusion.2), channel_id=1, source_target_pairs={{2,4},{3,5},{4,2},{5,3},{10,12},{11,13},{12,10},{13,11},{18,20},{1... | collective-permute-start | bytes 6291464 | tf_op jit(solution)/shard_map/ppermute | solution.py:344
  572.5 60.9 %collective-permute-start.44 = (bf16[256,4096]{1,0:T(8,128)(2,1)}, bf16[256,4096]{1,0:T(8,128)(2,1)}, u32[]{:S(2)}, u32[]{:S(2)}) collective-permute-start(bf16[256,4096]{1,0:T(8,128)(2,1)} %fusion.23), channel_id=1, source_target_pairs={{2,4},{3,5},{4,2},{5,3},{10,12},{11,13},{12,10},{13,11},{18,20},{1... | collective-permute-start | bytes 6291464 | tf_op jit(solution)/shard_map/ppermute | solution.py:344
  584.4 6.1 collective-permute-start.36
  592.5 11.2 %collective-permute-start.37 = (bf16[528,256]{1,0:T(8,128)(2,1)}, bf16[528,256]{1,0:T(8,128)(2,1)S(1)}, u32[]{:S(2)}, u32[]{:S(2)}) collective-permute-start(bf16[528,256]{1,0:T(8,128)(2,1)} %dynamic-slice_convert_fusion.2), channel_id=1, source_target_pairs={{0,8},{4,12},{8,0},{12,4},{16,24},{20,28},{24,16},{28,20},{1,9},{5... | collective-permute-start | bytes 811016 | tf_op jit(solution)/shard_map/ppermute | solution.py:744
  595.6 107.0 %collective-permute-start.42 = (bf16[256,4096]{1,0:T(8,128)(2,1)}, bf16[256,4096]{1,0:T(8,128)(2,1)}, u32[]{:S(2)}, u32[]{:S(2)}) collective-permute-start(bf16[256,4096]{1,0:T(8,128)(2,1)} %pad_maximum_fusion.3), channel_id=1, source_target_pairs={{0,1},{1,0},{2,3},{3,2},{4,5},{5,4},{6,7},{7,6},{8,9},{9,8},{10,11... | collective-permute-start | bytes 6291464 | tf_op jit(solution)/shard_map/ppermute | solution.py:322
  599.3 19.8 %all-to-all-start.1 = ((bf16[8,512,128]{2,1,0:T(8,128)(2,1)}), bf16[8,512,128]{2,1,0:T(8,128)(2,1)}, u32[]{:S(2)}, u32[]{:S(2)}) async-start(bf16[8,512,128]{2,1,0:T(8,128)(2,1)} %bitcast.260), calls=%async_computation.1 | async-start | bytes 2097152 | tf_op jit(solution)/shard_map/all_to_all | solution.py:880
  603.6 322.4 %all-gather.8.cloned.1.call-start = ((), (), s32[]{:S(2)}) async-start(), calls=%async_computation.6 | async-start | bytes 7077888 | tf_op jit(solution)/shard_map/all_gather | solution.py:943
  605.6 21.1 %collective-permute-start.38 = (bf16[528,128]{1,0:T(8,128)(2,1)S(1)}, bf16[528,128]{1,0:T(8,128)(2,1)S(1)}, u32[]{:S(2)}, u32[]{:S(2)}) collective-permute-start(bf16[528,128]{1,0:T(8,128)(2,1)S(1)} %dynamic-slice_convert_fusion.6), channel_id=1, source_target_pairs={{0,16},{4,20},{8,24},{12,28},{16,0},{20,4},{24,8},{28,12},{1,17},{... | collective-permute-start | bytes 405512 | tf_op jit(solution)/shard_map/ppermute | solution.py:744
  629.5 33.5 %collective-permute-start.39 = (bf16[2320,128]{1,0:T(8,128)(2,1)S(1)}, bf16[2320,128]{1,0:T(8,128)(2,1)}, u32[]{:S(2)}, u32[]{:S(2)}) collective-permute-start(bf16[2320,128]{1,0:T(8,128)(2,1)S(1)} %get-tuple-element.210), channel_id=1, source_target_pairs={{0,1},{1,2},{2,3},{3,0},{4,5},{5,6},{6,7},{7,4},{8,9},{9,10},{10,1... | collective-permute-start | bytes 1781768 | tf_op jit(solution)/shard_map/ppermute | solution.py:285
  629.5 40.4 %collective-permute-start.40 = (bf16[2320,128]{1,0:T(8,128)(2,1)S(1)}, bf16[2320,128]{1,0:T(8,128)(2,1)}, u32[]{:S(2)}, u32[]{:S(2)}) collective-permute-start(bf16[2320,128]{1,0:T(8,128)(2,1)S(1)} %get-tuple-element.211), channel_id=1, source_target_pairs={{0,2},{1,3},{2,0},{3,1},{4,6},{5,7},{6,4},{7,5},{8,10},{9,11},{10,... | collective-permute-start | bytes 1781768 | tf_op jit(solution)/shard_map/ppermute | solution.py:285
  629.8 72.8 %collective-permute-start.41 = (bf16[2320,128]{1,0:T(8,128)(2,1)S(1)}, bf16[2320,128]{1,0:T(8,128)(2,1)}, u32[]{:S(2)}, u32[]{:S(2)}) collective-permute-start(bf16[2320,128]{1,0:T(8,128)(2,1)S(1)} %get-tuple-element.208), channel_id=1, source_target_pairs={{0,3},{1,0},{2,1},{3,2},{4,7},{5,4},{6,5},{7,6},{8,11},{9,8},{10,9... | collective-permute-start | bytes 1781768 | tf_op jit(solution)/shard_map/ppermute | solution.py:285
  713.1 5.2 collective-permute-start.46
  715.1 80.6 %collective-permute-start.45 = (bf16[256,4096]{1,0:T(8,128)(2,1)}, bf16[256,4096]{1,0:T(8,128)(2,1)}, u32[]{:S(2)}, u32[]{:S(2)}) collective-permute-start(bf16[256,4096]{1,0:T(8,128)(2,1)} %pad_maximum_fusion.4), channel_id=1, source_target_pairs={{2,4},{3,5},{4,2},{5,3},{10,12},{11,13},{12,10},{13,11},{18,20},{1... | collective-permute-start | bytes 6291464 | tf_op jit(solution)/shard_map/ppermute | solution.py:344
  718.4 8.4 collective-permute-start.47
  727.9 64.9 %collective-permute-start.48 = (bf16[528,512]{1,0:T(8,128)(2,1)}, bf16[528,512]{1,0:T(8,128)(2,1)}, u32[]{:S(2)}, u32[]{:S(2)}) collective-permute-start(bf16[528,512]{1,0:T(8,128)(2,1)} %pad_maximum_fusion.6), channel_id=1, source_target_pairs={{0,4},{4,0},{8,12},{12,8},{16,20},{20,16},{24,28},{28,24},{1,5},{5... | collective-permute-start | bytes 1622024 | tf_op jit(solution)/shard_map/ppermute | solution.py:758
  830.0 7.7 collective-permute-start.49
  841.2 12.2 %collective-permute-start.51 = (bf16[128,1536]{1,0:T(8,128)(2,1)}, bf16[128,1536]{1,0:T(8,128)(2,1)S(1)}, u32[]{:S(2)}, u32[]{:S(2)}) collective-permute-start(bf16[128,1536]{1,0:T(8,128)(2,1)} %get-tuple-element.201), channel_id=1, source_target_pairs={{0,8},{4,12},{8,0},{12,4},{16,24},{20,28},{24,16},{28,20},{1,9},{5... | collective-permute-start | bytes 1179656 | tf_op jit(solution)/shard_map/ppermute | solution.py:709
  841.8 19.9 %collective-permute-start.50 = (bf16[128,1536]{1,0:T(8,128)(2,1)}, bf16[128,1536]{1,0:T(8,128)(2,1)S(1)}, u32[]{:S(2)}, u32[]{:S(2)}) collective-permute-start(bf16[128,1536]{1,0:T(8,128)(2,1)} %get-tuple-element.200), channel_id=1, source_target_pairs={{0,8},{4,12},{8,0},{12,4},{16,24},{20,28},{24,16},{28,20},{1,9},{5... | collective-permute-start | bytes 1179656 | tf_op jit(solution)/shard_map/ppermute | solution.py:709
  843.4 12.1 %collective-permute-start.54 = (bf16[128,1536]{1,0:T(8,128)(2,1)S(1)}, bf16[128,1536]{1,0:T(8,128)(2,1)S(1)}, u32[]{:S(2)}, u32[]{:S(2)}) collective-permute-start(bf16[128,1536]{1,0:T(8,128)(2,1)S(1)} %get-tuple-element.207), channel_id=1, source_target_pairs={{0,16},{4,20},{8,24},{12,28},{16,0},{20,4},{24,8},{28,12},{1,17},{... | collective-permute-start | bytes 1179656 | tf_op jit(solution)/shard_map/ppermute | solution.py:709
  844.5 27.9 %collective-permute-start.53 = (bf16[128,1536]{1,0:T(8,128)(2,1)S(1)}, bf16[128,1536]{1,0:T(8,128)(2,1)S(1)}, u32[]{:S(2)}, u32[]{:S(2)}) collective-permute-start(bf16[128,1536]{1,0:T(8,128)(2,1)S(1)} %get-tuple-element.206), channel_id=1, source_target_pairs={{0,16},{4,20},{8,24},{12,28},{16,0},{20,4},{24,8},{28,12},{1,17},{... | collective-permute-start | bytes 1179656 | tf_op jit(solution)/shard_map/ppermute | solution.py:709
  854.5 16.7 %collective-permute-start.52 = (bf16[128,1536]{1,0:T(8,128)(2,1)S(1)}, bf16[128,1536]{1,0:T(8,128)(2,1)S(1)}, u32[]{:S(2)}, u32[]{:S(2)}) collective-permute-start(bf16[128,1536]{1,0:T(8,128)(2,1)S(1)} %fusion.59), channel_id=1, source_target_pairs={{0,16},{4,20},{8,24},{12,28},{16,0},{20,4},{24,8},{28,12},{1,17},{... | collective-permute-start | bytes 1179656 | tf_op jit(solution)/shard_map/ppermute | solution.py:709
  855.8 16.7 %collective-permute-start.55 = (bf16[128,1536]{1,0:T(8,128)(2,1)S(1)}, bf16[128,1536]{1,0:T(8,128)(2,1)S(1)}, u32[]{:S(2)}, u32[]{:S(2)}) collective-permute-start(bf16[128,1536]{1,0:T(8,128)(2,1)S(1)} %fusion.57), channel_id=1, source_target_pairs={{0,8},{4,12},{8,0},{12,4},{16,24},{20,28},{24,16},{28,20},{1,9},{5... | collective-permute-start | bytes 1179656 | tf_op jit(solution)/shard_map/ppermute | solution.py:709
  890.1 1.1 collective-permute-start.56
  891.2 3.5 collective-permute-start.57
  894.8 3.5 collective-permute-start.58
  898.3 3.5 collective-permute-start.59
  901.9 4.4 collective-permute-start.60
  (93 other events, 958.5 us)
Sparse Core Ops, SparseCore 0:
  90.7 136.0 all-gather.3
  229.3 88.0 all-gather.5
  389.0 111.3 reduce-scatter.1
  502.9 11.4 sort.11.cloned.1.call-done
  880.6 43.9 all-gather.7
  (1 shorter events, 0.0 us)

commit v7 on v6

--- a/solution.py
+++ b/solution.py
@@ -153,10 +153,8 @@
     return (peak, total, first[2] + second[2])
 
 
-def layer_forward(embedded, docs, small, weights):
+def layer_forward(embedded, x0, act, docs, small, weights):
     base = L + 2
-    x0 = norm_rows(embedded, small[base], small[base + 1])
-    act = x0.astype(jnp.bfloat16)
     bias = jnp.concatenate([small[base + 6], jnp.zeros((D,), jnp.float32), small[base + 7]])
     qkv = (matmul(act, weights[:, 0 : 3 * D]) + bias).astype(jnp.bfloat16)
     out, lse = attend(qkv, docs)
@@ -198,8 +196,7 @@
     _, pull = jax.vjp(norm_rows, embedded, small[base], small[base + 1])
     dembed, dgain_emb, dshift_emb = pull(dxzero)
     dembed = mixed.received(dembed)
-    mixed.across()
-    (dembed,) = up.crossed(dembed)
+    mixed.across(up)
     up.finish()
     bias_qkv = jnp.sum(dqkv, axis=0, dtype=jnp.float32)
     vectors = jnp.stack(
@@ -315,10 +312,12 @@
             value, self.far, self.near = together(value, self.far, self.near)
         return value
 
-    def across(self):
+    def across(self, before=None):
         if self.paired:
             sides = swap_pairs(lax.axis_size("narrow"), 1)
             away = self.block(self.core, 1 - self.side, self.far)
+            if before is not None:
+                away, before.near = together(away, before.near)
             self.away = lax.ppermute(away, "narrow", sides)
 
     def crossed(self, *values):
@@ -326,12 +325,12 @@
             *values, self.away = together(*values, self.away)
         return values
 
-    def finish(self):
+    def finish(self, *values):
         if not self.paired:
             blocks = [matmul_tn(left, right).astype(jnp.bfloat16) for left, right in self.pairs]
             grad = jnp.concatenate(blocks, axis=1)
             self.result = lax.psum_scatter(grad, "narrow", scatter_dimension=0, tiled=True)
-            return
+            return values
         n_wide, n_narrow = lax.axis_size("wide"), lax.axis_size("narrow")
         total = self.block(self.core, self.side, self.near, self.away)
         moves = []
@@ -341,8 +340,10 @@
                     target_wide = wide - wide % 2 + narrow // 2
                     target = target_wide * n_narrow + 2 * (wide % 2) + narrow % 2
                     moves.append((wide * n_narrow + narrow, target))
+        total, *values = together(total, *values)
         moved = lax.ppermute(total, ("wide", "narrow"), moves)
         self.result = jnp.where(self.pair == self.core, total, moved)
+        return values
 
 
 def hosted_rows(token_ids, mlm_labels, mlm_valid, doc_ids, mlm_pos):
@@ -532,14 +533,14 @@
     )(ids, values)
 
 
-def add_kernel(ids_ref, *refs):
+def add_kernel(length, ids_ref, *refs):
     count = (len(refs) - 1) // 3
     rows_refs, out_ref, rows, sums = refs[:count], refs[count], refs[count + 1 : 2 * count + 1], refs[2 * count + 1 :]
-    size, length = out_ref.shape[0], rows_refs[0].shape[0]
+    size = out_ref.shape[0]
     each = ids_ref.shape[0] // count
     for part, held, rows_ref in zip(sums, rows, rows_refs):
         part[...] = jnp.zeros_like(part)
-        held[...] = rows_ref[...].astype(jnp.float32)
+        held[...] = rows_ref[0:length, :].astype(jnp.float32)
 
     @pl.loop(0, length, step=8)
     def _(first):
@@ -554,11 +555,11 @@
     out_ref[...] = total
 
 
-def added_rows(ids, values, size):
-    length, cols = values[0].shape
-    block = pl.BlockSpec((length, cols), lambda step, ids: (0, 0))
+def added_rows(ids, values, size, length):
+    cols = values[0].shape[1]
+    block = pl.BlockSpec(values[0].shape, lambda step, ids: (0, 0))
     return pl.pallas_call(
-        add_kernel,
+        functools.partial(add_kernel, length),
         grid_spec=pltpu.PrefetchScalarGridSpec(
             num_scalar_prefetch=1,
             grid=(1,),
@@ -606,7 +607,7 @@
             jax.ShapeDtypeStruct((rows, cols), jnp.float32),
             jax.ShapeDtypeStruct((1, block), jnp.float32),
         ],
-        compiler_params=pltpu.CompilerParams(vmem_limit_bytes=24 * 2**20),
+        compiler_params=pltpu.CompilerParams(vmem_limit_bytes=60 * 2**20),
         cost_estimate=FREE,
         name="span",
     )(momentum, grad, error)
@@ -653,7 +654,7 @@
             jax.ShapeDtypeStruct((1, rows, cols), jnp.float32),
             jax.ShapeDtypeStruct((parts, rows, cols // parts), jnp.bfloat16),
         ],
-        compiler_params=pltpu.CompilerParams(vmem_limit_bytes=24 * 2**20),
+        compiler_params=pltpu.CompilerParams(vmem_limit_bytes=60 * 2**20),
         cost_estimate=FREE,
         name="press",
     )(jnp.stack([scale, 1.0 / scale]), *spans)
@@ -808,8 +809,7 @@
         looked = lax.cond(owners.full, lambda: looked_up(owners.count), lambda: looked)
         looked = lax.all_to_all(looked.reshape(n_wide, L, -1), "wide", 0, 0)
         looked = looked.transpose(1, 0, 2).reshape(1, L, D)
-        table_low, weights, looked = together(table_low, weights, looked)
-        table_cols = lax.all_gather(table_low, "wide", axis=1, tiled=True)
+        looked, count, doc_ids, mlm_pos = together(looked, count, doc_ids, mlm_pos)
     else:
         local_ids = token_ids - narrow_me * vshard
         inside = (local_ids >= 0) & (local_ids < vshard)
@@ -821,7 +821,13 @@
     looked = looked.astype(jnp.float32)
     even_doc = (doc_ids % 2 == 0)[..., None]
     embedded = looked + small[0:L][None] + jnp.where(even_doc, small[L], small[L + 1])
-    htwo, kept = layer_forward(embedded.reshape(seqs * L, D), doc_ids, small, weights)
+    embedded = embedded.reshape(seqs * L, D)
+    x0 = norm_rows(embedded, small[L + 2], small[L + 3])
+    act = x0.astype(jnp.bfloat16)
+    if paired:
+        table_low, weights, act = together(table_low, weights, act)
+        table_cols = lax.all_gather(table_low, "wide", axis=1, tiled=True)
+    htwo, kept = layer_forward(embedded, x0, act, doc_ids, small, weights)
     hmask = jnp.take_along_axis(htwo.reshape(seqs, L, D), mlm_pos[..., None], axis=1)
     hmask = hmask.reshape(seqs * MPS, D).astype(jnp.bfloat16)
     if paired:
@@ -879,27 +885,25 @@
         cut = dembed.astype(jnp.bfloat16).reshape(L, n_wide, D // n_wide).transpose(1, 0, 2)
         cut = lax.all_to_all(cut, "wide", 0, 0).reshape(n_wide * L, D // n_wide)
         halved = small_halved(small_grad).astype(jnp.bfloat16)
+        down, up = pieces[2], pieces[1]
+        cut, mixed.away = together(cut, mixed.away)
+        cut, halved = mixed.finish(cut, halved)
         placed = put_rows(owners.owner_slots(), cut, n_narrow * owners.count)
         placed = placed.reshape(n_narrow, owners.count, -1)
-        near = placed[:, 0 : owners.room]
         wider = jnp.broadcast_to(halved[None], (n_narrow,) + halved.shape)
-        near = sent_around(jnp.concatenate([near, wider], axis=1))
-        down, up = pieces[2], pieces[1]
-        *near, mixed.away, down.result, up.result, table_head = together(
-            *near, mixed.away, down.result, up.result, table_head
-        )
-        mixed.finish()
-        table_grad = added_rows(packed_ids, [part[0 : owners.room] for part in near], vshard)
+        near = sent_around(jnp.concatenate([placed[:, 0 : owners.room], wider], axis=1))
+        table_grad = added_rows(packed_ids, near, vshard, owners.room)
         table_grad = lax.cond(
             owners.full,
-            lambda: added_rows(packed_ids, sent_around(placed), vshard),
+            lambda: added_rows(packed_ids, sent_around(placed), vshard, owners.count),
             lambda: table_grad,
         )
         table_mom, table_upd, table_norms = table_update(
             table_grad, table_head, table, table_m, table_v
         )
-        small_grad = small_total([part[owners.room :] for part in near])
-        mixed.result, table_norms, small_grad = together(mixed.result, table_norms, small_grad)
+        mixed.result, down.result, up.result, table_norms = together(
+            mixed.result, down.result, up.result, table_norms
+        )
     else:
         mixed.finish()
         group_rows = lax.all_gather(dembed_rows.astype(jnp.bfloat16), "narrow", axis=0, tiled=True)
@@ -918,6 +922,8 @@
             total = total + amount
         scale = total / (layer_m.shape[0] * layer_m.shape[1]) + MAG_EPS
         new_worker, sent = pressed(spans, scale, n_wide)
+        sent, *near = together(sent, *[part[owners.room :] for part in near])
+        small_grad = small_total(near)
         server_in = scattered_sum(sent) / n_wide + server_err
     else:
         worker_grad = jnp.concatenate([piece.result for piece in pieces], axis=1)

time: 950 us -> 1030 us (1.084)
  waiting for transfers between devices: 321 us -> 394 us
  local copies, waits for them, and re-layouts: 90.6 us -> 60 us
  starting transfers between devices: 78 us -> 103 us
  Pallas kernels: 149 us -> 164 us
    all_gather x1, waiting for transfers between devices: 0.01 us -> 81.1 us  [shards(): table_cols = lax.all_gather(table_low, 'wide', axis=1, tiled=True)]
    ppermute x6, waiting for transfers between devices: 92.2 us -> 131 us  [sent_around(): lax.ppermute(block(by), 'narrow', cycle(size, by))]
    unnamed x221 -> x219, local copies, waits for them, and re-layouts: 52.8 us -> 20.4 us
    all_to_all x1, waiting for transfers between devices: 23 us -> 0.01 us  [shards(): looked = lax.all_to_all(looked.reshape(n_wide, L, -1), 'wide', 0, 0)]
    ppermute x9, waiting for transfers between devices: 23.7 us -> 4.6 us  [gathered_near(): around.append(lax.ppermute(value, 'narrow', cycle(size, size - by)))]
    ppermute x3, waiting for transfers between devices: 70.9 us -> 89.1 us  [across(): self.away = lax.ppermute(away, 'narrow', sides)]
    all_gather x1, waiting for transfers between devices: 50.6 us -> 33.7 us  [shards(): weights = lax.all_gather(layer_rows, 'wide', axis=1, tiled=True)]
    ppermute x8, starting transfers between devices: 10.5 us -> 24.4 us  [summed_over(): value = value + lax.ppermute(value, axis, swap_pairs(size, bit))]
  transfers between devices with their start and end apart: 61 -> 61, of which waited for: 31 -> 30; matrix products, arithmetic and copies ran while one was open for 26% -> 19% of each run, Pallas kernels for 14% -> 10%
where the time goes in v7:
time: 1030 us; the launch traced here: 1020 us
  waiting for transfers between devices  394 us (38%)
  Pallas kernels  164 us (16%)
  matrix products  157 us (15%)
  other arithmetic  109 us (11%)
  starting transfers between devices  103 us (10%)
  local copies, waits for them, and re-layouts  60 us (6%)
  between operations  23.5 us (2%)
    ppermute x6, waiting for transfers between devices, sent_around(): lax.ppermute(block(by), 'narrow', cycle(size, by))  131 us
    ppermute x3, waiting for transfers between devices, across(): self.away = lax.ppermute(away, 'narrow', sides)  89.1 us
    all_gather x1, waiting for transfers between devices, shards(): table_cols = lax.all_gather(table_low, 'wide', axis=1, tiled=True)  81.1 us
    dot_general x5, matrix products, matmul(): return jnp.dot(left, right, preferred_element_type=jnp.float32)  59.9 us
    pallas_call x1, Pallas kernels, packed_rows(): pl.pallas_call(pack_kernel, grid_spec=pltpu.PrefetchScalarGridSpec(num_sc...  52.4 us
    dot_general x5, matrix products, matmul_nt(): lax.dot_general(left, right, (((1,), (1,)), ((), ())), preferred_element_...  40.6 us
    dot_general x16, matrix products, matmul_tn(): lax.dot_general(left, right, (((0,), (0,)), ((), ())), preferred_element_...  39 us
    all_gather x1, waiting for transfers between devices, shards(): weights = lax.all_gather(layer_rows, 'wide', axis=1, tiled=True)  33.7 us
  transfers between devices with their start and end apart: 61, of which 30 were waited for; matrix products, arithmetic and copies ran while one was open for 19% of the time, Pallas kernels for 10%

profile of v7, /device:TPU:0, one launch (start us, length us, event | category | flops | bytes accessed | tf_op | source)
XLA Modules:
  0.0 1021.6 jit_solution(17102483198415129995)
XLA Ops:
  26.6 52.4 %pack_rows.1 = bf16[4,4096,128]{2,1,0:T(8,128)(2,1)} custom-call(s32[16384]{0:T(1024)S(1)} %fusion.107.ids_ref, f32[7632,128]{1,0:T(8,128)S(1)} %copy-done.2), custom_call_target="tpu_custom_call" | custom-call | bytes 150000000 | tf_op jit(solution)/shard_map/pack_rows/pallas_call | solution.py:454
  84.3 11.8 %collective-permute-start.14 = (bf16[1792,128]{1,0:T(8,128)(2,1)S(1)}, bf16[1792,128]{1,0:T(8,128)(2,1)S(1)}, u32[]{:S(2)}, u32[]{:S(2)}) collective-permute-start(bf16[1792,128]{1,0:T(8,128)(2,1)S(1)} %get-tuple-element.240), channel_id=1, source_target_pairs={{0,3},{1,0},{2,1},{3,2},{4,7},{5,4},{6,5},{7,6},{8,11},{9,8},{10,9... | collective-permute-start | bytes 1376264 | tf_op jit(solution)/shard_map/ppermute | solution.py:282
  96.7 10.3 %collective-permute-done.14 = bf16[1792,128]{1,0:T(8,128)(2,1)S(1)} collective-permute-done((bf16[1792,128]{1,0:T(8,128)(2,1)S(1)}, bf16[1792,128]{1,0:T(8,128)(2,1)S(1)}, u32[]{:S(2)}, u32[]{:S(2)}) %collective-permute-start.14) | collective-permute-done | bytes 458784 | tf_op jit(solution)/shard_map/ppermute | solution.py:282
  107.0 29.3 %collective-permute-done.13 = bf16[1792,128]{1,0:T(8,128)(2,1)S(1)} collective-permute-done((bf16[1792,128]{1,0:T(8,128)(2,1)S(1)}, bf16[1792,128]{1,0:T(8,128)(2,1)S(1)}, u32[]{:S(2)}, u32[]{:S(2)}) %collective-permute-start.13) | collective-permute-done | bytes 458784 | tf_op jit(solution)/shard_map/ppermute | solution.py:282
  136.5 6.6 take_rows.3
  143.1 9.5 conditional.2
  152.6 3.6 all-to-all-start
  161.3 3.6 convert_element_type.376
  166.8 13.1 %collective-permute-start.16 = (f32[]{:T(128)}, f32[]{:T(128)}, u32[]{:S(2)}, u32[]{:S(2)}) collective-permute-start(f32[]{:T(128)} %add.750), channel_id=1, source_target_pairs={{0,8},{4,12},{8,0},{12,4},{16,24},{20,28},{24,16},{28,20},{1,9},{5... | collective-permute-start | bytes 20 | tf_op jit(solution)/shard_map/ppermute | solution.py:242
  192.8 33.7 %all-gather.4.cloned.1.call-done = bf16[1024,12288]{1,0:T(8,128)(2,1)} async-done(((bf16[1024,1536]{1,0:T(8,128)(2,1)}), bf16[1024,12288]{1,0:T(8,128)(2,1)}) %all-gather.4.cloned.1.call-update) | async-done | bytes 25165840 | tf_op jit(solution)/shard_map/all_gather | solution.py:800
  226.5 6.5 add_convert_fusion.1.q_ref.k_ref.v_ref
  233.1 11.7 %attend.1 = (bf16[512,1024]{1,0:T(8,128)(2,1)S(1)}, f32[8,2,512]{2,1,0:T(2,128)S(1)}) custom-call(bf16[512,3072]{1,0:T(8,128)(2,1)S(1)} %add_convert_fusion.1.q_ref.k_ref.v_ref, bf16[512,3072]{1,0:T(8,128)(2,1)S(1)} %add_convert_fusion.1.q_ref.k_ref.v_ref, bf16[512,3072]{1,0:T(8,128)(2,1)S(1)} %add_convert_fusion.1.q_ref.k_ref.v_ref, ...), custom_call_target="tpu_custom_call" | custom-call | tf_op jit(solution)/shard_map/attend/pallas_call | solution.py:86
  244.8 3.4 fusion.177
  249.2 26.1 %multiply_convert_fusion = (bf16[512,4096]{1,0:T(8,128)(2,1)S(1)}, f32[512,4096]{1,0:T(8,128)}, f32[512,4096]{1,0:T(8,128)}) fusion(f32[4096]{0:T(1024)S(1)} %bitcast.298, bf16[512,1024]{1,0:T(8,128)(2,1)S(1)} %fusion.39, bf16[1024,12288]{1,0:T(8,128)(2,1)} %all-gather.4.cloned.1.call-done), kind=kOutput, calls=%fused_computation.25 | convolution fusion | flops 4433379328 | bytes 30425088 | tf_op jit(solution)/shard_map/dot_general | solution.py:49
  275.3 9.2 fusion.178
  309.0 81.1 %all-gather.6.cloned.1.call-done = bf16[7632,1024]{1,0:T(8,128)(2,1)} async-done(((bf16[7632,128]{1,0:T(8,128)(2,1)}), bf16[7632,1024]{1,0:T(8,128)(2,1)}) %all-gather.6.cloned.1.call-update) | async-done | bytes 15630352 | tf_op jit(solution)/shard_map/all_gather | solution.py:829
  390.1 11.3 %fusion.179 = (f32[320]{0:T(512)S(1)}, f32[320,7632]{1,0:T(8,128)}) fusion(bf16[7632,1024]{1,0:T(8,128)(2,1)} %all-gather.6.cloned.1.call-done, bf16[560,1024]{1,0:T(8,128)(2,1)} %constant_dynamic-update-slice_fusion.7, s32[]{:T(128)S(6)} %select_n.430, pred[7632]{0:T(1024)(128)(4,1)S(1)} %broadcast_compare_fusion.1), kind=kOutput, calls=%fused_computation.437 | convolution fusion | flops 5006591488 | bytes 26063572 | tf_op jit(solution)/shard_map/dot_general | solution.py:59
  401.4 6.4 exponential_reduce_fusion
  416.2 9.7 fusion.159
  427.2 3.3 collective-permute-start.27
  430.6 17.7 %convert_bitcast_fusion = bf16[8,7632,128]{2,1,0:T(8,128)(2,1)} fusion(f32[320,7632]{1,0:T(8,128)} %get-tuple-element.290, f32[320]{0:T(512)S(1)} %get-tuple-element.274, f32[320]{0:T(512)S(1)} %get-tuple-element.181, s32[7632]{0:T(1024)S(1)} %iota_add_fusion, s32[320]{0:T(512)S(1)} %eq.135, bf16[560,1024]{1,0:T(8,128)(2,1)} %constant_dynamic-update-slice_fusion.7, ...), kind=kOutput, calls=%fused_computation.12 | convolution fusion | flops 5024176128 | bytes 26150468 | tf_op jit(solution)/shard_map/sv,swc->wvc/dot_general | solution.py:864
  450.3 3.3 scatter_custom_fusion
  464.3 3.5 fusion.76
  469.2 14.2 %add_convert_fusion = bf16[512,4096]{1,0:T(8,128)(2,1)S(1)} fusion(f32[512,4096]{1,0:T(8,128)} %get-tuple-element.197, f32[512,4096]{1,0:T(8,128)} %get-tuple-element.286, f32[4096]{0:T(1024)S(1)} %bitcast.299, bf16[512,1024]{1,0:T(8,128)(2,1)S(1)} %get-tuple-element.187, bf16[1024,12288]{1,0:T(8,128)(2,1)} %all-gather.4.cloned.1.call-done), kind=kOutput, calls=%fused_computation.24 | convolution fusion | flops 4326424576 | bytes 30425088 | tf_op jit(solution)/shard_map/dot_general | solution.py:49
  483.4 3.1 convolution_convert_fusion.1
  489.7 3.7 add_convert_fusion.3
  495.6 10.3 %multiply_reduce_fusion.3 = (f32[1024]{0:T(1024)S(1)}, f32[512]{0:T(512)S(1)}, f32[1024]{0:T(1024)S(1)}, f32[512,1024]{1,0:T(8,128)}) fusion(f32[512,1024]{1,0:T(8,128)S(1)} %copy-done.19, f32[512]{0:T(512)S(1)} %copy-done.72, f32[512]{0:T(512)S(1)} %copy-done.65, f32[1024]{0:T(1024)S(1)} %bitcast.288, bf16[512,4096]{1,0:T(8,128)(2,1)S(1)} %add_convert_fusion, ...), kind=kOutput, calls=%fused_computation.101 | convolution fusion | flops 4300207616 | bytes 18894848 | tf_op jit(solution)/shard_map/dot_general | solution.py:59
  511.6 3.3 fusion.47.do_ref
  515.0 16.5 %attend_back.1 = bf16[512,3072]{1,0:T(8,128)(2,1)S(1)} custom-call(bf16[512,3072]{1,0:T(8,128)(2,1)S(1)} %copy-done.1, bf16[512,3072]{1,0:T(8,128)(2,1)S(1)} %copy-done.1, bf16[512,3072]{1,0:T(8,128)(2,1)S(1)} %copy-done.1, bf16[512,1024]{1,0:T(8,128)(2,1)S(1)} %fusion.47.do_ref, f32[8,2,512]{2,1,0:T(2,128)S(1)} %get-tuple-element.110.lse_ref, ...), custom_call_target="tpu_custom_call" | custom-call | tf_op jit(solution)/shard_map/attend_back/pallas_call | solution.py:130
  531.5 10.2 collective-permute-done.32
  545.6 6.5 multiply_reduce_fusion.4
  552.1 4.3 fusion.24
  562.7 7.3 concatenate.123
  581.7 3.9 add_convert_fusion.2
  588.9 4.8 all-to-all-start.1
  596.9 30.8 %collective-permute-done.41 = bf16[256,4096]{1,0:T(8,128)(2,1)} collective-permute-done((bf16[256,4096]{1,0:T(8,128)(2,1)}, bf16[256,4096]{1,0:T(8,128)(2,1)}, u32[]{:S(2)}, u32[]{:S(2)}) %collective-permute-start.41) | collective-permute-done | bytes 2097184 | tf_op jit(solution)/shard_map/ppermute | solution.py:321
  627.6 6.5 fusion.23
  636.2 48.2 %collective-permute-done.35 = bf16[256,4096]{1,0:T(8,128)(2,1)} collective-permute-done((bf16[256,4096]{1,0:T(8,128)(2,1)}, bf16[256,4096]{1,0:T(8,128)(2,1)}, u32[]{:S(2)}, u32[]{:S(2)}) %collective-permute-start.35) | collective-permute-done | bytes 2097184 | tf_op jit(solution)/shard_map/ppermute | solution.py:321
  684.3 3.3 fusion.29
  691.6 3.1 broadcast_select_fusion.1.grad_ref
  694.7 7.4 put_rows.1
  708.6 3.1 broadcast_select_fusion.grad_ref
  711.7 15.2 %collective-permute-done.45.refs_3_ = bf16[2320,128]{1,0:T(8,128)(2,1)S(1)} collective-permute-done((bf16[2320,128]{1,0:T(8,128)(2,1)S(1)}, bf16[2320,128]{1,0:T(8,128)(2,1)S(1)}, u32[]{:S(2)}, u32[]{:S(2)}) %collective-permute-start.45) | collective-permute-done | bytes 593952 | tf_op jit(solution)/shard_map/ppermute | solution.py:282
  727.0 24.0 %collective-permute-done.43.refs_1_ = bf16[2320,128]{1,0:T(8,128)(2,1)S(1)} collective-permute-done((bf16[2320,128]{1,0:T(8,128)(2,1)S(1)}, bf16[2320,128]{1,0:T(8,128)(2,1)S(1)}, u32[]{:S(2)}, u32[]{:S(2)}) %collective-permute-start.43) | collective-permute-done | bytes 593952 | tf_op jit(solution)/shard_map/ppermute | solution.py:282
  751.0 52.0 %collective-permute-done.44.refs_2_ = bf16[2320,128]{1,0:T(8,128)(2,1)S(1)} collective-permute-done((bf16[2320,128]{1,0:T(8,128)(2,1)S(1)}, bf16[2320,128]{1,0:T(8,128)(2,1)S(1)}, u32[]{:S(2)}, u32[]{:S(2)}) %collective-permute-start.44) | collective-permute-done | bytes 593952 | tf_op jit(solution)/shard_map/ppermute | solution.py:282
  803.7 17.8 %add_rows.3 = f32[7632,128]{1,0:T(8,128)} custom-call(s32[16384]{0:T(1024)} %bitcast.266, bf16[2320,128]{1,0:T(8,128)(2,1)} %bitcast.263, bf16[2320,128]{1,0:T(8,128)(2,1)} %copy-done.54, bf16[2320,128]{1,0:T(8,128)(2,1)} %copy-done.55, bf16[2320,128]{1,0:T(8,128)(2,1)} %copy-done.53), custom_call_target="tpu_custom_call" | custom-call | tf_op jit(solution)/shard_map/add_rows/pallas_call | solution.py:561
  826.7 12.3 %update.1 = (f32[7632,128]{1,0:T(8,128)}, f32[7632,128]{1,0:T(8,128)}, f32[1,128]{1,0:T(1,128)}, f32[1,128]{1,0:T(1,128)}) custom-call(f32[7632,128]{1,0:T(8,128)} %get-tuple-element.296.grad_ref, bf16[7632,128]{1,0:T(8,128)(2,1)} %bitcast.264, f32[7632,128]{1,0:T(8,128)} %table_ref.3, f32[7632,128]{1,0:T(8,128)} %first_ref.1, f32[7632,128]{1,0:T(8,128)} %second_ref.1), custom_call_target="tpu_custom_call" | custom-call | tf_op jit(solution)/shard_map/update/pallas_call | solution.py:686
  841.6 6.5 span.3
  849.4 6.5 span.4
  857.2 6.6 span.5
  867.6 19.8 %press.1 = (f32[1,256,12288]{2,1,0:T(8,128)}, bf16[8,256,1536]{2,1,0:T(8,128)(2,1)}) custom-call(f32[2]{0:T(128)} %pad_maximum_fusion.10.scale_ref, f32[256,4096]{1,0:T(8,128)} %get-tuple-element.137.refs_0_, f32[256,4096]{1,0:T(8,128)} %get-tuple-element.138.refs_1_, f32[256,4096]{1,0:T(8,128)} %get-tuple-element.139.refs_2_), custom_call_target="tpu_custom_call" | custom-call | tf_op jit(solution)/shard_map/press/pallas_call | solution.py:645
  887.4 5.1 dynamic-slice_bitcast_fusion.9
  893.8 4.7 collective-permute-done.46
  906.3 7.9 collective-permute-done.48
  917.5 7.2 collective-permute-done.51
  927.0 5.0 collective-permute-done.49
  935.7 4.5 multiply_reduce_fusion.11
  942.9 3.7 collective-permute-done.58
  948.2 9.6 collective-permute-done.59
  961.4 5.0 multiply_reduce_fusion
  977.1 3.1 collective-permute-start.56
  982.6 3.6 collective-permute-done.57
  995.9 4.7 multiply_subtract_fusion.1
  1005.8 9.1 convert_element_type.484
  (508 shorter events, 206.7 us)
Async XLA Ops:
  7.2 219.3 %all-gather.4.cloned.1.call-start = ((), (), s32[]{:S(2)}) async-start(), calls=%async_computation.3 | async-start | bytes 28311552 | tf_op jit(solution)/shard_map/all_gather | solution.py:800
  8.0 1.3 collective-permute-start.9
  10.1 4.7 collective-permute-start.10
  14.9 9.2 collective-permute-start.11
  18.5 60.6 %collective-permute-start.8 = (bf16[256,1536]{1,0:T(8,128)(2,1)S(1)}, bf16[256,1536]{1,0:T(8,128)(2,1)S(1)}, u32[]{:S(2)}, u32[]{:S(2)}) collective-permute-start(bf16[256,1536]{1,0:T(8,128)(2,1)S(1)} %convert_element_type.377), channel_id=1, source_target_pairs={{0,1},{1,2},{2,3},{3,0},{4,5},{5,6},{6,7},{7,4},{8,9},{9,10},{10,1... | collective-permute-start | bytes 2359304 | tf_op jit(solution)/shard_map/ppermute | solution.py:252
  20.1 58.9 %collective-permute-start.7 = (bf16[256,1536]{1,0:T(8,128)(2,1)S(1)}, bf16[256,1536]{1,0:T(8,128)(2,1)S(1)}, u32[]{:S(2)}, u32[]{:S(2)}) collective-permute-start(bf16[256,1536]{1,0:T(8,128)(2,1)S(1)} %convert_element_type.377), channel_id=1, source_target_pairs={{0,2},{1,3},{2,0},{3,1},{4,6},{5,7},{6,4},{7,5},{8,10},{9,11},{10,... | collective-permute-start | bytes 2359304 | tf_op jit(solution)/shard_map/ppermute | solution.py:252
  22.7 56.3 %collective-permute-start.6 = (bf16[256,1536]{1,0:T(8,128)(2,1)S(1)}, bf16[256,1536]{1,0:T(8,128)(2,1)S(1)}, u32[]{:S(2)}, u32[]{:S(2)}) collective-permute-start(bf16[256,1536]{1,0:T(8,128)(2,1)S(1)} %convert_element_type.377), channel_id=1, source_target_pairs={{0,3},{1,0},{2,1},{3,2},{4,7},{5,4},{6,5},{7,6},{8,11},{9,8},{10,9... | collective-permute-start | bytes 2359304 | tf_op jit(solution)/shard_map/ppermute | solution.py:252
  84.3 22.8 %collective-permute-start.14 = (bf16[1792,128]{1,0:T(8,128)(2,1)S(1)}, bf16[1792,128]{1,0:T(8,128)(2,1)S(1)}, u32[]{:S(2)}, u32[]{:S(2)}) collective-permute-start(bf16[1792,128]{1,0:T(8,128)(2,1)S(1)} %get-tuple-element.240), channel_id=1, source_target_pairs={{0,3},{1,0},{2,1},{3,2},{4,7},{5,4},{6,5},{7,6},{8,11},{9,8},{10,9... | collective-permute-start | bytes 1376264 | tf_op jit(solution)/shard_map/ppermute | solution.py:282
  96.0 40.3 %collective-permute-start.13 = (bf16[1792,128]{1,0:T(8,128)(2,1)S(1)}, bf16[1792,128]{1,0:T(8,128)(2,1)S(1)}, u32[]{:S(2)}, u32[]{:S(2)}) collective-permute-start(bf16[1792,128]{1,0:T(8,128)(2,1)S(1)} %get-tuple-element.241), channel_id=1, source_target_pairs={{0,2},{1,3},{2,0},{3,1},{4,6},{5,7},{6,4},{7,5},{8,10},{9,11},{10,... | collective-permute-start | bytes 1376264 | tf_op jit(solution)/shard_map/ppermute | solution.py:282
  96.5 39.9 %collective-permute-start.12 = (bf16[1792,128]{1,0:T(8,128)(2,1)S(1)}, bf16[1792,128]{1,0:T(8,128)(2,1)S(1)}, u32[]{:S(2)}, u32[]{:S(2)}) collective-permute-start(bf16[1792,128]{1,0:T(8,128)(2,1)S(1)} %get-tuple-element.242), channel_id=1, source_target_pairs={{0,1},{1,2},{2,3},{3,0},{4,5},{5,6},{6,7},{7,4},{8,9},{9,10},{10,1... | collective-permute-start | bytes 1376264 | tf_op jit(solution)/shard_map/ppermute | solution.py:282
  152.6 34.5 %all-to-all-start = ((bf16[8,512,128]{2,1,0:T(8,128)(2,1)}), bf16[8,512,128]{2,1,0:T(8,128)(2,1)S(1)}, u32[]{:S(2)}, u32[]{:S(2)}) async-start(bf16[8,512,128]{2,1,0:T(8,128)(2,1)} %bitcast.17), calls=%async_computation | async-start | bytes 2097152 | tf_op jit(solution)/shard_map/all_to_all | solution.py:810
  156.2 143.3 %sort.9.cloned.1.call-start = ((), (), s32[]{:S(2)}) async-start(), calls=%async_computation.7 | async-start | bytes 196640 | tf_op jit(solution)/shard_map/sort | solution.py:419
  156.8 8.6 collective-permute-start.15
  157.2 29.8 %collective-permute-start.18 = (s32[1,592]{1,0:T(1,128)S(1)}, s32[1,592]{1,0:T(1,128)S(1)}, u32[]{:S(2)}, u32[]{:S(2)}) collective-permute-start(s32[1,592]{1,0:T(1,128)S(1)} %pad_add_fusion.3), channel_id=1, source_target_pairs={{0,0},{1,4},{2,1},{3,5},{4,2},{5,6},{6,3},{7,7},{8,8},{9,12},{10,9... | collective-permute-start | bytes 7112 | tf_op jit(solution)/shard_map/ppermute | solution.py:366
  160.6 84.1 %copy-start.57 = (f32[1,1024]{1,0:T(1,128)}, f32[1,1024]{1,0:T(1,128)S(1)}, u32[]{:S(2)}) copy-start(f32[1,1024]{1,0:T(1,128)S(1)} %get-tuple-element.235) | copy-start | bytes 12292
  166.8 15.3 %collective-permute-start.16 = (f32[]{:T(128)}, f32[]{:T(128)}, u32[]{:S(2)}, u32[]{:S(2)}) collective-permute-start(f32[]{:T(128)} %add.750), channel_id=1, source_target_pairs={{0,8},{4,12},{8,0},{12,4},{16,24},{20,28},{24,16},{28,20},{1,9},{5... | collective-permute-start | bytes 20 | tf_op jit(solution)/shard_map/ppermute | solution.py:242
  182.7 3.6 collective-permute-start.17
  287.7 102.5 %all-gather.6.cloned.1.call-start = ((), (), s32[]{:S(2)}) async-start(), calls=%async_computation.4 | async-start | bytes 17584128 | tf_op jit(solution)/shard_map/all_gather | solution.py:829
  288.4 538.3 %reduce-scatter.2.cloned.1.call-start = ((), (), s32[]{:S(2)}) async-start(), calls=%async_computation.5 | async-start | bytes 17584128 | tf_op jit(solution)/shard_map/reduce_scatter | solution.py:866
  290.3 16.0 %collective-permute-start.21 = (bf16[80,1024]{1,0:T(8,128)(2,1)S(1)}, bf16[80,1024]{1,0:T(8,128)(2,1)S(1)}, u32[]{:S(2)}, u32[]{:S(2)}) collective-permute-start(bf16[80,1024]{1,0:T(8,128)(2,1)S(1)} %select_convert_fusion), channel_id=1, source_target_pairs={{0,1},{1,2},{2,3},{3,0},{4,5},{5,6},{6,7},{7,4},{8,9},{9,10},{10,1... | collective-permute-start | bytes 491528 | tf_op jit(solution)/shard_map/ppermute | solution.py:252
  291.8 13.8 %collective-permute-start.20 = (bf16[80,1024]{1,0:T(8,128)(2,1)S(1)}, bf16[80,1024]{1,0:T(8,128)(2,1)S(1)}, u32[]{:S(2)}, u32[]{:S(2)}) collective-permute-start(bf16[80,1024]{1,0:T(8,128)(2,1)S(1)} %select_convert_fusion), channel_id=1, source_target_pairs={{0,2},{1,3},{2,0},{3,1},{4,6},{5,7},{6,4},{7,5},{8,10},{9,11},{10,... | collective-permute-start | bytes 491528 | tf_op jit(solution)/shard_map/ppermute | solution.py:252
  294.2 8.5 collective-permute-start.19
  407.9 7.6 collective-permute-start.24
  409.4 6.0 collective-permute-start.23
  411.8 3.6 collective-permute-start.22
  426.8 21.6 %collective-permute-start.25 = (bf16[80,1024]{1,0:T(8,128)(2,1)}, bf16[80,1024]{1,0:T(8,128)(2,1)}, u32[]{:S(2)}, u32[]{:S(2)}) collective-permute-start(bf16[80,1024]{1,0:T(8,128)(2,1)} %get-tuple-element.246), channel_id=1, source_target_pairs={{0,1},{1,2},{2,3},{3,0},{4,5},{5,6},{6,7},{7,4},{8,9},{9,10},{10,1... | collective-permute-start | bytes 491528 | tf_op jit(solution)/shard_map/ppermute | solution.py:269
  427.2 21.1 %collective-permute-start.27 = (bf16[80,1024]{1,0:T(8,128)(2,1)}, bf16[80,1024]{1,0:T(8,128)(2,1)}, u32[]{:S(2)}, u32[]{:S(2)}) collective-permute-start(bf16[80,1024]{1,0:T(8,128)(2,1)} %get-tuple-element.247), channel_id=1, source_target_pairs={{0,3},{1,0},{2,1},{3,2},{4,7},{5,4},{6,5},{7,6},{8,11},{9,8},{10,9... | collective-permute-start | bytes 491528 | tf_op jit(solution)/shard_map/ppermute | solution.py:269
  430.6 17.8 %collective-permute-start.26 = (bf16[80,1024]{1,0:T(8,128)(2,1)}, bf16[80,1024]{1,0:T(8,128)(2,1)}, u32[]{:S(2)}, u32[]{:S(2)}) collective-permute-start(bf16[80,1024]{1,0:T(8,128)(2,1)} %get-tuple-element.248), channel_id=1, source_target_pairs={{0,2},{1,3},{2,0},{3,1},{4,6},{5,7},{6,4},{7,5},{8,10},{9,11},{10,... | collective-permute-start | bytes 491528 | tf_op jit(solution)/shard_map/ppermute | solution.py:269
  463.8 19.6 %collective-permute-start.28 = (bf16[256,4096]{1,0:T(8,128)(2,1)}, bf16[256,4096]{1,0:T(8,128)(2,1)}, u32[]{:S(2)}, u32[]{:S(2)}) collective-permute-start(bf16[256,4096]{1,0:T(8,128)(2,1)} %convolution_convert_fusion.3), channel_id=1, source_target_pairs={{0,4},{4,0},{8,12},{12,8},{16,20},{20,16},{24,28},{28,24},{1,5},{5... | collective-permute-start | bytes 6291464 | tf_op jit(solution)/shard_map/ppermute | solution.py:295
  463.8 19.6 %collective-permute-start.29 = (bf16[256,4096]{1,0:T(8,128)(2,1)}, bf16[256,4096]{1,0:T(8,128)(2,1)S(1)}, u32[]{:S(2)}, u32[]{:S(2)}) collective-permute-start(bf16[256,4096]{1,0:T(8,128)(2,1)} %convolution_convert_fusion.2), channel_id=1, source_target_pairs={{0,4},{4,0},{8,12},{12,8},{16,20},{20,16},{24,28},{28,24},{1,5},{5... | collective-permute-start | bytes 6291464 | tf_op jit(solution)/shard_map/ppermute | solution.py:296
  486.6 28.4 %collective-permute-start.30 = (bf16[256,4096]{1,0:T(8,128)(2,1)}, bf16[256,4096]{1,0:T(8,128)(2,1)}, u32[]{:S(2)}, u32[]{:S(2)}) collective-permute-start(bf16[256,4096]{1,0:T(8,128)(2,1)} %convolution_convert_fusion.1), channel_id=1, source_target_pairs={{0,4},{4,0},{8,12},{12,8},{16,20},{20,16},{24,28},{28,24},{1,5},{5... | collective-permute-start | bytes 6291464 | tf_op jit(solution)/shard_map/ppermute | solution.py:295
  489.6 25.3 %collective-permute-start.31 = (bf16[256,4096]{1,0:T(8,128)(2,1)}, bf16[256,4096]{1,0:T(8,128)(2,1)}, u32[]{:S(2)}, u32[]{:S(2)}) collective-permute-start(bf16[256,4096]{1,0:T(8,128)(2,1)} %convolution_convert_fusion), channel_id=1, source_target_pairs={{0,4},{4,0},{8,12},{12,8},{16,20},{20,16},{24,28},{28,24},{1,5},{5... | collective-permute-start | bytes 6291464 | tf_op jit(solution)/shard_map/ppermute | solution.py:296
  493.4 48.3 %collective-permute-start.32 = (bf16[256,4096]{1,0:T(8,128)(2,1)}, bf16[256,4096]{1,0:T(8,128)(2,1)}, u32[]{:S(2)}, u32[]{:S(2)}) collective-permute-start(bf16[256,4096]{1,0:T(8,128)(2,1)} %add_convert_fusion.3), channel_id=1, source_target_pairs={{0,1},{1,0},{2,3},{3,2},{4,5},{5,4},{6,7},{7,6},{8,9},{9,8},{10,11... | collective-permute-start | bytes 6291464 | tf_op jit(solution)/shard_map/ppermute | solution.py:321
  542.9 16.8 %collective-permute-start.33 = (bf16[256,4096]{1,0:T(8,128)(2,1)S(1)}, bf16[256,4096]{1,0:T(8,128)(2,1)S(1)}, u32[]{:S(2)}, u32[]{:S(2)}) collective-permute-start(bf16[256,4096]{1,0:T(8,128)(2,1)S(1)} %pad_maximum_fusion.1), channel_id=1, source_target_pairs={{0,4},{4,0},{8,12},{12,8},{16,20},{20,16},{24,28},{28,24},{1,5},{5... | collective-permute-start | bytes 6291464 | tf_op jit(solution)/shard_map/ppermute | solution.py:295
  544.3 15.5 %collective-permute-start.34 = (bf16[256,4096]{1,0:T(8,128)(2,1)S(1)}, bf16[256,4096]{1,0:T(8,128)(2,1)S(1)}, u32[]{:S(2)}, u32[]{:S(2)}) collective-permute-start(bf16[256,4096]{1,0:T(8,128)(2,1)S(1)} %pad_maximum_fusion.2), channel_id=1, source_target_pairs={{0,4},{4,0},{8,12},{12,8},{16,20},{20,16},{24,28},{28,24},{1,5},{5... | collective-permute-start | bytes 6291464 | tf_op jit(solution)/shard_map/ppermute | solution.py:296
  556.4 71.2 %collective-permute-start.41 = (bf16[256,4096]{1,0:T(8,128)(2,1)}, bf16[256,4096]{1,0:T(8,128)(2,1)}, u32[]{:S(2)}, u32[]{:S(2)}) collective-permute-start(bf16[256,4096]{1,0:T(8,128)(2,1)} %fusion.24), channel_id=1, source_target_pairs={{0,1},{1,0},{2,3},{3,2},{4,5},{5,4},{6,7},{7,6},{8,9},{9,8},{10,11... | collective-permute-start | bytes 6291464 | tf_op jit(solution)/shard_map/ppermute | solution.py:321
  571.4 6.4 collective-permute-start.36
  577.5 106.9 %collective-permute-start.35 = (bf16[256,4096]{1,0:T(8,128)(2,1)}, bf16[256,4096]{1,0:T(8,128)(2,1)}, u32[]{:S(2)}, u32[]{:S(2)}) collective-permute-start(bf16[256,4096]{1,0:T(8,128)(2,1)} %pad_maximum_fusion.3), channel_id=1, source_target_pairs={{0,1},{1,0},{2,3},{3,2},{4,5},{5,4},{6,7},{7,6},{8,9},{9,8},{10,11... | collective-permute-start | bytes 6291464 | tf_op jit(solution)/shard_map/ppermute | solution.py:321
  579.7 14.0 %collective-permute-start.37 = (bf16[528,256]{1,0:T(8,128)(2,1)}, bf16[528,256]{1,0:T(8,128)(2,1)S(1)}, u32[]{:S(2)}, u32[]{:S(2)}) collective-permute-start(bf16[528,256]{1,0:T(8,128)(2,1)} %dynamic-slice_convert_fusion.2), channel_id=1, source_target_pairs={{0,8},{4,12},{8,0},{12,4},{16,24},{20,28},{24,16},{28,20},{1,9},{5... | collective-permute-start | bytes 811016 | tf_op jit(solution)/shard_map/ppermute | solution.py:745
  585.7 105.9 %collective-permute-start.40 = (bf16[256,4096]{1,0:T(8,128)(2,1)}, bf16[256,4096]{1,0:T(8,128)(2,1)}, u32[]{:S(2)}, u32[]{:S(2)}) collective-permute-start(bf16[256,4096]{1,0:T(8,128)(2,1)} %add_convert_fusion.2), channel_id=1, source_target_pairs={{2,4},{3,5},{4,2},{5,3},{10,12},{11,13},{12,10},{13,11},{18,20},{1... | collective-permute-start | bytes 6291464 | tf_op jit(solution)/shard_map/ppermute | solution.py:344
  588.9 47.3 %all-to-all-start.1 = ((bf16[8,512,128]{2,1,0:T(8,128)(2,1)}), bf16[8,512,128]{2,1,0:T(8,128)(2,1)}, u32[]{:S(2)}, u32[]{:S(2)}) async-start(bf16[8,512,128]{2,1,0:T(8,128)(2,1)} %bitcast.262), calls=%async_computation.1 | async-start | bytes 2097152 | tf_op jit(solution)/shard_map/all_to_all | solution.py:886
  593.6 412.2 %all-gather.8.cloned.1.call-start = ((), (), s32[]{:S(2)}) async-start(), calls=%async_computation.6 | async-start | bytes 7077888 | tf_op jit(solution)/shard_map/all_gather | solution.py:949
  594.8 41.3 %collective-permute-start.38 = (bf16[528,128]{1,0:T(8,128)(2,1)S(1)}, bf16[528,128]{1,0:T(8,128)(2,1)S(1)}, u32[]{:S(2)}, u32[]{:S(2)}) collective-permute-start(bf16[528,128]{1,0:T(8,128)(2,1)S(1)} %dynamic-slice_convert_fusion.6), channel_id=1, source_target_pairs={{0,16},{4,20},{8,24},{12,28},{16,0},{20,4},{24,8},{28,12},{1,17},{... | collective-permute-start | bytes 405512 | tf_op jit(solution)/shard_map/ppermute | solution.py:745
  634.1 74.5 %collective-permute-start.42 = (bf16[256,4096]{1,0:T(8,128)(2,1)}, bf16[256,4096]{1,0:T(8,128)(2,1)}, u32[]{:S(2)}, u32[]{:S(2)}) collective-permute-start(bf16[256,4096]{1,0:T(8,128)(2,1)} %fusion.23), channel_id=1, source_target_pairs={{2,4},{3,5},{4,2},{5,3},{10,12},{11,13},{12,10},{13,11},{18,20},{1... | collective-permute-start | bytes 6291464 | tf_op jit(solution)/shard_map/ppermute | solution.py:344
  689.6 135.5 %collective-permute-start.39 = (bf16[256,4096]{1,0:T(8,128)(2,1)S(1)}, bf16[256,4096]{1,0:T(8,128)(2,1)}, u32[]{:S(2)}, u32[]{:S(2)}) collective-permute-start(bf16[256,4096]{1,0:T(8,128)(2,1)S(1)} %pad_maximum_fusion.4), channel_id=1, source_target_pairs={{2,4},{3,5},{4,2},{5,3},{10,12},{11,13},{12,10},{13,11},{18,20},{1... | collective-permute-start | bytes 6291464 | tf_op jit(solution)/shard_map/ppermute | solution.py:344
  704.3 22.6 %collective-permute-start.45 = (bf16[2320,128]{1,0:T(8,128)(2,1)S(1)}, bf16[2320,128]{1,0:T(8,128)(2,1)S(1)}, u32[]{:S(2)}, u32[]{:S(2)}) collective-permute-start(bf16[2320,128]{1,0:T(8,128)(2,1)S(1)} %get-tuple-element.222), channel_id=1, source_target_pairs={{0,3},{1,0},{2,1},{3,2},{4,7},{5,4},{6,5},{7,6},{8,11},{9,8},{10,9... | collective-permute-start | bytes 1781768 | tf_op jit(solution)/shard_map/ppermute | solution.py:282
  705.5 45.4 %collective-permute-start.43 = (bf16[2320,128]{1,0:T(8,128)(2,1)S(1)}, bf16[2320,128]{1,0:T(8,128)(2,1)S(1)}, u32[]{:S(2)}, u32[]{:S(2)}) collective-permute-start(bf16[2320,128]{1,0:T(8,128)(2,1)S(1)} %get-tuple-element.224), channel_id=1, source_target_pairs={{0,1},{1,2},{2,3},{3,0},{4,5},{5,6},{6,7},{7,4},{8,9},{9,10},{10,1... | collective-permute-start | bytes 1781768 | tf_op jit(solution)/shard_map/ppermute | solution.py:282
  706.4 97.3 %copy-start.56 = (s32[4,4096]{1,0:T(4,128)S(1)}, s32[4,4096]{1,0:T(4,128)}, u32[]{:S(2)}) copy-start(s32[4,4096]{1,0:T(4,128)} %fusion.103) | copy-start | bytes 196612
  706.4 96.5 %collective-permute-start.44 = (bf16[2320,128]{1,0:T(8,128)(2,1)S(1)}, bf16[2320,128]{1,0:T(8,128)(2,1)S(1)}, u32[]{:S(2)}, u32[]{:S(2)}) collective-permute-start(bf16[2320,128]{1,0:T(8,128)(2,1)S(1)} %get-tuple-element.225), channel_id=1, source_target_pairs={{0,2},{1,3},{2,0},{3,1},{4,6},{5,7},{6,4},{7,5},{8,10},{9,11},{10,... | collective-permute-start | bytes 1781768 | tf_op jit(solution)/shard_map/ppermute | solution.py:282
  892.5 6.0 collective-permute-start.46
  902.0 12.2 %collective-permute-start.48 = (bf16[128,1536]{1,0:T(8,128)(2,1)}, bf16[128,1536]{1,0:T(8,128)(2,1)}, u32[]{:S(2)}, u32[]{:S(2)}) collective-permute-start(bf16[128,1536]{1,0:T(8,128)(2,1)} %get-tuple-element.215), channel_id=1, source_target_pairs={{0,8},{4,12},{8,0},{12,4},{16,24},{20,28},{24,16},{28,20},{1,9},{5... | collective-permute-start | bytes 1179656 | tf_op jit(solution)/shard_map/ppermute | solution.py:710
  904.0 23.0 %collective-permute-start.47 = (bf16[128,1536]{1,0:T(8,128)(2,1)}, bf16[128,1536]{1,0:T(8,128)(2,1)S(1)}, u32[]{:S(2)}, u32[]{:S(2)}) collective-permute-start(bf16[128,1536]{1,0:T(8,128)(2,1)} %get-tuple-element.214), channel_id=1, source_target_pairs={{0,8},{4,12},{8,0},{12,4},{16,24},{20,28},{24,16},{28,20},{1,9},{5... | collective-permute-start | bytes 1179656 | tf_op jit(solution)/shard_map/ppermute | solution.py:710
  904.2 29.0 %collective-permute-start.50 = (bf16[128,1536]{1,0:T(8,128)(2,1)S(1)}, bf16[128,1536]{1,0:T(8,128)(2,1)S(1)}, u32[]{:S(2)}, u32[]{:S(2)}) collective-permute-start(bf16[128,1536]{1,0:T(8,128)(2,1)S(1)} %get-tuple-element.220), channel_id=1, source_target_pairs={{0,16},{4,20},{8,24},{12,28},{16,0},{20,4},{24,8},{28,12},{1,17},{... | collective-permute-start | bytes 1179656 | tf_op jit(solution)/shard_map/ppermute | solution.py:710
  906.2 18.5 %collective-permute-start.51 = (bf16[128,1536]{1,0:T(8,128)(2,1)S(1)}, bf16[128,1536]{1,0:T(8,128)(2,1)S(1)}, u32[]{:S(2)}, u32[]{:S(2)}) collective-permute-start(bf16[128,1536]{1,0:T(8,128)(2,1)S(1)} %get-tuple-element.221), channel_id=1, source_target_pairs={{0,16},{4,20},{8,24},{12,28},{16,0},{20,4},{24,8},{28,12},{1,17},{... | collective-permute-start | bytes 1179656 | tf_op jit(solution)/shard_map/ppermute | solution.py:710
  915.5 16.5 %collective-permute-start.49 = (bf16[128,1536]{1,0:T(8,128)(2,1)S(1)}, bf16[128,1536]{1,0:T(8,128)(2,1)S(1)}, u32[]{:S(2)}, u32[]{:S(2)}) collective-permute-start(bf16[128,1536]{1,0:T(8,128)(2,1)S(1)} %fusion.56), channel_id=1, source_target_pairs={{0,16},{4,20},{8,24},{12,28},{16,0},{20,4},{24,8},{28,12},{1,17},{... | collective-permute-start | bytes 1179656 | tf_op jit(solution)/shard_map/ppermute | solution.py:710
  924.9 8.9 collective-permute-start.52
  941.5 5.1 collective-permute-start.58
  946.8 11.0 %collective-permute-start.59 = (bf16[528,256]{1,0:T(8,128)(2,1)S(1)}, bf16[528,256]{1,0:T(8,128)(2,1)S(1)}, u32[]{:S(2)}, u32[]{:S(2)}) collective-permute-start(bf16[528,256]{1,0:T(8,128)(2,1)S(1)} %pad_maximum_fusion.7), channel_id=1, source_target_pairs={{0,8},{4,12},{8,0},{12,4},{16,24},{20,28},{24,16},{28,20},{1,9},{5... | collective-permute-start | bytes 811016 | tf_op jit(solution)/shard_map/ppermute | solution.py:759
  958.0 2.1 collective-permute-start.60
  968.6 1.1 collective-permute-start.53
  969.7 3.9 collective-permute-start.54
  973.6 3.5 collective-permute-start.55
  977.1 4.6 collective-permute-start.56
  981.7 4.4 collective-permute-start.57
  (92 other events, 1086.4 us)
Sparse Core Ops, SparseCore 0:
  81.5 144.9 all-gather.3
  287.8 11.3 sort.11.cloned.1.call-done
  302.0 88.0 all-gather.5
  450.4 113.4 reduce-scatter.1
  940.4 48.0 all-gather.7
  (1 shorter events, 0.0 us)

commit v8 on v5

--- a/solution.py
+++ b/solution.py
@@ -153,10 +153,8 @@
     return (peak, total, first[2] + second[2])
 
 
-def layer_forward(embedded, docs, small, weights):
+def layer_forward(embedded, x0, act, docs, small, weights):
     base = L + 2
-    x0 = norm_rows(embedded, small[base], small[base + 1])
-    act = x0.astype(jnp.bfloat16)
     bias = jnp.concatenate([small[base + 6], jnp.zeros((D,), jnp.float32), small[base + 7]])
     qkv = (matmul(act, weights[:, 0 : 3 * D]) + bias).astype(jnp.bfloat16)
     out, lse = attend(qkv, docs)
@@ -181,7 +179,7 @@
     _, pull = jax.vjp(gelu_exact, upper)
     dupper = pull(dgated)[0].astype(jnp.bfloat16)
     dupper = down.received(dupper)
-    down.across()
+    dupper = down.across(dupper)
     up = WorkerPiece((fin, dupper))
     dhone = drtwo + matmul_nt(dupper, weights[:, 4 * D : 4 * D + FF])
     _, pull = jax.vjp(norm_rows, rone, small[base + 2], small[base + 3])
@@ -189,18 +187,16 @@
     dattn = drone.astype(jnp.bfloat16)
     dout = matmul_nt(dattn, weights[:, 3 * D : 4 * D]).astype(jnp.bfloat16)
     dout = up.received(dout)
-    up.across()
+    dout = up.across(dout)
     dqkv = attend_back(qkv, dout, lse, docs)
     (dqkv,) = down.crossed(dqkv)
     down.finish()
     mixed = WorkerPiece((act, dqkv), (out, dattn))
-    dxzero = drone + matmul_nt(dqkv, weights[:, 0 : 3 * D])
+    dxzero = drone + matmul_nt(mixed.across(dqkv), weights[:, 0 : 3 * D])
     _, pull = jax.vjp(norm_rows, embedded, small[base], small[base + 1])
     dembed, dgain_emb, dshift_emb = pull(dxzero)
-    dembed = mixed.received(dembed)
-    dembed, mixed.far = up.crossed(dembed, mixed.far) if up.paired else (dembed, None)
+    (dembed,) = up.crossed(dembed)
     up.finish()
-    mixed.across()
     bias_qkv = jnp.sum(dqkv, axis=0, dtype=jnp.float32)
     vectors = jnp.stack(
         [
@@ -281,8 +277,55 @@
     def block(by):
         return lax.dynamic_index_in_dim(blocks, lax.rem(place + by, size), 0, keepdims=False)
 
-    moved = [lax.ppermute(block(by), "narrow", cycle(size, by)) for by in range(1, size)]
-    return jnp.stack([block(0)] + moved)
+    return [block(0)] + [
+        lax.ppermute(block(by), "narrow", cycle(size, by)) for by in range(1, size)
+    ]
+
+
+def block_kernel(steps, place_ref, *refs):
+    pairs = len(steps) - 1
+    lefts, rights, terms, out_ref = refs[:pairs], refs[pairs : 2 * pairs], refs[2 * pairs : -1], refs[-1]
+    step = pl.program_id(0)
+    for index in range(pairs):
+
+        @pl.when((step >= steps[index]) & (step < steps[index + 1]))
+        def _():
+            total = matmul_tn(lefts[index][...], rights[index][...])
+            for term_ref in terms:
+                total = total + term_ref[...].astype(jnp.float32)
+            out_ref[...] = total.astype(jnp.bfloat16)
+
+
+def gradient_block(pairs, place, terms):
+    block = D
+    size = D // lax.axis_size("narrow")
+    steps = [0]
+    for _, right in pairs:
+        steps.append(steps[-1] + right.shape[1] // block)
+    tokens = pairs[0][0].shape[0]
+
+    def right_of(index):
+        low, count = steps[index], steps[index + 1] - steps[index]
+        return pl.BlockSpec(
+            (tokens, block), lambda step, place: (0, jnp.clip(step - low, 0, count - 1))
+        )
+
+    piece = pl.BlockSpec((size, block), lambda step, place: (0, step))
+    return pl.pallas_call(
+        functools.partial(block_kernel, steps),
+        grid_spec=pltpu.PrefetchScalarGridSpec(
+            num_scalar_prefetch=1,
+            grid=(steps[-1],),
+            in_specs=[pl.BlockSpec((tokens, size), lambda step, place: (0, place[0]))] * len(pairs)
+            + [right_of(index) for index in range(len(pairs))]
+            + [piece] * len(terms),
+            out_specs=piece,
+        ),
+        out_shape=jax.ShapeDtypeStruct((size, steps[-1] * block), jnp.bfloat16),
+        compiler_params=pltpu.CompilerParams(vmem_limit_bytes=24 * 2**20),
+        cost_estimate=FREE,
+        name="gradient_block",
+    )(place[None], *[left for left, _ in pairs], *[right for _, right in pairs], *terms)
 
 
 class WorkerPiece:
@@ -298,39 +341,32 @@
         self.near = lax.ppermute(self.block(1 - self.core, self.side), "wide", cores)
 
     def block(self, core, side, *terms):
-        rows = D // lax.axis_size("narrow")
-        blocks, start = [], 0
-        for left, right in self.pairs:
-            part = lax.dynamic_slice_in_dim(left, (2 * core + side) * rows, rows, 1)
-            total = matmul_tn(part, right)
-            for term in terms:
-                total = total + term[:, start : start + right.shape[1]].astype(jnp.float32)
-            blocks.append(total.astype(jnp.bfloat16))
-            start += right.shape[1]
-        return blocks[0] if len(blocks) == 1 else jnp.concatenate(blocks, axis=1)
+        return gradient_block(self.pairs, 2 * core + side, terms)
 
     def received(self, value):
         if self.paired:
             value, self.far, self.near = together(value, self.far, self.near)
         return value
 
-    def across(self):
+    def across(self, value):
         if self.paired:
             sides = swap_pairs(lax.axis_size("narrow"), 1)
             away = self.block(self.core, 1 - self.side, self.far)
+            away, value = together(away, value)
             self.away = lax.ppermute(away, "narrow", sides)
+        return value
 
     def crossed(self, *values):
         if self.paired:
             *values, self.away = together(*values, self.away)
         return values
 
-    def finish(self):
+    def finish(self, *values):
         if not self.paired:
             blocks = [matmul_tn(left, right).astype(jnp.bfloat16) for left, right in self.pairs]
             grad = jnp.concatenate(blocks, axis=1)
             self.result = lax.psum_scatter(grad, "narrow", scatter_dimension=0, tiled=True)
-            return
+            return values
         n_wide, n_narrow = lax.axis_size("wide"), lax.axis_size("narrow")
         total = self.block(self.core, self.side, self.near, self.away)
         moves = []
@@ -340,8 +376,10 @@
                     target_wide = wide - wide % 2 + narrow // 2
                     target = target_wide * n_narrow + 2 * (wide % 2) + narrow % 2
                     moves.append((wide * n_narrow + narrow, target))
+        total, *values = together(total, *values)
         moved = lax.ppermute(total, ("wide", "narrow"), moves)
         self.result = jnp.where(self.pair == self.core, total, moved)
+        return values
 
 
 def hosted_rows(token_ids, mlm_labels, mlm_valid, doc_ids, mlm_pos):
@@ -405,13 +443,6 @@
     def behind_slots(self, room):
         return self.behind * room + jnp.minimum(self.rank, room - 1)
 
-    def packed(self, slots):
-        base = self.vshard + 1
-        order = jnp.arange(self.count) * base + slots
-        order = jnp.where(slots < self.vshard, order, order + self.count * base)
-        order = lax.sort(order)
-        return order % base, order // base % self.count
-
 
 def pack_kernel(ids_ref, table_ref, out_ref, held, *rows):
     step, count, size = pl.program_id(0), out_ref.shape[1], table_ref.shape[0]
@@ -491,19 +522,18 @@
     )(ids, table)
 
 
-def add_kernel(length, ids_ref, from_ref, rows_ref, out_ref, rows, *sums):
-    size, each = out_ref.shape[0], rows_ref.shape[1]
+def add_kernel(ids_ref, values_ref, out_ref, rows, *sums):
+    size, length = out_ref.shape[0], rows.shape[1]
     for part in sums:
         part[...] = jnp.zeros_like(part)
-    rows[...] = rows_ref[...].astype(jnp.float32)
+    rows[...] = values_ref[:, 0:length, :].astype(jnp.float32)
 
     @pl.loop(0, length, step=8)
     def _(first):
         for by in range(8):
             for index, part in enumerate(sums):
-                place = ids_ref[index * each + first + by]
-                row = from_ref[index * each + first + by]
-                part[pl.ds(place, 1), :] += rows[index, pl.ds(row, 1), :]
+                place = ids_ref[index * length + first + by]
+                part[pl.ds(place, 1), :] += rows[index, pl.ds(first + by, 1), :]
 
     total = sums[0][0:size, :]
     for part in sums[1:]:
@@ -511,23 +541,24 @@
     out_ref[...] = total
 
 
-def added_rows(ids, rows, values, size, length):
-    places, count, cols = values.shape
+def added_rows(ids, values, size):
+    places, length = ids.shape
+    cols = values.shape[2]
     return pl.pallas_call(
-        functools.partial(add_kernel, length),
+        add_kernel,
         grid_spec=pltpu.PrefetchScalarGridSpec(
-            num_scalar_prefetch=2,
+            num_scalar_prefetch=1,
             grid=(1,),
-            in_specs=[pl.BlockSpec(values.shape, lambda step, ids, rows: (0, 0, 0))],
-            out_specs=pl.BlockSpec((size, cols), lambda step, ids, rows: (0, 0)),
-            scratch_shapes=[pltpu.VMEM(values.shape, jnp.float32)]
+            in_specs=[pl.BlockSpec(values.shape, lambda step, ids: (0, 0, 0))],
+            out_specs=pl.BlockSpec((size, cols), lambda step, ids: (0, 0)),
+            scratch_shapes=[pltpu.VMEM((places, length, cols), jnp.float32)]
             + [pltpu.VMEM((size + 8, cols), jnp.float32)] * places,
         ),
         out_shape=jax.ShapeDtypeStruct((size, cols), jnp.float32),
         compiler_params=pltpu.CompilerParams(vmem_limit_bytes=56 * 2**20),
-        cost_estimate=pl.CostEstimate(flops=0, bytes_accessed=5 * 10**7, transcendentals=0),
+        cost_estimate=FREE,
         name="add_rows",
-    )(ids.reshape(-1), rows.reshape(-1), values)
+    )(ids.reshape(-1), values)
 
 
 def span_kernel(momentum_ref, grad_ref, error_ref, span_ref, sum_ref):
@@ -562,7 +593,7 @@
             jax.ShapeDtypeStruct((rows, cols), jnp.float32),
             jax.ShapeDtypeStruct((1, block), jnp.float32),
         ],
-        compiler_params=pltpu.CompilerParams(vmem_limit_bytes=24 * 2**20),
+        compiler_params=pltpu.CompilerParams(vmem_limit_bytes=60 * 2**20),
         cost_estimate=FREE,
         name="span",
     )(momentum, grad, error)
@@ -609,7 +640,7 @@
             jax.ShapeDtypeStruct((1, rows, cols), jnp.float32),
             jax.ShapeDtypeStruct((parts, rows, cols // parts), jnp.bfloat16),
         ],
-        compiler_params=pltpu.CompilerParams(vmem_limit_bytes=24 * 2**20),
+        compiler_params=pltpu.CompilerParams(vmem_limit_bytes=60 * 2**20),
         cost_estimate=FREE,
         name="press",
     )(jnp.stack([scale, 1.0 / scale]), *spans)
@@ -693,7 +724,7 @@
 
 def small_halved(value):
     n_wide = lax.axis_size("wide")
-    for bit, place in zip((1, 2, 4), wide_places()):
+    for bit, place in list(zip((1, 2, 4), wide_places()))[::-1]:
         half = value.shape[1] // 2
         give = lax.dynamic_slice_in_dim(value, (1 - place) * half, half, 1).astype(jnp.bfloat16)
         keep = lax.dynamic_slice_in_dim(value, place * half, half, 1)
@@ -701,20 +732,9 @@
     return value
 
 
-def small_total(value):
-    n_wide, n_narrow = lax.axis_size("wide"), lax.axis_size("narrow")
-    bit = 1
-    while bit < n_narrow:
-        low = value.astype(jnp.bfloat16)
-        other = lax.ppermute(low, "narrow", swap_pairs(n_narrow, bit))
-        value = low.astype(jnp.float32) + other.astype(jnp.float32)
-        bit *= 2
-    value = value.astype(jnp.bfloat16)
-    for bit, place in reversed(list(zip((1, 2, 4), wide_places()))):
-        other = lax.ppermute(value, "wide", swap_pairs(n_wide, bit))
-        first, second = jnp.where(place == 0, value, other), jnp.where(place == 0, other, value)
-        value = jnp.concatenate([first, second], axis=1)
-    return value.astype(jnp.float32)
+def small_update(grad, first, second, weight):
+    first = BETA * first + (1.0 - BETA) * grad.astype(jnp.float32)
+    return first, first / (jnp.sqrt(second) + OPT_EPS) + DECAY * weight
 
 
 def shards(
@@ -757,19 +777,14 @@
 
         def looked_up(room):
             rows = sent_around(picked[:, 0:room])
-            return taken_rows(owners.behind_slots(room), rows.reshape(n_narrow * room, -1))
+            return taken_rows(owners.behind_slots(room), jnp.concatenate(rows, axis=0))
 
         layer_rows, picked = together(layer_rows, picked)
         looked = looked_up(owners.room)
         looked = lax.cond(owners.full, lambda: looked_up(owners.count), lambda: looked)
         looked = lax.all_to_all(looked.reshape(n_wide, L, -1), "wide", 0, 0)
         looked = looked.transpose(1, 0, 2).reshape(1, L, D)
-        looked, slots = together(looked, owners.slots)
-        packed_ids, packed_rows_at = owners.packed(slots)
-        table_low, weights, looked, packed_ids, packed_rows_at = together(
-            table_low, weights, looked, packed_ids, packed_rows_at
-        )
-        table_cols = lax.all_gather(table_low, "wide", axis=1, tiled=True)
+        looked, count, doc_ids, mlm_pos = together(looked, count, doc_ids, mlm_pos)
     else:
         local_ids = token_ids - narrow_me * vshard
         inside = (local_ids >= 0) & (local_ids < vshard)
@@ -781,7 +796,13 @@
     looked = looked.astype(jnp.float32)
     even_doc = (doc_ids % 2 == 0)[..., None]
     embedded = looked + small[0:L][None] + jnp.where(even_doc, small[L], small[L + 1])
-    htwo, kept = layer_forward(embedded.reshape(seqs * L, D), doc_ids, small, weights)
+    embedded = embedded.reshape(seqs * L, D)
+    x0 = norm_rows(embedded, small[L + 2], small[L + 3])
+    act = x0.astype(jnp.bfloat16)
+    if paired:
+        table_low, weights, act = together(table_low, weights, act)
+        table_cols = lax.all_gather(table_low, "wide", axis=1, tiled=True)
+    htwo, kept = layer_forward(embedded, x0, act, doc_ids, small, weights)
     hmask = jnp.take_along_axis(htwo.reshape(seqs, L, D), mlm_pos[..., None], axis=1)
     hmask = hmask.reshape(seqs * MPS, D).astype(jnp.bfloat16)
     if paired:
@@ -836,13 +857,13 @@
     if paired:
         cut = dembed.astype(jnp.bfloat16).reshape(L, n_wide, D // n_wide).transpose(1, 0, 2)
         cut = lax.all_to_all(cut, "wide", 0, 0).reshape(n_wide * L, D // n_wide)
-        small_grad = small_total(small_halved(small_grad))
+        halved = small_halved(small_grad).astype(jnp.bfloat16)
         down, up = pieces[2], pieces[1]
-        cut, mixed.away, small_grad, down.result, up.result, table_head = together(
-            cut, mixed.away, small_grad, down.result, up.result, table_head
+        cut, mixed.away, halved, down.result, up.result, table_head = together(
+            cut, mixed.away, halved, down.result, up.result, table_head
         )
         mixed.finish()
-        cut, mixed.result = together(cut, mixed.result)
+        cut, mixed.result = together(jnp.concatenate([cut, halved]), mixed.result)
         group_rows = lax.all_gather(cut, "narrow", axis=0)
     else:
         mixed.finish()
@@ -878,25 +899,30 @@
     server_low = server_out.astype(jnp.bfloat16)
     if paired:
         server_low, group_rows = together(server_low, group_rows)
-
-        def added(length):
-            return added_rows(packed_ids, packed_rows_at, group_rows, vshard, length)
-
-        table_grad = lax.cond(
-            owners.full, lambda: added(owners.count), lambda: added(owners.room)
-        )
+        table_grad = added_rows(owners.slots, group_rows, vshard)
         table_mom, table_upd, table_norms = table_update(
             table_grad, table_head, table, table_m, table_v
         )
+        eighth = D // n_wide
+        small_grad = jnp.sum(group_rows[:, n_wide * L :].astype(jnp.float32), axis=0)
+        small_grad = small_grad.astype(jnp.bfloat16)
+
+        def own(value):
+            return lax.dynamic_slice_in_dim(value, wide_me * eighth, eighth, 1)
+
+        _, own_upd = small_update(small_grad, own(small_m), own(small_v), own(small))
+        small_norm = jnp.where(narrow_me == 0, jnp.sum(own_upd * own_upd), 0.0)
     else:
         small_grad = lax.psum(small_grad, ("wide", "narrow"))
         table_mom = BETA * table_m + (1.0 - BETA) * table_grad
         table_upd = table_mom / (jnp.sqrt(table_v) + OPT_EPS) + DECAY * table
         table_norms = (jnp.sum(table * table)[None], jnp.sum(table_upd * table_upd)[None])
-    small_mom = BETA * small_m + (1.0 - BETA) * small_grad
-    small_upd = small_mom / (jnp.sqrt(small_v) + OPT_EPS) + DECAY * small
-    small_norms = (jnp.sum(small * small)[None], jnp.sum(small_upd * small_upd)[None])
     new_m = lax.all_gather(server_low, "wide", axis=1, tiled=True).astype(jnp.float32)
+    if paired:
+        small_grad = lax.all_gather(small_grad, "wide", axis=1, tiled=True)
+    small_mom, small_upd = small_update(small_grad, small_m, small_v, small)
+    if not paired:
+        small_norm = jnp.where((wide_me == 0) & (narrow_me == 0), jnp.sum(small_upd * small_upd), 0.0)
     layer_upd = server_out / (jnp.sqrt(layer_v) + OPT_EPS) + DECAY * layer
     column = wide_me * part_cols + jnp.arange(part_cols)
     which = (
@@ -907,11 +933,11 @@
     onehot = (which[:, None] == jnp.arange(4)[None]).astype(jnp.float32)
     wsq = jnp.sum(jnp.sum(layer * layer, axis=0)[:, None] * onehot, axis=0)
     usq = jnp.sum(jnp.sum(layer_upd * layer_upd, axis=0)[:, None] * onehot, axis=0)
-    parts = jnp.concatenate([wsq, usq, *table_norms, jnp.sum(own_loss)[None]])
+    parts = jnp.concatenate([wsq, usq, *table_norms, jnp.sum(own_loss)[None], small_norm[None]])
     sums = summed_over(summed_over(parts, "wide"), "narrow")
     loss_sum = sums[10]
-    wnorm = jnp.sqrt(jnp.concatenate([sums[0:4], sums[8:9], small_norms[0]]))
-    unorm = jnp.sqrt(jnp.concatenate([sums[4:8], sums[9:10], small_norms[1]]))
+    wnorm = jnp.sqrt(jnp.concatenate([sums[0:4], sums[8:9], jnp.sum(small * small)[None]]))
+    unorm = jnp.sqrt(jnp.concatenate([sums[4:8], sums[9:10], sums[11:12]]))
     ratio = wnorm / unorm
     new_layer = layer - RATE * jnp.sum(onehot * ratio[None, 0:4], axis=1)[None] * layer_upd
     new_table = table - RATE * ratio[4] * table_upd

time: 1050 us -> 967 us (0.921)
  waiting for transfers between devices: 411 us -> 305 us
  Pallas kernels: 142 us -> 214 us
  matrix products: 158 us -> 119 us
    all_gather x1, waiting for transfers between devices: 122 us -> 49 us  [shards(): weights = lax.all_gather(layer_rows, 'wide', axis=1, tiled=True)]
    ppermute x5 -> x0, waiting for transfers between devices: 63.2 us -> none  [the longest x2 48.2 us: small_total(): other = lax.ppermute(low, 'narrow', swap_pairs(n_narrow, bit))]
    pallas_call x1 -> x13, Pallas kernels: 18.4 us -> 76.4 us  [the longest x12 40.2 us: gradient_block(): pl.pallas_call(functools.partial(block_kernel, steps), grid_spec=pltpu.Pr...]
    dot_general x16 -> x0, matrix products: 36.4 us -> none  [matmul_tn(): lax.dot_general(left, right, (((0,), (0,)), ((), ())), preferred_element_...]
    ppermute x3, waiting for transfers between devices: 86.4 us -> 109 us  [across(): self.away = lax.ppermute(away, 'narrow', sides)]
    ppermute x5 -> x0, starting transfers between devices: 17.8 us -> none  [the longest x2 15.7 us: small_total(): other = lax.ppermute(low, 'narrow', swap_pairs(n_narrow, bit))]
    all_to_all x1, waiting for transfers between devices: 15.3 us -> 0.01 us  [shards(): looked = lax.all_to_all(looked.reshape(n_wide, L, -1), 'wide', 0, 0)]
    unnamed x223 -> x209, local copies, waits for them, and re-layouts: 43 us -> 41.2 us
  transfers between devices with their start and end apart: 61 -> 57, of which waited for: 33 -> 27; matrix products, arithmetic and copies ran while one was open for 23% -> 23% of each run, Pallas kernels for 11% -> 19%
where the time goes in v8:
time: 967 us; the launch traced here: 959 us
  waiting for transfers between devices  305 us (32%)
  Pallas kernels  214 us (22%)
  matrix products  119 us (12%)
  other arithmetic  113 us (12%)
  starting transfers between devices  101 us (10%)
  local copies, waits for them, and re-layouts  79.8 us (8%)
  between operations  23.9 us (2%)
    ppermute x3, waiting for transfers between devices, across(): self.away = lax.ppermute(away, 'narrow', sides)  109 us
    dot_general x5, matrix products, matmul(): return jnp.dot(left, right, preferred_element_type=jnp.float32)  59.6 us
    pallas_call x1, Pallas kernels, packed_rows(): pl.pallas_call(pack_kernel, grid_spec=pltpu.PrefetchScalarGridSpec(num_sc...  52.4 us
    all_gather x1, waiting for transfers between devices, shards(): weights = lax.all_gather(layer_rows, 'wide', axis=1, tiled=True)  49 us
    dot_general x5, matrix products, matmul_nt(): lax.dot_general(left, right, (((1,), (1,)), ((), ())), preferred_element_...  41.5 us
    unnamed x209, local copies, waits for them, and re-layouts  41.2 us
    all_gather x1, waiting for transfers between devices, shards(): group_rows = lax.all_gather(cut, 'narrow', axis=0)  40.6 us
    pallas_call x12, Pallas kernels, gradient_block(): pl.pallas_call(functools.partial(block_kernel, steps), grid_spec=pltpu.Pr...  40.2 us
  transfers between devices with their start and end apart: 57, of which 27 were waited for; matrix products, arithmetic and copies ran while one was open for 23% of the time, Pallas kernels for 19%

profile of v8, /device:TPU:0, one launch (start us, length us, event | category | flops | bytes accessed | tf_op | source)
XLA Modules:
  0.0 959.5 jit_solution(10621094917347720658)
XLA Ops:
  18.5 3.7 collective-permute-start.6
  25.7 52.4 %pack_rows.1 = bf16[4,4096,128]{2,1,0:T(8,128)(2,1)} custom-call(s32[16384]{0:T(1024)S(1)} %fusion.67.ids_ref, f32[7632,128]{1,0:T(8,128)S(1)} %copy-done.7), custom_call_target="tpu_custom_call" | custom-call | bytes 150000000 | tf_op jit(solution)/shard_map/pack_rows/pallas_call | solution.py:476
  78.1 10.1 %collective-permute-done.7 = bf16[256,1536]{1,0:T(8,128)(2,1)S(1)} collective-permute-done((bf16[256,1536]{1,0:T(8,128)(2,1)S(1)}, bf16[256,1536]{1,0:T(8,128)(2,1)S(1)}, u32[]{:S(2)}, u32[]{:S(2)}) %collective-permute-start.7) | collective-permute-done | bytes 786464 | tf_op jit(solution)/shard_map/ppermute | solution.py:251
  98.4 19.7 %collective-permute-done.10 = bf16[1792,128]{1,0:T(8,128)(2,1)S(1)} collective-permute-done((bf16[1792,128]{1,0:T(8,128)(2,1)S(1)}, bf16[1792,128]{1,0:T(8,128)(2,1)S(1)}, u32[]{:S(2)}, u32[]{:S(2)}) %collective-permute-start.10) | collective-permute-done | bytes 458784 | tf_op jit(solution)/shard_map/ppermute | solution.py:281
  118.1 9.0 collective-permute-done.11
  127.2 5.5 take_rows.3
  132.7 3.3 conditional.1
  137.0 3.6 all-to-all-start
  142.9 4.8 convert_element_type.296
  149.0 14.0 %collective-permute-start.13 = (f32[]{:T(128)}, f32[]{:T(128)}, u32[]{:S(2)}, u32[]{:S(2)}) collective-permute-start(f32[]{:T(128)} %add.629), channel_id=1, source_target_pairs={{0,8},{4,12},{8,0},{12,4},{16,24},{20,28},{24,16},{28,20},{1,9},{5... | collective-permute-start | bytes 20 | tf_op jit(solution)/shard_map/ppermute | solution.py:241
  176.5 49.0 %all-gather.7.cloned.1.call-done = bf16[1024,12288]{1,0:T(8,128)(2,1)} async-done(((bf16[1024,1536]{1,0:T(8,128)(2,1)}), bf16[1024,12288]{1,0:T(8,128)(2,1)}) %all-gather.7.cloned.1.call-update) | async-done | bytes 25165840 | tf_op jit(solution)/shard_map/all_gather | solution.py:775
  230.1 6.4 add_convert_fusion.1.q_ref.k_ref.v_ref
  236.5 11.7 %attend.1 = (bf16[512,1024]{1,0:T(8,128)(2,1)S(1)}, f32[8,2,512]{2,1,0:T(2,128)S(1)}) custom-call(bf16[512,3072]{1,0:T(8,128)(2,1)S(1)} %add_convert_fusion.1.q_ref.k_ref.v_ref, bf16[512,3072]{1,0:T(8,128)(2,1)S(1)} %add_convert_fusion.1.q_ref.k_ref.v_ref, bf16[512,3072]{1,0:T(8,128)(2,1)S(1)} %add_convert_fusion.1.q_ref.k_ref.v_ref, ...), custom_call_target="tpu_custom_call" | custom-call | tf_op jit(solution)/shard_map/attend/pallas_call | solution.py:86
  248.3 3.4 fusion.118
  252.5 26.0 %multiply_convert_fusion = (bf16[512,4096]{1,0:T(8,128)(2,1)S(1)}, f32[512,4096]{1,0:T(8,128)}, f32[512,4096]{1,0:T(8,128)}) fusion(f32[4096]{0:T(1024)S(1)} %bitcast.240, bf16[512,1024]{1,0:T(8,128)(2,1)S(1)} %fusion.33.refs_0_, bf16[1024,12288]{1,0:T(8,128)(2,1)} %all-gather.7.cloned.1.call-done), kind=kOutput, calls=%fused_computation.21 | convolution fusion | flops 4433379328 | bytes 30425088 | tf_op jit(solution)/shard_map/dot_general | solution.py:49
  278.6 9.2 fusion.119
  294.0 3.6 collective-permute-start.17
  303.9 8.7 collective-permute-done.17
  317.9 11.3 %fusion.120 = (f32[320]{0:T(512)S(1)}, f32[320,7632]{1,0:T(8,128)}) fusion(bf16[7632,1024]{1,0:T(8,128)(2,1)} %all-gather.9.cloned.1.call-done, bf16[560,1024]{1,0:T(8,128)(2,1)} %constant_dynamic-update-slice_fusion.7, s32[]{:T(128)S(6)} %select_n.334, pred[7632]{0:T(1024)(128)(4,1)} %broadcast_compare_fusion.1), kind=kOutput, calls=%fused_computation.323 | convolution fusion | flops 5006591488 | bytes 26064132 | tf_op jit(solution)/shard_map/dot_general | solution.py:59
  329.2 6.4 exponential_reduce_fusion
  344.6 10.0 %fusion.101 = f32[320,1024]{1,0:T(8,128)S(1)} fusion(bf16[7632,1024]{1,0:T(8,128)(2,1)} %all-gather.9.cloned.1.call-done, f32[320,7632]{1,0:T(8,128)S(1)} %copy-done.48, f32[320]{0:T(512)S(1)} %get-tuple-element.237, f32[320]{0:T(512)S(1)} %get-tuple-element.162, s32[7632]{0:T(1024)S(1)} %iota_add_fusion, s32[320]{0:T(512)S(1)} %copy-done.84), kind=kOutput, calls=%fused_computation.309 | convolution fusion | flops 5016360960 | bytes 26744384 | tf_op jit(solution)/shard_map/dot_general | solution.py:49
  360.4 17.8 %convert_bitcast_fusion = bf16[8,7632,128]{2,1,0:T(8,128)(2,1)} fusion(f32[320,7632]{1,0:T(8,128)} %get-tuple-element.254, f32[320]{0:T(512)} %copy-done.90, f32[320]{0:T(512)} %copy-done.89, s32[7632]{0:T(1024)S(1)} %iota_add_fusion, s32[320]{0:T(512)} %eq.121, bf16[560,1024]{1,0:T(8,128)(2,1)} %constant_dynamic-update-slice_fusion.7, s32[]{:T(128)S(6)} %select_n.334), kind=kOutput, calls=%fused_computation.8 | convolution fusion | flops 5024176128 | bytes 26152772 | tf_op jit(solution)/shard_map/sv,swc->wvc/dot_general | solution.py:837
  393.2 3.3 gradient_block.12
  397.0 13.7 %add_convert_fusion.refs_1_ = bf16[512,4096]{1,0:T(8,128)(2,1)S(1)} fusion(f32[512,4096]{1,0:T(8,128)} %get-tuple-element.180, f32[512,4096]{1,0:T(8,128)} %get-tuple-element.250, f32[4096]{0:T(1024)S(1)} %bitcast.241, bf16[512,1024]{1,0:T(8,128)(2,1)S(1)} %get-tuple-element.168.refs_0_, bf16[1024,12288]{1,0:T(8,128)(2,1)} %all-gather.7.cloned.1.call-done), kind=kOutput, calls=%fused_computation.20 | convolution fusion | flops 4326424576 | bytes 30425088 | tf_op jit(solution)/shard_map/dot_general | solution.py:49
  420.2 11.0 %multiply_reduce_fusion.2 = (f32[1024]{0:T(1024)S(1)}, f32[512]{0:T(512)S(1)}, f32[1024]{0:T(1024)S(1)}, f32[512,1024]{1,0:T(8,128)}) fusion(f32[512,1024]{1,0:T(8,128)} %copy-done.45, f32[512]{0:T(512)S(1)} %copy-done.73, f32[512]{0:T(512)S(1)} %copy-done.69, f32[1024]{0:T(1024)S(1)} %bitcast.230, bf16[512,4096]{1,0:T(8,128)(2,1)S(1)} %add_convert_fusion.refs_1_, ...), kind=kOutput, calls=%fused_computation.65 | convolution fusion | flops 4300207616 | bytes 18894848 | tf_op jit(solution)/shard_map/dot_general | solution.py:59
  431.2 3.5 fusion.106
  435.0 3.8 fusion.41.do_ref
  442.9 16.4 %attend_back.1.refs_2_ = bf16[512,3072]{1,0:T(8,128)(2,1)S(1)} custom-call(bf16[512,3072]{1,0:T(8,128)(2,1)S(1)} %copy-done.1, bf16[512,3072]{1,0:T(8,128)(2,1)S(1)} %copy-done.1, bf16[512,3072]{1,0:T(8,128)(2,1)S(1)} %copy-done.1, bf16[512,1024]{1,0:T(8,128)(2,1)S(1)} %fusion.41.do_ref, f32[8,2,512]{2,1,0:T(2,128)S(1)} %get-tuple-element.99.lse_ref, ...), custom_call_target="tpu_custom_call" | custom-call | tf_op jit(solution)/shard_map/attend_back/pallas_call | solution.py:130
  459.3 8.6 collective-permute-done.29.refs_3_
  467.9 3.3 gradient_block.18
  471.3 3.2 convert_reduce_fusion
  479.9 4.9 gradient_block.20
  487.8 4.1 gradient_block.19
  493.2 6.2 multiply_reduce_fusion.3
  500.4 44.9 %collective-permute-done.31.refs_3_ = bf16[256,4096]{1,0:T(8,128)(2,1)S(1)} collective-permute-done((bf16[256,4096]{1,0:T(8,128)(2,1)}, bf16[256,4096]{1,0:T(8,128)(2,1)S(1)}, u32[]{:S(2)}, u32[]{:S(2)}) %collective-permute-start.31) | collective-permute-done | bytes 2097184 | tf_op jit(solution)/shard_map/ppermute | solution.py:356
  548.1 6.9 concatenate.95
  563.8 3.5 gradient_block.21
  579.6 3.3 gradient_block.22
  584.0 4.3 all-to-all-start.1
  590.1 3.1 broadcast_select_fusion.2.grad_ref
  593.3 3.1 broadcast_select_fusion.1.grad_ref
  596.4 7.3 all-to-all-done.1
  603.7 55.2 %collective-permute-done.32.refs_5_ = bf16[256,4096]{1,0:T(8,128)(2,1)} collective-permute-done((bf16[256,4096]{1,0:T(8,128)(2,1)}, bf16[256,4096]{1,0:T(8,128)(2,1)}, u32[]{:S(2)}, u32[]{:S(2)}) %collective-permute-start.32) | collective-permute-done | bytes 2097184 | tf_op jit(solution)/shard_map/ppermute | solution.py:356
  662.6 5.1 gradient_block.23
  669.0 6.5 span.3
  676.7 6.5 span.4
  691.2 6.4 span.5
  700.3 19.8 %press.1 = (f32[1,256,12288]{2,1,0:T(8,128)}, bf16[8,256,1536]{2,1,0:T(8,128)(2,1)}) custom-call(f32[2]{0:T(128)} %pad_maximum_fusion.5.scale_ref, f32[256,4096]{1,0:T(8,128)} %get-tuple-element.120.refs_0_, f32[256,4096]{1,0:T(8,128)} %get-tuple-element.121.refs_1_, f32[256,4096]{1,0:T(8,128)} %get-tuple-element.122.refs_2_), custom_call_target="tpu_custom_call" | custom-call | tf_op jit(solution)/shard_map/press/pallas_call | solution.py:631
  720.0 5.1 dynamic-slice_bitcast_fusion.5
  725.1 27.8 %collective-permute-start.40 = (bf16[4,256,1536]{2,1,0:T(8,128)(2,1)}, bf16[4,256,1536]{2,1,0:T(8,128)(2,1)}, u32[]{:S(2)}, u32[]{:S(2)}) collective-permute-start(bf16[4,256,1536]{2,1,0:T(8,128)(2,1)} %get-tuple-element.190), channel_id=1, source_target_pairs={{0,4},{4,0},{8,12},{12,8},{16,20},{20,16},{24,28},{28,24},{1,5},{5... | collective-permute-start | bytes 9437192 | tf_op jit(solution)/shard_map/ppermute | solution.py:696
  754.4 4.2 collective-permute-done.40
  766.7 7.8 collective-permute-done.42
  779.0 4.0 collective-permute-done.41
  783.0 9.4 collective-permute-done.43
  796.6 5.0 multiply_reduce_fusion.10
  801.7 40.6 %all-gather.15.cloned.1.call-done = bf16[18496,128]{1,0:T(8,128)(2,1)} async-done(((bf16[4624,128]{1,0:T(8,128)(2,1)}), bf16[18496,128]{1,0:T(8,128)(2,1)}) %all-gather.15.cloned.1.call-update) | async-done | bytes 4734992 | tf_op jit(solution)/shard_map/all_gather | solution.py:867
  847.5 36.2 %add_rows.1.grad_ref = f32[7632,128]{1,0:T(8,128)} custom-call(s32[16384]{0:T(1024)} %copy-done.37, bf16[4,4624,128]{2,1,0:T(8,128)(2,1)} %bitcast.207), custom_call_target="tpu_custom_call" | custom-call | tf_op jit(solution)/shard_map/add_rows/pallas_call | solution.py:547
  883.7 12.8 %update.1 = (f32[7632,128]{1,0:T(8,128)}, f32[7632,128]{1,0:T(8,128)}, f32[1,128]{1,0:T(1,128)}, f32[1,128]{1,0:T(1,128)}) custom-call(f32[7632,128]{1,0:T(8,128)} %add_rows.1.grad_ref, bf16[7632,128]{1,0:T(8,128)(2,1)} %bitcast.211, f32[7632,128]{1,0:T(8,128)} %table_ref.3, f32[7632,128]{1,0:T(8,128)} %first_ref.1, f32[7632,128]{1,0:T(8,128)} %second_ref.1), custom_call_target="tpu_custom_call" | custom-call | tf_op jit(solution)/shard_map/update/pallas_call | solution.py:672
  911.7 3.5 collective-permute-done.50
  915.3 4.4 collective-permute-done.51
  929.4 3.4 multiply_subtract_fusion.2
  932.9 4.6 multiply_subtract_fusion
  937.5 5.9 multiply_subtract_fusion.1
  943.4 9.1 convert_element_type.365
  (460 shorter events, 204.1 us)
Async XLA Ops:
  7.2 218.3 %all-gather.7.cloned.1.call-start = ((), (), s32[]{:S(2)}) async-start(), calls=%async_computation.3 | async-start | bytes 28311552 | tf_op jit(solution)/shard_map/all_gather | solution.py:775
  8.0 1.3 collective-permute-start.3
  10.1 4.7 collective-permute-start.4
  14.9 8.3 collective-permute-start.5
  18.5 59.7 %collective-permute-start.6 = (bf16[256,1536]{1,0:T(8,128)(2,1)S(1)}, bf16[256,1536]{1,0:T(8,128)(2,1)S(1)}, u32[]{:S(2)}, u32[]{:S(2)}) collective-permute-start(bf16[256,1536]{1,0:T(8,128)(2,1)S(1)} %convert_element_type.293), channel_id=1, source_target_pairs={{0,3},{1,0},{2,1},{3,2},{4,7},{5,4},{6,5},{7,6},{8,11},{9,8},{10,9... | collective-permute-start | bytes 2359304 | tf_op jit(solution)/shard_map/ppermute | solution.py:251
  22.1 66.2 %collective-permute-start.7 = (bf16[256,1536]{1,0:T(8,128)(2,1)S(1)}, bf16[256,1536]{1,0:T(8,128)(2,1)S(1)}, u32[]{:S(2)}, u32[]{:S(2)}) collective-permute-start(bf16[256,1536]{1,0:T(8,128)(2,1)S(1)} %convert_element_type.293), channel_id=1, source_target_pairs={{0,2},{1,3},{2,0},{3,1},{4,6},{5,7},{6,4},{7,5},{8,10},{9,11},{10,... | collective-permute-start | bytes 2359304 | tf_op jit(solution)/shard_map/ppermute | solution.py:251
  22.1 66.2 %collective-permute-start.8 = (bf16[256,1536]{1,0:T(8,128)(2,1)S(1)}, bf16[256,1536]{1,0:T(8,128)(2,1)S(1)}, u32[]{:S(2)}, u32[]{:S(2)}) collective-permute-start(bf16[256,1536]{1,0:T(8,128)(2,1)S(1)} %convert_element_type.293), channel_id=1, source_target_pairs={{0,1},{1,2},{2,3},{3,0},{4,5},{5,6},{6,7},{7,4},{8,9},{9,10},{10,1... | collective-permute-start | bytes 2359304 | tf_op jit(solution)/shard_map/ppermute | solution.py:251
  23.4 67.4 %copy-start.62 = (s32[4,8,672]{2,1,0:T(8,128)}, s32[4,8,672]{2,1,0:T(8,128)S(1)}, u32[]{:S(2)}) copy-start(s32[4,8,672]{2,1,0:T(8,128)S(1)} %reshape.639) | copy-start | bytes 258052
  93.4 24.7 %collective-permute-start.10 = (bf16[1792,128]{1,0:T(8,128)(2,1)S(1)}, bf16[1792,128]{1,0:T(8,128)(2,1)S(1)}, u32[]{:S(2)}, u32[]{:S(2)}) collective-permute-start(bf16[1792,128]{1,0:T(8,128)(2,1)S(1)} %get-tuple-element.214), channel_id=1, source_target_pairs={{0,2},{1,3},{2,0},{3,1},{4,6},{5,7},{6,4},{7,5},{8,10},{9,11},{10,... | collective-permute-start | bytes 1376264 | tf_op jit(solution)/shard_map/ppermute | solution.py:281
  96.3 30.8 %collective-permute-start.11 = (bf16[1792,128]{1,0:T(8,128)(2,1)S(1)}, bf16[1792,128]{1,0:T(8,128)(2,1)S(1)}, u32[]{:S(2)}, u32[]{:S(2)}) collective-permute-start(bf16[1792,128]{1,0:T(8,128)(2,1)S(1)} %get-tuple-element.213), channel_id=1, source_target_pairs={{0,3},{1,0},{2,1},{3,2},{4,7},{5,4},{6,5},{7,6},{8,11},{9,8},{10,9... | collective-permute-start | bytes 1376264 | tf_op jit(solution)/shard_map/ppermute | solution.py:281
  96.7 30.3 %collective-permute-start.9 = (bf16[1792,128]{1,0:T(8,128)(2,1)S(1)}, bf16[1792,128]{1,0:T(8,128)(2,1)S(1)}, u32[]{:S(2)}, u32[]{:S(2)}) collective-permute-start(bf16[1792,128]{1,0:T(8,128)(2,1)S(1)} %get-tuple-element.215), channel_id=1, source_target_pairs={{0,1},{1,2},{2,3},{3,0},{4,5},{5,6},{6,7},{7,4},{8,9},{9,10},{10,1... | collective-permute-start | bytes 1376264 | tf_op jit(solution)/shard_map/ppermute | solution.py:281
  137.0 33.9 %all-to-all-start = ((bf16[8,512,128]{2,1,0:T(8,128)(2,1)}), bf16[8,512,128]{2,1,0:T(8,128)(2,1)S(1)}, u32[]{:S(2)}, u32[]{:S(2)}) async-start(bf16[8,512,128]{2,1,0:T(8,128)(2,1)} %bitcast.210), calls=%async_computation | async-start | bytes 2097152 | tf_op jit(solution)/shard_map/all_to_all | solution.py:785
  140.5 177.3 %all-gather.9.cloned.1.call-start = ((), (), s32[]{:S(2)}) async-start(), calls=%async_computation.4 | async-start | bytes 17584128 | tf_op jit(solution)/shard_map/all_gather | solution.py:804
  141.2 6.5 collective-permute-start.12
  141.6 28.8 %collective-permute-start.15 = (s32[1,592]{1,0:T(1,128)S(1)}, s32[1,592]{1,0:T(1,128)S(1)}, u32[]{:S(2)}, u32[]{:S(2)}) collective-permute-start(s32[1,592]{1,0:T(1,128)S(1)} %pad_add_fusion.3), channel_id=1, source_target_pairs={{0,0},{1,4},{2,1},{3,5},{4,2},{5,6},{6,3},{7,7},{8,8},{9,12},{10,9... | collective-permute-start | bytes 7112 | tf_op jit(solution)/shard_map/ppermute | solution.py:402
  142.9 105.3 %copy-start.64 = (f32[1,1024]{1,0:T(1,128)}, f32[1,1024]{1,0:T(1,128)S(1)}, u32[]{:S(2)}) copy-start(f32[1,1024]{1,0:T(1,128)S(1)} %get-tuple-element.208) | copy-start | bytes 12292
  149.0 16.4 %collective-permute-start.13 = (f32[]{:T(128)}, f32[]{:T(128)}, u32[]{:S(2)}, u32[]{:S(2)}) collective-permute-start(f32[]{:T(128)} %add.629), channel_id=1, source_target_pairs={{0,8},{4,12},{8,0},{12,4},{16,24},{20,28},{24,16},{28,20},{1,9},{5... | collective-permute-start | bytes 20 | tf_op jit(solution)/shard_map/ppermute | solution.py:241
  166.0 3.7 collective-permute-start.14
  170.4 66.1 %copy-start.38 = (s32[1,512]{1,0:T(1,128)}, s32[1,512]{1,0:T(1,128)S(1)}, u32[]{:S(2)}) copy-start(s32[1,512]{1,0:T(1,128)S(1)} %slice.212.query_doc_ref) | copy-start | bytes 6148
  174.8 73.4 %copy-start.66 = (f32[512]{0:T(512)}, f32[512]{0:T(512)S(1)}, u32[]{:S(2)}) copy-start(f32[512]{0:T(512)S(1)} %broadcast_multiply_fusion.3) | copy-start | bytes 6148
  175.2 73.1 %copy-start.70 = (f32[512]{0:T(512)}, f32[512]{0:T(512)S(1)}, u32[]{:S(2)}) copy-start(f32[512]{0:T(512)S(1)} %fusion.82) | copy-start | bytes 6148
  176.5 60.0 %copy-start.9 = (bf16[512,1024]{1,0:T(8,128)(2,1)}, bf16[512,1024]{1,0:T(8,128)(2,1)S(1)}, u32[]{:S(2)}) copy-start(bf16[512,1024]{1,0:T(8,128)(2,1)S(1)} %fusion.32.refs_0_) | copy-start | bytes 3145732
  225.5 433.4 %reduce-scatter.2.cloned.1.call-start = ((), (), s32[]{:S(2)}) async-start(), calls=%async_computation.5 | async-start | bytes 17584128 | tf_op jit(solution)/shard_map/reduce_scatter | solution.py:839
  252.5 187.7 %copy-start.18 = (bf16[512,1024]{1,0:T(8,128)(2,1)}, bf16[512,1024]{1,0:T(8,128)(2,1)S(1)}, u32[]{:S(2)}) copy-start(bf16[512,1024]{1,0:T(8,128)(2,1)S(1)} %fusion.33.refs_0_) | copy-start | bytes 3145732
  293.2 10.0 %collective-permute-start.16 = (bf16[80,1024]{1,0:T(8,128)(2,1)S(1)}, bf16[80,1024]{1,0:T(8,128)(2,1)S(1)}, u32[]{:S(2)}, u32[]{:S(2)}) collective-permute-start(bf16[80,1024]{1,0:T(8,128)(2,1)S(1)} %get-tuple-element.178), channel_id=1, source_target_pairs={{0,3},{1,0},{2,1},{3,2},{4,7},{5,4},{6,5},{7,6},{8,11},{9,8},{10,9... | collective-permute-start | bytes 491528 | tf_op jit(solution)/shard_map/ppermute | solution.py:251
  294.0 18.6 %collective-permute-start.17 = (bf16[80,1024]{1,0:T(8,128)(2,1)S(1)}, bf16[80,1024]{1,0:T(8,128)(2,1)}, u32[]{:S(2)}, u32[]{:S(2)}) collective-permute-start(bf16[80,1024]{1,0:T(8,128)(2,1)S(1)} %get-tuple-element.178), channel_id=1, source_target_pairs={{0,2},{1,3},{2,0},{3,1},{4,6},{5,7},{6,4},{7,5},{8,10},{9,11},{10,... | collective-permute-start | bytes 491528 | tf_op jit(solution)/shard_map/ppermute | solution.py:251
  301.7 12.5 %collective-permute-start.18 = (bf16[80,1024]{1,0:T(8,128)(2,1)S(1)}, bf16[80,1024]{1,0:T(8,128)(2,1)S(1)}, u32[]{:S(2)}, u32[]{:S(2)}) collective-permute-start(bf16[80,1024]{1,0:T(8,128)(2,1)S(1)} %get-tuple-element.178), channel_id=1, source_target_pairs={{0,1},{1,2},{2,3},{3,0},{4,5},{5,6},{6,7},{7,4},{8,9},{9,10},{10,1... | collective-permute-start | bytes 491528 | tf_op jit(solution)/shard_map/ppermute | solution.py:251
  335.7 3.7 collective-permute-start.19
  337.7 4.6 collective-permute-start.20
  337.7 5.5 collective-permute-start.21
  356.4 21.8 %collective-permute-start.22 = (bf16[80,1024]{1,0:T(8,128)(2,1)}, bf16[80,1024]{1,0:T(8,128)(2,1)}, u32[]{:S(2)}, u32[]{:S(2)}) collective-permute-start(bf16[80,1024]{1,0:T(8,128)(2,1)} %get-tuple-element.219), channel_id=1, source_target_pairs={{0,1},{1,2},{2,3},{3,0},{4,5},{5,6},{6,7},{7,4},{8,9},{9,10},{10,1... | collective-permute-start | bytes 491528 | tf_op jit(solution)/shard_map/ppermute | solution.py:268
  356.4 21.8 %collective-permute-start.23 = (bf16[80,1024]{1,0:T(8,128)(2,1)S(1)}, bf16[80,1024]{1,0:T(8,128)(2,1)}, u32[]{:S(2)}, u32[]{:S(2)}) collective-permute-start(bf16[80,1024]{1,0:T(8,128)(2,1)S(1)} %get-tuple-element.221), channel_id=1, source_target_pairs={{0,2},{1,3},{2,0},{3,1},{4,6},{5,7},{6,4},{7,5},{8,10},{9,11},{10,... | collective-permute-start | bytes 491528 | tf_op jit(solution)/shard_map/ppermute | solution.py:268
  357.5 20.6 %collective-permute-start.24 = (bf16[80,1024]{1,0:T(8,128)(2,1)S(1)}, bf16[80,1024]{1,0:T(8,128)(2,1)}, u32[]{:S(2)}, u32[]{:S(2)}) collective-permute-start(bf16[80,1024]{1,0:T(8,128)(2,1)S(1)} %get-tuple-element.220), channel_id=1, source_target_pairs={{0,3},{1,0},{2,1},{3,2},{4,7},{5,4},{6,5},{7,6},{8,11},{9,8},{10,9... | collective-permute-start | bytes 491528 | tf_op jit(solution)/shard_map/ppermute | solution.py:268
  393.2 17.6 %collective-permute-start.26 = (bf16[256,4096]{1,0:T(8,128)(2,1)S(1)}, bf16[256,4096]{1,0:T(8,128)(2,1)S(1)}, u32[]{:S(2)}, u32[]{:S(2)}) collective-permute-start(bf16[256,4096]{1,0:T(8,128)(2,1)S(1)} %gradient_block.13), channel_id=1, source_target_pairs={{0,4},{4,0},{8,12},{12,8},{16,20},{20,16},{24,28},{28,24},{1,5},{5... | collective-permute-start | bytes 6291464 | tf_op jit(solution)/shard_map/ppermute | solution.py:341
  396.5 15.6 %collective-permute-start.25 = (bf16[256,4096]{1,0:T(8,128)(2,1)}, bf16[256,4096]{1,0:T(8,128)(2,1)S(1)}, u32[]{:S(2)}, u32[]{:S(2)}) collective-permute-start(bf16[256,4096]{1,0:T(8,128)(2,1)} %gradient_block.12), channel_id=1, source_target_pairs={{0,4},{4,0},{8,12},{12,8},{16,20},{20,16},{24,28},{28,24},{1,5},{5... | collective-permute-start | bytes 6291464 | tf_op jit(solution)/shard_map/ppermute | solution.py:340
  419.6 19.2 %collective-permute-start.28 = (bf16[256,4096]{1,0:T(8,128)(2,1)S(1)}, bf16[256,4096]{1,0:T(8,128)(2,1)S(1)}, u32[]{:S(2)}, u32[]{:S(2)}) collective-permute-start(bf16[256,4096]{1,0:T(8,128)(2,1)S(1)} %gradient_block.16), channel_id=1, source_target_pairs={{0,4},{4,0},{8,12},{12,8},{16,20},{20,16},{24,28},{28,24},{1,5},{5... | collective-permute-start | bytes 6291464 | tf_op jit(solution)/shard_map/ppermute | solution.py:341
  419.8 20.4 %collective-permute-start.27 = (bf16[256,4096]{1,0:T(8,128)(2,1)S(1)}, bf16[256,4096]{1,0:T(8,128)(2,1)S(1)}, u32[]{:S(2)}, u32[]{:S(2)}) collective-permute-start(bf16[256,4096]{1,0:T(8,128)(2,1)S(1)} %gradient_block.15), channel_id=1, source_target_pairs={{0,4},{4,0},{8,12},{12,8},{16,20},{20,16},{24,28},{28,24},{1,5},{5... | collective-permute-start | bytes 6291464 | tf_op jit(solution)/shard_map/ppermute | solution.py:340
  420.2 47.7 %collective-permute-start.29 = (bf16[256,4096]{1,0:T(8,128)(2,1)S(1)}, bf16[256,4096]{1,0:T(8,128)(2,1)}, u32[]{:S(2)}, u32[]{:S(2)}) collective-permute-start(bf16[256,4096]{1,0:T(8,128)(2,1)S(1)} %gradient_block.14), channel_id=1, source_target_pairs={{0,1},{1,0},{2,3},{3,2},{4,5},{5,4},{6,7},{7,6},{8,9},{9,8},{10,11... | collective-permute-start | bytes 6291464 | tf_op jit(solution)/shard_map/ppermute | solution.py:356
  471.3 16.5 %collective-permute-start.30 = (bf16[256,4096]{1,0:T(8,128)(2,1)}, bf16[256,4096]{1,0:T(8,128)(2,1)}, u32[]{:S(2)}, u32[]{:S(2)}) collective-permute-start(bf16[256,4096]{1,0:T(8,128)(2,1)} %gradient_block.18), channel_id=1, source_target_pairs={{0,4},{4,0},{8,12},{12,8},{16,20},{20,16},{24,28},{28,24},{1,5},{5... | collective-permute-start | bytes 6291464 | tf_op jit(solution)/shard_map/ppermute | solution.py:340
  474.5 70.8 %collective-permute-start.31 = (bf16[256,4096]{1,0:T(8,128)(2,1)}, bf16[256,4096]{1,0:T(8,128)(2,1)S(1)}, u32[]{:S(2)}, u32[]{:S(2)}) collective-permute-start(bf16[256,4096]{1,0:T(8,128)(2,1)} %copy-done.29), channel_id=1, source_target_pairs={{0,1},{1,0},{2,3},{3,2},{4,5},{5,4},{6,7},{7,6},{8,9},{9,8},{10,11... | collective-permute-start | bytes 6291464 | tf_op jit(solution)/shard_map/ppermute | solution.py:356
  484.8 105.3 %collective-permute-start.36 = (bf16[256,4096]{1,0:T(8,128)(2,1)}, bf16[256,4096]{1,0:T(8,128)(2,1)}, u32[]{:S(2)}, u32[]{:S(2)}) collective-permute-start(bf16[256,4096]{1,0:T(8,128)(2,1)} %gradient_block.20), channel_id=1, source_target_pairs={{2,4},{3,5},{4,2},{5,3},{10,12},{11,13},{12,10},{13,11},{18,20},{1... | collective-permute-start | bytes 6291464 | tf_op jit(solution)/shard_map/ppermute | solution.py:380
  557.2 14.2 %collective-permute-start.33 = (bf16[528,512]{1,0:T(8,128)(2,1)}, bf16[528,512]{1,0:T(8,128)(2,1)}, u32[]{:S(2)}, u32[]{:S(2)}) collective-permute-start(bf16[528,512]{1,0:T(8,128)(2,1)} %dynamic-slice_convert_fusion), channel_id=1, source_target_pairs={{0,16},{4,20},{8,24},{12,28},{16,0},{20,4},{24,8},{28,12},{1,17},{... | collective-permute-start | bytes 1622024 | tf_op jit(solution)/shard_map/ppermute | solution.py:731
  567.4 25.9 %collective-permute-start.37 = (bf16[256,4096]{1,0:T(8,128)(2,1)}, bf16[256,4096]{1,0:T(8,128)(2,1)}, u32[]{:S(2)}, u32[]{:S(2)}) collective-permute-start(bf16[256,4096]{1,0:T(8,128)(2,1)} %gradient_block.21), channel_id=1, source_target_pairs={{2,4},{3,5},{4,2},{5,3},{10,12},{11,13},{12,10},{13,11},{18,20},{1... | collective-permute-start | bytes 6291464 | tf_op jit(solution)/shard_map/ppermute | solution.py:380
  574.3 14.1 %collective-permute-start.34 = (bf16[528,256]{1,0:T(8,128)(2,1)}, bf16[528,256]{1,0:T(8,128)(2,1)S(1)}, u32[]{:S(2)}, u32[]{:S(2)}) collective-permute-start(bf16[528,256]{1,0:T(8,128)(2,1)} %dynamic-slice_convert_fusion.1), channel_id=1, source_target_pairs={{0,8},{4,12},{8,0},{12,4},{16,24},{20,28},{24,16},{28,20},{1,9},{5... | collective-permute-start | bytes 811016 | tf_op jit(solution)/shard_map/ppermute | solution.py:731
  582.9 76.1 %collective-permute-start.38 = (bf16[256,4096]{1,0:T(8,128)(2,1)}, bf16[256,4096]{1,0:T(8,128)(2,1)}, u32[]{:S(2)}, u32[]{:S(2)}) collective-permute-start(bf16[256,4096]{1,0:T(8,128)(2,1)} %gradient_block.22), channel_id=1, source_target_pairs={{0,4},{4,0},{8,12},{12,8},{16,20},{20,16},{24,28},{28,24},{1,5},{5... | collective-permute-start | bytes 6291464 | tf_op jit(solution)/shard_map/ppermute | solution.py:341
  584.0 19.7 %all-to-all-start.1 = ((bf16[8,512,128]{2,1,0:T(8,128)(2,1)}), bf16[8,512,128]{2,1,0:T(8,128)(2,1)}, u32[]{:S(2)}, u32[]{:S(2)}) async-start(bf16[8,512,128]{2,1,0:T(8,128)(2,1)} %bitcast.209), calls=%async_computation.1 | async-start | bytes 2097152 | tf_op jit(solution)/shard_map/all_to_all | solution.py:859
  588.3 254.0 %all-gather.15.cloned.1.call-start = ((), (), s32[]{:S(2)}) async-start(), calls=%async_computation.8 | async-start | bytes 5918720 | tf_op jit(solution)/shard_map/all_gather | solution.py:867
  588.3 70.6 %collective-permute-start.32 = (bf16[256,4096]{1,0:T(8,128)(2,1)}, bf16[256,4096]{1,0:T(8,128)(2,1)}, u32[]{:S(2)}, u32[]{:S(2)}) collective-permute-start(bf16[256,4096]{1,0:T(8,128)(2,1)} %copy-done.30), channel_id=1, source_target_pairs={{0,1},{1,0},{2,3},{3,2},{4,5},{5,4},{6,7},{7,6},{8,9},{9,8},{10,11... | collective-permute-start | bytes 6291464 | tf_op jit(solution)/shard_map/ppermute | solution.py:356
  589.6 3.6 collective-permute-start.35
  667.7 20.4 %collective-permute-start.39 = (bf16[256,4096]{1,0:T(8,128)(2,1)}, bf16[256,4096]{1,0:T(8,128)(2,1)S(1)}, u32[]{:S(2)}, u32[]{:S(2)}) collective-permute-start(bf16[256,4096]{1,0:T(8,128)(2,1)} %gradient_block.23), channel_id=1, source_target_pairs={{2,4},{3,5},{4,2},{5,3},{10,12},{11,13},{12,10},{13,11},{18,20},{1... | collective-permute-start | bytes 6291464 | tf_op jit(solution)/shard_map/ppermute | solution.py:380
  725.1 33.5 %collective-permute-start.40 = (bf16[4,256,1536]{2,1,0:T(8,128)(2,1)}, bf16[4,256,1536]{2,1,0:T(8,128)(2,1)}, u32[]{:S(2)}, u32[]{:S(2)}) collective-permute-start(bf16[4,256,1536]{2,1,0:T(8,128)(2,1)} %get-tuple-element.190), channel_id=1, source_target_pairs={{0,4},{4,0},{8,12},{12,8},{16,20},{20,16},{24,28},{28,24},{1,5},{5... | collective-permute-start | bytes 9437192 | tf_op jit(solution)/shard_map/ppermute | solution.py:696
  753.0 184.5 %all-gather.11.cloned.1.call-start = ((), (), s32[]{:S(2)}) async-start(), calls=%async_computation.6 | async-start | bytes 1216512 | tf_op jit(solution)/shard_map/all_gather | solution.py:922
  762.4 12.2 %collective-permute-start.42 = (bf16[128,1536]{1,0:T(8,128)(2,1)}, bf16[128,1536]{1,0:T(8,128)(2,1)S(1)}, u32[]{:S(2)}, u32[]{:S(2)}) collective-permute-start(bf16[128,1536]{1,0:T(8,128)(2,1)} %get-tuple-element.192), channel_id=1, source_target_pairs={{0,8},{4,12},{8,0},{12,4},{16,24},{20,28},{24,16},{28,20},{1,9},{5... | collective-permute-start | bytes 1179656 | tf_op jit(solution)/shard_map/ppermute | solution.py:696
  763.9 19.1 %collective-permute-start.41 = (bf16[128,1536]{1,0:T(8,128)(2,1)}, bf16[128,1536]{1,0:T(8,128)(2,1)S(1)}, u32[]{:S(2)}, u32[]{:S(2)}) collective-permute-start(bf16[128,1536]{1,0:T(8,128)(2,1)} %get-tuple-element.191), channel_id=1, source_target_pairs={{0,8},{4,12},{8,0},{12,4},{16,24},{20,28},{24,16},{28,20},{1,9},{5... | collective-permute-start | bytes 1179656 | tf_op jit(solution)/shard_map/ppermute | solution.py:696
  764.6 12.6 %collective-permute-start.45 = (bf16[128,1536]{1,0:T(8,128)(2,1)S(1)}, bf16[128,1536]{1,0:T(8,128)(2,1)S(1)}, u32[]{:S(2)}, u32[]{:S(2)}) collective-permute-start(bf16[128,1536]{1,0:T(8,128)(2,1)S(1)} %get-tuple-element.198), channel_id=1, source_target_pairs={{0,16},{4,20},{8,24},{12,28},{16,0},{20,4},{24,8},{28,12},{1,17},{... | collective-permute-start | bytes 1179656 | tf_op jit(solution)/shard_map/ppermute | solution.py:696
  766.2 27.4 %collective-permute-start.44 = (bf16[128,1536]{1,0:T(8,128)(2,1)S(1)}, bf16[128,1536]{1,0:T(8,128)(2,1)S(1)}, u32[]{:S(2)}, u32[]{:S(2)}) collective-permute-start(bf16[128,1536]{1,0:T(8,128)(2,1)S(1)} %get-tuple-element.197), channel_id=1, source_target_pairs={{0,16},{4,20},{8,24},{12,28},{16,0},{20,4},{24,8},{28,12},{1,17},{... | collective-permute-start | bytes 1179656 | tf_op jit(solution)/shard_map/ppermute | solution.py:696
  775.7 16.7 %collective-permute-start.43 = (bf16[128,1536]{1,0:T(8,128)(2,1)S(1)}, bf16[128,1536]{1,0:T(8,128)(2,1)S(1)}, u32[]{:S(2)}, u32[]{:S(2)}) collective-permute-start(bf16[128,1536]{1,0:T(8,128)(2,1)S(1)} %fusion.50), channel_id=1, source_target_pairs={{0,16},{4,20},{8,24},{12,28},{16,0},{20,4},{24,8},{28,12},{1,17},{... | collective-permute-start | bytes 1179656 | tf_op jit(solution)/shard_map/ppermute | solution.py:696
  777.4 16.2 %collective-permute-start.46 = (bf16[128,1536]{1,0:T(8,128)(2,1)S(1)}, bf16[128,1536]{1,0:T(8,128)(2,1)S(1)}, u32[]{:S(2)}, u32[]{:S(2)}) collective-permute-start(bf16[128,1536]{1,0:T(8,128)(2,1)S(1)} %fusion.48), channel_id=1, source_target_pairs={{0,8},{4,12},{8,0},{12,4},{16,24},{20,28},{24,16},{28,20},{1,9},{5... | collective-permute-start | bytes 1179656 | tf_op jit(solution)/shard_map/ppermute | solution.py:696
  844.1 99.3 %all-gather.13.cloned.1.call-start = ((), (), s32[]{:S(2)}) async-start(), calls=%async_computation.7 | async-start | bytes 7077888 | tf_op jit(solution)/shard_map/all_gather | solution.py:920
  903.5 1.1 collective-permute-start.47
  904.6 3.5 collective-permute-start.48
  908.2 3.5 collective-permute-start.49
  911.7 3.5 collective-permute-start.50
  915.3 4.4 collective-permute-start.51
  (87 other events, 857.2 us)
Sparse Core Ops, SparseCore 0:
  90.7 134.7 all-gather.6
  227.9 88.4 all-gather.8
  379.6 111.4 reduce-scatter.1
  753.1 89.1 all-gather.14
  844.7 22.1 all-gather.10
  868.8 45.5 all-gather.12

commit v9 on v8

--- a/solution.py
+++ b/solution.py
@@ -151,6 +151,72 @@
     peak = jnp.maximum(first[0], second[0])
     total = first[1] * jnp.exp(first[0] - peak) + second[1] * jnp.exp(second[0] - peak)
     return (peak, total, first[2] + second[2])
+
+
+def embed_back_kernel(dqkv_ref, weight_ref, drone_ref, embedded_ref, gain_ref, even_ref, *refs):
+    dembed_ref, rows_ref, sums_ref, total = refs
+    step = pl.program_id(0)
+    dqkv = dqkv_ref[...]
+    part = matmul_nt(dqkv, weight_ref[...])
+    sums_ref[...] = jnp.sum(dqkv.astype(jnp.float32), axis=0, keepdims=True)
+
+    @pl.when(step == 0)
+    def _():
+        total[...] = drone_ref[...] + part
+
+    @pl.when(step > 0)
+    def _():
+        total[...] += part
+
+    @pl.when(step == pl.num_programs(0) - 1)
+    def _():
+        grad = total[...]
+        embedded = embedded_ref[...]
+        cent = embedded - jnp.mean(embedded, axis=1, keepdims=True)
+        scale = lax.rsqrt(jnp.mean(cent * cent, axis=1, keepdims=True) + LN_EPS)
+        normed = cent * scale
+        inner = grad * gain_ref[...]
+        inner_mean = jnp.mean(inner, axis=1, keepdims=True)
+        along = jnp.mean(inner * normed, axis=1, keepdims=True)
+        dembed = scale * (inner - inner_mean - normed * along)
+        dembed_ref[...] = dembed
+        even = even_ref[...]
+        rows_ref[0:1, :] = jnp.sum(grad * normed, axis=0, keepdims=True)
+        rows_ref[1:2, :] = jnp.sum(grad, axis=0, keepdims=True)
+        rows_ref[2:3, :] = jnp.sum(dembed * even, axis=0, keepdims=True)
+        rows_ref[3:4, :] = jnp.sum(dembed * (1.0 - even), axis=0, keepdims=True)
+        rows_ref[4:8, :] = jnp.zeros((4, D), jnp.float32)
+
+
+def embed_back(dqkv, weights, drone, embedded, gain, even):
+    tokens = dqkv.shape[0]
+    whole = pl.BlockSpec((tokens, D), lambda step: (0, 0))
+    return pl.pallas_call(
+        embed_back_kernel,
+        grid=(3,),
+        in_specs=[
+            pl.BlockSpec((tokens, D), lambda step: (0, step)),
+            pl.BlockSpec((D, D), lambda step: (0, step)),
+            whole,
+            whole,
+            pl.BlockSpec((1, D), lambda step: (0, 0)),
+            pl.BlockSpec((tokens, 1), lambda step: (0, 0)),
+        ],
+        out_specs=[
+            whole,
+            pl.BlockSpec((8, D), lambda step: (0, 0)),
+            pl.BlockSpec((1, D), lambda step: (0, step)),
+        ],
+        out_shape=[
+            jax.ShapeDtypeStruct((tokens, D), jnp.float32),
+            jax.ShapeDtypeStruct((8, D), jnp.float32),
+            jax.ShapeDtypeStruct((1, 3 * D), jnp.float32),
+        ],
+        scratch_shapes=[pltpu.VMEM((tokens, D), jnp.float32)],
+        compiler_params=pltpu.CompilerParams(vmem_limit_bytes=40 * 2**20),
+        cost_estimate=FREE,
+        name="embed_back",
+    )(dqkv, weights, drone, embedded, gain[None], even)
 
 
 def layer_forward(embedded, x0, act, docs, small, weights):
@@ -192,28 +258,29 @@
     (dqkv,) = down.crossed(dqkv)
     down.finish()
     mixed = WorkerPiece((act, dqkv), (out, dattn))
-    dxzero = drone + matmul_nt(mixed.across(dqkv), weights[:, 0 : 3 * D])
-    _, pull = jax.vjp(norm_rows, embedded, small[base], small[base + 1])
-    dembed, dgain_emb, dshift_emb = pull(dxzero)
+    even = (docs.reshape(L, 1) % 2 == 0).astype(jnp.float32)
+    dembed, embed_rows, bias_qkv = embed_back(
+        mixed.across(dqkv), weights, drone, embedded, small[base], even
+    )
     (dembed,) = up.crossed(dembed)
     up.finish()
-    bias_qkv = jnp.sum(dqkv, axis=0, dtype=jnp.float32)
     vectors = jnp.stack(
         [
-            dgain_emb,
-            dshift_emb,
+            embed_rows[0],
+            embed_rows[1],
             dgain_one,
             dshift_one,
             dgain_two,
             dshift_two,
-            bias_qkv[0:D],
-            bias_qkv[2 * D : 3 * D],
+            bias_qkv[0, 0:D],
+            bias_qkv[0, 2 * D : 3 * D],
             jnp.sum(dattn, axis=0, dtype=jnp.float32),
             jnp.sum(dffn, axis=0, dtype=jnp.float32),
         ]
     )
     bias_up = jnp.sum(dupper, axis=0, dtype=jnp.float32).reshape(FF // D, D)
-    return (dembed, jnp.concatenate([vectors, bias_up], axis=0), (mixed, up, down))
+    vectors = jnp.concatenate([embed_rows[2:4], vectors, bias_up], axis=0)
+    return (dembed, vectors, (mixed, up, down))
 
 
 def paired_mesh():
@@ -600,9 +667,10 @@
     return span, jnp.sum(sums)
 
 
-def press_kernel(steps, scale_ref, *refs):
-    *span_refs, error_ref, sent_ref = refs
-    step = pl.program_id(0)
+def press_kernel(steps, core_ref, scale_ref, *refs):
+    *span_refs, error_ref, give_ref, keep_ref = refs
+    core = pl.program_id(2)
+    step = pressed_step(pl.program_id(0), pl.program_id(1), core)
     scale = scale_ref[0]
     inverse = scale_ref[1]
     for index, span_ref in enumerate(span_refs):
@@ -612,38 +680,59 @@
             span = span_ref[...]
             sent = scale * jnp.tanh(span * inverse)
             error_ref[0] = span - sent
-            sent_ref[0] = sent.astype(jnp.bfloat16)
+            low = sent.astype(jnp.bfloat16)
+
+            @pl.when(core == core_ref[0])
+            def _():
+                keep_ref[0] = low
+
+            @pl.when(core != core_ref[0])
+            def _():
+                give_ref[0] = low
+
+
+def pressed_step(chip, column, core):
+    return (2 * chip + core) * 3 + column
 
 
 def pressed(spans, scale, parts):
     rows = spans[0].shape[0]
     cols = sum(span.shape[1] for span in spans)
-    block = 512
-    each = cols // parts // block
+    block = cols // parts // 3
     steps = [0]
     for span in spans:
         steps.append(steps[-1] + span.shape[1] // block)
 
     def of(index):
         low, count = steps[index], steps[index + 1] - steps[index]
-        return pl.BlockSpec((rows, block), lambda step: (0, jnp.clip(step - low, 0, count - 1)))
-
+
+        def place(chip, column, core, _):
+            return (0, jnp.clip(pressed_step(chip, column, core) - low, 0, count - 1))
+
+        return pl.BlockSpec((rows, block), place)
+
+    half = pl.BlockSpec((1, rows, block), lambda chip, column, core, _: (chip, 0, column))
+    half_shape = jax.ShapeDtypeStruct((parts // 2, rows, cols // parts), jnp.bfloat16)
     return pl.pallas_call(
         functools.partial(press_kernel, steps),
-        grid=(steps[-1],),
-        in_specs=[pl.BlockSpec(memory_space=pltpu.SMEM)] + [of(i) for i in range(len(spans))],
-        out_specs=[
-            pl.BlockSpec((1, rows, block), lambda step: (0, 0, step)),
-            pl.BlockSpec((1, rows, block), lambda step: (step // each, 0, step % each)),
-        ],
-        out_shape=[
-            jax.ShapeDtypeStruct((1, rows, cols), jnp.float32),
-            jax.ShapeDtypeStruct((parts, rows, cols // parts), jnp.bfloat16),
-        ],
+        grid_spec=pltpu.PrefetchScalarGridSpec(
+            num_scalar_prefetch=1,
+            grid=(parts // 2, 3, 2),
+            in_specs=[pl.BlockSpec(memory_space=pltpu.SMEM)] + [of(i) for i in range(len(spans))],
+            out_specs=[
+                pl.BlockSpec(
+                    (1, rows, block),
+                    lambda chip, column, core, _: (0, 0, pressed_step(chip, column, core)),
+                ),
+                half,
+                half,
+            ],
+        ),
+        out_shape=[jax.ShapeDtypeStruct((1, rows, cols), jnp.float32), half_shape, half_shape],
         compiler_params=pltpu.CompilerParams(vmem_limit_bytes=60 * 2**20),
         cost_estimate=FREE,
         name="press",
-    )(jnp.stack([scale, 1.0 / scale]), *spans)
+    )(wide_places()[0][None], jnp.stack([scale, 1.0 / scale]), *spans)
 
 
 def update_kernel(grad_ref, head_ref, table_ref, first_ref, second_ref, *out_refs):
@@ -688,28 +777,20 @@
     return wide_me % 2, wide_me // 2 % 2, wide_me // 4
 
 
-def scattered_sum(sent):
+def scattered_sum(give, keep):
     n_wide = lax.axis_size("wide")
-    core, x, y = wide_places()
+    _, x, y = wide_places()
 
     def send(value, bit):
         return lax.ppermute(value.astype(jnp.bfloat16), "wide", swap_pairs(n_wide, bit))
 
-    def pick(value, index):
-        return lax.dynamic_index_in_dim(value, index, 0, keepdims=False)
-
-    rows, cols = sent.shape[1:]
-    by_core = sent.reshape(n_wide // 2, 2, rows, cols)
-    give = lax.dynamic_index_in_dim(by_core, 1 - core, 1, keepdims=False)
-    keep = lax.dynamic_index_in_dim(by_core, core, 1, keepdims=False)
     take = send(give, 1)
-    half = rows // 2
+    half = keep.shape[1] // 2
 
     def chip(y_of, x_of, part):
-        low, high = part * half, (part + 1) * half
-        index = 2 * y_of + x_of
-        own, other = pick(keep[:, low:high], index), pick(take[:, low:high], index)
-        return own.astype(jnp.float32) + other.astype(jnp.float32)
+        start, size = (2 * y_of + x_of, part * half, 0), (1, half, keep.shape[2])
+        own, other = lax.dynamic_slice(keep, start, size), lax.dynamic_slice(take, start, size)
+        return own[0].astype(jnp.float32) + other[0].astype(jnp.float32)
 
     upper_far = send(chip(1 - y, 1 - x, 0), 2)
     lower_far = send(chip(1 - y, 1 - x, 1), 4)
@@ -848,22 +929,17 @@
         dhtwo.reshape(seqs * L, D), kept, doc_ids, small, weights
     )
     dembed_rows = dembed.reshape(seqs, L, D)
-    seg_even = jnp.sum(jnp.where(even_doc, dembed_rows, 0.0), axis=(0, 1))
-    seg_odd = jnp.sum(jnp.where(even_doc, 0.0, dembed_rows), axis=(0, 1))
-    small_grad = jnp.concatenate(
-        [jnp.sum(dembed_rows, axis=0), seg_even[None], seg_odd[None], vectors], axis=0
-    )
+    small_grad = jnp.concatenate([jnp.sum(dembed_rows, axis=0), vectors], axis=0)
     mixed = pieces[0]
     if paired:
         cut = dembed.astype(jnp.bfloat16).reshape(L, n_wide, D // n_wide).transpose(1, 0, 2)
         cut = lax.all_to_all(cut, "wide", 0, 0).reshape(n_wide * L, D // n_wide)
         halved = small_halved(small_grad).astype(jnp.bfloat16)
         down, up = pieces[2], pieces[1]
-        cut, mixed.away, halved, down.result, up.result, table_head = together(
-            cut, mixed.away, halved, down.result, up.result, table_head
+        mixed.finish()
+        cut, mixed.result, down.result, up.result, table_head = together(
+            jnp.concatenate([cut, halved]), mixed.result, down.result, up.result, table_head
         )
-        mixed.finish()
-        cut, mixed.result = together(jnp.concatenate([cut, halved]), mixed.result)
         group_rows = lax.all_gather(cut, "narrow", axis=0)
     else:
         mixed.finish()
@@ -882,8 +958,8 @@
             spans.insert(0, span)
             total = total + amount
         scale = total / (layer_m.shape[0] * layer_m.shape[1]) + MAG_EPS
-        new_worker, sent = pressed(spans, scale, n_wide)
-        server_in = scattered_sum(sent) / n_wide + server_err
+        new_worker, give, keep = pressed(spans, scale, n_wide)
+        server_in = scattered_sum(give, keep) / n_wide + server_err
     else:
         worker_grad = jnp.concatenate([piece.result for piece in pieces], axis=1)
         span = BETA * layer_m + (1.0 - BETA) * worker_grad.astype(jnp.float32) + worker_err[0]
@@ -898,7 +974,7 @@
     new_server = server_in - server_out
     server_low = server_out.astype(jnp.bfloat16)
     if paired:
-        server_low, group_rows = together(server_low, group_rows)
+        server_out, group_rows = together(server_out, group_rows)
         table_grad = added_rows(owners.slots, group_rows, vshard)
         table_mom, table_upd, table_norms = table_update(
             table_grad, table_head, table, table_m, table_v

time: 967 us -> 903 us (0.934)
  waiting for transfers between devices: 305 us -> 234 us
  local copies, waits for them, and re-layouts: 79.8 us -> 61.7 us
  Pallas kernels: 214 us -> 227 us
  starting transfers between devices: 101 us -> 111 us
    all_gather x1, waiting for transfers between devices: 40.6 us -> 0.01 us  [shards(): group_rows = lax.all_gather(cut, 'narrow', axis=0)]
    ppermute x3, waiting for transfers between devices: 109 us -> 74.9 us  [across(): self.away = lax.ppermute(away, 'narrow', sides)]
    ppermute x7, starting transfers between devices: 35.1 us -> 44.8 us  [send(): lax.ppermute(value.astype(jnp.bfloat16), 'wide', swap_pairs(n_wide, bit))]
    pallas_call x1 -> x2, Pallas kernels: 19.8 us -> 29.4 us  [the longest x1 21.3 us: pressed(): pl.pallas_call(functools.partial(press_kernel, steps), grid_spec=pltpu.Pr...]
    dot_general x5 -> x4, matrix products: 41.5 us -> 35.7 us  [matmul_nt(): lax.dot_general(left, right, (((1,), (1,)), ((), ())), preferred_element_...]
    unnamed x209 -> x183, local copies, waits for them, and re-layouts: 41.2 us -> 36.1 us
  transfers between devices with their start and end apart: 57 -> 57, of which waited for: 27 -> 29; matrix products, arithmetic and copies ran while one was open for 23% -> 25% of each run, Pallas kernels for 19% -> 25%
where the time goes in v9:
time: 903 us; the launch traced here: 896 us
  waiting for transfers between devices  234 us (26%)
  Pallas kernels  227 us (25%)
  other arithmetic  120 us (13%)
  matrix products  115 us (13%)
  starting transfers between devices  111 us (12%)
  local copies, waits for them, and re-layouts  61.7 us (7%)
  between operations  23.4 us (3%)
    ppermute x3, waiting for transfers between devices, across(): self.away = lax.ppermute(away, 'narrow', sides)  74.9 us
    dot_general x5, matrix products, matmul(): return jnp.dot(left, right, preferred_element_type=jnp.float32)  61.7 us
    pallas_call x1, Pallas kernels, packed_rows(): pl.pallas_call(pack_kernel, grid_spec=pltpu.PrefetchScalarGridSpec(num_sc...  52.4 us
    all_gather x1, waiting for transfers between devices, shards(): weights = lax.all_gather(layer_rows, 'wide', axis=1, tiled=True)  48.4 us
    ppermute x7, starting transfers between devices, send(): lax.ppermute(value.astype(jnp.bfloat16), 'wide', swap_pairs(n_wide, bit))  44.8 us
    pallas_call x12, Pallas kernels, gradient_block(): pl.pallas_call(functools.partial(block_kernel, steps), grid_spec=pltpu.Pr...  43 us
    pallas_call x1, Pallas kernels, added_rows(): pl.pallas_call(add_kernel, grid_spec=pltpu.PrefetchScalarGridSpec(num_sca...  36.2 us
    unnamed x183, local copies, waits for them, and re-layouts  36.1 us
  transfers between devices with their start and end apart: 57, of which 29 were waited for; matrix products, arithmetic and copies ran while one was open for 25% of the time, Pallas kernels for 25%

profile of v9, /device:TPU:0, one launch (start us, length us, event | category | flops | bytes accessed | tf_op | source)
XLA Modules:
  0.0 895.7 jit_solution(11260735346355064115)
XLA Ops:
  18.5 3.7 collective-permute-start.3
  25.7 52.4 %pack_rows.1 = bf16[4,4096,128]{2,1,0:T(8,128)(2,1)} custom-call(s32[16384]{0:T(1024)S(1)} %fusion.66.ids_ref, f32[7632,128]{1,0:T(8,128)S(1)} %copy-done.7), custom_call_target="tpu_custom_call" | custom-call | bytes 150000000 | tf_op jit(solution)/shard_map/pack_rows/pallas_call | solution.py:543
  78.1 10.2 %collective-permute-done.4 = bf16[256,1536]{1,0:T(8,128)(2,1)S(1)} collective-permute-done((bf16[256,1536]{1,0:T(8,128)(2,1)S(1)}, bf16[256,1536]{1,0:T(8,128)(2,1)S(1)}, u32[]{:S(2)}, u32[]{:S(2)}) %collective-permute-start.4) | collective-permute-done | bytes 786464 | tf_op jit(solution)/shard_map/ppermute | solution.py:318
  98.3 19.7 %collective-permute-done.10 = bf16[1792,128]{1,0:T(8,128)(2,1)S(1)} collective-permute-done((bf16[1792,128]{1,0:T(8,128)(2,1)S(1)}, bf16[1792,128]{1,0:T(8,128)(2,1)S(1)}, u32[]{:S(2)}, u32[]{:S(2)}) %collective-permute-start.10) | collective-permute-done | bytes 458784 | tf_op jit(solution)/shard_map/ppermute | solution.py:348
  118.1 9.0 %collective-permute-done.11 = bf16[1792,128]{1,0:T(8,128)(2,1)S(1)} collective-permute-done((bf16[1792,128]{1,0:T(8,128)(2,1)S(1)}, bf16[1792,128]{1,0:T(8,128)(2,1)S(1)}, u32[]{:S(2)}, u32[]{:S(2)}) %collective-permute-start.11) | collective-permute-done | bytes 458784 | tf_op jit(solution)/shard_map/ppermute | solution.py:348
  127.2 5.5 take_rows.3
  132.7 3.5 conditional.1
  137.2 3.6 all-to-all-start
  143.1 4.8 convert_element_type.287
  149.2 14.3 %collective-permute-start.13 = (f32[]{:T(128)}, f32[]{:T(128)}, u32[]{:S(2)}, u32[]{:S(2)}) collective-permute-start(f32[]{:T(128)} %add.630), channel_id=1, source_target_pairs={{0,8},{4,12},{8,0},{12,4},{16,24},{20,28},{24,16},{28,20},{1,9},{5... | collective-permute-start | bytes 20 | tf_op jit(solution)/shard_map/ppermute | solution.py:308
  177.3 48.4 %all-gather.7.cloned.1.call-done.weight_ref = bf16[1024,12288]{1,0:T(8,128)(2,1)} async-done(((bf16[1024,1536]{1,0:T(8,128)(2,1)}), bf16[1024,12288]{1,0:T(8,128)(2,1)}) %all-gather.7.cloned.1.call-update) | async-done | bytes 25165840 | tf_op jit(solution)/shard_map/all_gather | solution.py:856
  228.8 6.4 add_convert_fusion.1.q_ref.k_ref.v_ref
  235.3 11.7 %attend.1 = (bf16[512,1024]{1,0:T(8,128)(2,1)S(1)}, f32[8,2,512]{2,1,0:T(2,128)S(1)}) custom-call(bf16[512,3072]{1,0:T(8,128)(2,1)S(1)} %add_convert_fusion.1.q_ref.k_ref.v_ref, bf16[512,3072]{1,0:T(8,128)(2,1)S(1)} %add_convert_fusion.1.q_ref.k_ref.v_ref, bf16[512,3072]{1,0:T(8,128)(2,1)S(1)} %add_convert_fusion.1.q_ref.k_ref.v_ref, ...), custom_call_target="tpu_custom_call" | custom-call | tf_op jit(solution)/shard_map/attend/pallas_call | solution.py:86
  247.1 3.4 fusion.113
  251.4 26.1 %multiply_convert_fusion = (bf16[512,4096]{1,0:T(8,128)(2,1)S(1)}, f32[512,4096]{1,0:T(8,128)}, f32[512,4096]{1,0:T(8,128)}) fusion(f32[4096]{0:T(1024)S(1)} %bitcast.218, bf16[512,1024]{1,0:T(8,128)(2,1)S(1)} %fusion.30.refs_0_, bf16[1024,12288]{1,0:T(8,128)(2,1)} %all-gather.7.cloned.1.call-done.weight_ref), kind=kOutput, calls=%fused_computation.21 | convolution fusion | flops 4433379328 | bytes 30425088 | tf_op jit(solution)/shard_map/dot_general | solution.py:49
  277.5 9.2 %fusion.114 = (f32[512]{0:T(512)S(1)}, f32[512,1024]{1,0:T(8,128)S(1)}) fusion(f32[1024]{0:T(1024)S(1)} %bitcast.227, bf16[512,4096]{1,0:T(8,128)(2,1)S(1)} %get-tuple-element.175.refs_1_, bf16[1024,12288]{1,0:T(8,128)(2,1)} %all-gather.7.cloned.1.call-done.weight_ref, f32[1024]{0:T(1024)S(1)} %bitcast.215, f32[1024]{0:T(1024)S(1)} %bitcast.209, ...), kind=kOutput, calls=%fused_computation.310 | convolution fusion | flops 4298636800 | bytes 16795648 | tf_op jit(solution)/shard_map/dot_general | solution.py:59
  293.9 3.3 collective-permute-start.17
  302.3 10.1 %collective-permute-done.17 = bf16[80,1024]{1,0:T(8,128)(2,1)} collective-permute-done((bf16[80,1024]{1,0:T(8,128)(2,1)}, bf16[80,1024]{1,0:T(8,128)(2,1)}, u32[]{:S(2)}, u32[]{:S(2)}) %collective-permute-start.17) | collective-permute-done | bytes 163872 | tf_op jit(solution)/shard_map/ppermute | solution.py:318
  319.5 11.3 %fusion.115 = (f32[320]{0:T(512)S(1)}, f32[320,7632]{1,0:T(8,128)}) fusion(bf16[7632,1024]{1,0:T(8,128)(2,1)} %all-gather.9.cloned.1.call-done, bf16[560,1024]{1,0:T(8,128)(2,1)} %constant_dynamic-update-slice_fusion.7, s32[]{:T(128)S(6)} %select_n.331, pred[7632]{0:T(1024)(128)(4,1)S(1)} %copy-done.70), kind=kOutput, calls=%fused_computation.311 | convolution fusion | flops 5006591488 | bytes 26063572 | tf_op jit(solution)/shard_map/dot_general | solution.py:59
  330.9 6.5 exponential_reduce_fusion
  344.4 12.0 %fusion.100 = f32[320,1024]{1,0:T(8,128)S(1)} fusion(bf16[7632,1024]{1,0:T(8,128)(2,1)} %all-gather.9.cloned.1.call-done, f32[320,7632]{1,0:T(8,128)S(1)} %copy-done.45, f32[320]{0:T(512)S(1)} %get-tuple-element.227, f32[320]{0:T(512)S(1)} %get-tuple-element.163, s32[7632]{0:T(1024)S(1)} %copy-done.54, s32[320]{0:T(512)} %copy-done.71), kind=kOutput, calls=%fused_computation.300 | convolution fusion | flops 5016360960 | bytes 26744384 | tf_op jit(solution)/shard_map/dot_general | solution.py:49
  362.1 17.9 %convert_bitcast_fusion = bf16[8,7632,128]{2,1,0:T(8,128)(2,1)} fusion(f32[320,7632]{1,0:T(8,128)} %get-tuple-element.244, f32[320]{0:T(512)} %copy-done.76, f32[320]{0:T(512)S(1)} %get-tuple-element.163, s32[7632]{0:T(1024)S(1)} %copy-done.54, s32[320]{0:T(512)S(1)} %copy-done.72, bf16[560,1024]{1,0:T(8,128)(2,1)} %constant_dynamic-update-slice_fusion.7, ...), kind=kOutput, calls=%fused_computation.8 | convolution fusion | flops 5024176128 | bytes 26151236 | tf_op jit(solution)/shard_map/sv,swc->wvc/dot_general | solution.py:918
  385.8 3.2 multiply_reduce_fusion.1
  393.5 3.4 gradient_block.13
  400.0 13.7 %add_convert_fusion.refs_1_ = bf16[512,4096]{1,0:T(8,128)(2,1)S(1)} fusion(f32[512,4096]{1,0:T(8,128)} %get-tuple-element.176, f32[512,4096]{1,0:T(8,128)} %get-tuple-element.240, f32[4096]{0:T(1024)S(1)} %bitcast.219, bf16[512,1024]{1,0:T(8,128)(2,1)S(1)} %get-tuple-element.165.refs_0_, bf16[1024,12288]{1,0:T(8,128)(2,1)} %all-gather.7.cloned.1.call-done.weight_ref), kind=kOutput, calls=%fused_computation.20 | convolution fusion | flops 4326424576 | bytes 30425088 | tf_op jit(solution)/shard_map/dot_general | solution.py:49
  417.7 3.3 gradient_block.16
  424.3 11.6 %multiply_reduce_fusion.2 = (f32[1024]{0:T(1024)S(1)}, f32[512]{0:T(512)S(1)}, f32[1024]{0:T(1024)S(1)}, f32[512,1024]{1,0:T(8,128)}) fusion(f32[512,1024]{1,0:T(8,128)} %copy-done.43, f32[512]{0:T(512)S(1)} %fusion.81, f32[512]{0:T(512)S(1)} %broadcast_multiply_fusion.2, f32[1024]{0:T(1024)S(1)} %bitcast.210, ...), kind=kOutput, calls=%fused_computation.58 | convolution fusion | flops 4300207616 | bytes 18894848 | tf_op jit(solution)/shard_map/dot_general | solution.py:59
  440.5 3.6 fusion.37.do_ref
  445.5 3.4 gradient_block.17
  448.9 16.4 %attend_back.1.refs_2_.dqkv_ref = bf16[512,3072]{1,0:T(8,128)(2,1)S(1)} custom-call(bf16[512,3072]{1,0:T(8,128)(2,1)S(1)} %copy-done.1, bf16[512,3072]{1,0:T(8,128)(2,1)S(1)} %copy-done.1, bf16[512,3072]{1,0:T(8,128)(2,1)S(1)} %copy-done.1, bf16[512,1024]{1,0:T(8,128)(2,1)S(1)} %fusion.37.do_ref, f32[8,2,512]{2,1,0:T(2,128)S(1)} %get-tuple-element.100.lse_ref, ...), custom_call_target="tpu_custom_call" | custom-call | tf_op jit(solution)/shard_map/attend_back/pallas_call | solution.py:130
  465.3 6.3 collective-permute-done.29.refs_3_
  471.6 3.3 gradient_block.18
  476.1 3.2 convert_reduce_fusion
  483.0 3.4 gradient_block.20
  488.6 3.8 gradient_block.22
  496.5 4.8 gradient_block.19
  501.3 8.1 embed_back.1
  510.8 35.0 %collective-permute-done.31.refs_3_ = bf16[256,4096]{1,0:T(8,128)(2,1)} collective-permute-done((bf16[256,4096]{1,0:T(8,128)(2,1)}, bf16[256,4096]{1,0:T(8,128)(2,1)}, u32[]{:S(2)}, u32[]{:S(2)}) %collective-permute-start.31) | collective-permute-done | bytes 2097184 | tf_op jit(solution)/shard_map/ppermute | solution.py:423
  545.8 6.9 concatenate.96
  559.8 5.0 gradient_block.23
  574.8 4.2 all-to-all-start.1
  582.0 33.6 %collective-permute-done.36.refs_5_ = bf16[256,4096]{1,0:T(8,128)(2,1)} collective-permute-done((bf16[256,4096]{1,0:T(8,128)(2,1)}, bf16[256,4096]{1,0:T(8,128)(2,1)}, u32[]{:S(2)}, u32[]{:S(2)}) %collective-permute-start.36) | collective-permute-done | bytes 2097184 | tf_op jit(solution)/shard_map/ppermute | solution.py:423
  618.0 5.1 gradient_block.21
  635.8 6.9 span.3
  643.9 6.5 span.4
  651.7 6.5 span.5
  662.1 21.3 %press.1 = (f32[1,256,12288]{2,1,0:T(8,128)}, bf16[4,256,1536]{2,1,0:T(8,128)(2,1)}, bf16[4,256,1536]{2,1,0:T(8,128)(2,1)}) custom-call(s32[1]{0:T(128)} %bitcast.4.core_ref, f32[2]{0:T(128)} %pad_maximum_fusion.5.scale_ref, f32[256,4096]{1,0:T(8,128)} %get-tuple-element.121.refs_0_, f32[256,4096]{1,0:T(8,128)} %get-tuple-element.122.refs_1_, ...), custom_call_target="tpu_custom_call" | custom-call | tf_op jit(solution)/shard_map/press/pallas_call | solution.py:716
  683.5 39.3 %collective-permute-start.40 = (bf16[4,256,1536]{2,1,0:T(8,128)(2,1)}, bf16[4,256,1536]{2,1,0:T(8,128)(2,1)S(1)}, u32[]{:S(2)}, u32[]{:S(2)}) collective-permute-start(bf16[4,256,1536]{2,1,0:T(8,128)(2,1)} %get-tuple-element.125), channel_id=1, source_target_pairs={{0,4},{4,0},{8,12},{12,8},{16,20},{20,16},{24,28},{28,24},{1,5},{5... | collective-permute-start | bytes 9437192 | tf_op jit(solution)/shard_map/ppermute | solution.py:785
  722.7 5.5 collective-permute-done.40
  728.2 3.7 fusion.53
  734.0 9.9 %collective-permute-done.42 = bf16[128,1536]{1,0:T(8,128)(2,1)S(1)} collective-permute-done((bf16[128,1536]{1,0:T(8,128)(2,1)S(1)}, bf16[128,1536]{1,0:T(8,128)(2,1)S(1)}, u32[]{:S(2)}, u32[]{:S(2)}) %collective-permute-start.42) | collective-permute-done | bytes 393248 | tf_op jit(solution)/shard_map/ppermute | solution.py:785
  747.8 4.0 collective-permute-done.41
  751.8 6.3 collective-permute-done.43
  761.3 3.2 collective-permute-done.44
  764.5 3.1 collective-permute-done.46
  779.8 36.2 %add_rows.1.grad_ref = f32[7632,128]{1,0:T(8,128)} custom-call(s32[16384]{0:T(1024)} %copy-done.39, bf16[4,4624,128]{2,1,0:T(8,128)(2,1)} %bitcast.188), custom_call_target="tpu_custom_call" | custom-call | tf_op jit(solution)/shard_map/add_rows/pallas_call | solution.py:614
  816.1 12.4 %update.1 = (f32[7632,128]{1,0:T(8,128)}, f32[7632,128]{1,0:T(8,128)}, f32[1,128]{1,0:T(1,128)}, f32[1,128]{1,0:T(1,128)}) custom-call(f32[7632,128]{1,0:T(8,128)} %add_rows.1.grad_ref, bf16[7632,128]{1,0:T(8,128)(2,1)} %bitcast.191, f32[7632,128]{1,0:T(8,128)} %table_ref.3, f32[7632,128]{1,0:T(8,128)} %first_ref.1, f32[7632,128]{1,0:T(8,128)} %second_ref.1), custom_call_target="tpu_custom_call" | custom-call | tf_op jit(solution)/shard_map/update/pallas_call | solution.py:761
  833.5 3.2 multiply_reduce_fusion.8
  847.0 3.5 collective-permute-done.50
  850.9 4.0 collective-permute-done.51
  864.7 4.4 multiply_subtract_fusion.2
  869.0 4.6 multiply_subtract_fusion
  873.7 5.9 multiply_subtract_fusion.1
  879.6 9.1 %convert_element_type.365 = f32[256,12288]{1,0:T(8,128)} convert(bf16[256,12288]{1,0:T(8,128)(2,1)} %all-gather.13.cloned.1.call-done) | non-fusion elementwise | flops 3145728 | bytes 18874368 | tf_op jit(solution)/shard_map/convert_element_type | solution.py:996
  (427 shorter events, 198.4 us)
Async XLA Ops:
  7.2 218.5 %all-gather.7.cloned.1.call-start = ((), (), s32[]{:S(2)}) async-start(), calls=%async_computation.3 | async-start | bytes 28311552 | tf_op jit(solution)/shard_map/all_gather | solution.py:856
  8.0 1.3 collective-permute-start.6
  10.1 4.7 collective-permute-start.7
  14.9 8.3 collective-permute-start.8
  18.5 59.6 %collective-permute-start.3 = (bf16[256,1536]{1,0:T(8,128)(2,1)S(1)}, bf16[256,1536]{1,0:T(8,128)(2,1)S(1)}, u32[]{:S(2)}, u32[]{:S(2)}) collective-permute-start(bf16[256,1536]{1,0:T(8,128)(2,1)S(1)} %convert_element_type.288), channel_id=1, source_target_pairs={{0,3},{1,0},{2,1},{3,2},{4,7},{5,4},{6,5},{7,6},{8,11},{9,8},{10,9... | collective-permute-start | bytes 2359304 | tf_op jit(solution)/shard_map/ppermute | solution.py:318
  22.1 66.2 %collective-permute-start.4 = (bf16[256,1536]{1,0:T(8,128)(2,1)S(1)}, bf16[256,1536]{1,0:T(8,128)(2,1)S(1)}, u32[]{:S(2)}, u32[]{:S(2)}) collective-permute-start(bf16[256,1536]{1,0:T(8,128)(2,1)S(1)} %convert_element_type.288), channel_id=1, source_target_pairs={{0,2},{1,3},{2,0},{3,1},{4,6},{5,7},{6,4},{7,5},{8,10},{9,11},{10,... | collective-permute-start | bytes 2359304 | tf_op jit(solution)/shard_map/ppermute | solution.py:318
  22.1 66.2 %collective-permute-start.5 = (bf16[256,1536]{1,0:T(8,128)(2,1)S(1)}, bf16[256,1536]{1,0:T(8,128)(2,1)S(1)}, u32[]{:S(2)}, u32[]{:S(2)}) collective-permute-start(bf16[256,1536]{1,0:T(8,128)(2,1)S(1)} %convert_element_type.288), channel_id=1, source_target_pairs={{0,1},{1,2},{2,3},{3,0},{4,5},{5,6},{6,7},{7,4},{8,9},{9,10},{10,1... | collective-permute-start | bytes 2359304 | tf_op jit(solution)/shard_map/ppermute | solution.py:318
  25.7 52.4 %copy-start.39 = (s32[16384]{0:T(1024)}, s32[16384]{0:T(1024)S(1)}, u32[]{:S(2)}) copy-start(s32[16384]{0:T(1024)S(1)} %fusion.66.ids_ref) | copy-start | bytes 196612
  93.4 24.7 %collective-permute-start.10 = (bf16[1792,128]{1,0:T(8,128)(2,1)S(1)}, bf16[1792,128]{1,0:T(8,128)(2,1)S(1)}, u32[]{:S(2)}, u32[]{:S(2)}) collective-permute-start(bf16[1792,128]{1,0:T(8,128)(2,1)S(1)} %get-tuple-element.205), channel_id=1, source_target_pairs={{0,2},{1,3},{2,0},{3,1},{4,6},{5,7},{6,4},{7,5},{8,10},{9,11},{10,... | collective-permute-start | bytes 1376264 | tf_op jit(solution)/shard_map/ppermute | solution.py:348
  96.3 30.8 %collective-permute-start.11 = (bf16[1792,128]{1,0:T(8,128)(2,1)S(1)}, bf16[1792,128]{1,0:T(8,128)(2,1)S(1)}, u32[]{:S(2)}, u32[]{:S(2)}) collective-permute-start(bf16[1792,128]{1,0:T(8,128)(2,1)S(1)} %get-tuple-element.204), channel_id=1, source_target_pairs={{0,3},{1,0},{2,1},{3,2},{4,7},{5,4},{6,5},{7,6},{8,11},{9,8},{10,9... | collective-permute-start | bytes 1376264 | tf_op jit(solution)/shard_map/ppermute | solution.py:348
  96.7 30.3 %collective-permute-start.9 = (bf16[1792,128]{1,0:T(8,128)(2,1)S(1)}, bf16[1792,128]{1,0:T(8,128)(2,1)S(1)}, u32[]{:S(2)}, u32[]{:S(2)}) collective-permute-start(bf16[1792,128]{1,0:T(8,128)(2,1)S(1)} %get-tuple-element.206), channel_id=1, source_target_pairs={{0,1},{1,2},{2,3},{3,0},{4,5},{5,6},{6,7},{7,4},{8,9},{9,10},{10,1... | collective-permute-start | bytes 1376264 | tf_op jit(solution)/shard_map/ppermute | solution.py:348
  137.2 34.2 %all-to-all-start = ((bf16[8,512,128]{2,1,0:T(8,128)(2,1)}), bf16[8,512,128]{2,1,0:T(8,128)(2,1)S(1)}, u32[]{:S(2)}, u32[]{:S(2)}) async-start(bf16[8,512,128]{2,1,0:T(8,128)(2,1)} %bitcast.190), calls=%async_computation | async-start | bytes 2097152 | tf_op jit(solution)/shard_map/all_to_all | solution.py:866
  140.8 178.8 %all-gather.9.cloned.1.call-start = ((), (), s32[]{:S(2)}) async-start(), calls=%async_computation.4 | async-start | bytes 17584128 | tf_op jit(solution)/shard_map/all_gather | solution.py:885
  141.4 6.5 collective-permute-start.12
  141.8 29.0 %collective-permute-start.15 = (s32[1,592]{1,0:T(1,128)S(1)}, s32[1,592]{1,0:T(1,128)S(1)}, u32[]{:S(2)}, u32[]{:S(2)}) collective-permute-start(s32[1,592]{1,0:T(1,128)S(1)} %pad_add_fusion.3), channel_id=1, source_target_pairs={{0,0},{1,4},{2,1},{3,5},{4,2},{5,6},{6,3},{7,7},{8,8},{9,12},{10,9... | collective-permute-start | bytes 7112 | tf_op jit(solution)/shard_map/ppermute | solution.py:469
  149.2 16.7 %collective-permute-start.13 = (f32[]{:T(128)}, f32[]{:T(128)}, u32[]{:S(2)}, u32[]{:S(2)}) collective-permute-start(f32[]{:T(128)} %add.630), channel_id=1, source_target_pairs={{0,8},{4,12},{8,0},{12,4},{16,24},{20,28},{24,16},{28,20},{1,9},{5... | collective-permute-start | bytes 20 | tf_op jit(solution)/shard_map/ppermute | solution.py:308
  166.5 3.7 collective-permute-start.14
  176.8 70.2 %copy-start.22 = (f32[512,1024]{1,0:T(8,128)}, f32[512,1024]{1,0:T(8,128)S(1)}, u32[]{:S(2)}) copy-start(f32[512,1024]{1,0:T(8,128)S(1)} %get-tuple-element.178.embedded_ref) | copy-start | bytes 6291460
  176.9 51.1 %copy-start.68 = (f32[1,1024]{1,0:T(1,128)S(1)}, f32[1,1024]{1,0:T(1,128)}, u32[]{:S(2)}) copy-start(f32[1,1024]{1,0:T(1,128)} %get-tuple-element.197) | copy-start | bytes 12292
  176.9 51.1 %copy-start.69 = (f32[1,1024]{1,0:T(1,128)S(1)}, f32[1,1024]{1,0:T(1,128)}, u32[]{:S(2)}) copy-start(f32[1,1024]{1,0:T(1,128)} %get-tuple-element.198) | copy-start | bytes 12292
  176.9 51.9 %copy-start.78 = (s32[1,80]{1,0:T(1,128)S(1)}, s32[1,80]{1,0:T(1,128)}, u32[]{:S(2)}) copy-start(s32[1,80]{1,0:T(1,128)} %slice.194) | copy-start | bytes 964
  177.3 58.0 %copy-start.9 = (bf16[512,1024]{1,0:T(8,128)(2,1)}, bf16[512,1024]{1,0:T(8,128)(2,1)S(1)}, u32[]{:S(2)}) copy-start(bf16[512,1024]{1,0:T(8,128)(2,1)S(1)} %fusion.31.refs_0_) | copy-start | bytes 3145732
  225.7 410.0 %reduce-scatter.2.cloned.1.call-start = ((), (), s32[]{:S(2)}) async-start(), calls=%async_computation.5 | async-start | bytes 17584128 | tf_op jit(solution)/shard_map/reduce_scatter | solution.py:920
  251.4 194.1 %copy-start.18 = (bf16[512,1024]{1,0:T(8,128)(2,1)}, bf16[512,1024]{1,0:T(8,128)(2,1)S(1)}, u32[]{:S(2)}) copy-start(bf16[512,1024]{1,0:T(8,128)(2,1)S(1)} %fusion.30.refs_0_) | copy-start | bytes 3145732
  293.1 7.6 collective-permute-start.16
  293.9 18.5 %collective-permute-start.17 = (bf16[80,1024]{1,0:T(8,128)(2,1)}, bf16[80,1024]{1,0:T(8,128)(2,1)}, u32[]{:S(2)}, u32[]{:S(2)}) collective-permute-start(bf16[80,1024]{1,0:T(8,128)(2,1)} %get-tuple-element.174), channel_id=1, source_target_pairs={{0,2},{1,3},{2,0},{3,1},{4,6},{5,7},{6,4},{7,5},{8,10},{9,11},{10,... | collective-permute-start | bytes 491528 | tf_op jit(solution)/shard_map/ppermute | solution.py:318
  297.4 16.6 %collective-permute-start.18 = (bf16[80,1024]{1,0:T(8,128)(2,1)}, bf16[80,1024]{1,0:T(8,128)(2,1)S(1)}, u32[]{:S(2)}, u32[]{:S(2)}) collective-permute-start(bf16[80,1024]{1,0:T(8,128)(2,1)} %get-tuple-element.174), channel_id=1, source_target_pairs={{0,1},{1,2},{2,3},{3,0},{4,5},{5,6},{6,7},{7,4},{8,9},{9,10},{10,1... | collective-permute-start | bytes 491528 | tf_op jit(solution)/shard_map/ppermute | solution.py:318
  337.4 3.7 collective-permute-start.19
  337.7 4.6 collective-permute-start.20
  337.8 5.8 collective-permute-start.21
  358.2 21.7 %collective-permute-start.22 = (bf16[80,1024]{1,0:T(8,128)(2,1)}, bf16[80,1024]{1,0:T(8,128)(2,1)}, u32[]{:S(2)}, u32[]{:S(2)}) collective-permute-start(bf16[80,1024]{1,0:T(8,128)(2,1)} %get-tuple-element.207), channel_id=1, source_target_pairs={{0,1},{1,2},{2,3},{3,0},{4,5},{5,6},{6,7},{7,4},{8,9},{9,10},{10,1... | collective-permute-start | bytes 491528 | tf_op jit(solution)/shard_map/ppermute | solution.py:335
  358.7 21.2 %collective-permute-start.23 = (bf16[80,1024]{1,0:T(8,128)(2,1)}, bf16[80,1024]{1,0:T(8,128)(2,1)}, u32[]{:S(2)}, u32[]{:S(2)}) collective-permute-start(bf16[80,1024]{1,0:T(8,128)(2,1)} %get-tuple-element.209), channel_id=1, source_target_pairs={{0,2},{1,3},{2,0},{3,1},{4,6},{5,7},{6,4},{7,5},{8,10},{9,11},{10,... | collective-permute-start | bytes 491528 | tf_op jit(solution)/shard_map/ppermute | solution.py:335
  360.8 19.2 %collective-permute-start.24 = (bf16[80,1024]{1,0:T(8,128)(2,1)}, bf16[80,1024]{1,0:T(8,128)(2,1)}, u32[]{:S(2)}, u32[]{:S(2)}) collective-permute-start(bf16[80,1024]{1,0:T(8,128)(2,1)} %get-tuple-element.208), channel_id=1, source_target_pairs={{0,3},{1,0},{2,1},{3,2},{4,7},{5,4},{6,5},{7,6},{8,11},{9,8},{10,9... | collective-permute-start | bytes 491528 | tf_op jit(solution)/shard_map/ppermute | solution.py:335
  397.0 16.7 %collective-permute-start.26 = (bf16[256,4096]{1,0:T(8,128)(2,1)}, bf16[256,4096]{1,0:T(8,128)(2,1)S(1)}, u32[]{:S(2)}, u32[]{:S(2)}) collective-permute-start(bf16[256,4096]{1,0:T(8,128)(2,1)} %gradient_block.13), channel_id=1, source_target_pairs={{0,4},{4,0},{8,12},{12,8},{16,20},{20,16},{24,28},{28,24},{1,5},{5... | collective-permute-start | bytes 6291464 | tf_op jit(solution)/shard_map/ppermute | solution.py:408
  399.4 15.7 %collective-permute-start.25 = (bf16[256,4096]{1,0:T(8,128)(2,1)S(1)}, bf16[256,4096]{1,0:T(8,128)(2,1)S(1)}, u32[]{:S(2)}, u32[]{:S(2)}) collective-permute-start(bf16[256,4096]{1,0:T(8,128)(2,1)S(1)} %gradient_block.12), channel_id=1, source_target_pairs={{0,4},{4,0},{8,12},{12,8},{16,20},{20,16},{24,28},{28,24},{1,5},{5... | collective-permute-start | bytes 6291464 | tf_op jit(solution)/shard_map/ppermute | solution.py:407
  423.4 20.7 %collective-permute-start.28 = (bf16[256,4096]{1,0:T(8,128)(2,1)}, bf16[256,4096]{1,0:T(8,128)(2,1)S(1)}, u32[]{:S(2)}, u32[]{:S(2)}) collective-permute-start(bf16[256,4096]{1,0:T(8,128)(2,1)} %gradient_block.16), channel_id=1, source_target_pairs={{0,4},{4,0},{8,12},{12,8},{16,20},{20,16},{24,28},{28,24},{1,5},{5... | collective-permute-start | bytes 6291464 | tf_op jit(solution)/shard_map/ppermute | solution.py:408
  423.5 21.9 %collective-permute-start.27 = (bf16[256,4096]{1,0:T(8,128)(2,1)S(1)}, bf16[256,4096]{1,0:T(8,128)(2,1)S(1)}, u32[]{:S(2)}, u32[]{:S(2)}) collective-permute-start(bf16[256,4096]{1,0:T(8,128)(2,1)S(1)} %gradient_block.15), channel_id=1, source_target_pairs={{0,4},{4,0},{8,12},{12,8},{16,20},{20,16},{24,28},{28,24},{1,5},{5... | collective-permute-start | bytes 6291464 | tf_op jit(solution)/shard_map/ppermute | solution.py:407
  424.0 47.6 %collective-permute-start.29 = (bf16[256,4096]{1,0:T(8,128)(2,1)S(1)}, bf16[256,4096]{1,0:T(8,128)(2,1)S(1)}, u32[]{:S(2)}, u32[]{:S(2)}) collective-permute-start(bf16[256,4096]{1,0:T(8,128)(2,1)S(1)} %gradient_block.14), channel_id=1, source_target_pairs={{0,1},{1,0},{2,3},{3,2},{4,5},{5,4},{6,7},{7,6},{8,9},{9,8},{10,11... | collective-permute-start | bytes 6291464 | tf_op jit(solution)/shard_map/ppermute | solution.py:423
  475.0 21.5 %collective-permute-start.30 = (bf16[256,4096]{1,0:T(8,128)(2,1)}, bf16[256,4096]{1,0:T(8,128)(2,1)}, u32[]{:S(2)}, u32[]{:S(2)}) collective-permute-start(bf16[256,4096]{1,0:T(8,128)(2,1)} %gradient_block.18), channel_id=1, source_target_pairs={{0,4},{4,0},{8,12},{12,8},{16,20},{20,16},{24,28},{28,24},{1,5},{5... | collective-permute-start | bytes 6291464 | tf_op jit(solution)/shard_map/ppermute | solution.py:407
  475.0 70.8 %collective-permute-start.31 = (bf16[256,4096]{1,0:T(8,128)(2,1)}, bf16[256,4096]{1,0:T(8,128)(2,1)}, u32[]{:S(2)}, u32[]{:S(2)}) collective-permute-start(bf16[256,4096]{1,0:T(8,128)(2,1)} %gradient_block.17), channel_id=1, source_target_pairs={{0,1},{1,0},{2,3},{3,2},{4,5},{5,4},{6,7},{7,6},{8,9},{9,8},{10,11... | collective-permute-start | bytes 6291464 | tf_op jit(solution)/shard_map/ppermute | solution.py:423
  492.4 131.5 %collective-permute-start.38 = (bf16[256,4096]{1,0:T(8,128)(2,1)}, bf16[256,4096]{1,0:T(8,128)(2,1)}, u32[]{:S(2)}, u32[]{:S(2)}) collective-permute-start(bf16[256,4096]{1,0:T(8,128)(2,1)} %gradient_block.22), channel_id=1, source_target_pairs={{2,4},{3,5},{4,2},{5,3},{10,12},{11,13},{12,10},{13,11},{18,20},{1... | collective-permute-start | bytes 6291464 | tf_op jit(solution)/shard_map/ppermute | solution.py:447
  494.6 87.5 %collective-permute-start.35 = (bf16[256,4096]{1,0:T(8,128)(2,1)}, bf16[256,4096]{1,0:T(8,128)(2,1)}, u32[]{:S(2)}, u32[]{:S(2)}) collective-permute-start(bf16[256,4096]{1,0:T(8,128)(2,1)} %gradient_block.20), channel_id=1, source_target_pairs={{0,4},{4,0},{8,12},{12,8},{16,20},{20,16},{24,28},{28,24},{1,5},{5... | collective-permute-start | bytes 6291464 | tf_op jit(solution)/shard_map/ppermute | solution.py:408
  545.8 69.8 %collective-permute-start.36 = (bf16[256,4096]{1,0:T(8,128)(2,1)}, bf16[256,4096]{1,0:T(8,128)(2,1)}, u32[]{:S(2)}, u32[]{:S(2)}) collective-permute-start(bf16[256,4096]{1,0:T(8,128)(2,1)} %gradient_block.19), channel_id=1, source_target_pairs={{0,1},{1,0},{2,3},{3,2},{4,5},{5,4},{6,7},{7,6},{8,9},{9,8},{10,11... | collective-permute-start | bytes 6291464 | tf_op jit(solution)/shard_map/ppermute | solution.py:423
  554.8 14.2 %collective-permute-start.32 = (bf16[528,512]{1,0:T(8,128)(2,1)}, bf16[528,512]{1,0:T(8,128)(2,1)}, u32[]{:S(2)}, u32[]{:S(2)}) collective-permute-start(bf16[528,512]{1,0:T(8,128)(2,1)} %dynamic-slice_convert_fusion), channel_id=1, source_target_pairs={{0,16},{4,20},{8,24},{12,28},{16,0},{20,4},{24,8},{28,12},{1,17},{... | collective-permute-start | bytes 1622024 | tf_op jit(solution)/shard_map/ppermute | solution.py:812
  564.9 64.6 %collective-permute-start.39 = (bf16[256,4096]{1,0:T(8,128)(2,1)}, bf16[256,4096]{1,0:T(8,128)(2,1)}, u32[]{:S(2)}, u32[]{:S(2)}) collective-permute-start(bf16[256,4096]{1,0:T(8,128)(2,1)} %gradient_block.23), channel_id=1, source_target_pairs={{2,4},{3,5},{4,2},{5,3},{10,12},{11,13},{12,10},{13,11},{18,20},{1... | collective-permute-start | bytes 6291464 | tf_op jit(solution)/shard_map/ppermute | solution.py:447
  572.0 8.8 collective-permute-start.33
  574.8 52.3 %all-to-all-start.1 = ((bf16[8,512,128]{2,1,0:T(8,128)(2,1)}), bf16[8,512,128]{2,1,0:T(8,128)(2,1)}, u32[]{:S(2)}, u32[]{:S(2)}) async-start(bf16[8,512,128]{2,1,0:T(8,128)(2,1)} %bitcast_bitcast_fusion), calls=%async_computation.1 | async-start | bytes 2097152 | tf_op jit(solution)/shard_map/all_to_all | solution.py:936
  579.1 193.8 %all-gather.15.cloned.1.call-start = ((), (), s32[]{:S(2)}) async-start(), calls=%async_computation.8 | async-start | bytes 5918720 | tf_op jit(solution)/shard_map/all_gather | solution.py:943
  581.9 45.2 %collective-permute-start.34 = (bf16[528,128]{1,0:T(8,128)(2,1)S(1)}, bf16[528,128]{1,0:T(8,128)(2,1)S(1)}, u32[]{:S(2)}, u32[]{:S(2)}) collective-permute-start(bf16[528,128]{1,0:T(8,128)(2,1)S(1)} %dynamic-slice_convert_fusion.5), channel_id=1, source_target_pairs={{0,4},{4,0},{8,12},{12,8},{16,20},{20,16},{24,28},{28,24},{1,5},{5... | collective-permute-start | bytes 405512 | tf_op jit(solution)/shard_map/ppermute | solution.py:812
  623.1 9.4 %collective-permute-start.37 = (bf16[256,4096]{1,0:T(8,128)(2,1)}, bf16[256,4096]{1,0:T(8,128)(2,1)S(1)}, u32[]{:S(2)}, u32[]{:S(2)}) collective-permute-start(bf16[256,4096]{1,0:T(8,128)(2,1)} %gradient_block.21), channel_id=1, source_target_pairs={{2,4},{3,5},{4,2},{5,3},{10,12},{11,13},{12,10},{13,11},{18,20},{1... | collective-permute-start | bytes 6291464 | tf_op jit(solution)/shard_map/ppermute | solution.py:447
  635.7 237.9 %all-gather.11.cloned.1.call-start = ((), (), s32[]{:S(2)}) async-start(), calls=%async_computation.6 | async-start | bytes 1216512 | tf_op jit(solution)/shard_map/all_gather | solution.py:998
  683.5 44.8 %collective-permute-start.40 = (bf16[4,256,1536]{2,1,0:T(8,128)(2,1)}, bf16[4,256,1536]{2,1,0:T(8,128)(2,1)S(1)}, u32[]{:S(2)}, u32[]{:S(2)}) collective-permute-start(bf16[4,256,1536]{2,1,0:T(8,128)(2,1)} %get-tuple-element.125), channel_id=1, source_target_pairs={{0,4},{4,0},{8,12},{12,8},{16,20},{20,16},{24,28},{28,24},{1,5},{5... | collective-permute-start | bytes 9437192 | tf_op jit(solution)/shard_map/ppermute | solution.py:785
  731.9 11.9 %collective-permute-start.42 = (bf16[128,1536]{1,0:T(8,128)(2,1)S(1)}, bf16[128,1536]{1,0:T(8,128)(2,1)S(1)}, u32[]{:S(2)}, u32[]{:S(2)}) collective-permute-start(bf16[128,1536]{1,0:T(8,128)(2,1)S(1)} %get-tuple-element.190), channel_id=1, source_target_pairs={{0,8},{4,12},{8,0},{12,4},{16,24},{20,28},{24,16},{28,20},{1,9},{5... | collective-permute-start | bytes 1179656 | tf_op jit(solution)/shard_map/ppermute | solution.py:785
  733.4 18.4 %collective-permute-start.41 = (bf16[128,1536]{1,0:T(8,128)(2,1)}, bf16[128,1536]{1,0:T(8,128)(2,1)S(1)}, u32[]{:S(2)}, u32[]{:S(2)}) collective-permute-start(bf16[128,1536]{1,0:T(8,128)(2,1)} %get-tuple-element.187), channel_id=1, source_target_pairs={{0,8},{4,12},{8,0},{12,4},{16,24},{20,28},{24,16},{28,20},{1,9},{5... | collective-permute-start | bytes 1179656 | tf_op jit(solution)/shard_map/ppermute | solution.py:785
  734.0 17.8 %collective-permute-start.45 = (bf16[128,1536]{1,0:T(8,128)(2,1)}, bf16[128,1536]{1,0:T(8,128)(2,1)}, u32[]{:S(2)}, u32[]{:S(2)}) collective-permute-start(bf16[128,1536]{1,0:T(8,128)(2,1)} %get-tuple-element.188), channel_id=1, source_target_pairs={{0,16},{4,20},{8,24},{12,28},{16,0},{20,4},{24,8},{28,12},{1,17},{... | collective-permute-start | bytes 1179656 | tf_op jit(solution)/shard_map/ppermute | solution.py:785
  745.8 12.3 %collective-permute-start.43 = (bf16[128,1536]{1,0:T(8,128)(2,1)}, bf16[128,1536]{1,0:T(8,128)(2,1)S(1)}, u32[]{:S(2)}, u32[]{:S(2)}) collective-permute-start(bf16[128,1536]{1,0:T(8,128)(2,1)} %fusion.48), channel_id=1, source_target_pairs={{0,16},{4,20},{8,24},{12,28},{16,0},{20,4},{24,8},{28,12},{1,17},{... | collective-permute-start | bytes 1179656 | tf_op jit(solution)/shard_map/ppermute | solution.py:785
  745.8 18.8 %collective-permute-start.44 = (bf16[128,1536]{1,0:T(8,128)(2,1)}, bf16[128,1536]{1,0:T(8,128)(2,1)S(1)}, u32[]{:S(2)}, u32[]{:S(2)}) collective-permute-start(bf16[128,1536]{1,0:T(8,128)(2,1)} %get-tuple-element.189), channel_id=1, source_target_pairs={{0,16},{4,20},{8,24},{12,28},{16,0},{20,4},{24,8},{28,12},{1,17},{... | collective-permute-start | bytes 1179656 | tf_op jit(solution)/shard_map/ppermute | solution.py:785
  759.9 7.8 collective-permute-start.46
  774.8 104.7 %all-gather.13.cloned.1.call-start = ((), (), s32[]{:S(2)}) async-start(), calls=%async_computation.7 | async-start | bytes 7077888 | tf_op jit(solution)/shard_map/all_gather | solution.py:996
  838.8 1.1 collective-permute-start.47
  839.9 3.5 collective-permute-start.48
  843.4 3.5 collective-permute-start.49
  847.0 3.5 collective-permute-start.50
  850.5 4.4 collective-permute-start.51
  (74 other events, 669.2 us)
Sparse Core Ops, SparseCore 0:
  90.7 134.9 all-gather.6
  228.2 88.2 all-gather.8
  382.2 110.9 reduce-scatter.1
  635.9 126.9 all-gather.14
  775.0 22.3 all-gather.10
  799.2 45.5 all-gather.12

commit v10 on v9

--- a/solution.py
+++ b/solution.py
@@ -39,10 +39,6 @@
     cent = x - mean
     var = jnp.mean(cent * cent, axis=-1, keepdims=True)
     return cent * lax.rsqrt(var + LN_EPS) * gain + shift
-
-
-def gelu_exact(upper):
-    return jax.nn.gelu(upper, approximate=False)
 
 
 def matmul(left, right):
@@ -219,6 +215,35 @@
     )(dqkv, weights, drone, embedded, gain[None], even)
 
 
+def ffn_kernel(fin_ref, weight_ref, bias_ref, gated_ref, slope_ref):
+    upper = matmul(fin_ref[...], weight_ref[...]) + bias_ref[...]
+    below = 0.5 + 0.5 * lax.erf(upper * 0.7071067811865476)
+    gated_ref[...] = (upper * below).astype(jnp.bfloat16)
+    density = 0.3989422804014327 * jnp.exp(-0.5 * upper * upper)
+    slope_ref[...] = (below + upper * density).astype(jnp.bfloat16)
+
+
+def ffn_up(fin, weights, bias):
+    tokens = fin.shape[0]
+    block = 512
+    first = 4 * D // block
+    out = pl.BlockSpec((tokens, block), lambda step: (0, step))
+    return pl.pallas_call(
+        ffn_kernel,
+        grid=(FF // block,),
+        in_specs=[
+            pl.BlockSpec((tokens, D), lambda step: (0, 0)),
+            pl.BlockSpec((D, block), lambda step: (0, first + step)),
+            pl.BlockSpec((1, block), lambda step: (0, step)),
+        ],
+        out_specs=[out, out],
+        out_shape=[jax.ShapeDtypeStruct((tokens, FF), jnp.bfloat16)] * 2,
+        compiler_params=pltpu.CompilerParams(vmem_limit_bytes=32 * 2**20),
+        cost_estimate=pl.CostEstimate(flops=2 * tokens * D * FF, bytes_accessed=0, transcendentals=0),
+        name="ffn_up",
+    )(fin, weights, bias)
+
+
 def layer_forward(embedded, x0, act, docs, small, weights):
     base = L + 2
     bias = jnp.concatenate([small[base + 6], jnp.zeros((D,), jnp.float32), small[base + 7]])
@@ -227,23 +252,21 @@
     rone = x0 + (matmul(out, weights[:, 3 * D : 4 * D]) + small[base + 8])
     hone = norm_rows(rone, small[base + 2], small[base + 3])
     fin = hone.astype(jnp.bfloat16)
-    upper = matmul(fin, weights[:, 4 * D : 4 * D + FF]) + small[base + 10 :].reshape(FF)
-    gated = gelu_exact(upper).astype(jnp.bfloat16)
+    gated, slope = ffn_up(fin, weights, small[base + 10 :].reshape(1, FF))
     rtwo = hone + (matmul_nt(gated, weights[:, 4 * D + FF :]) + small[base + 9])
     htwo = norm_rows(rtwo, small[base + 4], small[base + 5])
-    return (htwo, (embedded, act, qkv, lse, out, rone, fin, upper, gated, rtwo))
+    return (htwo, (embedded, act, qkv, lse, out, rone, fin, slope, gated, rtwo))
 
 
 def layer_backward(dhtwo, kept, docs, small, weights):
-    embedded, act, qkv, lse, out, rone, fin, upper, gated, rtwo = kept
+    embedded, act, qkv, lse, out, rone, fin, slope, gated, rtwo = kept
     base = L + 2
     _, pull = jax.vjp(norm_rows, rtwo, small[base + 4], small[base + 5])
     drtwo, dgain_two, dshift_two = pull(dhtwo)
     dffn = drtwo.astype(jnp.bfloat16)
     down = WorkerPiece((dffn, gated))
     dgated = matmul(dffn, weights[:, 4 * D + FF :])
-    _, pull = jax.vjp(gelu_exact, upper)
-    dupper = pull(dgated)[0].astype(jnp.bfloat16)
+    dupper = (dgated * slope.astype(jnp.float32)).astype(jnp.bfloat16)
     dupper = down.received(dupper)
     dupper = down.across(dupper)
     up = WorkerPiece((fin, dupper))
@@ -318,9 +341,11 @@
         around.append(lax.ppermute(value, "narrow", cycle(size, size - by)))
     if beside is not None:
         *around, beside = together(*around, beside)
-    twice = jnp.concatenate(around + around[:-1], axis=0)
-    start = lax.rem(size - lax.axis_index("narrow"), size) * rows
-    whole = lax.dynamic_slice_in_dim(twice, start, size * rows, 0)
+    place = lax.axis_index("narrow")
+    whole = jnp.zeros((size * rows,) + value.shape[1:], value.dtype)
+    for by, part in enumerate(around):
+        start = lax.rem(place + by, size) * rows
+        whole = lax.dynamic_update_slice_in_dim(whole, part, start, 0)
     return whole if beside is None else (whole, beside)
 
 
@@ -661,7 +686,7 @@
             jax.ShapeDtypeStruct((1, block), jnp.float32),
         ],
         compiler_params=pltpu.CompilerParams(vmem_limit_bytes=60 * 2**20),
-        cost_estimate=FREE,
+        cost_estimate=pl.CostEstimate(flops=0, bytes_accessed=2 * 10**7, transcendentals=0),
         name="span",
     )(momentum, grad, error)
     return span, jnp.sum(sums)
@@ -937,8 +962,10 @@
         halved = small_halved(small_grad).astype(jnp.bfloat16)
         down, up = pieces[2], pieces[1]
         mixed.finish()
-        cut, mixed.result, down.result, up.result, table_head = together(
-            jnp.concatenate([cut, halved]), mixed.result, down.result, up.result, table_head
+        spans = [span_of(layer_m, up.result, worker_err, 4 * D)]
+        spans.append(span_of(layer_m, down.result, worker_err, 8 * D))
+        cut, mixed.result, spans, table_head = together(
+            jnp.concatenate([cut, halved]), mixed.result, spans, table_head
         )
         group_rows = lax.all_gather(cut, "narrow", axis=0)
     else:
@@ -952,11 +979,9 @@
         table_grad = table_grad.astype(jnp.float32)
     part_cols = layer.shape[1]
     if paired:
-        spans, total, start = [], 0.0, [0, 4 * D, 8 * D]
-        for piece, first in zip(pieces[::-1], start[::-1]):
-            span, amount = span_of(layer_m, piece.result, worker_err, first)
-            spans.insert(0, span)
-            total = total + amount
+        spans.insert(0, span_of(layer_m, mixed.result, worker_err, 0))
+        total = sum(amount for _, amount in spans)
+        spans = [span for span, _ in spans]
         scale = total / (layer_m.shape[0] * layer_m.shape[1]) + MAG_EPS
         new_worker, give, keep = pressed(spans, scale, n_wide)
         server_in = scattered_sum(give, keep) / n_wide + server_err
@@ -993,8 +1018,9 @@
         table_mom = BETA * table_m + (1.0 - BETA) * table_grad
         table_upd = table_mom / (jnp.sqrt(table_v) + OPT_EPS) + DECAY * table
         table_norms = (jnp.sum(table * table)[None], jnp.sum(table_upd * table_upd)[None])
-    new_m = lax.all_gather(server_low, "wide", axis=1, tiled=True).astype(jnp.float32)
+    new_m = lax.all_gather(server_low, "wide", axis=1, tiled=True)
     if paired:
+        small_grad, new_m = together(small_grad, new_m)
         small_grad = lax.all_gather(small_grad, "wide", axis=1, tiled=True)
     small_mom, small_upd = small_update(small_grad, small_m, small_v, small)
     if not paired:
@@ -1025,7 +1051,7 @@
         new_small,
         small_mom,
         new_layer,
-        new_m,
+        new_m.astype(jnp.float32),
         new_worker,
         new_server,
         jnp.stack([wnorm, unorm]),

time: 903 us -> 902 us (level)
  matrix products: 115 us -> 80 us
  starting transfers between devices: 111 us -> 145 us
  Pallas kernels: 227 us -> 243 us
  other arithmetic: 120 us -> 108 us
    dot_general x5 -> x4, matrix products: 61.7 us -> 29.6 us  [matmul(): return jnp.dot(left, right, preferred_element_type=jnp.float32)]
    ppermute x7, starting transfers between devices: 44.8 us -> 64.9 us  [send(): lax.ppermute(value.astype(jnp.bfloat16), 'wide', swap_pairs(n_wide, bit))]
    ppermute x3, waiting for transfers between devices: 74.9 us -> 56.2 us  [across(): self.away = lax.ppermute(away, 'narrow', sides)]
    all_gather x1, waiting for transfers between devices: 0.01 us -> 17.4 us  [shards(): table_cols = lax.all_gather(table_low, 'wide', axis=1, tiled=True)]
    ppermute x9, waiting for transfers between devices: 26 us -> 12.3 us  [gathered_near(): around.append(lax.ppermute(value, 'narrow', cycle(size, size - by)))]
    pallas_call x0 -> x1, Pallas kernels: none -> 11 us  [ffn_up(): pl.pallas_call(ffn_kernel, grid=(FF // block,), in_specs=[pl.BlockSpec((t...]
    all_gather x1, waiting for transfers between devices: 0.01 us -> 10.2 us  [shards(): small_grad = lax.all_gather(small_grad, 'wide', axis=1, tiled=True)]
    ppermute x3, waiting for transfers between devices: 28.7 us -> 38.9 us  [sent_around(): lax.ppermute(block(by), 'narrow', cycle(size, by))]
  transfers between devices with their start and end apart: 57 -> 57, of which waited for: 29 -> 29; matrix products, arithmetic and copies ran while one was open for 25% -> 21% of each run, Pallas kernels for 25% -> 27%
where the time goes in v10:
time: 902 us; the launch traced here: 894 us
  Pallas kernels  243 us (27%)
  waiting for transfers between devices  231 us (26%)
  starting transfers between devices  145 us (16%)
  other arithmetic  108 us (12%)
  matrix products  80 us (9%)
  local copies, waits for them, and re-layouts  59.4 us (7%)
  between operations  23.6 us (3%)
    ppermute x7, starting transfers between devices, send(): lax.ppermute(value.astype(jnp.bfloat16), 'wide', swap_pairs(n_wide, bit))  64.9 us
    ppermute x3, waiting for transfers between devices, across(): self.away = lax.ppermute(away, 'narrow', sides)  56.2 us
    pallas_call x1, Pallas kernels, packed_rows(): pl.pallas_call(pack_kernel, grid_spec=pltpu.PrefetchScalarGridSpec(num_sc...  52.4 us
    pallas_call x12, Pallas kernels, gradient_block(): pl.pallas_call(functools.partial(block_kernel, steps), grid_spec=pltpu.Pr...  48.2 us
    all_gather x1, waiting for transfers between devices, shards(): weights = lax.all_gather(layer_rows, 'wide', axis=1, tiled=True)  40.8 us
    ppermute x3, waiting for transfers between devices, sent_around(): lax.ppermute(block(by), 'narrow', cycle(size, by))  38.9 us
    pallas_call x1, Pallas kernels, added_rows(): pl.pallas_call(add_kernel, grid_spec=pltpu.PrefetchScalarGridSpec(num_sca...  36.2 us
    dot_general x4, matrix products, matmul_nt(): lax.dot_general(left, right, (((1,), (1,)), ((), ())), preferred_element_...  32.3 us
  transfers between devices with their start and end apart: 57, of which 29 were waited for; matrix products, arithmetic and copies ran while one was open for 21% of the time, Pallas kernels for 27%

profile of v10, /device:TPU:0, one launch (start us, length us, event | category | flops | bytes accessed | tf_op | source)
XLA Modules:
  0.0 894.0 jit_solution(14681479526539594808)
XLA Ops:
  26.6 52.4 %pack_rows.1 = bf16[4,4096,128]{2,1,0:T(8,128)(2,1)} custom-call(s32[16384]{0:T(1024)S(1)} %fusion.57.ids_ref, f32[7632,128]{1,0:T(8,128)S(1)} %copy-done.8), custom_call_target="tpu_custom_call" | custom-call | bytes 150000000 | tf_op jit(solution)/shard_map/pack_rows/pallas_call | solution.py:568
  87.2 10.9 %collective-permute-start.11 = (bf16[1792,128]{1,0:T(8,128)(2,1)S(1)}, bf16[1792,128]{1,0:T(8,128)(2,1)S(1)}, u32[]{:S(2)}, u32[]{:S(2)}) collective-permute-start(bf16[1792,128]{1,0:T(8,128)(2,1)S(1)} %get-tuple-element.214), channel_id=1, source_target_pairs={{0,3},{1,0},{2,1},{3,2},{4,7},{5,4},{6,5},{7,6},{8,11},{9,8},{10,9... | collective-permute-start | bytes 1376264 | tf_op jit(solution)/shard_map/ppermute | solution.py:373
  98.8 10.3 %collective-permute-done.11 = bf16[1792,128]{1,0:T(8,128)(2,1)S(1)} collective-permute-done((bf16[1792,128]{1,0:T(8,128)(2,1)S(1)}, bf16[1792,128]{1,0:T(8,128)(2,1)S(1)}, u32[]{:S(2)}, u32[]{:S(2)}) %collective-permute-start.11) | collective-permute-done | bytes 458784 | tf_op jit(solution)/shard_map/ppermute | solution.py:373
  109.1 28.5 %collective-permute-done.10 = bf16[1792,128]{1,0:T(8,128)(2,1)S(1)} collective-permute-done((bf16[1792,128]{1,0:T(8,128)(2,1)S(1)}, bf16[1792,128]{1,0:T(8,128)(2,1)S(1)}, u32[]{:S(2)}, u32[]{:S(2)}) %collective-permute-start.10) | collective-permute-done | bytes 458784 | tf_op jit(solution)/shard_map/ppermute | solution.py:373
  137.8 5.5 take_rows.3
  143.3 3.5 conditional.1
  147.7 3.6 all-to-all-start
  153.6 3.6 convert_element_type.287
  158.5 16.5 %collective-permute-start.13 = (f32[]{:T(128)}, f32[]{:T(128)}, u32[]{:S(2)}, u32[]{:S(2)}) collective-permute-start(f32[]{:T(128)} %add.645), channel_id=1, source_target_pairs={{0,8},{4,12},{8,0},{12,4},{16,24},{20,28},{24,16},{28,20},{1,9},{5... | collective-permute-start | bytes 20 | tf_op jit(solution)/shard_map/ppermute | solution.py:331
  188.0 40.8 %all-gather.7.cloned.1.call-done.weight_ref = bf16[1024,12288]{1,0:T(8,128)(2,1)} async-done(((bf16[1024,1536]{1,0:T(8,128)(2,1)}), bf16[1024,12288]{1,0:T(8,128)(2,1)}) %all-gather.7.cloned.1.call-update) | async-done | bytes 25165840 | tf_op jit(solution)/shard_map/all_gather | solution.py:881
  232.2 6.5 add_convert_fusion.q_ref.k_ref.v_ref
  238.7 11.7 %attend.1 = (bf16[512,1024]{1,0:T(8,128)(2,1)S(1)}, f32[8,2,512]{2,1,0:T(2,128)S(1)}) custom-call(bf16[512,3072]{1,0:T(8,128)(2,1)S(1)} %add_convert_fusion.q_ref.k_ref.v_ref, bf16[512,3072]{1,0:T(8,128)(2,1)S(1)} %add_convert_fusion.q_ref.k_ref.v_ref, bf16[512,3072]{1,0:T(8,128)(2,1)S(1)} %add_convert_fusion.q_ref.k_ref.v_ref, ...), custom_call_target="tpu_custom_call" | custom-call | tf_op jit(solution)/shard_map/attend/pallas_call | solution.py:82
  250.5 3.5 fusion.91
  254.8 11.0 %ffn_up.1 = (bf16[512,4096]{1,0:T(8,128)(2,1)S(1)}, bf16[512,4096]{1,0:T(8,128)(2,1)S(1)}) custom-call(bf16[512,1024]{1,0:T(8,128)(2,1)S(1)} %fusion.22.fin_ref.refs_0_, bf16[1024,12288]{1,0:T(8,128)(2,1)} %all-gather.7.cloned.1.call-done.weight_ref, f32[1,4096]{1,0:T(1,128)S(1)} %bitcast.181), custom_call_target="tpu_custom_call" | custom-call | flops 4294967296 | tf_op jit(solution)/shard_map/ffn_up/pallas_call | solution.py:231
  267.8 9.5 %fusion.92 = (f32[512]{0:T(512)S(1)}, f32[512,1024]{1,0:T(8,128)S(1)}) fusion(f32[1024]{0:T(1024)S(1)} %bitcast.223, bf16[512,4096]{1,0:T(8,128)(2,1)S(1)} %get-tuple-element.97.refs_1_, bf16[1024,12288]{1,0:T(8,128)(2,1)} %all-gather.7.cloned.1.call-done.weight_ref, f32[1024]{0:T(1024)S(1)} %bitcast.213, f32[1024]{0:T(1024)S(1)} %bitcast.207, ...), kind=kOutput, calls=%fused_computation.266 | convolution fusion | flops 4298636800 | bytes 16795648 | tf_op jit(solution)/shard_map/dot_general | solution.py:55
  289.6 5.9 collective-permute-done.16
  300.9 17.4 %all-gather.9.cloned.1.call-done = bf16[7632,1024]{1,0:T(8,128)(2,1)} async-done(((bf16[7632,128]{1,0:T(8,128)(2,1)}), bf16[7632,1024]{1,0:T(8,128)(2,1)}) %all-gather.9.cloned.1.call-update) | async-done | bytes 15630352 | tf_op jit(solution)/shard_map/all_gather | solution.py:910
  318.3 9.2 %fusion.93 = (f32[320]{0:T(512)S(1)}, f32[320,7632]{1,0:T(8,128)S(1)}) fusion(bf16[320,1024]{1,0:T(8,128)(2,1)} %constant_dynamic-update-slice_fusion.4, bf16[7632,1024]{1,0:T(8,128)(2,1)} %all-gather.9.cloned.1.call-done, pred[7632]{0:T(1024)(128)(4,1)S(1)} %broadcast_compare_fusion.1), kind=kOutput, calls=%fused_computation.267 | convolution fusion | flops 5006591488 | bytes 26063568 | tf_op jit(solution)/shard_map/dot_general | solution.py:55
  340.3 9.2 %fusion.79 = f32[320,1024]{1,0:T(8,128)S(1)} fusion(bf16[7632,1024]{1,0:T(8,128)(2,1)} %all-gather.9.cloned.1.call-done, f32[320,7632]{1,0:T(8,128)S(1)} %get-tuple-element.253, f32[320]{0:T(512)S(1)} %get-tuple-element.237, f32[320]{0:T(512)S(1)} %get-tuple-element.175, s32[7632]{0:T(1024)S(1)} %iota_add_fusion, s32[320]{0:T(512)S(1)} %eq.135), kind=kOutput, calls=%fused_computation.256 | convolution fusion | flops 5016360960 | bytes 26744384 | tf_op jit(solution)/shard_map/dot_general | solution.py:45
  351.4 4.3 collective-permute-start.24
  355.6 17.9 %convert_bitcast_fusion = bf16[8,7632,128]{2,1,0:T(8,128)(2,1)} fusion(f32[320,7632]{1,0:T(8,128)} %copy-done.47, f32[320]{0:T(512)S(1)} %get-tuple-element.237, f32[320]{0:T(512)S(1)} %get-tuple-element.175, s32[7632]{0:T(1024)S(1)} %iota_add_fusion, s32[320]{0:T(512)S(1)} %eq.135, bf16[320,1024]{1,0:T(8,128)(2,1)} %constant_dynamic-update-slice_fusion.4), kind=kOutput, calls=%fused_computation.8 | convolution fusion | flops 5024176128 | bytes 26089024 | tf_op jit(solution)/shard_map/sv,swc->wvc/dot_general | solution.py:943
  385.8 3.4 gradient_block.13
  389.2 3.4 gradient_block.12
  393.2 10.4 %multiply_convert_fusion.refs_1_ = bf16[512,4096]{1,0:T(8,128)(2,1)S(1)} fusion(bf16[512,4096]{1,0:T(8,128)(2,1)} %copy-done.38, bf16[512,1024]{1,0:T(8,128)(2,1)S(1)} %get-tuple-element.177.refs_0_, bf16[1024,12288]{1,0:T(8,128)(2,1)} %all-gather.7.cloned.1.call-done.weight_ref), kind=kOutput, calls=%fused_computation.20 | convolution fusion | flops 4301258752 | bytes 17825792 | tf_op jit(solution)/shard_map/dot_general | solution.py:45
  403.6 4.3 gradient_block.14
  410.4 3.3 gradient_block.15
  414.9 10.4 %multiply_reduce_fusion.2 = (f32[1024]{0:T(1024)S(1)}, f32[512]{0:T(512)S(1)}, f32[1024]{0:T(1024)S(1)}, f32[512,1024]{1,0:T(8,128)}) fusion(f32[512,1024]{1,0:T(8,128)S(1)} %copy-done.44, f32[512]{0:T(512)S(1)} %fusion.71, f32[512]{0:T(512)S(1)} %broadcast_multiply_fusion.2, f32[1024]{0:T(1024)S(1)} %bitcast.208, ...), kind=kOutput, calls=%fused_computation.40 | convolution fusion | flops 4300207616 | bytes 18894848 | tf_op jit(solution)/shard_map/dot_general | solution.py:55
  429.2 3.3 fusion.29.do_ref
  432.5 3.5 gradient_block.17
  436.0 16.6 %attend_back.1.refs_2_.dqkv_ref = bf16[512,3072]{1,0:T(8,128)(2,1)S(1)} custom-call(bf16[512,3072]{1,0:T(8,128)(2,1)S(1)} %copy-done.1, bf16[512,3072]{1,0:T(8,128)(2,1)S(1)} %copy-done.1, bf16[512,3072]{1,0:T(8,128)(2,1)S(1)} %copy-done.1, bf16[512,1024]{1,0:T(8,128)(2,1)S(1)} %fusion.29.do_ref, f32[8,2,512]{2,1,0:T(2,128)S(1)} %get-tuple-element.108.lse_ref, ...), custom_call_target="tpu_custom_call" | custom-call | tf_op jit(solution)/shard_map/attend_back/pallas_call | solution.py:126
  452.6 9.2 %collective-permute-done.29.refs_3_ = bf16[256,4096]{1,0:T(8,128)(2,1)S(1)} collective-permute-done((bf16[256,4096]{1,0:T(8,128)(2,1)S(1)}, bf16[256,4096]{1,0:T(8,128)(2,1)S(1)}, u32[]{:S(2)}, u32[]{:S(2)}) %collective-permute-start.29) | collective-permute-done | bytes 2097184 | tf_op jit(solution)/shard_map/ppermute | solution.py:448
  461.8 3.3 gradient_block.18
  473.7 3.3 gradient_block.20
  477.2 5.0 gradient_block.19
  482.2 8.2 embed_back.1
  491.7 21.8 %collective-permute-done.31.refs_3_ = bf16[256,4096]{1,0:T(8,128)(2,1)} collective-permute-done((bf16[256,4096]{1,0:T(8,128)(2,1)}, bf16[256,4096]{1,0:T(8,128)(2,1)}, u32[]{:S(2)}, u32[]{:S(2)}) %collective-permute-start.31) | collective-permute-done | bytes 2097184 | tf_op jit(solution)/shard_map/ppermute | solution.py:448
  514.3 6.9 concatenate.84
  529.5 5.7 gradient_block.23
  537.3 4.9 gradient_block.22
  549.9 4.2 all-to-all-start.1
  559.0 25.2 %collective-permute-done.36.refs_5_ = bf16[256,4096]{1,0:T(8,128)(2,1)} collective-permute-done((bf16[256,4096]{1,0:T(8,128)(2,1)}, bf16[256,4096]{1,0:T(8,128)(2,1)}, u32[]{:S(2)}, u32[]{:S(2)}) %collective-permute-start.36) | collective-permute-done | bytes 2097184 | tf_op jit(solution)/shard_map/ppermute | solution.py:448
  586.6 5.5 gradient_block.21
  596.4 4.6 broadcast_select_fusion
  601.0 6.5 span.4
  608.8 6.4 span.3
  616.5 3.2 broadcast_select_fusion.2.grad_ref
  619.9 6.4 span.5
  630.2 21.1 %press.1 = (f32[1,256,12288]{2,1,0:T(8,128)}, bf16[4,256,1536]{2,1,0:T(8,128)(2,1)}, bf16[4,256,1536]{2,1,0:T(8,128)(2,1)}) custom-call(s32[1]{0:T(128)} %bitcast.4.core_ref, f32[2]{0:T(128)} %pad_maximum_fusion.5.scale_ref, f32[256,4096]{1,0:T(8,128)} %get-tuple-element.131.refs_0_, f32[256,4096]{1,0:T(8,128)} %get-tuple-element.132.refs_1_, ...), custom_call_target="tpu_custom_call" | custom-call | tf_op jit(solution)/shard_map/press/pallas_call | solution.py:741
  651.3 57.4 %collective-permute-start.40 = (bf16[4,256,1536]{2,1,0:T(8,128)(2,1)}, bf16[4,256,1536]{2,1,0:T(8,128)(2,1)S(1)}, u32[]{:S(2)}, u32[]{:S(2)}) collective-permute-start(bf16[4,256,1536]{2,1,0:T(8,128)(2,1)} %get-tuple-element.135), channel_id=1, source_target_pairs={{0,4},{4,0},{8,12},{12,8},{16,20},{20,16},{24,28},{28,24},{1,5},{5... | collective-permute-start | bytes 9437192 | tf_op jit(solution)/shard_map/ppermute | solution.py:810
  708.8 5.5 collective-permute-done.40
  714.3 3.8 fusion.44
  722.0 8.0 collective-permute-done.42
  734.0 3.9 collective-permute-done.41
  737.9 6.3 collective-permute-done.43
  763.2 5.4 all-gather.15.cloned.1.call-done
  768.6 36.2 %add_rows.1.grad_ref = f32[7632,128]{1,0:T(8,128)} custom-call(s32[16384]{0:T(1024)} %copy-done.37, bf16[4,4624,128]{2,1,0:T(8,128)(2,1)} %bitcast.185), custom_call_target="tpu_custom_call" | custom-call | tf_op jit(solution)/shard_map/add_rows/pallas_call | solution.py:639
  804.8 12.4 %update.1 = (f32[7632,128]{1,0:T(8,128)}, f32[7632,128]{1,0:T(8,128)}, f32[1,128]{1,0:T(1,128)}, f32[1,128]{1,0:T(1,128)}) custom-call(f32[7632,128]{1,0:T(8,128)} %add_rows.1.grad_ref, bf16[7632,128]{1,0:T(8,128)(2,1)} %bitcast.189, f32[7632,128]{1,0:T(8,128)} %table_ref.3, f32[7632,128]{1,0:T(8,128)} %first_ref.1, f32[7632,128]{1,0:T(8,128)} %second_ref.1), custom_call_target="tpu_custom_call" | custom-call | tf_op jit(solution)/shard_map/update/pallas_call | solution.py:786
  836.9 3.5 collective-permute-done.50
  841.2 3.6 collective-permute-done.51
  854.5 4.2 multiply_subtract_fusion.2
  858.7 5.7 multiply_subtract_fusion
  864.5 6.3 convert_element_type.365
  870.8 10.2 %all-gather.13.cloned.1.call-done = bf16[528,1024]{1,0:T(8,128)(2,1)} async-done(((bf16[528,128]{1,0:T(8,128)(2,1)}), bf16[528,1024]{1,0:T(8,128)(2,1)}) %all-gather.13.cloned.1.call-update) | async-done | bytes 1081360 | tf_op jit(solution)/shard_map/all_gather | solution.py:1024
  880.9 6.0 multiply_subtract_fusion.1
  (406 shorter events, 200.0 us)
Async XLA Ops:
  7.2 221.5 %all-gather.7.cloned.1.call-start = ((), (), s32[]{:S(2)}) async-start(), calls=%async_computation.3 | async-start | bytes 28311552 | tf_op jit(solution)/shard_map/all_gather | solution.py:881
  8.0 1.3 collective-permute-start.6
  10.1 4.7 collective-permute-start.7
  14.9 9.2 %collective-permute-start.8 = (s32[4,4,672]{2,1,0:T(4,128)S(1)}, s32[4,4,672]{2,1,0:T(4,128)S(1)}, u32[]{:S(2)}, u32[]{:S(2)}) collective-permute-start(s32[4,4,672]{2,1,0:T(4,128)S(1)} %pad_add_fusion.1), channel_id=1, source_target_pairs={{0,16},{4,20},{8,24},{12,28},{16,0},{20,4},{24,8},{28,12},{1,17},{... | collective-permute-start | bytes 129032 | tf_op jit(solution)/shard_map/ppermute | solution.py:481
  18.5 60.6 %copy-start.54 = (bf16[256,1536]{1,0:T(8,128)(2,1)}, bf16[256,1536]{1,0:T(8,128)(2,1)S(1)}, u32[]{:S(2)}) copy-start(bf16[256,1536]{1,0:T(8,128)(2,1)S(1)} %convert_element_type.288) | copy-start | bytes 2359300
  18.5 60.6 %collective-permute-start.5 = (bf16[256,1536]{1,0:T(8,128)(2,1)S(1)}, bf16[256,1536]{1,0:T(8,128)(2,1)S(1)}, u32[]{:S(2)}, u32[]{:S(2)}) collective-permute-start(bf16[256,1536]{1,0:T(8,128)(2,1)S(1)} %convert_element_type.288), channel_id=1, source_target_pairs={{0,1},{1,2},{2,3},{3,0},{4,5},{5,6},{6,7},{7,4},{8,9},{9,10},{10,1... | collective-permute-start | bytes 2359304 | tf_op jit(solution)/shard_map/ppermute | solution.py:341
  20.1 59.0 %collective-permute-start.4 = (bf16[256,1536]{1,0:T(8,128)(2,1)S(1)}, bf16[256,1536]{1,0:T(8,128)(2,1)S(1)}, u32[]{:S(2)}, u32[]{:S(2)}) collective-permute-start(bf16[256,1536]{1,0:T(8,128)(2,1)S(1)} %convert_element_type.288), channel_id=1, source_target_pairs={{0,2},{1,3},{2,0},{3,1},{4,6},{5,7},{6,4},{7,5},{8,10},{9,11},{10,... | collective-permute-start | bytes 2359304 | tf_op jit(solution)/shard_map/ppermute | solution.py:341
  22.7 58.1 %collective-permute-start.3 = (bf16[256,1536]{1,0:T(8,128)(2,1)S(1)}, bf16[256,1536]{1,0:T(8,128)(2,1)}, u32[]{:S(2)}, u32[]{:S(2)}) collective-permute-start(bf16[256,1536]{1,0:T(8,128)(2,1)S(1)} %convert_element_type.288), channel_id=1, source_target_pairs={{0,3},{1,0},{2,1},{3,2},{4,7},{5,4},{6,5},{7,6},{8,11},{9,8},{10,9... | collective-permute-start | bytes 2359304 | tf_op jit(solution)/shard_map/ppermute | solution.py:341
  24.3 60.2 %copy-start.59 = (s32[4,8,672]{2,1,0:T(8,128)}, s32[4,8,672]{2,1,0:T(8,128)S(1)}, u32[]{:S(2)}) copy-start(s32[4,8,672]{2,1,0:T(8,128)S(1)} %reshape.680) | copy-start | bytes 258052
  26.6 52.4 %copy-start.37 = (s32[16384]{0:T(1024)}, s32[16384]{0:T(1024)S(1)}, u32[]{:S(2)}) copy-start(s32[16384]{0:T(1024)S(1)} %fusion.57.ids_ref) | copy-start | bytes 196612
  87.2 21.9 %collective-permute-start.11 = (bf16[1792,128]{1,0:T(8,128)(2,1)S(1)}, bf16[1792,128]{1,0:T(8,128)(2,1)S(1)}, u32[]{:S(2)}, u32[]{:S(2)}) collective-permute-start(bf16[1792,128]{1,0:T(8,128)(2,1)S(1)} %get-tuple-element.214), channel_id=1, source_target_pairs={{0,3},{1,0},{2,1},{3,2},{4,7},{5,4},{6,5},{7,6},{8,11},{9,8},{10,9... | collective-permute-start | bytes 1376264 | tf_op jit(solution)/shard_map/ppermute | solution.py:373
  98.1 39.6 %collective-permute-start.10 = (bf16[1792,128]{1,0:T(8,128)(2,1)S(1)}, bf16[1792,128]{1,0:T(8,128)(2,1)S(1)}, u32[]{:S(2)}, u32[]{:S(2)}) collective-permute-start(bf16[1792,128]{1,0:T(8,128)(2,1)S(1)} %get-tuple-element.215), channel_id=1, source_target_pairs={{0,2},{1,3},{2,0},{3,1},{4,6},{5,7},{6,4},{7,5},{8,10},{9,11},{10,... | collective-permute-start | bytes 1376264 | tf_op jit(solution)/shard_map/ppermute | solution.py:373
  98.1 39.6 %collective-permute-start.9 = (bf16[1792,128]{1,0:T(8,128)(2,1)S(1)}, bf16[1792,128]{1,0:T(8,128)(2,1)S(1)}, u32[]{:S(2)}, u32[]{:S(2)}) collective-permute-start(bf16[1792,128]{1,0:T(8,128)(2,1)S(1)} %get-tuple-element.216), channel_id=1, source_target_pairs={{0,1},{1,2},{2,3},{3,0},{4,5},{5,6},{6,7},{7,4},{8,9},{9,10},{10,1... | collective-permute-start | bytes 1376264 | tf_op jit(solution)/shard_map/ppermute | solution.py:373
  147.7 34.3 %all-to-all-start = ((bf16[8,512,128]{2,1,0:T(8,128)(2,1)}), bf16[8,512,128]{2,1,0:T(8,128)(2,1)S(1)}, u32[]{:S(2)}, u32[]{:S(2)}) async-start(bf16[8,512,128]{2,1,0:T(8,128)(2,1)} %bitcast.188), calls=%async_computation | async-start | bytes 2097152 | tf_op jit(solution)/shard_map/all_to_all | solution.py:891
  151.3 167.0 %all-gather.9.cloned.1.call-start = ((), (), s32[]{:S(2)}) async-start(), calls=%async_computation.4 | async-start | bytes 17584128 | tf_op jit(solution)/shard_map/all_gather | solution.py:910
  151.9 5.2 collective-permute-start.12
  152.3 29.7 %collective-permute-start.15 = (s32[1,592]{1,0:T(1,128)S(1)}, s32[1,592]{1,0:T(1,128)S(1)}, u32[]{:S(2)}, u32[]{:S(2)}) collective-permute-start(s32[1,592]{1,0:T(1,128)S(1)} %pad_add_fusion.3), channel_id=1, source_target_pairs={{0,0},{1,4},{2,1},{3,5},{4,2},{5,6},{6,3},{7,7},{8,8},{9,12},{10,9... | collective-permute-start | bytes 7112 | tf_op jit(solution)/shard_map/ppermute | solution.py:494
  158.5 18.7 %collective-permute-start.13 = (f32[]{:T(128)}, f32[]{:T(128)}, u32[]{:S(2)}, u32[]{:S(2)}) collective-permute-start(f32[]{:T(128)} %add.645), channel_id=1, source_target_pairs={{0,8},{4,12},{8,0},{12,4},{16,24},{20,28},{24,16},{28,20},{1,9},{5... | collective-permute-start | bytes 20 | tf_op jit(solution)/shard_map/ppermute | solution.py:331
  177.8 3.6 collective-permute-start.14
  182.0 49.0 %copy-start.71 = (s32[1,80]{1,0:T(1,128)}, s32[1,80]{1,0:T(1,128)S(1)}, u32[]{:S(2)}) copy-start(s32[1,80]{1,0:T(1,128)S(1)} %slice.193) | copy-start | bytes 964
  187.5 62.9 %copy-start.22 = (f32[512,1024]{1,0:T(8,128)}, f32[512,1024]{1,0:T(8,128)S(1)}, u32[]{:S(2)}) copy-start(f32[512,1024]{1,0:T(8,128)S(1)} %get-tuple-element.188.embedded_ref) | copy-start | bytes 6291460
  187.9 50.7 %copy-start.11 = (bf16[512,1024]{1,0:T(8,128)(2,1)}, bf16[512,1024]{1,0:T(8,128)(2,1)S(1)}, u32[]{:S(2)}) copy-start(bf16[512,1024]{1,0:T(8,128)(2,1)S(1)} %fusion.23.refs_0_) | copy-start | bytes 3145732
  228.7 391.1 %reduce-scatter.2.cloned.1.call-start = ((), (), s32[]{:S(2)}) async-start(), calls=%async_computation.5 | async-start | bytes 17584128 | tf_op jit(solution)/shard_map/reduce_scatter | solution.py:945
  254.7 177.7 %copy-start.9 = (bf16[512,1024]{1,0:T(8,128)(2,1)}, bf16[512,1024]{1,0:T(8,128)(2,1)S(1)}, u32[]{:S(2)}) copy-start(bf16[512,1024]{1,0:T(8,128)(2,1)S(1)} %fusion.22.fin_ref.refs_0_) | copy-start | bytes 3145732
  284.6 12.5 %collective-permute-start.17 = (bf16[80,1024]{1,0:T(8,128)(2,1)}, bf16[80,1024]{1,0:T(8,128)(2,1)}, u32[]{:S(2)}, u32[]{:S(2)}) collective-permute-start(bf16[80,1024]{1,0:T(8,128)(2,1)} %get-tuple-element.186), channel_id=1, source_target_pairs={{0,2},{1,3},{2,0},{3,1},{4,6},{5,7},{6,4},{7,5},{8,10},{9,11},{10,... | collective-permute-start | bytes 491528 | tf_op jit(solution)/shard_map/ppermute | solution.py:341
  287.1 8.4 collective-permute-start.16
  288.7 11.5 %collective-permute-start.18 = (bf16[80,1024]{1,0:T(8,128)(2,1)}, bf16[80,1024]{1,0:T(8,128)(2,1)S(1)}, u32[]{:S(2)}, u32[]{:S(2)}) collective-permute-start(bf16[80,1024]{1,0:T(8,128)(2,1)} %get-tuple-element.186), channel_id=1, source_target_pairs={{0,1},{1,2},{2,3},{3,0},{4,5},{5,6},{6,7},{7,4},{8,9},{9,10},{10,1... | collective-permute-start | bytes 491528 | tf_op jit(solution)/shard_map/ppermute | solution.py:341
  330.3 6.1 collective-permute-start.20
  332.7 3.6 collective-permute-start.19
  334.2 5.4 collective-permute-start.21
  351.4 22.1 %collective-permute-start.22 = (bf16[80,1024]{1,0:T(8,128)(2,1)}, bf16[80,1024]{1,0:T(8,128)(2,1)}, u32[]{:S(2)}, u32[]{:S(2)}) collective-permute-start(bf16[80,1024]{1,0:T(8,128)(2,1)} %get-tuple-element.217), channel_id=1, source_target_pairs={{0,1},{1,2},{2,3},{3,0},{4,5},{5,6},{6,7},{7,4},{8,9},{9,10},{10,1... | collective-permute-start | bytes 491528 | tf_op jit(solution)/shard_map/ppermute | solution.py:360
  351.4 22.1 %collective-permute-start.24 = (bf16[80,1024]{1,0:T(8,128)(2,1)}, bf16[80,1024]{1,0:T(8,128)(2,1)}, u32[]{:S(2)}, u32[]{:S(2)}) collective-permute-start(bf16[80,1024]{1,0:T(8,128)(2,1)} %get-tuple-element.218), channel_id=1, source_target_pairs={{0,3},{1,0},{2,1},{3,2},{4,7},{5,4},{6,5},{7,6},{8,11},{9,8},{10,9... | collective-permute-start | bytes 491528 | tf_op jit(solution)/shard_map/ppermute | solution.py:360
  355.6 17.9 %collective-permute-start.23 = (bf16[80,1024]{1,0:T(8,128)(2,1)}, bf16[80,1024]{1,0:T(8,128)(2,1)}, u32[]{:S(2)}, u32[]{:S(2)}) collective-permute-start(bf16[80,1024]{1,0:T(8,128)(2,1)} %get-tuple-element.219), channel_id=1, source_target_pairs={{0,2},{1,3},{2,0},{3,1},{4,6},{5,7},{6,4},{7,5},{8,10},{9,11},{10,... | collective-permute-start | bytes 491528 | tf_op jit(solution)/shard_map/ppermute | solution.py:360
  392.6 10.9 %collective-permute-start.25 = (bf16[256,4096]{1,0:T(8,128)(2,1)}, bf16[256,4096]{1,0:T(8,128)(2,1)}, u32[]{:S(2)}, u32[]{:S(2)}) collective-permute-start(bf16[256,4096]{1,0:T(8,128)(2,1)} %gradient_block.12), channel_id=1, source_target_pairs={{0,4},{4,0},{8,12},{12,8},{16,20},{20,16},{24,28},{28,24},{1,5},{5... | collective-permute-start | bytes 6291464 | tf_op jit(solution)/shard_map/ppermute | solution.py:432
  392.6 10.9 %collective-permute-start.26 = (bf16[256,4096]{1,0:T(8,128)(2,1)}, bf16[256,4096]{1,0:T(8,128)(2,1)}, u32[]{:S(2)}, u32[]{:S(2)}) collective-permute-start(bf16[256,4096]{1,0:T(8,128)(2,1)} %gradient_block.13), channel_id=1, source_target_pairs={{0,4},{4,0},{8,12},{12,8},{16,20},{20,16},{24,28},{28,24},{1,5},{5... | collective-permute-start | bytes 6291464 | tf_op jit(solution)/shard_map/ppermute | solution.py:433
  413.7 18.8 %collective-permute-start.27 = (bf16[256,4096]{1,0:T(8,128)(2,1)}, bf16[256,4096]{1,0:T(8,128)(2,1)S(1)}, u32[]{:S(2)}, u32[]{:S(2)}) collective-permute-start(bf16[256,4096]{1,0:T(8,128)(2,1)} %gradient_block.15), channel_id=1, source_target_pairs={{0,4},{4,0},{8,12},{12,8},{16,20},{20,16},{24,28},{28,24},{1,5},{5... | collective-permute-start | bytes 6291464 | tf_op jit(solution)/shard_map/ppermute | solution.py:432
  413.8 18.7 %collective-permute-start.28 = (bf16[256,4096]{1,0:T(8,128)(2,1)S(1)}, bf16[256,4096]{1,0:T(8,128)(2,1)S(1)}, u32[]{:S(2)}, u32[]{:S(2)}) collective-permute-start(bf16[256,4096]{1,0:T(8,128)(2,1)S(1)} %gradient_block.16), channel_id=1, source_target_pairs={{0,4},{4,0},{8,12},{12,8},{16,20},{20,16},{24,28},{28,24},{1,5},{5... | collective-permute-start | bytes 6291464 | tf_op jit(solution)/shard_map/ppermute | solution.py:433
  414.2 47.6 %collective-permute-start.29 = (bf16[256,4096]{1,0:T(8,128)(2,1)S(1)}, bf16[256,4096]{1,0:T(8,128)(2,1)S(1)}, u32[]{:S(2)}, u32[]{:S(2)}) collective-permute-start(bf16[256,4096]{1,0:T(8,128)(2,1)S(1)} %gradient_block.14), channel_id=1, source_target_pairs={{0,1},{1,0},{2,3},{3,2},{4,5},{5,4},{6,7},{7,6},{8,9},{9,8},{10,11... | collective-permute-start | bytes 6291464 | tf_op jit(solution)/shard_map/ppermute | solution.py:448
  465.2 12.0 %collective-permute-start.30 = (bf16[256,4096]{1,0:T(8,128)(2,1)}, bf16[256,4096]{1,0:T(8,128)(2,1)}, u32[]{:S(2)}, u32[]{:S(2)}) collective-permute-start(bf16[256,4096]{1,0:T(8,128)(2,1)} %gradient_block.18), channel_id=1, source_target_pairs={{0,4},{4,0},{8,12},{12,8},{16,20},{20,16},{24,28},{28,24},{1,5},{5... | collective-permute-start | bytes 6291464 | tf_op jit(solution)/shard_map/ppermute | solution.py:432
  465.2 48.4 %collective-permute-start.31 = (bf16[256,4096]{1,0:T(8,128)(2,1)}, bf16[256,4096]{1,0:T(8,128)(2,1)}, u32[]{:S(2)}, u32[]{:S(2)}) collective-permute-start(bf16[256,4096]{1,0:T(8,128)(2,1)} %gradient_block.17), channel_id=1, source_target_pairs={{0,1},{1,0},{2,3},{3,2},{4,5},{5,4},{6,7},{7,6},{8,9},{9,8},{10,11... | collective-permute-start | bytes 6291464 | tf_op jit(solution)/shard_map/ppermute | solution.py:448
  477.0 82.0 %collective-permute-start.35 = (bf16[256,4096]{1,0:T(8,128)(2,1)}, bf16[256,4096]{1,0:T(8,128)(2,1)}, u32[]{:S(2)}, u32[]{:S(2)}) collective-permute-start(bf16[256,4096]{1,0:T(8,128)(2,1)} %gradient_block.20), channel_id=1, source_target_pairs={{0,4},{4,0},{8,12},{12,8},{16,20},{20,16},{24,28},{28,24},{1,5},{5... | collective-permute-start | bytes 6291464 | tf_op jit(solution)/shard_map/ppermute | solution.py:433
  513.6 70.6 %collective-permute-start.36 = (bf16[256,4096]{1,0:T(8,128)(2,1)}, bf16[256,4096]{1,0:T(8,128)(2,1)}, u32[]{:S(2)}, u32[]{:S(2)}) collective-permute-start(bf16[256,4096]{1,0:T(8,128)(2,1)} %gradient_block.19), channel_id=1, source_target_pairs={{0,1},{1,0},{2,3},{3,2},{4,5},{5,4},{6,7},{7,6},{8,9},{9,8},{10,11... | collective-permute-start | bytes 6291464 | tf_op jit(solution)/shard_map/ppermute | solution.py:448
  523.3 21.0 %collective-permute-start.32 = (bf16[528,512]{1,0:T(8,128)(2,1)}, bf16[528,512]{1,0:T(8,128)(2,1)}, u32[]{:S(2)}, u32[]{:S(2)}) collective-permute-start(bf16[528,512]{1,0:T(8,128)(2,1)} %dynamic-slice_convert_fusion), channel_id=1, source_target_pairs={{0,16},{4,20},{8,24},{12,28},{16,0},{20,4},{24,8},{28,12},{1,17},{... | collective-permute-start | bytes 1622024 | tf_op jit(solution)/shard_map/ppermute | solution.py:837
  535.1 61.2 %collective-permute-start.39 = (bf16[256,4096]{1,0:T(8,128)(2,1)}, bf16[256,4096]{1,0:T(8,128)(2,1)}, u32[]{:S(2)}, u32[]{:S(2)}) collective-permute-start(bf16[256,4096]{1,0:T(8,128)(2,1)} %gradient_block.23), channel_id=1, source_target_pairs={{2,4},{3,5},{4,2},{5,3},{10,12},{11,13},{12,10},{13,11},{18,20},{1... | collective-permute-start | bytes 6291464 | tf_op jit(solution)/shard_map/ppermute | solution.py:472
  542.2 54.1 %collective-permute-start.38 = (bf16[256,4096]{1,0:T(8,128)(2,1)}, bf16[256,4096]{1,0:T(8,128)(2,1)}, u32[]{:S(2)}, u32[]{:S(2)}) collective-permute-start(bf16[256,4096]{1,0:T(8,128)(2,1)} %gradient_block.22), channel_id=1, source_target_pairs={{2,4},{3,5},{4,2},{5,3},{10,12},{11,13},{12,10},{13,11},{18,20},{1... | collective-permute-start | bytes 6291464 | tf_op jit(solution)/shard_map/ppermute | solution.py:472
  547.3 8.9 collective-permute-start.33
  549.9 44.1 %all-to-all-start.1 = ((bf16[8,512,128]{2,1,0:T(8,128)(2,1)}), bf16[8,512,128]{2,1,0:T(8,128)(2,1)}, u32[]{:S(2)}, u32[]{:S(2)}) async-start(bf16[8,512,128]{2,1,0:T(8,128)(2,1)} %bitcast_bitcast_fusion), calls=%async_computation.1 | async-start | bytes 2097152 | tf_op jit(solution)/shard_map/all_to_all | solution.py:961
  554.1 214.4 %all-gather.15.cloned.1.call-start = ((), (), s32[]{:S(2)}) async-start(), calls=%async_computation.8 | async-start | bytes 5918720 | tf_op jit(solution)/shard_map/all_gather | solution.py:970
  558.0 34.9 %collective-permute-start.34 = (bf16[528,128]{1,0:T(8,128)(2,1)}, bf16[528,128]{1,0:T(8,128)(2,1)}, u32[]{:S(2)}, u32[]{:S(2)}) collective-permute-start(bf16[528,128]{1,0:T(8,128)(2,1)} %dynamic-slice_convert_fusion.5), channel_id=1, source_target_pairs={{0,4},{4,0},{8,12},{12,8},{16,20},{20,16},{24,28},{28,24},{1,5},{5... | collective-permute-start | bytes 405512 | tf_op jit(solution)/shard_map/ppermute | solution.py:837
  592.1 24.4 %collective-permute-start.37 = (bf16[256,4096]{1,0:T(8,128)(2,1)}, bf16[256,4096]{1,0:T(8,128)(2,1)S(1)}, u32[]{:S(2)}, u32[]{:S(2)}) collective-permute-start(bf16[256,4096]{1,0:T(8,128)(2,1)} %gradient_block.21), channel_id=1, source_target_pairs={{2,4},{3,5},{4,2},{5,3},{10,12},{11,13},{12,10},{13,11},{18,20},{1... | collective-permute-start | bytes 6291464 | tf_op jit(solution)/shard_map/ppermute | solution.py:472
  619.8 238.9 %all-gather.11.cloned.1.call-start = ((), (), s32[]{:S(2)}) async-start(), calls=%async_computation.6 | async-start | bytes 7077888 | tf_op jit(solution)/shard_map/all_gather | solution.py:1021
  651.3 62.9 %collective-permute-start.40 = (bf16[4,256,1536]{2,1,0:T(8,128)(2,1)}, bf16[4,256,1536]{2,1,0:T(8,128)(2,1)S(1)}, u32[]{:S(2)}, u32[]{:S(2)}) collective-permute-start(bf16[4,256,1536]{2,1,0:T(8,128)(2,1)} %get-tuple-element.135), channel_id=1, source_target_pairs={{0,4},{4,0},{8,12},{12,8},{16,20},{20,16},{24,28},{28,24},{1,5},{5... | collective-permute-start | bytes 9437192 | tf_op jit(solution)/shard_map/ppermute | solution.py:810
  718.1 11.9 %collective-permute-start.42 = (bf16[128,1536]{1,0:T(8,128)(2,1)S(1)}, bf16[128,1536]{1,0:T(8,128)(2,1)S(1)}, u32[]{:S(2)}, u32[]{:S(2)}) collective-permute-start(bf16[128,1536]{1,0:T(8,128)(2,1)S(1)} %get-tuple-element.200), channel_id=1, source_target_pairs={{0,8},{4,12},{8,0},{12,4},{16,24},{20,28},{24,16},{28,20},{1,9},{5... | collective-permute-start | bytes 1179656 | tf_op jit(solution)/shard_map/ppermute | solution.py:810
  719.6 18.3 %collective-permute-start.41 = (bf16[128,1536]{1,0:T(8,128)(2,1)}, bf16[128,1536]{1,0:T(8,128)(2,1)S(1)}, u32[]{:S(2)}, u32[]{:S(2)}) collective-permute-start(bf16[128,1536]{1,0:T(8,128)(2,1)} %get-tuple-element.197), channel_id=1, source_target_pairs={{0,8},{4,12},{8,0},{12,4},{16,24},{20,28},{24,16},{28,20},{1,9},{5... | collective-permute-start | bytes 1179656 | tf_op jit(solution)/shard_map/ppermute | solution.py:810
  720.1 17.8 %collective-permute-start.45 = (bf16[128,1536]{1,0:T(8,128)(2,1)}, bf16[128,1536]{1,0:T(8,128)(2,1)}, u32[]{:S(2)}, u32[]{:S(2)}) collective-permute-start(bf16[128,1536]{1,0:T(8,128)(2,1)} %get-tuple-element.198), channel_id=1, source_target_pairs={{0,16},{4,20},{8,24},{12,28},{16,0},{20,4},{24,8},{28,12},{1,17},{... | collective-permute-start | bytes 1179656 | tf_op jit(solution)/shard_map/ppermute | solution.py:810
  731.9 12.3 %collective-permute-start.43 = (bf16[128,1536]{1,0:T(8,128)(2,1)}, bf16[128,1536]{1,0:T(8,128)(2,1)S(1)}, u32[]{:S(2)}, u32[]{:S(2)}) collective-permute-start(bf16[128,1536]{1,0:T(8,128)(2,1)} %fusion.40), channel_id=1, source_target_pairs={{0,16},{4,20},{8,24},{12,28},{16,0},{20,4},{24,8},{28,12},{1,17},{... | collective-permute-start | bytes 1179656 | tf_op jit(solution)/shard_map/ppermute | solution.py:810
  733.8 17.0 %collective-permute-start.44 = (bf16[128,1536]{1,0:T(8,128)(2,1)}, bf16[128,1536]{1,0:T(8,128)(2,1)S(1)}, u32[]{:S(2)}, u32[]{:S(2)}) collective-permute-start(bf16[128,1536]{1,0:T(8,128)(2,1)} %get-tuple-element.199), channel_id=1, source_target_pairs={{0,16},{4,20},{8,24},{12,28},{16,0},{20,4},{24,8},{28,12},{1,17},{... | collective-permute-start | bytes 1179656 | tf_op jit(solution)/shard_map/ppermute | solution.py:810
  746.0 7.8 collective-permute-start.46
  760.5 120.4 %all-gather.13.cloned.1.call-start = ((), (), s32[]{:S(2)}) async-start(), calls=%async_computation.7 | async-start | bytes 1216512 | tf_op jit(solution)/shard_map/all_gather | solution.py:1024
  828.7 1.1 collective-permute-start.47
  829.8 3.5 collective-permute-start.48
  833.3 3.5 collective-permute-start.49
  836.9 3.5 collective-permute-start.50
  840.4 4.4 collective-permute-start.51
  (67 other events, 440.7 us)
Sparse Core Ops, SparseCore 0:
  84.5 144.1 all-gather.6
  231.2 87.1 all-gather.8
  375.7 111.6 reduce-scatter.1
  619.9 148.5 all-gather.14
  771.0 43.9 all-gather.10
  858.9 22.0 all-gather.12

commit v11 on v10

--- a/solution.py
+++ b/solution.py
@@ -577,7 +577,7 @@
         ),
         out_shape=jax.ShapeDtypeStruct((places, count, cols), jnp.bfloat16),
         compiler_params=pltpu.CompilerParams(vmem_limit_bytes=40 * 2**20),
-        cost_estimate=pl.CostEstimate(flops=0, bytes_accessed=15 * 10**7, transcendentals=0),
+        cost_estimate=pl.CostEstimate(flops=0, bytes_accessed=0, transcendentals=0),
         name="pack_rows",
     )(ids.reshape(-1), table)
 
@@ -961,6 +961,7 @@
         cut = lax.all_to_all(cut, "wide", 0, 0).reshape(n_wide * L, D // n_wide)
         halved = small_halved(small_grad).astype(jnp.bfloat16)
         down, up = pieces[2], pieces[1]
+        mixed.away, down.result = together(mixed.away, down.result)
         mixed.finish()
         spans = [span_of(layer_m, up.result, worker_err, 4 * D)]
         spans.append(span_of(layer_m, down.result, worker_err, 8 * D))
@@ -1020,10 +1021,10 @@
         table_norms = (jnp.sum(table * table)[None], jnp.sum(table_upd * table_upd)[None])
     new_m = lax.all_gather(server_low, "wide", axis=1, tiled=True)
     if paired:
-        small_grad, new_m = together(small_grad, new_m)
+        small_grad, new_m, table_norms = together(small_grad, new_m, table_norms)
         small_grad = lax.all_gather(small_grad, "wide", axis=1, tiled=True)
-    small_mom, small_upd = small_update(small_grad, small_m, small_v, small)
     if not paired:
+        _, small_upd = small_update(small_grad, small_m, small_v, small)
         small_norm = jnp.where((wide_me == 0) & (narrow_me == 0), jnp.sum(small_upd * small_upd), 0.0)
     layer_upd = server_out / (jnp.sqrt(layer_v) + OPT_EPS) + DECAY * layer
     column = wide_me * part_cols + jnp.arange(part_cols)
@@ -1037,6 +1038,9 @@
     usq = jnp.sum(jnp.sum(layer_upd * layer_upd, axis=0)[:, None] * onehot, axis=0)
     parts = jnp.concatenate([wsq, usq, *table_norms, jnp.sum(own_loss)[None], small_norm[None]])
     sums = summed_over(summed_over(parts, "wide"), "narrow")
+    if paired:
+        sums, small_grad = together(sums, small_grad)
+    small_mom, small_upd = small_update(small_grad, small_m, small_v, small)
     loss_sum = sums[10]
     wnorm = jnp.sqrt(jnp.concatenate([sums[0:4], sums[8:9], jnp.sum(small * small)[None]]))
     unorm = jnp.sqrt(jnp.concatenate([sums[4:8], sums[9:10], sums[11:12]]))

time: 902 us -> 884 us (0.980)
  starting transfers between devices: 145 us -> 113 us
  waiting for transfers between devices: 231 us -> 243 us
    ppermute x7, starting transfers between devices: 64.9 us -> 32.7 us  [send(): lax.ppermute(value.astype(jnp.bfloat16), 'wide', swap_pairs(n_wide, bit))]
    all_gather x1, waiting for transfers between devices: 10.2 us -> 0.01 us  [shards(): small_grad = lax.all_gather(small_grad, 'wide', axis=1, tiled=True)]
    ppermute x3, waiting for transfers between devices: 56.2 us -> 66.4 us  [across(): self.away = lax.ppermute(away, 'narrow', sides)]
    ppermute x3, waiting for transfers between devices: 1.98 us -> 12 us  [small_halved(): lax.ppermute(give, 'wide', swap_pairs(n_wide, bit)).astype(jnp.float32)]
    unnamed x154 -> x160, local copies, waits for them, and re-layouts: 29.7 us -> 37.9 us
  transfers between devices with their start and end apart: 57 -> 57, of which waited for: 29 -> 28; matrix products, arithmetic and copies ran while one was open for 21% -> 19% of each run, Pallas kernels for 27% -> 27%
where the time goes in v11:
time: 884 us; the launch traced here: 876 us
  waiting for transfers between devices  243 us (27%)
  Pallas kernels  240 us (27%)
  starting transfers between devices  113 us (13%)
  other arithmetic  107 us (12%)
  matrix products  80.4 us (9%)
  local copies, waits for them, and re-layouts  65.4 us (7%)
  between operations  23.6 us (3%)
    ppermute x3, waiting for transfers between devices, across(): self.away = lax.ppermute(away, 'narrow', sides)  66.4 us
    pallas_call x1, Pallas kernels, packed_rows(): pl.pallas_call(pack_kernel, grid_spec=pltpu.PrefetchScalarGridSpec(num_sc...  52.4 us
    pallas_call x12, Pallas kernels, gradient_block(): pl.pallas_call(functools.partial(block_kernel, steps), grid_spec=pltpu.Pr...  45.2 us
    all_gather x1, waiting for transfers between devices, shards(): weights = lax.all_gather(layer_rows, 'wide', axis=1, tiled=True)  40.7 us
    ppermute x3, waiting for transfers between devices, sent_around(): lax.ppermute(block(by), 'narrow', cycle(size, by))  38.9 us
    unnamed x160, local copies, waits for them, and re-layouts  37.9 us
    pallas_call x1, Pallas kernels, added_rows(): pl.pallas_call(add_kernel, grid_spec=pltpu.PrefetchScalarGridSpec(num_sca...  36.1 us
    dot_general x4, matrix products, matmul_nt(): lax.dot_general(left, right, (((1,), (1,)), ((), ())), preferred_element_...  33.5 us
  transfers between devices with their start and end apart: 57, of which 28 were waited for; matrix products, arithmetic and copies ran while one was open for 19% of the time, Pallas kernels for 27%

profile of v11, /device:TPU:0, one launch (start us, length us, event | category | flops | bytes accessed | tf_op | source)
XLA Modules:
  0.0 875.5 jit_solution(7323857064317833561)
XLA Ops:
  26.6 52.4 %pack_rows.1 = bf16[4,4096,128]{2,1,0:T(8,128)(2,1)} custom-call(s32[16384]{0:T(1024)S(1)} %fusion.57.ids_ref, f32[7632,128]{1,0:T(8,128)S(1)} %copy-done.8), custom_call_target="tpu_custom_call" | custom-call | tf_op jit(solution)/shard_map/pack_rows/pallas_call | solution.py:568
  87.2 10.9 %collective-permute-start.11 = (bf16[1792,128]{1,0:T(8,128)(2,1)S(1)}, bf16[1792,128]{1,0:T(8,128)(2,1)S(1)}, u32[]{:S(2)}, u32[]{:S(2)}) collective-permute-start(bf16[1792,128]{1,0:T(8,128)(2,1)S(1)} %get-tuple-element.226), channel_id=1, source_target_pairs={{0,3},{1,0},{2,1},{3,2},{4,7},{5,4},{6,5},{7,6},{8,11},{9,8},{10,9... | collective-permute-start | bytes 1376264 | tf_op jit(solution)/shard_map/ppermute | solution.py:373
  98.8 10.3 %collective-permute-done.11 = bf16[1792,128]{1,0:T(8,128)(2,1)S(1)} collective-permute-done((bf16[1792,128]{1,0:T(8,128)(2,1)S(1)}, bf16[1792,128]{1,0:T(8,128)(2,1)S(1)}, u32[]{:S(2)}, u32[]{:S(2)}) %collective-permute-start.11) | collective-permute-done | bytes 458784 | tf_op jit(solution)/shard_map/ppermute | solution.py:373
  109.1 28.5 %collective-permute-done.10 = bf16[1792,128]{1,0:T(8,128)(2,1)S(1)} collective-permute-done((bf16[1792,128]{1,0:T(8,128)(2,1)S(1)}, bf16[1792,128]{1,0:T(8,128)(2,1)S(1)}, u32[]{:S(2)}, u32[]{:S(2)}) %collective-permute-start.10) | collective-permute-done | bytes 458784 | tf_op jit(solution)/shard_map/ppermute | solution.py:373
  137.8 5.5 take_rows.3
  143.3 3.5 conditional.1
  147.7 3.6 all-to-all-start
  153.6 3.6 convert_element_type.287
  158.5 16.5 %collective-permute-start.13 = (f32[]{:T(128)}, f32[]{:T(128)}, u32[]{:S(2)}, u32[]{:S(2)}) collective-permute-start(f32[]{:T(128)} %add.645), channel_id=1, source_target_pairs={{0,8},{4,12},{8,0},{12,4},{16,24},{20,28},{24,16},{28,20},{1,9},{5... | collective-permute-start | bytes 20 | tf_op jit(solution)/shard_map/ppermute | solution.py:331
  188.0 40.7 %all-gather.7.cloned.1.call-done.weight_ref = bf16[1024,12288]{1,0:T(8,128)(2,1)} async-done(((bf16[1024,1536]{1,0:T(8,128)(2,1)}), bf16[1024,12288]{1,0:T(8,128)(2,1)}) %all-gather.7.cloned.1.call-update) | async-done | bytes 25165840 | tf_op jit(solution)/shard_map/all_gather | solution.py:881
  230.7 6.4 add_convert_fusion.q_ref.k_ref.v_ref
  237.1 11.7 %attend.1 = (bf16[512,1024]{1,0:T(8,128)(2,1)S(1)}, f32[8,2,512]{2,1,0:T(2,128)S(1)}) custom-call(bf16[512,3072]{1,0:T(8,128)(2,1)S(1)} %add_convert_fusion.q_ref.k_ref.v_ref, bf16[512,3072]{1,0:T(8,128)(2,1)S(1)} %add_convert_fusion.q_ref.k_ref.v_ref, bf16[512,3072]{1,0:T(8,128)(2,1)S(1)} %add_convert_fusion.q_ref.k_ref.v_ref, ...), custom_call_target="tpu_custom_call" | custom-call | tf_op jit(solution)/shard_map/attend/pallas_call | solution.py:82
  248.8 3.4 fusion.91
  253.1 11.0 %ffn_up.1 = (bf16[512,4096]{1,0:T(8,128)(2,1)S(1)}, bf16[512,4096]{1,0:T(8,128)(2,1)S(1)}) custom-call(bf16[512,1024]{1,0:T(8,128)(2,1)S(1)} %fusion.22.fin_ref.refs_0_, bf16[1024,12288]{1,0:T(8,128)(2,1)} %all-gather.7.cloned.1.call-done.weight_ref, f32[1,4096]{1,0:T(1,128)S(1)} %bitcast.181), custom_call_target="tpu_custom_call" | custom-call | flops 4294967296 | tf_op jit(solution)/shard_map/ffn_up/pallas_call | solution.py:231
  266.1 9.9 %fusion.92 = (f32[512]{0:T(512)S(1)}, f32[512,1024]{1,0:T(8,128)S(1)}) fusion(f32[1024]{0:T(1024)S(1)} %bitcast.223, bf16[512,4096]{1,0:T(8,128)(2,1)S(1)} %get-tuple-element.103.refs_1_, bf16[1024,12288]{1,0:T(8,128)(2,1)} %all-gather.7.cloned.1.call-done.weight_ref, f32[1024]{0:T(1024)S(1)} %bitcast.213, f32[1024]{0:T(1024)S(1)} %bitcast.207, ...), kind=kOutput, calls=%fused_computation.266 | convolution fusion | flops 4298636800 | bytes 16795648 | tf_op jit(solution)/shard_map/dot_general | solution.py:55
  288.2 5.9 collective-permute-done.16
  299.6 18.7 %all-gather.9.cloned.1.call-done = bf16[7632,1024]{1,0:T(8,128)(2,1)} async-done(((bf16[7632,128]{1,0:T(8,128)(2,1)}), bf16[7632,1024]{1,0:T(8,128)(2,1)}) %all-gather.9.cloned.1.call-update) | async-done | bytes 15630352 | tf_op jit(solution)/shard_map/all_gather | solution.py:910
  318.3 9.1 %fusion.93 = (f32[320]{0:T(512)S(1)}, f32[320,7632]{1,0:T(8,128)S(1)}) fusion(bf16[320,1024]{1,0:T(8,128)(2,1)} %constant_dynamic-update-slice_fusion.4, bf16[7632,1024]{1,0:T(8,128)(2,1)} %all-gather.9.cloned.1.call-done, pred[7632]{0:T(1024)(128)(4,1)S(1)} %broadcast_compare_fusion.1), kind=kOutput, calls=%fused_computation.267 | convolution fusion | flops 5006591488 | bytes 26063568 | tf_op jit(solution)/shard_map/dot_general | solution.py:55
  340.2 8.9 %fusion.79 = f32[320,1024]{1,0:T(8,128)S(1)} fusion(bf16[7632,1024]{1,0:T(8,128)(2,1)} %all-gather.9.cloned.1.call-done, f32[320,7632]{1,0:T(8,128)S(1)} %get-tuple-element.265, f32[320]{0:T(512)S(1)} %get-tuple-element.249, f32[320]{0:T(512)S(1)} %get-tuple-element.187, s32[7632]{0:T(1024)S(1)} %iota_add_fusion, s32[320]{0:T(512)S(1)} %eq.135), kind=kOutput, calls=%fused_computation.256 | convolution fusion | flops 5016360960 | bytes 26744384 | tf_op jit(solution)/shard_map/dot_general | solution.py:45
  350.9 4.3 collective-permute-start.24
  355.2 17.8 %convert_bitcast_fusion = bf16[8,7632,128]{2,1,0:T(8,128)(2,1)} fusion(f32[320,7632]{1,0:T(8,128)} %copy-done.51, f32[320]{0:T(512)S(1)} %get-tuple-element.249, f32[320]{0:T(512)S(1)} %get-tuple-element.187, s32[7632]{0:T(1024)S(1)} %iota_add_fusion, s32[320]{0:T(512)S(1)} %eq.135, bf16[320,1024]{1,0:T(8,128)(2,1)} %constant_dynamic-update-slice_fusion.4), kind=kOutput, calls=%fused_computation.8 | convolution fusion | flops 5024176128 | bytes 26089024 | tf_op jit(solution)/shard_map/sv,swc->wvc/dot_general | solution.py:943
  385.4 3.4 gradient_block.13
  388.8 3.4 gradient_block.12
  392.7 10.3 %multiply_convert_fusion.refs_1_ = bf16[512,4096]{1,0:T(8,128)(2,1)S(1)} fusion(bf16[512,4096]{1,0:T(8,128)(2,1)} %copy-done.42, bf16[512,1024]{1,0:T(8,128)(2,1)S(1)} %get-tuple-element.189.refs_0_, bf16[1024,12288]{1,0:T(8,128)(2,1)} %all-gather.7.cloned.1.call-done.weight_ref), kind=kOutput, calls=%fused_computation.20 | convolution fusion | flops 4301258752 | bytes 17825792 | tf_op jit(solution)/shard_map/dot_general | solution.py:45
  403.1 4.3 gradient_block.14
  409.8 3.3 gradient_block.15
  414.3 11.2 %multiply_reduce_fusion.2 = (f32[1024]{0:T(1024)S(1)}, f32[512]{0:T(512)S(1)}, f32[1024]{0:T(1024)S(1)}, f32[512,1024]{1,0:T(8,128)}) fusion(f32[512,1024]{1,0:T(8,128)} %copy-done.47, f32[512]{0:T(512)S(1)} %fusion.71, f32[512]{0:T(512)S(1)} %broadcast_multiply_fusion.2, f32[1024]{0:T(1024)S(1)} %bitcast.208, ...), kind=kOutput, calls=%fused_computation.40 | convolution fusion | flops 4300207616 | bytes 18894848 | tf_op jit(solution)/shard_map/dot_general | solution.py:55
  432.8 3.4 gradient_block.17
  436.5 16.6 %attend_back.1.refs_2_.dqkv_ref = bf16[512,3072]{1,0:T(8,128)(2,1)S(1)} custom-call(bf16[512,3072]{1,0:T(8,128)(2,1)S(1)} %copy-done.1, bf16[512,3072]{1,0:T(8,128)(2,1)S(1)} %copy-done.1, bf16[512,3072]{1,0:T(8,128)(2,1)S(1)} %copy-done.1, bf16[512,1024]{1,0:T(8,128)(2,1)S(1)} %fusion.29.do_ref, f32[8,2,512]{2,1,0:T(2,128)S(1)} %get-tuple-element.114.lse_ref, ...), custom_call_target="tpu_custom_call" | custom-call | tf_op jit(solution)/shard_map/attend_back/pallas_call | solution.py:126
  453.1 8.2 collective-permute-done.29.refs_3_
  461.3 3.3 gradient_block.18
  470.4 4.9 gradient_block.21
  478.0 3.3 convert_reduce_fusion
  485.0 4.0 gradient_block.19
  490.4 8.1 embed_back.1
  499.8 35.7 %collective-permute-done.31.refs_3_ = bf16[256,4096]{1,0:T(8,128)(2,1)} collective-permute-done((bf16[256,4096]{1,0:T(8,128)(2,1)}, bf16[256,4096]{1,0:T(8,128)(2,1)}, u32[]{:S(2)}, u32[]{:S(2)}) %collective-permute-start.31) | collective-permute-done | bytes 2097184 | tf_op jit(solution)/shard_map/ppermute | solution.py:448
  535.5 6.9 concatenate.84
  548.9 3.3 gradient_block.20
  557.2 4.2 gradient_block.23
  563.8 4.2 all-to-all-start.1
  577.2 11.0 %collective-permute-done.33 = bf16[528,256]{1,0:T(8,128)(2,1)S(1)} collective-permute-done((bf16[528,256]{1,0:T(8,128)(2,1)S(1)}, bf16[528,256]{1,0:T(8,128)(2,1)S(1)}, u32[]{:S(2)}, u32[]{:S(2)}) %collective-permute-start.33) | collective-permute-done | bytes 270368 | tf_op jit(solution)/shard_map/ppermute | solution.py:837
  588.3 22.5 %collective-permute-done.36.refs_5_ = bf16[256,4096]{1,0:T(8,128)(2,1)} collective-permute-done((bf16[256,4096]{1,0:T(8,128)(2,1)}, bf16[256,4096]{1,0:T(8,128)(2,1)}, u32[]{:S(2)}, u32[]{:S(2)}) %collective-permute-start.36) | collective-permute-done | bytes 2097184 | tf_op jit(solution)/shard_map/ppermute | solution.py:448
  610.8 5.2 gradient_block.22
  624.5 6.4 span.3
  632.2 6.5 span.4
  643.3 6.4 span.5
  653.6 21.1 %press.1 = (f32[1,256,12288]{2,1,0:T(8,128)}, bf16[4,256,1536]{2,1,0:T(8,128)(2,1)}, bf16[4,256,1536]{2,1,0:T(8,128)(2,1)}) custom-call(s32[1]{0:T(128)} %bitcast.4.core_ref, f32[2]{0:T(128)} %pad_maximum_fusion.5.scale_ref, f32[256,4096]{1,0:T(8,128)} %get-tuple-element.139.refs_0_, f32[256,4096]{1,0:T(8,128)} %get-tuple-element.140.refs_1_, ...), custom_call_target="tpu_custom_call" | custom-call | tf_op jit(solution)/shard_map/press/pallas_call | solution.py:741
  674.8 26.1 %collective-permute-start.40 = (bf16[4,256,1536]{2,1,0:T(8,128)(2,1)}, bf16[4,256,1536]{2,1,0:T(8,128)(2,1)S(1)}, u32[]{:S(2)}, u32[]{:S(2)}) collective-permute-start(bf16[4,256,1536]{2,1,0:T(8,128)(2,1)} %get-tuple-element.143), channel_id=1, source_target_pairs={{0,4},{4,0},{8,12},{12,8},{16,20},{20,16},{24,28},{28,24},{1,5},{5... | collective-permute-start | bytes 9437192 | tf_op jit(solution)/shard_map/ppermute | solution.py:810
  700.8 5.5 collective-permute-done.40
  706.3 3.7 fusion.44
  713.5 8.5 collective-permute-done.42
  725.9 4.0 collective-permute-done.41
  729.9 6.3 collective-permute-done.43
  739.1 3.6 collective-permute-done.44
  752.6 5.9 all-gather.15.cloned.1.call-done
  758.5 36.1 %add_rows.1.grad_ref = f32[7632,128]{1,0:T(8,128)} custom-call(s32[16384]{0:T(1024)} %copy-done.41, bf16[4,4624,128]{2,1,0:T(8,128)(2,1)} %bitcast.185), custom_call_target="tpu_custom_call" | custom-call | tf_op jit(solution)/shard_map/add_rows/pallas_call | solution.py:639
  794.6 12.6 %update.1 = (f32[7632,128]{1,0:T(8,128)}, f32[7632,128]{1,0:T(8,128)}, f32[1,128]{1,0:T(1,128)}, f32[1,128]{1,0:T(1,128)}) custom-call(f32[7632,128]{1,0:T(8,128)} %add_rows.1.grad_ref, bf16[7632,128]{1,0:T(8,128)(2,1)} %bitcast.189, f32[7632,128]{1,0:T(8,128)} %table_ref.3, f32[7632,128]{1,0:T(8,128)} %first_ref.1, f32[7632,128]{1,0:T(8,128)} %second_ref.1), custom_call_target="tpu_custom_call" | custom-call | tf_op jit(solution)/shard_map/update/pallas_call | solution.py:786
  816.6 3.3 multiply_reduce_fusion.8
  822.1 9.1 %convert_element_type.365 = f32[256,12288]{1,0:T(8,128)} convert(bf16[256,12288]{1,0:T(8,128)(2,1)} %all-gather.11.cloned.1.call-done) | non-fusion elementwise | flops 3145728 | bytes 18874368 | tf_op jit(solution)/shard_map/convert_element_type | solution.py:1058
  838.2 3.5 collective-permute-done.50
  842.6 3.6 collective-permute-done.51
  850.3 4.4 multiply_subtract_fusion.2
  860.4 4.8 multiply_subtract_fusion
  865.2 3.3 multiply_subtract_fusion.1
  (412 shorter events, 204.2 us)
Async XLA Ops:
  7.2 221.5 %all-gather.7.cloned.1.call-start = ((), (), s32[]{:S(2)}) async-start(), calls=%async_computation.3 | async-start | bytes 28311552 | tf_op jit(solution)/shard_map/all_gather | solution.py:881
  8.0 1.3 collective-permute-start.6
  10.1 4.7 collective-permute-start.7
  14.9 9.2 %collective-permute-start.8 = (s32[4,4,672]{2,1,0:T(4,128)S(1)}, s32[4,4,672]{2,1,0:T(4,128)S(1)}, u32[]{:S(2)}, u32[]{:S(2)}) collective-permute-start(s32[4,4,672]{2,1,0:T(4,128)S(1)} %pad_add_fusion.1), channel_id=1, source_target_pairs={{0,16},{4,20},{8,24},{12,28},{16,0},{20,4},{24,8},{28,12},{1,17},{... | collective-permute-start | bytes 129032 | tf_op jit(solution)/shard_map/ppermute | solution.py:481
  18.5 60.6 %copy-start.55 = (bf16[256,1536]{1,0:T(8,128)(2,1)}, bf16[256,1536]{1,0:T(8,128)(2,1)S(1)}, u32[]{:S(2)}) copy-start(bf16[256,1536]{1,0:T(8,128)(2,1)S(1)} %convert_element_type.288) | copy-start | bytes 2359300
  18.5 60.5 %collective-permute-start.5 = (bf16[256,1536]{1,0:T(8,128)(2,1)S(1)}, bf16[256,1536]{1,0:T(8,128)(2,1)S(1)}, u32[]{:S(2)}, u32[]{:S(2)}) collective-permute-start(bf16[256,1536]{1,0:T(8,128)(2,1)S(1)} %convert_element_type.288), channel_id=1, source_target_pairs={{0,1},{1,2},{2,3},{3,0},{4,5},{5,6},{6,7},{7,4},{8,9},{9,10},{10,1... | collective-permute-start | bytes 2359304 | tf_op jit(solution)/shard_map/ppermute | solution.py:341
  20.1 58.9 %collective-permute-start.4 = (bf16[256,1536]{1,0:T(8,128)(2,1)S(1)}, bf16[256,1536]{1,0:T(8,128)(2,1)S(1)}, u32[]{:S(2)}, u32[]{:S(2)}) collective-permute-start(bf16[256,1536]{1,0:T(8,128)(2,1)S(1)} %convert_element_type.288), channel_id=1, source_target_pairs={{0,2},{1,3},{2,0},{3,1},{4,6},{5,7},{6,4},{7,5},{8,10},{9,11},{10,... | collective-permute-start | bytes 2359304 | tf_op jit(solution)/shard_map/ppermute | solution.py:341
  22.7 58.1 %collective-permute-start.3 = (bf16[256,1536]{1,0:T(8,128)(2,1)S(1)}, bf16[256,1536]{1,0:T(8,128)(2,1)}, u32[]{:S(2)}, u32[]{:S(2)}) collective-permute-start(bf16[256,1536]{1,0:T(8,128)(2,1)S(1)} %convert_element_type.288), channel_id=1, source_target_pairs={{0,3},{1,0},{2,1},{3,2},{4,7},{5,4},{6,5},{7,6},{8,11},{9,8},{10,9... | collective-permute-start | bytes 2359304 | tf_op jit(solution)/shard_map/ppermute | solution.py:341
  26.6 52.4 %copy-start.41 = (s32[16384]{0:T(1024)}, s32[16384]{0:T(1024)S(1)}, u32[]{:S(2)}) copy-start(s32[16384]{0:T(1024)S(1)} %fusion.57.ids_ref) | copy-start | bytes 196612
  87.2 21.9 %collective-permute-start.11 = (bf16[1792,128]{1,0:T(8,128)(2,1)S(1)}, bf16[1792,128]{1,0:T(8,128)(2,1)S(1)}, u32[]{:S(2)}, u32[]{:S(2)}) collective-permute-start(bf16[1792,128]{1,0:T(8,128)(2,1)S(1)} %get-tuple-element.226), channel_id=1, source_target_pairs={{0,3},{1,0},{2,1},{3,2},{4,7},{5,4},{6,5},{7,6},{8,11},{9,8},{10,9... | collective-permute-start | bytes 1376264 | tf_op jit(solution)/shard_map/ppermute | solution.py:373
  98.1 39.6 %collective-permute-start.10 = (bf16[1792,128]{1,0:T(8,128)(2,1)S(1)}, bf16[1792,128]{1,0:T(8,128)(2,1)S(1)}, u32[]{:S(2)}, u32[]{:S(2)}) collective-permute-start(bf16[1792,128]{1,0:T(8,128)(2,1)S(1)} %get-tuple-element.227), channel_id=1, source_target_pairs={{0,2},{1,3},{2,0},{3,1},{4,6},{5,7},{6,4},{7,5},{8,10},{9,11},{10,... | collective-permute-start | bytes 1376264 | tf_op jit(solution)/shard_map/ppermute | solution.py:373
  98.1 39.6 %collective-permute-start.9 = (bf16[1792,128]{1,0:T(8,128)(2,1)S(1)}, bf16[1792,128]{1,0:T(8,128)(2,1)S(1)}, u32[]{:S(2)}, u32[]{:S(2)}) collective-permute-start(bf16[1792,128]{1,0:T(8,128)(2,1)S(1)} %get-tuple-element.228), channel_id=1, source_target_pairs={{0,1},{1,2},{2,3},{3,0},{4,5},{5,6},{6,7},{7,4},{8,9},{9,10},{10,1... | collective-permute-start | bytes 1376264 | tf_op jit(solution)/shard_map/ppermute | solution.py:373
  147.7 34.4 %all-to-all-start = ((bf16[8,512,128]{2,1,0:T(8,128)(2,1)}), bf16[8,512,128]{2,1,0:T(8,128)(2,1)S(1)}, u32[]{:S(2)}, u32[]{:S(2)}) async-start(bf16[8,512,128]{2,1,0:T(8,128)(2,1)} %bitcast.188), calls=%async_computation | async-start | bytes 2097152 | tf_op jit(solution)/shard_map/all_to_all | solution.py:891
  151.3 167.0 %all-gather.9.cloned.1.call-start = ((), (), s32[]{:S(2)}) async-start(), calls=%async_computation.4 | async-start | bytes 17584128 | tf_op jit(solution)/shard_map/all_gather | solution.py:910
  151.9 5.2 collective-permute-start.12
  152.3 29.8 %collective-permute-start.15 = (s32[1,592]{1,0:T(1,128)S(1)}, s32[1,592]{1,0:T(1,128)S(1)}, u32[]{:S(2)}, u32[]{:S(2)}) collective-permute-start(s32[1,592]{1,0:T(1,128)S(1)} %pad_add_fusion.3), channel_id=1, source_target_pairs={{0,0},{1,4},{2,1},{3,5},{4,2},{5,6},{6,3},{7,7},{8,8},{9,12},{10,9... | collective-permute-start | bytes 7112 | tf_op jit(solution)/shard_map/ppermute | solution.py:494
  158.5 18.6 %collective-permute-start.13 = (f32[]{:T(128)}, f32[]{:T(128)}, u32[]{:S(2)}, u32[]{:S(2)}) collective-permute-start(f32[]{:T(128)} %add.645), channel_id=1, source_target_pairs={{0,8},{4,12},{8,0},{12,4},{16,24},{20,28},{24,16},{28,20},{1,9},{5... | collective-permute-start | bytes 20 | tf_op jit(solution)/shard_map/ppermute | solution.py:331
  177.8 3.6 collective-permute-start.14
  182.1 48.0 %copy-start.74 = (s32[1,80]{1,0:T(1,128)}, s32[1,80]{1,0:T(1,128)S(1)}, u32[]{:S(2)}) copy-start(s32[1,80]{1,0:T(1,128)S(1)} %slice.193) | copy-start | bytes 964
  187.6 61.2 %copy-start.23 = (f32[512,1024]{1,0:T(8,128)}, f32[512,1024]{1,0:T(8,128)S(1)}, u32[]{:S(2)}) copy-start(f32[512,1024]{1,0:T(8,128)S(1)} %get-tuple-element.200.embedded_ref) | copy-start | bytes 6291460
  188.0 49.1 %copy-start.12 = (bf16[512,1024]{1,0:T(8,128)(2,1)}, bf16[512,1024]{1,0:T(8,128)(2,1)S(1)}, u32[]{:S(2)}) copy-start(bf16[512,1024]{1,0:T(8,128)(2,1)S(1)} %fusion.23.refs_0_) | copy-start | bytes 3145732
  228.7 414.5 %reduce-scatter.2.cloned.1.call-start = ((), (), s32[]{:S(2)}) async-start(), calls=%async_computation.5 | async-start | bytes 17584128 | tf_op jit(solution)/shard_map/reduce_scatter | solution.py:945
  253.1 179.7 %copy-start.10 = (bf16[512,1024]{1,0:T(8,128)(2,1)}, bf16[512,1024]{1,0:T(8,128)(2,1)S(1)}, u32[]{:S(2)}) copy-start(bf16[512,1024]{1,0:T(8,128)(2,1)S(1)} %fusion.22.fin_ref.refs_0_) | copy-start | bytes 3145732
  283.4 12.4 %collective-permute-start.17 = (bf16[80,1024]{1,0:T(8,128)(2,1)}, bf16[80,1024]{1,0:T(8,128)(2,1)}, u32[]{:S(2)}, u32[]{:S(2)}) collective-permute-start(bf16[80,1024]{1,0:T(8,128)(2,1)} %get-tuple-element.198), channel_id=1, source_target_pairs={{0,2},{1,3},{2,0},{3,1},{4,6},{5,7},{6,4},{7,5},{8,10},{9,11},{10,... | collective-permute-start | bytes 491528 | tf_op jit(solution)/shard_map/ppermute | solution.py:341
  285.7 8.4 collective-permute-start.16
  287.4 11.5 %collective-permute-start.18 = (bf16[80,1024]{1,0:T(8,128)(2,1)}, bf16[80,1024]{1,0:T(8,128)(2,1)S(1)}, u32[]{:S(2)}, u32[]{:S(2)}) collective-permute-start(bf16[80,1024]{1,0:T(8,128)(2,1)} %get-tuple-element.198), channel_id=1, source_target_pairs={{0,1},{1,2},{2,3},{3,0},{4,5},{5,6},{6,7},{7,4},{8,9},{9,10},{10,1... | collective-permute-start | bytes 491528 | tf_op jit(solution)/shard_map/ppermute | solution.py:341
  330.1 6.1 collective-permute-start.20
  332.6 3.6 collective-permute-start.19
  334.0 5.4 collective-permute-start.21
  350.9 22.1 %collective-permute-start.22 = (bf16[80,1024]{1,0:T(8,128)(2,1)}, bf16[80,1024]{1,0:T(8,128)(2,1)}, u32[]{:S(2)}, u32[]{:S(2)}) collective-permute-start(bf16[80,1024]{1,0:T(8,128)(2,1)} %get-tuple-element.229), channel_id=1, source_target_pairs={{0,1},{1,2},{2,3},{3,0},{4,5},{5,6},{6,7},{7,4},{8,9},{9,10},{10,1... | collective-permute-start | bytes 491528 | tf_op jit(solution)/shard_map/ppermute | solution.py:360
  350.9 22.1 %collective-permute-start.24 = (bf16[80,1024]{1,0:T(8,128)(2,1)}, bf16[80,1024]{1,0:T(8,128)(2,1)}, u32[]{:S(2)}, u32[]{:S(2)}) collective-permute-start(bf16[80,1024]{1,0:T(8,128)(2,1)} %get-tuple-element.230), channel_id=1, source_target_pairs={{0,3},{1,0},{2,1},{3,2},{4,7},{5,4},{6,5},{7,6},{8,11},{9,8},{10,9... | collective-permute-start | bytes 491528 | tf_op jit(solution)/shard_map/ppermute | solution.py:360
  355.2 17.8 %collective-permute-start.23 = (bf16[80,1024]{1,0:T(8,128)(2,1)}, bf16[80,1024]{1,0:T(8,128)(2,1)}, u32[]{:S(2)}, u32[]{:S(2)}) collective-permute-start(bf16[80,1024]{1,0:T(8,128)(2,1)} %get-tuple-element.231), channel_id=1, source_target_pairs={{0,2},{1,3},{2,0},{3,1},{4,6},{5,7},{6,4},{7,5},{8,10},{9,11},{10,... | collective-permute-start | bytes 491528 | tf_op jit(solution)/shard_map/ppermute | solution.py:360
  392.2 10.8 %collective-permute-start.25 = (bf16[256,4096]{1,0:T(8,128)(2,1)}, bf16[256,4096]{1,0:T(8,128)(2,1)}, u32[]{:S(2)}, u32[]{:S(2)}) collective-permute-start(bf16[256,4096]{1,0:T(8,128)(2,1)} %gradient_block.12), channel_id=1, source_target_pairs={{0,4},{4,0},{8,12},{12,8},{16,20},{20,16},{24,28},{28,24},{1,5},{5... | collective-permute-start | bytes 6291464 | tf_op jit(solution)/shard_map/ppermute | solution.py:432
  392.2 10.8 %collective-permute-start.26 = (bf16[256,4096]{1,0:T(8,128)(2,1)}, bf16[256,4096]{1,0:T(8,128)(2,1)}, u32[]{:S(2)}, u32[]{:S(2)}) collective-permute-start(bf16[256,4096]{1,0:T(8,128)(2,1)} %gradient_block.13), channel_id=1, source_target_pairs={{0,4},{4,0},{8,12},{12,8},{16,20},{20,16},{24,28},{28,24},{1,5},{5... | collective-permute-start | bytes 6291464 | tf_op jit(solution)/shard_map/ppermute | solution.py:433
  413.1 19.6 %collective-permute-start.27 = (bf16[256,4096]{1,0:T(8,128)(2,1)}, bf16[256,4096]{1,0:T(8,128)(2,1)S(1)}, u32[]{:S(2)}, u32[]{:S(2)}) collective-permute-start(bf16[256,4096]{1,0:T(8,128)(2,1)} %gradient_block.15), channel_id=1, source_target_pairs={{0,4},{4,0},{8,12},{12,8},{16,20},{20,16},{24,28},{28,24},{1,5},{5... | collective-permute-start | bytes 6291464 | tf_op jit(solution)/shard_map/ppermute | solution.py:432
  413.2 19.5 %collective-permute-start.28 = (bf16[256,4096]{1,0:T(8,128)(2,1)S(1)}, bf16[256,4096]{1,0:T(8,128)(2,1)S(1)}, u32[]{:S(2)}, u32[]{:S(2)}) collective-permute-start(bf16[256,4096]{1,0:T(8,128)(2,1)S(1)} %gradient_block.16), channel_id=1, source_target_pairs={{0,4},{4,0},{8,12},{12,8},{16,20},{20,16},{24,28},{28,24},{1,5},{5... | collective-permute-start | bytes 6291464 | tf_op jit(solution)/shard_map/ppermute | solution.py:433
  413.6 47.6 %collective-permute-start.29 = (bf16[256,4096]{1,0:T(8,128)(2,1)S(1)}, bf16[256,4096]{1,0:T(8,128)(2,1)S(1)}, u32[]{:S(2)}, u32[]{:S(2)}) collective-permute-start(bf16[256,4096]{1,0:T(8,128)(2,1)S(1)} %gradient_block.14), channel_id=1, source_target_pairs={{0,1},{1,0},{2,3},{3,2},{4,5},{5,4},{6,7},{7,6},{8,9},{9,8},{10,11... | collective-permute-start | bytes 6291464 | tf_op jit(solution)/shard_map/ppermute | solution.py:448
  464.6 16.7 %collective-permute-start.30 = (bf16[256,4096]{1,0:T(8,128)(2,1)}, bf16[256,4096]{1,0:T(8,128)(2,1)}, u32[]{:S(2)}, u32[]{:S(2)}) collective-permute-start(bf16[256,4096]{1,0:T(8,128)(2,1)} %gradient_block.18), channel_id=1, source_target_pairs={{0,4},{4,0},{8,12},{12,8},{16,20},{20,16},{24,28},{28,24},{1,5},{5... | collective-permute-start | bytes 6291464 | tf_op jit(solution)/shard_map/ppermute | solution.py:432
  464.6 70.8 %collective-permute-start.31 = (bf16[256,4096]{1,0:T(8,128)(2,1)}, bf16[256,4096]{1,0:T(8,128)(2,1)}, u32[]{:S(2)}, u32[]{:S(2)}) collective-permute-start(bf16[256,4096]{1,0:T(8,128)(2,1)} %gradient_block.17), channel_id=1, source_target_pairs={{0,1},{1,0},{2,3},{3,2},{4,5},{5,4},{6,7},{7,6},{8,9},{9,8},{10,11... | collective-permute-start | bytes 6291464 | tf_op jit(solution)/shard_map/ppermute | solution.py:448
  475.3 98.8 %collective-permute-start.37 = (bf16[256,4096]{1,0:T(8,128)(2,1)}, bf16[256,4096]{1,0:T(8,128)(2,1)}, u32[]{:S(2)}, u32[]{:S(2)}) collective-permute-start(bf16[256,4096]{1,0:T(8,128)(2,1)} %gradient_block.21), channel_id=1, source_target_pairs={{2,4},{3,5},{4,2},{5,3},{10,12},{11,13},{12,10},{13,11},{18,20},{1... | collective-permute-start | bytes 6291464 | tf_op jit(solution)/shard_map/ppermute | solution.py:472
  544.5 26.0 %collective-permute-start.32 = (bf16[528,512]{1,0:T(8,128)(2,1)}, bf16[528,512]{1,0:T(8,128)(2,1)}, u32[]{:S(2)}, u32[]{:S(2)}) collective-permute-start(bf16[528,512]{1,0:T(8,128)(2,1)} %dynamic-slice_convert_fusion), channel_id=1, source_target_pairs={{0,16},{4,20},{8,24},{12,28},{16,0},{20,4},{24,8},{28,12},{1,17},{... | collective-permute-start | bytes 1622024 | tf_op jit(solution)/shard_map/ppermute | solution.py:837
  545.2 65.6 %collective-permute-start.36 = (bf16[256,4096]{1,0:T(8,128)(2,1)}, bf16[256,4096]{1,0:T(8,128)(2,1)}, u32[]{:S(2)}, u32[]{:S(2)}) collective-permute-start(bf16[256,4096]{1,0:T(8,128)(2,1)} %copy-done.37), channel_id=1, source_target_pairs={{0,1},{1,0},{2,3},{3,2},{4,5},{5,4},{6,7},{7,6},{8,9},{9,8},{10,11... | collective-permute-start | bytes 6291464 | tf_op jit(solution)/shard_map/ppermute | solution.py:448
  552.2 58.7 %collective-permute-start.35 = (bf16[256,4096]{1,0:T(8,128)(2,1)}, bf16[256,4096]{1,0:T(8,128)(2,1)}, u32[]{:S(2)}, u32[]{:S(2)}) collective-permute-start(bf16[256,4096]{1,0:T(8,128)(2,1)} %gradient_block.20), channel_id=1, source_target_pairs={{0,4},{4,0},{8,12},{12,8},{16,20},{20,16},{24,28},{28,24},{1,5},{5... | collective-permute-start | bytes 6291464 | tf_op jit(solution)/shard_map/ppermute | solution.py:433
  563.8 56.8 %all-to-all-start.1 = ((bf16[8,512,128]{2,1,0:T(8,128)(2,1)}), bf16[8,512,128]{2,1,0:T(8,128)(2,1)}, u32[]{:S(2)}, u32[]{:S(2)}) async-start(bf16[8,512,128]{2,1,0:T(8,128)(2,1)} %bitcast_bitcast_fusion), calls=%async_computation.1 | async-start | bytes 2097152 | tf_op jit(solution)/shard_map/all_to_all | solution.py:961
  568.1 190.4 %all-gather.15.cloned.1.call-start = ((), (), s32[]{:S(2)}) async-start(), calls=%async_computation.8 | async-start | bytes 5918720 | tf_op jit(solution)/shard_map/all_gather | solution.py:971
  568.1 54.8 %collective-permute-start.39 = (bf16[256,4096]{1,0:T(8,128)(2,1)}, bf16[256,4096]{1,0:T(8,128)(2,1)}, u32[]{:S(2)}, u32[]{:S(2)}) collective-permute-start(bf16[256,4096]{1,0:T(8,128)(2,1)} %copy-done.33), channel_id=1, source_target_pairs={{2,4},{3,5},{4,2},{5,3},{10,12},{11,13},{12,10},{13,11},{18,20},{1... | collective-permute-start | bytes 6291464 | tf_op jit(solution)/shard_map/ppermute | solution.py:472
  572.2 38.7 %copy-start.16 = (bf16[512,1024]{1,0:T(8,128)(2,1)S(1)}, bf16[512,1024]{1,0:T(8,128)(2,1)}, u32[]{:S(2)}) copy-start(bf16[512,1024]{1,0:T(8,128)(2,1)} %copy-done.12) | copy-start | bytes 3145732
  572.2 16.1 %collective-permute-start.33 = (bf16[528,256]{1,0:T(8,128)(2,1)S(1)}, bf16[528,256]{1,0:T(8,128)(2,1)S(1)}, u32[]{:S(2)}, u32[]{:S(2)}) collective-permute-start(bf16[528,256]{1,0:T(8,128)(2,1)S(1)} %dynamic-slice_convert_fusion.1), channel_id=1, source_target_pairs={{0,8},{4,12},{8,0},{12,4},{16,24},{20,28},{24,16},{28,20},{1,9},{5... | collective-permute-start | bytes 811016 | tf_op jit(solution)/shard_map/ppermute | solution.py:837
  616.0 24.1 %collective-permute-start.38 = (bf16[256,4096]{1,0:T(8,128)(2,1)}, bf16[256,4096]{1,0:T(8,128)(2,1)}, u32[]{:S(2)}, u32[]{:S(2)}) collective-permute-start(bf16[256,4096]{1,0:T(8,128)(2,1)} %gradient_block.22), channel_id=1, source_target_pairs={{2,4},{3,5},{4,2},{5,3},{10,12},{11,13},{12,10},{13,11},{18,20},{1... | collective-permute-start | bytes 6291464 | tf_op jit(solution)/shard_map/ppermute | solution.py:472
  618.2 1.4 collective-permute-start.34
  643.2 168.2 %all-gather.11.cloned.1.call-start = ((), (), s32[]{:S(2)}) async-start(), calls=%async_computation.6 | async-start | bytes 7077888 | tf_op jit(solution)/shard_map/all_gather | solution.py:1022
  674.8 31.6 %collective-permute-start.40 = (bf16[4,256,1536]{2,1,0:T(8,128)(2,1)}, bf16[4,256,1536]{2,1,0:T(8,128)(2,1)S(1)}, u32[]{:S(2)}, u32[]{:S(2)}) collective-permute-start(bf16[4,256,1536]{2,1,0:T(8,128)(2,1)} %get-tuple-element.143), channel_id=1, source_target_pairs={{0,4},{4,0},{8,12},{12,8},{16,20},{20,16},{24,28},{28,24},{1,5},{5... | collective-permute-start | bytes 9437192 | tf_op jit(solution)/shard_map/ppermute | solution.py:810
  710.0 11.9 %collective-permute-start.42 = (bf16[128,1536]{1,0:T(8,128)(2,1)S(1)}, bf16[128,1536]{1,0:T(8,128)(2,1)S(1)}, u32[]{:S(2)}, u32[]{:S(2)}) collective-permute-start(bf16[128,1536]{1,0:T(8,128)(2,1)S(1)} %get-tuple-element.212), channel_id=1, source_target_pairs={{0,8},{4,12},{8,0},{12,4},{16,24},{20,28},{24,16},{28,20},{1,9},{5... | collective-permute-start | bytes 1179656 | tf_op jit(solution)/shard_map/ppermute | solution.py:810
  711.1 18.8 %collective-permute-start.41 = (bf16[128,1536]{1,0:T(8,128)(2,1)}, bf16[128,1536]{1,0:T(8,128)(2,1)S(1)}, u32[]{:S(2)}, u32[]{:S(2)}) collective-permute-start(bf16[128,1536]{1,0:T(8,128)(2,1)} %get-tuple-element.209), channel_id=1, source_target_pairs={{0,8},{4,12},{8,0},{12,4},{16,24},{20,28},{24,16},{28,20},{1,9},{5... | collective-permute-start | bytes 1179656 | tf_op jit(solution)/shard_map/ppermute | solution.py:810
  712.1 17.8 %collective-permute-start.45 = (bf16[128,1536]{1,0:T(8,128)(2,1)}, bf16[128,1536]{1,0:T(8,128)(2,1)}, u32[]{:S(2)}, u32[]{:S(2)}) collective-permute-start(bf16[128,1536]{1,0:T(8,128)(2,1)} %get-tuple-element.210), channel_id=1, source_target_pairs={{0,16},{4,20},{8,24},{12,28},{16,0},{20,4},{24,8},{28,12},{1,17},{... | collective-permute-start | bytes 1179656 | tf_op jit(solution)/shard_map/ppermute | solution.py:810
  723.9 12.3 %collective-permute-start.43 = (bf16[128,1536]{1,0:T(8,128)(2,1)}, bf16[128,1536]{1,0:T(8,128)(2,1)S(1)}, u32[]{:S(2)}, u32[]{:S(2)}) collective-permute-start(bf16[128,1536]{1,0:T(8,128)(2,1)} %fusion.40), channel_id=1, source_target_pairs={{0,16},{4,20},{8,24},{12,28},{16,0},{20,4},{24,8},{28,12},{1,17},{... | collective-permute-start | bytes 1179656 | tf_op jit(solution)/shard_map/ppermute | solution.py:810
  725.3 17.4 %collective-permute-start.44 = (bf16[128,1536]{1,0:T(8,128)(2,1)}, bf16[128,1536]{1,0:T(8,128)(2,1)S(1)}, u32[]{:S(2)}, u32[]{:S(2)}) collective-permute-start(bf16[128,1536]{1,0:T(8,128)(2,1)} %get-tuple-element.211), channel_id=1, source_target_pairs={{0,16},{4,20},{8,24},{12,28},{16,0},{20,4},{24,8},{28,12},{1,17},{... | collective-permute-start | bytes 1179656 | tf_op jit(solution)/shard_map/ppermute | solution.py:810
  737.9 7.8 collective-permute-start.46
  752.4 93.8 %all-gather.13.cloned.1.call-start = ((), (), s32[]{:S(2)}) async-start(), calls=%async_computation.7 | async-start | bytes 1216512 | tf_op jit(solution)/shard_map/all_gather | solution.py:1025
  822.1 9.1 %collective-permute-start.47 = (f32[12]{0:T(128)S(1)}, f32[12]{0:T(128)S(1)}, u32[]{:S(2)}, u32[]{:S(2)}) collective-permute-start(f32[12]{0:T(128)S(1)} %concatenate.87), channel_id=1, source_target_pairs={{0,4},{4,0},{8,12},{12,8},{16,20},{20,16},{24,28},{28,24},{1,5},{5... | collective-permute-start | bytes 152 | tf_op jit(solution)/shard_map/ppermute | solution.py:331
  831.1 3.5 collective-permute-start.48
  834.7 3.5 collective-permute-start.49
  838.2 3.5 collective-permute-start.50
  841.8 4.4 collective-permute-start.51
  (70 other events, 523.6 us)
Sparse Core Ops, SparseCore 0:
  84.5 144.1 all-gather.6
  231.2 87.0 all-gather.8
  375.2 111.6 reduce-scatter.1
  643.4 115.0 all-gather.14
  761.0 43.9 all-gather.10
  811.6 22.2 all-gather.12

commit v12 on v11

--- a/solution.py
+++ b/solution.py
@@ -874,18 +874,25 @@
             token_ids, mlm_labels, mlm_valid, doc_ids, mlm_pos
         )
         owners = Owners(token_ids.reshape(n_narrow, n_wide * L), vshard)
-        picked = packed_rows(owners.slots, table)
-        layer_rows, picked = gathered_near(layer_low, picked)
+        table_cut = vshard // 2 // 16 * 16
+        table_first = lax.all_gather(table_low[0:table_cut], "wide", axis=1, tiled=True)
+        half = layer_low.shape[0] // 2
+        first_rows = gathered_near(layer_low[0:half])
+        first_rows, table_first = together(first_rows, table_first)
+        slots, first_rows = together(owners.slots, first_rows)
+        first_weights = lax.all_gather(first_rows, "wide", axis=1, tiled=True)
+        picked = packed_rows(slots, table)
+        last_rows, picked = gathered_near(layer_low[half:], picked)
+        last_weights = lax.all_gather(last_rows, "wide", axis=1, tiled=True)
     else:
         layer_rows = lax.all_gather(layer_low, "narrow", axis=0, tiled=True)
-    weights = lax.all_gather(layer_rows, "wide", axis=1, tiled=True)
+        weights = lax.all_gather(layer_rows, "wide", axis=1, tiled=True)
     if paired:
 
         def looked_up(room):
             rows = sent_around(picked[:, 0:room])
             return taken_rows(owners.behind_slots(room), jnp.concatenate(rows, axis=0))
 
-        layer_rows, picked = together(layer_rows, picked)
         looked = looked_up(owners.room)
         looked = lax.cond(owners.full, lambda: looked_up(owners.count), lambda: looked)
         looked = lax.all_to_all(looked.reshape(n_wide, L, -1), "wide", 0, 0)
@@ -906,8 +913,18 @@
     x0 = norm_rows(embedded, small[L + 2], small[L + 3])
     act = x0.astype(jnp.bfloat16)
     if paired:
-        table_low, weights, act = together(table_low, weights, act)
-        table_cols = lax.all_gather(table_low, "wide", axis=1, tiled=True)
+        whole = jnp.zeros((n_narrow, 2, half, last_weights.shape[1]), jnp.bfloat16)
+        cut_shape = (n_narrow, 1, half, last_weights.shape[1])
+        whole = lax.dynamic_update_slice(whole, first_weights.reshape(cut_shape), (0, 0, 0, 0))
+        last_weights, act, whole = together(last_weights, act, whole)
+        whole = lax.dynamic_update_slice(whole, last_weights.reshape(cut_shape), (0, 1, 0, 0))
+        weights = whole.reshape(D, -1)
+        table_last, last_weights = together(table_low[table_cut:], last_weights)
+        table_last = lax.all_gather(table_last, "wide", axis=1, tiled=True)
+        table_cols = lax.dynamic_update_slice(
+            jnp.zeros((vshard, D), jnp.bfloat16), table_first, (0, 0)
+        )
+        table_cols = lax.dynamic_update_slice(table_cols, table_last, (table_cut, 0))
     htwo, kept = layer_forward(embedded, x0, act, doc_ids, small, weights)
     hmask = jnp.take_along_axis(htwo.reshape(seqs, L, D), mlm_pos[..., None], axis=1)
     hmask = hmask.reshape(seqs * MPS, D).astype(jnp.bfloat16)

time: 884 us -> 897 us (1.015)
  local copies, waits for them, and re-layouts: 65.4 us -> 107 us
  waiting for transfers between devices: 243 us -> 216 us
    all_gather x2 -> x4, waiting for transfers between devices: 59.4 us -> 9.37 us  [the longest x1 9.35 us: shards(): lax.all_gather(table_low[0:table_cut], 'wide', axis=1, tiled=True)]
    dynamic_update_slice x0 -> x3, local copies, waits for them, and re-layouts: none -> 32.1 us  [the longest x1 14.3 us: shards(): lax.dynamic_update_slice(whole, first_weights.reshape(cut_shape), (0, 0,...]
    ppermute x9 -> x12, waiting for transfers between devices: 12.3 us -> 39.2 us  [gathered_near(): around.append(lax.ppermute(value, 'narrow', cycle(size, size - by)))]
    ppermute x3, waiting for transfers between devices: 38.9 us -> 28.6 us  [sent_around(): lax.ppermute(block(by), 'narrow', cycle(size, by))]
    ppermute x9 -> x12, starting transfers between devices: 14.7 us -> 23.3 us  [gathered_near(): around.append(lax.ppermute(value, 'narrow', cycle(size, size - by)))]
    unnamed x160 -> x177, local copies, waits for them, and re-layouts: 37.9 us -> 43.2 us
  transfers between devices with their start and end apart: 57 -> 62, of which waited for: 28 -> 30; matrix products, arithmetic and copies ran while one was open for 19% -> 23% of each run, Pallas kernels for 27% -> 27%
where the time goes in v12:
time: 897 us; the launch traced here: 888 us
  Pallas kernels  240 us (27%)
  waiting for transfers between devices  216 us (24%)
  starting transfers between devices  111 us (12%)
  local copies, waits for them, and re-layouts  107 us (12%)
  other arithmetic  106 us (12%)
  matrix products  80.3 us (9%)
  between operations  23.7 us (3%)
    ppermute x3, waiting for transfers between devices, across(): self.away = lax.ppermute(away, 'narrow', sides)  72.3 us
    pallas_call x1, Pallas kernels, packed_rows(): pl.pallas_call(pack_kernel, grid_spec=pltpu.PrefetchScalarGridSpec(num_sc...  52.4 us
    pallas_call x12, Pallas kernels, gradient_block(): pl.pallas_call(functools.partial(block_kernel, steps), grid_spec=pltpu.Pr...  45.4 us
    unnamed x177, local copies, waits for them, and re-layouts  43.2 us
    ppermute x12, waiting for transfers between devices, gathered_near(): around.append(lax.ppermute(value, 'narrow', cycle(size, size - by)))  39.2 us
    pallas_call x1, Pallas kernels, added_rows(): pl.pallas_call(add_kernel, grid_spec=pltpu.PrefetchScalarGridSpec(num_sca...  36.2 us
    ppermute x7, waiting for transfers between devices, send(): lax.ppermute(value.astype(jnp.bfloat16), 'wide', swap_pairs(n_wide, bit))  33.4 us
    dot_general x4, matrix products, matmul_nt(): lax.dot_general(left, right, (((1,), (1,)), ((), ())), preferred_element_...  32.2 us
  transfers between devices with their start and end apart: 62, of which 30 were waited for; matrix products, arithmetic and copies ran while one was open for 23% of the time, Pallas kernels for 27%

profile of v12, /device:TPU:0, one launch (start us, length us, event | category | flops | bytes accessed | tf_op | source)
XLA Modules:
  0.0 888.2 jit_solution(10380773198601426464)
XLA Ops:
  20.4 3.7 collective-permute-start.9
  26.2 7.4 collective-permute-done.9
  34.7 21.9 %collective-permute-done.10 = bf16[128,1536]{1,0:T(8,128)(2,1)} collective-permute-done((bf16[128,1536]{1,0:T(8,128)(2,1)S(1)}, bf16[128,1536]{1,0:T(8,128)(2,1)}, u32[]{:S(2)}, u32[]{:S(2)}) %collective-permute-start.10) | collective-permute-done | bytes 393248 | tf_op jit(solution)/shard_map/ppermute | solution.py:341
  58.7 9.3 %all-gather.9.cloned.1.call-done = bf16[3808,1024]{1,0:T(8,128)(2,1)} async-done(((bf16[3808,128]{1,0:T(8,128)(2,1)}), bf16[3808,1024]{1,0:T(8,128)(2,1)}) %all-gather.9.cloned.1.call-update) | async-done | bytes 7798800 | tf_op jit(solution)/shard_map/all_gather | solution.py:878
  68.1 3.4 collective-permute-start.3
  74.7 52.4 %pack_rows.1 = bf16[4,4096,128]{2,1,0:T(8,128)(2,1)} custom-call(s32[16384]{0:T(1024)S(1)} %bitcast.189, f32[7632,128]{1,0:T(8,128)S(1)} %copy-done.8), custom_call_target="tpu_custom_call" | custom-call | tf_op jit(solution)/shard_map/pack_rows/pallas_call | solution.py:568
  136.1 10.5 %collective-permute-done.12 = bf16[1792,128]{1,0:T(8,128)(2,1)S(1)} collective-permute-done((bf16[1792,128]{1,0:T(8,128)(2,1)S(1)}, bf16[1792,128]{1,0:T(8,128)(2,1)S(1)}, u32[]{:S(2)}, u32[]{:S(2)}) %collective-permute-start.12) | collective-permute-done | bytes 458784 | tf_op jit(solution)/shard_map/ppermute | solution.py:373
  146.7 18.0 %collective-permute-done.13 = bf16[1792,128]{1,0:T(8,128)(2,1)S(1)} collective-permute-done((bf16[1792,128]{1,0:T(8,128)(2,1)S(1)}, bf16[1792,128]{1,0:T(8,128)(2,1)S(1)}, u32[]{:S(2)}, u32[]{:S(2)}) %collective-permute-start.13) | collective-permute-done | bytes 458784 | tf_op jit(solution)/shard_map/ppermute | solution.py:373
  164.8 5.5 take_rows.3
  170.3 3.5 conditional.1
  174.8 3.6 all-to-all-start
  184.2 17.6 %collective-permute-start.16 = (f32[]{:T(128)}, f32[]{:T(128)}, u32[]{:S(2)}, u32[]{:S(2)}) collective-permute-start(f32[]{:T(128)} %add.654), channel_id=1, source_target_pairs={{0,8},{4,12},{8,0},{12,4},{16,24},{20,28},{24,16},{28,20},{1,9},{5... | collective-permute-start | bytes 20 | tf_op jit(solution)/shard_map/ppermute | solution.py:331
  215.5 14.3 %dynamic_update_slice.66 = bf16[4,2,128,12288]{3,2,1,0:T(8,128)(2,1)} pad(bf16[4,1,128,12288]{3,2,1,0:T(8,128)(2,1)} %bitcast.202, bf16[]{:T(256)} %constant.264.clone.1), padding=0_0x0_1x0_0x0_0 | pad | bytes 37748736 | tf_op jit(solution)/shard_map/dynamic_update_slice | solution.py:918
  235.0 10.7 %constant_dynamic-update-slice_fusion.8 = bf16[4,2,128,12288]{3,2,1,0:T(8,128)(2,1)} fusion(bf16[4,2,128,12288]{3,2,1,0:T(8,128)(2,1)} %dynamic_update_slice.66, bf16[4,1,128,12288]{3,2,1,0:T(8,128)(2,1)} %bitcast.203), kind=kLoop, calls=%fused_computation.174 | loop fusion | bytes 25165824 | tf_op jit(solution)/shard_map/dynamic_update_slice | solution.py:920
  245.7 6.7 add_convert_fusion.q_ref.k_ref.v_ref
  252.4 11.7 %attend.1 = (bf16[512,1024]{1,0:T(8,128)(2,1)S(1)}, f32[8,2,512]{2,1,0:T(2,128)S(1)}) custom-call(bf16[512,3072]{1,0:T(8,128)(2,1)S(1)} %add_convert_fusion.q_ref.k_ref.v_ref, bf16[512,3072]{1,0:T(8,128)(2,1)S(1)} %add_convert_fusion.q_ref.k_ref.v_ref, bf16[512,3072]{1,0:T(8,128)(2,1)S(1)} %add_convert_fusion.q_ref.k_ref.v_ref, ...), custom_call_target="tpu_custom_call" | custom-call | tf_op jit(solution)/shard_map/attend/pallas_call | solution.py:82
  264.1 3.9 fusion.92
  268.9 11.0 %ffn_up.1 = (bf16[512,4096]{1,0:T(8,128)(2,1)S(1)}, bf16[512,4096]{1,0:T(8,128)(2,1)S(1)}) custom-call(bf16[512,1024]{1,0:T(8,128)(2,1)S(1)} %fusion.22.fin_ref.refs_0_, bf16[1024,12288]{1,0:T(8,128)(2,1)} %bitcast.196, f32[1,4096]{1,0:T(1,128)S(1)} %bitcast.190), custom_call_target="tpu_custom_call" | custom-call | flops 4294967296 | tf_op jit(solution)/shard_map/ffn_up/pallas_call | solution.py:231
  282.0 9.2 %fusion.93 = (f32[512]{0:T(512)S(1)}, f32[512,1024]{1,0:T(8,128)S(1)}) fusion(f32[1024]{0:T(1024)S(1)} %bitcast.244, bf16[512,4096]{1,0:T(8,128)(2,1)S(1)} %get-tuple-element.110.refs_1_, bf16[1024,12288]{1,0:T(8,128)(2,1)} %bitcast.197, f32[1024]{0:T(1024)S(1)} %bitcast.234, f32[1024]{0:T(1024)S(1)} %bitcast.228, f32[512]{0:T(512)S(1)} %fusion.71, ...), kind=kOutput, calls=%fused_computation.276 | convolution fusion | flops 4298636800 | bytes 16795648 | tf_op jit(solution)/shard_map/dot_general | solution.py:55
  298.4 10.7 %collective-permute-start.19 = (bf16[80,1024]{1,0:T(8,128)(2,1)S(1)}, bf16[80,1024]{1,0:T(8,128)(2,1)S(1)}, u32[]{:S(2)}, u32[]{:S(2)}) collective-permute-start(bf16[80,1024]{1,0:T(8,128)(2,1)S(1)} %get-tuple-element.206), channel_id=1, source_target_pairs={{0,3},{1,0},{2,1},{3,2},{4,7},{5,4},{6,5},{7,6},{8,11},{9,8},{10,9... | collective-permute-start | bytes 491528 | tf_op jit(solution)/shard_map/ppermute | solution.py:341
  310.2 7.2 constant_dynamic-update-slice_fusion.18
  320.5 4.2 collective-permute-done.21
  325.4 7.2 constant_dynamic-update-slice_fusion.17
  332.5 9.1 %fusion.94 = (f32[320]{0:T(512)S(1)}, f32[320,7632]{1,0:T(8,128)S(1)}) fusion(bf16[320,1024]{1,0:T(8,128)(2,1)} %constant_dynamic-update-slice_fusion.4, bf16[7632,1024]{1,0:T(8,128)(2,1)} %constant_dynamic-update-slice_fusion.17, pred[7632]{0:T(1024)(128)(4,1)S(1)} %copy-done.74), kind=kOutput, calls=%fused_computation.277 | convolution fusion | flops 5006591488 | bytes 26063568 | tf_op jit(solution)/shard_map/dot_general | solution.py:55
  351.4 10.5 %fusion.79 = f32[320,1024]{1,0:T(8,128)S(1)} fusion(bf16[7632,1024]{1,0:T(8,128)(2,1)} %constant_dynamic-update-slice_fusion.17, f32[320,7632]{1,0:T(8,128)S(1)} %get-tuple-element.279, f32[320]{0:T(512)S(1)} %get-tuple-element.263, f32[320]{0:T(512)S(1)} %get-tuple-element.195, s32[7632]{0:T(1024)S(1)} %copy-done.65, s32[320]{0:T(512)} %copy-done.76), kind=kOutput, calls=%fused_computation.265 | convolution fusion | flops 5016360960 | bytes 26744384 | tf_op jit(solution)/shard_map/dot_general | solution.py:45
  368.3 17.8 %convert_bitcast_fusion = bf16[8,7632,128]{2,1,0:T(8,128)(2,1)} fusion(f32[320,7632]{1,0:T(8,128)} %copy-done.46, f32[320]{0:T(512)S(1)} %get-tuple-element.263, f32[320]{0:T(512)S(1)} %get-tuple-element.195, s32[7632]{0:T(1024)S(1)} %copy-done.65, s32[320]{0:T(512)S(1)} %copy-done.77, bf16[320,1024]{1,0:T(8,128)(2,1)} %constant_dynamic-update-slice_fusion.4), kind=kOutput, calls=%fused_computation.8 | convolution fusion | flops 5024176128 | bytes 26089024 | tf_op jit(solution)/shard_map/sv,swc->wvc/dot_general | solution.py:960
  399.5 3.4 gradient_block.13
  402.9 3.3 gradient_block.12
  406.8 9.0 %multiply_convert_fusion.refs_1_ = bf16[512,4096]{1,0:T(8,128)(2,1)S(1)} fusion(bf16[512,4096]{1,0:T(8,128)(2,1)} %copy-done.37, bf16[512,1024]{1,0:T(8,128)(2,1)S(1)} %get-tuple-element.197.refs_0_, bf16[1024,12288]{1,0:T(8,128)(2,1)} %bitcast.198), kind=kOutput, calls=%fused_computation.20 | convolution fusion | flops 4301258752 | bytes 17825792 | tf_op jit(solution)/shard_map/dot_general | solution.py:45
  415.9 4.3 gradient_block.14
  426.0 10.5 %multiply_reduce_fusion.2 = (f32[1024]{0:T(1024)S(1)}, f32[512]{0:T(512)S(1)}, f32[1024]{0:T(1024)S(1)}, f32[512,1024]{1,0:T(8,128)}) fusion(f32[512,1024]{1,0:T(8,128)S(1)} %copy-done.43, f32[512]{0:T(512)S(1)} %fusion.71, f32[512]{0:T(512)S(1)} %broadcast_multiply_fusion.2, f32[1024]{0:T(1024)S(1)} %bitcast.229, ...), kind=kOutput, calls=%fused_computation.40 | convolution fusion | flops 4300207616 | bytes 18894848 | tf_op jit(solution)/shard_map/dot_general | solution.py:55
  440.4 3.4 fusion.29.do_ref
  443.8 3.4 gradient_block.17
  447.3 16.6 %attend_back.1.refs_2_.dqkv_ref = bf16[512,3072]{1,0:T(8,128)(2,1)S(1)} custom-call(bf16[512,3072]{1,0:T(8,128)(2,1)S(1)} %copy-done.1, bf16[512,3072]{1,0:T(8,128)(2,1)S(1)} %copy-done.1, bf16[512,3072]{1,0:T(8,128)(2,1)S(1)} %copy-done.1, bf16[512,1024]{1,0:T(8,128)(2,1)S(1)} %fusion.29.do_ref, f32[8,2,512]{2,1,0:T(2,128)S(1)} %get-tuple-element.122.lse_ref, ...), custom_call_target="tpu_custom_call" | custom-call | tf_op jit(solution)/shard_map/attend_back/pallas_call | solution.py:126
  463.9 9.8 %collective-permute-done.32.refs_3_ = bf16[256,4096]{1,0:T(8,128)(2,1)} collective-permute-done((bf16[256,4096]{1,0:T(8,128)(2,1)S(1)}, bf16[256,4096]{1,0:T(8,128)(2,1)}, u32[]{:S(2)}, u32[]{:S(2)}) %collective-permute-start.32) | collective-permute-done | bytes 2097184 | tf_op jit(solution)/shard_map/ppermute | solution.py:448
  473.6 3.3 gradient_block.18
  480.7 5.2 gradient_block.21
  495.6 4.1 gradient_block.19
  501.0 8.1 embed_back.1
  510.5 37.4 %collective-permute-done.34.refs_3_ = bf16[256,4096]{1,0:T(8,128)(2,1)} collective-permute-done((bf16[256,4096]{1,0:T(8,128)(2,1)}, bf16[256,4096]{1,0:T(8,128)(2,1)}, u32[]{:S(2)}, u32[]{:S(2)}) %collective-permute-start.34) | collective-permute-done | bytes 2097184 | tf_op jit(solution)/shard_map/ppermute | solution.py:448
  547.8 6.9 concatenate.85
  570.6 5.0 gradient_block.23
  578.7 4.2 all-to-all-start.1
  590.2 13.0 %collective-permute-done.36 = bf16[528,256]{1,0:T(8,128)(2,1)S(1)} collective-permute-done((bf16[528,256]{1,0:T(8,128)(2,1)S(1)}, bf16[528,256]{1,0:T(8,128)(2,1)S(1)}, u32[]{:S(2)}, u32[]{:S(2)}) %collective-permute-start.36) | collective-permute-done | bytes 270368 | tf_op jit(solution)/shard_map/ppermute | solution.py:837
  603.2 25.1 %collective-permute-done.39.refs_5_ = bf16[256,4096]{1,0:T(8,128)(2,1)} collective-permute-done((bf16[256,4096]{1,0:T(8,128)(2,1)}, bf16[256,4096]{1,0:T(8,128)(2,1)}, u32[]{:S(2)}, u32[]{:S(2)}) %collective-permute-start.39) | collective-permute-done | bytes 2097184 | tf_op jit(solution)/shard_map/ppermute | solution.py:448
  628.4 5.2 gradient_block.22
  642.3 6.5 span.3
  650.1 6.5 span.4
  661.1 6.4 span.5
  671.4 21.2 %press.1 = (f32[1,256,12288]{2,1,0:T(8,128)}, bf16[4,256,1536]{2,1,0:T(8,128)(2,1)}, bf16[4,256,1536]{2,1,0:T(8,128)(2,1)}) custom-call(s32[1]{0:T(128)} %bitcast.4.core_ref, f32[2]{0:T(128)} %pad_maximum_fusion.5.scale_ref, f32[256,4096]{1,0:T(8,128)} %get-tuple-element.147.refs_0_, f32[256,4096]{1,0:T(8,128)} %get-tuple-element.148.refs_1_, ...), custom_call_target="tpu_custom_call" | custom-call | tf_op jit(solution)/shard_map/press/pallas_call | solution.py:741
  692.6 24.0 %collective-permute-start.43 = (bf16[4,256,1536]{2,1,0:T(8,128)(2,1)}, bf16[4,256,1536]{2,1,0:T(8,128)(2,1)S(1)}, u32[]{:S(2)}, u32[]{:S(2)}) collective-permute-start(bf16[4,256,1536]{2,1,0:T(8,128)(2,1)} %get-tuple-element.151), channel_id=1, source_target_pairs={{0,4},{4,0},{8,12},{12,8},{16,20},{20,16},{24,28},{28,24},{1,5},{5... | collective-permute-start | bytes 9437192 | tf_op jit(solution)/shard_map/ppermute | solution.py:810
  716.6 5.5 collective-permute-done.43
  722.1 3.7 fusion.44
  727.9 9.9 %collective-permute-done.45 = bf16[128,1536]{1,0:T(8,128)(2,1)S(1)} collective-permute-done((bf16[128,1536]{1,0:T(8,128)(2,1)S(1)}, bf16[128,1536]{1,0:T(8,128)(2,1)S(1)}, u32[]{:S(2)}, u32[]{:S(2)}) %collective-permute-start.45) | collective-permute-done | bytes 393248 | tf_op jit(solution)/shard_map/ppermute | solution.py:810
  741.7 3.9 collective-permute-done.44
  745.7 6.3 collective-permute-done.46
  753.8 4.6 collective-permute-done.47
  771.8 36.2 %add_rows.1.grad_ref = f32[7632,128]{1,0:T(8,128)} custom-call(s32[16384]{0:T(1024)} %fusion.57.ids_ref, bf16[4,4624,128]{2,1,0:T(8,128)(2,1)} %bitcast.204), custom_call_target="tpu_custom_call" | custom-call | tf_op jit(solution)/shard_map/add_rows/pallas_call | solution.py:639
  807.9 12.6 %update.1 = (f32[7632,128]{1,0:T(8,128)}, f32[7632,128]{1,0:T(8,128)}, f32[1,128]{1,0:T(1,128)}, f32[1,128]{1,0:T(1,128)}) custom-call(f32[7632,128]{1,0:T(8,128)} %add_rows.1.grad_ref, bf16[7632,128]{1,0:T(8,128)(2,1)} %bitcast.208, f32[7632,128]{1,0:T(8,128)} %table_ref.3, f32[7632,128]{1,0:T(8,128)} %first_ref.1, f32[7632,128]{1,0:T(8,128)} %second_ref.1), custom_call_target="tpu_custom_call" | custom-call | tf_op jit(solution)/shard_map/update/pallas_call | solution.py:786
  835.4 9.1 %convert_element_type.365 = f32[256,12288]{1,0:T(8,128)} convert(bf16[256,12288]{1,0:T(8,128)(2,1)} %all-gather.17.cloned.1.call-done) | non-fusion elementwise | flops 3145728 | bytes 18874368 | tf_op jit(solution)/shard_map/convert_element_type | solution.py:1075
  851.6 3.5 collective-permute-done.53
  855.9 3.6 collective-permute-done.54
  863.7 4.4 multiply_subtract_fusion.2
  872.6 3.5 multiply_subtract_fusion.1
  (451 shorter events, 221.1 us)
Async XLA Ops:
  7.2 60.9 %all-gather.9.cloned.1.call-start = ((), (), s32[]{:S(2)}) async-start(), calls=%async_computation.3 | async-start | bytes 8773632 | tf_op jit(solution)/shard_map/all_gather | solution.py:878
  11.8 203.6 %all-gather.13.cloned.1.call-start = ((), (), s32[]{:S(2)}) async-start(), calls=%async_computation.5 | async-start | bytes 14155776 | tf_op jit(solution)/shard_map/all_gather | solution.py:883
  12.0 1.3 collective-permute-start.6
  13.4 4.7 collective-permute-start.7
  18.1 7.0 collective-permute-start.8
  20.4 13.3 %collective-permute-start.9 = (bf16[128,1536]{1,0:T(8,128)(2,1)S(1)}, bf16[128,1536]{1,0:T(8,128)(2,1)}, u32[]{:S(2)}, u32[]{:S(2)}) collective-permute-start(bf16[128,1536]{1,0:T(8,128)(2,1)S(1)} %get-tuple-element.242), channel_id=1, source_target_pairs={{0,3},{1,0},{2,1},{3,2},{4,7},{5,4},{6,5},{7,6},{8,11},{9,8},{10,9... | collective-permute-start | bytes 1179656 | tf_op jit(solution)/shard_map/ppermute | solution.py:341
  24.1 32.6 %collective-permute-start.10 = (bf16[128,1536]{1,0:T(8,128)(2,1)S(1)}, bf16[128,1536]{1,0:T(8,128)(2,1)}, u32[]{:S(2)}, u32[]{:S(2)}) collective-permute-start(bf16[128,1536]{1,0:T(8,128)(2,1)S(1)} %get-tuple-element.242), channel_id=1, source_target_pairs={{0,2},{1,3},{2,0},{3,1},{4,6},{5,7},{6,4},{7,5},{8,10},{9,11},{10,... | collective-permute-start | bytes 1179656 | tf_op jit(solution)/shard_map/ppermute | solution.py:341
  24.1 33.6 %collective-permute-start.11 = (bf16[128,1536]{1,0:T(8,128)(2,1)S(1)}, bf16[128,1536]{1,0:T(8,128)(2,1)}, u32[]{:S(2)}, u32[]{:S(2)}) collective-permute-start(bf16[128,1536]{1,0:T(8,128)(2,1)S(1)} %get-tuple-element.242), channel_id=1, source_target_pairs={{0,1},{1,2},{2,3},{3,0},{4,5},{5,6},{6,7},{7,4},{8,9},{9,10},{10,1... | collective-permute-start | bytes 1179656 | tf_op jit(solution)/shard_map/ppermute | solution.py:341
  25.3 207.4 %copy-start.60 = (s32[4,8,672]{2,1,0:T(8,128)}, s32[4,8,672]{2,1,0:T(8,128)S(1)}, u32[]{:S(2)}) copy-start(s32[4,8,672]{2,1,0:T(8,128)S(1)} %reshape.693) | copy-start | bytes 258052
  68.1 161.7 %all-gather.11.cloned.1.call-start = ((), (), s32[]{:S(2)}) async-start(), calls=%async_computation.4 | async-start | bytes 14155776 | tf_op jit(solution)/shard_map/all_gather | solution.py:886
  68.1 59.0 %collective-permute-start.3 = (bf16[128,1536]{1,0:T(8,128)(2,1)S(1)}, bf16[128,1536]{1,0:T(8,128)(2,1)S(1)}, u32[]{:S(2)}, u32[]{:S(2)}) collective-permute-start(bf16[128,1536]{1,0:T(8,128)(2,1)S(1)} %get-tuple-element.97), channel_id=1, source_target_pairs={{0,3},{1,0},{2,1},{3,2},{4,7},{5,4},{6,5},{7,6},{8,11},{9,8},{10,9... | collective-permute-start | bytes 1179656 | tf_op jit(solution)/shard_map/ppermute | solution.py:341
  71.5 55.6 %collective-permute-start.4 = (bf16[128,1536]{1,0:T(8,128)(2,1)S(1)}, bf16[128,1536]{1,0:T(8,128)(2,1)S(1)}, u32[]{:S(2)}, u32[]{:S(2)}) collective-permute-start(bf16[128,1536]{1,0:T(8,128)(2,1)S(1)} %get-tuple-element.97), channel_id=1, source_target_pairs={{0,2},{1,3},{2,0},{3,1},{4,6},{5,7},{6,4},{7,5},{8,10},{9,11},{10,... | collective-permute-start | bytes 1179656 | tf_op jit(solution)/shard_map/ppermute | solution.py:341
  71.5 55.6 %collective-permute-start.5 = (bf16[128,1536]{1,0:T(8,128)(2,1)S(1)}, bf16[128,1536]{1,0:T(8,128)(2,1)S(1)}, u32[]{:S(2)}, u32[]{:S(2)}) collective-permute-start(bf16[128,1536]{1,0:T(8,128)(2,1)S(1)} %get-tuple-element.97), channel_id=1, source_target_pairs={{0,1},{1,2},{2,3},{3,0},{4,5},{5,6},{6,7},{7,4},{8,9},{9,10},{10,1... | collective-permute-start | bytes 1179656 | tf_op jit(solution)/shard_map/ppermute | solution.py:341
  131.2 15.4 %collective-permute-start.12 = (bf16[1792,128]{1,0:T(8,128)(2,1)S(1)}, bf16[1792,128]{1,0:T(8,128)(2,1)S(1)}, u32[]{:S(2)}, u32[]{:S(2)}) collective-permute-start(bf16[1792,128]{1,0:T(8,128)(2,1)S(1)} %get-tuple-element.238), channel_id=1, source_target_pairs={{0,1},{1,2},{2,3},{3,0},{4,5},{5,6},{6,7},{7,4},{8,9},{9,10},{10,1... | collective-permute-start | bytes 1376264 | tf_op jit(solution)/shard_map/ppermute | solution.py:373
  133.7 31.1 %collective-permute-start.13 = (bf16[1792,128]{1,0:T(8,128)(2,1)S(1)}, bf16[1792,128]{1,0:T(8,128)(2,1)S(1)}, u32[]{:S(2)}, u32[]{:S(2)}) collective-permute-start(bf16[1792,128]{1,0:T(8,128)(2,1)S(1)} %get-tuple-element.237), channel_id=1, source_target_pairs={{0,2},{1,3},{2,0},{3,1},{4,6},{5,7},{6,4},{7,5},{8,10},{9,11},{10,... | collective-permute-start | bytes 1376264 | tf_op jit(solution)/shard_map/ppermute | solution.py:373
  134.6 30.2 %collective-permute-start.14 = (bf16[1792,128]{1,0:T(8,128)(2,1)S(1)}, bf16[1792,128]{1,0:T(8,128)(2,1)S(1)}, u32[]{:S(2)}, u32[]{:S(2)}) collective-permute-start(bf16[1792,128]{1,0:T(8,128)(2,1)S(1)} %get-tuple-element.236), channel_id=1, source_target_pairs={{0,3},{1,0},{2,1},{3,2},{4,7},{5,4},{6,5},{7,6},{8,11},{9,8},{10,9... | collective-permute-start | bytes 1376264 | tf_op jit(solution)/shard_map/ppermute | solution.py:373
  174.8 34.7 %all-to-all-start = ((bf16[8,512,128]{2,1,0:T(8,128)(2,1)}), bf16[8,512,128]{2,1,0:T(8,128)(2,1)S(1)}, u32[]{:S(2)}, u32[]{:S(2)}) async-start(bf16[8,512,128]{2,1,0:T(8,128)(2,1)} %bitcast.207), calls=%async_computation | async-start | bytes 2097152 | tf_op jit(solution)/shard_map/all_to_all | solution.py:898
  178.4 147.0 %all-gather.15.cloned.1.call-start = ((), (), s32[]{:S(2)}) async-start(), calls=%async_computation.6 | async-start | bytes 8810496 | tf_op jit(solution)/shard_map/all_gather | solution.py:923
  179.0 3.9 collective-permute-start.15
  179.4 29.6 %collective-permute-start.18 = (s32[1,592]{1,0:T(1,128)S(1)}, s32[1,592]{1,0:T(1,128)S(1)}, u32[]{:S(2)}, u32[]{:S(2)}) collective-permute-start(s32[1,592]{1,0:T(1,128)S(1)} %pad_add_fusion.3), channel_id=1, source_target_pairs={{0,0},{1,4},{2,1},{3,5},{4,2},{5,6},{6,3},{7,7},{8,8},{9,12},{10,9... | collective-permute-start | bytes 7112 | tf_op jit(solution)/shard_map/ppermute | solution.py:494
  184.2 19.8 %collective-permute-start.16 = (f32[]{:T(128)}, f32[]{:T(128)}, u32[]{:S(2)}, u32[]{:S(2)}) collective-permute-start(f32[]{:T(128)} %add.654), channel_id=1, source_target_pairs={{0,8},{4,12},{8,0},{12,4},{16,24},{20,28},{24,16},{28,20},{1,9},{5... | collective-permute-start | bytes 20 | tf_op jit(solution)/shard_map/ppermute | solution.py:331
  204.6 3.7 collective-permute-start.17
  229.8 431.2 %reduce-scatter.2.cloned.1.call-start = ((), (), s32[]{:S(2)}) async-start(), calls=%async_computation.7 | async-start | bytes 17584128 | tf_op jit(solution)/shard_map/reduce_scatter | solution.py:962
  268.9 174.9 %copy-start.10 = (bf16[512,1024]{1,0:T(8,128)(2,1)}, bf16[512,1024]{1,0:T(8,128)(2,1)S(1)}, u32[]{:S(2)}) copy-start(bf16[512,1024]{1,0:T(8,128)(2,1)S(1)} %fusion.22.fin_ref.refs_0_) | copy-start | bytes 3145732
  298.4 19.2 %collective-permute-start.19 = (bf16[80,1024]{1,0:T(8,128)(2,1)S(1)}, bf16[80,1024]{1,0:T(8,128)(2,1)S(1)}, u32[]{:S(2)}, u32[]{:S(2)}) collective-permute-start(bf16[80,1024]{1,0:T(8,128)(2,1)S(1)} %get-tuple-element.206), channel_id=1, source_target_pairs={{0,3},{1,0},{2,1},{3,2},{4,7},{5,4},{6,5},{7,6},{8,11},{9,8},{10,9... | collective-permute-start | bytes 491528 | tf_op jit(solution)/shard_map/ppermute | solution.py:341
  309.1 10.7 %collective-permute-start.20 = (bf16[80,1024]{1,0:T(8,128)(2,1)S(1)}, bf16[80,1024]{1,0:T(8,128)(2,1)S(1)}, u32[]{:S(2)}, u32[]{:S(2)}) collective-permute-start(bf16[80,1024]{1,0:T(8,128)(2,1)S(1)} %get-tuple-element.206), channel_id=1, source_target_pairs={{0,2},{1,3},{2,0},{3,1},{4,6},{5,7},{6,4},{7,5},{8,10},{9,11},{10,... | collective-permute-start | bytes 491528 | tf_op jit(solution)/shard_map/ppermute | solution.py:341
  317.3 7.3 collective-permute-start.21
  344.4 3.7 collective-permute-start.22
  345.3 4.5 collective-permute-start.23
  345.3 5.4 collective-permute-start.24
  363.8 22.3 %collective-permute-start.25 = (bf16[80,1024]{1,0:T(8,128)(2,1)}, bf16[80,1024]{1,0:T(8,128)(2,1)}, u32[]{:S(2)}, u32[]{:S(2)}) collective-permute-start(bf16[80,1024]{1,0:T(8,128)(2,1)} %get-tuple-element.239), channel_id=1, source_target_pairs={{0,1},{1,2},{2,3},{3,0},{4,5},{5,6},{6,7},{7,4},{8,9},{9,10},{10,1... | collective-permute-start | bytes 491528 | tf_op jit(solution)/shard_map/ppermute | solution.py:360
  364.1 22.0 %collective-permute-start.26 = (bf16[80,1024]{1,0:T(8,128)(2,1)}, bf16[80,1024]{1,0:T(8,128)(2,1)}, u32[]{:S(2)}, u32[]{:S(2)}) collective-permute-start(bf16[80,1024]{1,0:T(8,128)(2,1)} %get-tuple-element.241), channel_id=1, source_target_pairs={{0,2},{1,3},{2,0},{3,1},{4,6},{5,7},{6,4},{7,5},{8,10},{9,11},{10,... | collective-permute-start | bytes 491528 | tf_op jit(solution)/shard_map/ppermute | solution.py:360
  366.1 20.0 %collective-permute-start.27 = (bf16[80,1024]{1,0:T(8,128)(2,1)}, bf16[80,1024]{1,0:T(8,128)(2,1)}, u32[]{:S(2)}, u32[]{:S(2)}) collective-permute-start(bf16[80,1024]{1,0:T(8,128)(2,1)} %get-tuple-element.240), channel_id=1, source_target_pairs={{0,3},{1,0},{2,1},{3,2},{4,7},{5,4},{6,5},{7,6},{8,11},{9,8},{10,9... | collective-permute-start | bytes 491528 | tf_op jit(solution)/shard_map/ppermute | solution.py:360
  402.9 12.9 %collective-permute-start.29 = (bf16[256,4096]{1,0:T(8,128)(2,1)}, bf16[256,4096]{1,0:T(8,128)(2,1)}, u32[]{:S(2)}, u32[]{:S(2)}) collective-permute-start(bf16[256,4096]{1,0:T(8,128)(2,1)} %gradient_block.13), channel_id=1, source_target_pairs={{0,4},{4,0},{8,12},{12,8},{16,20},{20,16},{24,28},{28,24},{1,5},{5... | collective-permute-start | bytes 6291464 | tf_op jit(solution)/shard_map/ppermute | solution.py:433
  406.3 9.6 %collective-permute-start.28 = (bf16[256,4096]{1,0:T(8,128)(2,1)}, bf16[256,4096]{1,0:T(8,128)(2,1)}, u32[]{:S(2)}, u32[]{:S(2)}) collective-permute-start(bf16[256,4096]{1,0:T(8,128)(2,1)} %gradient_block.12), channel_id=1, source_target_pairs={{0,4},{4,0},{8,12},{12,8},{16,20},{20,16},{24,28},{28,24},{1,5},{5... | collective-permute-start | bytes 6291464 | tf_op jit(solution)/shard_map/ppermute | solution.py:432
  425.1 18.7 %collective-permute-start.31 = (bf16[256,4096]{1,0:T(8,128)(2,1)S(1)}, bf16[256,4096]{1,0:T(8,128)(2,1)S(1)}, u32[]{:S(2)}, u32[]{:S(2)}) collective-permute-start(bf16[256,4096]{1,0:T(8,128)(2,1)S(1)} %gradient_block.16), channel_id=1, source_target_pairs={{0,4},{4,0},{8,12},{12,8},{16,20},{20,16},{24,28},{28,24},{1,5},{5... | collective-permute-start | bytes 6291464 | tf_op jit(solution)/shard_map/ppermute | solution.py:433
  425.5 18.3 %collective-permute-start.30 = (bf16[256,4096]{1,0:T(8,128)(2,1)S(1)}, bf16[256,4096]{1,0:T(8,128)(2,1)S(1)}, u32[]{:S(2)}, u32[]{:S(2)}) collective-permute-start(bf16[256,4096]{1,0:T(8,128)(2,1)S(1)} %gradient_block.15), channel_id=1, source_target_pairs={{0,4},{4,0},{8,12},{12,8},{16,20},{20,16},{24,28},{28,24},{1,5},{5... | collective-permute-start | bytes 6291464 | tf_op jit(solution)/shard_map/ppermute | solution.py:432
  425.7 48.0 %collective-permute-start.32 = (bf16[256,4096]{1,0:T(8,128)(2,1)S(1)}, bf16[256,4096]{1,0:T(8,128)(2,1)}, u32[]{:S(2)}, u32[]{:S(2)}) collective-permute-start(bf16[256,4096]{1,0:T(8,128)(2,1)S(1)} %gradient_block.14), channel_id=1, source_target_pairs={{0,1},{1,0},{2,3},{3,2},{4,5},{5,4},{6,7},{7,6},{8,9},{9,8},{10,11... | collective-permute-start | bytes 6291464 | tf_op jit(solution)/shard_map/ppermute | solution.py:448
  477.0 14.9 %collective-permute-start.33 = (bf16[256,4096]{1,0:T(8,128)(2,1)}, bf16[256,4096]{1,0:T(8,128)(2,1)}, u32[]{:S(2)}, u32[]{:S(2)}) collective-permute-start(bf16[256,4096]{1,0:T(8,128)(2,1)} %gradient_block.18), channel_id=1, source_target_pairs={{0,4},{4,0},{8,12},{12,8},{16,20},{20,16},{24,28},{28,24},{1,5},{5... | collective-permute-start | bytes 6291464 | tf_op jit(solution)/shard_map/ppermute | solution.py:432
  477.0 70.8 %collective-permute-start.34 = (bf16[256,4096]{1,0:T(8,128)(2,1)}, bf16[256,4096]{1,0:T(8,128)(2,1)}, u32[]{:S(2)}, u32[]{:S(2)}) collective-permute-start(bf16[256,4096]{1,0:T(8,128)(2,1)} %gradient_block.17), channel_id=1, source_target_pairs={{0,1},{1,0},{2,3},{3,2},{4,5},{5,4},{6,7},{7,6},{8,9},{9,8},{10,11... | collective-permute-start | bytes 6291464 | tf_op jit(solution)/shard_map/ppermute | solution.py:448
  485.9 101.1 %collective-permute-start.40 = (bf16[256,4096]{1,0:T(8,128)(2,1)}, bf16[256,4096]{1,0:T(8,128)(2,1)}, u32[]{:S(2)}, u32[]{:S(2)}) collective-permute-start(bf16[256,4096]{1,0:T(8,128)(2,1)} %gradient_block.21), channel_id=1, source_target_pairs={{2,4},{3,5},{4,2},{5,3},{10,12},{11,13},{12,10},{13,11},{18,20},{1... | collective-permute-start | bytes 6291464 | tf_op jit(solution)/shard_map/ppermute | solution.py:472
  556.9 26.6 %collective-permute-start.35 = (bf16[528,512]{1,0:T(8,128)(2,1)}, bf16[528,512]{1,0:T(8,128)(2,1)}, u32[]{:S(2)}, u32[]{:S(2)}) collective-permute-start(bf16[528,512]{1,0:T(8,128)(2,1)} %dynamic-slice_convert_fusion), channel_id=1, source_target_pairs={{0,16},{4,20},{8,24},{12,28},{16,0},{20,4},{24,8},{28,12},{1,17},{... | collective-permute-start | bytes 1622024 | tf_op jit(solution)/shard_map/ppermute | solution.py:837
  558.6 69.8 %collective-permute-start.39 = (bf16[256,4096]{1,0:T(8,128)(2,1)}, bf16[256,4096]{1,0:T(8,128)(2,1)}, u32[]{:S(2)}, u32[]{:S(2)}) collective-permute-start(bf16[256,4096]{1,0:T(8,128)(2,1)} %copy-done.35), channel_id=1, source_target_pairs={{0,1},{1,0},{2,3},{3,2},{4,5},{5,4},{6,7},{7,6},{8,9},{9,8},{10,11... | collective-permute-start | bytes 6291464 | tf_op jit(solution)/shard_map/ppermute | solution.py:448
  565.6 62.8 %collective-permute-start.38 = (bf16[256,4096]{1,0:T(8,128)(2,1)}, bf16[256,4096]{1,0:T(8,128)(2,1)}, u32[]{:S(2)}, u32[]{:S(2)}) collective-permute-start(bf16[256,4096]{1,0:T(8,128)(2,1)} %gradient_block.20), channel_id=1, source_target_pairs={{0,4},{4,0},{8,12},{12,8},{16,20},{20,16},{24,28},{28,24},{1,5},{5... | collective-permute-start | bytes 6291464 | tf_op jit(solution)/shard_map/ppermute | solution.py:433
  575.6 63.6 %collective-permute-start.42 = (bf16[256,4096]{1,0:T(8,128)(2,1)}, bf16[256,4096]{1,0:T(8,128)(2,1)}, u32[]{:S(2)}, u32[]{:S(2)}) collective-permute-start(bf16[256,4096]{1,0:T(8,128)(2,1)} %gradient_block.23), channel_id=1, source_target_pairs={{2,4},{3,5},{4,2},{5,3},{10,12},{11,13},{12,10},{13,11},{18,20},{1... | collective-permute-start | bytes 6291464 | tf_op jit(solution)/shard_map/ppermute | solution.py:472
  578.7 58.1 %all-to-all-start.1 = ((bf16[8,512,128]{2,1,0:T(8,128)(2,1)}), bf16[8,512,128]{2,1,0:T(8,128)(2,1)}, u32[]{:S(2)}, u32[]{:S(2)}) async-start(bf16[8,512,128]{2,1,0:T(8,128)(2,1)} %bitcast_bitcast_fusion), calls=%async_computation.1 | async-start | bytes 2097152 | tf_op jit(solution)/shard_map/all_to_all | solution.py:978
  583.0 188.8 %all-gather.21.cloned.1.call-start = ((), (), s32[]{:S(2)}) async-start(), calls=%async_computation.10 | async-start | bytes 5918720 | tf_op jit(solution)/shard_map/all_gather | solution.py:988
  585.1 18.0 %collective-permute-start.36 = (bf16[528,256]{1,0:T(8,128)(2,1)S(1)}, bf16[528,256]{1,0:T(8,128)(2,1)S(1)}, u32[]{:S(2)}, u32[]{:S(2)}) collective-permute-start(bf16[528,256]{1,0:T(8,128)(2,1)S(1)} %dynamic-slice_convert_fusion.1), channel_id=1, source_target_pairs={{0,8},{4,12},{8,0},{12,4},{16,24},{20,28},{24,16},{28,20},{1,9},{5... | collective-permute-start | bytes 811016 | tf_op jit(solution)/shard_map/ppermute | solution.py:837
  633.5 24.3 %collective-permute-start.41 = (bf16[256,4096]{1,0:T(8,128)(2,1)}, bf16[256,4096]{1,0:T(8,128)(2,1)S(1)}, u32[]{:S(2)}, u32[]{:S(2)}) collective-permute-start(bf16[256,4096]{1,0:T(8,128)(2,1)} %gradient_block.22), channel_id=1, source_target_pairs={{2,4},{3,5},{4,2},{5,3},{10,12},{11,13},{12,10},{13,11},{18,20},{1... | collective-permute-start | bytes 6291464 | tf_op jit(solution)/shard_map/ppermute | solution.py:472
  634.4 1.5 collective-permute-start.37
  661.0 163.8 %all-gather.17.cloned.1.call-start = ((), (), s32[]{:S(2)}) async-start(), calls=%async_computation.8 | async-start | bytes 7077888 | tf_op jit(solution)/shard_map/all_gather | solution.py:1039
  692.6 29.5 %collective-permute-start.43 = (bf16[4,256,1536]{2,1,0:T(8,128)(2,1)}, bf16[4,256,1536]{2,1,0:T(8,128)(2,1)S(1)}, u32[]{:S(2)}, u32[]{:S(2)}) collective-permute-start(bf16[4,256,1536]{2,1,0:T(8,128)(2,1)} %get-tuple-element.151), channel_id=1, source_target_pairs={{0,4},{4,0},{8,12},{12,8},{16,20},{20,16},{24,28},{28,24},{1,5},{5... | collective-permute-start | bytes 9437192 | tf_op jit(solution)/shard_map/ppermute | solution.py:810
  725.8 12.0 %collective-permute-start.45 = (bf16[128,1536]{1,0:T(8,128)(2,1)S(1)}, bf16[128,1536]{1,0:T(8,128)(2,1)S(1)}, u32[]{:S(2)}, u32[]{:S(2)}) collective-permute-start(bf16[128,1536]{1,0:T(8,128)(2,1)S(1)} %get-tuple-element.222), channel_id=1, source_target_pairs={{0,8},{4,12},{8,0},{12,4},{16,24},{20,28},{24,16},{28,20},{1,9},{5... | collective-permute-start | bytes 1179656 | tf_op jit(solution)/shard_map/ppermute | solution.py:810
  725.8 19.8 %collective-permute-start.44 = (bf16[128,1536]{1,0:T(8,128)(2,1)}, bf16[128,1536]{1,0:T(8,128)(2,1)S(1)}, u32[]{:S(2)}, u32[]{:S(2)}) collective-permute-start(bf16[128,1536]{1,0:T(8,128)(2,1)} %get-tuple-element.219), channel_id=1, source_target_pairs={{0,8},{4,12},{8,0},{12,4},{16,24},{20,28},{24,16},{28,20},{1,9},{5... | collective-permute-start | bytes 1179656 | tf_op jit(solution)/shard_map/ppermute | solution.py:810
  727.9 17.8 %collective-permute-start.48 = (bf16[128,1536]{1,0:T(8,128)(2,1)}, bf16[128,1536]{1,0:T(8,128)(2,1)}, u32[]{:S(2)}, u32[]{:S(2)}) collective-permute-start(bf16[128,1536]{1,0:T(8,128)(2,1)} %get-tuple-element.220), channel_id=1, source_target_pairs={{0,16},{4,20},{8,24},{12,28},{16,0},{20,4},{24,8},{28,12},{1,17},{... | collective-permute-start | bytes 1179656 | tf_op jit(solution)/shard_map/ppermute | solution.py:810
  739.7 12.3 %collective-permute-start.46 = (bf16[128,1536]{1,0:T(8,128)(2,1)}, bf16[128,1536]{1,0:T(8,128)(2,1)S(1)}, u32[]{:S(2)}, u32[]{:S(2)}) collective-permute-start(bf16[128,1536]{1,0:T(8,128)(2,1)} %fusion.40), channel_id=1, source_target_pairs={{0,16},{4,20},{8,24},{12,28},{16,0},{20,4},{24,8},{28,12},{1,17},{... | collective-permute-start | bytes 1179656 | tf_op jit(solution)/shard_map/ppermute | solution.py:810
  739.7 18.7 %collective-permute-start.47 = (bf16[128,1536]{1,0:T(8,128)(2,1)}, bf16[128,1536]{1,0:T(8,128)(2,1)S(1)}, u32[]{:S(2)}, u32[]{:S(2)}) collective-permute-start(bf16[128,1536]{1,0:T(8,128)(2,1)} %get-tuple-element.221), channel_id=1, source_target_pairs={{0,16},{4,20},{8,24},{12,28},{16,0},{20,4},{24,8},{28,12},{1,17},{... | collective-permute-start | bytes 1179656 | tf_op jit(solution)/shard_map/ppermute | solution.py:810
  753.8 7.8 collective-permute-start.49
  768.2 91.3 %all-gather.19.cloned.1.call-start = ((), (), s32[]{:S(2)}) async-start(), calls=%async_computation.9 | async-start | bytes 1216512 | tf_op jit(solution)/shard_map/all_gather | solution.py:1042
  835.4 9.1 %collective-permute-start.50 = (f32[12]{0:T(128)S(1)}, f32[12]{0:T(128)S(1)}, u32[]{:S(2)}, u32[]{:S(2)}) collective-permute-start(f32[12]{0:T(128)S(1)} %concatenate.88), channel_id=1, source_target_pairs={{0,4},{4,0},{8,12},{12,8},{16,20},{20,16},{24,28},{28,24},{1,5},{5... | collective-permute-start | bytes 152 | tf_op jit(solution)/shard_map/ppermute | solution.py:331
  844.5 3.5 collective-permute-start.51
  848.0 3.5 collective-permute-start.52
  851.6 3.5 collective-permute-start.53
  855.1 4.4 collective-permute-start.54
  (82 other events, 875.8 us)
Sparse Core Ops, SparseCore 0:
  12.0 56.0 all-gather.8
  70.5 72.1 all-gather.12
  145.2 83.3 all-gather.10
  230.9 60.4 all-gather.14
  388.3 110.9 reduce-scatter.1
  661.1 110.5 all-gather.20
  774.4 43.9 all-gather.16
  825.0 22.1 all-gather.18

commit v13 on v11

--- a/solution.py
+++ b/solution.py
@@ -615,17 +615,21 @@
 
 
 def add_kernel(ids_ref, values_ref, out_ref, rows, *sums):
-    size, length = out_ref.shape[0], rows.shape[1]
+    size = out_ref.shape[0]
+    places, length = rows.shape[0:2]
+    split = len(sums) // places
+    each = length // split
     for part in sums:
         part[...] = jnp.zeros_like(part)
     rows[...] = values_ref[:, 0:length, :].astype(jnp.float32)
 
-    @pl.loop(0, length, step=8)
+    @pl.loop(0, each, step=8)
     def _(first):
         for by in range(8):
             for index, part in enumerate(sums):
-                place = ids_ref[index * length + first + by]
-                part[pl.ds(place, 1), :] += rows[index, pl.ds(first + by, 1), :]
+                at = index % split * each + first + by
+                place = ids_ref[index // split * length + at]
+                part[pl.ds(place, 1), :] += rows[index // split, pl.ds(at, 1), :]
 
     total = sums[0][0:size, :]
     for part in sums[1:]:
@@ -644,10 +648,10 @@
             in_specs=[pl.BlockSpec(values.shape, lambda step, ids: (0, 0, 0))],
             out_specs=pl.BlockSpec((size, cols), lambda step, ids: (0, 0)),
             scratch_shapes=[pltpu.VMEM((places, length, cols), jnp.float32)]
-            + [pltpu.VMEM((size + 8, cols), jnp.float32)] * places,
+            + [pltpu.VMEM((size + 8, cols), jnp.float32)] * (2 * places),
         ),
         out_shape=jax.ShapeDtypeStruct((size, cols), jnp.float32),
-        compiler_params=pltpu.CompilerParams(vmem_limit_bytes=56 * 2**20),
+        compiler_params=pltpu.CompilerParams(vmem_limit_bytes=62 * 2**20),
         cost_estimate=FREE,
         name="add_rows",
     )(ids.reshape(-1), values)
@@ -873,9 +877,12 @@
         token_ids, mlm_labels, mlm_valid, doc_ids, mlm_pos = hosted_rows(
             token_ids, mlm_labels, mlm_valid, doc_ids, mlm_pos
         )
+        table_cut = vshard * 5 // 8 // 16 * 16
+        table_first = lax.all_gather(table_low[0:table_cut], "wide", axis=1, tiled=True)
         owners = Owners(token_ids.reshape(n_narrow, n_wide * L), vshard)
         picked = packed_rows(owners.slots, table)
         layer_rows, picked = gathered_near(layer_low, picked)
+        layer_rows, table_first = together(layer_rows, table_first)
     else:
         layer_rows = lax.all_gather(layer_low, "narrow", axis=0, tiled=True)
     weights = lax.all_gather(layer_rows, "wide", axis=1, tiled=True)
@@ -906,8 +913,13 @@
     x0 = norm_rows(embedded, small[L + 2], small[L + 3])
     act = x0.astype(jnp.bfloat16)
     if paired:
-        table_low, weights, act = together(table_low, weights, act)
-        table_cols = lax.all_gather(table_low, "wide", axis=1, tiled=True)
+        table_cols = jnp.zeros((vshard, D), jnp.bfloat16)
+        table_cols = lax.dynamic_update_slice(table_cols, table_first, (0, 0))
+        table_last, weights, act, table_cols = together(
+            table_low[table_cut:], weights, act, table_cols
+        )
+        table_last = lax.all_gather(table_last, "wide", axis=1, tiled=True)
+        table_cols = lax.dynamic_update_slice(table_cols, table_last, (table_cut, 0))
     htwo, kept = layer_forward(embedded, x0, act, doc_ids, small, weights)
     hmask = jnp.take_along_axis(htwo.reshape(seqs, L, D), mlm_pos[..., None], axis=1)
     hmask = hmask.reshape(seqs * MPS, D).astype(jnp.bfloat16)
@@ -999,8 +1011,21 @@
     server_out = sscale * jnp.tanh(server_in / sscale)
     new_server = server_in - server_out
     server_low = server_out.astype(jnp.bfloat16)
+    layer_upd = server_out / (jnp.sqrt(layer_v) + OPT_EPS) + DECAY * layer
+    column = wide_me * part_cols + jnp.arange(part_cols)
+    which = (
+        (column >= 3 * D).astype(jnp.int32)
+        + (column >= 4 * D).astype(jnp.int32)
+        + (column >= 4 * D + FF).astype(jnp.int32)
+    )
+    onehot = (which[:, None] == jnp.arange(4)[None]).astype(jnp.float32)
+    wsq = jnp.sum(jnp.sum(layer * layer, axis=0)[:, None] * onehot, axis=0)
+    usq = jnp.sum(jnp.sum(layer_upd * layer_upd, axis=0)[:, None] * onehot, axis=0)
+    small_square = jnp.sum(small * small)[None]
     if paired:
-        server_out, group_rows = together(server_out, group_rows)
+        new_server, wsq, usq, small_square, group_rows = together(
+            new_server, wsq, usq, small_square, group_rows
+        )
         table_grad = added_rows(owners.slots, group_rows, vshard)
         table_mom, table_upd, table_norms = table_update(
             table_grad, table_head, table, table_m, table_v
@@ -1026,23 +1051,13 @@
     if not paired:
         _, small_upd = small_update(small_grad, small_m, small_v, small)
         small_norm = jnp.where((wide_me == 0) & (narrow_me == 0), jnp.sum(small_upd * small_upd), 0.0)
-    layer_upd = server_out / (jnp.sqrt(layer_v) + OPT_EPS) + DECAY * layer
-    column = wide_me * part_cols + jnp.arange(part_cols)
-    which = (
-        (column >= 3 * D).astype(jnp.int32)
-        + (column >= 4 * D).astype(jnp.int32)
-        + (column >= 4 * D + FF).astype(jnp.int32)
-    )
-    onehot = (which[:, None] == jnp.arange(4)[None]).astype(jnp.float32)
-    wsq = jnp.sum(jnp.sum(layer * layer, axis=0)[:, None] * onehot, axis=0)
-    usq = jnp.sum(jnp.sum(layer_upd * layer_upd, axis=0)[:, None] * onehot, axis=0)
     parts = jnp.concatenate([wsq, usq, *table_norms, jnp.sum(own_loss)[None], small_norm[None]])
     sums = summed_over(summed_over(parts, "wide"), "narrow")
     if paired:
         sums, small_grad = together(sums, small_grad)
     small_mom, small_upd = small_update(small_grad, small_m, small_v, small)
     loss_sum = sums[10]
-    wnorm = jnp.sqrt(jnp.concatenate([sums[0:4], sums[8:9], jnp.sum(small * small)[None]]))
+    wnorm = jnp.sqrt(jnp.concatenate([sums[0:4], sums[8:9], small_square]))
     unorm = jnp.sqrt(jnp.concatenate([sums[4:8], sums[9:10], sums[11:12]]))
     ratio = wnorm / unorm
     new_layer = layer - RATE * jnp.sum(onehot * ratio[None, 0:4], axis=1)[None] * layer_upd

time: 884 us -> 865 us (0.979)
  waiting for transfers between devices: 243 us -> 212 us
  local copies, waits for them, and re-layouts: 65.4 us -> 86.3 us
  Pallas kernels: 240 us -> 230 us
    all_gather x1 -> x2, waiting for transfers between devices: 18.7 us -> 0.02 us  [the longest x1 0.02 us: shards(): lax.all_gather(table_low[0:table_cut], 'wide', axis=1, tiled=True)]
    dynamic_update_slice x0 -> x2, local copies, waits for them, and re-layouts: none -> 15.6 us  [the longest x1 9.82 us: shards(): table_cols = lax.dynamic_update_slice(table_cols, table_first, (0, 0))]
    pallas_call x1, Pallas kernels: 36.1 us -> 25 us  [added_rows(): pl.pallas_call(add_kernel, grid_spec=pltpu.PrefetchScalarGridSpec(num_sca...]
    all_gather x1, waiting for transfers between devices: 40.7 us -> 30.8 us  [shards(): weights = lax.all_gather(layer_rows, 'wide', axis=1, tiled=True)]
    unnamed x160 -> x168, local copies, waits for them, and re-layouts: 37.9 us -> 40.1 us
  transfers between devices with their start and end apart: 57 -> 58, of which waited for: 28 -> 28; matrix products, arithmetic and copies ran while one was open for 19% -> 20% of each run, Pallas kernels for 27% -> 27%
where the time goes in v13:
time: 865 us; the launch traced here: 857 us
  Pallas kernels  230 us (27%)
  waiting for transfers between devices  212 us (25%)
  starting transfers between devices  120 us (14%)
  other arithmetic  102 us (12%)
  local copies, waits for them, and re-layouts  86.3 us (10%)
  matrix products  79.7 us (9%)
  between operations  23.3 us (3%)
    ppermute x3, waiting for transfers between devices, across(): self.away = lax.ppermute(away, 'narrow', sides)  67.6 us
    pallas_call x1, Pallas kernels, packed_rows(): pl.pallas_call(pack_kernel, grid_spec=pltpu.PrefetchScalarGridSpec(num_sc...  52.4 us
    pallas_call x12, Pallas kernels, gradient_block(): pl.pallas_call(functools.partial(block_kernel, steps), grid_spec=pltpu.Pr...  45.3 us
    unnamed x168, local copies, waits for them, and re-layouts  40.1 us
    ppermute x3, waiting for transfers between devices, sent_around(): lax.ppermute(block(by), 'narrow', cycle(size, by))  38.9 us
    dot_general x4, matrix products, matmul_nt(): lax.dot_general(left, right, (((1,), (1,)), ((), ())), preferred_element_...  32.9 us
    ppermute x7, starting transfers between devices, send(): lax.ppermute(value.astype(jnp.bfloat16), 'wide', swap_pairs(n_wide, bit))  32.6 us
    ppermute x7, waiting for transfers between devices, send(): lax.ppermute(value.astype(jnp.bfloat16), 'wide', swap_pairs(n_wide, bit))  31.1 us
  transfers between devices with their start and end apart: 58, of which 28 were waited for; matrix products, arithmetic and copies ran while one was open for 20% of the time, Pallas kernels for 27%

profile of v13, /device:TPU:0, one launch (start us, length us, event | category | flops | bytes accessed | tf_op | source)
XLA Modules:
  0.0 856.6 jit_solution(198958966527229693)
XLA Ops:
  28.5 52.4 %pack_rows.1 = bf16[4,4096,128]{2,1,0:T(8,128)(2,1)} custom-call(s32[16384]{0:T(1024)S(1)} %fusion.59.ids_ref, f32[7632,128]{1,0:T(8,128)S(1)} %copy-done.8), custom_call_target="tpu_custom_call" | custom-call | tf_op jit(solution)/shard_map/pack_rows/pallas_call | solution.py:568
  89.1 10.9 %collective-permute-start.11 = (bf16[1792,128]{1,0:T(8,128)(2,1)S(1)}, bf16[1792,128]{1,0:T(8,128)(2,1)S(1)}, u32[]{:S(2)}, u32[]{:S(2)}) collective-permute-start(bf16[1792,128]{1,0:T(8,128)(2,1)S(1)} %get-tuple-element.238), channel_id=1, source_target_pairs={{0,3},{1,0},{2,1},{3,2},{4,7},{5,4},{6,5},{7,6},{8,11},{9,8},{10,9... | collective-permute-start | bytes 1376264 | tf_op jit(solution)/shard_map/ppermute | solution.py:373
  100.7 10.3 %collective-permute-done.11 = bf16[1792,128]{1,0:T(8,128)(2,1)S(1)} collective-permute-done((bf16[1792,128]{1,0:T(8,128)(2,1)S(1)}, bf16[1792,128]{1,0:T(8,128)(2,1)S(1)}, u32[]{:S(2)}, u32[]{:S(2)}) %collective-permute-start.11) | collective-permute-done | bytes 458784 | tf_op jit(solution)/shard_map/ppermute | solution.py:373
  111.0 28.5 %collective-permute-done.10 = bf16[1792,128]{1,0:T(8,128)(2,1)S(1)} collective-permute-done((bf16[1792,128]{1,0:T(8,128)(2,1)S(1)}, bf16[1792,128]{1,0:T(8,128)(2,1)S(1)}, u32[]{:S(2)}, u32[]{:S(2)}) %collective-permute-start.10) | collective-permute-done | bytes 458784 | tf_op jit(solution)/shard_map/ppermute | solution.py:373
  139.7 5.5 take_rows.3
  145.2 3.5 conditional.1
  149.7 3.6 all-to-all-start
  158.8 18.1 %collective-permute-start.13 = (f32[]{:T(128)}, f32[]{:T(128)}, u32[]{:S(2)}, u32[]{:S(2)}) collective-permute-start(f32[]{:T(128)} %add.643), channel_id=1, source_target_pairs={{0,8},{4,12},{8,0},{12,4},{16,24},{20,28},{24,16},{28,20},{1,9},{5... | collective-permute-start | bytes 20 | tf_op jit(solution)/shard_map/ppermute | solution.py:331
  184.1 9.8 %dynamic_update_slice.46 = bf16[7632,1024]{1,0:T(8,128)(2,1)} pad(bf16[4768,1024]{1,0:T(8,128)(2,1)} %all-gather.8.cloned.1.call-done, bf16[]{:T(256)} %constant.258.clone.1), padding=0_2864x0_0 | pad | bytes 25395202 | tf_op jit(solution)/shard_map/dynamic_update_slice | solution.py:917
  199.9 30.8 %all-gather.10.cloned.1.call-done.weight_ref = bf16[1024,12288]{1,0:T(8,128)(2,1)} async-done(((bf16[1024,1536]{1,0:T(8,128)(2,1)}), bf16[1024,12288]{1,0:T(8,128)(2,1)}) %all-gather.10.cloned.1.call-update) | async-done | bytes 25165840 | tf_op jit(solution)/shard_map/all_gather | solution.py:888
  232.5 6.4 add_convert_fusion.q_ref.k_ref.v_ref
  239.0 11.7 %attend.1 = (bf16[512,1024]{1,0:T(8,128)(2,1)S(1)}, f32[8,2,512]{2,1,0:T(2,128)S(1)}) custom-call(bf16[512,3072]{1,0:T(8,128)(2,1)S(1)} %add_convert_fusion.q_ref.k_ref.v_ref, bf16[512,3072]{1,0:T(8,128)(2,1)S(1)} %add_convert_fusion.q_ref.k_ref.v_ref, bf16[512,3072]{1,0:T(8,128)(2,1)S(1)} %add_convert_fusion.q_ref.k_ref.v_ref, ...), custom_call_target="tpu_custom_call" | custom-call | tf_op jit(solution)/shard_map/attend/pallas_call | solution.py:82
  250.7 3.4 fusion.93
  254.9 11.3 %ffn_up.1 = (bf16[512,4096]{1,0:T(8,128)(2,1)S(1)}, bf16[512,4096]{1,0:T(8,128)(2,1)S(1)}) custom-call(bf16[512,1024]{1,0:T(8,128)(2,1)S(1)} %fusion.22.fin_ref.refs_0_, bf16[1024,12288]{1,0:T(8,128)(2,1)} %all-gather.10.cloned.1.call-done.weight_ref, f32[1,4096]{1,0:T(1,128)S(1)} %bitcast.181), custom_call_target="tpu_custom_call" | custom-call | flops 4294967296 | tf_op jit(solution)/shard_map/ffn_up/pallas_call | solution.py:231
  268.2 9.2 %fusion.94 = (f32[512]{0:T(512)S(1)}, f32[512,1024]{1,0:T(8,128)S(1)}) fusion(f32[1024]{0:T(1024)S(1)} %bitcast.223, bf16[512,4096]{1,0:T(8,128)(2,1)S(1)} %get-tuple-element.111.refs_1_, bf16[1024,12288]{1,0:T(8,128)(2,1)} %all-gather.10.cloned.1.call-done.weight_ref, f32[1024]{0:T(1024)S(1)} %bitcast.213, f32[1024]{0:T(1024)S(1)} %bitcast.207, ...), kind=kOutput, calls=%fused_computation.268 | convolution fusion | flops 4298636800 | bytes 16795648 | tf_op jit(solution)/shard_map/dot_general | solution.py:55
  289.5 6.1 collective-permute-done.16
  300.8 5.8 constant_dynamic-update-slice_fusion.4
  306.6 9.1 %fusion.95 = (f32[320]{0:T(512)S(1)}, f32[320,7632]{1,0:T(8,128)S(1)}) fusion(bf16[320,1024]{1,0:T(8,128)(2,1)} %constant_dynamic-update-slice_fusion.5, bf16[7632,1024]{1,0:T(8,128)(2,1)} %constant_dynamic-update-slice_fusion.4, pred[7632]{0:T(1024)(128)(4,1)S(1)} %broadcast_compare_fusion.1), kind=kOutput, calls=%fused_computation.269 | convolution fusion | flops 5006591488 | bytes 26063568 | tf_op jit(solution)/shard_map/dot_general | solution.py:55
  318.5 5.6 collective-permute-start.20
  324.0 3.4 collective-permute-start.19
  328.8 4.1 collective-permute-done.21
  333.5 8.9 %fusion.80 = f32[320,1024]{1,0:T(8,128)S(1)} fusion(bf16[7632,1024]{1,0:T(8,128)(2,1)} %constant_dynamic-update-slice_fusion.4, f32[320,7632]{1,0:T(8,128)S(1)} %get-tuple-element.282, f32[320]{0:T(512)S(1)} %get-tuple-element.266, f32[320]{0:T(512)S(1)} %get-tuple-element.195, s32[7632]{0:T(1024)S(1)} %iota_add_fusion, s32[320]{0:T(512)S(1)} %eq.132), kind=kOutput, calls=%fused_computation.258 | convolution fusion | flops 5016360960 | bytes 26744384 | tf_op jit(solution)/shard_map/dot_general | solution.py:45
  344.3 4.3 collective-permute-start.24
  348.6 17.9 %convert_bitcast_fusion = bf16[8,7632,128]{2,1,0:T(8,128)(2,1)} fusion(f32[320,7632]{1,0:T(8,128)} %copy-done.52, f32[320]{0:T(512)S(1)} %get-tuple-element.266, f32[320]{0:T(512)S(1)} %get-tuple-element.195, s32[7632]{0:T(1024)S(1)} %iota_add_fusion, s32[320]{0:T(512)S(1)} %eq.132, bf16[320,1024]{1,0:T(8,128)(2,1)} %constant_dynamic-update-slice_fusion.5), kind=kOutput, calls=%fused_computation.8 | convolution fusion | flops 5024176128 | bytes 26089024 | tf_op jit(solution)/shard_map/sv,swc->wvc/dot_general | solution.py:955
  379.4 3.4 gradient_block.13
  382.9 3.4 gradient_block.12
  386.8 10.0 %multiply_convert_fusion.refs_1_ = bf16[512,4096]{1,0:T(8,128)(2,1)S(1)} fusion(bf16[512,4096]{1,0:T(8,128)(2,1)} %copy-done.42, bf16[512,1024]{1,0:T(8,128)(2,1)S(1)} %get-tuple-element.201.refs_0_, bf16[1024,12288]{1,0:T(8,128)(2,1)} %all-gather.10.cloned.1.call-done.weight_ref), kind=kOutput, calls=%fused_computation.20 | convolution fusion | flops 4301258752 | bytes 17825792 | tf_op jit(solution)/shard_map/dot_general | solution.py:45
  396.8 4.3 gradient_block.14
  403.6 3.3 gradient_block.15
  407.4 11.3 %multiply_reduce_fusion.2 = (f32[1024]{0:T(1024)S(1)}, f32[512]{0:T(512)S(1)}, f32[1024]{0:T(1024)S(1)}, f32[512,1024]{1,0:T(8,128)}) fusion(f32[512,1024]{1,0:T(8,128)} %copy-done.47, f32[512]{0:T(512)S(1)} %fusion.73, f32[512]{0:T(512)S(1)} %broadcast_multiply_fusion.2, f32[1024]{0:T(1024)S(1)} %bitcast.208, ...), kind=kOutput, calls=%fused_computation.40 | convolution fusion | flops 4300207616 | bytes 18894848 | tf_op jit(solution)/shard_map/dot_general | solution.py:55
  426.0 3.4 gradient_block.17
  429.7 16.6 %attend_back.1.refs_2_.dqkv_ref = bf16[512,3072]{1,0:T(8,128)(2,1)S(1)} custom-call(bf16[512,3072]{1,0:T(8,128)(2,1)S(1)} %copy-done.1, bf16[512,3072]{1,0:T(8,128)(2,1)S(1)} %copy-done.1, bf16[512,3072]{1,0:T(8,128)(2,1)S(1)} %copy-done.1, bf16[512,1024]{1,0:T(8,128)(2,1)S(1)} %fusion.29.do_ref, f32[8,2,512]{2,1,0:T(2,128)S(1)} %get-tuple-element.123.lse_ref, ...), custom_call_target="tpu_custom_call" | custom-call | tf_op jit(solution)/shard_map/attend_back/pallas_call | solution.py:126
  446.2 8.8 %collective-permute-done.29.refs_3_ = bf16[256,4096]{1,0:T(8,128)(2,1)S(1)} collective-permute-done((bf16[256,4096]{1,0:T(8,128)(2,1)S(1)}, bf16[256,4096]{1,0:T(8,128)(2,1)S(1)}, u32[]{:S(2)}, u32[]{:S(2)}) %collective-permute-start.29) | collective-permute-done | bytes 2097184 | tf_op jit(solution)/shard_map/ppermute | solution.py:448
  455.0 3.3 gradient_block.18
  463.6 5.0 gradient_block.21
  471.4 3.3 convert_reduce_fusion
  478.4 4.0 gradient_block.19
  483.8 8.1 embed_back.1
  493.2 36.0 %collective-permute-done.31.refs_3_ = bf16[256,4096]{1,0:T(8,128)(2,1)} collective-permute-done((bf16[256,4096]{1,0:T(8,128)(2,1)}, bf16[256,4096]{1,0:T(8,128)(2,1)}, u32[]{:S(2)}, u32[]{:S(2)}) %collective-permute-start.31) | collective-permute-done | bytes 2097184 | tf_op jit(solution)/shard_map/ppermute | solution.py:448
  529.2 6.9 concatenate.84
  542.1 3.3 gradient_block.20
  550.4 4.2 gradient_block.23
  557.1 4.2 all-to-all-start.1
  570.5 11.0 %collective-permute-done.33 = bf16[528,256]{1,0:T(8,128)(2,1)S(1)} collective-permute-done((bf16[528,256]{1,0:T(8,128)(2,1)S(1)}, bf16[528,256]{1,0:T(8,128)(2,1)S(1)}, u32[]{:S(2)}, u32[]{:S(2)}) %collective-permute-start.33) | collective-permute-done | bytes 270368 | tf_op jit(solution)/shard_map/ppermute | solution.py:841
  581.6 22.9 %collective-permute-done.36.refs_5_ = bf16[256,4096]{1,0:T(8,128)(2,1)} collective-permute-done((bf16[256,4096]{1,0:T(8,128)(2,1)}, bf16[256,4096]{1,0:T(8,128)(2,1)}, u32[]{:S(2)}, u32[]{:S(2)}) %collective-permute-start.36) | collective-permute-done | bytes 2097184 | tf_op jit(solution)/shard_map/ppermute | solution.py:448
  604.5 5.2 gradient_block.22
  618.1 6.5 span.3
  625.9 6.5 span.4
  636.9 6.4 span.5
  647.2 21.1 %press.1 = (f32[1,256,12288]{2,1,0:T(8,128)}, bf16[4,256,1536]{2,1,0:T(8,128)(2,1)}, bf16[4,256,1536]{2,1,0:T(8,128)(2,1)}) custom-call(s32[1]{0:T(128)} %bitcast.4.core_ref, f32[2]{0:T(128)} %pad_maximum_fusion.5.scale_ref, f32[256,4096]{1,0:T(8,128)} %get-tuple-element.148.refs_0_, f32[256,4096]{1,0:T(8,128)} %get-tuple-element.149.refs_1_, ...), custom_call_target="tpu_custom_call" | custom-call | tf_op jit(solution)/shard_map/press/pallas_call | solution.py:745
  668.3 26.1 %collective-permute-start.40 = (bf16[4,256,1536]{2,1,0:T(8,128)(2,1)}, bf16[4,256,1536]{2,1,0:T(8,128)(2,1)S(1)}, u32[]{:S(2)}, u32[]{:S(2)}) collective-permute-start(bf16[4,256,1536]{2,1,0:T(8,128)(2,1)} %get-tuple-element.152), channel_id=1, source_target_pairs={{0,4},{4,0},{8,12},{12,8},{16,20},{20,16},{24,28},{28,24},{1,5},{5... | collective-permute-start | bytes 9437192 | tf_op jit(solution)/shard_map/ppermute | solution.py:814
  694.4 5.5 collective-permute-done.40
  708.3 8.5 collective-permute-done.42
  720.7 4.0 collective-permute-done.41
  724.6 6.4 collective-permute-done.43
  733.7 3.7 collective-permute-done.44
  744.5 5.0 fusion.53
  751.5 25.0 %add_rows.1.grad_ref = f32[7632,128]{1,0:T(8,128)} custom-call(s32[16384]{0:T(1024)} %copy-done.41, bf16[4,4624,128]{2,1,0:T(8,128)(2,1)} %bitcast.185), custom_call_target="tpu_custom_call" | custom-call | tf_op jit(solution)/shard_map/add_rows/pallas_call | solution.py:643
  776.5 13.4 %update.1 = (f32[7632,128]{1,0:T(8,128)}, f32[7632,128]{1,0:T(8,128)}, f32[1,128]{1,0:T(1,128)}, f32[1,128]{1,0:T(1,128)}) custom-call(f32[7632,128]{1,0:T(8,128)} %add_rows.1.grad_ref, bf16[7632,128]{1,0:T(8,128)(2,1)} %bitcast.189, f32[7632,128]{1,0:T(8,128)} %table_ref.3, f32[7632,128]{1,0:T(8,128)} %first_ref.1, f32[7632,128]{1,0:T(8,128)} %second_ref.1), custom_call_target="tpu_custom_call" | custom-call | tf_op jit(solution)/shard_map/update/pallas_call | solution.py:790
  794.4 3.6 all-gather.14.cloned.1.call-done
  804.2 9.1 %convert_element_type.365 = f32[256,12288]{1,0:T(8,128)} convert(bf16[256,12288]{1,0:T(8,128)(2,1)} %all-gather.14.cloned.1.call-done) | non-fusion elementwise | flops 3145728 | bytes 18874368 | tf_op jit(solution)/shard_map/convert_element_type | solution.py:1073
  833.6 3.4 multiply_subtract_fusion.2
  841.5 4.8 multiply_subtract_fusion
  846.3 3.3 multiply_subtract_fusion.1
  (425 shorter events, 208.8 us)
Async XLA Ops:
  7.2 77.5 %all-gather.8.cloned.1.call-start = ((), (), s32[]{:S(2)}) async-start(), calls=%async_computation.3 | async-start | bytes 10985472 | tf_op jit(solution)/shard_map/all_gather | solution.py:881
  11.9 218.7 %all-gather.10.cloned.1.call-start = ((), (), s32[]{:S(2)}) async-start(), calls=%async_computation.4 | async-start | bytes 28311552 | tf_op jit(solution)/shard_map/all_gather | solution.py:888
  12.1 1.3 collective-permute-start.6
  13.5 4.7 collective-permute-start.7
  18.2 7.8 collective-permute-start.8
  20.4 60.6 %copy-start.56 = (bf16[256,1536]{1,0:T(8,128)(2,1)}, bf16[256,1536]{1,0:T(8,128)(2,1)S(1)}, u32[]{:S(2)}) copy-start(bf16[256,1536]{1,0:T(8,128)(2,1)S(1)} %convert_element_type.285) | copy-start | bytes 2359300
  20.4 60.6 %collective-permute-start.5 = (bf16[256,1536]{1,0:T(8,128)(2,1)S(1)}, bf16[256,1536]{1,0:T(8,128)(2,1)S(1)}, u32[]{:S(2)}, u32[]{:S(2)}) collective-permute-start(bf16[256,1536]{1,0:T(8,128)(2,1)S(1)} %convert_element_type.285), channel_id=1, source_target_pairs={{0,1},{1,2},{2,3},{3,0},{4,5},{5,6},{6,7},{7,4},{8,9},{9,10},{10,1... | collective-permute-start | bytes 2359304 | tf_op jit(solution)/shard_map/ppermute | solution.py:341
  22.0 59.0 %collective-permute-start.4 = (bf16[256,1536]{1,0:T(8,128)(2,1)S(1)}, bf16[256,1536]{1,0:T(8,128)(2,1)S(1)}, u32[]{:S(2)}, u32[]{:S(2)}) collective-permute-start(bf16[256,1536]{1,0:T(8,128)(2,1)S(1)} %convert_element_type.285), channel_id=1, source_target_pairs={{0,2},{1,3},{2,0},{3,1},{4,6},{5,7},{6,4},{7,5},{8,10},{9,11},{10,... | collective-permute-start | bytes 2359304 | tf_op jit(solution)/shard_map/ppermute | solution.py:341
  24.6 58.1 %collective-permute-start.3 = (bf16[256,1536]{1,0:T(8,128)(2,1)S(1)}, bf16[256,1536]{1,0:T(8,128)(2,1)}, u32[]{:S(2)}, u32[]{:S(2)}) collective-permute-start(bf16[256,1536]{1,0:T(8,128)(2,1)S(1)} %convert_element_type.285), channel_id=1, source_target_pairs={{0,3},{1,0},{2,1},{3,2},{4,7},{5,4},{6,5},{7,6},{8,11},{9,8},{10,9... | collective-permute-start | bytes 2359304 | tf_op jit(solution)/shard_map/ppermute | solution.py:341
  28.5 52.4 %copy-start.41 = (s32[16384]{0:T(1024)}, s32[16384]{0:T(1024)S(1)}, u32[]{:S(2)}) copy-start(s32[16384]{0:T(1024)S(1)} %fusion.59.ids_ref) | copy-start | bytes 196612
  89.1 21.9 %collective-permute-start.11 = (bf16[1792,128]{1,0:T(8,128)(2,1)S(1)}, bf16[1792,128]{1,0:T(8,128)(2,1)S(1)}, u32[]{:S(2)}, u32[]{:S(2)}) collective-permute-start(bf16[1792,128]{1,0:T(8,128)(2,1)S(1)} %get-tuple-element.238), channel_id=1, source_target_pairs={{0,3},{1,0},{2,1},{3,2},{4,7},{5,4},{6,5},{7,6},{8,11},{9,8},{10,9... | collective-permute-start | bytes 1376264 | tf_op jit(solution)/shard_map/ppermute | solution.py:373
  100.0 39.6 %collective-permute-start.10 = (bf16[1792,128]{1,0:T(8,128)(2,1)S(1)}, bf16[1792,128]{1,0:T(8,128)(2,1)S(1)}, u32[]{:S(2)}, u32[]{:S(2)}) collective-permute-start(bf16[1792,128]{1,0:T(8,128)(2,1)S(1)} %get-tuple-element.239), channel_id=1, source_target_pairs={{0,2},{1,3},{2,0},{3,1},{4,6},{5,7},{6,4},{7,5},{8,10},{9,11},{10,... | collective-permute-start | bytes 1376264 | tf_op jit(solution)/shard_map/ppermute | solution.py:373
  100.0 39.6 %collective-permute-start.9 = (bf16[1792,128]{1,0:T(8,128)(2,1)S(1)}, bf16[1792,128]{1,0:T(8,128)(2,1)S(1)}, u32[]{:S(2)}, u32[]{:S(2)}) collective-permute-start(bf16[1792,128]{1,0:T(8,128)(2,1)S(1)} %get-tuple-element.240), channel_id=1, source_target_pairs={{0,1},{1,2},{2,3},{3,0},{4,5},{5,6},{6,7},{7,4},{8,9},{9,10},{10,1... | collective-permute-start | bytes 1376264 | tf_op jit(solution)/shard_map/ppermute | solution.py:373
  149.7 44.3 %all-to-all-start = ((bf16[8,512,128]{2,1,0:T(8,128)(2,1)}), bf16[8,512,128]{2,1,0:T(8,128)(2,1)S(1)}, u32[]{:S(2)}, u32[]{:S(2)}) async-start(bf16[8,512,128]{2,1,0:T(8,128)(2,1)} %bitcast.188), calls=%async_computation | async-start | bytes 2097152 | tf_op jit(solution)/shard_map/all_to_all | solution.py:898
  153.2 147.6 %all-gather.12.cloned.1.call-start = ((), (), s32[]{:S(2)}) async-start(), calls=%async_computation.5 | async-start | bytes 6598656 | tf_op jit(solution)/shard_map/all_gather | solution.py:921
  153.9 3.7 collective-permute-start.12
  154.2 29.8 %collective-permute-start.15 = (s32[1,592]{1,0:T(1,128)S(1)}, s32[1,592]{1,0:T(1,128)S(1)}, u32[]{:S(2)}, u32[]{:S(2)}) collective-permute-start(s32[1,592]{1,0:T(1,128)S(1)} %pad_add_fusion.3), channel_id=1, source_target_pairs={{0,0},{1,4},{2,1},{3,5},{4,2},{5,6},{6,3},{7,7},{8,8},{9,12},{10,9... | collective-permute-start | bytes 7112 | tf_op jit(solution)/shard_map/ppermute | solution.py:494
  158.8 20.4 %collective-permute-start.13 = (f32[]{:T(128)}, f32[]{:T(128)}, u32[]{:S(2)}, u32[]{:S(2)}) collective-permute-start(f32[]{:T(128)} %add.643), channel_id=1, source_target_pairs={{0,8},{4,12},{8,0},{12,4},{16,24},{20,28},{24,16},{28,20},{1,9},{5... | collective-permute-start | bytes 20 | tf_op jit(solution)/shard_map/ppermute | solution.py:331
  179.8 3.7 collective-permute-start.14
  184.1 47.9 %copy-start.78 = (s32[1,80]{1,0:T(1,128)}, s32[1,80]{1,0:T(1,128)S(1)}, u32[]{:S(2)}) copy-start(s32[1,80]{1,0:T(1,128)S(1)} %slice.203) | copy-start | bytes 964
  199.4 51.2 %copy-start.23 = (f32[512,1024]{1,0:T(8,128)}, f32[512,1024]{1,0:T(8,128)S(1)}, u32[]{:S(2)}) copy-start(f32[512,1024]{1,0:T(8,128)S(1)} %get-tuple-element.212.embedded_ref) | copy-start | bytes 6291460
  199.8 39.1 %copy-start.12 = (bf16[512,1024]{1,0:T(8,128)(2,1)}, bf16[512,1024]{1,0:T(8,128)(2,1)S(1)}, u32[]{:S(2)}) copy-start(bf16[512,1024]{1,0:T(8,128)(2,1)S(1)} %fusion.23.refs_0_) | copy-start | bytes 3145732
  230.6 406.2 %reduce-scatter.2.cloned.1.call-start = ((), (), s32[]{:S(2)}) async-start(), calls=%async_computation.6 | async-start | bytes 17584128 | tf_op jit(solution)/shard_map/reduce_scatter | solution.py:957
  254.9 171.0 %copy-start.10 = (bf16[512,1024]{1,0:T(8,128)(2,1)}, bf16[512,1024]{1,0:T(8,128)(2,1)S(1)}, u32[]{:S(2)}) copy-start(bf16[512,1024]{1,0:T(8,128)(2,1)S(1)} %fusion.22.fin_ref.refs_0_) | copy-start | bytes 3145732
  284.8 12.4 %collective-permute-start.17 = (bf16[80,1024]{1,0:T(8,128)(2,1)}, bf16[80,1024]{1,0:T(8,128)(2,1)}, u32[]{:S(2)}, u32[]{:S(2)}) collective-permute-start(bf16[80,1024]{1,0:T(8,128)(2,1)} %get-tuple-element.210), channel_id=1, source_target_pairs={{0,2},{1,3},{2,0},{3,1},{4,6},{5,7},{6,4},{7,5},{8,10},{9,11},{10,... | collective-permute-start | bytes 491528 | tf_op jit(solution)/shard_map/ppermute | solution.py:341
  287.0 8.6 collective-permute-start.16
  288.7 11.5 %collective-permute-start.18 = (bf16[80,1024]{1,0:T(8,128)(2,1)}, bf16[80,1024]{1,0:T(8,128)(2,1)S(1)}, u32[]{:S(2)}, u32[]{:S(2)}) collective-permute-start(bf16[80,1024]{1,0:T(8,128)(2,1)} %get-tuple-element.210), channel_id=1, source_target_pairs={{0,1},{1,2},{2,3},{3,0},{4,5},{5,6},{6,7},{7,4},{8,9},{9,10},{10,1... | collective-permute-start | bytes 491528 | tf_op jit(solution)/shard_map/ppermute | solution.py:341
  318.5 10.3 %collective-permute-start.20 = (f32[1,3,320]{2,1,0:T(4,128)S(1)}, f32[1,3,320]{2,1,0:T(4,128)S(1)}, u32[]{:S(2)}, u32[]{:S(2)}) collective-permute-start(f32[1,3,320]{2,1,0:T(4,128)S(1)} %maximum_bitcast_fusion), channel_id=1, source_target_pairs={{0,2},{1,3},{2,0},{3,1},{4,6},{5,7},{6,4},{7,5},{8,10},{9,11},{10,... | collective-permute-start | bytes 11528 | tf_op jit(solution)/shard_map/ppermute | solution.py:341
  324.0 4.7 collective-permute-start.19
  327.4 5.4 collective-permute-start.21
  344.3 22.1 %collective-permute-start.22 = (bf16[80,1024]{1,0:T(8,128)(2,1)}, bf16[80,1024]{1,0:T(8,128)(2,1)}, u32[]{:S(2)}, u32[]{:S(2)}) collective-permute-start(bf16[80,1024]{1,0:T(8,128)(2,1)} %get-tuple-element.246), channel_id=1, source_target_pairs={{0,1},{1,2},{2,3},{3,0},{4,5},{5,6},{6,7},{7,4},{8,9},{9,10},{10,1... | collective-permute-start | bytes 491528 | tf_op jit(solution)/shard_map/ppermute | solution.py:360
  344.3 22.1 %collective-permute-start.24 = (bf16[80,1024]{1,0:T(8,128)(2,1)}, bf16[80,1024]{1,0:T(8,128)(2,1)}, u32[]{:S(2)}, u32[]{:S(2)}) collective-permute-start(bf16[80,1024]{1,0:T(8,128)(2,1)} %get-tuple-element.247), channel_id=1, source_target_pairs={{0,3},{1,0},{2,1},{3,2},{4,7},{5,4},{6,5},{7,6},{8,11},{9,8},{10,9... | collective-permute-start | bytes 491528 | tf_op jit(solution)/shard_map/ppermute | solution.py:360
  348.6 17.9 %collective-permute-start.23 = (bf16[80,1024]{1,0:T(8,128)(2,1)}, bf16[80,1024]{1,0:T(8,128)(2,1)}, u32[]{:S(2)}, u32[]{:S(2)}) collective-permute-start(bf16[80,1024]{1,0:T(8,128)(2,1)} %get-tuple-element.248), channel_id=1, source_target_pairs={{0,2},{1,3},{2,0},{3,1},{4,6},{5,7},{6,4},{7,5},{8,10},{9,11},{10,... | collective-permute-start | bytes 491528 | tf_op jit(solution)/shard_map/ppermute | solution.py:360
  386.3 10.5 %collective-permute-start.25 = (bf16[256,4096]{1,0:T(8,128)(2,1)}, bf16[256,4096]{1,0:T(8,128)(2,1)}, u32[]{:S(2)}, u32[]{:S(2)}) collective-permute-start(bf16[256,4096]{1,0:T(8,128)(2,1)} %gradient_block.12), channel_id=1, source_target_pairs={{0,4},{4,0},{8,12},{12,8},{16,20},{20,16},{24,28},{28,24},{1,5},{5... | collective-permute-start | bytes 6291464 | tf_op jit(solution)/shard_map/ppermute | solution.py:432
  386.3 10.5 %collective-permute-start.26 = (bf16[256,4096]{1,0:T(8,128)(2,1)}, bf16[256,4096]{1,0:T(8,128)(2,1)}, u32[]{:S(2)}, u32[]{:S(2)}) collective-permute-start(bf16[256,4096]{1,0:T(8,128)(2,1)} %gradient_block.13), channel_id=1, source_target_pairs={{0,4},{4,0},{8,12},{12,8},{16,20},{20,16},{24,28},{28,24},{1,5},{5... | collective-permute-start | bytes 6291464 | tf_op jit(solution)/shard_map/ppermute | solution.py:433
  406.9 19.0 %collective-permute-start.27 = (bf16[256,4096]{1,0:T(8,128)(2,1)}, bf16[256,4096]{1,0:T(8,128)(2,1)S(1)}, u32[]{:S(2)}, u32[]{:S(2)}) collective-permute-start(bf16[256,4096]{1,0:T(8,128)(2,1)} %gradient_block.15), channel_id=1, source_target_pairs={{0,4},{4,0},{8,12},{12,8},{16,20},{20,16},{24,28},{28,24},{1,5},{5... | collective-permute-start | bytes 6291464 | tf_op jit(solution)/shard_map/ppermute | solution.py:432
  406.9 19.0 %collective-permute-start.28 = (bf16[256,4096]{1,0:T(8,128)(2,1)S(1)}, bf16[256,4096]{1,0:T(8,128)(2,1)S(1)}, u32[]{:S(2)}, u32[]{:S(2)}) collective-permute-start(bf16[256,4096]{1,0:T(8,128)(2,1)S(1)} %gradient_block.16), channel_id=1, source_target_pairs={{0,4},{4,0},{8,12},{12,8},{16,20},{20,16},{24,28},{28,24},{1,5},{5... | collective-permute-start | bytes 6291464 | tf_op jit(solution)/shard_map/ppermute | solution.py:433
  407.4 47.6 %collective-permute-start.29 = (bf16[256,4096]{1,0:T(8,128)(2,1)S(1)}, bf16[256,4096]{1,0:T(8,128)(2,1)S(1)}, u32[]{:S(2)}, u32[]{:S(2)}) collective-permute-start(bf16[256,4096]{1,0:T(8,128)(2,1)S(1)} %gradient_block.14), channel_id=1, source_target_pairs={{0,1},{1,0},{2,3},{3,2},{4,5},{5,4},{6,7},{7,6},{8,9},{9,8},{10,11... | collective-permute-start | bytes 6291464 | tf_op jit(solution)/shard_map/ppermute | solution.py:448
  458.3 16.4 %collective-permute-start.30 = (bf16[256,4096]{1,0:T(8,128)(2,1)}, bf16[256,4096]{1,0:T(8,128)(2,1)}, u32[]{:S(2)}, u32[]{:S(2)}) collective-permute-start(bf16[256,4096]{1,0:T(8,128)(2,1)} %gradient_block.18), channel_id=1, source_target_pairs={{0,4},{4,0},{8,12},{12,8},{16,20},{20,16},{24,28},{28,24},{1,5},{5... | collective-permute-start | bytes 6291464 | tf_op jit(solution)/shard_map/ppermute | solution.py:432
  458.3 70.8 %collective-permute-start.31 = (bf16[256,4096]{1,0:T(8,128)(2,1)}, bf16[256,4096]{1,0:T(8,128)(2,1)}, u32[]{:S(2)}, u32[]{:S(2)}) collective-permute-start(bf16[256,4096]{1,0:T(8,128)(2,1)} %gradient_block.17), channel_id=1, source_target_pairs={{0,1},{1,0},{2,3},{3,2},{4,5},{5,4},{6,7},{7,6},{8,9},{9,8},{10,11... | collective-permute-start | bytes 6291464 | tf_op jit(solution)/shard_map/ppermute | solution.py:448
  468.6 98.7 %collective-permute-start.37 = (bf16[256,4096]{1,0:T(8,128)(2,1)}, bf16[256,4096]{1,0:T(8,128)(2,1)}, u32[]{:S(2)}, u32[]{:S(2)}) collective-permute-start(bf16[256,4096]{1,0:T(8,128)(2,1)} %gradient_block.21), channel_id=1, source_target_pairs={{2,4},{3,5},{4,2},{5,3},{10,12},{11,13},{12,10},{13,11},{18,20},{1... | collective-permute-start | bytes 6291464 | tf_op jit(solution)/shard_map/ppermute | solution.py:472
  538.2 25.5 %collective-permute-start.32 = (bf16[528,512]{1,0:T(8,128)(2,1)}, bf16[528,512]{1,0:T(8,128)(2,1)}, u32[]{:S(2)}, u32[]{:S(2)}) collective-permute-start(bf16[528,512]{1,0:T(8,128)(2,1)} %dynamic-slice_convert_fusion), channel_id=1, source_target_pairs={{0,16},{4,20},{8,24},{12,28},{16,0},{20,4},{24,8},{28,12},{1,17},{... | collective-permute-start | bytes 1622024 | tf_op jit(solution)/shard_map/ppermute | solution.py:841
  538.4 66.0 %collective-permute-start.36 = (bf16[256,4096]{1,0:T(8,128)(2,1)}, bf16[256,4096]{1,0:T(8,128)(2,1)}, u32[]{:S(2)}, u32[]{:S(2)}) collective-permute-start(bf16[256,4096]{1,0:T(8,128)(2,1)} %copy-done.37), channel_id=1, source_target_pairs={{0,1},{1,0},{2,3},{3,2},{4,5},{5,4},{6,7},{7,6},{8,9},{9,8},{10,11... | collective-permute-start | bytes 6291464 | tf_op jit(solution)/shard_map/ppermute | solution.py:448
  545.4 59.0 %collective-permute-start.35 = (bf16[256,4096]{1,0:T(8,128)(2,1)}, bf16[256,4096]{1,0:T(8,128)(2,1)}, u32[]{:S(2)}, u32[]{:S(2)}) collective-permute-start(bf16[256,4096]{1,0:T(8,128)(2,1)} %gradient_block.20), channel_id=1, source_target_pairs={{0,4},{4,0},{8,12},{12,8},{16,20},{20,16},{24,28},{28,24},{1,5},{5... | collective-permute-start | bytes 6291464 | tf_op jit(solution)/shard_map/ppermute | solution.py:433
  557.1 57.2 %all-to-all-start.1 = ((bf16[8,512,128]{2,1,0:T(8,128)(2,1)}), bf16[8,512,128]{2,1,0:T(8,128)(2,1)}, u32[]{:S(2)}, u32[]{:S(2)}) async-start(bf16[8,512,128]{2,1,0:T(8,128)(2,1)} %bitcast_bitcast_fusion), calls=%async_computation.1 | async-start | bytes 2097152 | tf_op jit(solution)/shard_map/all_to_all | solution.py:973
  561.3 190.2 %all-gather.18.cloned.1.call-start = ((), (), s32[]{:S(2)}) async-start(), calls=%async_computation.9 | async-start | bytes 5918720 | tf_op jit(solution)/shard_map/all_gather | solution.py:983
  561.4 55.2 %collective-permute-start.39 = (bf16[256,4096]{1,0:T(8,128)(2,1)}, bf16[256,4096]{1,0:T(8,128)(2,1)}, u32[]{:S(2)}, u32[]{:S(2)}) collective-permute-start(bf16[256,4096]{1,0:T(8,128)(2,1)} %copy-done.33), channel_id=1, source_target_pairs={{2,4},{3,5},{4,2},{5,3},{10,12},{11,13},{12,10},{13,11},{18,20},{1... | collective-permute-start | bytes 6291464 | tf_op jit(solution)/shard_map/ppermute | solution.py:472
  565.4 16.1 %collective-permute-start.33 = (bf16[528,256]{1,0:T(8,128)(2,1)S(1)}, bf16[528,256]{1,0:T(8,128)(2,1)S(1)}, u32[]{:S(2)}, u32[]{:S(2)}) collective-permute-start(bf16[528,256]{1,0:T(8,128)(2,1)S(1)} %dynamic-slice_convert_fusion.1), channel_id=1, source_target_pairs={{0,8},{4,12},{8,0},{12,4},{16,24},{20,28},{24,16},{28,20},{1,9},{5... | collective-permute-start | bytes 811016 | tf_op jit(solution)/shard_map/ppermute | solution.py:841
  609.6 24.0 %collective-permute-start.38 = (bf16[256,4096]{1,0:T(8,128)(2,1)}, bf16[256,4096]{1,0:T(8,128)(2,1)}, u32[]{:S(2)}, u32[]{:S(2)}) collective-permute-start(bf16[256,4096]{1,0:T(8,128)(2,1)} %gradient_block.22), channel_id=1, source_target_pairs={{2,4},{3,5},{4,2},{5,3},{10,12},{11,13},{12,10},{13,11},{18,20},{1... | collective-permute-start | bytes 6291464 | tf_op jit(solution)/shard_map/ppermute | solution.py:472
  611.8 1.4 collective-permute-start.34
  636.8 161.2 %all-gather.14.cloned.1.call-start = ((), (), s32[]{:S(2)}) async-start(), calls=%async_computation.7 | async-start | bytes 7077888 | tf_op jit(solution)/shard_map/all_gather | solution.py:1047
  668.3 31.6 %collective-permute-start.40 = (bf16[4,256,1536]{2,1,0:T(8,128)(2,1)}, bf16[4,256,1536]{2,1,0:T(8,128)(2,1)S(1)}, u32[]{:S(2)}, u32[]{:S(2)}) collective-permute-start(bf16[4,256,1536]{2,1,0:T(8,128)(2,1)} %get-tuple-element.152), channel_id=1, source_target_pairs={{0,4},{4,0},{8,12},{12,8},{16,20},{20,16},{24,28},{28,24},{1,5},{5... | collective-permute-start | bytes 9437192 | tf_op jit(solution)/shard_map/ppermute | solution.py:814
  704.8 11.9 %collective-permute-start.42 = (bf16[128,1536]{1,0:T(8,128)(2,1)S(1)}, bf16[128,1536]{1,0:T(8,128)(2,1)S(1)}, u32[]{:S(2)}, u32[]{:S(2)}) collective-permute-start(bf16[128,1536]{1,0:T(8,128)(2,1)S(1)} %get-tuple-element.224), channel_id=1, source_target_pairs={{0,8},{4,12},{8,0},{12,4},{16,24},{20,28},{24,16},{28,20},{1,9},{5... | collective-permute-start | bytes 1179656 | tf_op jit(solution)/shard_map/ppermute | solution.py:814
  705.8 18.9 %collective-permute-start.41 = (bf16[128,1536]{1,0:T(8,128)(2,1)}, bf16[128,1536]{1,0:T(8,128)(2,1)S(1)}, u32[]{:S(2)}, u32[]{:S(2)}) collective-permute-start(bf16[128,1536]{1,0:T(8,128)(2,1)} %get-tuple-element.221), channel_id=1, source_target_pairs={{0,8},{4,12},{8,0},{12,4},{16,24},{20,28},{24,16},{28,20},{1,9},{5... | collective-permute-start | bytes 1179656 | tf_op jit(solution)/shard_map/ppermute | solution.py:814
  706.9 17.8 %collective-permute-start.45 = (bf16[128,1536]{1,0:T(8,128)(2,1)}, bf16[128,1536]{1,0:T(8,128)(2,1)}, u32[]{:S(2)}, u32[]{:S(2)}) collective-permute-start(bf16[128,1536]{1,0:T(8,128)(2,1)} %get-tuple-element.222), channel_id=1, source_target_pairs={{0,16},{4,20},{8,24},{12,28},{16,0},{20,4},{24,8},{28,12},{1,17},{... | collective-permute-start | bytes 1179656 | tf_op jit(solution)/shard_map/ppermute | solution.py:814
  718.7 12.4 %collective-permute-start.43 = (bf16[128,1536]{1,0:T(8,128)(2,1)}, bf16[128,1536]{1,0:T(8,128)(2,1)}, u32[]{:S(2)}, u32[]{:S(2)}) collective-permute-start(bf16[128,1536]{1,0:T(8,128)(2,1)} %fusion.40), channel_id=1, source_target_pairs={{0,16},{4,20},{8,24},{12,28},{16,0},{20,4},{24,8},{28,12},{1,17},{... | collective-permute-start | bytes 1179656 | tf_op jit(solution)/shard_map/ppermute | solution.py:814
  720.1 17.3 %collective-permute-start.44 = (bf16[128,1536]{1,0:T(8,128)(2,1)}, bf16[128,1536]{1,0:T(8,128)(2,1)S(1)}, u32[]{:S(2)}, u32[]{:S(2)}) collective-permute-start(bf16[128,1536]{1,0:T(8,128)(2,1)} %get-tuple-element.223), channel_id=1, source_target_pairs={{0,16},{4,20},{8,24},{12,28},{16,0},{20,4},{24,8},{28,12},{1,17},{... | collective-permute-start | bytes 1179656 | tf_op jit(solution)/shard_map/ppermute | solution.py:814
  732.7 7.8 collective-permute-start.46
  749.6 78.8 %all-gather.16.cloned.1.call-start = ((), (), s32[]{:S(2)}) async-start(), calls=%async_computation.8 | async-start | bytes 1216512 | tf_op jit(solution)/shard_map/all_gather | solution.py:1050
  804.0 9.3 %collective-permute-start.47 = (f32[12]{0:T(128)S(1)}, f32[12]{0:T(128)S(1)}, u32[]{:S(2)}, u32[]{:S(2)}) collective-permute-start(f32[12]{0:T(128)S(1)} %concatenate.87), channel_id=1, source_target_pairs={{0,4},{4,0},{8,12},{12,8},{16,20},{20,16},{24,28},{28,24},{1,5},{5... | collective-permute-start | bytes 152 | tf_op jit(solution)/shard_map/ppermute | solution.py:331
  813.3 3.5 collective-permute-start.48
  816.8 3.5 collective-permute-start.49
  820.4 3.5 collective-permute-start.50
  823.9 4.4 collective-permute-start.51
  (75 other events, 585.6 us)
Sparse Core Ops, SparseCore 0:
  12.1 64.7 all-gather.7
  86.4 144.1 all-gather.9
  233.1 43.8 all-gather.11
  368.6 111.4 reduce-scatter.1
  637.0 114.5 all-gather.17
  754.0 43.9 all-gather.13
  800.6 23.7 all-gather.15

commit v14 on v13

--- a/solution.py
+++ b/solution.py
@@ -470,7 +470,8 @@
                     moves.append((wide * n_narrow + narrow, target))
         total, *values = together(total, *values)
         moved = lax.ppermute(total, ("wide", "narrow"), moves)
-        self.result = jnp.where(self.pair == self.core, total, moved)
+        self.stays = (self.pair == self.core).astype(jnp.int32)
+        self.result = (total, moved)
         return values
 
 
@@ -657,34 +658,45 @@
     )(ids.reshape(-1), values)
 
 
-def span_kernel(momentum_ref, grad_ref, error_ref, span_ref, sum_ref):
-    grad = grad_ref[...].astype(jnp.float32)
-    span = BETA * momentum_ref[...] + (1.0 - BETA) * grad + error_ref[0]
-    span_ref[...] = span
-
+def span_kernel(stays_ref, momentum_ref, total_ref, moved_ref, error_ref, span_ref, sum_ref):
     @pl.when(pl.program_id(0) == 0)
     def _():
         sum_ref[...] = jnp.zeros_like(sum_ref)
 
-    sum_ref[...] += jnp.sum(jnp.abs(span), axis=0, keepdims=True)
-
-
-def span_of(momentum, grad, error, start):
-    rows, cols = grad.shape
+    def write(grad_ref):
+        grad = grad_ref[...].astype(jnp.float32)
+        span = BETA * momentum_ref[...] + (1.0 - BETA) * grad + error_ref[0]
+        span_ref[...] = span
+        sum_ref[...] += jnp.sum(jnp.abs(span), axis=0, keepdims=True)
+
+    @pl.when(stays_ref[0] == 1)
+    def _():
+        write(total_ref)
+
+    @pl.when(stays_ref[0] != 1)
+    def _():
+        write(moved_ref)
+
+
+def span_of(momentum, piece, error, start):
+    total, moved = piece.result
+    rows, cols = total.shape
     block = 1024
     first = start // block
+    grad = pl.BlockSpec((rows, block), lambda step, _: (0, step))
     span, sums = pl.pallas_call(
         span_kernel,
-        grid=(cols // block,),
-        in_specs=[
-            pl.BlockSpec((rows, block), lambda step: (0, first + step)),
-            pl.BlockSpec((rows, block), lambda step: (0, step)),
-            pl.BlockSpec((1, rows, block), lambda step: (0, 0, first + step)),
-        ],
-        out_specs=[
-            pl.BlockSpec((rows, block), lambda step: (0, step)),
-            pl.BlockSpec((1, block), lambda step: (0, 0)),
-        ],
+        grid_spec=pltpu.PrefetchScalarGridSpec(
+            num_scalar_prefetch=1,
+            grid=(cols // block,),
+            in_specs=[
+                pl.BlockSpec((rows, block), lambda step, _: (0, first + step)),
+                grad,
+                grad,
+                pl.BlockSpec((1, rows, block), lambda step, _: (0, 0, first + step)),
+            ],
+            out_specs=[grad, pl.BlockSpec((1, block), lambda step, _: (0, 0))],
+        ),
         out_shape=[
             jax.ShapeDtypeStruct((rows, cols), jnp.float32),
             jax.ShapeDtypeStruct((1, block), jnp.float32),
@@ -692,7 +704,7 @@
         compiler_params=pltpu.CompilerParams(vmem_limit_bytes=60 * 2**20),
         cost_estimate=pl.CostEstimate(flops=0, bytes_accessed=2 * 10**7, transcendentals=0),
         name="span",
-    )(momentum, grad, error)
+    )(piece.stays[None], momentum, total, moved, error)
     return span, jnp.sum(sums)
 
 
@@ -975,8 +987,8 @@
         down, up = pieces[2], pieces[1]
         mixed.away, down.result = together(mixed.away, down.result)
         mixed.finish()
-        spans = [span_of(layer_m, up.result, worker_err, 4 * D)]
-        spans.append(span_of(layer_m, down.result, worker_err, 8 * D))
+        spans = [span_of(layer_m, up, worker_err, 4 * D)]
+        spans.append(span_of(layer_m, down, worker_err, 8 * D))
         cut, mixed.result, spans, table_head = together(
             jnp.concatenate([cut, halved]), mixed.result, spans, table_head
         )
@@ -992,7 +1004,7 @@
         table_grad = table_grad.astype(jnp.float32)
     part_cols = layer.shape[1]
     if paired:
-        spans.insert(0, span_of(layer_m, mixed.result, worker_err, 0))
+        spans.insert(0, span_of(layer_m, pieces[0], worker_err, 0))
         total = sum(amount for _, amount in spans)
         spans = [span for span, _ in spans]
         scale = total / (layer_m.shape[0] * layer_m.shape[1]) + MAG_EPS

time: 865 us -> 852 us (0.985)
  waiting for transfers between devices: 212 us -> 230 us
  starting transfers between devices: 120 us -> 103 us
  other arithmetic: 102 us -> 91.2 us
    ppermute x7, starting transfers between devices: 32.6 us -> 12.2 us  [send(): lax.ppermute(value.astype(jnp.bfloat16), 'wide', swap_pairs(n_wide, bit))]
    ppermute x3, waiting for transfers between devices: 67.6 us -> 83.5 us  [across(): self.away = lax.ppermute(away, 'narrow', sides)]
    all_to_all x1, waiting for transfers between devices: 0.01 us -> 10.8 us  [shards(): cut = lax.all_to_all(cut, 'wide', 0, 0).reshape(n_wide * L, D // n_wide)]
    unnamed x168 -> x156, local copies, waits for them, and re-layouts: 40.1 us -> 33.3 us
  transfers between devices with their start and end apart: 58 -> 58, of which waited for: 28 -> 28; matrix products, arithmetic and copies ran while one was open for 20% -> 20% of each run, Pallas kernels for 27% -> 28%
where the time goes in v14:
time: 852 us; the launch traced here: 843 us
  Pallas kernels  233 us (27%)
  waiting for transfers between devices  230 us (27%)
  starting transfers between devices  103 us (12%)
  other arithmetic  91.2 us (11%)
  matrix products  79.6 us (9%)
  local copies, waits for them, and re-layouts  79.5 us (9%)
  between operations  23.5 us (3%)
    ppermute x3, waiting for transfers between devices, across(): self.away = lax.ppermute(away, 'narrow', sides)  83.5 us
    pallas_call x1, Pallas kernels, packed_rows(): pl.pallas_call(pack_kernel, grid_spec=pltpu.PrefetchScalarGridSpec(num_sc...  52.4 us
    pallas_call x12, Pallas kernels, gradient_block(): pl.pallas_call(functools.partial(block_kernel, steps), grid_spec=pltpu.Pr...  46.9 us
    ppermute x3, waiting for transfers between devices, sent_around(): lax.ppermute(block(by), 'narrow', cycle(size, by))  38.9 us
    ppermute x7, waiting for transfers between devices, send(): lax.ppermute(value.astype(jnp.bfloat16), 'wide', swap_pairs(n_wide, bit))  33.4 us
    unnamed x156, local copies, waits for them, and re-layouts  33.3 us
    dot_general x4, matrix products, matmul_nt(): lax.dot_general(left, right, (((1,), (1,)), ((), ())), preferred_element_...  32.8 us
    all_gather x1, waiting for transfers between devices, shards(): weights = lax.all_gather(layer_rows, 'wide', axis=1, tiled=True)  31 us
  transfers between devices with their start and end apart: 58, of which 28 were waited for; matrix products, arithmetic and copies ran while one was open for 20% of the time, Pallas kernels for 28%

profile of v14, /device:TPU:0, one launch (start us, length us, event | category | flops | bytes accessed | tf_op | source)
XLA Modules:
  0.0 843.4 jit_solution(14252719420073272804)
XLA Ops:
  28.5 52.4 %pack_rows.1 = bf16[4,4096,128]{2,1,0:T(8,128)(2,1)} custom-call(s32[16384]{0:T(1024)S(1)} %fusion.59.ids_ref, f32[7632,128]{1,0:T(8,128)S(1)} %copy-done.8), custom_call_target="tpu_custom_call" | custom-call | tf_op jit(solution)/shard_map/pack_rows/pallas_call | solution.py:569
  89.1 10.9 %collective-permute-start.11 = (bf16[1792,128]{1,0:T(8,128)(2,1)S(1)}, bf16[1792,128]{1,0:T(8,128)(2,1)S(1)}, u32[]{:S(2)}, u32[]{:S(2)}) collective-permute-start(bf16[1792,128]{1,0:T(8,128)(2,1)S(1)} %get-tuple-element.242), channel_id=1, source_target_pairs={{0,3},{1,0},{2,1},{3,2},{4,7},{5,4},{6,5},{7,6},{8,11},{9,8},{10,9... | collective-permute-start | bytes 1376264 | tf_op jit(solution)/shard_map/ppermute | solution.py:373
  100.7 10.3 %collective-permute-done.11 = bf16[1792,128]{1,0:T(8,128)(2,1)S(1)} collective-permute-done((bf16[1792,128]{1,0:T(8,128)(2,1)S(1)}, bf16[1792,128]{1,0:T(8,128)(2,1)S(1)}, u32[]{:S(2)}, u32[]{:S(2)}) %collective-permute-start.11) | collective-permute-done | bytes 458784 | tf_op jit(solution)/shard_map/ppermute | solution.py:373
  111.0 28.5 %collective-permute-done.10 = bf16[1792,128]{1,0:T(8,128)(2,1)S(1)} collective-permute-done((bf16[1792,128]{1,0:T(8,128)(2,1)S(1)}, bf16[1792,128]{1,0:T(8,128)(2,1)S(1)}, u32[]{:S(2)}, u32[]{:S(2)}) %collective-permute-start.10) | collective-permute-done | bytes 458784 | tf_op jit(solution)/shard_map/ppermute | solution.py:373
  139.7 5.5 take_rows.3
  145.2 3.5 conditional.1
  149.7 3.6 all-to-all-start
  158.9 18.1 %collective-permute-start.13 = (f32[]{:T(128)}, f32[]{:T(128)}, u32[]{:S(2)}, u32[]{:S(2)}) collective-permute-start(f32[]{:T(128)} %add.643), channel_id=1, source_target_pairs={{0,8},{4,12},{8,0},{12,4},{16,24},{20,28},{24,16},{28,20},{1,9},{5... | collective-permute-start | bytes 20 | tf_op jit(solution)/shard_map/ppermute | solution.py:331
  184.0 9.8 %dynamic_update_slice.46 = bf16[7632,1024]{1,0:T(8,128)(2,1)} pad(bf16[4768,1024]{1,0:T(8,128)(2,1)} %all-gather.8.cloned.1.call-done, bf16[]{:T(256)} %constant.259.clone.1), padding=0_2864x0_0 | pad | bytes 25395202 | tf_op jit(solution)/shard_map/dynamic_update_slice | solution.py:929
  199.6 31.0 %all-gather.10.cloned.1.call-done.weight_ref = bf16[1024,12288]{1,0:T(8,128)(2,1)} async-done(((bf16[1024,1536]{1,0:T(8,128)(2,1)}), bf16[1024,12288]{1,0:T(8,128)(2,1)}) %all-gather.10.cloned.1.call-update) | async-done | bytes 25165840 | tf_op jit(solution)/shard_map/all_gather | solution.py:900
  232.6 6.4 add_convert_fusion.q_ref.k_ref.v_ref
  239.0 11.7 %attend.1 = (bf16[512,1024]{1,0:T(8,128)(2,1)S(1)}, f32[8,2,512]{2,1,0:T(2,128)S(1)}) custom-call(bf16[512,3072]{1,0:T(8,128)(2,1)S(1)} %add_convert_fusion.q_ref.k_ref.v_ref, bf16[512,3072]{1,0:T(8,128)(2,1)S(1)} %add_convert_fusion.q_ref.k_ref.v_ref, bf16[512,3072]{1,0:T(8,128)(2,1)S(1)} %add_convert_fusion.q_ref.k_ref.v_ref, ...), custom_call_target="tpu_custom_call" | custom-call | tf_op jit(solution)/shard_map/attend/pallas_call | solution.py:82
  250.8 3.4 fusion.93
  255.0 11.3 %ffn_up.1 = (bf16[512,4096]{1,0:T(8,128)(2,1)S(1)}, bf16[512,4096]{1,0:T(8,128)(2,1)S(1)}) custom-call(bf16[512,1024]{1,0:T(8,128)(2,1)S(1)} %fusion.22.fin_ref.refs_0_, bf16[1024,12288]{1,0:T(8,128)(2,1)} %all-gather.10.cloned.1.call-done.weight_ref, f32[1,4096]{1,0:T(1,128)S(1)} %bitcast.182), custom_call_target="tpu_custom_call" | custom-call | flops 4294967296 | tf_op jit(solution)/shard_map/ffn_up/pallas_call | solution.py:231
  268.3 9.2 %fusion.94 = (f32[512]{0:T(512)S(1)}, f32[512,1024]{1,0:T(8,128)S(1)}) fusion(f32[1024]{0:T(1024)S(1)} %bitcast.225, bf16[512,4096]{1,0:T(8,128)(2,1)S(1)} %get-tuple-element.113.refs_1_, bf16[1024,12288]{1,0:T(8,128)(2,1)} %all-gather.10.cloned.1.call-done.weight_ref, f32[1024]{0:T(1024)S(1)} %bitcast.215, f32[1024]{0:T(1024)S(1)} %bitcast.209, ...), kind=kOutput, calls=%fused_computation.265 | convolution fusion | flops 4298636800 | bytes 16795648 | tf_op jit(solution)/shard_map/dot_general | solution.py:55
  289.6 6.1 collective-permute-done.16
  300.9 5.9 constant_dynamic-update-slice_fusion.4
  306.8 9.1 %fusion.95 = (f32[320]{0:T(512)S(1)}, f32[320,7632]{1,0:T(8,128)S(1)}) fusion(bf16[320,1024]{1,0:T(8,128)(2,1)} %constant_dynamic-update-slice_fusion.5, bf16[7632,1024]{1,0:T(8,128)(2,1)} %constant_dynamic-update-slice_fusion.4, pred[7632]{0:T(1024)(128)(4,1)S(1)} %broadcast_compare_fusion.1), kind=kOutput, calls=%fused_computation.266 | convolution fusion | flops 5006591488 | bytes 26063568 | tf_op jit(solution)/shard_map/dot_general | solution.py:55
  318.6 5.6 collective-permute-start.20
  324.2 3.4 collective-permute-start.19
  328.9 4.1 collective-permute-done.21
  333.7 8.9 %fusion.80 = f32[320,1024]{1,0:T(8,128)S(1)} fusion(bf16[7632,1024]{1,0:T(8,128)(2,1)} %constant_dynamic-update-slice_fusion.4, f32[320,7632]{1,0:T(8,128)S(1)} %get-tuple-element.286, f32[320]{0:T(512)S(1)} %get-tuple-element.270, f32[320]{0:T(512)S(1)} %get-tuple-element.199, s32[7632]{0:T(1024)S(1)} %iota_add_fusion, s32[320]{0:T(512)S(1)} %eq.133), kind=kOutput, calls=%fused_computation.255 | convolution fusion | flops 5016360960 | bytes 26744384 | tf_op jit(solution)/shard_map/dot_general | solution.py:45
  344.4 4.3 collective-permute-start.24
  348.7 17.9 %convert_bitcast_fusion = bf16[8,7632,128]{2,1,0:T(8,128)(2,1)} fusion(f32[320,7632]{1,0:T(8,128)} %copy-done.46, f32[320]{0:T(512)S(1)} %get-tuple-element.270, f32[320]{0:T(512)S(1)} %get-tuple-element.199, s32[7632]{0:T(1024)S(1)} %iota_add_fusion, s32[320]{0:T(512)S(1)} %eq.133, bf16[320,1024]{1,0:T(8,128)(2,1)} %constant_dynamic-update-slice_fusion.5), kind=kOutput, calls=%fused_computation.8 | convolution fusion | flops 5024176128 | bytes 26089024 | tf_op jit(solution)/shard_map/sv,swc->wvc/dot_general | solution.py:967
  379.5 3.4 gradient_block.13
  383.0 3.4 gradient_block.12
  386.9 10.0 %multiply_convert_fusion.refs_1_ = bf16[512,4096]{1,0:T(8,128)(2,1)S(1)} fusion(bf16[512,4096]{1,0:T(8,128)(2,1)} %copy-done.36, bf16[512,1024]{1,0:T(8,128)(2,1)S(1)} %get-tuple-element.205.refs_0_, bf16[1024,12288]{1,0:T(8,128)(2,1)} %all-gather.10.cloned.1.call-done.weight_ref), kind=kOutput, calls=%fused_computation.20 | convolution fusion | flops 4301258752 | bytes 17825792 | tf_op jit(solution)/shard_map/dot_general | solution.py:45
  396.9 4.3 gradient_block.14
  403.7 3.3 gradient_block.15
  407.6 11.2 %multiply_reduce_fusion.2 = (f32[1024]{0:T(1024)S(1)}, f32[512]{0:T(512)S(1)}, f32[1024]{0:T(1024)S(1)}, f32[512,1024]{1,0:T(8,128)}) fusion(f32[512,1024]{1,0:T(8,128)} %copy-done.41, f32[512]{0:T(512)S(1)} %fusion.73, f32[512]{0:T(512)S(1)} %broadcast_multiply_fusion.2, f32[1024]{0:T(1024)S(1)} %bitcast.210, ...), kind=kOutput, calls=%fused_computation.40 | convolution fusion | flops 4300207616 | bytes 18894848 | tf_op jit(solution)/shard_map/dot_general | solution.py:55
  422.8 3.3 fusion.29.do_ref
  426.1 3.4 gradient_block.17
  429.7 16.6 %attend_back.1.refs_2_.dqkv_ref = bf16[512,3072]{1,0:T(8,128)(2,1)S(1)} custom-call(bf16[512,3072]{1,0:T(8,128)(2,1)S(1)} %copy-done.1, bf16[512,3072]{1,0:T(8,128)(2,1)S(1)} %copy-done.1, bf16[512,3072]{1,0:T(8,128)(2,1)S(1)} %copy-done.1, bf16[512,1024]{1,0:T(8,128)(2,1)S(1)} %fusion.29.do_ref, f32[8,2,512]{2,1,0:T(2,128)S(1)} %get-tuple-element.125.lse_ref, ...), custom_call_target="tpu_custom_call" | custom-call | tf_op jit(solution)/shard_map/attend_back/pallas_call | solution.py:126
  446.3 8.7 %collective-permute-done.29.refs_3_ = bf16[256,4096]{1,0:T(8,128)(2,1)S(1)} collective-permute-done((bf16[256,4096]{1,0:T(8,128)(2,1)S(1)}, bf16[256,4096]{1,0:T(8,128)(2,1)S(1)}, u32[]{:S(2)}, u32[]{:S(2)}) %collective-permute-start.29) | collective-permute-done | bytes 2097184 | tf_op jit(solution)/shard_map/ppermute | solution.py:448
  455.1 3.3 gradient_block.18
  463.7 5.0 gradient_block.21.total_ref
  470.7 4.8 gradient_block.19
  477.2 3.3 gradient_block.20
  491.0 8.1 embed_back.1
  500.4 29.2 %collective-permute-done.31.refs_3_ = bf16[256,4096]{1,0:T(8,128)(2,1)} collective-permute-done((bf16[256,4096]{1,0:T(8,128)(2,1)}, bf16[256,4096]{1,0:T(8,128)(2,1)}, u32[]{:S(2)}, u32[]{:S(2)}) %collective-permute-start.31) | collective-permute-done | bytes 2097184 | tf_op jit(solution)/shard_map/ppermute | solution.py:448
  529.6 6.9 concatenate.84
  544.0 5.1 gradient_block.23.total_ref
  551.2 45.5 %collective-permute-done.36.refs_5_ = bf16[256,4096]{1,0:T(8,128)(2,1)} collective-permute-done((bf16[256,4096]{1,0:T(8,128)(2,1)}, bf16[256,4096]{1,0:T(8,128)(2,1)}, u32[]{:S(2)}, u32[]{:S(2)}) %collective-permute-start.36) | collective-permute-done | bytes 2097184 | tf_op jit(solution)/shard_map/ppermute | solution.py:448
  596.7 5.1 gradient_block.22.total_ref
  607.2 3.6 all-to-all-start.1
  615.3 10.8 %all-to-all-done.1 = bf16[8,512,128]{2,1,0:T(8,128)(2,1)S(1)} async-done(((bf16[8,512,128]{2,1,0:T(8,128)(2,1)}), bf16[8,512,128]{2,1,0:T(8,128)(2,1)S(1)}, u32[]{:S(2)}, u32[]{:S(2)}) %all-to-all-start.1) | async-done | bytes 1048608 | tf_op jit(solution)/shard_map/all_to_all | solution.py:985
  627.2 7.1 span.3
  635.6 7.1 span.4
  644.0 7.1 span.5
  655.0 21.6 %press.1 = (f32[1,256,12288]{2,1,0:T(8,128)}, bf16[4,256,1536]{2,1,0:T(8,128)(2,1)}, bf16[4,256,1536]{2,1,0:T(8,128)(2,1)}) custom-call(s32[1]{0:T(128)} %bitcast.4.core_ref, f32[2]{0:T(128)} %pad_maximum_fusion.5.scale_ref, f32[256,4096]{1,0:T(8,128)} %get-tuple-element.152.refs_0_, f32[256,4096]{1,0:T(8,128)} %get-tuple-element.153.refs_1_, ...), custom_call_target="tpu_custom_call" | custom-call | tf_op jit(solution)/shard_map/press/pallas_call | solution.py:757
  676.6 8.0 collective-permute-start.40
  684.5 5.5 collective-permute-done.40
  691.7 3.2 fusion.44
  697.0 9.9 %collective-permute-done.42 = bf16[128,1536]{1,0:T(8,128)(2,1)S(1)} collective-permute-done((bf16[128,1536]{1,0:T(8,128)(2,1)S(1)}, bf16[128,1536]{1,0:T(8,128)(2,1)S(1)}, u32[]{:S(2)}, u32[]{:S(2)}) %collective-permute-start.42) | collective-permute-done | bytes 393248 | tf_op jit(solution)/shard_map/ppermute | solution.py:826
  710.8 3.9 collective-permute-done.41
  714.8 6.4 collective-permute-done.43
  723.0 4.5 collective-permute-done.44
  734.7 5.0 fusion.53
  741.3 25.1 %add_rows.1.grad_ref = f32[7632,128]{1,0:T(8,128)} custom-call(s32[16384]{0:T(1024)} %copy-done.35, bf16[4,4624,128]{2,1,0:T(8,128)(2,1)} %bitcast.186), custom_call_target="tpu_custom_call" | custom-call | tf_op jit(solution)/shard_map/add_rows/pallas_call | solution.py:644
  766.4 12.6 %update.1 = (f32[7632,128]{1,0:T(8,128)}, f32[7632,128]{1,0:T(8,128)}, f32[1,128]{1,0:T(1,128)}, f32[1,128]{1,0:T(1,128)}) custom-call(f32[7632,128]{1,0:T(8,128)} %add_rows.1.grad_ref, bf16[7632,128]{1,0:T(8,128)(2,1)} %bitcast.191, f32[7632,128]{1,0:T(8,128)} %table_ref.3, f32[7632,128]{1,0:T(8,128)} %first_ref.1, f32[7632,128]{1,0:T(8,128)} %second_ref.1), custom_call_target="tpu_custom_call" | custom-call | tf_op jit(solution)/shard_map/update/pallas_call | solution.py:802
  791.2 9.1 %convert_element_type.368 = f32[256,12288]{1,0:T(8,128)} convert(bf16[256,12288]{1,0:T(8,128)(2,1)} %all-gather.14.cloned.1.call-done) | non-fusion elementwise | flops 3145728 | bytes 18874368 | tf_op jit(solution)/shard_map/convert_element_type | solution.py:1085
  820.5 3.4 multiply_subtract_fusion.2
  828.3 4.8 multiply_subtract_fusion
  833.1 3.3 multiply_subtract_fusion.1
  (410 shorter events, 193.5 us)
Async XLA Ops:
  7.2 77.5 %all-gather.8.cloned.1.call-start = ((), (), s32[]{:S(2)}) async-start(), calls=%async_computation.3 | async-start | bytes 10985472 | tf_op jit(solution)/shard_map/all_gather | solution.py:893
  11.9 218.7 %all-gather.10.cloned.1.call-start = ((), (), s32[]{:S(2)}) async-start(), calls=%async_computation.4 | async-start | bytes 28311552 | tf_op jit(solution)/shard_map/all_gather | solution.py:900
  12.1 1.3 collective-permute-start.6
  13.5 4.7 collective-permute-start.7
  18.2 7.8 collective-permute-start.8
  20.4 60.6 %copy-start.51 = (bf16[256,1536]{1,0:T(8,128)(2,1)}, bf16[256,1536]{1,0:T(8,128)(2,1)S(1)}, u32[]{:S(2)}) copy-start(bf16[256,1536]{1,0:T(8,128)(2,1)S(1)} %convert_element_type.288) | copy-start | bytes 2359300
  20.4 60.6 %collective-permute-start.5 = (bf16[256,1536]{1,0:T(8,128)(2,1)S(1)}, bf16[256,1536]{1,0:T(8,128)(2,1)S(1)}, u32[]{:S(2)}, u32[]{:S(2)}) collective-permute-start(bf16[256,1536]{1,0:T(8,128)(2,1)S(1)} %convert_element_type.288), channel_id=1, source_target_pairs={{0,1},{1,2},{2,3},{3,0},{4,5},{5,6},{6,7},{7,4},{8,9},{9,10},{10,1... | collective-permute-start | bytes 2359304 | tf_op jit(solution)/shard_map/ppermute | solution.py:341
  22.0 59.0 %collective-permute-start.4 = (bf16[256,1536]{1,0:T(8,128)(2,1)S(1)}, bf16[256,1536]{1,0:T(8,128)(2,1)S(1)}, u32[]{:S(2)}, u32[]{:S(2)}) collective-permute-start(bf16[256,1536]{1,0:T(8,128)(2,1)S(1)} %convert_element_type.288), channel_id=1, source_target_pairs={{0,2},{1,3},{2,0},{3,1},{4,6},{5,7},{6,4},{7,5},{8,10},{9,11},{10,... | collective-permute-start | bytes 2359304 | tf_op jit(solution)/shard_map/ppermute | solution.py:341
  24.6 58.1 %collective-permute-start.3 = (bf16[256,1536]{1,0:T(8,128)(2,1)S(1)}, bf16[256,1536]{1,0:T(8,128)(2,1)}, u32[]{:S(2)}, u32[]{:S(2)}) collective-permute-start(bf16[256,1536]{1,0:T(8,128)(2,1)S(1)} %convert_element_type.288), channel_id=1, source_target_pairs={{0,3},{1,0},{2,1},{3,2},{4,7},{5,4},{6,5},{7,6},{8,11},{9,8},{10,9... | collective-permute-start | bytes 2359304 | tf_op jit(solution)/shard_map/ppermute | solution.py:341
  89.1 21.9 %collective-permute-start.11 = (bf16[1792,128]{1,0:T(8,128)(2,1)S(1)}, bf16[1792,128]{1,0:T(8,128)(2,1)S(1)}, u32[]{:S(2)}, u32[]{:S(2)}) collective-permute-start(bf16[1792,128]{1,0:T(8,128)(2,1)S(1)} %get-tuple-element.242), channel_id=1, source_target_pairs={{0,3},{1,0},{2,1},{3,2},{4,7},{5,4},{6,5},{7,6},{8,11},{9,8},{10,9... | collective-permute-start | bytes 1376264 | tf_op jit(solution)/shard_map/ppermute | solution.py:373
  100.0 39.6 %collective-permute-start.10 = (bf16[1792,128]{1,0:T(8,128)(2,1)S(1)}, bf16[1792,128]{1,0:T(8,128)(2,1)S(1)}, u32[]{:S(2)}, u32[]{:S(2)}) collective-permute-start(bf16[1792,128]{1,0:T(8,128)(2,1)S(1)} %get-tuple-element.243), channel_id=1, source_target_pairs={{0,2},{1,3},{2,0},{3,1},{4,6},{5,7},{6,4},{7,5},{8,10},{9,11},{10,... | collective-permute-start | bytes 1376264 | tf_op jit(solution)/shard_map/ppermute | solution.py:373
  100.0 39.6 %collective-permute-start.9 = (bf16[1792,128]{1,0:T(8,128)(2,1)S(1)}, bf16[1792,128]{1,0:T(8,128)(2,1)S(1)}, u32[]{:S(2)}, u32[]{:S(2)}) collective-permute-start(bf16[1792,128]{1,0:T(8,128)(2,1)S(1)} %get-tuple-element.244), channel_id=1, source_target_pairs={{0,1},{1,2},{2,3},{3,0},{4,5},{5,6},{6,7},{7,4},{8,9},{9,10},{10,1... | collective-permute-start | bytes 1376264 | tf_op jit(solution)/shard_map/ppermute | solution.py:373
  149.7 44.1 %all-to-all-start = ((bf16[8,512,128]{2,1,0:T(8,128)(2,1)}), bf16[8,512,128]{2,1,0:T(8,128)(2,1)S(1)}, u32[]{:S(2)}, u32[]{:S(2)}) async-start(bf16[8,512,128]{2,1,0:T(8,128)(2,1)} %bitcast.190), calls=%async_computation | async-start | bytes 2097152 | tf_op jit(solution)/shard_map/all_to_all | solution.py:910
  153.2 147.7 %all-gather.12.cloned.1.call-start = ((), (), s32[]{:S(2)}) async-start(), calls=%async_computation.5 | async-start | bytes 6598656 | tf_op jit(solution)/shard_map/all_gather | solution.py:933
  153.9 3.7 collective-permute-start.12
  154.2 29.7 %collective-permute-start.15 = (s32[1,592]{1,0:T(1,128)S(1)}, s32[1,592]{1,0:T(1,128)S(1)}, u32[]{:S(2)}, u32[]{:S(2)}) collective-permute-start(s32[1,592]{1,0:T(1,128)S(1)} %pad_add_fusion.3), channel_id=1, source_target_pairs={{0,0},{1,4},{2,1},{3,5},{4,2},{5,6},{6,3},{7,7},{8,8},{9,12},{10,9... | collective-permute-start | bytes 7112 | tf_op jit(solution)/shard_map/ppermute | solution.py:495
  158.9 20.2 %collective-permute-start.13 = (f32[]{:T(128)}, f32[]{:T(128)}, u32[]{:S(2)}, u32[]{:S(2)}) collective-permute-start(f32[]{:T(128)} %add.643), channel_id=1, source_target_pairs={{0,8},{4,12},{8,0},{12,4},{16,24},{20,28},{24,16},{28,20},{1,9},{5... | collective-permute-start | bytes 20 | tf_op jit(solution)/shard_map/ppermute | solution.py:331
  179.7 3.6 collective-permute-start.14
  230.6 413.3 %reduce-scatter.2.cloned.1.call-start = ((), (), s32[]{:S(2)}) async-start(), calls=%async_computation.6 | async-start | bytes 17584128 | tf_op jit(solution)/shard_map/reduce_scatter | solution.py:969
  255.0 171.1 %copy-start.10 = (bf16[512,1024]{1,0:T(8,128)(2,1)}, bf16[512,1024]{1,0:T(8,128)(2,1)S(1)}, u32[]{:S(2)}) copy-start(bf16[512,1024]{1,0:T(8,128)(2,1)S(1)} %fusion.22.fin_ref.refs_0_) | copy-start | bytes 3145732
  284.8 12.4 %collective-permute-start.17 = (bf16[80,1024]{1,0:T(8,128)(2,1)}, bf16[80,1024]{1,0:T(8,128)(2,1)}, u32[]{:S(2)}, u32[]{:S(2)}) collective-permute-start(bf16[80,1024]{1,0:T(8,128)(2,1)} %get-tuple-element.214), channel_id=1, source_target_pairs={{0,2},{1,3},{2,0},{3,1},{4,6},{5,7},{6,4},{7,5},{8,10},{9,11},{10,... | collective-permute-start | bytes 491528 | tf_op jit(solution)/shard_map/ppermute | solution.py:341
  287.1 8.6 %collective-permute-start.16 = (bf16[80,1024]{1,0:T(8,128)(2,1)}, bf16[80,1024]{1,0:T(8,128)(2,1)}, u32[]{:S(2)}, u32[]{:S(2)}) collective-permute-start(bf16[80,1024]{1,0:T(8,128)(2,1)} %get-tuple-element.214), channel_id=1, source_target_pairs={{0,3},{1,0},{2,1},{3,2},{4,7},{5,4},{6,5},{7,6},{8,11},{9,8},{10,9... | collective-permute-start | bytes 491528 | tf_op jit(solution)/shard_map/ppermute | solution.py:341
  288.7 11.5 %collective-permute-start.18 = (bf16[80,1024]{1,0:T(8,128)(2,1)}, bf16[80,1024]{1,0:T(8,128)(2,1)S(1)}, u32[]{:S(2)}, u32[]{:S(2)}) collective-permute-start(bf16[80,1024]{1,0:T(8,128)(2,1)} %get-tuple-element.214), channel_id=1, source_target_pairs={{0,1},{1,2},{2,3},{3,0},{4,5},{5,6},{6,7},{7,4},{8,9},{9,10},{10,1... | collective-permute-start | bytes 491528 | tf_op jit(solution)/shard_map/ppermute | solution.py:341
  318.6 10.3 %collective-permute-start.20 = (f32[1,3,320]{2,1,0:T(4,128)S(1)}, f32[1,3,320]{2,1,0:T(4,128)S(1)}, u32[]{:S(2)}, u32[]{:S(2)}) collective-permute-start(f32[1,3,320]{2,1,0:T(4,128)S(1)} %maximum_bitcast_fusion), channel_id=1, source_target_pairs={{0,2},{1,3},{2,0},{3,1},{4,6},{5,7},{6,4},{7,5},{8,10},{9,11},{10,... | collective-permute-start | bytes 11528 | tf_op jit(solution)/shard_map/ppermute | solution.py:341
  324.2 4.7 collective-permute-start.19
  327.6 5.4 collective-permute-start.21
  344.4 22.2 %collective-permute-start.22 = (bf16[80,1024]{1,0:T(8,128)(2,1)}, bf16[80,1024]{1,0:T(8,128)(2,1)}, u32[]{:S(2)}, u32[]{:S(2)}) collective-permute-start(bf16[80,1024]{1,0:T(8,128)(2,1)} %get-tuple-element.250), channel_id=1, source_target_pairs={{0,1},{1,2},{2,3},{3,0},{4,5},{5,6},{6,7},{7,4},{8,9},{9,10},{10,1... | collective-permute-start | bytes 491528 | tf_op jit(solution)/shard_map/ppermute | solution.py:360
  344.4 22.2 %collective-permute-start.24 = (bf16[80,1024]{1,0:T(8,128)(2,1)}, bf16[80,1024]{1,0:T(8,128)(2,1)}, u32[]{:S(2)}, u32[]{:S(2)}) collective-permute-start(bf16[80,1024]{1,0:T(8,128)(2,1)} %get-tuple-element.251), channel_id=1, source_target_pairs={{0,3},{1,0},{2,1},{3,2},{4,7},{5,4},{6,5},{7,6},{8,11},{9,8},{10,9... | collective-permute-start | bytes 491528 | tf_op jit(solution)/shard_map/ppermute | solution.py:360
  348.7 17.9 %collective-permute-start.23 = (bf16[80,1024]{1,0:T(8,128)(2,1)}, bf16[80,1024]{1,0:T(8,128)(2,1)}, u32[]{:S(2)}, u32[]{:S(2)}) collective-permute-start(bf16[80,1024]{1,0:T(8,128)(2,1)} %get-tuple-element.252), channel_id=1, source_target_pairs={{0,2},{1,3},{2,0},{3,1},{4,6},{5,7},{6,4},{7,5},{8,10},{9,11},{10,... | collective-permute-start | bytes 491528 | tf_op jit(solution)/shard_map/ppermute | solution.py:360
  386.3 10.5 %collective-permute-start.25 = (bf16[256,4096]{1,0:T(8,128)(2,1)}, bf16[256,4096]{1,0:T(8,128)(2,1)}, u32[]{:S(2)}, u32[]{:S(2)}) collective-permute-start(bf16[256,4096]{1,0:T(8,128)(2,1)} %gradient_block.12), channel_id=1, source_target_pairs={{0,4},{4,0},{8,12},{12,8},{16,20},{20,16},{24,28},{28,24},{1,5},{5... | collective-permute-start | bytes 6291464 | tf_op jit(solution)/shard_map/ppermute | solution.py:432
  386.4 10.5 %collective-permute-start.26 = (bf16[256,4096]{1,0:T(8,128)(2,1)}, bf16[256,4096]{1,0:T(8,128)(2,1)}, u32[]{:S(2)}, u32[]{:S(2)}) collective-permute-start(bf16[256,4096]{1,0:T(8,128)(2,1)} %gradient_block.13), channel_id=1, source_target_pairs={{0,4},{4,0},{8,12},{12,8},{16,20},{20,16},{24,28},{28,24},{1,5},{5... | collective-permute-start | bytes 6291464 | tf_op jit(solution)/shard_map/ppermute | solution.py:433
  407.0 19.0 %collective-permute-start.27 = (bf16[256,4096]{1,0:T(8,128)(2,1)}, bf16[256,4096]{1,0:T(8,128)(2,1)S(1)}, u32[]{:S(2)}, u32[]{:S(2)}) collective-permute-start(bf16[256,4096]{1,0:T(8,128)(2,1)} %gradient_block.15), channel_id=1, source_target_pairs={{0,4},{4,0},{8,12},{12,8},{16,20},{20,16},{24,28},{28,24},{1,5},{5... | collective-permute-start | bytes 6291464 | tf_op jit(solution)/shard_map/ppermute | solution.py:432
  407.0 19.0 %collective-permute-start.28 = (bf16[256,4096]{1,0:T(8,128)(2,1)S(1)}, bf16[256,4096]{1,0:T(8,128)(2,1)S(1)}, u32[]{:S(2)}, u32[]{:S(2)}) collective-permute-start(bf16[256,4096]{1,0:T(8,128)(2,1)S(1)} %gradient_block.16), channel_id=1, source_target_pairs={{0,4},{4,0},{8,12},{12,8},{16,20},{20,16},{24,28},{28,24},{1,5},{5... | collective-permute-start | bytes 6291464 | tf_op jit(solution)/shard_map/ppermute | solution.py:433
  407.5 47.5 %collective-permute-start.29 = (bf16[256,4096]{1,0:T(8,128)(2,1)S(1)}, bf16[256,4096]{1,0:T(8,128)(2,1)S(1)}, u32[]{:S(2)}, u32[]{:S(2)}) collective-permute-start(bf16[256,4096]{1,0:T(8,128)(2,1)S(1)} %gradient_block.14), channel_id=1, source_target_pairs={{0,1},{1,0},{2,3},{3,2},{4,5},{5,4},{6,7},{7,6},{8,9},{9,8},{10,11... | collective-permute-start | bytes 6291464 | tf_op jit(solution)/shard_map/ppermute | solution.py:448
  458.4 12.3 %collective-permute-start.30 = (bf16[256,4096]{1,0:T(8,128)(2,1)}, bf16[256,4096]{1,0:T(8,128)(2,1)}, u32[]{:S(2)}, u32[]{:S(2)}) collective-permute-start(bf16[256,4096]{1,0:T(8,128)(2,1)} %gradient_block.18), channel_id=1, source_target_pairs={{0,4},{4,0},{8,12},{12,8},{16,20},{20,16},{24,28},{28,24},{1,5},{5... | collective-permute-start | bytes 6291464 | tf_op jit(solution)/shard_map/ppermute | solution.py:432
  458.4 71.2 %collective-permute-start.31 = (bf16[256,4096]{1,0:T(8,128)(2,1)}, bf16[256,4096]{1,0:T(8,128)(2,1)}, u32[]{:S(2)}, u32[]{:S(2)}) collective-permute-start(bf16[256,4096]{1,0:T(8,128)(2,1)} %gradient_block.17), channel_id=1, source_target_pairs={{0,1},{1,0},{2,3},{3,2},{4,5},{5,4},{6,7},{7,6},{8,9},{9,8},{10,11... | collective-permute-start | bytes 6291464 | tf_op jit(solution)/shard_map/ppermute | solution.py:448
  468.8 82.4 %collective-permute-start.37 = (bf16[256,4096]{1,0:T(8,128)(2,1)}, bf16[256,4096]{1,0:T(8,128)(2,1)}, u32[]{:S(2)}, u32[]{:S(2)}) collective-permute-start(bf16[256,4096]{1,0:T(8,128)(2,1)} %gradient_block.21.total_ref), channel_id=1, source_target_pairs={{2,4},{3,5},{4,2},{5,3},{10,12},{11,13},{12,10},{13,11},{18,20},{1... | collective-permute-start | bytes 6291464 | tf_op jit(solution)/shard_map/ppermute | solution.py:472
  475.5 121.2 %collective-permute-start.36 = (bf16[256,4096]{1,0:T(8,128)(2,1)}, bf16[256,4096]{1,0:T(8,128)(2,1)}, u32[]{:S(2)}, u32[]{:S(2)}) collective-permute-start(bf16[256,4096]{1,0:T(8,128)(2,1)} %gradient_block.19), channel_id=1, source_target_pairs={{0,1},{1,0},{2,3},{3,2},{4,5},{5,4},{6,7},{7,6},{8,9},{9,8},{10,11... | collective-permute-start | bytes 6291464 | tf_op jit(solution)/shard_map/ppermute | solution.py:448
  480.5 116.1 %collective-permute-start.35 = (bf16[256,4096]{1,0:T(8,128)(2,1)}, bf16[256,4096]{1,0:T(8,128)(2,1)}, u32[]{:S(2)}, u32[]{:S(2)}) collective-permute-start(bf16[256,4096]{1,0:T(8,128)(2,1)} %gradient_block.20), channel_id=1, source_target_pairs={{0,4},{4,0},{8,12},{12,8},{16,20},{20,16},{24,28},{28,24},{1,5},{5... | collective-permute-start | bytes 6291464 | tf_op jit(solution)/shard_map/ppermute | solution.py:433
  538.6 65.7 %collective-permute-start.32 = (bf16[528,512]{1,0:T(8,128)(2,1)}, bf16[528,512]{1,0:T(8,128)(2,1)}, u32[]{:S(2)}, u32[]{:S(2)}) collective-permute-start(bf16[528,512]{1,0:T(8,128)(2,1)} %dynamic-slice_convert_fusion), channel_id=1, source_target_pairs={{0,16},{4,20},{8,24},{12,28},{16,0},{20,4},{24,8},{28,12},{1,17},{... | collective-permute-start | bytes 1622024 | tf_op jit(solution)/shard_map/ppermute | solution.py:853
  544.0 52.7 %copy-start.15 = (bf16[512,1024]{1,0:T(8,128)(2,1)S(1)}, bf16[512,1024]{1,0:T(8,128)(2,1)}, u32[]{:S(2)}) copy-start(bf16[512,1024]{1,0:T(8,128)(2,1)} %copy-done.12) | copy-start | bytes 3145732
  544.0 52.7 %copy-start.18 = (bf16[512,1024]{1,0:T(8,128)(2,1)S(1)}, bf16[512,1024]{1,0:T(8,128)(2,1)}, u32[]{:S(2)}) copy-start(bf16[512,1024]{1,0:T(8,128)(2,1)} %copy-done.16) | copy-start | bytes 3145732
  544.0 52.7 %copy-start.26 = (bf16[512,1024]{1,0:T(8,128)(2,1)S(1)}, bf16[512,1024]{1,0:T(8,128)(2,1)}, u32[]{:S(2)}) copy-start(bf16[512,1024]{1,0:T(8,128)(2,1)} %copy-done.23) | copy-start | bytes 3145732
  549.0 55.3 %copy-start.49 = (f32[528,1024]{1,0:T(8,128)S(1)}, f32[528,1024]{1,0:T(8,128)}, u32[]{:S(2)}) copy-start(f32[528,1024]{1,0:T(8,128)} %concatenate.84) | copy-start | bytes 6488068
  549.1 78.2 %collective-permute-start.39 = (bf16[256,4096]{1,0:T(8,128)(2,1)}, bf16[256,4096]{1,0:T(8,128)(2,1)}, u32[]{:S(2)}, u32[]{:S(2)}) collective-permute-start(bf16[256,4096]{1,0:T(8,128)(2,1)} %gradient_block.23.total_ref), channel_id=1, source_target_pairs={{2,4},{3,5},{4,2},{5,3},{10,12},{11,13},{12,10},{13,11},{18,20},{1... | collective-permute-start | bytes 6291464 | tf_op jit(solution)/shard_map/ppermute | solution.py:472
  601.8 42.1 %collective-permute-start.38 = (bf16[256,4096]{1,0:T(8,128)(2,1)}, bf16[256,4096]{1,0:T(8,128)(2,1)}, u32[]{:S(2)}, u32[]{:S(2)}) collective-permute-start(bf16[256,4096]{1,0:T(8,128)(2,1)} %gradient_block.22.total_ref), channel_id=1, source_target_pairs={{2,4},{3,5},{4,2},{5,3},{10,12},{11,13},{12,10},{13,11},{18,20},{1... | collective-permute-start | bytes 6291464 | tf_op jit(solution)/shard_map/ppermute | solution.py:472
  605.7 8.1 collective-permute-start.33
  607.2 18.9 %all-to-all-start.1 = ((bf16[8,512,128]{2,1,0:T(8,128)(2,1)}), bf16[8,512,128]{2,1,0:T(8,128)(2,1)S(1)}, u32[]{:S(2)}, u32[]{:S(2)}) async-start(bf16[8,512,128]{2,1,0:T(8,128)(2,1)} %bitcast_bitcast_fusion), calls=%async_computation.1 | async-start | bytes 2097152 | tf_op jit(solution)/shard_map/all_to_all | solution.py:985
  610.8 130.5 %all-gather.18.cloned.1.call-start = ((), (), s32[]{:S(2)}) async-start(), calls=%async_computation.9 | async-start | bytes 5918720 | tf_op jit(solution)/shard_map/all_gather | solution.py:995
  613.9 1.4 collective-permute-start.34
  644.0 141.0 %all-gather.14.cloned.1.call-start = ((), (), s32[]{:S(2)}) async-start(), calls=%async_computation.7 | async-start | bytes 7077888 | tf_op jit(solution)/shard_map/all_gather | solution.py:1059
  676.6 13.5 %collective-permute-start.40 = (bf16[4,256,1536]{2,1,0:T(8,128)(2,1)}, bf16[4,256,1536]{2,1,0:T(8,128)(2,1)S(1)}, u32[]{:S(2)}, u32[]{:S(2)}) collective-permute-start(bf16[4,256,1536]{2,1,0:T(8,128)(2,1)} %get-tuple-element.156), channel_id=1, source_target_pairs={{0,4},{4,0},{8,12},{12,8},{16,20},{20,16},{24,28},{28,24},{1,5},{5... | collective-permute-start | bytes 9437192 | tf_op jit(solution)/shard_map/ppermute | solution.py:826
  694.9 12.0 %collective-permute-start.42 = (bf16[128,1536]{1,0:T(8,128)(2,1)S(1)}, bf16[128,1536]{1,0:T(8,128)(2,1)S(1)}, u32[]{:S(2)}, u32[]{:S(2)}) collective-permute-start(bf16[128,1536]{1,0:T(8,128)(2,1)S(1)} %get-tuple-element.228), channel_id=1, source_target_pairs={{0,8},{4,12},{8,0},{12,4},{16,24},{20,28},{24,16},{28,20},{1,9},{5... | collective-permute-start | bytes 1179656 | tf_op jit(solution)/shard_map/ppermute | solution.py:826
  695.1 19.7 %collective-permute-start.41 = (bf16[128,1536]{1,0:T(8,128)(2,1)}, bf16[128,1536]{1,0:T(8,128)(2,1)S(1)}, u32[]{:S(2)}, u32[]{:S(2)}) collective-permute-start(bf16[128,1536]{1,0:T(8,128)(2,1)} %get-tuple-element.225), channel_id=1, source_target_pairs={{0,8},{4,12},{8,0},{12,4},{16,24},{20,28},{24,16},{28,20},{1,9},{5... | collective-permute-start | bytes 1179656 | tf_op jit(solution)/shard_map/ppermute | solution.py:826
  697.0 17.8 %collective-permute-start.45 = (bf16[128,1536]{1,0:T(8,128)(2,1)}, bf16[128,1536]{1,0:T(8,128)(2,1)}, u32[]{:S(2)}, u32[]{:S(2)}) collective-permute-start(bf16[128,1536]{1,0:T(8,128)(2,1)} %get-tuple-element.226), channel_id=1, source_target_pairs={{0,16},{4,20},{8,24},{12,28},{16,0},{20,4},{24,8},{28,12},{1,17},{... | collective-permute-start | bytes 1179656 | tf_op jit(solution)/shard_map/ppermute | solution.py:826
  708.8 12.4 %collective-permute-start.43 = (bf16[128,1536]{1,0:T(8,128)(2,1)}, bf16[128,1536]{1,0:T(8,128)(2,1)}, u32[]{:S(2)}, u32[]{:S(2)}) collective-permute-start(bf16[128,1536]{1,0:T(8,128)(2,1)} %fusion.40), channel_id=1, source_target_pairs={{0,16},{4,20},{8,24},{12,28},{16,0},{20,4},{24,8},{28,12},{1,17},{... | collective-permute-start | bytes 1179656 | tf_op jit(solution)/shard_map/ppermute | solution.py:826
  708.8 18.7 %collective-permute-start.44 = (bf16[128,1536]{1,0:T(8,128)(2,1)}, bf16[128,1536]{1,0:T(8,128)(2,1)S(1)}, u32[]{:S(2)}, u32[]{:S(2)}) collective-permute-start(bf16[128,1536]{1,0:T(8,128)(2,1)} %get-tuple-element.227), channel_id=1, source_target_pairs={{0,16},{4,20},{8,24},{12,28},{16,0},{20,4},{24,8},{28,12},{1,17},{... | collective-permute-start | bytes 1179656 | tf_op jit(solution)/shard_map/ppermute | solution.py:826
  722.9 7.8 collective-permute-start.46
  739.7 75.6 %all-gather.16.cloned.1.call-start = ((), (), s32[]{:S(2)}) async-start(), calls=%async_computation.8 | async-start | bytes 1216512 | tf_op jit(solution)/shard_map/all_gather | solution.py:1062
  790.9 9.3 %collective-permute-start.47 = (f32[12]{0:T(128)S(1)}, f32[12]{0:T(128)S(1)}, u32[]{:S(2)}, u32[]{:S(2)}) collective-permute-start(f32[12]{0:T(128)S(1)} %concatenate.87), channel_id=1, source_target_pairs={{0,4},{4,0},{8,12},{12,8},{16,20},{20,16},{24,28},{28,24},{1,5},{5... | collective-permute-start | bytes 152 | tf_op jit(solution)/shard_map/ppermute | solution.py:331
  800.2 3.5 collective-permute-start.48
  803.8 3.5 collective-permute-start.49
  807.3 3.5 collective-permute-start.50
  810.9 4.4 collective-permute-start.51
  (69 other events, 619.7 us)
Sparse Core Ops, SparseCore 0:
  12.1 64.7 all-gather.7
  86.4 144.1 all-gather.9
  233.1 43.8 all-gather.11
  368.8 111.5 reduce-scatter.1
  644.1 94.2 all-gather.17
  740.9 43.9 all-gather.13
  787.6 23.7 all-gather.15

commit v15 on v14

--- a/solution.py
+++ b/solution.py
@@ -1063,15 +1063,22 @@
     if not paired:
         _, small_upd = small_update(small_grad, small_m, small_v, small)
         small_norm = jnp.where((wide_me == 0) & (narrow_me == 0), jnp.sum(small_upd * small_upd), 0.0)
-    parts = jnp.concatenate([wsq, usq, *table_norms, jnp.sum(own_loss)[None], small_norm[None]])
+    alone = (wide_me == 0) & (narrow_me == 0)
+    none = jnp.zeros((1,), jnp.float32)
+    loss_part, small_part = jnp.sum(own_loss)[None], jnp.where(alone, small_square, 0.0)
+    parts = jnp.stack(
+        [
+            jnp.concatenate([wsq, table_norms[0], small_part, loss_part, none]),
+            jnp.concatenate([usq, table_norms[1], small_norm[None], none, none]),
+        ]
+    )
     sums = summed_over(summed_over(parts, "wide"), "narrow")
     if paired:
         sums, small_grad = together(sums, small_grad)
     small_mom, small_upd = small_update(small_grad, small_m, small_v, small)
-    loss_sum = sums[10]
-    wnorm = jnp.sqrt(jnp.concatenate([sums[0:4], sums[8:9], small_square]))
-    unorm = jnp.sqrt(jnp.concatenate([sums[4:8], sums[9:10], sums[11:12]]))
-    ratio = wnorm / unorm
+    loss_sum = sums[0, 6]
+    norms = jnp.sqrt(sums[:, 0:6])
+    ratio = norms[0] / norms[1]
     new_layer = layer - RATE * jnp.sum(onehot * ratio[None, 0:4], axis=1)[None] * layer_upd
     new_table = table - RATE * ratio[4] * table_upd
     new_small = small - RATE * ratio[5] * small_upd
@@ -1085,7 +1092,7 @@
         new_m.astype(jnp.float32),
         new_worker,
         new_server,
-        jnp.stack([wnorm, unorm]),
+        norms,
     )
 
 

time: 852 us -> 845 us (level)
    unnamed x156 -> x158, local copies, waits for them, and re-layouts: 33.3 us -> 33.2 us
where the time goes in v15:
time: 845 us; the launch traced here: 837 us
  Pallas kernels  233 us (28%)
  waiting for transfers between devices  229 us (27%)
  starting transfers between devices  103 us (12%)
  other arithmetic  86.4 us (10%)
  matrix products  79.6 us (9%)
  local copies, waits for them, and re-layouts  78.6 us (9%)
  between operations  24.3 us (3%)
    ppermute x3, waiting for transfers between devices, across(): self.away = lax.ppermute(away, 'narrow', sides)  83.7 us
    pallas_call x1, Pallas kernels, packed_rows(): pl.pallas_call(pack_kernel, grid_spec=pltpu.PrefetchScalarGridSpec(num_sc...  52.4 us
    pallas_call x12, Pallas kernels, gradient_block(): pl.pallas_call(functools.partial(block_kernel, steps), grid_spec=pltpu.Pr...  47 us
    ppermute x3, waiting for transfers between devices, sent_around(): lax.ppermute(block(by), 'narrow', cycle(size, by))  38.9 us
    ppermute x7, waiting for transfers between devices, send(): lax.ppermute(value.astype(jnp.bfloat16), 'wide', swap_pairs(n_wide, bit))  33.5 us
    unnamed x158, local copies, waits for them, and re-layouts  33.2 us
    dot_general x4, matrix products, matmul_nt(): lax.dot_general(left, right, (((1,), (1,)), ((), ())), preferred_element_...  32.9 us
    all_gather x1, waiting for transfers between devices, shards(): weights = lax.all_gather(layer_rows, 'wide', axis=1, tiled=True)  30.9 us
  transfers between devices with their start and end apart: 58, of which 28 were waited for; matrix products, arithmetic and copies ran while one was open for 20% of the time, Pallas kernels for 28%

profile of v15, /device:TPU:0, one launch (start us, length us, event | category | flops | bytes accessed | tf_op | source)
XLA Modules:
  0.0 837.5 jit_solution(7437530764463968772)
XLA Ops:
  28.5 52.4 %pack_rows.1 = bf16[4,4096,128]{2,1,0:T(8,128)(2,1)} custom-call(s32[16384]{0:T(1024)S(1)} %fusion.59.ids_ref, f32[7632,128]{1,0:T(8,128)S(1)} %copy-done.8), custom_call_target="tpu_custom_call" | custom-call | tf_op jit(solution)/shard_map/pack_rows/pallas_call | solution.py:569
  89.1 10.9 %collective-permute-start.11 = (bf16[1792,128]{1,0:T(8,128)(2,1)S(1)}, bf16[1792,128]{1,0:T(8,128)(2,1)S(1)}, u32[]{:S(2)}, u32[]{:S(2)}) collective-permute-start(bf16[1792,128]{1,0:T(8,128)(2,1)S(1)} %get-tuple-element.242), channel_id=1, source_target_pairs={{0,3},{1,0},{2,1},{3,2},{4,7},{5,4},{6,5},{7,6},{8,11},{9,8},{10,9... | collective-permute-start | bytes 1376264 | tf_op jit(solution)/shard_map/ppermute | solution.py:373
  100.7 10.3 %collective-permute-done.11 = bf16[1792,128]{1,0:T(8,128)(2,1)S(1)} collective-permute-done((bf16[1792,128]{1,0:T(8,128)(2,1)S(1)}, bf16[1792,128]{1,0:T(8,128)(2,1)S(1)}, u32[]{:S(2)}, u32[]{:S(2)}) %collective-permute-start.11) | collective-permute-done | bytes 458784 | tf_op jit(solution)/shard_map/ppermute | solution.py:373
  111.0 28.5 %collective-permute-done.10 = bf16[1792,128]{1,0:T(8,128)(2,1)S(1)} collective-permute-done((bf16[1792,128]{1,0:T(8,128)(2,1)S(1)}, bf16[1792,128]{1,0:T(8,128)(2,1)S(1)}, u32[]{:S(2)}, u32[]{:S(2)}) %collective-permute-start.10) | collective-permute-done | bytes 458784 | tf_op jit(solution)/shard_map/ppermute | solution.py:373
  139.7 5.5 take_rows.3
  145.2 3.5 conditional.1
  149.7 3.6 all-to-all-start
  158.9 18.1 %collective-permute-start.13 = (f32[]{:T(128)}, f32[]{:T(128)}, u32[]{:S(2)}, u32[]{:S(2)}) collective-permute-start(f32[]{:T(128)} %add.643), channel_id=1, source_target_pairs={{0,8},{4,12},{8,0},{12,4},{16,24},{20,28},{24,16},{28,20},{1,9},{5... | collective-permute-start | bytes 20 | tf_op jit(solution)/shard_map/ppermute | solution.py:331
  184.0 9.8 %dynamic_update_slice.46 = bf16[7632,1024]{1,0:T(8,128)(2,1)} pad(bf16[4768,1024]{1,0:T(8,128)(2,1)} %all-gather.8.cloned.1.call-done, bf16[]{:T(256)} %constant.264.clone.1), padding=0_2864x0_0 | pad | bytes 25395202 | tf_op jit(solution)/shard_map/dynamic_update_slice | solution.py:929
  199.7 30.9 %all-gather.10.cloned.1.call-done.weight_ref = bf16[1024,12288]{1,0:T(8,128)(2,1)} async-done(((bf16[1024,1536]{1,0:T(8,128)(2,1)}), bf16[1024,12288]{1,0:T(8,128)(2,1)}) %all-gather.10.cloned.1.call-update) | async-done | bytes 25165840 | tf_op jit(solution)/shard_map/all_gather | solution.py:900
  232.6 6.4 add_convert_fusion.q_ref.k_ref.v_ref
  239.1 11.7 %attend.1 = (bf16[512,1024]{1,0:T(8,128)(2,1)S(1)}, f32[8,2,512]{2,1,0:T(2,128)S(1)}) custom-call(bf16[512,3072]{1,0:T(8,128)(2,1)S(1)} %add_convert_fusion.q_ref.k_ref.v_ref, bf16[512,3072]{1,0:T(8,128)(2,1)S(1)} %add_convert_fusion.q_ref.k_ref.v_ref, bf16[512,3072]{1,0:T(8,128)(2,1)S(1)} %add_convert_fusion.q_ref.k_ref.v_ref, ...), custom_call_target="tpu_custom_call" | custom-call | tf_op jit(solution)/shard_map/attend/pallas_call | solution.py:82
  250.8 3.4 fusion.92
  255.0 11.3 %ffn_up.1 = (bf16[512,4096]{1,0:T(8,128)(2,1)S(1)}, bf16[512,4096]{1,0:T(8,128)(2,1)S(1)}) custom-call(bf16[512,1024]{1,0:T(8,128)(2,1)S(1)} %fusion.22.fin_ref.refs_0_, bf16[1024,12288]{1,0:T(8,128)(2,1)} %all-gather.10.cloned.1.call-done.weight_ref, f32[1,4096]{1,0:T(1,128)S(1)} %bitcast.180), custom_call_target="tpu_custom_call" | custom-call | flops 4294967296 | tf_op jit(solution)/shard_map/ffn_up/pallas_call | solution.py:231
  268.3 9.2 %fusion.93 = (f32[512]{0:T(512)S(1)}, f32[512,1024]{1,0:T(8,128)S(1)}) fusion(f32[1024]{0:T(1024)S(1)} %bitcast.225, bf16[512,4096]{1,0:T(8,128)(2,1)S(1)} %get-tuple-element.113.refs_1_, bf16[1024,12288]{1,0:T(8,128)(2,1)} %all-gather.10.cloned.1.call-done.weight_ref, f32[1024]{0:T(1024)S(1)} %bitcast.213, f32[1024]{0:T(1024)S(1)} %bitcast.207, ...), kind=kOutput, calls=%fused_computation.262 | convolution fusion | flops 4298636800 | bytes 16795648 | tf_op jit(solution)/shard_map/dot_general | solution.py:55
  289.5 6.1 collective-permute-done.16
  300.9 5.8 constant_dynamic-update-slice_fusion.4
  306.7 9.1 %fusion.94 = (f32[320]{0:T(512)S(1)}, f32[320,7632]{1,0:T(8,128)S(1)}) fusion(bf16[320,1024]{1,0:T(8,128)(2,1)} %constant_dynamic-update-slice_fusion.5, bf16[7632,1024]{1,0:T(8,128)(2,1)} %constant_dynamic-update-slice_fusion.4, pred[7632]{0:T(1024)(128)(4,1)S(1)} %broadcast_compare_fusion.1), kind=kOutput, calls=%fused_computation.263 | convolution fusion | flops 5006591488 | bytes 26063568 | tf_op jit(solution)/shard_map/dot_general | solution.py:55
  318.5 5.6 collective-permute-start.20
  324.1 3.4 collective-permute-start.19
  328.8 4.1 collective-permute-done.21
  333.6 8.9 %fusion.80 = f32[320,1024]{1,0:T(8,128)S(1)} fusion(bf16[7632,1024]{1,0:T(8,128)(2,1)} %constant_dynamic-update-slice_fusion.4, f32[320,7632]{1,0:T(8,128)S(1)} %get-tuple-element.278, f32[320]{0:T(512)S(1)} %get-tuple-element.270, f32[320]{0:T(512)S(1)} %get-tuple-element.199, s32[7632]{0:T(1024)S(1)} %iota_add_fusion, s32[320]{0:T(512)S(1)} %eq.137), kind=kOutput, calls=%fused_computation.253 | convolution fusion | flops 5016360960 | bytes 26744384 | tf_op jit(solution)/shard_map/dot_general | solution.py:45
  344.3 4.3 collective-permute-start.24
  348.6 17.8 %convert_bitcast_fusion = bf16[8,7632,128]{2,1,0:T(8,128)(2,1)} fusion(f32[320,7632]{1,0:T(8,128)} %copy-done.46, f32[320]{0:T(512)S(1)} %get-tuple-element.270, f32[320]{0:T(512)S(1)} %get-tuple-element.199, s32[7632]{0:T(1024)S(1)} %iota_add_fusion, s32[320]{0:T(512)S(1)} %eq.137, bf16[320,1024]{1,0:T(8,128)(2,1)} %constant_dynamic-update-slice_fusion.5), kind=kOutput, calls=%fused_computation.8 | convolution fusion | flops 5024176128 | bytes 26089024 | tf_op jit(solution)/shard_map/sv,swc->wvc/dot_general | solution.py:967
  379.4 3.5 gradient_block.13
  382.9 3.4 gradient_block.12
  386.8 10.0 %multiply_convert_fusion.refs_1_ = bf16[512,4096]{1,0:T(8,128)(2,1)S(1)} fusion(bf16[512,4096]{1,0:T(8,128)(2,1)} %copy-done.36, bf16[512,1024]{1,0:T(8,128)(2,1)S(1)} %get-tuple-element.205.refs_0_, bf16[1024,12288]{1,0:T(8,128)(2,1)} %all-gather.10.cloned.1.call-done.weight_ref), kind=kOutput, calls=%fused_computation.20 | convolution fusion | flops 4301258752 | bytes 17825792 | tf_op jit(solution)/shard_map/dot_general | solution.py:45
  396.8 4.3 gradient_block.14
  403.6 3.3 gradient_block.15
  407.4 11.3 %multiply_reduce_fusion.2 = (f32[1024]{0:T(1024)S(1)}, f32[512]{0:T(512)S(1)}, f32[1024]{0:T(1024)S(1)}, f32[512,1024]{1,0:T(8,128)}) fusion(f32[512,1024]{1,0:T(8,128)} %copy-done.41, f32[512]{0:T(512)S(1)} %fusion.73, f32[512]{0:T(512)S(1)} %broadcast_multiply_fusion.2, f32[1024]{0:T(1024)S(1)} %bitcast.208, ...), kind=kOutput, calls=%fused_computation.40 | convolution fusion | flops 4300207616 | bytes 18894848 | tf_op jit(solution)/shard_map/dot_general | solution.py:55
  422.7 3.3 fusion.29.do_ref
  426.0 3.5 gradient_block.17
  429.6 16.6 %attend_back.1.refs_2_.dqkv_ref = bf16[512,3072]{1,0:T(8,128)(2,1)S(1)} custom-call(bf16[512,3072]{1,0:T(8,128)(2,1)S(1)} %copy-done.1, bf16[512,3072]{1,0:T(8,128)(2,1)S(1)} %copy-done.1, bf16[512,3072]{1,0:T(8,128)(2,1)S(1)} %copy-done.1, bf16[512,1024]{1,0:T(8,128)(2,1)S(1)} %fusion.29.do_ref, f32[8,2,512]{2,1,0:T(2,128)S(1)} %get-tuple-element.125.lse_ref, ...), custom_call_target="tpu_custom_call" | custom-call | tf_op jit(solution)/shard_map/attend_back/pallas_call | solution.py:126
  446.2 8.8 %collective-permute-done.29.refs_3_ = bf16[256,4096]{1,0:T(8,128)(2,1)S(1)} collective-permute-done((bf16[256,4096]{1,0:T(8,128)(2,1)S(1)}, bf16[256,4096]{1,0:T(8,128)(2,1)S(1)}, u32[]{:S(2)}, u32[]{:S(2)}) %collective-permute-start.29) | collective-permute-done | bytes 2097184 | tf_op jit(solution)/shard_map/ppermute | solution.py:448
  455.0 3.3 gradient_block.18
  463.6 5.0 gradient_block.21.total_ref
  470.6 4.8 gradient_block.19
  477.1 3.3 gradient_block.20
  490.9 8.1 embed_back.1
  500.3 29.3 %collective-permute-done.31.refs_3_ = bf16[256,4096]{1,0:T(8,128)(2,1)} collective-permute-done((bf16[256,4096]{1,0:T(8,128)(2,1)}, bf16[256,4096]{1,0:T(8,128)(2,1)}, u32[]{:S(2)}, u32[]{:S(2)}) %collective-permute-start.31) | collective-permute-done | bytes 2097184 | tf_op jit(solution)/shard_map/ppermute | solution.py:448
  529.6 6.9 concatenate.51
  543.9 5.1 gradient_block.23.total_ref
  551.0 45.6 %collective-permute-done.36.refs_5_ = bf16[256,4096]{1,0:T(8,128)(2,1)} collective-permute-done((bf16[256,4096]{1,0:T(8,128)(2,1)}, bf16[256,4096]{1,0:T(8,128)(2,1)}, u32[]{:S(2)}, u32[]{:S(2)}) %collective-permute-start.36) | collective-permute-done | bytes 2097184 | tf_op jit(solution)/shard_map/ppermute | solution.py:448
  596.6 5.2 gradient_block.22.total_ref
  607.0 3.6 all-to-all-start.1
  615.3 10.6 %all-to-all-done.1 = bf16[8,512,128]{2,1,0:T(8,128)(2,1)S(1)} async-done(((bf16[8,512,128]{2,1,0:T(8,128)(2,1)}), bf16[8,512,128]{2,1,0:T(8,128)(2,1)S(1)}, u32[]{:S(2)}, u32[]{:S(2)}) %all-to-all-start.1) | async-done | bytes 1048608 | tf_op jit(solution)/shard_map/all_to_all | solution.py:985
  627.0 7.1 span.3
  635.4 7.1 span.4
  643.8 7.1 span.5
  654.8 21.6 %press.1 = (f32[1,256,12288]{2,1,0:T(8,128)}, bf16[4,256,1536]{2,1,0:T(8,128)(2,1)}, bf16[4,256,1536]{2,1,0:T(8,128)(2,1)}) custom-call(s32[1]{0:T(128)} %bitcast.4.core_ref, f32[2]{0:T(128)} %pad_maximum_fusion.5.scale_ref, f32[256,4096]{1,0:T(8,128)} %get-tuple-element.152.refs_0_, f32[256,4096]{1,0:T(8,128)} %get-tuple-element.153.refs_1_, ...), custom_call_target="tpu_custom_call" | custom-call | tf_op jit(solution)/shard_map/press/pallas_call | solution.py:757
  676.4 8.1 collective-permute-start.40
  684.5 5.5 collective-permute-done.40
  691.6 3.2 fusion.44
  696.9 9.9 %collective-permute-done.42 = bf16[128,1536]{1,0:T(8,128)(2,1)S(1)} collective-permute-done((bf16[128,1536]{1,0:T(8,128)(2,1)S(1)}, bf16[128,1536]{1,0:T(8,128)(2,1)S(1)}, u32[]{:S(2)}, u32[]{:S(2)}) %collective-permute-start.42) | collective-permute-done | bytes 393248 | tf_op jit(solution)/shard_map/ppermute | solution.py:826
  710.8 3.9 collective-permute-done.41
  714.7 6.4 collective-permute-done.43
  722.9 4.6 collective-permute-done.44
  734.6 5.0 fusion.53
  741.2 25.1 %add_rows.1.grad_ref = f32[7632,128]{1,0:T(8,128)} custom-call(s32[16384]{0:T(1024)} %copy-done.35, bf16[4,4624,128]{2,1,0:T(8,128)(2,1)} %bitcast.184), custom_call_target="tpu_custom_call" | custom-call | tf_op jit(solution)/shard_map/add_rows/pallas_call | solution.py:644
  766.4 12.5 %update.1 = (f32[7632,128]{1,0:T(8,128)}, f32[7632,128]{1,0:T(8,128)}, f32[1,128]{1,0:T(1,128)}, f32[1,128]{1,0:T(1,128)}) custom-call(f32[7632,128]{1,0:T(8,128)} %add_rows.1.grad_ref, bf16[7632,128]{1,0:T(8,128)(2,1)} %bitcast.189, f32[7632,128]{1,0:T(8,128)} %table_ref.3, f32[7632,128]{1,0:T(8,128)} %first_ref.1, f32[7632,128]{1,0:T(8,128)} %second_ref.1), custom_call_target="tpu_custom_call" | custom-call | tf_op jit(solution)/shard_map/update/pallas_call | solution.py:802
  806.0 9.1 %convert_element_type.368 = f32[256,12288]{1,0:T(8,128)} convert(bf16[256,12288]{1,0:T(8,128)(2,1)} %all-gather.14.cloned.1.call-done) | non-fusion elementwise | flops 3145728 | bytes 18874368 | tf_op jit(solution)/shard_map/convert_element_type | solution.py:1092
  818.9 3.4 multiply_subtract_fusion.2
  822.4 4.8 multiply_subtract_fusion
  827.1 3.3 multiply_subtract_fusion.1
  (414 shorter events, 186.5 us)
Async XLA Ops:
  7.2 77.5 %all-gather.8.cloned.1.call-start = ((), (), s32[]{:S(2)}) async-start(), calls=%async_computation.3 | async-start | bytes 10985472 | tf_op jit(solution)/shard_map/all_gather | solution.py:893
  11.9 218.7 %all-gather.10.cloned.1.call-start = ((), (), s32[]{:S(2)}) async-start(), calls=%async_computation.4 | async-start | bytes 28311552 | tf_op jit(solution)/shard_map/all_gather | solution.py:900
  12.1 1.3 collective-permute-start.6
  13.5 4.7 collective-permute-start.7
  18.2 7.8 collective-permute-start.8
  20.4 60.6 %copy-start.51 = (bf16[256,1536]{1,0:T(8,128)(2,1)}, bf16[256,1536]{1,0:T(8,128)(2,1)S(1)}, u32[]{:S(2)}) copy-start(bf16[256,1536]{1,0:T(8,128)(2,1)S(1)} %convert_element_type.288) | copy-start | bytes 2359300
  20.4 60.6 %collective-permute-start.5 = (bf16[256,1536]{1,0:T(8,128)(2,1)S(1)}, bf16[256,1536]{1,0:T(8,128)(2,1)S(1)}, u32[]{:S(2)}, u32[]{:S(2)}) collective-permute-start(bf16[256,1536]{1,0:T(8,128)(2,1)S(1)} %convert_element_type.288), channel_id=1, source_target_pairs={{0,1},{1,2},{2,3},{3,0},{4,5},{5,6},{6,7},{7,4},{8,9},{9,10},{10,1... | collective-permute-start | bytes 2359304 | tf_op jit(solution)/shard_map/ppermute | solution.py:341
  22.0 59.0 %collective-permute-start.4 = (bf16[256,1536]{1,0:T(8,128)(2,1)S(1)}, bf16[256,1536]{1,0:T(8,128)(2,1)S(1)}, u32[]{:S(2)}, u32[]{:S(2)}) collective-permute-start(bf16[256,1536]{1,0:T(8,128)(2,1)S(1)} %convert_element_type.288), channel_id=1, source_target_pairs={{0,2},{1,3},{2,0},{3,1},{4,6},{5,7},{6,4},{7,5},{8,10},{9,11},{10,... | collective-permute-start | bytes 2359304 | tf_op jit(solution)/shard_map/ppermute | solution.py:341
  24.6 58.1 %collective-permute-start.3 = (bf16[256,1536]{1,0:T(8,128)(2,1)S(1)}, bf16[256,1536]{1,0:T(8,128)(2,1)}, u32[]{:S(2)}, u32[]{:S(2)}) collective-permute-start(bf16[256,1536]{1,0:T(8,128)(2,1)S(1)} %convert_element_type.288), channel_id=1, source_target_pairs={{0,3},{1,0},{2,1},{3,2},{4,7},{5,4},{6,5},{7,6},{8,11},{9,8},{10,9... | collective-permute-start | bytes 2359304 | tf_op jit(solution)/shard_map/ppermute | solution.py:341
  89.1 21.9 %collective-permute-start.11 = (bf16[1792,128]{1,0:T(8,128)(2,1)S(1)}, bf16[1792,128]{1,0:T(8,128)(2,1)S(1)}, u32[]{:S(2)}, u32[]{:S(2)}) collective-permute-start(bf16[1792,128]{1,0:T(8,128)(2,1)S(1)} %get-tuple-element.242), channel_id=1, source_target_pairs={{0,3},{1,0},{2,1},{3,2},{4,7},{5,4},{6,5},{7,6},{8,11},{9,8},{10,9... | collective-permute-start | bytes 1376264 | tf_op jit(solution)/shard_map/ppermute | solution.py:373
  100.0 39.6 %collective-permute-start.10 = (bf16[1792,128]{1,0:T(8,128)(2,1)S(1)}, bf16[1792,128]{1,0:T(8,128)(2,1)S(1)}, u32[]{:S(2)}, u32[]{:S(2)}) collective-permute-start(bf16[1792,128]{1,0:T(8,128)(2,1)S(1)} %get-tuple-element.243), channel_id=1, source_target_pairs={{0,2},{1,3},{2,0},{3,1},{4,6},{5,7},{6,4},{7,5},{8,10},{9,11},{10,... | collective-permute-start | bytes 1376264 | tf_op jit(solution)/shard_map/ppermute | solution.py:373
  100.0 39.6 %collective-permute-start.9 = (bf16[1792,128]{1,0:T(8,128)(2,1)S(1)}, bf16[1792,128]{1,0:T(8,128)(2,1)S(1)}, u32[]{:S(2)}, u32[]{:S(2)}) collective-permute-start(bf16[1792,128]{1,0:T(8,128)(2,1)S(1)} %get-tuple-element.244), channel_id=1, source_target_pairs={{0,1},{1,2},{2,3},{3,0},{4,5},{5,6},{6,7},{7,4},{8,9},{9,10},{10,1... | collective-permute-start | bytes 1376264 | tf_op jit(solution)/shard_map/ppermute | solution.py:373
  149.7 44.2 %all-to-all-start = ((bf16[8,512,128]{2,1,0:T(8,128)(2,1)}), bf16[8,512,128]{2,1,0:T(8,128)(2,1)S(1)}, u32[]{:S(2)}, u32[]{:S(2)}) async-start(bf16[8,512,128]{2,1,0:T(8,128)(2,1)} %bitcast.188), calls=%async_computation | async-start | bytes 2097152 | tf_op jit(solution)/shard_map/all_to_all | solution.py:910
  153.2 147.7 %all-gather.12.cloned.1.call-start = ((), (), s32[]{:S(2)}) async-start(), calls=%async_computation.5 | async-start | bytes 6598656 | tf_op jit(solution)/shard_map/all_gather | solution.py:933
  153.9 3.7 collective-permute-start.12
  154.2 29.7 %collective-permute-start.15 = (s32[1,592]{1,0:T(1,128)S(1)}, s32[1,592]{1,0:T(1,128)S(1)}, u32[]{:S(2)}, u32[]{:S(2)}) collective-permute-start(s32[1,592]{1,0:T(1,128)S(1)} %pad_add_fusion.3), channel_id=1, source_target_pairs={{0,0},{1,4},{2,1},{3,5},{4,2},{5,6},{6,3},{7,7},{8,8},{9,12},{10,9... | collective-permute-start | bytes 7112 | tf_op jit(solution)/shard_map/ppermute | solution.py:495
  158.9 20.2 %collective-permute-start.13 = (f32[]{:T(128)}, f32[]{:T(128)}, u32[]{:S(2)}, u32[]{:S(2)}) collective-permute-start(f32[]{:T(128)} %add.643), channel_id=1, source_target_pairs={{0,8},{4,12},{8,0},{12,4},{16,24},{20,28},{24,16},{28,20},{1,9},{5... | collective-permute-start | bytes 20 | tf_op jit(solution)/shard_map/ppermute | solution.py:331
  179.7 3.6 collective-permute-start.14
  230.6 413.1 %reduce-scatter.2.cloned.1.call-start = ((), (), s32[]{:S(2)}) async-start(), calls=%async_computation.6 | async-start | bytes 17584128 | tf_op jit(solution)/shard_map/reduce_scatter | solution.py:969
  255.0 170.9 %copy-start.10 = (bf16[512,1024]{1,0:T(8,128)(2,1)}, bf16[512,1024]{1,0:T(8,128)(2,1)S(1)}, u32[]{:S(2)}) copy-start(bf16[512,1024]{1,0:T(8,128)(2,1)S(1)} %fusion.22.fin_ref.refs_0_) | copy-start | bytes 3145732
  284.8 12.4 %collective-permute-start.17 = (bf16[80,1024]{1,0:T(8,128)(2,1)}, bf16[80,1024]{1,0:T(8,128)(2,1)}, u32[]{:S(2)}, u32[]{:S(2)}) collective-permute-start(bf16[80,1024]{1,0:T(8,128)(2,1)} %get-tuple-element.214), channel_id=1, source_target_pairs={{0,2},{1,3},{2,0},{3,1},{4,6},{5,7},{6,4},{7,5},{8,10},{9,11},{10,... | collective-permute-start | bytes 491528 | tf_op jit(solution)/shard_map/ppermute | solution.py:341
  287.0 8.6 %collective-permute-start.16 = (bf16[80,1024]{1,0:T(8,128)(2,1)}, bf16[80,1024]{1,0:T(8,128)(2,1)}, u32[]{:S(2)}, u32[]{:S(2)}) collective-permute-start(bf16[80,1024]{1,0:T(8,128)(2,1)} %get-tuple-element.214), channel_id=1, source_target_pairs={{0,3},{1,0},{2,1},{3,2},{4,7},{5,4},{6,5},{7,6},{8,11},{9,8},{10,9... | collective-permute-start | bytes 491528 | tf_op jit(solution)/shard_map/ppermute | solution.py:341
  288.7 11.5 %collective-permute-start.18 = (bf16[80,1024]{1,0:T(8,128)(2,1)}, bf16[80,1024]{1,0:T(8,128)(2,1)S(1)}, u32[]{:S(2)}, u32[]{:S(2)}) collective-permute-start(bf16[80,1024]{1,0:T(8,128)(2,1)} %get-tuple-element.214), channel_id=1, source_target_pairs={{0,1},{1,2},{2,3},{3,0},{4,5},{5,6},{6,7},{7,4},{8,9},{9,10},{10,1... | collective-permute-start | bytes 491528 | tf_op jit(solution)/shard_map/ppermute | solution.py:341
  318.5 10.3 %collective-permute-start.20 = (f32[1,3,320]{2,1,0:T(4,128)S(1)}, f32[1,3,320]{2,1,0:T(4,128)S(1)}, u32[]{:S(2)}, u32[]{:S(2)}) collective-permute-start(f32[1,3,320]{2,1,0:T(4,128)S(1)} %maximum_bitcast_fusion), channel_id=1, source_target_pairs={{0,2},{1,3},{2,0},{3,1},{4,6},{5,7},{6,4},{7,5},{8,10},{9,11},{10,... | collective-permute-start | bytes 11528 | tf_op jit(solution)/shard_map/ppermute | solution.py:341
  324.1 4.7 collective-permute-start.19
  327.5 5.4 collective-permute-start.21
  344.3 22.1 %collective-permute-start.22 = (bf16[80,1024]{1,0:T(8,128)(2,1)}, bf16[80,1024]{1,0:T(8,128)(2,1)}, u32[]{:S(2)}, u32[]{:S(2)}) collective-permute-start(bf16[80,1024]{1,0:T(8,128)(2,1)} %get-tuple-element.250), channel_id=1, source_target_pairs={{0,1},{1,2},{2,3},{3,0},{4,5},{5,6},{6,7},{7,4},{8,9},{9,10},{10,1... | collective-permute-start | bytes 491528 | tf_op jit(solution)/shard_map/ppermute | solution.py:360
  344.3 22.1 %collective-permute-start.24 = (bf16[80,1024]{1,0:T(8,128)(2,1)}, bf16[80,1024]{1,0:T(8,128)(2,1)}, u32[]{:S(2)}, u32[]{:S(2)}) collective-permute-start(bf16[80,1024]{1,0:T(8,128)(2,1)} %get-tuple-element.251), channel_id=1, source_target_pairs={{0,3},{1,0},{2,1},{3,2},{4,7},{5,4},{6,5},{7,6},{8,11},{9,8},{10,9... | collective-permute-start | bytes 491528 | tf_op jit(solution)/shard_map/ppermute | solution.py:360
  348.6 17.8 %collective-permute-start.23 = (bf16[80,1024]{1,0:T(8,128)(2,1)}, bf16[80,1024]{1,0:T(8,128)(2,1)}, u32[]{:S(2)}, u32[]{:S(2)}) collective-permute-start(bf16[80,1024]{1,0:T(8,128)(2,1)} %get-tuple-element.252), channel_id=1, source_target_pairs={{0,2},{1,3},{2,0},{3,1},{4,6},{5,7},{6,4},{7,5},{8,10},{9,11},{10,... | collective-permute-start | bytes 491528 | tf_op jit(solution)/shard_map/ppermute | solution.py:360
  386.3 10.5 %collective-permute-start.25 = (bf16[256,4096]{1,0:T(8,128)(2,1)}, bf16[256,4096]{1,0:T(8,128)(2,1)}, u32[]{:S(2)}, u32[]{:S(2)}) collective-permute-start(bf16[256,4096]{1,0:T(8,128)(2,1)} %gradient_block.12), channel_id=1, source_target_pairs={{0,4},{4,0},{8,12},{12,8},{16,20},{20,16},{24,28},{28,24},{1,5},{5... | collective-permute-start | bytes 6291464 | tf_op jit(solution)/shard_map/ppermute | solution.py:432
  386.3 10.5 %collective-permute-start.26 = (bf16[256,4096]{1,0:T(8,128)(2,1)}, bf16[256,4096]{1,0:T(8,128)(2,1)}, u32[]{:S(2)}, u32[]{:S(2)}) collective-permute-start(bf16[256,4096]{1,0:T(8,128)(2,1)} %gradient_block.13), channel_id=1, source_target_pairs={{0,4},{4,0},{8,12},{12,8},{16,20},{20,16},{24,28},{28,24},{1,5},{5... | collective-permute-start | bytes 6291464 | tf_op jit(solution)/shard_map/ppermute | solution.py:433
  406.9 19.0 %collective-permute-start.27 = (bf16[256,4096]{1,0:T(8,128)(2,1)}, bf16[256,4096]{1,0:T(8,128)(2,1)S(1)}, u32[]{:S(2)}, u32[]{:S(2)}) collective-permute-start(bf16[256,4096]{1,0:T(8,128)(2,1)} %gradient_block.15), channel_id=1, source_target_pairs={{0,4},{4,0},{8,12},{12,8},{16,20},{20,16},{24,28},{28,24},{1,5},{5... | collective-permute-start | bytes 6291464 | tf_op jit(solution)/shard_map/ppermute | solution.py:432
  406.9 19.0 %collective-permute-start.28 = (bf16[256,4096]{1,0:T(8,128)(2,1)S(1)}, bf16[256,4096]{1,0:T(8,128)(2,1)S(1)}, u32[]{:S(2)}, u32[]{:S(2)}) collective-permute-start(bf16[256,4096]{1,0:T(8,128)(2,1)S(1)} %gradient_block.16), channel_id=1, source_target_pairs={{0,4},{4,0},{8,12},{12,8},{16,20},{20,16},{24,28},{28,24},{1,5},{5... | collective-permute-start | bytes 6291464 | tf_op jit(solution)/shard_map/ppermute | solution.py:433
  407.4 47.6 %collective-permute-start.29 = (bf16[256,4096]{1,0:T(8,128)(2,1)S(1)}, bf16[256,4096]{1,0:T(8,128)(2,1)S(1)}, u32[]{:S(2)}, u32[]{:S(2)}) collective-permute-start(bf16[256,4096]{1,0:T(8,128)(2,1)S(1)} %gradient_block.14), channel_id=1, source_target_pairs={{0,1},{1,0},{2,3},{3,2},{4,5},{5,4},{6,7},{7,6},{8,9},{9,8},{10,11... | collective-permute-start | bytes 6291464 | tf_op jit(solution)/shard_map/ppermute | solution.py:448
  458.3 12.3 %collective-permute-start.30 = (bf16[256,4096]{1,0:T(8,128)(2,1)}, bf16[256,4096]{1,0:T(8,128)(2,1)}, u32[]{:S(2)}, u32[]{:S(2)}) collective-permute-start(bf16[256,4096]{1,0:T(8,128)(2,1)} %gradient_block.18), channel_id=1, source_target_pairs={{0,4},{4,0},{8,12},{12,8},{16,20},{20,16},{24,28},{28,24},{1,5},{5... | collective-permute-start | bytes 6291464 | tf_op jit(solution)/shard_map/ppermute | solution.py:432
  458.3 71.2 %collective-permute-start.31 = (bf16[256,4096]{1,0:T(8,128)(2,1)}, bf16[256,4096]{1,0:T(8,128)(2,1)}, u32[]{:S(2)}, u32[]{:S(2)}) collective-permute-start(bf16[256,4096]{1,0:T(8,128)(2,1)} %gradient_block.17), channel_id=1, source_target_pairs={{0,1},{1,0},{2,3},{3,2},{4,5},{5,4},{6,7},{7,6},{8,9},{9,8},{10,11... | collective-permute-start | bytes 6291464 | tf_op jit(solution)/shard_map/ppermute | solution.py:448
  468.6 82.4 %collective-permute-start.37 = (bf16[256,4096]{1,0:T(8,128)(2,1)}, bf16[256,4096]{1,0:T(8,128)(2,1)}, u32[]{:S(2)}, u32[]{:S(2)}) collective-permute-start(bf16[256,4096]{1,0:T(8,128)(2,1)} %gradient_block.21.total_ref), channel_id=1, source_target_pairs={{2,4},{3,5},{4,2},{5,3},{10,12},{11,13},{12,10},{13,11},{18,20},{1... | collective-permute-start | bytes 6291464 | tf_op jit(solution)/shard_map/ppermute | solution.py:472
  475.4 121.2 %collective-permute-start.36 = (bf16[256,4096]{1,0:T(8,128)(2,1)}, bf16[256,4096]{1,0:T(8,128)(2,1)}, u32[]{:S(2)}, u32[]{:S(2)}) collective-permute-start(bf16[256,4096]{1,0:T(8,128)(2,1)} %gradient_block.19), channel_id=1, source_target_pairs={{0,1},{1,0},{2,3},{3,2},{4,5},{5,4},{6,7},{7,6},{8,9},{9,8},{10,11... | collective-permute-start | bytes 6291464 | tf_op jit(solution)/shard_map/ppermute | solution.py:448
  480.4 116.2 %collective-permute-start.35 = (bf16[256,4096]{1,0:T(8,128)(2,1)}, bf16[256,4096]{1,0:T(8,128)(2,1)}, u32[]{:S(2)}, u32[]{:S(2)}) collective-permute-start(bf16[256,4096]{1,0:T(8,128)(2,1)} %gradient_block.20), channel_id=1, source_target_pairs={{0,4},{4,0},{8,12},{12,8},{16,20},{20,16},{24,28},{28,24},{1,5},{5... | collective-permute-start | bytes 6291464 | tf_op jit(solution)/shard_map/ppermute | solution.py:433
  538.6 65.7 %collective-permute-start.32 = (bf16[528,512]{1,0:T(8,128)(2,1)}, bf16[528,512]{1,0:T(8,128)(2,1)}, u32[]{:S(2)}, u32[]{:S(2)}) collective-permute-start(bf16[528,512]{1,0:T(8,128)(2,1)} %dynamic-slice_convert_fusion), channel_id=1, source_target_pairs={{0,16},{4,20},{8,24},{12,28},{16,0},{20,4},{24,8},{28,12},{1,17},{... | collective-permute-start | bytes 1622024 | tf_op jit(solution)/shard_map/ppermute | solution.py:853
  543.9 52.7 %copy-start.15 = (bf16[512,1024]{1,0:T(8,128)(2,1)S(1)}, bf16[512,1024]{1,0:T(8,128)(2,1)}, u32[]{:S(2)}) copy-start(bf16[512,1024]{1,0:T(8,128)(2,1)} %copy-done.12) | copy-start | bytes 3145732
  543.9 52.7 %copy-start.18 = (bf16[512,1024]{1,0:T(8,128)(2,1)S(1)}, bf16[512,1024]{1,0:T(8,128)(2,1)}, u32[]{:S(2)}) copy-start(bf16[512,1024]{1,0:T(8,128)(2,1)} %copy-done.16) | copy-start | bytes 3145732
  543.9 52.7 %copy-start.26 = (bf16[512,1024]{1,0:T(8,128)(2,1)S(1)}, bf16[512,1024]{1,0:T(8,128)(2,1)}, u32[]{:S(2)}) copy-start(bf16[512,1024]{1,0:T(8,128)(2,1)} %copy-done.23) | copy-start | bytes 3145732
  548.9 55.4 %copy-start.49 = (f32[528,1024]{1,0:T(8,128)S(1)}, f32[528,1024]{1,0:T(8,128)}, u32[]{:S(2)}) copy-start(f32[528,1024]{1,0:T(8,128)} %concatenate.51) | copy-start | bytes 6488068
  548.9 78.0 %collective-permute-start.39 = (bf16[256,4096]{1,0:T(8,128)(2,1)}, bf16[256,4096]{1,0:T(8,128)(2,1)}, u32[]{:S(2)}, u32[]{:S(2)}) collective-permute-start(bf16[256,4096]{1,0:T(8,128)(2,1)} %gradient_block.23.total_ref), channel_id=1, source_target_pairs={{2,4},{3,5},{4,2},{5,3},{10,12},{11,13},{12,10},{13,11},{18,20},{1... | collective-permute-start | bytes 6291464 | tf_op jit(solution)/shard_map/ppermute | solution.py:472
  601.8 42.0 %collective-permute-start.38 = (bf16[256,4096]{1,0:T(8,128)(2,1)}, bf16[256,4096]{1,0:T(8,128)(2,1)}, u32[]{:S(2)}, u32[]{:S(2)}) collective-permute-start(bf16[256,4096]{1,0:T(8,128)(2,1)} %gradient_block.22.total_ref), channel_id=1, source_target_pairs={{2,4},{3,5},{4,2},{5,3},{10,12},{11,13},{12,10},{13,11},{18,20},{1... | collective-permute-start | bytes 6291464 | tf_op jit(solution)/shard_map/ppermute | solution.py:472
  605.6 8.1 collective-permute-start.33
  607.0 18.9 %all-to-all-start.1 = ((bf16[8,512,128]{2,1,0:T(8,128)(2,1)}), bf16[8,512,128]{2,1,0:T(8,128)(2,1)S(1)}, u32[]{:S(2)}, u32[]{:S(2)}) async-start(bf16[8,512,128]{2,1,0:T(8,128)(2,1)} %bitcast_bitcast_fusion), calls=%async_computation.1 | async-start | bytes 2097152 | tf_op jit(solution)/shard_map/all_to_all | solution.py:985
  610.5 130.7 %all-gather.18.cloned.1.call-start = ((), (), s32[]{:S(2)}) async-start(), calls=%async_computation.9 | async-start | bytes 5918720 | tf_op jit(solution)/shard_map/all_gather | solution.py:995
  613.8 1.4 collective-permute-start.34
  643.8 141.0 %all-gather.14.cloned.1.call-start = ((), (), s32[]{:S(2)}) async-start(), calls=%async_computation.7 | async-start | bytes 7077888 | tf_op jit(solution)/shard_map/all_gather | solution.py:1059
  676.4 13.6 %collective-permute-start.40 = (bf16[4,256,1536]{2,1,0:T(8,128)(2,1)}, bf16[4,256,1536]{2,1,0:T(8,128)(2,1)S(1)}, u32[]{:S(2)}, u32[]{:S(2)}) collective-permute-start(bf16[4,256,1536]{2,1,0:T(8,128)(2,1)} %get-tuple-element.156), channel_id=1, source_target_pairs={{0,4},{4,0},{8,12},{12,8},{16,20},{20,16},{24,28},{28,24},{1,5},{5... | collective-permute-start | bytes 9437192 | tf_op jit(solution)/shard_map/ppermute | solution.py:826
  694.9 12.0 %collective-permute-start.42 = (bf16[128,1536]{1,0:T(8,128)(2,1)S(1)}, bf16[128,1536]{1,0:T(8,128)(2,1)S(1)}, u32[]{:S(2)}, u32[]{:S(2)}) collective-permute-start(bf16[128,1536]{1,0:T(8,128)(2,1)S(1)} %get-tuple-element.228), channel_id=1, source_target_pairs={{0,8},{4,12},{8,0},{12,4},{16,24},{20,28},{24,16},{28,20},{1,9},{5... | collective-permute-start | bytes 1179656 | tf_op jit(solution)/shard_map/ppermute | solution.py:826
  694.9 19.8 %collective-permute-start.41 = (bf16[128,1536]{1,0:T(8,128)(2,1)}, bf16[128,1536]{1,0:T(8,128)(2,1)S(1)}, u32[]{:S(2)}, u32[]{:S(2)}) collective-permute-start(bf16[128,1536]{1,0:T(8,128)(2,1)} %get-tuple-element.225), channel_id=1, source_target_pairs={{0,8},{4,12},{8,0},{12,4},{16,24},{20,28},{24,16},{28,20},{1,9},{5... | collective-permute-start | bytes 1179656 | tf_op jit(solution)/shard_map/ppermute | solution.py:826
  696.9 17.8 %collective-permute-start.45 = (bf16[128,1536]{1,0:T(8,128)(2,1)}, bf16[128,1536]{1,0:T(8,128)(2,1)}, u32[]{:S(2)}, u32[]{:S(2)}) collective-permute-start(bf16[128,1536]{1,0:T(8,128)(2,1)} %get-tuple-element.226), channel_id=1, source_target_pairs={{0,16},{4,20},{8,24},{12,28},{16,0},{20,4},{24,8},{28,12},{1,17},{... | collective-permute-start | bytes 1179656 | tf_op jit(solution)/shard_map/ppermute | solution.py:826
  708.7 12.4 %collective-permute-start.43 = (bf16[128,1536]{1,0:T(8,128)(2,1)}, bf16[128,1536]{1,0:T(8,128)(2,1)}, u32[]{:S(2)}, u32[]{:S(2)}) collective-permute-start(bf16[128,1536]{1,0:T(8,128)(2,1)} %fusion.40), channel_id=1, source_target_pairs={{0,16},{4,20},{8,24},{12,28},{16,0},{20,4},{24,8},{28,12},{1,17},{... | collective-permute-start | bytes 1179656 | tf_op jit(solution)/shard_map/ppermute | solution.py:826
  708.7 18.7 %collective-permute-start.44 = (bf16[128,1536]{1,0:T(8,128)(2,1)}, bf16[128,1536]{1,0:T(8,128)(2,1)S(1)}, u32[]{:S(2)}, u32[]{:S(2)}) collective-permute-start(bf16[128,1536]{1,0:T(8,128)(2,1)} %get-tuple-element.227), channel_id=1, source_target_pairs={{0,16},{4,20},{8,24},{12,28},{16,0},{20,4},{24,8},{28,12},{1,17},{... | collective-permute-start | bytes 1179656 | tf_op jit(solution)/shard_map/ppermute | solution.py:826
  722.8 7.8 collective-permute-start.46
  739.7 75.4 %all-gather.16.cloned.1.call-start = ((), (), s32[]{:S(2)}) async-start(), calls=%async_computation.8 | async-start | bytes 1216512 | tf_op jit(solution)/shard_map/all_gather | solution.py:1062
  791.5 1.2 collective-permute-start.47
  792.7 3.6 collective-permute-start.48
  796.4 3.6 collective-permute-start.49
  800.0 3.6 collective-permute-start.50
  803.6 11.5 %collective-permute-start.51 = (f32[2,8]{1,0:T(2,128)S(1)}, f32[2,8]{1,0:T(2,128)S(1)}, u32[]{:S(2)}, u32[]{:S(2)}) collective-permute-start(f32[2,8]{1,0:T(2,128)S(1)} %add.756), channel_id=1, source_target_pairs={{0,2},{1,3},{2,0},{3,1},{4,6},{5,7},{6,4},{7,5},{8,10},{9,11},{10,... | collective-permute-start | bytes 200 | tf_op jit(solution)/shard_map/ppermute | solution.py:331
  (70 other events, 621.7 us)
Sparse Core Ops, SparseCore 0:
  12.1 64.7 all-gather.7
  86.4 144.1 all-gather.9
  233.1 43.8 all-gather.11
  368.6 111.4 reduce-scatter.1
  643.9 94.3 all-gather.17
  740.8 43.9 all-gather.13
  787.4 23.7 all-gather.15

commit v16 on v15

--- a/solution.py
+++ b/solution.py
@@ -225,7 +225,7 @@
 
 def ffn_up(fin, weights, bias):
     tokens = fin.shape[0]
-    block = 512
+    block = 1024
     first = 4 * D // block
     out = pl.BlockSpec((tokens, block), lambda step: (0, step))
     return pl.pallas_call(
@@ -238,7 +238,7 @@
         ],
         out_specs=[out, out],
         out_shape=[jax.ShapeDtypeStruct((tokens, FF), jnp.bfloat16)] * 2,
-        compiler_params=pltpu.CompilerParams(vmem_limit_bytes=32 * 2**20),
+        compiler_params=pltpu.CompilerParams(vmem_limit_bytes=48 * 2**20),
         cost_estimate=pl.CostEstimate(flops=2 * tokens * D * FF, bytes_accessed=0, transcendentals=0),
         name="ffn_up",
     )(fin, weights, bias)
@@ -796,7 +796,7 @@
 
 def table_update(grad, head, table, first, second):
     size, cols = table.shape
-    block = size // 9 if size % 9 == 0 and size // 9 % 16 == 0 else size
+    block = size // 3 if size % 3 == 0 and size // 3 % 16 == 0 else size
     whole = pl.BlockSpec((block, cols), lambda step: (step, 0))
     line = pl.BlockSpec((1, cols), lambda step: (0, 0))
     moment, update, *sums = pl.pallas_call(

time: 845 us -> 843 us (level)
    unnamed x158 -> x156, local copies, waits for them, and re-layouts: 33.2 us -> 31.1 us
  transfers between devices with their start and end apart: 58 -> 58, of which waited for: 28 -> 29; matrix products, arithmetic and copies ran while one was open for 20% -> 20% of each run, Pallas kernels for 28% -> 28%
where the time goes in v16:
time: 843 us; the launch traced here: 835 us
  waiting for transfers between devices  232 us (28%)
  Pallas kernels  232 us (28%)
  starting transfers between devices  102 us (12%)
  other arithmetic  86.3 us (10%)
  matrix products  79.1 us (9%)
  local copies, waits for them, and re-layouts  76.5 us (9%)
  between operations  24.2 us (3%)
    ppermute x3, waiting for transfers between devices, across(): self.away = lax.ppermute(away, 'narrow', sides)  84.1 us
    pallas_call x1, Pallas kernels, packed_rows(): pl.pallas_call(pack_kernel, grid_spec=pltpu.PrefetchScalarGridSpec(num_sc...  52.4 us
    pallas_call x12, Pallas kernels, gradient_block(): pl.pallas_call(functools.partial(block_kernel, steps), grid_spec=pltpu.Pr...  47.1 us
    ppermute x3, waiting for transfers between devices, sent_around(): lax.ppermute(block(by), 'narrow', cycle(size, by))  38.9 us
    ppermute x7, waiting for transfers between devices, send(): lax.ppermute(value.astype(jnp.bfloat16), 'wide', swap_pairs(n_wide, bit))  33.4 us
    dot_general x4, matrix products, matmul_nt(): lax.dot_general(left, right, (((1,), (1,)), ((), ())), preferred_element_...  32.4 us
    unnamed x156, local copies, waits for them, and re-layouts  31.1 us
    all_gather x1, waiting for transfers between devices, shards(): weights = lax.all_gather(layer_rows, 'wide', axis=1, tiled=True)  30.6 us
  transfers between devices with their start and end apart: 58, of which 29 were waited for; matrix products, arithmetic and copies ran while one was open for 20% of the time, Pallas kernels for 28%

profile of v16, /device:TPU:0, one launch (start us, length us, event | category | flops | bytes accessed | tf_op | source)
XLA Modules:
  0.0 835.3 jit_solution(4984276042050605676)
XLA Ops:
  28.5 52.4 %pack_rows.1 = bf16[4,4096,128]{2,1,0:T(8,128)(2,1)} custom-call(s32[16384]{0:T(1024)S(1)} %fusion.59.ids_ref, f32[7632,128]{1,0:T(8,128)S(1)} %copy-done.8), custom_call_target="tpu_custom_call" | custom-call | tf_op jit(solution)/shard_map/pack_rows/pallas_call | solution.py:569
  89.1 10.9 %collective-permute-start.11 = (bf16[1792,128]{1,0:T(8,128)(2,1)S(1)}, bf16[1792,128]{1,0:T(8,128)(2,1)S(1)}, u32[]{:S(2)}, u32[]{:S(2)}) collective-permute-start(bf16[1792,128]{1,0:T(8,128)(2,1)S(1)} %get-tuple-element.242), channel_id=1, source_target_pairs={{0,3},{1,0},{2,1},{3,2},{4,7},{5,4},{6,5},{7,6},{8,11},{9,8},{10,9... | collective-permute-start | bytes 1376264 | tf_op jit(solution)/shard_map/ppermute | solution.py:373
  100.7 10.3 %collective-permute-done.11 = bf16[1792,128]{1,0:T(8,128)(2,1)S(1)} collective-permute-done((bf16[1792,128]{1,0:T(8,128)(2,1)S(1)}, bf16[1792,128]{1,0:T(8,128)(2,1)S(1)}, u32[]{:S(2)}, u32[]{:S(2)}) %collective-permute-start.11) | collective-permute-done | bytes 458784 | tf_op jit(solution)/shard_map/ppermute | solution.py:373
  111.0 28.5 %collective-permute-done.10 = bf16[1792,128]{1,0:T(8,128)(2,1)S(1)} collective-permute-done((bf16[1792,128]{1,0:T(8,128)(2,1)S(1)}, bf16[1792,128]{1,0:T(8,128)(2,1)S(1)}, u32[]{:S(2)}, u32[]{:S(2)}) %collective-permute-start.10) | collective-permute-done | bytes 458784 | tf_op jit(solution)/shard_map/ppermute | solution.py:373
  139.7 5.5 take_rows.3
  145.2 3.5 conditional.1
  149.7 3.6 all-to-all-start
  158.9 18.1 %collective-permute-start.13 = (f32[]{:T(128)}, f32[]{:T(128)}, u32[]{:S(2)}, u32[]{:S(2)}) collective-permute-start(f32[]{:T(128)} %add.643), channel_id=1, source_target_pairs={{0,8},{4,12},{8,0},{12,4},{16,24},{20,28},{24,16},{28,20},{1,9},{5... | collective-permute-start | bytes 20 | tf_op jit(solution)/shard_map/ppermute | solution.py:331
  184.3 9.8 %dynamic_update_slice.46 = bf16[7632,1024]{1,0:T(8,128)(2,1)} pad(bf16[4768,1024]{1,0:T(8,128)(2,1)} %all-gather.8.cloned.1.call-done, bf16[]{:T(256)} %constant.264.clone.1), padding=0_2864x0_0 | pad | bytes 25395202 | tf_op jit(solution)/shard_map/dynamic_update_slice | solution.py:929
  200.0 30.6 %all-gather.10.cloned.1.call-done.weight_ref = bf16[1024,12288]{1,0:T(8,128)(2,1)} async-done(((bf16[1024,1536]{1,0:T(8,128)(2,1)}), bf16[1024,12288]{1,0:T(8,128)(2,1)}) %all-gather.10.cloned.1.call-update) | async-done | bytes 25165840 | tf_op jit(solution)/shard_map/all_gather | solution.py:900
  232.6 6.4 add_convert_fusion.q_ref.k_ref.v_ref
  239.0 11.7 %attend.1 = (bf16[512,1024]{1,0:T(8,128)(2,1)S(1)}, f32[8,2,512]{2,1,0:T(2,128)S(1)}) custom-call(bf16[512,3072]{1,0:T(8,128)(2,1)S(1)} %add_convert_fusion.q_ref.k_ref.v_ref, bf16[512,3072]{1,0:T(8,128)(2,1)S(1)} %add_convert_fusion.q_ref.k_ref.v_ref, bf16[512,3072]{1,0:T(8,128)(2,1)S(1)} %add_convert_fusion.q_ref.k_ref.v_ref, ...), custom_call_target="tpu_custom_call" | custom-call | tf_op jit(solution)/shard_map/attend/pallas_call | solution.py:82
  250.7 3.4 fusion.92
  255.0 11.6 %ffn_up.1 = (bf16[512,4096]{1,0:T(8,128)(2,1)S(1)}, bf16[512,4096]{1,0:T(8,128)(2,1)}) custom-call(bf16[512,1024]{1,0:T(8,128)(2,1)S(1)} %fusion.22.fin_ref.refs_0_, bf16[1024,12288]{1,0:T(8,128)(2,1)} %all-gather.10.cloned.1.call-done.weight_ref, f32[1,4096]{1,0:T(1,128)S(1)} %bitcast.180), custom_call_target="tpu_custom_call" | custom-call | flops 4294967296 | tf_op jit(solution)/shard_map/ffn_up/pallas_call | solution.py:231
  266.6 8.8 %fusion.93 = (f32[512]{0:T(512)S(1)}, f32[512,1024]{1,0:T(8,128)S(1)}) fusion(f32[1024]{0:T(1024)S(1)} %bitcast.225, bf16[512,4096]{1,0:T(8,128)(2,1)S(1)} %get-tuple-element.113.refs_1_, bf16[1024,12288]{1,0:T(8,128)(2,1)} %all-gather.10.cloned.1.call-done.weight_ref, f32[1024]{0:T(1024)S(1)} %bitcast.213, f32[1024]{0:T(1024)S(1)} %bitcast.207, ...), kind=kOutput, calls=%fused_computation.262 | convolution fusion | flops 4298636800 | bytes 16795648 | tf_op jit(solution)/shard_map/dot_general | solution.py:55
  287.3 6.1 collective-permute-done.16
  298.6 5.8 constant_dynamic-update-slice_fusion.4
  304.4 9.1 %fusion.94 = (f32[320]{0:T(512)S(1)}, f32[320,7632]{1,0:T(8,128)S(1)}) fusion(bf16[320,1024]{1,0:T(8,128)(2,1)} %constant_dynamic-update-slice_fusion.5, bf16[7632,1024]{1,0:T(8,128)(2,1)} %constant_dynamic-update-slice_fusion.4, pred[7632]{0:T(1024)(128)(4,1)S(1)} %broadcast_compare_fusion.1), kind=kOutput, calls=%fused_computation.263 | convolution fusion | flops 5006591488 | bytes 26063568 | tf_op jit(solution)/shard_map/dot_general | solution.py:55
  316.3 5.6 collective-permute-start.20
  321.9 3.4 collective-permute-start.19
  326.6 4.1 collective-permute-done.21
  331.4 8.9 %fusion.80 = f32[320,1024]{1,0:T(8,128)S(1)} fusion(bf16[7632,1024]{1,0:T(8,128)(2,1)} %constant_dynamic-update-slice_fusion.4, f32[320,7632]{1,0:T(8,128)S(1)} %get-tuple-element.278, f32[320]{0:T(512)S(1)} %get-tuple-element.270, f32[320]{0:T(512)S(1)} %get-tuple-element.199, s32[7632]{0:T(1024)S(1)} %iota_add_fusion, s32[320]{0:T(512)S(1)} %eq.137), kind=kOutput, calls=%fused_computation.253 | convolution fusion | flops 5016360960 | bytes 26744384 | tf_op jit(solution)/shard_map/dot_general | solution.py:45
  342.1 4.3 collective-permute-start.24
  346.4 17.8 %convert_bitcast_fusion = bf16[8,7632,128]{2,1,0:T(8,128)(2,1)} fusion(f32[320,7632]{1,0:T(8,128)} %copy-done.45, f32[320]{0:T(512)S(1)} %get-tuple-element.270, f32[320]{0:T(512)S(1)} %get-tuple-element.199, s32[7632]{0:T(1024)S(1)} %iota_add_fusion, s32[320]{0:T(512)S(1)} %eq.137, bf16[320,1024]{1,0:T(8,128)(2,1)} %constant_dynamic-update-slice_fusion.5), kind=kOutput, calls=%fused_computation.8 | convolution fusion | flops 5024176128 | bytes 26089024 | tf_op jit(solution)/shard_map/sv,swc->wvc/dot_general | solution.py:967
  377.3 3.5 gradient_block.13
  380.7 3.4 gradient_block.12
  384.6 10.0 %multiply_convert_fusion.refs_1_ = bf16[512,4096]{1,0:T(8,128)(2,1)S(1)} fusion(bf16[512,4096]{1,0:T(8,128)(2,1)} %get-tuple-element.118, bf16[512,1024]{1,0:T(8,128)(2,1)S(1)} %get-tuple-element.205.refs_0_, bf16[1024,12288]{1,0:T(8,128)(2,1)} %all-gather.10.cloned.1.call-done.weight_ref), kind=kOutput, calls=%fused_computation.20 | convolution fusion | flops 4301258752 | bytes 17825792 | tf_op jit(solution)/shard_map/dot_general | solution.py:45
  394.7 4.3 gradient_block.14
  401.4 3.3 gradient_block.15
  405.2 11.3 %multiply_reduce_fusion.2 = (f32[1024]{0:T(1024)S(1)}, f32[512]{0:T(512)S(1)}, f32[1024]{0:T(1024)S(1)}, f32[512,1024]{1,0:T(8,128)}) fusion(f32[512,1024]{1,0:T(8,128)} %copy-done.40, f32[512]{0:T(512)S(1)} %fusion.73, f32[512]{0:T(512)S(1)} %broadcast_multiply_fusion.2, f32[1024]{0:T(1024)S(1)} %bitcast.208, ...), kind=kOutput, calls=%fused_computation.40 | convolution fusion | flops 4300207616 | bytes 18894848 | tf_op jit(solution)/shard_map/dot_general | solution.py:55
  420.5 3.3 fusion.29.do_ref
  423.8 3.5 gradient_block.17
  427.3 16.6 %attend_back.1.refs_2_.dqkv_ref = bf16[512,3072]{1,0:T(8,128)(2,1)S(1)} custom-call(bf16[512,3072]{1,0:T(8,128)(2,1)S(1)} %copy-done.1, bf16[512,3072]{1,0:T(8,128)(2,1)S(1)} %copy-done.1, bf16[512,3072]{1,0:T(8,128)(2,1)S(1)} %copy-done.1, bf16[512,1024]{1,0:T(8,128)(2,1)S(1)} %fusion.29.do_ref, f32[8,2,512]{2,1,0:T(2,128)S(1)} %get-tuple-element.125.lse_ref, ...), custom_call_target="tpu_custom_call" | custom-call | tf_op jit(solution)/shard_map/attend_back/pallas_call | solution.py:126
  443.9 8.9 %collective-permute-done.29.refs_3_ = bf16[256,4096]{1,0:T(8,128)(2,1)S(1)} collective-permute-done((bf16[256,4096]{1,0:T(8,128)(2,1)S(1)}, bf16[256,4096]{1,0:T(8,128)(2,1)S(1)}, u32[]{:S(2)}, u32[]{:S(2)}) %collective-permute-start.29) | collective-permute-done | bytes 2097184 | tf_op jit(solution)/shard_map/ppermute | solution.py:448
  452.8 3.3 gradient_block.18
  461.5 5.1 gradient_block.21.total_ref
  468.5 4.8 gradient_block.19
  475.0 3.3 gradient_block.20
  488.6 8.1 embed_back.1
  498.0 29.4 %collective-permute-done.31.refs_3_ = bf16[256,4096]{1,0:T(8,128)(2,1)} collective-permute-done((bf16[256,4096]{1,0:T(8,128)(2,1)}, bf16[256,4096]{1,0:T(8,128)(2,1)}, u32[]{:S(2)}, u32[]{:S(2)}) %collective-permute-start.31) | collective-permute-done | bytes 2097184 | tf_op jit(solution)/shard_map/ppermute | solution.py:448
  527.4 6.9 concatenate.51
  541.4 5.1 gradient_block.23.total_ref
  548.6 45.8 %collective-permute-done.36.refs_5_ = bf16[256,4096]{1,0:T(8,128)(2,1)} collective-permute-done((bf16[256,4096]{1,0:T(8,128)(2,1)}, bf16[256,4096]{1,0:T(8,128)(2,1)}, u32[]{:S(2)}, u32[]{:S(2)}) %collective-permute-start.36) | collective-permute-done | bytes 2097184 | tf_op jit(solution)/shard_map/ppermute | solution.py:448
  594.4 5.2 gradient_block.22.total_ref
  605.0 3.6 all-to-all-start.1
  613.1 10.8 %all-to-all-done.1 = bf16[8,512,128]{2,1,0:T(8,128)(2,1)S(1)} async-done(((bf16[8,512,128]{2,1,0:T(8,128)(2,1)}), bf16[8,512,128]{2,1,0:T(8,128)(2,1)S(1)}, u32[]{:S(2)}, u32[]{:S(2)}) %all-to-all-start.1) | async-done | bytes 1048608 | tf_op jit(solution)/shard_map/all_to_all | solution.py:985
  625.0 7.1 span.3
  633.4 7.1 span.4
  641.8 7.1 span.5
  652.8 21.6 %press.1 = (f32[1,256,12288]{2,1,0:T(8,128)}, bf16[4,256,1536]{2,1,0:T(8,128)(2,1)}, bf16[4,256,1536]{2,1,0:T(8,128)(2,1)}) custom-call(s32[1]{0:T(128)} %bitcast.4.core_ref, f32[2]{0:T(128)} %pad_maximum_fusion.5.scale_ref, f32[256,4096]{1,0:T(8,128)} %get-tuple-element.152.refs_0_, f32[256,4096]{1,0:T(8,128)} %get-tuple-element.153.refs_1_, ...), custom_call_target="tpu_custom_call" | custom-call | tf_op jit(solution)/shard_map/press/pallas_call | solution.py:757
  674.4 7.9 collective-permute-start.40
  682.3 5.5 collective-permute-done.40
  694.7 9.9 %collective-permute-done.42 = bf16[128,1536]{1,0:T(8,128)(2,1)S(1)} collective-permute-done((bf16[128,1536]{1,0:T(8,128)(2,1)S(1)}, bf16[128,1536]{1,0:T(8,128)(2,1)S(1)}, u32[]{:S(2)}, u32[]{:S(2)}) %collective-permute-start.42) | collective-permute-done | bytes 393248 | tf_op jit(solution)/shard_map/ppermute | solution.py:826
  708.6 3.9 collective-permute-done.41
  712.5 6.4 collective-permute-done.43
  720.8 4.5 collective-permute-done.44
  732.4 5.0 fusion.53
  739.1 25.1 %add_rows.1.grad_ref = f32[7632,128]{1,0:T(8,128)} custom-call(s32[16384]{0:T(1024)} %copy-done.35, bf16[4,4624,128]{2,1,0:T(8,128)(2,1)} %bitcast.184), custom_call_target="tpu_custom_call" | custom-call | tf_op jit(solution)/shard_map/add_rows/pallas_call | solution.py:644
  764.1 10.8 %update.1 = (f32[7632,128]{1,0:T(8,128)}, f32[7632,128]{1,0:T(8,128)}, f32[1,128]{1,0:T(1,128)}, f32[1,128]{1,0:T(1,128)}) custom-call(f32[7632,128]{1,0:T(8,128)} %add_rows.1.grad_ref, bf16[7632,128]{1,0:T(8,128)(2,1)} %bitcast.189, f32[7632,128]{1,0:T(8,128)} %table_ref.3, f32[7632,128]{1,0:T(8,128)} %first_ref.1, f32[7632,128]{1,0:T(8,128)} %second_ref.1), custom_call_target="tpu_custom_call" | custom-call | tf_op jit(solution)/shard_map/update/pallas_call | solution.py:802
  779.3 3.3 all-gather.14.cloned.1.call-done
  803.8 9.1 %convert_element_type.368 = f32[256,12288]{1,0:T(8,128)} convert(bf16[256,12288]{1,0:T(8,128)(2,1)} %all-gather.14.cloned.1.call-done) | non-fusion elementwise | flops 3145728 | bytes 18874368 | tf_op jit(solution)/shard_map/convert_element_type | solution.py:1092
  816.7 3.4 multiply_subtract_fusion.2
  820.2 4.8 multiply_subtract_fusion
  824.9 3.3 multiply_subtract_fusion.1
  (412 shorter events, 186.0 us)
Async XLA Ops:
  7.2 77.5 %all-gather.8.cloned.1.call-start = ((), (), s32[]{:S(2)}) async-start(), calls=%async_computation.3 | async-start | bytes 10985472 | tf_op jit(solution)/shard_map/all_gather | solution.py:893
  11.9 218.7 %all-gather.10.cloned.1.call-start = ((), (), s32[]{:S(2)}) async-start(), calls=%async_computation.4 | async-start | bytes 28311552 | tf_op jit(solution)/shard_map/all_gather | solution.py:900
  12.1 1.3 collective-permute-start.6
  13.5 4.7 collective-permute-start.7
  18.2 7.8 collective-permute-start.8
  20.4 60.6 %copy-start.50 = (bf16[256,1536]{1,0:T(8,128)(2,1)}, bf16[256,1536]{1,0:T(8,128)(2,1)S(1)}, u32[]{:S(2)}) copy-start(bf16[256,1536]{1,0:T(8,128)(2,1)S(1)} %convert_element_type.288) | copy-start | bytes 2359300
  20.4 60.6 %collective-permute-start.5 = (bf16[256,1536]{1,0:T(8,128)(2,1)S(1)}, bf16[256,1536]{1,0:T(8,128)(2,1)S(1)}, u32[]{:S(2)}, u32[]{:S(2)}) collective-permute-start(bf16[256,1536]{1,0:T(8,128)(2,1)S(1)} %convert_element_type.288), channel_id=1, source_target_pairs={{0,1},{1,2},{2,3},{3,0},{4,5},{5,6},{6,7},{7,4},{8,9},{9,10},{10,1... | collective-permute-start | bytes 2359304 | tf_op jit(solution)/shard_map/ppermute | solution.py:341
  22.0 59.0 %collective-permute-start.4 = (bf16[256,1536]{1,0:T(8,128)(2,1)S(1)}, bf16[256,1536]{1,0:T(8,128)(2,1)S(1)}, u32[]{:S(2)}, u32[]{:S(2)}) collective-permute-start(bf16[256,1536]{1,0:T(8,128)(2,1)S(1)} %convert_element_type.288), channel_id=1, source_target_pairs={{0,2},{1,3},{2,0},{3,1},{4,6},{5,7},{6,4},{7,5},{8,10},{9,11},{10,... | collective-permute-start | bytes 2359304 | tf_op jit(solution)/shard_map/ppermute | solution.py:341
  24.6 58.1 %collective-permute-start.3 = (bf16[256,1536]{1,0:T(8,128)(2,1)S(1)}, bf16[256,1536]{1,0:T(8,128)(2,1)}, u32[]{:S(2)}, u32[]{:S(2)}) collective-permute-start(bf16[256,1536]{1,0:T(8,128)(2,1)S(1)} %convert_element_type.288), channel_id=1, source_target_pairs={{0,3},{1,0},{2,1},{3,2},{4,7},{5,4},{6,5},{7,6},{8,11},{9,8},{10,9... | collective-permute-start | bytes 2359304 | tf_op jit(solution)/shard_map/ppermute | solution.py:341
  89.1 21.9 %collective-permute-start.11 = (bf16[1792,128]{1,0:T(8,128)(2,1)S(1)}, bf16[1792,128]{1,0:T(8,128)(2,1)S(1)}, u32[]{:S(2)}, u32[]{:S(2)}) collective-permute-start(bf16[1792,128]{1,0:T(8,128)(2,1)S(1)} %get-tuple-element.242), channel_id=1, source_target_pairs={{0,3},{1,0},{2,1},{3,2},{4,7},{5,4},{6,5},{7,6},{8,11},{9,8},{10,9... | collective-permute-start | bytes 1376264 | tf_op jit(solution)/shard_map/ppermute | solution.py:373
  100.0 39.6 %collective-permute-start.10 = (bf16[1792,128]{1,0:T(8,128)(2,1)S(1)}, bf16[1792,128]{1,0:T(8,128)(2,1)S(1)}, u32[]{:S(2)}, u32[]{:S(2)}) collective-permute-start(bf16[1792,128]{1,0:T(8,128)(2,1)S(1)} %get-tuple-element.243), channel_id=1, source_target_pairs={{0,2},{1,3},{2,0},{3,1},{4,6},{5,7},{6,4},{7,5},{8,10},{9,11},{10,... | collective-permute-start | bytes 1376264 | tf_op jit(solution)/shard_map/ppermute | solution.py:373
  100.0 39.6 %collective-permute-start.9 = (bf16[1792,128]{1,0:T(8,128)(2,1)S(1)}, bf16[1792,128]{1,0:T(8,128)(2,1)S(1)}, u32[]{:S(2)}, u32[]{:S(2)}) collective-permute-start(bf16[1792,128]{1,0:T(8,128)(2,1)S(1)} %get-tuple-element.244), channel_id=1, source_target_pairs={{0,1},{1,2},{2,3},{3,0},{4,5},{5,6},{6,7},{7,4},{8,9},{9,10},{10,1... | collective-permute-start | bytes 1376264 | tf_op jit(solution)/shard_map/ppermute | solution.py:373
  149.7 44.4 %all-to-all-start = ((bf16[8,512,128]{2,1,0:T(8,128)(2,1)}), bf16[8,512,128]{2,1,0:T(8,128)(2,1)S(1)}, u32[]{:S(2)}, u32[]{:S(2)}) async-start(bf16[8,512,128]{2,1,0:T(8,128)(2,1)} %bitcast.188), calls=%async_computation | async-start | bytes 2097152 | tf_op jit(solution)/shard_map/all_to_all | solution.py:910
  153.2 145.4 %all-gather.12.cloned.1.call-start = ((), (), s32[]{:S(2)}) async-start(), calls=%async_computation.5 | async-start | bytes 6598656 | tf_op jit(solution)/shard_map/all_gather | solution.py:933
  153.9 3.7 collective-permute-start.12
  154.2 30.0 %collective-permute-start.15 = (s32[1,592]{1,0:T(1,128)S(1)}, s32[1,592]{1,0:T(1,128)S(1)}, u32[]{:S(2)}, u32[]{:S(2)}) collective-permute-start(s32[1,592]{1,0:T(1,128)S(1)} %pad_add_fusion.3), channel_id=1, source_target_pairs={{0,0},{1,4},{2,1},{3,5},{4,2},{5,6},{6,3},{7,7},{8,8},{9,12},{10,9... | collective-permute-start | bytes 7112 | tf_op jit(solution)/shard_map/ppermute | solution.py:495
  158.9 20.4 %collective-permute-start.13 = (f32[]{:T(128)}, f32[]{:T(128)}, u32[]{:S(2)}, u32[]{:S(2)}) collective-permute-start(f32[]{:T(128)} %add.643), channel_id=1, source_target_pairs={{0,8},{4,12},{8,0},{12,4},{16,24},{20,28},{24,16},{28,20},{1,9},{5... | collective-permute-start | bytes 20 | tf_op jit(solution)/shard_map/ppermute | solution.py:331
  179.9 3.7 collective-permute-start.14
  230.6 411.1 %reduce-scatter.2.cloned.1.call-start = ((), (), s32[]{:S(2)}) async-start(), calls=%async_computation.6 | async-start | bytes 17584128 | tf_op jit(solution)/shard_map/reduce_scatter | solution.py:969
  254.9 168.8 %copy-start.10 = (bf16[512,1024]{1,0:T(8,128)(2,1)}, bf16[512,1024]{1,0:T(8,128)(2,1)S(1)}, u32[]{:S(2)}) copy-start(bf16[512,1024]{1,0:T(8,128)(2,1)S(1)} %fusion.22.fin_ref.refs_0_) | copy-start | bytes 3145732
  282.7 12.4 %collective-permute-start.17 = (bf16[80,1024]{1,0:T(8,128)(2,1)}, bf16[80,1024]{1,0:T(8,128)(2,1)}, u32[]{:S(2)}, u32[]{:S(2)}) collective-permute-start(bf16[80,1024]{1,0:T(8,128)(2,1)} %get-tuple-element.214), channel_id=1, source_target_pairs={{0,2},{1,3},{2,0},{3,1},{4,6},{5,7},{6,4},{7,5},{8,10},{9,11},{10,... | collective-permute-start | bytes 491528 | tf_op jit(solution)/shard_map/ppermute | solution.py:341
  284.8 8.6 %collective-permute-start.16 = (bf16[80,1024]{1,0:T(8,128)(2,1)}, bf16[80,1024]{1,0:T(8,128)(2,1)}, u32[]{:S(2)}, u32[]{:S(2)}) collective-permute-start(bf16[80,1024]{1,0:T(8,128)(2,1)} %get-tuple-element.214), channel_id=1, source_target_pairs={{0,3},{1,0},{2,1},{3,2},{4,7},{5,4},{6,5},{7,6},{8,11},{9,8},{10,9... | collective-permute-start | bytes 491528 | tf_op jit(solution)/shard_map/ppermute | solution.py:341
  286.4 11.5 %collective-permute-start.18 = (bf16[80,1024]{1,0:T(8,128)(2,1)}, bf16[80,1024]{1,0:T(8,128)(2,1)S(1)}, u32[]{:S(2)}, u32[]{:S(2)}) collective-permute-start(bf16[80,1024]{1,0:T(8,128)(2,1)} %get-tuple-element.214), channel_id=1, source_target_pairs={{0,1},{1,2},{2,3},{3,0},{4,5},{5,6},{6,7},{7,4},{8,9},{9,10},{10,1... | collective-permute-start | bytes 491528 | tf_op jit(solution)/shard_map/ppermute | solution.py:341
  316.3 10.4 %collective-permute-start.20 = (f32[1,3,320]{2,1,0:T(4,128)S(1)}, f32[1,3,320]{2,1,0:T(4,128)S(1)}, u32[]{:S(2)}, u32[]{:S(2)}) collective-permute-start(f32[1,3,320]{2,1,0:T(4,128)S(1)} %maximum_bitcast_fusion), channel_id=1, source_target_pairs={{0,2},{1,3},{2,0},{3,1},{4,6},{5,7},{6,4},{7,5},{8,10},{9,11},{10,... | collective-permute-start | bytes 11528 | tf_op jit(solution)/shard_map/ppermute | solution.py:341
  321.9 4.7 collective-permute-start.19
  325.3 5.4 collective-permute-start.21
  342.1 22.1 %collective-permute-start.22 = (bf16[80,1024]{1,0:T(8,128)(2,1)}, bf16[80,1024]{1,0:T(8,128)(2,1)}, u32[]{:S(2)}, u32[]{:S(2)}) collective-permute-start(bf16[80,1024]{1,0:T(8,128)(2,1)} %get-tuple-element.250), channel_id=1, source_target_pairs={{0,1},{1,2},{2,3},{3,0},{4,5},{5,6},{6,7},{7,4},{8,9},{9,10},{10,1... | collective-permute-start | bytes 491528 | tf_op jit(solution)/shard_map/ppermute | solution.py:360
  342.1 22.1 %collective-permute-start.24 = (bf16[80,1024]{1,0:T(8,128)(2,1)}, bf16[80,1024]{1,0:T(8,128)(2,1)}, u32[]{:S(2)}, u32[]{:S(2)}) collective-permute-start(bf16[80,1024]{1,0:T(8,128)(2,1)} %get-tuple-element.251), channel_id=1, source_target_pairs={{0,3},{1,0},{2,1},{3,2},{4,7},{5,4},{6,5},{7,6},{8,11},{9,8},{10,9... | collective-permute-start | bytes 491528 | tf_op jit(solution)/shard_map/ppermute | solution.py:360
  346.4 17.8 %collective-permute-start.23 = (bf16[80,1024]{1,0:T(8,128)(2,1)}, bf16[80,1024]{1,0:T(8,128)(2,1)}, u32[]{:S(2)}, u32[]{:S(2)}) collective-permute-start(bf16[80,1024]{1,0:T(8,128)(2,1)} %get-tuple-element.252), channel_id=1, source_target_pairs={{0,2},{1,3},{2,0},{3,1},{4,6},{5,7},{6,4},{7,5},{8,10},{9,11},{10,... | collective-permute-start | bytes 491528 | tf_op jit(solution)/shard_map/ppermute | solution.py:360
  384.1 10.5 %collective-permute-start.25 = (bf16[256,4096]{1,0:T(8,128)(2,1)}, bf16[256,4096]{1,0:T(8,128)(2,1)}, u32[]{:S(2)}, u32[]{:S(2)}) collective-permute-start(bf16[256,4096]{1,0:T(8,128)(2,1)} %gradient_block.12), channel_id=1, source_target_pairs={{0,4},{4,0},{8,12},{12,8},{16,20},{20,16},{24,28},{28,24},{1,5},{5... | collective-permute-start | bytes 6291464 | tf_op jit(solution)/shard_map/ppermute | solution.py:432
  384.1 10.5 %collective-permute-start.26 = (bf16[256,4096]{1,0:T(8,128)(2,1)}, bf16[256,4096]{1,0:T(8,128)(2,1)}, u32[]{:S(2)}, u32[]{:S(2)}) collective-permute-start(bf16[256,4096]{1,0:T(8,128)(2,1)} %gradient_block.13), channel_id=1, source_target_pairs={{0,4},{4,0},{8,12},{12,8},{16,20},{20,16},{24,28},{28,24},{1,5},{5... | collective-permute-start | bytes 6291464 | tf_op jit(solution)/shard_map/ppermute | solution.py:433
  404.7 19.0 %collective-permute-start.27 = (bf16[256,4096]{1,0:T(8,128)(2,1)}, bf16[256,4096]{1,0:T(8,128)(2,1)S(1)}, u32[]{:S(2)}, u32[]{:S(2)}) collective-permute-start(bf16[256,4096]{1,0:T(8,128)(2,1)} %gradient_block.15), channel_id=1, source_target_pairs={{0,4},{4,0},{8,12},{12,8},{16,20},{20,16},{24,28},{28,24},{1,5},{5... | collective-permute-start | bytes 6291464 | tf_op jit(solution)/shard_map/ppermute | solution.py:432
  404.8 19.0 %collective-permute-start.28 = (bf16[256,4096]{1,0:T(8,128)(2,1)S(1)}, bf16[256,4096]{1,0:T(8,128)(2,1)S(1)}, u32[]{:S(2)}, u32[]{:S(2)}) collective-permute-start(bf16[256,4096]{1,0:T(8,128)(2,1)S(1)} %gradient_block.16), channel_id=1, source_target_pairs={{0,4},{4,0},{8,12},{12,8},{16,20},{20,16},{24,28},{28,24},{1,5},{5... | collective-permute-start | bytes 6291464 | tf_op jit(solution)/shard_map/ppermute | solution.py:433
  405.2 47.6 %collective-permute-start.29 = (bf16[256,4096]{1,0:T(8,128)(2,1)S(1)}, bf16[256,4096]{1,0:T(8,128)(2,1)S(1)}, u32[]{:S(2)}, u32[]{:S(2)}) collective-permute-start(bf16[256,4096]{1,0:T(8,128)(2,1)S(1)} %gradient_block.14), channel_id=1, source_target_pairs={{0,1},{1,0},{2,3},{3,2},{4,5},{5,4},{6,7},{7,6},{8,9},{9,8},{10,11... | collective-permute-start | bytes 6291464 | tf_op jit(solution)/shard_map/ppermute | solution.py:448
  456.2 12.3 %collective-permute-start.30 = (bf16[256,4096]{1,0:T(8,128)(2,1)}, bf16[256,4096]{1,0:T(8,128)(2,1)}, u32[]{:S(2)}, u32[]{:S(2)}) collective-permute-start(bf16[256,4096]{1,0:T(8,128)(2,1)} %gradient_block.18), channel_id=1, source_target_pairs={{0,4},{4,0},{8,12},{12,8},{16,20},{20,16},{24,28},{28,24},{1,5},{5... | collective-permute-start | bytes 6291464 | tf_op jit(solution)/shard_map/ppermute | solution.py:432
  456.2 71.2 %collective-permute-start.31 = (bf16[256,4096]{1,0:T(8,128)(2,1)}, bf16[256,4096]{1,0:T(8,128)(2,1)}, u32[]{:S(2)}, u32[]{:S(2)}) collective-permute-start(bf16[256,4096]{1,0:T(8,128)(2,1)} %gradient_block.17), channel_id=1, source_target_pairs={{0,1},{1,0},{2,3},{3,2},{4,5},{5,4},{6,7},{7,6},{8,9},{9,8},{10,11... | collective-permute-start | bytes 6291464 | tf_op jit(solution)/shard_map/ppermute | solution.py:448
  466.5 82.1 %collective-permute-start.37 = (bf16[256,4096]{1,0:T(8,128)(2,1)}, bf16[256,4096]{1,0:T(8,128)(2,1)}, u32[]{:S(2)}, u32[]{:S(2)}) collective-permute-start(bf16[256,4096]{1,0:T(8,128)(2,1)} %gradient_block.21.total_ref), channel_id=1, source_target_pairs={{2,4},{3,5},{4,2},{5,3},{10,12},{11,13},{12,10},{13,11},{18,20},{1... | collective-permute-start | bytes 6291464 | tf_op jit(solution)/shard_map/ppermute | solution.py:472
  473.3 121.1 %collective-permute-start.36 = (bf16[256,4096]{1,0:T(8,128)(2,1)}, bf16[256,4096]{1,0:T(8,128)(2,1)}, u32[]{:S(2)}, u32[]{:S(2)}) collective-permute-start(bf16[256,4096]{1,0:T(8,128)(2,1)} %gradient_block.19), channel_id=1, source_target_pairs={{0,1},{1,0},{2,3},{3,2},{4,5},{5,4},{6,7},{7,6},{8,9},{9,8},{10,11... | collective-permute-start | bytes 6291464 | tf_op jit(solution)/shard_map/ppermute | solution.py:448
  478.3 116.1 %collective-permute-start.35 = (bf16[256,4096]{1,0:T(8,128)(2,1)}, bf16[256,4096]{1,0:T(8,128)(2,1)}, u32[]{:S(2)}, u32[]{:S(2)}) collective-permute-start(bf16[256,4096]{1,0:T(8,128)(2,1)} %gradient_block.20), channel_id=1, source_target_pairs={{0,4},{4,0},{8,12},{12,8},{16,20},{20,16},{24,28},{28,24},{1,5},{5... | collective-permute-start | bytes 6291464 | tf_op jit(solution)/shard_map/ppermute | solution.py:433
  536.4 65.7 %collective-permute-start.32 = (bf16[528,512]{1,0:T(8,128)(2,1)}, bf16[528,512]{1,0:T(8,128)(2,1)}, u32[]{:S(2)}, u32[]{:S(2)}) collective-permute-start(bf16[528,512]{1,0:T(8,128)(2,1)} %dynamic-slice_convert_fusion), channel_id=1, source_target_pairs={{0,16},{4,20},{8,24},{12,28},{16,0},{20,4},{24,8},{28,12},{1,17},{... | collective-permute-start | bytes 1622024 | tf_op jit(solution)/shard_map/ppermute | solution.py:853
  541.4 53.0 %copy-start.15 = (bf16[512,1024]{1,0:T(8,128)(2,1)S(1)}, bf16[512,1024]{1,0:T(8,128)(2,1)}, u32[]{:S(2)}) copy-start(bf16[512,1024]{1,0:T(8,128)(2,1)} %copy-done.12) | copy-start | bytes 3145732
  541.4 53.0 %copy-start.18 = (bf16[512,1024]{1,0:T(8,128)(2,1)S(1)}, bf16[512,1024]{1,0:T(8,128)(2,1)}, u32[]{:S(2)}) copy-start(bf16[512,1024]{1,0:T(8,128)(2,1)} %copy-done.16) | copy-start | bytes 3145732
  541.4 53.0 %copy-start.26 = (bf16[512,1024]{1,0:T(8,128)(2,1)S(1)}, bf16[512,1024]{1,0:T(8,128)(2,1)}, u32[]{:S(2)}) copy-start(bf16[512,1024]{1,0:T(8,128)(2,1)} %copy-done.23) | copy-start | bytes 3145732
  546.5 55.6 %copy-start.48 = (f32[528,1024]{1,0:T(8,128)S(1)}, f32[528,1024]{1,0:T(8,128)}, u32[]{:S(2)}) copy-start(f32[528,1024]{1,0:T(8,128)} %concatenate.51) | copy-start | bytes 6488068
  546.5 78.5 %collective-permute-start.39 = (bf16[256,4096]{1,0:T(8,128)(2,1)}, bf16[256,4096]{1,0:T(8,128)(2,1)}, u32[]{:S(2)}, u32[]{:S(2)}) collective-permute-start(bf16[256,4096]{1,0:T(8,128)(2,1)} %gradient_block.23.total_ref), channel_id=1, source_target_pairs={{2,4},{3,5},{4,2},{5,3},{10,12},{11,13},{12,10},{13,11},{18,20},{1... | collective-permute-start | bytes 6291464 | tf_op jit(solution)/shard_map/ppermute | solution.py:472
  599.6 42.2 %collective-permute-start.38 = (bf16[256,4096]{1,0:T(8,128)(2,1)}, bf16[256,4096]{1,0:T(8,128)(2,1)}, u32[]{:S(2)}, u32[]{:S(2)}) collective-permute-start(bf16[256,4096]{1,0:T(8,128)(2,1)} %gradient_block.22.total_ref), channel_id=1, source_target_pairs={{2,4},{3,5},{4,2},{5,3},{10,12},{11,13},{12,10},{13,11},{18,20},{1... | collective-permute-start | bytes 6291464 | tf_op jit(solution)/shard_map/ppermute | solution.py:472
  603.5 8.1 collective-permute-start.33
  605.0 18.9 %all-to-all-start.1 = ((bf16[8,512,128]{2,1,0:T(8,128)(2,1)}), bf16[8,512,128]{2,1,0:T(8,128)(2,1)S(1)}, u32[]{:S(2)}, u32[]{:S(2)}) async-start(bf16[8,512,128]{2,1,0:T(8,128)(2,1)} %bitcast_bitcast_fusion), calls=%async_computation.1 | async-start | bytes 2097152 | tf_op jit(solution)/shard_map/all_to_all | solution.py:985
  608.5 130.5 %all-gather.18.cloned.1.call-start = ((), (), s32[]{:S(2)}) async-start(), calls=%async_computation.9 | async-start | bytes 5918720 | tf_op jit(solution)/shard_map/all_gather | solution.py:995
  611.7 1.4 collective-permute-start.34
  641.8 140.8 %all-gather.14.cloned.1.call-start = ((), (), s32[]{:S(2)}) async-start(), calls=%async_computation.7 | async-start | bytes 7077888 | tf_op jit(solution)/shard_map/all_gather | solution.py:1059
  674.4 13.4 %collective-permute-start.40 = (bf16[4,256,1536]{2,1,0:T(8,128)(2,1)}, bf16[4,256,1536]{2,1,0:T(8,128)(2,1)S(1)}, u32[]{:S(2)}, u32[]{:S(2)}) collective-permute-start(bf16[4,256,1536]{2,1,0:T(8,128)(2,1)} %get-tuple-element.156), channel_id=1, source_target_pairs={{0,4},{4,0},{8,12},{12,8},{16,20},{20,16},{24,28},{28,24},{1,5},{5... | collective-permute-start | bytes 9437192 | tf_op jit(solution)/shard_map/ppermute | solution.py:826
  692.7 12.0 %collective-permute-start.42 = (bf16[128,1536]{1,0:T(8,128)(2,1)S(1)}, bf16[128,1536]{1,0:T(8,128)(2,1)S(1)}, u32[]{:S(2)}, u32[]{:S(2)}) collective-permute-start(bf16[128,1536]{1,0:T(8,128)(2,1)S(1)} %get-tuple-element.228), channel_id=1, source_target_pairs={{0,8},{4,12},{8,0},{12,4},{16,24},{20,28},{24,16},{28,20},{1,9},{5... | collective-permute-start | bytes 1179656 | tf_op jit(solution)/shard_map/ppermute | solution.py:826
  692.9 19.6 %collective-permute-start.41 = (bf16[128,1536]{1,0:T(8,128)(2,1)}, bf16[128,1536]{1,0:T(8,128)(2,1)S(1)}, u32[]{:S(2)}, u32[]{:S(2)}) collective-permute-start(bf16[128,1536]{1,0:T(8,128)(2,1)} %get-tuple-element.225), channel_id=1, source_target_pairs={{0,8},{4,12},{8,0},{12,4},{16,24},{20,28},{24,16},{28,20},{1,9},{5... | collective-permute-start | bytes 1179656 | tf_op jit(solution)/shard_map/ppermute | solution.py:826
  694.7 17.8 %collective-permute-start.45 = (bf16[128,1536]{1,0:T(8,128)(2,1)}, bf16[128,1536]{1,0:T(8,128)(2,1)}, u32[]{:S(2)}, u32[]{:S(2)}) collective-permute-start(bf16[128,1536]{1,0:T(8,128)(2,1)} %get-tuple-element.226), channel_id=1, source_target_pairs={{0,16},{4,20},{8,24},{12,28},{16,0},{20,4},{24,8},{28,12},{1,17},{... | collective-permute-start | bytes 1179656 | tf_op jit(solution)/shard_map/ppermute | solution.py:826
  706.5 12.4 %collective-permute-start.43 = (bf16[128,1536]{1,0:T(8,128)(2,1)}, bf16[128,1536]{1,0:T(8,128)(2,1)}, u32[]{:S(2)}, u32[]{:S(2)}) collective-permute-start(bf16[128,1536]{1,0:T(8,128)(2,1)} %fusion.40), channel_id=1, source_target_pairs={{0,16},{4,20},{8,24},{12,28},{16,0},{20,4},{24,8},{28,12},{1,17},{... | collective-permute-start | bytes 1179656 | tf_op jit(solution)/shard_map/ppermute | solution.py:826
  706.5 18.7 %collective-permute-start.44 = (bf16[128,1536]{1,0:T(8,128)(2,1)}, bf16[128,1536]{1,0:T(8,128)(2,1)S(1)}, u32[]{:S(2)}, u32[]{:S(2)}) collective-permute-start(bf16[128,1536]{1,0:T(8,128)(2,1)} %get-tuple-element.227), channel_id=1, source_target_pairs={{0,16},{4,20},{8,24},{12,28},{16,0},{20,4},{24,8},{28,12},{1,17},{... | collective-permute-start | bytes 1179656 | tf_op jit(solution)/shard_map/ppermute | solution.py:826
  720.6 7.8 collective-permute-start.46
  737.5 75.4 %all-gather.16.cloned.1.call-start = ((), (), s32[]{:S(2)}) async-start(), calls=%async_computation.8 | async-start | bytes 1216512 | tf_op jit(solution)/shard_map/all_gather | solution.py:1062
  789.3 1.2 collective-permute-start.47
  790.5 3.6 collective-permute-start.48
  794.2 3.6 collective-permute-start.49
  797.8 3.6 collective-permute-start.50
  801.4 11.5 %collective-permute-start.51 = (f32[2,8]{1,0:T(2,128)S(1)}, f32[2,8]{1,0:T(2,128)S(1)}, u32[]{:S(2)}, u32[]{:S(2)}) collective-permute-start(f32[2,8]{1,0:T(2,128)S(1)} %add.756), channel_id=1, source_target_pairs={{0,2},{1,3},{2,0},{3,1},{4,6},{5,7},{6,4},{7,5},{8,10},{9,11},{10,... | collective-permute-start | bytes 200 | tf_op jit(solution)/shard_map/ppermute | solution.py:331
  (69 other events, 615.7 us)
Sparse Core Ops, SparseCore 0:
  12.1 64.7 all-gather.7
  86.4 144.1 all-gather.9
  233.1 43.8 all-gather.11
  366.4 112.1 reduce-scatter.1
  641.9 94.1 all-gather.17
  738.6 43.9 all-gather.13
  785.2 23.7 all-gather.15
